TPU v7x, 32 devices: a whole 2x2x4 slice. The times are simulated.
32 devices in a mesh: groups: 2 (over y), adapter: 4 (over z), tensor: 4 (over x, core).
Axes of the slice: x: 2, y: 2, z: 4, core: 2. Of those that a mesh axis runs over, the one named last changes fastest.
Arguments:
- tokens: bfloat16 [128, 8192], P(('groups', 'adapter'), 'tensor'), parts along dimension 0, may hold values from -6 to 6
- base_up_weight: bfloat16 [8192, 28672], P('tensor', 'adapter'), may hold values from -0.0625 to 0.0625
- adapter_shrink_weight: bfloat16 [4, 8192, 64], P('adapter', 'tensor'), may hold values from -0.0625 to 0.0625
- adapter_expand_weight: bfloat16 [4, 64, 28672], P('adapter', 'tensor'), may hold values from -0.75 to 0.75
- row_adapter_index: int32 [128, 1], P('groups'), parts along dimension 0, may hold values from 0 to 3; in each aligned block of 64 rows (0 to 63, 64 to 127, ...) at most 32 rows name the same one
- adapter_slot_index: int32 [4], replicated, may hold values from 0 to 3, each once
Outputs:
- mixed: bfloat16 [128, 28672], P(('groups', 'tensor'), 'adapter'), parts along dimension 0
There are 2 independent parts, one for each index of `groups`. A program takes and returns all parts, laid end to end along the dimension named above; an argument that names none is the same for every part. Nothing has to cross between parts.
Inputs may be any that keep to these rules, and one draw needn't show every extreme that they name: `row_adapter_index`: every adapter is named by at least one row and by at most 32 rows; some adapter by exactly 32. A permutation: adapter a's matrices are adapter_shrink_weight[adapter_slot_index[a]] and adapter_expand_weight[adapter_slot_index[a]].
All inputs are finite; a program needn't handle non-finite values.
Results may differ from a plain program's by a relative error of at most 0.0031.
Values may be sent and summed in bfloat16 or wider, within the bound.
No kernel may reach another device: no remote copies, remote signals or barrier semaphores. Data moves between devices by JAX's collectives and lax.ppermute only.
A program may use at most 128 MiB of HBM per device.

v0:
```python
import jax
import jax.numpy as jnp
from jax import lax
from jax.sharding import PartitionSpec as P

adapter_scale = 0.5


def on_device(
    tokens,
    base_up_weight,
    adapter_shrink_weight,
    adapter_expand_weight,
    row_adapter_index,
    adapter_slot_index,
):
    owner_count = lax.axis_size("adapter")
    owner_index = lax.axis_index("adapter")
    tensor_index = lax.axis_index("tensor")
    row_count = row_adapter_index.shape[0]
    capacity = 2 * (row_count // owner_count)
    column_width = base_up_weight.shape[1]
    adapter_rank_block = adapter_expand_weight.shape[1]
    local_shrink_weight = adapter_shrink_weight[0]
    owner_of_row = jnp.take(adapter_slot_index, row_adapter_index[:, 0], axis=0)
    member = (owner_of_row[:, None] == jnp.arange(owner_count, dtype=jnp.int32)[None, :]).astype(
        jnp.int32
    )
    position = jnp.sum(jnp.cumsum(member, axis=0) * member, axis=1) - 1
    target = owner_of_row * capacity + position
    row_table = jnp.full((owner_count * capacity,), row_count, jnp.int32)
    row_table = row_table.at[target].set(jnp.arange(row_count, dtype=jnp.int32))
    row_table = row_table.reshape(owner_count, capacity)
    own_rows = lax.dynamic_index_in_dim(row_table, owner_index, 0, keepdims=False)
    piece = lax.all_gather(tokens, "adapter", axis=0, tiled=True)
    base_piece = jnp.dot(piece, base_up_weight, preferred_element_type=jnp.float32)
    shrink_piece = jnp.dot(piece, local_shrink_weight, preferred_element_type=jnp.float32)
    joined = jnp.concatenate([base_piece, shrink_piece], axis=1)
    base_part = joined[:, :column_width]
    shrink_part = jnp.take(joined[:, column_width:], own_rows, axis=0, mode="fill", fill_value=0.0)
    shrunk_rows = lax.psum(shrink_part, "tensor")
    shrunk_rows = (adapter_scale * shrunk_rows).astype(jnp.bfloat16)
    local_shrunk_rows = lax.dynamic_slice_in_dim(
        shrunk_rows, tensor_index * adapter_rank_block, adapter_rank_block, 1
    )
    expanded_output = jnp.dot(
        local_shrunk_rows, adapter_expand_weight[0], preferred_element_type=jnp.float32
    )
    expanded_output = expanded_output.reshape(capacity, owner_count, column_width)
    returned = lax.all_to_all(expanded_output, "adapter", split_axis=1, concat_axis=0, tiled=True)
    delta_rows = returned.reshape(owner_count * capacity, column_width)
    total = base_part.at[row_table.reshape(-1)].add(delta_rows, mode="drop")
    return lax.psum_scatter(total, "tensor", scatter_dimension=0, tiled=True).astype(jnp.bfloat16)


def solution(mesh):
    placed = (
        P(("groups", "adapter"), "tensor"),
        P("tensor", "adapter"),
        P("adapter", "tensor", None),
        P("adapter", "tensor", None),
        P("groups", None),
        P(),
    )
    return jax.shard_map(
        on_device,
        mesh=mesh,
        in_specs=placed,
        out_specs=P(("groups", "tensor"), "adapter"),
        check_vma=False,
    )
```

profile of v0, /device:TPU:0, one launch (start us, length us, event | category | flops | bytes accessed | tf_op | source)
XLA Modules:
  0.0 179.4 jit_solution(9126291899340240684)
XLA Ops:
  6.5 0.0 copy-start
  6.5 1.4 fusion.16
  8.0 3.2 %fusion.21 = s32[64]{0:T(128)S(1)} fusion(s32[]{:T(128)} %bitcast.3, s32[]{:T(128)} %bitcast.2, s32[]{:T(128)} %bitcast.1, s32[]{:T(128)} %bitcast, s32[64,1]{0,1:T(1,128)} %param.10), kind=kLoop, calls=%fused_computation.37 | loop fusion | flops 832 | bytes 528 | tf_op jit(solution)/shard_map/eq | solution.py:26
  11.1 0.1 fusion.5
  11.2 0.1 reduce_window_sum.11
  11.3 0.2 select_reduce_fusion
  11.5 3.2 %fusion.10 = s32[64]{0:T(128)S(1)} fusion(s32[64]{0:T(128)S(1)} %select_reduce_fusion, s32[]{:T(128)} %bitcast.3, s32[]{:T(128)} %bitcast.2, s32[]{:T(128)} %bitcast.1, s32[]{:T(128)} %bitcast, s32[64,1]{0,1:T(1,128)} %param.10), kind=kLoop, calls=%fused_computation.27 | loop fusion | flops 1216 | bytes 784 | tf_op jit(solution)/shard_map/select_n | solution.py:32
  14.7 0.8 scatter_custom_fusion
  15.5 0.1 reshape.58
  15.6 15.8 %all_gather.3 = bf16[64,2048]{1,0:T(8,128)(2,1)S(1)} all-gather(bf16[16,2048]{1,0:T(8,128)(2,1)} %param.6), channel_id=1, replica_groups=mesh['groups'=2,'adapter'=4,'tensor'=4] {'adapter'}, dimensions={0}, use_global_device_ids=true | all-gather | bytes 327680 | tf_op jit(solution)/shard_map/all_gather | solution.py:35
  31.4 0.0 copy-done
  31.4 0.2 fusion.3
  31.7 0.6 gather_fusion
  32.2 0.1 copy.7
  32.3 10.3 %psum.7 = f32[32,64]{0,1:T(8,128)S(1)} all-reduce(f32[32,64]{0,1:T(8,128)S(1)} %broadcast_select_fusion), channel_id=1, replica_groups=mesh['groups'=2,'adapter'=4,'tensor'=4] {'tensor'}, use_global_device_ids=true, to_apply=%region_3.4 | all-reduce | flops 2048 | bytes 16384 | tf_op jit(solution)/shard_map/psum | solution.py:41
  42.6 3.7 %fusion = f32[32,4,7168]{2,0,1:T(8,128)} fusion(bf16[2,4,8,7168]{3,2,1,0:T(8,128)(2,1)} %bitcast.39, f32[32,64]{0,1:T(8,128)S(1)} %psum.7, s32[]{:T(128)S(6)} %select_n.55), kind=kOutput, calls=%fused_computation.3 | convolution fusion | flops 29361152 | bytes 4595716 | tf_op jit(solution)/shard_map/dot_general | solution.py:46
  46.3 5.2 %all-to-all-start = ((f32[32,4,7168]{2,0,1:T(8,128)}), f32[32,4,7168]{2,0,1:T(8,128)}, u32[]{:S(2)}, u32[]{:S(2)}) async-start(f32[32,4,7168]{2,0,1:T(8,128)} %fusion), calls=%async_computation | async-start | bytes 7340032 | tf_op jit(solution)/shard_map/all_to_all | solution.py:50
  51.5 0.0 reduce-scatter.2.cloned.1.call-start
  51.5 12.0 %fusion.17 = f32[64,7168]{1,0:T(8,128)S(1)} fusion(bf16[64,2048]{1,0:T(8,128)(2,1)S(1)} %all_gather.3, bf16[2048,7168]{1,0:T(8,128)(2,1)} %param.7), kind=kOutput, calls=%fused_computation.36 | convolution fusion | flops 1879048192 | bytes 31457280 | tf_op jit(solution)/shard_map/dot_general | solution.py:36
  63.5 70.3 %all-to-all-done = f32[32,4,7168]{2,0,1:T(8,128)} async-done(((f32[32,4,7168]{2,0,1:T(8,128)}), f32[32,4,7168]{2,0,1:T(8,128)}, u32[]{:S(2)}, u32[]{:S(2)}) %all-to-all-start) | async-done | bytes 3670048 | tf_op jit(solution)/shard_map/all_to_all | solution.py:50
  133.7 7.0 %scatter_fusion = f32[64,7168]{1,0:T(8,128)S(1)} fusion(f32[64,7168]{1,0:T(8,128)S(1)} %fusion.17, s32[128]{0:T(128)S(1)} %compare_select_fusion.2, f32[128,7168]{1,0:T(8,128)} %bitcast.16), kind=kCustom, calls=%fused_computation.2 | custom fusion | flops 917504 | bytes 11010560 | tf_op jit(solution)/shard_map/scatter-add | solution.py:52
  140.8 0.0 copy-start.1
  140.8 1.2 copy-done.1
  142.0 0.0 reduce-scatter.2.cloned.1.call-update
  142.0 28.8 %reduce-scatter.2.cloned.1.call-done = f32[16,7168]{1,0:T(8,128)} async-done(((f32[64,7168]{1,0:T(8,128)}), f32[16,7168]{1,0:T(8,128)}) %reduce-scatter.2.cloned.1.call-update) | async-done | bytes 458768 | tf_op jit(solution)/shard_map/reduce_scatter | solution.py:53
  170.8 1.7 convert_element_type.11
  (6 shorter events, 0.0 us)
Async XLA Ops:
  6.5 24.9 %copy-start = (bf16[1,2048,64]{1,2,0:T(8,128)(2,1)S(1)}, bf16[1,2048,64]{1,2,0:T(8,128)(2,1)}, u32[]{:S(2)}) copy-start(bf16[1,2048,64]{1,2,0:T(8,128)(2,1)} %param.8) | copy-start | bytes 786436
  46.3 87.4 %all-to-all-start = ((f32[32,4,7168]{2,0,1:T(8,128)}), f32[32,4,7168]{2,0,1:T(8,128)}, u32[]{:S(2)}, u32[]{:S(2)}) async-start(f32[32,4,7168]{2,0,1:T(8,128)} %fusion), calls=%async_computation | async-start | bytes 7340032 | tf_op jit(solution)/shard_map/all_to_all | solution.py:50
  51.5 119.4 %reduce-scatter.2.cloned.1.call-start = ((), (), s32[]{:S(2)}) async-start(), calls=%async_computation.2 | async-start | bytes 2293760 | tf_op jit(solution)/shard_map/reduce_scatter | solution.py:53
  140.8 1.3 copy-start.1
Sparse Core Ops, SparseCore 0:
  142.2 28.6 reduce-scatter.1
where the time goes:
time: 180 us; the launch traced here: 179 us
  waiting for transfers between devices  99.1 us (55%)
  blocking collectives  26.1 us (14%)
  matrix products  15.9 us (9%)
  other arithmetic  15.5 us (9%)
  between operations  13.5 us (8%)
  starting transfers between devices  5.16 us (3%)
  local copies, waits for them, and re-layouts  4.18 us (2%)
    all_to_all x1, waiting for transfers between devices, on_device(): lax.all_to_all(expanded_output, 'adapter', split_axis=1, concat_axis=0, t...  70.3 us
    reduce_scatter x1, waiting for transfers between devices, on_device(): lax.psum_scatter(total, 'tensor', scatter_dimension=0, tiled=True)  28.8 us
    all_gather x1, blocking collectives, on_device(): piece = lax.all_gather(tokens, 'adapter', axis=0, tiled=True)  15.8 us
    dot_general x1, matrix products, on_device(): jnp.dot(piece, base_up_weight, preferred_element_type=jnp.float32)  12 us
    psum x1, blocking collectives, on_device(): shrunk_rows = lax.psum(shrink_part, 'tensor')  10.3 us
    scatter-add x1, other arithmetic, on_device(): total = base_part.at[row_table.reshape(-1)].add(delta_rows, mode='drop')  7.02 us
    all_to_all x1, starting transfers between devices, on_device(): lax.all_to_all(expanded_output, 'adapter', split_axis=1, concat_axis=0, t...  5.16 us
    dot_general x1, matrix products, on_device(): jnp.dot(local_shrunk_rows, adapter_expand_weight[0], preferred_element_ty...  3.69 us
  transfers between devices with their start and end apart: 2, of which 2 were waited for; matrix products, arithmetic and copies ran while one was open for 7% of the time, Pallas kernels for 0%

commit v1 on v0

v1 whole, which is shorter than its diff:
```python
import functools

import jax
import jax.numpy as jnp
from jax import lax
from jax.experimental import pallas as pl
from jax.experimental.pallas import tpu as pltpu
from jax.sharding import PartitionSpec as P

adapter_scale = 0.5
lane = 128
f32 = jnp.float32
bf16 = jnp.bfloat16


def general(
    tokens,
    base_up_weight,
    adapter_shrink_weight,
    adapter_expand_weight,
    row_adapter_index,
    adapter_slot_index,
):
    owner_count = lax.axis_size("adapter")
    owner_index = lax.axis_index("adapter")
    tensor_index = lax.axis_index("tensor")
    rank_block = adapter_expand_weight.shape[1]
    columns = base_up_weight.shape[1]
    slot = jnp.take(adapter_slot_index, row_adapter_index[:, 0], axis=0)
    rows = lax.all_gather(tokens, "adapter", axis=0, tiled=True)
    expand = adapter_expand_weight[0].reshape(rank_block, owner_count, columns)
    expand = lax.all_to_all(expand, "adapter", split_axis=1, concat_axis=1, tiled=True)
    shrunk = jnp.dot(rows, adapter_shrink_weight[0], preferred_element_type=f32)
    shrunk = jnp.where((slot == owner_index)[:, None], shrunk, 0.0)
    shrunk = lax.psum(shrunk, ("adapter", "tensor"))
    shrunk = (adapter_scale * shrunk).astype(bf16)
    shrunk = lax.dynamic_slice_in_dim(shrunk, tensor_index * rank_block, rank_block, 1)
    chosen = slot[:, None] == jnp.arange(owner_count, dtype=jnp.int32)[None, :]
    spread = jnp.where(chosen[:, None, :], shrunk[:, :, None], jnp.zeros((), bf16))
    total = jnp.dot(rows, base_up_weight, preferred_element_type=f32)
    total = total + jnp.dot(
        spread.reshape(-1, rank_block * owner_count),
        expand.reshape(rank_block * owner_count, columns),
        preferred_element_type=f32,
    )
    return lax.psum_scatter(total, "tensor", scatter_dimension=0, tiled=True).astype(bf16)


def gather_kernel(place, slots, index, *refs):
    owner_count = len(refs) - 1 - 1 - 4
    blocks = refs[:owner_count]
    shrink = refs[owner_count]
    rows_out = refs[owner_count + 1]
    parts_out = refs[owner_count + 2 :]
    a, t = place[0], place[1]
    height = blocks[0].shape[0]
    for j in range(owner_count):
        where = lax.rem(a + j, owner_count)
        rows_out[pl.ds(pl.multiple_of(where * height, height), height), :] = blocks[j][...]
    product = lax.dot_general(
        shrink[...], rows_out[...], (((1,), (1,)), ((), ())), preferred_element_type=f32
    )
    named = index[...]
    slot = jnp.zeros_like(named)
    for k in range(slots.shape[0]):
        slot = jnp.where(named == k, slots[k], slot)
    product = jnp.where(slot == a, product, 0.0)
    rank_block = parts_out[0].shape[0]
    for m in range(4):
        for block in range(4):
            @pl.when(lax.bitwise_xor(t, m) == block)
            def _():
                parts_out[m][...] = product[block * rank_block : (block + 1) * rank_block, :]


def base_kernel(place, rows, weight, total, ordered):
    t = place[1]
    height = rows.shape[0] // 4

    @pl.when(pl.program_id(0) == 0)
    def _():
        for i, flip in enumerate((0, 2, 1, 3)):
            start = pl.multiple_of(lax.bitwise_xor(t, flip) * height, height)
            ordered[i * height : (i + 1) * height, :] = rows[pl.ds(start, height), :]

    total[...] = jnp.dot(ordered[...], weight[...], preferred_element_type=f32)


def delta_kernel(place, base, own, *refs):
    owner_count = (len(refs) - 4 + 1) // 2
    others = refs[: owner_count - 1]
    shrunk = refs[owner_count - 1 : 2 * owner_count - 1]
    keep, send, flat, ordered = refs[2 * owner_count - 1 :]
    t = place[1]
    row_count = base.shape[0]
    height = row_count // 4

    @pl.when(pl.program_id(0) == 0)
    def _():
        stacked = jnp.concatenate([part[...].astype(f32) for part in shrunk], axis=0)
        flat[...] = stacked.T
        for i, flip in enumerate((0, 2, 1, 3)):
            start = pl.multiple_of(lax.bitwise_xor(t, flip) * height, height)
            ordered[i * height : (i + 1) * height, :] = flat[pl.ds(start, height), :].astype(bf16)

    expand = jnp.concatenate([own[0]] + [part[...] for part in others], axis=0)
    total = base[...] + jnp.dot(ordered[...], expand, preferred_element_type=f32)
    keep[...] = total[: row_count // 2]
    send[...] = total[row_count // 2 :]


def column_block(width):
    for size in (512, 256, 128):
        if width % size == 0:
            return size


def base_half(place, rows, weight, half_width, flip):
    row_count, depth = rows.shape
    block = column_block(half_width)
    steps = half_width // block

    def weight_map(i, place):
        return (0, lax.bitwise_xor(place[2], flip) * steps + i)

    return pl.pallas_call(
        base_kernel,
        grid_spec=pltpu.PrefetchScalarGridSpec(
            num_scalar_prefetch=1,
            grid=(steps,),
            in_specs=[
                pl.BlockSpec((row_count, depth), lambda i, place: (0, 0)),
                pl.BlockSpec((depth, block), weight_map),
            ],
            out_specs=pl.BlockSpec((row_count, block), lambda i, place: (0, i)),
            scratch_shapes=[pltpu.VMEM((row_count, depth), bf16)],
        ),
        out_shape=jax.ShapeDtypeStruct((row_count, half_width), f32),
        cost_estimate=pl.CostEstimate(
            flops=2 * row_count * depth * half_width,
            bytes_accessed=2 * depth * half_width,
            transcendentals=0,
        ),
        compiler_params=pltpu.CompilerParams(vmem_limit_bytes=24 << 20),
        name="base_half",
    )(place, rows, weight)


def delta_half(place, base, own, others, shrunk, flip):
    row_count, half_width = base.shape
    rank_block = own.shape[1]
    owner_count = len(shrunk)
    block = column_block(half_width)
    steps = half_width // block

    def own_map(i, place):
        return (0, 0, (2 * place[0] + lax.bitwise_xor(place[2], flip)) * steps + i)

    return pl.pallas_call(
        delta_kernel,
        grid_spec=pltpu.PrefetchScalarGridSpec(
            num_scalar_prefetch=1,
            grid=(steps,),
            in_specs=[
                pl.BlockSpec((row_count, block), lambda i, place: (0, i)),
                pl.BlockSpec((1, rank_block, block), own_map),
            ]
            + [pl.BlockSpec((rank_block, block), lambda i, place: (0, i))] * (owner_count - 1)
            + [pl.BlockSpec((rank_block, row_count), lambda i, place: (0, 0))] * owner_count,
            out_specs=[pl.BlockSpec((row_count // 2, block), lambda i, place: (0, i))] * 2,
            scratch_shapes=[
                pltpu.VMEM((row_count, rank_block * owner_count), f32),
                pltpu.VMEM((row_count, rank_block * owner_count), bf16),
            ],
        ),
        out_shape=[jax.ShapeDtypeStruct((row_count // 2, half_width), f32)] * 2,
        cost_estimate=pl.CostEstimate(
            flops=2 * row_count * rank_block * owner_count * half_width,
            bytes_accessed=12 * row_count * half_width,
            transcendentals=0,
        ),
        compiler_params=pltpu.CompilerParams(vmem_limit_bytes=24 << 20),
        name="delta_half",
    )(place, base, own, *others, *shrunk)


def paired(
    tokens,
    base_up_weight,
    adapter_shrink_weight,
    adapter_expand_weight,
    row_adapter_index,
    adapter_slot_index,
):
    owner_count = lax.axis_size("adapter")
    g = lax.axis_index("groups")
    a = lax.axis_index("adapter")
    t = lax.axis_index("tensor")
    place = jnp.stack([a, t, g]).astype(jnp.int32)
    height, depth = tokens.shape
    row_count = height * owner_count
    columns = base_up_weight.shape[1]
    half_width = columns // 2
    rank_block = adapter_expand_weight.shape[1]
    rank = adapter_shrink_weight.shape[2]

    def from_owner(x, j):
        return lax.ppermute(x, "adapter", [(s, (s - j) % owner_count) for s in range(owner_count)])

    def from_tensor(x, m):
        return lax.ppermute(x, "tensor", [(s, s ^ m) for s in range(4)])

    def from_group(x):
        return lax.ppermute(x, "groups", [(0, 1), (1, 0)])

    others = range(1, owner_count)
    blocks = [tokens] + [from_owner(tokens, j) for j in others]

    expand_near = []
    for j in others:
        to = lax.rem(a - j + owner_count, owner_count)
        piece = lax.dynamic_slice(
            adapter_expand_weight[0],
            (0, to * columns + g * half_width),
            (rank_block, half_width),
        )
        expand_near.append(from_owner(piece, j))
    expand_far = [from_group(x) for x in expand_near]

    full = pl.BlockSpec(memory_space=pltpu.VMEM)
    small = pl.BlockSpec(memory_space=pltpu.SMEM)
    gathered = pl.pallas_call(
        gather_kernel,
        in_specs=[small, small] + [full] * (owner_count + 2),
        out_specs=[full] * 5,
        out_shape=[jax.ShapeDtypeStruct((row_count, depth), bf16)]
        + [jax.ShapeDtypeStruct((rank_block, row_count), f32)] * 4,
        cost_estimate=pl.CostEstimate(
            flops=2 * row_count * depth * rank,
            bytes_accessed=4 * row_count * depth + 2 * depth * rank,
            transcendentals=0,
        ),
        name="gather_rows",
    )(
        place,
        adapter_slot_index,
        row_adapter_index.reshape(1, row_count),
        *blocks,
        adapter_shrink_weight[0].T,
    )
    rows, shrink_parts = gathered[0], gathered[1:]
    shrunk = shrink_parts[0]
    for m in (1, 2, 3):
        shrunk = shrunk + from_tensor(shrink_parts[m], m)
    shrunk = (adapter_scale * shrunk).astype(bf16)
    shrunk = [shrunk] + [from_owner(shrunk, j) for j in others]

    halves = []
    for flip, expand in ((0, expand_near), (1, expand_far)):
        base = base_half(place, rows, base_up_weight, half_width, flip)
        keep, send = delta_half(place, base, adapter_expand_weight, expand, shrunk, flip)
        both = keep + from_tensor(send, 1)
        middle = row_count // 4
        crossed = from_tensor(both[middle:].astype(bf16), 2)
        halves.append((both[:middle] + crossed.astype(f32)).astype(bf16))
    first = jnp.where(g == 0, halves[0], halves[1])
    second = jnp.where(g == 0, halves[1], halves[0])
    return jnp.concatenate([first, second], axis=1)


def on_device(tokens, base_up_weight, adapter_shrink_weight, adapter_expand_weight, *index):
    pairs = lax.axis_size("groups") == 2 and lax.axis_size("tensor") == 4
    few = lax.axis_size("adapter") <= 8
    even = base_up_weight.shape[1] % (2 * lane) == 0 and tokens.shape[0] % 16 == 0
    arrange = paired if pairs and few and even else general
    return arrange(
        tokens, base_up_weight, adapter_shrink_weight, adapter_expand_weight, *index
    )


def solution(mesh):
    placed = (
        P(("groups", "adapter"), "tensor"),
        P("tensor", "adapter"),
        P("adapter", "tensor", None),
        P("adapter", "tensor", None),
        P("groups", None),
        P(),
    )
    return jax.shard_map(
        on_device,
        mesh=mesh,
        in_specs=placed,
        out_specs=P(("groups", "tensor"), "adapter"),
        check_vma=False,
    )
```

time: 180 us -> 69.7 us (0.39)
  waiting for transfers between devices: 99.1 us -> 14.9 us
  blocking collectives: 26.1 us -> 0 us
  starting transfers between devices: 5.16 us -> 22.9 us
  Pallas kernels: 0 us -> 16.6 us
  matrix products: 15.9 us -> 0 us
  between operations: 13.5 us -> 0.13 us
  other arithmetic: 15.5 us -> 2.21 us
  local copies, waits for them, and re-layouts: 4.18 us -> 12.7 us
    all_to_all x1 -> x0, waiting for transfers between devices: 70.3 us -> none  [on_device(): lax.all_to_all(expanded_output, 'adapter', split_axis=1, concat_axis=0, t...]
    reduce_scatter x1 -> x0, waiting for transfers between devices: 28.8 us -> none  [on_device(): lax.psum_scatter(total, 'tensor', scatter_dimension=0, tiled=True)]
    ppermute x0 -> x19, starting transfers between devices: none -> 22.9 us  [the longest x9 14.2 us: from_owner(): lax.ppermute(x, 'adapter', [(s, (s - j) % owner_count) for s in range(own...]
    pallas_call x0 -> x5, Pallas kernels: none -> 16.6 us  [the longest x2 10.2 us: base_half(): pl.pallas_call(base_kernel, grid_spec=pltpu.PrefetchScalarGridSpec(num_sc...]
    dot_general x3 -> x0, matrix products: 15.9 us -> none  [the longest x1 12 us: on_device(): jnp.dot(piece, base_up_weight, preferred_element_type=jnp.float32)]
    all_gather x1 -> x0, blocking collectives: 15.8 us -> none  [on_device(): piece = lax.all_gather(tokens, 'adapter', axis=0, tiled=True)]
    ppermute x0 -> x19, waiting for transfers between devices: none -> 14.9 us  [the longest x9 10.1 us: from_owner(): lax.ppermute(x, 'adapter', [(s, (s - j) % owner_count) for s in range(own...]
    unnamed x4 -> x14, local copies, waits for them, and re-layouts: 1.25 us -> 11.6 us
  transfers between devices with their start and end apart: 2 -> 19, of which waited for: 2 -> 6; matrix products, arithmetic and copies ran while one was open for 7% -> 4% of each run, Pallas kernels for 0% -> 21%
where the time goes in v1:
time: 69.7 us; the launch traced here: 69.4 us
  starting transfers between devices  22.9 us (33%)
  Pallas kernels  16.6 us (24%)
  waiting for transfers between devices  14.9 us (21%)
  local copies, waits for them, and re-layouts  12.7 us (18%)
  other arithmetic  2.21 us (3%)
    ppermute x9, starting transfers between devices, from_owner(): lax.ppermute(x, 'adapter', [(s, (s - j) % owner_count) for s in range(own...  14.2 us
    unnamed x14, local copies, waits for them, and re-layouts  11.6 us
    pallas_call x2, Pallas kernels, base_half(): pl.pallas_call(base_kernel, grid_spec=pltpu.PrefetchScalarGridSpec(num_sc...  10.2 us
    ppermute x9, waiting for transfers between devices, from_owner(): lax.ppermute(x, 'adapter', [(s, (s - j) % owner_count) for s in range(own...  10.1 us
    ppermute x7, starting transfers between devices, from_tensor(): return lax.ppermute(x, 'tensor', [(s, s ^ m) for s in range(4)])  5.18 us
    ppermute x7, waiting for transfers between devices, from_tensor(): return lax.ppermute(x, 'tensor', [(s, s ^ m) for s in range(4)])  4.83 us
    pallas_call x2, Pallas kernels, delta_half(): pl.pallas_call(delta_kernel, grid_spec=pltpu.PrefetchScalarGridSpec(num_s...  4.27 us
    ppermute x3, starting transfers between devices, from_group(): return lax.ppermute(x, 'groups', [(0, 1), (1, 0)])  3.55 us
  transfers between devices with their start and end apart: 19, of which 6 were waited for; matrix products, arithmetic and copies ran while one was open for 4% of the time, Pallas kernels for 21%

profile of v1, /device:TPU:0, one launch (start us, length us, event | category | flops | bytes accessed | tf_op | source)
XLA Modules:
  0.0 69.4 jit_solution(15677255910249847071)
XLA Ops:
  0.0 5.0 %collective-permute-start = (bf16[16,2048]{1,0:T(8,128)(2,1)}, bf16[16,2048]{1,0:T(8,128)(2,1)S(1)}, u32[]{:S(2)}, u32[]{:S(2)}) collective-permute-start(bf16[16,2048]{1,0:T(8,128)(2,1)} %refs_0_.1), channel_id=1, source_target_pairs={{0,12},{4,0},{8,4},{12,8},{1,13},{5,1},{9,5},{13,9},{2,14},{6,2},{... | collective-permute-start | bytes 196616 | tf_op jit(solution)/shard_map/ppermute | solution.py:208
  5.0 0.0 collective-permute-start.1
  5.1 1.0 %collective-permute-start.2 = (bf16[16,2048]{1,0:T(8,128)(2,1)}, bf16[16,2048]{1,0:T(8,128)(2,1)S(1)}, u32[]{:S(2)}, u32[]{:S(2)}) collective-permute-start(bf16[16,2048]{1,0:T(8,128)(2,1)} %refs_0_.1), channel_id=1, source_target_pairs={{0,4},{4,8},{8,12},{12,0},{1,5},{5,9},{9,13},{13,1},{2,6},{6,10},{... | collective-permute-start | bytes 196616 | tf_op jit(solution)/shard_map/ppermute | solution.py:208
  6.1 0.7 pad_add_fusion.place
  6.7 1.1 %collective-permute-done.refs_1_ = bf16[16,2048]{1,0:T(8,128)(2,1)S(1)} collective-permute-done((bf16[16,2048]{1,0:T(8,128)(2,1)}, bf16[16,2048]{1,0:T(8,128)(2,1)S(1)}, u32[]{:S(2)}, u32[]{:S(2)}) %collective-permute-start) | collective-permute-done | bytes 65568 | tf_op jit(solution)/shard_map/ppermute | solution.py:208
  7.9 3.9 %collective-permute-done.1.refs_2_ = bf16[16,2048]{1,0:T(8,128)(2,1)S(1)} collective-permute-done((bf16[16,2048]{1,0:T(8,128)(2,1)}, bf16[16,2048]{1,0:T(8,128)(2,1)S(1)}, u32[]{:S(2)}, u32[]{:S(2)}) %collective-permute-start.1) | collective-permute-done | bytes 65568 | tf_op jit(solution)/shard_map/ppermute | solution.py:208
  11.7 0.6 copy-done.5
  12.3 0.0 copy-done.6
  12.4 2.1 %gather_rows.1 = (bf16[64,2048]{1,0:T(8,128)(2,1)}, f32[16,64]{1,0:T(8,128)}, f32[16,64]{1,0:T(8,128)}, f32[16,64]{1,0:T(8,128)}, f32[16,64]{1,0:T(8,128)}) custom-call(s32[3]{0:T(128)} %pad_add_fusion.place, s32[4]{0:T(128)} %slots.1, s32[1,64]{1,0:T(1,128)} %bitcast.14, bf16[16,2048]{1,0:T(8,128)(2,1)} %refs_0_.1, bf16[16,2048]{1,0:T(8,128)(2,1)} %copy-done.4, ...), custom_call_target="tpu_custom_call" | custom-call | flops 16777216 | bytes 786432 | tf_op jit(solution)/shard_map/gather_rows/pallas_call | solution.py:232
  14.5 0.9 %collective-permute-start.8 = (f32[16,64]{1,0:T(8,128)}, f32[16,64]{1,0:T(8,128)S(1)}, u32[]{:S(2)}, u32[]{:S(2)}) collective-permute-start(f32[16,64]{1,0:T(8,128)} %get-tuple-element.18), channel_id=1, source_target_pairs={{0,3},{1,2},{2,1},{3,0},{4,7},{5,6},{6,5},{7,4},{8,11},{9,10},{10,... | collective-permute-start | bytes 12296 | tf_op jit(solution)/shard_map/ppermute | solution.py:211
  15.4 0.6 collective-permute-start.7
  16.1 0.3 collective-permute-start.6
  16.4 1.0 %dynamic-slice_bitcast_fusion = (bf16[16,3584]{1,0:T(8,128)(2,1)S(1)}, bf16[16,3584]{1,0:T(8,128)(2,1)S(1)}, bf16[16,3584]{1,0:T(8,128)(2,1)S(1)}) fusion(bf16[1,16,28672]{2,1,0:T(8,128)(2,1)} %own.3, s32[]{:T(128)S(6)} %select_n.24, s32[]{:T(128)S(6)} %select_n.23, s32[]{:T(128)S(6)} %select_n.22), kind=kLoop, calls=%fused_computation.7 | loop fusion | bytes 688140 | tf_op jit(solution)/shard_map/dynamic_slice | solution.py:222
  17.4 1.9 %collective-permute-start.3 = (bf16[16,3584]{1,0:T(8,128)(2,1)S(1)}, bf16[16,3584]{1,0:T(8,128)(2,1)S(1)}, u32[]{:S(2)}, u32[]{:S(2)}) collective-permute-start(bf16[16,3584]{1,0:T(8,128)(2,1)S(1)} %get-tuple-element.27), channel_id=1, source_target_pairs={{0,12},{4,0},{8,4},{12,8},{1,13},{5,1},{9,5},{13,9},{2,14},{6,2},{... | collective-permute-start | bytes 344072 | tf_op jit(solution)/shard_map/ppermute | solution.py:208
  19.4 0.0 collective-permute-start.4
  19.4 0.0 collective-permute-done.8
  19.4 1.9 %collective-permute-start.5 = (bf16[16,3584]{1,0:T(8,128)(2,1)S(1)}, bf16[16,3584]{1,0:T(8,128)(2,1)S(1)}, u32[]{:S(2)}, u32[]{:S(2)}) collective-permute-start(bf16[16,3584]{1,0:T(8,128)(2,1)S(1)} %get-tuple-element.25), channel_id=1, source_target_pairs={{0,4},{4,8},{8,12},{12,0},{1,5},{5,9},{9,13},{13,1},{2,6},{6,10},{... | collective-permute-start | bytes 344072 | tf_op jit(solution)/shard_map/ppermute | solution.py:208
  21.3 0.0 collective-permute-done.7
  21.3 0.0 collective-permute-done.6
  21.3 0.7 %multiply_convert_fusion.refs_3_ = bf16[16,64]{1,0:T(8,128)(2,1)S(1)} fusion(f32[16,64]{1,0:T(8,128)S(1)} %collective-permute-done.8, f32[16,64]{1,0:T(8,128)S(1)} %collective-permute-done.7, f32[16,64]{1,0:T(8,128)} %get-tuple-element.15, f32[16,64]{1,0:T(8,128)S(1)} %collective-permute-done.6), kind=kLoop, calls=%fused_computation.12 | loop fusion | flops 5120 | bytes 18432 | tf_op jit(solution)/shard_map/convert_element_type | solution.py:255
  22.0 1.9 %collective-permute-start.9 = (bf16[16,64]{1,0:T(8,128)(2,1)S(1)}, bf16[16,64]{1,0:T(8,128)(2,1)S(1)}, u32[]{:S(2)}, u32[]{:S(2)}) collective-permute-start(bf16[16,64]{1,0:T(8,128)(2,1)S(1)} %multiply_convert_fusion.refs_3_), channel_id=1, source_target_pairs={{0,12},{4,0},{8,4},{12,8},{1,13},{5,1},{9,5},{13,9},{2,14},{6,2},{... | collective-permute-start | bytes 6152 | tf_op jit(solution)/shard_map/ppermute | solution.py:208
  23.9 1.5 %collective-permute-start.14 = (bf16[16,3584]{1,0:T(8,128)(2,1)S(1)}, bf16[16,3584]{1,0:T(8,128)(2,1)S(1)}, u32[]{:S(2)}, u32[]{:S(2)}) collective-permute-start(bf16[16,3584]{1,0:T(8,128)(2,1)S(1)} %collective-permute-done.3.refs_0_), channel_id=1, source_target_pairs={{0,16},{16,0},{1,17},{17,1},{2,18},{18,2},{3,19},{19,3},{4,20},{20... | collective-permute-start | bytes 344072 | tf_op jit(solution)/shard_map/ppermute | solution.py:214
  25.4 4.8 %collective-permute-done.4.refs_1_ = bf16[16,3584]{1,0:T(8,128)(2,1)S(1)} collective-permute-done((bf16[16,3584]{1,0:T(8,128)(2,1)S(1)}, bf16[16,3584]{1,0:T(8,128)(2,1)S(1)}, u32[]{:S(2)}, u32[]{:S(2)}) %collective-permute-start.4) | collective-permute-done | bytes 114720 | tf_op jit(solution)/shard_map/ppermute | solution.py:208
  30.2 1.5 %collective-permute-start.15 = (bf16[16,3584]{1,0:T(8,128)(2,1)S(1)}, bf16[16,3584]{1,0:T(8,128)(2,1)S(1)}, u32[]{:S(2)}, u32[]{:S(2)}) collective-permute-start(bf16[16,3584]{1,0:T(8,128)(2,1)S(1)} %collective-permute-done.4.refs_1_), channel_id=1, source_target_pairs={{0,16},{16,0},{1,17},{17,1},{2,18},{18,2},{3,19},{19,3},{4,20},{20... | collective-permute-start | bytes 344072 | tf_op jit(solution)/shard_map/ppermute | solution.py:214
  31.7 0.0 collective-permute-done.5.refs_2_
  31.7 0.5 collective-permute-start.16
  32.2 9.3 %copy-done = bf16[2048,7168]{1,0:T(8,128)(2,1)S(1)} copy-done((bf16[2048,7168]{1,0:T(8,128)(2,1)S(1)}, bf16[2048,7168]{1,0:T(8,128)(2,1)}, u32[]{:S(2)}) %copy-start) | copy-done | bytes 29360152
  41.6 0.9 %copy-done.2 = bf16[64,2048]{1,0:T(8,128)(2,1)S(1)} copy-done((bf16[64,2048]{1,0:T(8,128)(2,1)S(1)}, bf16[64,2048]{1,0:T(8,128)(2,1)}, u32[]{:S(2)}) %copy-start.2) | copy-done | bytes 262168
  42.5 0.7 copy-done.3
  43.2 5.1 %base_half.2.base = f32[64,3584]{1,0:T(8,128)S(1)} custom-call(s32[3]{0:T(128)S(1)} %copy-done.3, bf16[64,2048]{1,0:T(8,128)(2,1)S(1)} %copy-done.2, bf16[2048,7168]{1,0:T(8,128)(2,1)S(1)} %copy-done), custom_call_target="tpu_custom_call" | custom-call | flops 939524096 | bytes 14680064 | tf_op jit(solution)/shard_map/base_half/pallas_call | solution.py:126
  48.3 2.3 %collective-permute-start.10 = (bf16[16,64]{1,0:T(8,128)(2,1)S(1)}, bf16[16,64]{1,0:T(8,128)(2,1)S(1)}, u32[]{:S(2)}, u32[]{:S(2)}) collective-permute-start(bf16[16,64]{1,0:T(8,128)(2,1)S(1)} %multiply_convert_fusion.refs_3_), channel_id=1, source_target_pairs={{0,8},{4,12},{8,0},{12,4},{1,9},{5,13},{9,1},{13,5},{2,10},{6,14},... | collective-permute-start | bytes 6152 | tf_op jit(solution)/shard_map/ppermute | solution.py:208
  50.7 5.1 %base_half.3.base = f32[64,3584]{1,0:T(8,128)S(1)} custom-call(s32[3]{0:T(128)S(1)} %copy-done.3, bf16[64,2048]{1,0:T(8,128)(2,1)S(1)} %copy-done.2, bf16[2048,7168]{1,0:T(8,128)(2,1)S(1)} %copy-done), custom_call_target="tpu_custom_call" | custom-call | flops 939524096 | bytes 14680064 | tf_op jit(solution)/shard_map/base_half/pallas_call | solution.py:126
  55.8 0.0 collective-permute-done.10.refs_5_
  55.8 0.3 collective-permute-done.11.refs_6_
  56.1 2.1 %delta_half.2 = (f32[32,3584]{1,0:T(8,128)S(1)}, f32[32,3584]{1,0:T(8,128)S(1)}) custom-call(s32[3]{0:T(128)S(1)} %copy-done.3, f32[64,3584]{1,0:T(8,128)S(1)} %base_half.2.base, bf16[1,16,28672]{2,1,0:T(8,128)(2,1)S(1)} %copy-done.1, bf16[16,3584]{1,0:T(8,128)(2,1)S(1)} %collective-permute-done.3.refs_0_, ...), custom_call_target="tpu_custom_call" | custom-call | flops 29360128 | bytes 2752512 | tf_op jit(solution)/shard_map/delta_half/pallas_call | solution.py:159
  58.2 0.1 collective-permute-start.12
  58.3 0.0 collective-permute-done.15.refs_1_
  58.3 0.0 collective-permute-done.16.refs_2_
  58.3 2.1 %delta_half.3 = (f32[32,3584]{1,0:T(8,128)S(1)}, f32[32,3584]{1,0:T(8,128)S(1)}) custom-call(s32[3]{0:T(128)S(1)} %copy-done.3, f32[64,3584]{1,0:T(8,128)S(1)} %base_half.3.base, bf16[1,16,28672]{2,1,0:T(8,128)(2,1)S(1)} %copy-done.1, bf16[16,3584]{1,0:T(8,128)(2,1)S(1)} %collective-permute-done.14.refs_0_, ...), custom_call_target="tpu_custom_call" | custom-call | flops 29360128 | bytes 2752512 | tf_op jit(solution)/shard_map/delta_half/pallas_call | solution.py:159
  60.5 0.6 collective-permute-start.17
  61.0 0.0 collective-permute-done.12
  61.1 1.3 %collective-permute-start.13 = (bf16[16,3584]{1,0:T(8,128)(2,1)S(1)}, bf16[16,3584]{1,0:T(8,128)(2,1)S(1)}, u32[]{:S(2)}, u32[]{:S(2)}) collective-permute-start(bf16[16,3584]{1,0:T(8,128)(2,1)S(1)} %slice.39), channel_id=1, source_target_pairs={{0,2},{1,3},{2,0},{3,1},{4,6},{5,7},{6,4},{7,5},{8,10},{9,11},{10,... | collective-permute-start | bytes 344072 | tf_op jit(solution)/shard_map/ppermute | solution.py:211
  62.4 0.0 collective-permute-done.17
  62.5 1.4 %collective-permute-start.18 = (bf16[16,3584]{1,0:T(8,128)(2,1)S(1)}, bf16[16,3584]{1,0:T(8,128)(2,1)S(1)}, u32[]{:S(2)}, u32[]{:S(2)}) collective-permute-start(bf16[16,3584]{1,0:T(8,128)(2,1)S(1)} %slice.38), channel_id=1, source_target_pairs={{0,2},{1,3},{2,0},{3,1},{4,6},{5,7},{6,4},{7,5},{8,10},{9,11},{10,... | collective-permute-start | bytes 344072 | tf_op jit(solution)/shard_map/ppermute | solution.py:211
  63.9 3.0 %collective-permute-done.13 = bf16[16,3584]{1,0:T(8,128)(2,1)S(1)} collective-permute-done((bf16[16,3584]{1,0:T(8,128)(2,1)S(1)}, bf16[16,3584]{1,0:T(8,128)(2,1)S(1)}, u32[]{:S(2)}, u32[]{:S(2)}) %collective-permute-start.13) | collective-permute-done | bytes 114720 | tf_op jit(solution)/shard_map/ppermute | solution.py:211
  66.9 1.8 %collective-permute-done.18 = bf16[16,3584]{1,0:T(8,128)(2,1)S(1)} collective-permute-done((bf16[16,3584]{1,0:T(8,128)(2,1)S(1)}, bf16[16,3584]{1,0:T(8,128)(2,1)S(1)}, u32[]{:S(2)}, u32[]{:S(2)}) %collective-permute-start.18) | collective-permute-done | bytes 114720 | tf_op jit(solution)/shard_map/ppermute | solution.py:211
  68.7 0.1 broadcast_select_fusion.1
  68.7 0.7 %pad_maximum_fusion = bf16[16,7168]{1,0:T(8,128)(2,1)} fusion(bf16[16,3584]{1,0:T(8,128)(2,1)S(1)} %get-tuple-element.24, bf16[16,3584]{1,0:T(8,128)(2,1)S(1)} %get-tuple-element.23), kind=kLoop, calls=%fused_computation.6 | loop fusion | flops 458752 | bytes 458752 | tf_op jit(solution)/shard_map/concatenate | solution.py:268
  (18 shorter events, 0.2 us)
Async XLA Ops:
  0.0 7.9 %collective-permute-start = (bf16[16,2048]{1,0:T(8,128)(2,1)}, bf16[16,2048]{1,0:T(8,128)(2,1)S(1)}, u32[]{:S(2)}, u32[]{:S(2)}) collective-permute-start(bf16[16,2048]{1,0:T(8,128)(2,1)} %refs_0_.1), channel_id=1, source_target_pairs={{0,12},{4,0},{8,4},{12,8},{1,13},{5,1},{9,5},{13,9},{2,14},{6,2},{... | collective-permute-start | bytes 196616 | tf_op jit(solution)/shard_map/ppermute | solution.py:208
  5.0 6.7 %collective-permute-start.1 = (bf16[16,2048]{1,0:T(8,128)(2,1)}, bf16[16,2048]{1,0:T(8,128)(2,1)S(1)}, u32[]{:S(2)}, u32[]{:S(2)}) collective-permute-start(bf16[16,2048]{1,0:T(8,128)(2,1)} %refs_0_.1), channel_id=1, source_target_pairs={{0,8},{4,12},{8,0},{12,4},{1,9},{5,13},{9,1},{13,5},{2,10},{6,14},... | collective-permute-start | bytes 196616 | tf_op jit(solution)/shard_map/ppermute | solution.py:208
  5.1 6.7 %collective-permute-start.2 = (bf16[16,2048]{1,0:T(8,128)(2,1)}, bf16[16,2048]{1,0:T(8,128)(2,1)S(1)}, u32[]{:S(2)}, u32[]{:S(2)}) collective-permute-start(bf16[16,2048]{1,0:T(8,128)(2,1)} %refs_0_.1), channel_id=1, source_target_pairs={{0,4},{4,8},{8,12},{12,0},{1,5},{5,9},{9,13},{13,1},{2,6},{6,10},{... | collective-permute-start | bytes 196616 | tf_op jit(solution)/shard_map/ppermute | solution.py:208
  7.9 3.9 %copy-start.4 = (bf16[16,2048]{1,0:T(8,128)(2,1)}, bf16[16,2048]{1,0:T(8,128)(2,1)S(1)}, u32[]{:S(2)}) copy-start(bf16[16,2048]{1,0:T(8,128)(2,1)S(1)} %collective-permute-done.refs_1_) | copy-start | bytes 196612
  11.7 0.6 copy-start.5
  11.7 0.6 copy-start.6
  14.5 4.8 %collective-permute-start.8 = (f32[16,64]{1,0:T(8,128)}, f32[16,64]{1,0:T(8,128)S(1)}, u32[]{:S(2)}, u32[]{:S(2)}) collective-permute-start(f32[16,64]{1,0:T(8,128)} %get-tuple-element.18), channel_id=1, source_target_pairs={{0,3},{1,2},{2,1},{3,0},{4,7},{5,6},{6,5},{7,4},{8,11},{9,10},{10,... | collective-permute-start | bytes 12296 | tf_op jit(solution)/shard_map/ppermute | solution.py:211
  15.4 5.8 %collective-permute-start.7 = (f32[16,64]{1,0:T(8,128)}, f32[16,64]{1,0:T(8,128)S(1)}, u32[]{:S(2)}, u32[]{:S(2)}) collective-permute-start(f32[16,64]{1,0:T(8,128)} %get-tuple-element.17), channel_id=1, source_target_pairs={{0,2},{1,3},{2,0},{3,1},{4,6},{5,7},{6,4},{7,5},{8,10},{9,11},{10,... | collective-permute-start | bytes 12296 | tf_op jit(solution)/shard_map/ppermute | solution.py:211
  16.1 5.2 %collective-permute-start.6 = (f32[16,64]{1,0:T(8,128)}, f32[16,64]{1,0:T(8,128)S(1)}, u32[]{:S(2)}, u32[]{:S(2)}) collective-permute-start(f32[16,64]{1,0:T(8,128)} %get-tuple-element.16), channel_id=1, source_target_pairs={{0,1},{1,0},{2,3},{3,2},{4,5},{5,4},{6,7},{7,6},{8,9},{9,8},{10,11... | collective-permute-start | bytes 12296 | tf_op jit(solution)/shard_map/ppermute | solution.py:211
  17.4 6.5 %collective-permute-start.3 = (bf16[16,3584]{1,0:T(8,128)(2,1)S(1)}, bf16[16,3584]{1,0:T(8,128)(2,1)S(1)}, u32[]{:S(2)}, u32[]{:S(2)}) collective-permute-start(bf16[16,3584]{1,0:T(8,128)(2,1)S(1)} %get-tuple-element.27), channel_id=1, source_target_pairs={{0,12},{4,0},{8,4},{12,8},{1,13},{5,1},{9,5},{13,9},{2,14},{6,2},{... | collective-permute-start | bytes 344072 | tf_op jit(solution)/shard_map/ppermute | solution.py:208
  19.4 10.8 %collective-permute-start.4 = (bf16[16,3584]{1,0:T(8,128)(2,1)S(1)}, bf16[16,3584]{1,0:T(8,128)(2,1)S(1)}, u32[]{:S(2)}, u32[]{:S(2)}) collective-permute-start(bf16[16,3584]{1,0:T(8,128)(2,1)S(1)} %get-tuple-element.26), channel_id=1, source_target_pairs={{0,8},{4,12},{8,0},{12,4},{1,9},{5,13},{9,1},{13,5},{2,10},{6,14},... | collective-permute-start | bytes 344072 | tf_op jit(solution)/shard_map/ppermute | solution.py:208
  19.4 12.4 %collective-permute-start.5 = (bf16[16,3584]{1,0:T(8,128)(2,1)S(1)}, bf16[16,3584]{1,0:T(8,128)(2,1)S(1)}, u32[]{:S(2)}, u32[]{:S(2)}) collective-permute-start(bf16[16,3584]{1,0:T(8,128)(2,1)S(1)} %get-tuple-element.25), channel_id=1, source_target_pairs={{0,4},{4,8},{8,12},{12,0},{1,5},{5,9},{9,13},{13,1},{2,6},{6,10},{... | collective-permute-start | bytes 344072 | tf_op jit(solution)/shard_map/ppermute | solution.py:208
  22.0 28.7 %collective-permute-start.9 = (bf16[16,64]{1,0:T(8,128)(2,1)S(1)}, bf16[16,64]{1,0:T(8,128)(2,1)S(1)}, u32[]{:S(2)}, u32[]{:S(2)}) collective-permute-start(bf16[16,64]{1,0:T(8,128)(2,1)S(1)} %multiply_convert_fusion.refs_3_), channel_id=1, source_target_pairs={{0,12},{4,0},{8,4},{12,8},{1,13},{5,1},{9,5},{13,9},{2,14},{6,2},{... | collective-permute-start | bytes 6152 | tf_op jit(solution)/shard_map/ppermute | solution.py:208
  23.9 34.4 %collective-permute-start.14 = (bf16[16,3584]{1,0:T(8,128)(2,1)S(1)}, bf16[16,3584]{1,0:T(8,128)(2,1)S(1)}, u32[]{:S(2)}, u32[]{:S(2)}) collective-permute-start(bf16[16,3584]{1,0:T(8,128)(2,1)S(1)} %collective-permute-done.3.refs_0_), channel_id=1, source_target_pairs={{0,16},{16,0},{1,17},{17,1},{2,18},{18,2},{3,19},{19,3},{4,20},{20... | collective-permute-start | bytes 344072 | tf_op jit(solution)/shard_map/ppermute | solution.py:214
  30.2 28.1 %collective-permute-start.15 = (bf16[16,3584]{1,0:T(8,128)(2,1)S(1)}, bf16[16,3584]{1,0:T(8,128)(2,1)S(1)}, u32[]{:S(2)}, u32[]{:S(2)}) collective-permute-start(bf16[16,3584]{1,0:T(8,128)(2,1)S(1)} %collective-permute-done.4.refs_1_), channel_id=1, source_target_pairs={{0,16},{16,0},{1,17},{17,1},{2,18},{18,2},{3,19},{19,3},{4,20},{20... | collective-permute-start | bytes 344072 | tf_op jit(solution)/shard_map/ppermute | solution.py:214
  31.7 26.6 %collective-permute-start.16 = (bf16[16,3584]{1,0:T(8,128)(2,1)S(1)}, bf16[16,3584]{1,0:T(8,128)(2,1)S(1)}, u32[]{:S(2)}, u32[]{:S(2)}) collective-permute-start(bf16[16,3584]{1,0:T(8,128)(2,1)S(1)} %collective-permute-done.5.refs_2_), channel_id=1, source_target_pairs={{0,16},{16,0},{1,17},{17,1},{2,18},{18,2},{3,19},{19,3},{4,20},{20... | collective-permute-start | bytes 344072 | tf_op jit(solution)/shard_map/ppermute | solution.py:214
  32.2 9.4 %copy-start = (bf16[2048,7168]{1,0:T(8,128)(2,1)S(1)}, bf16[2048,7168]{1,0:T(8,128)(2,1)}, u32[]{:S(2)}) copy-start(bf16[2048,7168]{1,0:T(8,128)(2,1)} %weight.3) | copy-start | bytes 88080384
  41.6 0.9 %copy-start.2 = (bf16[64,2048]{1,0:T(8,128)(2,1)S(1)}, bf16[64,2048]{1,0:T(8,128)(2,1)}, u32[]{:S(2)}) copy-start(bf16[64,2048]{1,0:T(8,128)(2,1)} %get-tuple-element.14.rows) | copy-start | bytes 786436
  42.5 0.7 copy-start.3
  43.2 12.9 %copy-start.1 = (bf16[1,16,28672]{2,1,0:T(8,128)(2,1)S(1)}, bf16[1,16,28672]{2,1,0:T(8,128)(2,1)}, u32[]{:S(2)}) copy-start(bf16[1,16,28672]{2,1,0:T(8,128)(2,1)} %own.3) | copy-start | bytes 2752516
  48.3 7.5 %collective-permute-start.10 = (bf16[16,64]{1,0:T(8,128)(2,1)S(1)}, bf16[16,64]{1,0:T(8,128)(2,1)S(1)}, u32[]{:S(2)}, u32[]{:S(2)}) collective-permute-start(bf16[16,64]{1,0:T(8,128)(2,1)S(1)} %multiply_convert_fusion.refs_3_), channel_id=1, source_target_pairs={{0,8},{4,12},{8,0},{12,4},{1,9},{5,13},{9,1},{13,5},{2,10},{6,14},... | collective-permute-start | bytes 6152 | tf_op jit(solution)/shard_map/ppermute | solution.py:208
  50.6 5.4 %collective-permute-start.11 = (bf16[16,64]{1,0:T(8,128)(2,1)S(1)}, bf16[16,64]{1,0:T(8,128)(2,1)S(1)}, u32[]{:S(2)}, u32[]{:S(2)}) collective-permute-start(bf16[16,64]{1,0:T(8,128)(2,1)S(1)} %multiply_convert_fusion.refs_3_), channel_id=1, source_target_pairs={{0,4},{4,8},{8,12},{12,0},{1,5},{5,9},{9,13},{13,1},{2,6},{6,10},{... | collective-permute-start | bytes 6152 | tf_op jit(solution)/shard_map/ppermute | solution.py:208
  58.2 2.8 %collective-permute-start.12 = (f32[32,3584]{1,0:T(8,128)S(1)}, f32[32,3584]{1,0:T(8,128)S(1)}, u32[]{:S(2)}, u32[]{:S(2)}) collective-permute-start(f32[32,3584]{1,0:T(8,128)S(1)} %get-tuple-element.20), channel_id=1, source_target_pairs={{0,1},{1,0},{2,3},{3,2},{4,5},{5,4},{6,7},{7,6},{8,9},{9,8},{10,11... | collective-permute-start | bytes 1376264 | tf_op jit(solution)/shard_map/ppermute | solution.py:211
  60.5 2.0 %collective-permute-start.17 = (f32[32,3584]{1,0:T(8,128)S(1)}, f32[32,3584]{1,0:T(8,128)S(1)}, u32[]{:S(2)}, u32[]{:S(2)}) collective-permute-start(f32[32,3584]{1,0:T(8,128)S(1)} %get-tuple-element.22), channel_id=1, source_target_pairs={{0,1},{1,0},{2,3},{3,2},{4,5},{5,4},{6,7},{7,6},{8,9},{9,8},{10,11... | collective-permute-start | bytes 1376264 | tf_op jit(solution)/shard_map/ppermute | solution.py:211
  61.1 5.8 %collective-permute-start.13 = (bf16[16,3584]{1,0:T(8,128)(2,1)S(1)}, bf16[16,3584]{1,0:T(8,128)(2,1)S(1)}, u32[]{:S(2)}, u32[]{:S(2)}) collective-permute-start(bf16[16,3584]{1,0:T(8,128)(2,1)S(1)} %slice.39), channel_id=1, source_target_pairs={{0,2},{1,3},{2,0},{3,1},{4,6},{5,7},{6,4},{7,5},{8,10},{9,11},{10,... | collective-permute-start | bytes 344072 | tf_op jit(solution)/shard_map/ppermute | solution.py:211
  62.5 6.2 %collective-permute-start.18 = (bf16[16,3584]{1,0:T(8,128)(2,1)S(1)}, bf16[16,3584]{1,0:T(8,128)(2,1)S(1)}, u32[]{:S(2)}, u32[]{:S(2)}) collective-permute-start(bf16[16,3584]{1,0:T(8,128)(2,1)S(1)} %slice.38), channel_id=1, source_target_pairs={{0,2},{1,3},{2,0},{3,1},{4,6},{5,7},{6,4},{7,5},{8,10},{9,11},{10,... | collective-permute-start | bytes 344072 | tf_op jit(solution)/shard_map/ppermute | solution.py:211

commit v2 on v1

v2 whole, which is shorter than its diff:
```python
import functools

import jax
import jax.numpy as jnp
from jax import lax
from jax.experimental import pallas as pl
from jax.experimental.pallas import tpu as pltpu
from jax.sharding import PartitionSpec as P

adapter_scale = 0.5
lane = 128
f32 = jnp.float32
bf16 = jnp.bfloat16


def general(
    tokens,
    base_up_weight,
    adapter_shrink_weight,
    adapter_expand_weight,
    row_adapter_index,
    adapter_slot_index,
):
    owner_count = lax.axis_size("adapter")
    owner_index = lax.axis_index("adapter")
    tensor_index = lax.axis_index("tensor")
    rank_block = adapter_expand_weight.shape[1]
    columns = base_up_weight.shape[1]
    slot = jnp.take(adapter_slot_index, row_adapter_index[:, 0], axis=0)
    rows = lax.all_gather(tokens, "adapter", axis=0, tiled=True)
    expand = adapter_expand_weight[0].reshape(rank_block, owner_count, columns)
    expand = lax.all_to_all(expand, "adapter", split_axis=1, concat_axis=1, tiled=True)
    shrunk = jnp.dot(rows, adapter_shrink_weight[0], preferred_element_type=f32)
    shrunk = jnp.where((slot == owner_index)[:, None], shrunk, 0.0)
    shrunk = lax.psum(shrunk, ("adapter", "tensor"))
    shrunk = (adapter_scale * shrunk).astype(bf16)
    shrunk = lax.dynamic_slice_in_dim(shrunk, tensor_index * rank_block, rank_block, 1)
    chosen = slot[:, None] == jnp.arange(owner_count, dtype=jnp.int32)[None, :]
    spread = jnp.where(chosen[:, None, :], shrunk[:, :, None], jnp.zeros((), bf16))
    total = jnp.dot(rows, base_up_weight, preferred_element_type=f32)
    total = total + jnp.dot(
        spread.reshape(-1, rank_block * owner_count),
        expand.reshape(rank_block * owner_count, columns),
        preferred_element_type=f32,
    )
    return lax.psum_scatter(total, "tensor", scatter_dimension=0, tiled=True).astype(bf16)


vmem = pl.BlockSpec(memory_space=pltpu.VMEM)
smem = pl.BlockSpec(memory_space=pltpu.SMEM)
anywhere = pl.BlockSpec(memory_space=pl.ANY)


def kernel_call(kernel, name, flops, moved, mib, **specs):
    return pl.pallas_call(
        kernel,
        cost_estimate=pl.CostEstimate(flops=flops, bytes_accessed=moved, transcendentals=0),
        compiler_params=pltpu.CompilerParams(vmem_limit_bytes=mib << 20),
        name=name,
        **specs,
    )


def cut_kernel(owner_count, half_width, expand, *refs):
    pieces, sem = refs[:-1], refs[-1]
    g, a = lax.axis_index("groups"), lax.axis_index("adapter")
    copies = []
    for n, piece in enumerate(pieces):
        to = lax.rem(a - (n + 1) + owner_count, owner_count)
        start = pl.multiple_of((2 * to + g) * half_width, half_width)
        copies.append(
            pltpu.make_async_copy(expand.at[0, :, pl.ds(start, half_width)], piece, sem.at[n])
        )
    for copy in copies:
        copy.start()
    for copy in copies:
        copy.wait()


def load_kernel(parts, weight, expand, after, held, own, sem):
    a = lax.axis_index("adapter")
    depth, columns = held.shape
    step = depth // parts
    copies = []
    for n in range(parts):
        span = pl.ds(n * step, step)
        copies.append(pltpu.make_async_copy(weight.at[span], held.at[span], sem.at[n]))
    start = pl.multiple_of(a * columns, columns)
    copies.append(
        pltpu.make_async_copy(expand.at[0, :, pl.ds(start, columns)], own, sem.at[parts])
    )
    for copy in copies:
        copy.start()
    for copy in copies:
        copy.wait()


def gather_kernel(owner_count, slots, index, *refs):
    blocks = refs[:owner_count]
    shrink, after, rows_out = refs[owner_count : owner_count + 3]
    parts_out = refs[owner_count + 3 : owner_count + 7]
    rows = refs[owner_count + 7]
    a, t = lax.axis_index("adapter"), lax.axis_index("tensor")
    height = blocks[0].shape[0]
    for j in range(owner_count):
        where = lax.rem(a + j, owner_count)
        rows[pl.ds(pl.multiple_of(where * height, height), height), :] = blocks[j][...]
    quarter = rows.shape[0] // 4
    for i, flip in enumerate((0, 2, 1, 3)):
        start = pl.multiple_of(lax.bitwise_xor(t, flip) * quarter, quarter)
        rows_out[i * quarter : (i + 1) * quarter, :] = rows[pl.ds(start, quarter), :]
    product = lax.dot_general(
        shrink[...], rows[...], (((1,), (1,)), ((), ())), preferred_element_type=f32
    )
    named = index[...]
    slot = jnp.zeros_like(named)
    for k in range(slots.shape[0]):
        slot = jnp.where(named == k, slots[k], slot)
    product = jnp.where(slot == a, product, 0.0)
    rank_block = parts_out[0].shape[0]
    for m in range(4):
        for block in range(4):
            @pl.when(lax.bitwise_xor(t, m) == block)
            def _():
                parts_out[m][...] = product[block * rank_block : (block + 1) * rank_block, :]


def base_kernel(flip, block, rows, weight, after, total):
    half = lax.bitwise_xor(lax.axis_index("groups"), flip)
    half_width = total.shape[1]

    @pl.loop(0, half_width // block)
    def _(i):
        column = pl.multiple_of(i * block, block)
        source = pl.multiple_of(half * half_width + column, block)
        total[:, pl.ds(column, block)] = jnp.dot(
            rows[...], weight[:, pl.ds(source, block)], preferred_element_type=f32
        )


def delta_kernel(flip, block, base, own, *refs):
    keep, send, flat, ordered = refs[-4:]
    owner_count = (len(refs) - 4 + 1) // 2
    others = refs[: owner_count - 1]
    shrunk = refs[owner_count - 1 : 2 * owner_count - 1]
    t = lax.axis_index("tensor")
    half = lax.bitwise_xor(lax.axis_index("groups"), flip)
    row_count, half_width = base.shape
    quarter = row_count // 4
    stacked = jnp.concatenate([part[...].astype(f32) for part in shrunk], axis=0)
    flat[...] = stacked.T
    for i, turn in enumerate((0, 2, 1, 3)):
        start = pl.multiple_of(lax.bitwise_xor(t, turn) * quarter, quarter)
        ordered[i * quarter : (i + 1) * quarter, :] = flat[pl.ds(start, quarter), :].astype(bf16)
    left = ordered[...]
    for column in range(0, half_width, block):
        span = pl.ds(column, block)
        source = pl.multiple_of(half * half_width + column, block)
        expand = jnp.concatenate(
            [own[:, pl.ds(source, block)]] + [part[:, span] for part in others], axis=0
        )
        total = base[:, span] + jnp.dot(left, expand, preferred_element_type=f32)
        keep[:, span] = total[: row_count // 2]
        send[:, span] = total[row_count // 2 :]


def column_block(width):
    for size in (512, 256, 128):
        if width % size == 0:
            return size


def paired(
    tokens,
    base_up_weight,
    adapter_shrink_weight,
    adapter_expand_weight,
    row_adapter_index,
    adapter_slot_index,
):
    owner_count = lax.axis_size("adapter")
    g = lax.axis_index("groups")
    height, depth = tokens.shape
    row_count = height * owner_count
    columns = base_up_weight.shape[1]
    half_width = columns // 2
    rank_block = adapter_expand_weight.shape[1]
    rank = adapter_shrink_weight.shape[2]
    block = column_block(half_width)

    def from_owner(x, j):
        return lax.ppermute(x, "adapter", [(s, (s - j) % owner_count) for s in range(owner_count)])

    def from_tensor(x, m):
        return lax.ppermute(x, "tensor", [(s, s ^ m) for s in range(4)])

    def from_group(x):
        return lax.ppermute(x, "groups", [(0, 1), (1, 0)])

    weight = pltpu.with_memory_space_constraint(base_up_weight, pltpu.HBM)
    expand = pltpu.with_memory_space_constraint(adapter_expand_weight, pltpu.HBM)
    others = range(1, owner_count)
    blocks = [tokens] + [from_owner(tokens, j) for j in others]

    pieces = kernel_call(
        functools.partial(cut_kernel, owner_count, half_width),
        "cut_expand",
        1,
        1,
        1,
        in_specs=[anywhere],
        out_specs=[vmem] * (owner_count - 1),
        out_shape=[pltpu.VMEM((rank_block, half_width), bf16)] * (owner_count - 1),
        scratch_shapes=[pltpu.SemaphoreType.DMA((owner_count - 1,))],
    )(expand)
    near = [from_owner(piece, j) for piece, j in zip(pieces, others)]

    parts = 8
    held, own = kernel_call(
        functools.partial(load_kernel, parts),
        "load_weights",
        1,
        1,
        1,
        in_specs=[anywhere] * 3,
        out_specs=[vmem] * 2,
        out_shape=[pltpu.VMEM((depth, columns), bf16), pltpu.VMEM((rank_block, columns), bf16)],
        scratch_shapes=[pltpu.SemaphoreType.DMA((parts + 1,))],
    )(weight, expand, pieces[0])

    gathered = kernel_call(
        functools.partial(gather_kernel, owner_count),
        "gather_rows",
        2 * row_count * depth * rank,
        4 * row_count * depth + 2 * depth * rank,
        4,
        in_specs=[smem, vmem] + [vmem] * (owner_count + 1) + [anywhere],
        out_specs=[vmem] * 5,
        out_shape=[jax.ShapeDtypeStruct((row_count, depth), bf16)]
        + [jax.ShapeDtypeStruct((rank_block, row_count), f32)] * 4,
        scratch_shapes=[pltpu.VMEM((row_count, depth), bf16)],
    )(
        adapter_slot_index,
        row_adapter_index.reshape(1, row_count),
        *blocks,
        adapter_shrink_weight[0].T,
        own,
    )
    rows, shrink_parts = gathered[0], gathered[1:]

    def base_half(flip, after):
        return kernel_call(
            functools.partial(base_kernel, flip, block),
            "base_half",
            2 * row_count * depth * half_width,
            2 * depth * half_width,
            4,
            in_specs=[vmem, vmem, anywhere],
            out_specs=vmem,
            out_shape=jax.ShapeDtypeStruct((row_count, half_width), f32),
        )(rows, held, after)

    def delta_half(flip, base, expand, shrunk):
        return kernel_call(
            functools.partial(delta_kernel, flip, block),
            "delta_half",
            2 * row_count * rank_block * owner_count * half_width,
            12 * row_count * half_width,
            8,
            in_specs=[vmem] * (2 + 2 * owner_count - 1),
            out_specs=[vmem] * 2,
            out_shape=[jax.ShapeDtypeStruct((row_count // 2, half_width), f32)] * 2,
            scratch_shapes=[
                pltpu.VMEM((row_count, rank_block * owner_count), f32),
                pltpu.VMEM((row_count, rank_block * owner_count), bf16),
            ],
        )(base, own, *expand, *shrunk)

    base_first = base_half(0, shrink_parts[0])
    received = [from_tensor(shrink_parts[m], m) for m in (1, 2, 3)]
    *received, base_first = lax.optimization_barrier((*received, base_first))
    shrunk = shrink_parts[0] + received[0] + received[1] + received[2]
    shrunk = (adapter_scale * shrunk).astype(bf16)
    base_second = base_half(1, shrunk)
    shrunk = [shrunk] + [from_owner(shrunk, j) for j in others]
    *near, base_second = lax.optimization_barrier((*near, base_second))
    far = [from_group(x) for x in near]

    halves = []
    for flip, base, pieces in ((0, base_first, near), (1, base_second, far)):
        keep, send = delta_half(flip, base, pieces, shrunk)
        both = keep + from_tensor(send, 1)
        middle = row_count // 4
        crossed = from_tensor(both[middle:].astype(bf16), 2)
        halves.append((both[:middle] + crossed.astype(f32)).astype(bf16))
    first = jnp.where(g == 0, halves[0], halves[1])
    second = jnp.where(g == 0, halves[1], halves[0])
    return jnp.concatenate([first, second], axis=1)


def on_device(tokens, base_up_weight, adapter_shrink_weight, adapter_expand_weight, *index):
    pairs = lax.axis_size("groups") == 2 and lax.axis_size("tensor") == 4
    few = lax.axis_size("adapter") <= 8
    even = base_up_weight.shape[1] % (2 * lane) == 0 and tokens.shape[0] % 16 == 0
    arrange = paired if pairs and few and even else general
    return arrange(
        tokens, base_up_weight, adapter_shrink_weight, adapter_expand_weight, *index
    )


def solution(mesh):
    placed = (
        P(("groups", "adapter"), "tensor"),
        P("tensor", "adapter"),
        P("adapter", "tensor", None),
        P("adapter", "tensor", None),
        P("groups", None),
        P(),
    )
    return jax.shard_map(
        on_device,
        mesh=mesh,
        in_specs=placed,
        out_specs=P(("groups", "tensor"), "adapter"),
        check_vma=False,
    )
```

time: 69.7 us -> 56.8 us (0.81)
  local copies, waits for them, and re-layouts: 12.7 us -> 0.04 us
  starting transfers between devices: 22.9 us -> 19.3 us
  waiting for transfers between devices: 14.9 us -> 17.3 us
  Pallas kernels: 16.6 us -> 18.9 us
  other arithmetic: 2.21 us -> 0.87 us
    unnamed x14 -> x8, local copies, waits for them, and re-layouts: 11.6 us -> 0.01 us
    ppermute x9, starting transfers between devices: 14.2 us -> 11.1 us  [from_owner(): lax.ppermute(x, 'adapter', [(s, (s - j) % owner_count) for s in range(own...]
    pallas_call x5 -> x7, Pallas kernels: 16.6 us -> 18.9 us  [the longest x1 9.5 us: paired(): kernel_call(functools.partial(load_kernel, parts), 'load_weights', 1, 1,...]
    ppermute x7, waiting for transfers between devices: 4.83 us -> 6.36 us  [from_tensor(): return lax.ppermute(x, 'tensor', [(s, s ^ m) for s in range(4)])]
    dynamic_slice x1 -> x0, local copies, waits for them, and re-layouts: 1.03 us -> none  [paired(): lax.dynamic_slice(adapter_expand_weight[0], (0, to * columns + g * half_w...]
    ppermute x9, waiting for transfers between devices: 10.1 us -> 10.9 us  [from_owner(): lax.ppermute(x, 'adapter', [(s, (s - j) % owner_count) for s in range(own...]
  transfers between devices with their start and end apart: 19 -> 19, of which waited for: 6 -> 7; matrix products, arithmetic and copies ran while one was open for 4% -> 0% of each run, Pallas kernels for 21% -> 33%
where the time goes in v2:
time: 56.8 us; the launch traced here: 56.7 us
  starting transfers between devices  19.3 us (34%)
  Pallas kernels  18.9 us (33%)
  waiting for transfers between devices  17.3 us (30%)
  other arithmetic  0.87 us (2%)
    ppermute x9, starting transfers between devices, from_owner(): lax.ppermute(x, 'adapter', [(s, (s - j) % owner_count) for s in range(own...  11.1 us
    ppermute x9, waiting for transfers between devices, from_owner(): lax.ppermute(x, 'adapter', [(s, (s - j) % owner_count) for s in range(own...  10.9 us
    pallas_call x1, Pallas kernels, paired(): kernel_call(functools.partial(load_kernel, parts), 'load_weights', 1, 1,...  9.5 us
    pallas_call x2, Pallas kernels, base_half(): kernel_call(functools.partial(base_kernel, flip, block), 'base_half', 2 *...  6.83 us
    ppermute x7, waiting for transfers between devices, from_tensor(): return lax.ppermute(x, 'tensor', [(s, s ^ m) for s in range(4)])  6.36 us
    ppermute x7, starting transfers between devices, from_tensor(): return lax.ppermute(x, 'tensor', [(s, s ^ m) for s in range(4)])  4.7 us
    ppermute x3, starting transfers between devices, from_group(): return lax.ppermute(x, 'groups', [(0, 1), (1, 0)])  3.55 us
  transfers between devices with their start and end apart: 19, of which 7 were waited for; matrix products, arithmetic and copies ran while one was open for 0% of the time, Pallas kernels for 33%

profile of v2, /device:TPU:0, one launch (start us, length us, event | category | flops | bytes accessed | tf_op | source)
XLA Modules:
  0.0 56.7 jit_solution(13658011467263584932)
XLA Ops:
  0.0 5.1 %collective-permute-start = (bf16[16,2048]{1,0:T(8,128)(2,1)}, bf16[16,2048]{1,0:T(8,128)(2,1)S(1)}, u32[]{:S(2)}, u32[]{:S(2)}) collective-permute-start(bf16[16,2048]{1,0:T(8,128)(2,1)} %refs_0_.1), channel_id=1, source_target_pairs={{0,12},{4,0},{8,4},{12,8},{1,13},{5,1},{9,5},{13,9},{2,14},{6,2},{... | collective-permute-start | bytes 196616 | tf_op jit(solution)/shard_map/ppermute | solution.py:192
  5.1 0.0 collective-permute-start.1
  5.1 1.0 %collective-permute-start.2 = (bf16[16,2048]{1,0:T(8,128)(2,1)}, bf16[16,2048]{1,0:T(8,128)(2,1)S(1)}, u32[]{:S(2)}, u32[]{:S(2)}) collective-permute-start(bf16[16,2048]{1,0:T(8,128)(2,1)} %refs_0_.1), channel_id=1, source_target_pairs={{0,4},{4,8},{8,12},{12,0},{1,5},{5,9},{9,13},{13,1},{2,6},{6,10},{... | collective-permute-start | bytes 196616 | tf_op jit(solution)/shard_map/ppermute | solution.py:192
  6.1 1.0 %cut_expand.1 = (bf16[16,3584]{1,0:T(8,128)(2,1)S(1)}, bf16[16,3584]{1,0:T(8,128)(2,1)S(1)}, bf16[16,3584]{1,0:T(8,128)(2,1)S(1)}) custom-call(bf16[1,16,28672]{2,1,0:T(8,128)(2,1)} %expand.3), custom_call_target="tpu_custom_call" | custom-call | flops 1 | bytes 1 | tf_op jit(solution)/shard_map/cut_expand/pallas_call | solution.py:205
  7.2 2.9 %collective-permute-start.6 = (bf16[16,3584]{1,0:T(8,128)(2,1)S(1)}, bf16[16,3584]{1,0:T(8,128)(2,1)S(1)}, u32[]{:S(2)}, u32[]{:S(2)}) collective-permute-start(bf16[16,3584]{1,0:T(8,128)(2,1)S(1)} %get-tuple-element.27.after), channel_id=1, source_target_pairs={{0,12},{4,0},{8,4},{12,8},{1,13},{5,1},{9,5},{13,9},{2,14},{6,2},{... | collective-permute-start | bytes 344072 | tf_op jit(solution)/shard_map/ppermute | solution.py:192
  10.0 1.1 %collective-permute-start.7 = (bf16[16,3584]{1,0:T(8,128)(2,1)S(1)}, bf16[16,3584]{1,0:T(8,128)(2,1)S(1)}, u32[]{:S(2)}, u32[]{:S(2)}) collective-permute-start(bf16[16,3584]{1,0:T(8,128)(2,1)S(1)} %get-tuple-element.36), channel_id=1, source_target_pairs={{0,8},{4,12},{8,0},{12,4},{1,9},{5,13},{9,1},{13,5},{2,10},{6,14},... | collective-permute-start | bytes 344072 | tf_op jit(solution)/shard_map/ppermute | solution.py:192
  11.2 9.5 %load_weights.1 = (bf16[2048,7168]{1,0:T(8,128)(2,1)S(1)}, bf16[16,7168]{1,0:T(8,128)(2,1)S(1)}) custom-call(bf16[2048,7168]{1,0:T(8,128)(2,1)} %weight.1, bf16[1,16,28672]{2,1,0:T(8,128)(2,1)} %expand.3, bf16[16,3584]{1,0:T(8,128)(2,1)S(1)} %get-tuple-element.27.after), custom_call_target="tpu_custom_call" | custom-call | flops 1 | bytes 1 | tf_op jit(solution)/shard_map/load_weights/pallas_call | solution.py:219
  20.7 0.0 collective-permute-done.refs_1_
  20.7 0.0 collective-permute-done.1.refs_2_
  20.7 0.0 collective-permute-done.2.refs_3_
  20.7 0.0 copy-done.1
  20.7 0.9 %gather_rows.1 = (bf16[64,2048]{1,0:T(8,128)(2,1)S(1)}, f32[16,64]{1,0:T(8,128)S(1)}, f32[16,64]{1,0:T(8,128)S(1)}, f32[16,64]{1,0:T(8,128)S(1)}, f32[16,64]{1,0:T(8,128)S(1)}) custom-call(s32[4]{0:T(128)S(1)} %copy-done.2, s32[1,64]{1,0:T(1,128)S(1)} %bitcast.5, bf16[16,2048]{1,0:T(8,128)(2,1)S(1)} %copy-done.1, ...), custom_call_target="tpu_custom_call" | custom-call | flops 16777216 | bytes 786432 | tf_op jit(solution)/shard_map/gather_rows/pallas_call | solution.py:231
  21.6 0.1 collective-permute-start.3
  21.7 1.6 %collective-permute-start.4 = (f32[16,64]{1,0:T(8,128)S(1)}, f32[16,64]{1,0:T(8,128)S(1)}, u32[]{:S(2)}, u32[]{:S(2)}) collective-permute-start(f32[16,64]{1,0:T(8,128)S(1)} %get-tuple-element.30), channel_id=1, source_target_pairs={{0,2},{1,3},{2,0},{3,1},{4,6},{5,7},{6,4},{7,5},{8,10},{9,11},{10,... | collective-permute-start | bytes 12296 | tf_op jit(solution)/shard_map/ppermute | solution.py:195
  23.3 0.3 collective-permute-start.5
  23.6 3.4 %base_half.2.base = f32[64,3584]{1,0:T(8,128)S(1)} custom-call(bf16[64,2048]{1,0:T(8,128)(2,1)S(1)} %get-tuple-element.32.rows, bf16[2048,7168]{1,0:T(8,128)(2,1)S(1)} %get-tuple-element.33.weight, f32[16,64]{1,0:T(8,128)S(1)} %get-tuple-element.34.after), custom_call_target="tpu_custom_call" | custom-call | flops 939524096 | bytes 14680064 | tf_op jit(solution)/shard_map/base_half/pallas_call | solution.py:252
  27.0 0.0 collective-permute-done.3
  27.0 0.1 collective-permute-start.8
  27.1 0.0 collective-permute-done.4
  27.1 0.0 collective-permute-done.5
  27.1 3.4 %base_half.3.base = f32[64,3584]{1,0:T(8,128)S(1)} custom-call(bf16[64,2048]{1,0:T(8,128)(2,1)S(1)} %get-tuple-element.32.rows, bf16[2048,7168]{1,0:T(8,128)(2,1)S(1)} %get-tuple-element.33.weight, bf16[16,64]{1,0:T(8,128)(2,1)S(1)} %multiply_convert_fusion.after.refs_3_), custom_call_target="tpu_custom_call" | custom-call | flops 939524096 | bytes 14680064 | tf_op jit(solution)/shard_map/base_half/pallas_call | solution.py:252
  30.5 0.0 collective-permute-done.6.refs_0_
  30.5 0.0 collective-permute-done.7.refs_1_
  30.5 3.7 %collective-permute-done.8.refs_2_ = bf16[16,3584]{1,0:T(8,128)(2,1)S(1)} collective-permute-done((bf16[16,3584]{1,0:T(8,128)(2,1)S(1)}, bf16[16,3584]{1,0:T(8,128)(2,1)S(1)}, u32[]{:S(2)}, u32[]{:S(2)}) %collective-permute-start.8) | collective-permute-done | bytes 114720 | tf_op jit(solution)/shard_map/ppermute | solution.py:192
  34.2 1.5 %collective-permute-start.14 = (bf16[16,3584]{1,0:T(8,128)(2,1)S(1)}, bf16[16,3584]{1,0:T(8,128)(2,1)S(1)}, u32[]{:S(2)}, u32[]{:S(2)}) collective-permute-start(bf16[16,3584]{1,0:T(8,128)(2,1)S(1)} %collective-permute-done.6.refs_0_), channel_id=1, source_target_pairs={{0,16},{16,0},{1,17},{17,1},{2,18},{18,2},{3,19},{19,3},{4,20},{20... | collective-permute-start | bytes 344072 | tf_op jit(solution)/shard_map/ppermute | solution.py:198
  35.8 0.5 collective-permute-start.15
  36.3 1.5 %collective-permute-start.16 = (bf16[16,3584]{1,0:T(8,128)(2,1)S(1)}, bf16[16,3584]{1,0:T(8,128)(2,1)S(1)}, u32[]{:S(2)}, u32[]{:S(2)}) collective-permute-start(bf16[16,3584]{1,0:T(8,128)(2,1)S(1)} %collective-permute-done.8.refs_2_), channel_id=1, source_target_pairs={{0,16},{16,0},{1,17},{17,1},{2,18},{18,2},{3,19},{19,3},{4,20},{20... | collective-permute-start | bytes 344072 | tf_op jit(solution)/shard_map/ppermute | solution.py:198
  37.8 0.0 collective-permute-start.10
  37.8 0.7 %collective-permute-start.11 = (bf16[16,64]{1,0:T(8,128)(2,1)S(1)}, bf16[16,64]{1,0:T(8,128)(2,1)S(1)}, u32[]{:S(2)}, u32[]{:S(2)}) collective-permute-start(bf16[16,64]{1,0:T(8,128)(2,1)S(1)} %multiply_convert_fusion.after.refs_3_), channel_id=1, source_target_pairs={{0,4},{4,8},{8,12},{12,0},{1,5},{5,9},{9,13},{13,1},{2,6},{6,10},{... | collective-permute-start | bytes 6152 | tf_op jit(solution)/shard_map/ppermute | solution.py:192
  38.5 3.8 %collective-permute-done.10.refs_5_ = bf16[16,64]{1,0:T(8,128)(2,1)S(1)} collective-permute-done((bf16[16,64]{1,0:T(8,128)(2,1)S(1)}, bf16[16,64]{1,0:T(8,128)(2,1)S(1)}, u32[]{:S(2)}, u32[]{:S(2)}) %collective-permute-start.10) | collective-permute-done | bytes 2080 | tf_op jit(solution)/shard_map/ppermute | solution.py:192
  42.3 0.2 collective-permute-start.9
  42.5 0.7 %collective-permute-done.11.refs_6_ = bf16[16,64]{1,0:T(8,128)(2,1)S(1)} collective-permute-done((bf16[16,64]{1,0:T(8,128)(2,1)S(1)}, bf16[16,64]{1,0:T(8,128)(2,1)S(1)}, u32[]{:S(2)}, u32[]{:S(2)}) %collective-permute-start.11) | collective-permute-done | bytes 2080 | tf_op jit(solution)/shard_map/ppermute | solution.py:192
  43.2 2.7 %collective-permute-done.9.refs_4_ = bf16[16,64]{1,0:T(8,128)(2,1)S(1)} collective-permute-done((bf16[16,64]{1,0:T(8,128)(2,1)S(1)}, bf16[16,64]{1,0:T(8,128)(2,1)S(1)}, u32[]{:S(2)}, u32[]{:S(2)}) %collective-permute-start.9) | collective-permute-done | bytes 2080 | tf_op jit(solution)/shard_map/ppermute | solution.py:192
  45.9 0.3 delta_half.2
  46.2 0.1 collective-permute-start.12
  46.3 0.0 collective-permute-done.14.refs_0_
  46.3 0.0 collective-permute-done.15.refs_1_
  46.3 0.0 collective-permute-done.16.refs_2_
  46.4 0.3 delta_half.3
  46.7 0.5 collective-permute-start.17
  47.3 0.9 %collective-permute-done.12 = f32[32,3584]{1,0:T(8,128)S(1)} collective-permute-done((f32[32,3584]{1,0:T(8,128)S(1)}, f32[32,3584]{1,0:T(8,128)S(1)}, u32[]{:S(2)}, u32[]{:S(2)}) %collective-permute-start.12) | collective-permute-done | bytes 458784 | tf_op jit(solution)/shard_map/ppermute | solution.py:195
  48.2 1.5 %collective-permute-start.13 = (bf16[16,3584]{1,0:T(8,128)(2,1)S(1)}, bf16[16,3584]{1,0:T(8,128)(2,1)S(1)}, u32[]{:S(2)}, u32[]{:S(2)}) collective-permute-start(bf16[16,3584]{1,0:T(8,128)(2,1)S(1)} %slice.39), channel_id=1, source_target_pairs={{0,2},{1,3},{2,0},{3,1},{4,6},{5,7},{6,4},{7,5},{8,10},{9,11},{10,... | collective-permute-start | bytes 344072 | tf_op jit(solution)/shard_map/ppermute | solution.py:195
  49.8 0.0 collective-permute-done.17
  49.8 0.6 %collective-permute-start.18 = (bf16[16,3584]{1,0:T(8,128)(2,1)S(1)}, bf16[16,3584]{1,0:T(8,128)(2,1)S(1)}, u32[]{:S(2)}, u32[]{:S(2)}) collective-permute-start(bf16[16,3584]{1,0:T(8,128)(2,1)S(1)} %slice.38), channel_id=1, source_target_pairs={{0,2},{1,3},{2,0},{3,1},{4,6},{5,7},{6,4},{7,5},{8,10},{9,11},{10,... | collective-permute-start | bytes 344072 | tf_op jit(solution)/shard_map/ppermute | solution.py:195
  50.4 3.8 %collective-permute-done.13 = bf16[16,3584]{1,0:T(8,128)(2,1)S(1)} collective-permute-done((bf16[16,3584]{1,0:T(8,128)(2,1)S(1)}, bf16[16,3584]{1,0:T(8,128)(2,1)S(1)}, u32[]{:S(2)}, u32[]{:S(2)}) %collective-permute-start.13) | collective-permute-done | bytes 114720 | tf_op jit(solution)/shard_map/ppermute | solution.py:195
  54.3 1.7 %collective-permute-done.18 = bf16[16,3584]{1,0:T(8,128)(2,1)S(1)} collective-permute-done((bf16[16,3584]{1,0:T(8,128)(2,1)S(1)}, bf16[16,3584]{1,0:T(8,128)(2,1)S(1)}, u32[]{:S(2)}, u32[]{:S(2)}) %collective-permute-start.18) | collective-permute-done | bytes 114720 | tf_op jit(solution)/shard_map/ppermute | solution.py:195
  55.9 0.1 broadcast_select_fusion.1
  56.0 0.7 %pad_maximum_fusion = bf16[16,7168]{1,0:T(8,128)(2,1)} fusion(bf16[16,3584]{1,0:T(8,128)(2,1)S(1)} %get-tuple-element.50, bf16[16,3584]{1,0:T(8,128)(2,1)S(1)} %get-tuple-element.49), kind=kLoop, calls=%fused_computation.6 | loop fusion | flops 458752 | bytes 458752 | tf_op jit(solution)/shard_map/concatenate | solution.py:298
  (12 shorter events, 0.1 us)
Async XLA Ops:
  0.0 20.7 %copy-start.1 = (bf16[16,2048]{1,0:T(8,128)(2,1)S(1)}, bf16[16,2048]{1,0:T(8,128)(2,1)}, u32[]{:S(2)}) copy-start(bf16[16,2048]{1,0:T(8,128)(2,1)} %refs_0_.1) | copy-start | bytes 196612
  0.0 20.7 %copy-start.3 = (s32[64,1]{0,1:T(1,128)S(1)}, s32[64,1]{0,1:T(1,128)}, u32[]{:S(2)}) copy-start(s32[64,1]{0,1:T(1,128)} %param.10) | copy-start | bytes 772
  0.0 20.7 %copy-start = (bf16[1,2048,64]{1,2,0:T(8,128)(2,1)S(1)}, bf16[1,2048,64]{1,2,0:T(8,128)(2,1)}, u32[]{:S(2)}) copy-start(bf16[1,2048,64]{1,2,0:T(8,128)(2,1)} %param.8) | copy-start | bytes 786436
  0.0 20.7 %copy-start.2 = (s32[4]{0:T(128)S(1)}, s32[4]{0:T(128)}, u32[]{:S(2)}) copy-start(s32[4]{0:T(128)} %slots.1) | copy-start | bytes 52
  0.0 20.7 %collective-permute-start = (bf16[16,2048]{1,0:T(8,128)(2,1)}, bf16[16,2048]{1,0:T(8,128)(2,1)S(1)}, u32[]{:S(2)}, u32[]{:S(2)}) collective-permute-start(bf16[16,2048]{1,0:T(8,128)(2,1)} %refs_0_.1), channel_id=1, source_target_pairs={{0,12},{4,0},{8,4},{12,8},{1,13},{5,1},{9,5},{13,9},{2,14},{6,2},{... | collective-permute-start | bytes 196616 | tf_op jit(solution)/shard_map/ppermute | solution.py:192
  5.1 15.6 %collective-permute-start.1 = (bf16[16,2048]{1,0:T(8,128)(2,1)}, bf16[16,2048]{1,0:T(8,128)(2,1)S(1)}, u32[]{:S(2)}, u32[]{:S(2)}) collective-permute-start(bf16[16,2048]{1,0:T(8,128)(2,1)} %refs_0_.1), channel_id=1, source_target_pairs={{0,8},{4,12},{8,0},{12,4},{1,9},{5,13},{9,1},{13,5},{2,10},{6,14},... | collective-permute-start | bytes 196616 | tf_op jit(solution)/shard_map/ppermute | solution.py:192
  5.1 15.6 %collective-permute-start.2 = (bf16[16,2048]{1,0:T(8,128)(2,1)}, bf16[16,2048]{1,0:T(8,128)(2,1)S(1)}, u32[]{:S(2)}, u32[]{:S(2)}) collective-permute-start(bf16[16,2048]{1,0:T(8,128)(2,1)} %refs_0_.1), channel_id=1, source_target_pairs={{0,4},{4,8},{8,12},{12,0},{1,5},{5,9},{9,13},{13,1},{2,6},{6,10},{... | collective-permute-start | bytes 196616 | tf_op jit(solution)/shard_map/ppermute | solution.py:192
  7.2 23.4 %collective-permute-start.6 = (bf16[16,3584]{1,0:T(8,128)(2,1)S(1)}, bf16[16,3584]{1,0:T(8,128)(2,1)S(1)}, u32[]{:S(2)}, u32[]{:S(2)}) collective-permute-start(bf16[16,3584]{1,0:T(8,128)(2,1)S(1)} %get-tuple-element.27.after), channel_id=1, source_target_pairs={{0,12},{4,0},{8,4},{12,8},{1,13},{5,1},{9,5},{13,9},{2,14},{6,2},{... | collective-permute-start | bytes 344072 | tf_op jit(solution)/shard_map/ppermute | solution.py:192
  10.0 20.5 %collective-permute-start.7 = (bf16[16,3584]{1,0:T(8,128)(2,1)S(1)}, bf16[16,3584]{1,0:T(8,128)(2,1)S(1)}, u32[]{:S(2)}, u32[]{:S(2)}) collective-permute-start(bf16[16,3584]{1,0:T(8,128)(2,1)S(1)} %get-tuple-element.36), channel_id=1, source_target_pairs={{0,8},{4,12},{8,0},{12,4},{1,9},{5,13},{9,1},{13,5},{2,10},{6,14},... | collective-permute-start | bytes 344072 | tf_op jit(solution)/shard_map/ppermute | solution.py:192
  21.6 5.4 %collective-permute-start.3 = (f32[16,64]{1,0:T(8,128)S(1)}, f32[16,64]{1,0:T(8,128)S(1)}, u32[]{:S(2)}, u32[]{:S(2)}) collective-permute-start(f32[16,64]{1,0:T(8,128)S(1)} %get-tuple-element.29), channel_id=1, source_target_pairs={{0,1},{1,0},{2,3},{3,2},{4,5},{5,4},{6,7},{7,6},{8,9},{9,8},{10,11... | collective-permute-start | bytes 12296 | tf_op jit(solution)/shard_map/ppermute | solution.py:195
  21.7 5.4 %collective-permute-start.4 = (f32[16,64]{1,0:T(8,128)S(1)}, f32[16,64]{1,0:T(8,128)S(1)}, u32[]{:S(2)}, u32[]{:S(2)}) collective-permute-start(f32[16,64]{1,0:T(8,128)S(1)} %get-tuple-element.30), channel_id=1, source_target_pairs={{0,2},{1,3},{2,0},{3,1},{4,6},{5,7},{6,4},{7,5},{8,10},{9,11},{10,... | collective-permute-start | bytes 12296 | tf_op jit(solution)/shard_map/ppermute | solution.py:195
  23.3 3.8 %collective-permute-start.5 = (f32[16,64]{1,0:T(8,128)S(1)}, f32[16,64]{1,0:T(8,128)S(1)}, u32[]{:S(2)}, u32[]{:S(2)}) collective-permute-start(f32[16,64]{1,0:T(8,128)S(1)} %get-tuple-element.31), channel_id=1, source_target_pairs={{0,3},{1,2},{2,1},{3,0},{4,7},{5,6},{6,5},{7,4},{8,11},{9,10},{10,... | collective-permute-start | bytes 12296 | tf_op jit(solution)/shard_map/ppermute | solution.py:195
  27.0 7.2 %collective-permute-start.8 = (bf16[16,3584]{1,0:T(8,128)(2,1)S(1)}, bf16[16,3584]{1,0:T(8,128)(2,1)S(1)}, u32[]{:S(2)}, u32[]{:S(2)}) collective-permute-start(bf16[16,3584]{1,0:T(8,128)(2,1)S(1)} %get-tuple-element.37), channel_id=1, source_target_pairs={{0,4},{4,8},{8,12},{12,0},{1,5},{5,9},{9,13},{13,1},{2,6},{6,10},{... | collective-permute-start | bytes 344072 | tf_op jit(solution)/shard_map/ppermute | solution.py:192
  34.2 12.1 %collective-permute-start.14 = (bf16[16,3584]{1,0:T(8,128)(2,1)S(1)}, bf16[16,3584]{1,0:T(8,128)(2,1)S(1)}, u32[]{:S(2)}, u32[]{:S(2)}) collective-permute-start(bf16[16,3584]{1,0:T(8,128)(2,1)S(1)} %collective-permute-done.6.refs_0_), channel_id=1, source_target_pairs={{0,16},{16,0},{1,17},{17,1},{2,18},{18,2},{3,19},{19,3},{4,20},{20... | collective-permute-start | bytes 344072 | tf_op jit(solution)/shard_map/ppermute | solution.py:198
  35.8 10.6 %collective-permute-start.15 = (bf16[16,3584]{1,0:T(8,128)(2,1)S(1)}, bf16[16,3584]{1,0:T(8,128)(2,1)S(1)}, u32[]{:S(2)}, u32[]{:S(2)}) collective-permute-start(bf16[16,3584]{1,0:T(8,128)(2,1)S(1)} %collective-permute-done.7.refs_1_), channel_id=1, source_target_pairs={{0,16},{16,0},{1,17},{17,1},{2,18},{18,2},{3,19},{19,3},{4,20},{20... | collective-permute-start | bytes 344072 | tf_op jit(solution)/shard_map/ppermute | solution.py:198
  36.3 10.1 %collective-permute-start.16 = (bf16[16,3584]{1,0:T(8,128)(2,1)S(1)}, bf16[16,3584]{1,0:T(8,128)(2,1)S(1)}, u32[]{:S(2)}, u32[]{:S(2)}) collective-permute-start(bf16[16,3584]{1,0:T(8,128)(2,1)S(1)} %collective-permute-done.8.refs_2_), channel_id=1, source_target_pairs={{0,16},{16,0},{1,17},{17,1},{2,18},{18,2},{3,19},{19,3},{4,20},{20... | collective-permute-start | bytes 344072 | tf_op jit(solution)/shard_map/ppermute | solution.py:198
  37.8 4.5 %collective-permute-start.10 = (bf16[16,64]{1,0:T(8,128)(2,1)S(1)}, bf16[16,64]{1,0:T(8,128)(2,1)S(1)}, u32[]{:S(2)}, u32[]{:S(2)}) collective-permute-start(bf16[16,64]{1,0:T(8,128)(2,1)S(1)} %multiply_convert_fusion.after.refs_3_), channel_id=1, source_target_pairs={{0,8},{4,12},{8,0},{12,4},{1,9},{5,13},{9,1},{13,5},{2,10},{6,14},... | collective-permute-start | bytes 6152 | tf_op jit(solution)/shard_map/ppermute | solution.py:192
  37.8 5.4 %collective-permute-start.11 = (bf16[16,64]{1,0:T(8,128)(2,1)S(1)}, bf16[16,64]{1,0:T(8,128)(2,1)S(1)}, u32[]{:S(2)}, u32[]{:S(2)}) collective-permute-start(bf16[16,64]{1,0:T(8,128)(2,1)S(1)} %multiply_convert_fusion.after.refs_3_), channel_id=1, source_target_pairs={{0,4},{4,8},{8,12},{12,0},{1,5},{5,9},{9,13},{13,1},{2,6},{6,10},{... | collective-permute-start | bytes 6152 | tf_op jit(solution)/shard_map/ppermute | solution.py:192
  42.3 3.6 %collective-permute-start.9 = (bf16[16,64]{1,0:T(8,128)(2,1)S(1)}, bf16[16,64]{1,0:T(8,128)(2,1)S(1)}, u32[]{:S(2)}, u32[]{:S(2)}) collective-permute-start(bf16[16,64]{1,0:T(8,128)(2,1)S(1)} %multiply_convert_fusion.after.refs_3_), channel_id=1, source_target_pairs={{0,12},{4,0},{8,4},{12,8},{1,13},{5,1},{9,5},{13,9},{2,14},{6,2},{... | collective-permute-start | bytes 6152 | tf_op jit(solution)/shard_map/ppermute | solution.py:192
  46.2 1.9 %collective-permute-start.12 = (f32[32,3584]{1,0:T(8,128)S(1)}, f32[32,3584]{1,0:T(8,128)S(1)}, u32[]{:S(2)}, u32[]{:S(2)}) collective-permute-start(f32[32,3584]{1,0:T(8,128)S(1)} %get-tuple-element.45), channel_id=1, source_target_pairs={{0,1},{1,0},{2,3},{3,2},{4,5},{5,4},{6,7},{7,6},{8,9},{9,8},{10,11... | collective-permute-start | bytes 1376264 | tf_op jit(solution)/shard_map/ppermute | solution.py:195
  46.7 3.0 %collective-permute-start.17 = (f32[32,3584]{1,0:T(8,128)S(1)}, f32[32,3584]{1,0:T(8,128)S(1)}, u32[]{:S(2)}, u32[]{:S(2)}) collective-permute-start(f32[32,3584]{1,0:T(8,128)S(1)} %get-tuple-element.48), channel_id=1, source_target_pairs={{0,1},{1,0},{2,3},{3,2},{4,5},{5,4},{6,7},{7,6},{8,9},{9,8},{10,11... | collective-permute-start | bytes 1376264 | tf_op jit(solution)/shard_map/ppermute | solution.py:195
  48.2 6.1 %collective-permute-start.13 = (bf16[16,3584]{1,0:T(8,128)(2,1)S(1)}, bf16[16,3584]{1,0:T(8,128)(2,1)S(1)}, u32[]{:S(2)}, u32[]{:S(2)}) collective-permute-start(bf16[16,3584]{1,0:T(8,128)(2,1)S(1)} %slice.39), channel_id=1, source_target_pairs={{0,2},{1,3},{2,0},{3,1},{4,6},{5,7},{6,4},{7,5},{8,10},{9,11},{10,... | collective-permute-start | bytes 344072 | tf_op jit(solution)/shard_map/ppermute | solution.py:195
  49.8 6.1 %collective-permute-start.18 = (bf16[16,3584]{1,0:T(8,128)(2,1)S(1)}, bf16[16,3584]{1,0:T(8,128)(2,1)S(1)}, u32[]{:S(2)}, u32[]{:S(2)}) collective-permute-start(bf16[16,3584]{1,0:T(8,128)(2,1)S(1)} %slice.38), channel_id=1, source_target_pairs={{0,2},{1,3},{2,0},{3,1},{4,6},{5,7},{6,4},{7,5},{8,10},{9,11},{10,... | collective-permute-start | bytes 344072 | tf_op jit(solution)/shard_map/ppermute | solution.py:195

commit v3 on v2

--- a/solution.py
+++ b/solution.py
@@ -61,34 +61,19 @@
     )
 
 
-def cut_kernel(owner_count, half_width, expand, *refs):
-    pieces, sem = refs[:-1], refs[-1]
-    g, a = lax.axis_index("groups"), lax.axis_index("adapter")
+def cut_kernel(expand, *refs):
+    chunks, sem = refs[:-1], refs[-1]
+    g = lax.axis_index("groups")
+    owner_count, _, width = chunks[0].shape
     copies = []
-    for n, piece in enumerate(pieces):
-        to = lax.rem(a - (n + 1) + owner_count, owner_count)
-        start = pl.multiple_of((2 * to + g) * half_width, half_width)
-        copies.append(
-            pltpu.make_async_copy(expand.at[0, :, pl.ds(start, half_width)], piece, sem.at[n])
-        )
-    for copy in copies:
-        copy.start()
-    for copy in copies:
-        copy.wait()
-
-
-def load_kernel(parts, weight, expand, after, held, own, sem):
-    a = lax.axis_index("adapter")
-    depth, columns = held.shape
-    step = depth // parts
-    copies = []
-    for n in range(parts):
-        span = pl.ds(n * step, step)
-        copies.append(pltpu.make_async_copy(weight.at[span], held.at[span], sem.at[n]))
-    start = pl.multiple_of(a * columns, columns)
-    copies.append(
-        pltpu.make_async_copy(expand.at[0, :, pl.ds(start, columns)], own, sem.at[parts])
-    )
+    for n, chunk in enumerate(chunks):
+        for to in range(owner_count):
+            start = pl.multiple_of(((2 * to + g) * len(chunks) + n) * width, width)
+            copies.append(
+                pltpu.make_async_copy(
+                    expand.at[0, :, pl.ds(start, width)], chunk.at[to], sem.at[n, to]
+                )
+            )
     for copy in copies:
         copy.start()
     for copy in copies:
@@ -125,43 +110,75 @@
                 parts_out[m][...] = product[block * rank_block : (block + 1) * rank_block, :]
 
 
-def base_kernel(flip, block, rows, weight, after, total):
+def weight_copies(flip, block, weight, first, count, target, sem):
     half = lax.bitwise_xor(lax.axis_index("groups"), flip)
-    half_width = total.shape[1]
-
-    @pl.loop(0, half_width // block)
-    def _(i):
-        column = pl.multiple_of(i * block, block)
-        source = pl.multiple_of(half * half_width + column, block)
-        total[:, pl.ds(column, block)] = jnp.dot(
-            rows[...], weight[:, pl.ds(source, block)], preferred_element_type=f32
+    half_width = weight.shape[1] // 2
+    copies = []
+    for n in range(count):
+        start = pl.multiple_of(half * half_width + (first + n) * block, block)
+        copies.append(
+            pltpu.make_async_copy(weight.at[:, pl.ds(start, block)], target.at[n], sem.at[n])
         )
-
-
-def delta_kernel(flip, block, base, own, *refs):
+    return copies
+
+
+def load_kernel(block, counts, weight, after, held, sem):
+    copies, at = [], 0
+    for flip, count in enumerate(counts):
+        if count == 0:
+            continue
+        span = pl.ds(at, count)
+        copies += weight_copies(flip, block, weight, 0, count, held.at[span], sem.at[span])
+        at += count
+    for copy in copies:
+        copy.start()
+    for copy in copies:
+        copy.wait()
+
+
+def base_kernel(flip, block, first, held_count, rows, weight, *refs):
+    *held, _, total, streamed, sem = refs
+    stream_count = streamed.shape[0]
+    copies = weight_copies(flip, block, weight, held_count, stream_count, streamed, sem)
+    for copy in copies:
+        copy.start()
+    for n in range(held_count):
+        total[:, n * block : (n + 1) * block] = jnp.dot(
+            rows[...], held[0][first + n], preferred_element_type=f32
+        )
+    for n in range(stream_count):
+        copies[n].wait()
+        at = (held_count + n) * block
+        total[:, at : at + block] = jnp.dot(
+            rows[...], streamed[n], preferred_element_type=f32
+        )
+
+
+def delta_kernel(owner_count, block, base, *refs):
+    shrunk, chunks = refs[:owner_count], refs[owner_count:-5]
     keep, send, flat, ordered = refs[-4:]
-    owner_count = (len(refs) - 4 + 1) // 2
-    others = refs[: owner_count - 1]
-    shrunk = refs[owner_count - 1 : 2 * owner_count - 1]
-    t = lax.axis_index("tensor")
-    half = lax.bitwise_xor(lax.axis_index("groups"), flip)
-    row_count, half_width = base.shape
+    a, t = lax.axis_index("adapter"), lax.axis_index("tensor")
+    row_count = base.shape[0]
     quarter = row_count // 4
-    stacked = jnp.concatenate([part[...].astype(f32) for part in shrunk], axis=0)
-    flat[...] = stacked.T
+    rank_block = shrunk[0].shape[0]
+    for j in range(owner_count):
+        start = pl.multiple_of(lax.rem(a + j, owner_count) * rank_block, rank_block)
+        flat[pl.ds(start, rank_block), :] = shrunk[j][...].astype(f32)
+    turned = flat[...].T
+    flat[...] = turned
     for i, turn in enumerate((0, 2, 1, 3)):
         start = pl.multiple_of(lax.bitwise_xor(t, turn) * quarter, quarter)
         ordered[i * quarter : (i + 1) * quarter, :] = flat[pl.ds(start, quarter), :].astype(bf16)
     left = ordered[...]
-    for column in range(0, half_width, block):
-        span = pl.ds(column, block)
-        source = pl.multiple_of(half * half_width + column, block)
-        expand = jnp.concatenate(
-            [own[:, pl.ds(source, block)]] + [part[:, span] for part in others], axis=0
-        )
-        total = base[:, span] + jnp.dot(left, expand, preferred_element_type=f32)
-        keep[:, span] = total[: row_count // 2]
-        send[:, span] = total[row_count // 2 :]
+    at = 0
+    for chunk in chunks:
+        for column in range(0, chunk.shape[1], block):
+            total = base[:, at : at + block] + jnp.dot(
+                left, chunk[:, column : column + block], preferred_element_type=f32
+            )
+            keep[:, at : at + block] = total[: row_count // 2]
+            send[:, at : at + block] = total[row_count // 2 :]
+            at += block
 
 
 def column_block(width):
@@ -202,31 +219,34 @@
     others = range(1, owner_count)
     blocks = [tokens] + [from_owner(tokens, j) for j in others]
 
-    pieces = kernel_call(
-        functools.partial(cut_kernel, owner_count, half_width),
+    chunk_count = 1
+    width = half_width // chunk_count
+    chunks = kernel_call(
+        cut_kernel,
         "cut_expand",
         1,
         1,
         1,
         in_specs=[anywhere],
-        out_specs=[vmem] * (owner_count - 1),
-        out_shape=[pltpu.VMEM((rank_block, half_width), bf16)] * (owner_count - 1),
-        scratch_shapes=[pltpu.SemaphoreType.DMA((owner_count - 1,))],
+        out_specs=vmem,
+        out_shape=pltpu.VMEM((owner_count, rank_block, width), bf16),
+        scratch_shapes=[pltpu.SemaphoreType.DMA((chunk_count, owner_count))],
     )(expand)
-    near = [from_owner(piece, j) for piece, j in zip(pieces, others)]
-
-    parts = 8
-    held, own = kernel_call(
-        functools.partial(load_kernel, parts),
+    near = lax.all_to_all(chunks, "adapter", split_axis=0, concat_axis=0, tiled=True)
+
+    block_count = half_width // block
+    counts = [block_count - 1, 0]
+    held = kernel_call(
+        functools.partial(load_kernel, block, counts),
         "load_weights",
         1,
         1,
         1,
-        in_specs=[anywhere] * 3,
-        out_specs=[vmem] * 2,
-        out_shape=[pltpu.VMEM((depth, columns), bf16), pltpu.VMEM((rank_block, columns), bf16)],
-        scratch_shapes=[pltpu.SemaphoreType.DMA((parts + 1,))],
-    )(weight, expand, pieces[0])
+        in_specs=[anywhere] * 2,
+        out_specs=vmem,
+        out_shape=pltpu.VMEM((sum(counts), depth, block), bf16),
+        scratch_shapes=[pltpu.SemaphoreType.DMA((sum(counts),))],
+    )(weight, chunks)
 
     gathered = kernel_call(
         functools.partial(gather_kernel, owner_count),
@@ -244,54 +264,61 @@
         row_adapter_index.reshape(1, row_count),
         *blocks,
         adapter_shrink_weight[0].T,
-        own,
+        held,
     )
     rows, shrink_parts = gathered[0], gathered[1:]
 
     def base_half(flip, after):
+        stream_count = block_count - counts[flip]
+        kept = [held] if counts[flip] else []
         return kernel_call(
-            functools.partial(base_kernel, flip, block),
+            functools.partial(base_kernel, flip, block, sum(counts[:flip]), counts[flip]),
             "base_half",
             2 * row_count * depth * half_width,
             2 * depth * half_width,
-            4,
-            in_specs=[vmem, vmem, anywhere],
+            4 + (stream_count * depth * block * 2 >> 20),
+            in_specs=[vmem, anywhere] + [vmem] * len(kept) + [anywhere],
             out_specs=vmem,
             out_shape=jax.ShapeDtypeStruct((row_count, half_width), f32),
-        )(rows, held, after)
-
-    def delta_half(flip, base, expand, shrunk):
+            scratch_shapes=[
+                pltpu.VMEM((stream_count, depth, block), bf16),
+                pltpu.SemaphoreType.DMA((stream_count,)),
+            ],
+        )(rows, weight, *kept, after)
+
+    def delta_half(base, shrunk, chunks, after):
         return kernel_call(
-            functools.partial(delta_kernel, flip, block),
+            functools.partial(delta_kernel, owner_count, column_block(width)),
             "delta_half",
             2 * row_count * rank_block * owner_count * half_width,
             12 * row_count * half_width,
             8,
-            in_specs=[vmem] * (2 + 2 * owner_count - 1),
+            in_specs=[vmem] * (1 + owner_count + chunk_count) + [anywhere],
             out_specs=[vmem] * 2,
             out_shape=[jax.ShapeDtypeStruct((row_count // 2, half_width), f32)] * 2,
             scratch_shapes=[
-                pltpu.VMEM((row_count, rank_block * owner_count), f32),
+                pltpu.VMEM((rank_block * owner_count, row_count), f32),
                 pltpu.VMEM((row_count, rank_block * owner_count), bf16),
             ],
-        )(base, own, *expand, *shrunk)
+        )(base, *shrunk, chunks.reshape(owner_count * rank_block, width), after)
 
     base_first = base_half(0, shrink_parts[0])
     received = [from_tensor(shrink_parts[m], m) for m in (1, 2, 3)]
-    *received, base_first = lax.optimization_barrier((*received, base_first))
+    *received, near, base_first = lax.optimization_barrier((*received, near, base_first))
     shrunk = shrink_parts[0] + received[0] + received[1] + received[2]
     shrunk = (adapter_scale * shrunk).astype(bf16)
     base_second = base_half(1, shrunk)
     shrunk = [shrunk] + [from_owner(shrunk, j) for j in others]
-    *near, base_second = lax.optimization_barrier((*near, base_second))
-    far = [from_group(x) for x in near]
+    far = from_group(near)
 
     halves = []
-    for flip, base, pieces in ((0, base_first, near), (1, base_second, far)):
-        keep, send = delta_half(flip, base, pieces, shrunk)
+    after = shrunk[0]
+    middle = row_count // 4
+    for base, chunks in ((base_first, near), (base_second, far)):
+        keep, send = delta_half(base, shrunk, chunks, after)
         both = keep + from_tensor(send, 1)
-        middle = row_count // 4
-        crossed = from_tensor(both[middle:].astype(bf16), 2)
+        after = both[middle:].astype(bf16)
+        crossed = from_tensor(after, 2)
         halves.append((both[:middle] + crossed.astype(f32)).astype(bf16))
     first = jnp.where(g == 0, halves[0], halves[1])
     second = jnp.where(g == 0, halves[1], halves[0])

time: 56.8 us -> 63.7 us (1.12)
  waiting for transfers between devices: 17.3 us -> 23.3 us
  starting transfers between devices: 19.3 us -> 20.7 us
    all_to_all x0 -> x1, starting transfers between devices: none -> 6.34 us  [paired(): lax.all_to_all(chunks, 'adapter', split_axis=0, concat_axis=0, tiled=True)]
    ppermute x3 -> x1, waiting for transfers between devices: 0.01 us -> 5.35 us  [from_group(): return lax.ppermute(x, 'groups', [(0, 1), (1, 0)])]
    ppermute x9 -> x6, starting transfers between devices: 11.1 us -> 7.58 us  [from_owner(): lax.ppermute(x, 'adapter', [(s, (s - j) % owner_count) for s in range(own...]
    ppermute x9 -> x6, waiting for transfers between devices: 10.9 us -> 13.1 us  [from_owner(): lax.ppermute(x, 'adapter', [(s, (s - j) % owner_count) for s in range(own...]
    ppermute x3 -> x1, starting transfers between devices: 3.55 us -> 1.6 us  [from_group(): return lax.ppermute(x, 'groups', [(0, 1), (1, 0)])]
    ppermute x7, waiting for transfers between devices: 6.36 us -> 4.81 us  [from_tensor(): return lax.ppermute(x, 'tensor', [(s, s ^ m) for s in range(4)])]
  transfers between devices with their start and end apart: 19 -> 15, of which waited for: 7 -> 9; matrix products, arithmetic and copies ran while one was open for 0% -> 0% of each run, Pallas kernels for 33% -> 25%
where the time goes in v3:
time: 63.7 us; the launch traced here: 63.5 us
  waiting for transfers between devices  23.3 us (37%)
  starting transfers between devices  20.7 us (32%)
  Pallas kernels  18.3 us (29%)
  other arithmetic  0.89 us (1%)
    ppermute x6, waiting for transfers between devices, from_owner(): lax.ppermute(x, 'adapter', [(s, (s - j) % owner_count) for s in range(own...  13.1 us
    pallas_call x2, Pallas kernels, base_half(): kernel_call(functools.partial(base_kernel, flip, block, sum(counts[:flip]...  10.1 us
    ppermute x6, starting transfers between devices, from_owner(): lax.ppermute(x, 'adapter', [(s, (s - j) % owner_count) for s in range(own...  7.58 us
    all_to_all x1, starting transfers between devices, paired(): lax.all_to_all(chunks, 'adapter', split_axis=0, concat_axis=0, tiled=True)  6.34 us
    ppermute x1, waiting for transfers between devices, from_group(): return lax.ppermute(x, 'groups', [(0, 1), (1, 0)])  5.35 us
    ppermute x7, starting transfers between devices, from_tensor(): return lax.ppermute(x, 'tensor', [(s, s ^ m) for s in range(4)])  5.2 us
    ppermute x7, waiting for transfers between devices, from_tensor(): return lax.ppermute(x, 'tensor', [(s, s ^ m) for s in range(4)])  4.81 us
    pallas_call x1, Pallas kernels, paired(): kernel_call(functools.partial(load_kernel, block, counts), 'load_weights'...  4.79 us
  transfers between devices with their start and end apart: 15, of which 9 were waited for; matrix products, arithmetic and copies ran while one was open for 0% of the time, Pallas kernels for 25%

profile of v3, /device:TPU:0, one launch (start us, length us, event | category | flops | bytes accessed | tf_op | source)
XLA Modules:
  0.0 63.5 jit_solution(889674779011320522)
XLA Ops:
  0.0 0.0 copy-start.1
  0.0 0.0 copy-start.3
  0.0 0.0 copy-start
  0.0 1.9 %cut_expand.1.after = bf16[4,16,3584]{2,1,0:T(8,128)(2,1)} custom-call(bf16[1,16,28672]{2,1,0:T(8,128)(2,1)} %expand.1), custom_call_target="tpu_custom_call" | custom-call | flops 1 | bytes 1 | tf_op jit(solution)/shard_map/cut_expand/pallas_call | solution.py:224
  1.9 6.3 %all-to-all-start = ((bf16[4,16,3584]{2,1,0:T(8,128)(2,1)}), bf16[4,16,3584]{2,1,0:T(8,128)(2,1)S(1)}, u32[]{:S(2)}, u32[]{:S(2)}) async-start(bf16[4,16,3584]{2,1,0:T(8,128)(2,1)} %cut_expand.1.after), calls=%async_computation | async-start | bytes 917504 | tf_op jit(solution)/shard_map/all_to_all | solution.py:235
  8.3 3.8 %collective-permute-start = (bf16[16,2048]{1,0:T(8,128)(2,1)}, bf16[16,2048]{1,0:T(8,128)(2,1)S(1)}, u32[]{:S(2)}, u32[]{:S(2)}) collective-permute-start(bf16[16,2048]{1,0:T(8,128)(2,1)} %refs_0_.1), channel_id=1, source_target_pairs={{0,12},{4,0},{8,4},{12,8},{1,13},{5,1},{9,5},{13,9},{2,14},{6,2},{... | collective-permute-start | bytes 196616 | tf_op jit(solution)/shard_map/ppermute | solution.py:209
  12.1 0.0 collective-permute-start.1
  12.1 1.1 %collective-permute-start.2 = (bf16[16,2048]{1,0:T(8,128)(2,1)}, bf16[16,2048]{1,0:T(8,128)(2,1)S(1)}, u32[]{:S(2)}, u32[]{:S(2)}) collective-permute-start(bf16[16,2048]{1,0:T(8,128)(2,1)} %refs_0_.1), channel_id=1, source_target_pairs={{0,4},{4,8},{8,12},{12,0},{1,5},{5,9},{9,13},{13,1},{2,6},{6,10},{... | collective-permute-start | bytes 196616 | tf_op jit(solution)/shard_map/ppermute | solution.py:209
  13.2 4.8 %load_weights.1.refs_5_.refs_0_ = bf16[6,2048,512]{2,1,0:T(8,128)(2,1)S(1)} custom-call(bf16[2048,7168]{1,0:T(8,128)(2,1)} %weight.5, bf16[4,16,3584]{2,1,0:T(8,128)(2,1)} %cut_expand.1.after), custom_call_target="tpu_custom_call" | custom-call | flops 1 | bytes 1 | tf_op jit(solution)/shard_map/load_weights/pallas_call | solution.py:239
  18.0 0.5 collective-permute-done.refs_1_
  18.5 8.5 %collective-permute-done.1.refs_2_ = bf16[16,2048]{1,0:T(8,128)(2,1)S(1)} collective-permute-done((bf16[16,2048]{1,0:T(8,128)(2,1)}, bf16[16,2048]{1,0:T(8,128)(2,1)S(1)}, u32[]{:S(2)}, u32[]{:S(2)}) %collective-permute-start.1) | collective-permute-done | bytes 65568 | tf_op jit(solution)/shard_map/ppermute | solution.py:209
  27.0 0.0 collective-permute-done.2.refs_3_
  27.0 0.0 copy-done.1
  27.0 0.0 copy-done.3
  27.0 0.0 copy-done
  27.0 0.0 copy-done.2
  27.0 0.9 %gather_rows.1 = (bf16[64,2048]{1,0:T(8,128)(2,1)S(1)}, f32[16,64]{1,0:T(8,128)S(1)}, f32[16,64]{1,0:T(8,128)S(1)}, f32[16,64]{1,0:T(8,128)S(1)}, f32[16,64]{1,0:T(8,128)S(1)}) custom-call(s32[4]{0:T(128)S(1)} %copy-done.2, s32[1,64]{1,0:T(1,128)S(1)} %bitcast.9, bf16[16,2048]{1,0:T(8,128)(2,1)S(1)} %copy-done.1, ...), custom_call_target="tpu_custom_call" | custom-call | flops 16777216 | bytes 786432 | tf_op jit(solution)/shard_map/gather_rows/pallas_call | solution.py:251
  27.9 0.1 collective-permute-start.3
  28.0 1.5 %collective-permute-start.4 = (f32[16,64]{1,0:T(8,128)S(1)}, f32[16,64]{1,0:T(8,128)S(1)}, u32[]{:S(2)}, u32[]{:S(2)}) collective-permute-start(f32[16,64]{1,0:T(8,128)S(1)} %get-tuple-element.20), channel_id=1, source_target_pairs={{0,2},{1,3},{2,0},{3,1},{4,6},{5,7},{6,4},{7,5},{8,10},{9,11},{10,... | collective-permute-start | bytes 12296 | tf_op jit(solution)/shard_map/ppermute | solution.py:212
  29.5 0.3 collective-permute-start.5
  29.8 4.2 %base_half.2.base = f32[64,3584]{1,0:T(8,128)S(1)} custom-call(bf16[64,2048]{1,0:T(8,128)(2,1)S(1)} %get-tuple-element.22.rows, bf16[2048,7168]{1,0:T(8,128)(2,1)} %weight.5, bf16[6,2048,512]{2,1,0:T(8,128)(2,1)S(1)} %load_weights.1.refs_5_.refs_0_, f32[16,64]{1,0:T(8,128)S(1)} %get-tuple-element.23.refs_1_), custom_call_target="tpu_custom_call" | custom-call | flops 939524096 | bytes 14680064 | tf_op jit(solution)/shard_map/base_half/pallas_call | solution.py:274
  34.0 0.0 collective-permute-done.3
  34.0 0.0 collective-permute-done.4
  34.0 0.0 collective-permute-done.5
  34.0 0.0 all-to-all-done
  34.1 0.8 %collective-permute-start.6 = (bf16[16,64]{1,0:T(8,128)(2,1)S(1)}, bf16[16,64]{1,0:T(8,128)(2,1)S(1)}, u32[]{:S(2)}, u32[]{:S(2)}) collective-permute-start(bf16[16,64]{1,0:T(8,128)(2,1)S(1)} %multiply_convert_fusion.refs_0_.refs_5_), channel_id=1, source_target_pairs={{0,12},{4,0},{8,4},{12,8},{1,13},{5,1},{9,5},{13,9},{2,14},{6,2},{... | collective-permute-start | bytes 6152 | tf_op jit(solution)/shard_map/ppermute | solution.py:209
  34.9 0.6 collective-permute-start.7
  35.5 1.2 %collective-permute-start.8 = (bf16[16,64]{1,0:T(8,128)(2,1)S(1)}, bf16[16,64]{1,0:T(8,128)(2,1)S(1)}, u32[]{:S(2)}, u32[]{:S(2)}) collective-permute-start(bf16[16,64]{1,0:T(8,128)(2,1)S(1)} %multiply_convert_fusion.refs_0_.refs_5_), channel_id=1, source_target_pairs={{0,4},{4,8},{8,12},{12,0},{1,5},{5,9},{9,13},{13,1},{2,6},{6,10},{... | collective-permute-start | bytes 6152 | tf_op jit(solution)/shard_map/ppermute | solution.py:209
  36.7 1.0 %collective-permute-done.6.refs_1_ = bf16[16,64]{1,0:T(8,128)(2,1)S(1)} collective-permute-done((bf16[16,64]{1,0:T(8,128)(2,1)S(1)}, bf16[16,64]{1,0:T(8,128)(2,1)S(1)}, u32[]{:S(2)}, u32[]{:S(2)}) %collective-permute-start.6) | collective-permute-done | bytes 2080 | tf_op jit(solution)/shard_map/ppermute | solution.py:209
  37.7 1.7 %collective-permute-done.7.refs_2_ = bf16[16,64]{1,0:T(8,128)(2,1)S(1)} collective-permute-done((bf16[16,64]{1,0:T(8,128)(2,1)S(1)}, bf16[16,64]{1,0:T(8,128)(2,1)S(1)}, u32[]{:S(2)}, u32[]{:S(2)}) %collective-permute-start.7) | collective-permute-done | bytes 2080 | tf_op jit(solution)/shard_map/ppermute | solution.py:209
  39.4 1.5 %collective-permute-done.8.refs_3_ = bf16[16,64]{1,0:T(8,128)(2,1)S(1)} collective-permute-done((bf16[16,64]{1,0:T(8,128)(2,1)S(1)}, bf16[16,64]{1,0:T(8,128)(2,1)S(1)}, u32[]{:S(2)}, u32[]{:S(2)}) %collective-permute-start.8) | collective-permute-done | bytes 2080 | tf_op jit(solution)/shard_map/ppermute | solution.py:209
  40.9 0.4 delta_half.2
  41.2 0.1 collective-permute-start.9
  41.3 1.6 %collective-permute-start.11 = (bf16[4,16,3584]{2,1,0:T(8,128)(2,1)S(1)}, bf16[4,16,3584]{2,1,0:T(8,128)(2,1)S(1)}, u32[]{:S(2)}, u32[]{:S(2)}) collective-permute-start(bf16[4,16,3584]{2,1,0:T(8,128)(2,1)S(1)} %all-to-all-done), channel_id=1, source_target_pairs={{0,16},{16,0},{1,17},{17,1},{2,18},{18,2},{3,19},{19,3},{4,20},{20... | collective-permute-start | bytes 1376264 | tf_op jit(solution)/shard_map/ppermute | solution.py:215
  42.9 5.9 %base_half.3.base = f32[64,3584]{1,0:T(8,128)S(1)} custom-call(bf16[64,2048]{1,0:T(8,128)(2,1)S(1)} %get-tuple-element.22.rows, bf16[2048,7168]{1,0:T(8,128)(2,1)} %weight.5, bf16[16,64]{1,0:T(8,128)(2,1)S(1)} %multiply_convert_fusion.refs_0_.refs_5_), custom_call_target="tpu_custom_call" | custom-call | flops 939524096 | bytes 14680064 | tf_op jit(solution)/shard_map/base_half/pallas_call | solution.py:274
  48.8 0.0 collective-permute-done.9
  48.8 0.1 add.24
  48.9 5.4 %collective-permute-done.11 = bf16[4,16,3584]{2,1,0:T(8,128)(2,1)S(1)} collective-permute-done((bf16[4,16,3584]{2,1,0:T(8,128)(2,1)S(1)}, bf16[4,16,3584]{2,1,0:T(8,128)(2,1)S(1)}, u32[]{:S(2)}, u32[]{:S(2)}) %collective-permute-start.11) | collective-permute-done | bytes 458784 | tf_op jit(solution)/shard_map/ppermute | solution.py:215
  54.2 0.4 delta_half.3
  54.6 0.1 collective-permute-start.12
  54.7 1.6 %collective-permute-start.10 = (bf16[16,3584]{1,0:T(8,128)(2,1)S(1)}, bf16[16,3584]{1,0:T(8,128)(2,1)S(1)}, u32[]{:S(2)}, u32[]{:S(2)}) collective-permute-start(bf16[16,3584]{1,0:T(8,128)(2,1)S(1)} %slice.39.refs_5_), channel_id=1, source_target_pairs={{0,2},{1,3},{2,0},{3,1},{4,6},{5,7},{6,4},{7,5},{8,10},{9,11},{10,... | collective-permute-start | bytes 344072 | tf_op jit(solution)/shard_map/ppermute | solution.py:212
  56.2 0.2 collective-permute-done.12
  56.5 0.1 add.26
  56.6 1.6 %collective-permute-start.13 = (bf16[16,3584]{1,0:T(8,128)(2,1)S(1)}, bf16[16,3584]{1,0:T(8,128)(2,1)S(1)}, u32[]{:S(2)}, u32[]{:S(2)}) collective-permute-start(bf16[16,3584]{1,0:T(8,128)(2,1)S(1)} %slice.38), channel_id=1, source_target_pairs={{0,2},{1,3},{2,0},{3,1},{4,6},{5,7},{6,4},{7,5},{8,10},{9,11},{10,... | collective-permute-start | bytes 344072 | tf_op jit(solution)/shard_map/ppermute | solution.py:212
  58.1 2.6 %collective-permute-done.10 = bf16[16,3584]{1,0:T(8,128)(2,1)S(1)} collective-permute-done((bf16[16,3584]{1,0:T(8,128)(2,1)S(1)}, bf16[16,3584]{1,0:T(8,128)(2,1)S(1)}, u32[]{:S(2)}, u32[]{:S(2)}) %collective-permute-start.10) | collective-permute-done | bytes 114720 | tf_op jit(solution)/shard_map/ppermute | solution.py:212
  60.7 2.0 %collective-permute-done.13 = bf16[16,3584]{1,0:T(8,128)(2,1)S(1)} collective-permute-done((bf16[16,3584]{1,0:T(8,128)(2,1)S(1)}, bf16[16,3584]{1,0:T(8,128)(2,1)S(1)}, u32[]{:S(2)}, u32[]{:S(2)}) %collective-permute-start.13) | collective-permute-done | bytes 114720 | tf_op jit(solution)/shard_map/ppermute | solution.py:212
  62.7 0.1 broadcast_select_fusion.1
  62.8 0.7 %pad_maximum_fusion = bf16[16,7168]{1,0:T(8,128)(2,1)} fusion(bf16[16,3584]{1,0:T(8,128)(2,1)S(1)} %get-tuple-element.34, bf16[16,3584]{1,0:T(8,128)(2,1)S(1)} %get-tuple-element.33), kind=kLoop, calls=%fused_computation.6 | loop fusion | flops 458752 | bytes 458752 | tf_op jit(solution)/shard_map/concatenate | solution.py:325
  (4 shorter events, 0.0 us)
Async XLA Ops:
  0.0 27.0 %copy-start.1 = (bf16[16,2048]{1,0:T(8,128)(2,1)S(1)}, bf16[16,2048]{1,0:T(8,128)(2,1)}, u32[]{:S(2)}) copy-start(bf16[16,2048]{1,0:T(8,128)(2,1)} %refs_0_.1) | copy-start | bytes 196612
  0.0 27.0 %copy-start.3 = (s32[64,1]{0,1:T(1,128)S(1)}, s32[64,1]{0,1:T(1,128)}, u32[]{:S(2)}) copy-start(s32[64,1]{0,1:T(1,128)} %param.10) | copy-start | bytes 772
  0.0 27.0 %copy-start = (bf16[1,2048,64]{1,2,0:T(8,128)(2,1)S(1)}, bf16[1,2048,64]{1,2,0:T(8,128)(2,1)}, u32[]{:S(2)}) copy-start(bf16[1,2048,64]{1,2,0:T(8,128)(2,1)} %param.8) | copy-start | bytes 786436
  0.0 27.0 %copy-start.2 = (s32[4]{0:T(128)S(1)}, s32[4]{0:T(128)}, u32[]{:S(2)}) copy-start(s32[4]{0:T(128)} %slots.1) | copy-start | bytes 52
  1.9 32.1 %all-to-all-start = ((bf16[4,16,3584]{2,1,0:T(8,128)(2,1)}), bf16[4,16,3584]{2,1,0:T(8,128)(2,1)S(1)}, u32[]{:S(2)}, u32[]{:S(2)}) async-start(bf16[4,16,3584]{2,1,0:T(8,128)(2,1)} %cut_expand.1.after), calls=%async_computation | async-start | bytes 917504 | tf_op jit(solution)/shard_map/all_to_all | solution.py:235
  8.3 10.2 %collective-permute-start = (bf16[16,2048]{1,0:T(8,128)(2,1)}, bf16[16,2048]{1,0:T(8,128)(2,1)S(1)}, u32[]{:S(2)}, u32[]{:S(2)}) collective-permute-start(bf16[16,2048]{1,0:T(8,128)(2,1)} %refs_0_.1), channel_id=1, source_target_pairs={{0,12},{4,0},{8,4},{12,8},{1,13},{5,1},{9,5},{13,9},{2,14},{6,2},{... | collective-permute-start | bytes 196616 | tf_op jit(solution)/shard_map/ppermute | solution.py:209
  12.1 14.9 %collective-permute-start.1 = (bf16[16,2048]{1,0:T(8,128)(2,1)}, bf16[16,2048]{1,0:T(8,128)(2,1)S(1)}, u32[]{:S(2)}, u32[]{:S(2)}) collective-permute-start(bf16[16,2048]{1,0:T(8,128)(2,1)} %refs_0_.1), channel_id=1, source_target_pairs={{0,8},{4,12},{8,0},{12,4},{1,9},{5,13},{9,1},{13,5},{2,10},{6,14},... | collective-permute-start | bytes 196616 | tf_op jit(solution)/shard_map/ppermute | solution.py:209
  12.1 14.9 %collective-permute-start.2 = (bf16[16,2048]{1,0:T(8,128)(2,1)}, bf16[16,2048]{1,0:T(8,128)(2,1)S(1)}, u32[]{:S(2)}, u32[]{:S(2)}) collective-permute-start(bf16[16,2048]{1,0:T(8,128)(2,1)} %refs_0_.1), channel_id=1, source_target_pairs={{0,4},{4,8},{8,12},{12,0},{1,5},{5,9},{9,13},{13,1},{2,6},{6,10},{... | collective-permute-start | bytes 196616 | tf_op jit(solution)/shard_map/ppermute | solution.py:209
  27.9 6.1 %collective-permute-start.3 = (f32[16,64]{1,0:T(8,128)S(1)}, f32[16,64]{1,0:T(8,128)S(1)}, u32[]{:S(2)}, u32[]{:S(2)}) collective-permute-start(f32[16,64]{1,0:T(8,128)S(1)} %get-tuple-element.19), channel_id=1, source_target_pairs={{0,1},{1,0},{2,3},{3,2},{4,5},{5,4},{6,7},{7,6},{8,9},{9,8},{10,11... | collective-permute-start | bytes 12296 | tf_op jit(solution)/shard_map/ppermute | solution.py:212
  28.0 6.1 %collective-permute-start.4 = (f32[16,64]{1,0:T(8,128)S(1)}, f32[16,64]{1,0:T(8,128)S(1)}, u32[]{:S(2)}, u32[]{:S(2)}) collective-permute-start(f32[16,64]{1,0:T(8,128)S(1)} %get-tuple-element.20), channel_id=1, source_target_pairs={{0,2},{1,3},{2,0},{3,1},{4,6},{5,7},{6,4},{7,5},{8,10},{9,11},{10,... | collective-permute-start | bytes 12296 | tf_op jit(solution)/shard_map/ppermute | solution.py:212
  29.5 4.5 %collective-permute-start.5 = (f32[16,64]{1,0:T(8,128)S(1)}, f32[16,64]{1,0:T(8,128)S(1)}, u32[]{:S(2)}, u32[]{:S(2)}) collective-permute-start(f32[16,64]{1,0:T(8,128)S(1)} %get-tuple-element.21), channel_id=1, source_target_pairs={{0,3},{1,2},{2,1},{3,0},{4,7},{5,6},{6,5},{7,4},{8,11},{9,10},{10,... | collective-permute-start | bytes 12296 | tf_op jit(solution)/shard_map/ppermute | solution.py:212
  34.1 3.7 %collective-permute-start.6 = (bf16[16,64]{1,0:T(8,128)(2,1)S(1)}, bf16[16,64]{1,0:T(8,128)(2,1)S(1)}, u32[]{:S(2)}, u32[]{:S(2)}) collective-permute-start(bf16[16,64]{1,0:T(8,128)(2,1)S(1)} %multiply_convert_fusion.refs_0_.refs_5_), channel_id=1, source_target_pairs={{0,12},{4,0},{8,4},{12,8},{1,13},{5,1},{9,5},{13,9},{2,14},{6,2},{... | collective-permute-start | bytes 6152 | tf_op jit(solution)/shard_map/ppermute | solution.py:209
  34.9 4.5 %collective-permute-start.7 = (bf16[16,64]{1,0:T(8,128)(2,1)S(1)}, bf16[16,64]{1,0:T(8,128)(2,1)S(1)}, u32[]{:S(2)}, u32[]{:S(2)}) collective-permute-start(bf16[16,64]{1,0:T(8,128)(2,1)S(1)} %multiply_convert_fusion.refs_0_.refs_5_), channel_id=1, source_target_pairs={{0,8},{4,12},{8,0},{12,4},{1,9},{5,13},{9,1},{13,5},{2,10},{6,14},... | collective-permute-start | bytes 6152 | tf_op jit(solution)/shard_map/ppermute | solution.py:209
  35.5 5.4 %collective-permute-start.8 = (bf16[16,64]{1,0:T(8,128)(2,1)S(1)}, bf16[16,64]{1,0:T(8,128)(2,1)S(1)}, u32[]{:S(2)}, u32[]{:S(2)}) collective-permute-start(bf16[16,64]{1,0:T(8,128)(2,1)S(1)} %multiply_convert_fusion.refs_0_.refs_5_), channel_id=1, source_target_pairs={{0,4},{4,8},{8,12},{12,0},{1,5},{5,9},{9,13},{13,1},{2,6},{6,10},{... | collective-permute-start | bytes 6152 | tf_op jit(solution)/shard_map/ppermute | solution.py:209
  41.2 7.6 %collective-permute-start.9 = (f32[32,3584]{1,0:T(8,128)S(1)}, f32[32,3584]{1,0:T(8,128)S(1)}, u32[]{:S(2)}, u32[]{:S(2)}) collective-permute-start(f32[32,3584]{1,0:T(8,128)S(1)} %get-tuple-element.30), channel_id=1, source_target_pairs={{0,1},{1,0},{2,3},{3,2},{4,5},{5,4},{6,7},{7,6},{8,9},{9,8},{10,11... | collective-permute-start | bytes 1376264 | tf_op jit(solution)/shard_map/ppermute | solution.py:212
  41.3 12.9 %collective-permute-start.11 = (bf16[4,16,3584]{2,1,0:T(8,128)(2,1)S(1)}, bf16[4,16,3584]{2,1,0:T(8,128)(2,1)S(1)}, u32[]{:S(2)}, u32[]{:S(2)}) collective-permute-start(bf16[4,16,3584]{2,1,0:T(8,128)(2,1)S(1)} %all-to-all-done), channel_id=1, source_target_pairs={{0,16},{16,0},{1,17},{17,1},{2,18},{18,2},{3,19},{19,3},{4,20},{20... | collective-permute-start | bytes 1376264 | tf_op jit(solution)/shard_map/ppermute | solution.py:215
  54.6 1.9 %collective-permute-start.12 = (f32[32,3584]{1,0:T(8,128)S(1)}, f32[32,3584]{1,0:T(8,128)S(1)}, u32[]{:S(2)}, u32[]{:S(2)}) collective-permute-start(f32[32,3584]{1,0:T(8,128)S(1)} %get-tuple-element.32), channel_id=1, source_target_pairs={{0,1},{1,0},{2,3},{3,2},{4,5},{5,4},{6,7},{7,6},{8,9},{9,8},{10,11... | collective-permute-start | bytes 1376264 | tf_op jit(solution)/shard_map/ppermute | solution.py:212
  54.7 6.0 %collective-permute-start.10 = (bf16[16,3584]{1,0:T(8,128)(2,1)S(1)}, bf16[16,3584]{1,0:T(8,128)(2,1)S(1)}, u32[]{:S(2)}, u32[]{:S(2)}) collective-permute-start(bf16[16,3584]{1,0:T(8,128)(2,1)S(1)} %slice.39.refs_5_), channel_id=1, source_target_pairs={{0,2},{1,3},{2,0},{3,1},{4,6},{5,7},{6,4},{7,5},{8,10},{9,11},{10,... | collective-permute-start | bytes 344072 | tf_op jit(solution)/shard_map/ppermute | solution.py:212
  56.6 6.1 %collective-permute-start.13 = (bf16[16,3584]{1,0:T(8,128)(2,1)S(1)}, bf16[16,3584]{1,0:T(8,128)(2,1)S(1)}, u32[]{:S(2)}, u32[]{:S(2)}) collective-permute-start(bf16[16,3584]{1,0:T(8,128)(2,1)S(1)} %slice.38), channel_id=1, source_target_pairs={{0,2},{1,3},{2,0},{3,1},{4,6},{5,7},{6,4},{7,5},{8,10},{9,11},{10,... | collective-permute-start | bytes 344072 | tf_op jit(solution)/shard_map/ppermute | solution.py:212

commit v4 on v2

v4 whole, which is shorter than its diff:
```python
import functools

import jax
import jax.numpy as jnp
from jax import lax
from jax.experimental import pallas as pl
from jax.experimental.pallas import tpu as pltpu
from jax.sharding import PartitionSpec as P

adapter_scale = 0.5
lane = 128
f32 = jnp.float32
bf16 = jnp.bfloat16


def general(
    tokens,
    base_up_weight,
    adapter_shrink_weight,
    adapter_expand_weight,
    row_adapter_index,
    adapter_slot_index,
):
    owner_count = lax.axis_size("adapter")
    owner_index = lax.axis_index("adapter")
    tensor_index = lax.axis_index("tensor")
    rank_block = adapter_expand_weight.shape[1]
    columns = base_up_weight.shape[1]
    slot = jnp.take(adapter_slot_index, row_adapter_index[:, 0], axis=0)
    rows = lax.all_gather(tokens, "adapter", axis=0, tiled=True)
    expand = adapter_expand_weight[0].reshape(rank_block, owner_count, columns)
    expand = lax.all_to_all(expand, "adapter", split_axis=1, concat_axis=1, tiled=True)
    shrunk = jnp.dot(rows, adapter_shrink_weight[0], preferred_element_type=f32)
    shrunk = jnp.where((slot == owner_index)[:, None], shrunk, 0.0)
    shrunk = lax.psum(shrunk, ("adapter", "tensor"))
    shrunk = (adapter_scale * shrunk).astype(bf16)
    shrunk = lax.dynamic_slice_in_dim(shrunk, tensor_index * rank_block, rank_block, 1)
    chosen = slot[:, None] == jnp.arange(owner_count, dtype=jnp.int32)[None, :]
    spread = jnp.where(chosen[:, None, :], shrunk[:, :, None], jnp.zeros((), bf16))
    total = jnp.dot(rows, base_up_weight, preferred_element_type=f32)
    total = total + jnp.dot(
        spread.reshape(-1, rank_block * owner_count),
        expand.reshape(rank_block * owner_count, columns),
        preferred_element_type=f32,
    )
    return lax.psum_scatter(total, "tensor", scatter_dimension=0, tiled=True).astype(bf16)


vmem = pl.BlockSpec(memory_space=pltpu.VMEM)
smem = pl.BlockSpec(memory_space=pltpu.SMEM)
anywhere = pl.BlockSpec(memory_space=pl.ANY)


def kernel_call(kernel, name, flops, moved, mib, **specs):
    return pl.pallas_call(
        kernel,
        cost_estimate=pl.CostEstimate(flops=flops, bytes_accessed=moved, transcendentals=0),
        compiler_params=pltpu.CompilerParams(vmem_limit_bytes=mib << 20),
        name=name,
        **specs,
    )


def cut_kernel(owner_count, offsets, far_width, expand, *refs):
    pieces, sem = refs[:-1], refs[-1]
    g, a = lax.axis_index("groups"), lax.axis_index("adapter")
    near_width = pieces[0].shape[1]
    columns = near_width + far_width
    copies = []
    for n, (j, piece) in enumerate(zip(offsets, pieces)):
        to = lax.rem(a - j + owner_count, owner_count)
        start = pl.multiple_of(to * columns + g * far_width, lane)
        copies.append(
            pltpu.make_async_copy(expand.at[0, :, pl.ds(start, near_width)], piece, sem.at[n])
        )
    for copy in copies:
        copy.start()
    for copy in copies:
        copy.wait()


def weight_copies(start, block, weight, target, sem):
    copies = []
    for n in range(target.shape[0]):
        span = pl.ds(pl.multiple_of(start + n * block, lane), block)
        copies.append(pltpu.make_async_copy(weight.at[:, span], target.at[n], sem.at[n]))
    return copies


def load_kernel(starts, counts, block, weight, expand, after, held, own, sem, own_sem):
    a = lax.axis_index("adapter")
    columns = own.shape[1]
    copies, at = [], 0
    for start_of, count in zip(starts, counts):
        span = pl.ds(at, count)
        copies += weight_copies(start_of(), block, weight, held.at[span], sem.at[span])
        at += count
    start = pl.multiple_of(a * columns, columns)
    copies.append(pltpu.make_async_copy(expand.at[0, :, pl.ds(start, columns)], own, own_sem))
    for copy in copies:
        copy.start()
    for copy in copies:
        copy.wait()


def gather_kernel(owner_count, slots, index, *refs):
    blocks = refs[:owner_count]
    shrink, _, rows_out, keep, send, rows, partial = refs[owner_count:]
    a, t = lax.axis_index("adapter"), lax.axis_index("tensor")
    height = blocks[0].shape[0]
    for j in range(owner_count):
        where = lax.rem(a + j, owner_count)
        rows[pl.ds(pl.multiple_of(where * height, height), height), :] = blocks[j][...]
    quarter = rows.shape[0] // 4
    for i, flip in enumerate((0, 2, 1, 3)):
        start = pl.multiple_of(lax.bitwise_xor(t, flip) * quarter, quarter)
        rows_out[i * quarter : (i + 1) * quarter, :] = rows[pl.ds(start, quarter), :]
    product = lax.dot_general(
        shrink[...], rows[...], (((1,), (1,)), ((), ())), preferred_element_type=f32
    )
    partial[...] = jnp.where(slot_of(index, slots) == a, product, 0.0)
    rank_block = partial.shape[0] // 4
    for i, flip in enumerate((0, 2, 1, 3)):
        start = pl.multiple_of(lax.bitwise_xor(t, flip) * rank_block, rank_block)
        target = keep if i < 2 else send
        at = i % 2 * rank_block
        target[at : at + rank_block, :] = partial[pl.ds(start, rank_block), :]


def slot_of(index, slots):
    named = index[...]
    slot = jnp.zeros_like(named)
    for k in range(slots.shape[0]):
        slot = jnp.where(named == k, slots[k], slot)
    return slot


def part_start(near_width, far_width, is_far, first):
    g = lax.axis_index("groups")
    return ((1 - g) * near_width if is_far else g * far_width) + first


def base_kernel(start_of, block, first, held_count, rows, weight, held, *refs):
    total, streamed, sem = refs[-3:]
    copies = []
    if held_count * block < total.shape[1]:
        copies = weight_copies(start_of() + held_count * block, block, weight, streamed, sem)
    for copy in copies:
        copy.start()
    for n in range(total.shape[1] // block):
        if n < held_count:
            part = held[first + n]
        else:
            copies[n - held_count].wait()
            part = streamed[n - held_count]
        total[:, n * block : (n + 1) * block] = jnp.dot(
            rows[...], part, preferred_element_type=f32
        )


def forward_kernel(owner_count, far_width, *refs):
    near, packed = refs[: owner_count - 1], refs[-1]
    height, near_width = near[0].shape
    start = pl.multiple_of(lax.axis_index("groups") * (near_width - far_width), lane)
    for n, piece in enumerate(near):
        packed[n * height : (n + 1) * height, :] = piece[:, pl.ds(start, far_width)]


def delta_kernel(owner_count, offsets, start_of, block, base_count, piece_count, slots, index, *refs):
    bases, refs = refs[:base_count], refs[base_count:]
    own, shrunk = refs[:2]
    pieces = refs[2 : 2 + piece_count]
    *outs, flat, ordered = refs[-6:]
    a, t = lax.axis_index("adapter"), lax.axis_index("tensor")
    row_count = bases[0].shape[0]
    quarter = row_count // 4
    slot = slot_of(index, slots)
    merged = shrunk[...].astype(f32)
    spread = [
        jnp.where(slot == lax.rem(a + j, owner_count), merged, 0.0) for j in (0, *offsets)
    ]
    flat[...] = jnp.concatenate(spread, axis=0).T
    for i, turn in enumerate((0, 2, 1, 3)):
        start = pl.multiple_of(lax.bitwise_xor(t, turn) * quarter, quarter)
        ordered[i * quarter : (i + 1) * quarter, :] = flat[pl.ds(start, quarter), :].astype(bf16)
    left = ordered[...]
    at = 0
    for base in bases:
        for column in range(0, base.shape[1], block):
            source = pl.multiple_of(start_of() + at, lane)
            expand = jnp.concatenate(
                [own[:, pl.ds(source, block)]] + [piece[:, at : at + block] for piece in pieces],
                axis=0,
            )
            total = base[:, column : column + block] + jnp.dot(
                left, expand, preferred_element_type=f32
            )
            for n, out in enumerate(outs):
                out[:, at : at + block] = total[n * quarter : (n + 1) * quarter]
            at += block


def column_block(width):
    for size in (512, 256, 128):
        if width % size == 0:
            return size


def paired(
    tokens,
    base_up_weight,
    adapter_shrink_weight,
    adapter_expand_weight,
    row_adapter_index,
    adapter_slot_index,
):
    owner_count = lax.axis_size("adapter")
    g = lax.axis_index("groups")
    height, depth = tokens.shape
    row_count = height * owner_count
    columns = base_up_weight.shape[1]
    rank_block = adapter_expand_weight.shape[1]
    rank = adapter_shrink_weight.shape[2]
    block = column_block(columns)
    block_count = columns // block
    near_count = max(1, block_count * 8 // 14)
    near_width = near_count * block
    far_width = columns - near_width

    def from_owner(x, j):
        return lax.ppermute(x, "adapter", [(s, (s - j) % owner_count) for s in range(owner_count)])

    def from_tensor(x, m):
        return lax.ppermute(x, "tensor", [(s, s ^ m) for s in range(4)])

    def from_mirror(x, m):
        return lax.ppermute(x, "adapter", [(s, s ^ m) for s in range(owner_count)])

    def from_group(x):
        return lax.ppermute(x, "groups", [(0, 1), (1, 0)])

    weight = pltpu.with_memory_space_constraint(base_up_weight, pltpu.HBM)
    expand = pltpu.with_memory_space_constraint(adapter_expand_weight, pltpu.HBM)
    index = row_adapter_index.reshape(1, row_count)
    others = range(1, owner_count)
    offsets = (2, 1, 3)
    blocks = [tokens] + [from_owner(tokens, j) for j in others]

    pieces = kernel_call(
        functools.partial(cut_kernel, owner_count, offsets, far_width),
        "cut_expand",
        1,
        1,
        1,
        in_specs=[anywhere],
        out_specs=[vmem] * (owner_count - 1),
        out_shape=[pltpu.VMEM((rank_block, near_width), bf16)] * (owner_count - 1),
        scratch_shapes=[pltpu.SemaphoreType.DMA((owner_count - 1,))],
    )(expand)

    def split(count):
        return [(0, count - count // 2), (count - count // 2, count // 2)]

    parts = [(False, *span) for span in split(near_count)]
    parts += [(True, *span) for span in split(block_count - near_count)]
    held_counts = [min(part[2], count) for part, count in zip(parts, (4, 2, 1, 1))]
    starts = [
        functools.partial(part_start, near_width, far_width, is_far, first * block)
        for is_far, first, _ in parts
    ]
    held, own = kernel_call(
        functools.partial(load_kernel, starts, held_counts, block),
        "load_weights",
        1,
        1,
        1,
        in_specs=[anywhere] * 3,
        out_specs=[vmem] * 2,
        out_shape=[
            pltpu.VMEM((sum(held_counts), depth, block), bf16),
            pltpu.VMEM((rank_block, columns), bf16),
        ],
        scratch_shapes=[pltpu.SemaphoreType.DMA((sum(held_counts),)), pltpu.SemaphoreType.DMA],
    )(weight, expand, pieces[0])

    near = [from_owner(pieces[0], offsets[0])]
    *late, own = lax.optimization_barrier((*pieces[1:], own))
    near += [from_owner(piece, j) for piece, j in zip(late, offsets[1:])]
    rows, keep, send = kernel_call(
        functools.partial(gather_kernel, owner_count),
        "gather_rows",
        1,
        1,
        4,
        in_specs=[smem, vmem] + [vmem] * (owner_count + 1) + [anywhere],
        out_specs=[vmem] * 3,
        out_shape=[jax.ShapeDtypeStruct((row_count, depth), bf16)]
        + [jax.ShapeDtypeStruct((rank // 2, row_count), f32)] * 2,
        scratch_shapes=[pltpu.VMEM((row_count, depth), bf16), pltpu.VMEM((rank, row_count), f32)],
    )(adapter_slot_index, index, *blocks, adapter_shrink_weight[0].T, own)

    def base_part(n, *after):
        is_far, first, count = parts[n]
        stream_count = max(1, count - held_counts[n])
        return kernel_call(
            functools.partial(base_kernel, starts[n], block, sum(held_counts[:n]), held_counts[n]),
            "base_part",
            1 if is_far else 2 * row_count * depth * count * block,
            1 if is_far else 2 * depth * count * block,
            4 + (stream_count * depth * block * 2 >> 20),
            in_specs=[vmem, anywhere, vmem] + [anywhere] * len(after),
            out_specs=vmem,
            out_shape=jax.ShapeDtypeStruct((row_count, count * block), f32),
            scratch_shapes=[
                pltpu.VMEM((stream_count, depth, block), bf16),
                pltpu.SemaphoreType.DMA((stream_count,)),
            ],
        )(rows, weight, held, *after)

    def delta_part(is_far, bases, pieces, shrunk):
        start_of = functools.partial(part_start, near_width, far_width, is_far, 0)
        width = sum(base.shape[1] for base in bases)
        return kernel_call(
            functools.partial(
                delta_kernel, owner_count, offsets, start_of, block, len(bases), len(pieces)
            ),
            "delta_part",
            1,
            1,
            8,
            in_specs=[smem] + [vmem] * (3 + len(bases) + len(pieces)),
            out_specs=[vmem] * 4,
            out_shape=[jax.ShapeDtypeStruct((row_count // 4, width), f32)] * 4,
            scratch_shapes=[
                pltpu.VMEM((row_count, rank_block * owner_count), f32),
                pltpu.VMEM((row_count, rank_block * owner_count), bf16),
            ],
        )(adapter_slot_index, index, *bases, own, shrunk, *pieces)

    arrived = from_tensor(send, 1)
    base_0 = base_part(0, send)
    arrived, base_0 = lax.optimization_barrier((arrived, base_0))
    pair = keep + arrived
    arrived = from_tensor(pair[rank_block:], 2)
    base_1 = base_part(1, pair)
    arrived, base_1, *near = lax.optimization_barrier((arrived, base_1, *near))
    shrunk = (adapter_scale * (pair[:rank_block] + arrived)).astype(bf16)
    packed = kernel_call(
        functools.partial(forward_kernel, owner_count, far_width),
        "pack_far",
        1,
        1,
        2,
        in_specs=[vmem] * (owner_count - 1),
        out_specs=vmem,
        out_shape=jax.ShapeDtypeStruct(((owner_count - 1) * rank_block, far_width), bf16),
    )(*near)
    far = from_group(packed)
    steps = []
    m = 1
    while m < owner_count:
        steps.append(m)
        m *= 2
    base_far = []
    for m, n in zip(steps, (2, 3)):
        arrived = from_mirror(shrunk, m)
        base = base_part(n, shrunk, packed)
        arrived, base = lax.optimization_barrier((arrived, base))
        base_far.append(base)
        shrunk = shrunk + arrived

    halves = []
    for is_far, bases, pieces in ((False, [base_0, base_1], near), (True, base_far, [far])):
        own_keep, cross_keep, own_send, cross_send = delta_part(is_far, bases, pieces, shrunk)
        cross = cross_keep + from_tensor(cross_send, 1)
        kept = own_keep + from_tensor(own_send, 1)
        crossed = from_tensor(cross.astype(bf16), 2)
        halves.append((kept + crossed.astype(f32)).astype(bf16))
    first = jnp.concatenate(halves, axis=1)
    second = jnp.concatenate(halves[::-1], axis=1)
    return jnp.where(g == 0, first, second)


def on_device(tokens, base_up_weight, adapter_shrink_weight, adapter_expand_weight, *index):
    pairs = lax.axis_size("groups") == 2 and lax.axis_size("tensor") == 4
    few = lax.axis_size("adapter") == 4
    even = base_up_weight.shape[1] % (2 * lane) == 0 and tokens.shape[0] % 16 == 0
    arrange = paired if pairs and few and even else general
    return arrange(
        tokens, base_up_weight, adapter_shrink_weight, adapter_expand_weight, *index
    )


def solution(mesh):
    placed = (
        P(("groups", "adapter"), "tensor"),
        P("tensor", "adapter"),
        P("adapter", "tensor", None),
        P("adapter", "tensor", None),
        P("groups", None),
        P(),
    )
    return jax.shard_map(
        on_device,
        mesh=mesh,
        in_specs=placed,
        out_specs=P(("groups", "tensor"), "adapter"),
        check_vma=False,
    )
```

time: 56.8 us -> 50.6 us (0.89)
  waiting for transfers between devices: 17.3 us -> 9.24 us
  Pallas kernels: 18.9 us -> 20.9 us
    ppermute x9 -> x6, waiting for transfers between devices: 10.9 us -> 3.62 us  [from_owner(): lax.ppermute(x, 'adapter', [(s, (s - j) % owner_count) for s in range(own...]
    ppermute x0 -> x2, starting transfers between devices: none -> 2.34 us  [from_mirror(): return lax.ppermute(x, 'adapter', [(s, s ^ m) for s in range(owner_count)])]
    pallas_call x6 -> x9, Pallas kernels: 18.1 us -> 20.1 us  [the longest x4 11.1 us: base_part(): kernel_call(functools.partial(base_kernel, starts[n], block, sum(held_cou...]
    ppermute x3 -> x1, starting transfers between devices: 3.55 us -> 1.58 us  [from_group(): return lax.ppermute(x, 'groups', [(0, 1), (1, 0)])]
    ppermute x7 -> x8, waiting for transfers between devices: 6.36 us -> 5.07 us  [from_tensor(): return lax.ppermute(x, 'tensor', [(s, s ^ m) for s in range(4)])]
    ppermute x9 -> x6, starting transfers between devices: 11.1 us -> 10.1 us  [from_owner(): lax.ppermute(x, 'adapter', [(s, (s - j) % owner_count) for s in range(own...]
    concatenate x1 -> x0, other arithmetic: 0.7 us -> none  [paired(): return jnp.concatenate([first, second], axis=1)]
    select_n x1, other arithmetic: 0.06 us -> 0.75 us  [paired(): return jnp.where(g == 0, first, second)]
  transfers between devices with their start and end apart: 19 -> 17, of which waited for: 7 -> 4; matrix products, arithmetic and copies ran while one was open for 0% -> 0% of each run, Pallas kernels for 33% -> 41%
where the time goes in v4:
time: 50.6 us; the launch traced here: 50.5 us
  Pallas kernels  20.9 us (41%)
  starting transfers between devices  19.3 us (38%)
  waiting for transfers between devices  9.24 us (18%)
  other arithmetic  0.9 us (2%)
    pallas_call x4, Pallas kernels, base_part(): kernel_call(functools.partial(base_kernel, starts[n], block, sum(held_cou...  11.1 us
    ppermute x6, starting transfers between devices, from_owner(): lax.ppermute(x, 'adapter', [(s, (s - j) % owner_count) for s in range(own...  10.1 us
    pallas_call x1, Pallas kernels, paired(): kernel_call(functools.partial(load_kernel, starts, held_counts, block), '...  6.06 us
    ppermute x8, starting transfers between devices, from_tensor(): return lax.ppermute(x, 'tensor', [(s, s ^ m) for s in range(4)])  5.21 us
    ppermute x8, waiting for transfers between devices, from_tensor(): return lax.ppermute(x, 'tensor', [(s, s ^ m) for s in range(4)])  5.07 us
    ppermute x6, waiting for transfers between devices, from_owner(): lax.ppermute(x, 'adapter', [(s, (s - j) % owner_count) for s in range(own...  3.62 us
    ppermute x2, starting transfers between devices, from_mirror(): return lax.ppermute(x, 'adapter', [(s, s ^ m) for s in range(owner_count)])  2.34 us
    pallas_call x2, Pallas kernels, delta_part(): kernel_call(functools.partial(delta_kernel, owner_count, offsets, start_o...  1.8 us
  transfers between devices with their start and end apart: 17, of which 4 were waited for; matrix products, arithmetic and copies ran while one was open for 0% of the time, Pallas kernels for 41%

profile of v4, /device:TPU:0, one launch (start us, length us, event | category | flops | bytes accessed | tf_op | source)
XLA Modules:
  0.0 50.5 jit_solution(3676749897725699037)
XLA Ops:
  0.0 5.1 %collective-permute-start = (bf16[16,2048]{1,0:T(8,128)(2,1)}, bf16[16,2048]{1,0:T(8,128)(2,1)S(1)}, u32[]{:S(2)}, u32[]{:S(2)}) collective-permute-start(bf16[16,2048]{1,0:T(8,128)(2,1)} %refs_0_.1), channel_id=1, source_target_pairs={{0,12},{4,0},{8,4},{12,8},{1,13},{5,1},{9,5},{13,9},{2,14},{6,2},{... | collective-permute-start | bytes 196616 | tf_op jit(solution)/shard_map/ppermute | solution.py:231
  5.1 0.0 collective-permute-start.1
  5.1 1.0 %collective-permute-start.2 = (bf16[16,2048]{1,0:T(8,128)(2,1)}, bf16[16,2048]{1,0:T(8,128)(2,1)S(1)}, u32[]{:S(2)}, u32[]{:S(2)}) collective-permute-start(bf16[16,2048]{1,0:T(8,128)(2,1)} %refs_0_.1), channel_id=1, source_target_pairs={{0,4},{4,8},{8,12},{12,0},{1,5},{5,9},{9,13},{13,1},{2,6},{6,10},{... | collective-permute-start | bytes 196616 | tf_op jit(solution)/shard_map/ppermute | solution.py:231
  6.1 1.1 %cut_expand.1 = (bf16[16,4096]{1,0:T(8,128)(2,1)S(1)}, bf16[16,4096]{1,0:T(8,128)(2,1)S(1)}, bf16[16,4096]{1,0:T(8,128)(2,1)S(1)}) custom-call(bf16[1,16,28672]{2,1,0:T(8,128)(2,1)} %expand.3), custom_call_target="tpu_custom_call" | custom-call | flops 1 | bytes 1 | tf_op jit(solution)/shard_map/cut_expand/pallas_call | solution.py:249
  7.2 6.1 %load_weights.1 = (bf16[8,2048,512]{2,1,0:T(8,128)(2,1)S(1)}, bf16[16,7168]{1,0:T(8,128)(2,1)S(1)}) custom-call(bf16[2048,7168]{1,0:T(8,128)(2,1)} %weight.9, bf16[1,16,28672]{2,1,0:T(8,128)(2,1)} %expand.3, bf16[16,4096]{1,0:T(8,128)(2,1)S(1)} %get-tuple-element.37.after), custom_call_target="tpu_custom_call" | custom-call | flops 1 | bytes 1 | tf_op jit(solution)/shard_map/load_weights/pallas_call | solution.py:271
  13.3 2.9 %collective-permute-start.6 = (bf16[16,4096]{1,0:T(8,128)(2,1)S(1)}, bf16[16,4096]{1,0:T(8,128)(2,1)S(1)}, u32[]{:S(2)}, u32[]{:S(2)}) collective-permute-start(bf16[16,4096]{1,0:T(8,128)(2,1)S(1)} %get-tuple-element.46), channel_id=1, source_target_pairs={{0,12},{4,0},{8,4},{12,8},{1,13},{5,1},{9,5},{13,9},{2,14},{6,2},{... | collective-permute-start | bytes 393224 | tf_op jit(solution)/shard_map/ppermute | solution.py:231
  16.1 0.0 collective-permute-start.7
  16.1 0.0 collective-permute-done.refs_1_
  16.1 1.1 %collective-permute-start.5 = (bf16[16,4096]{1,0:T(8,128)(2,1)S(1)}, bf16[16,4096]{1,0:T(8,128)(2,1)S(1)}, u32[]{:S(2)}, u32[]{:S(2)}) collective-permute-start(bf16[16,4096]{1,0:T(8,128)(2,1)S(1)} %get-tuple-element.37.after), channel_id=1, source_target_pairs={{0,8},{4,12},{8,0},{12,4},{1,9},{5,13},{9,1},{13,5},{2,10},{6,14},... | collective-permute-start | bytes 393224 | tf_op jit(solution)/shard_map/ppermute | solution.py:231
  17.3 0.0 collective-permute-done.1.refs_2_
  17.3 0.0 collective-permute-done.2.refs_3_
  17.3 0.0 copy-done.1
  17.3 0.0 copy-done.3
  17.3 0.0 copy-done
  17.3 0.0 copy-done.2
  17.3 0.8 %gather_rows.1 = (bf16[64,2048]{1,0:T(8,128)(2,1)S(1)}, f32[32,64]{1,0:T(8,128)S(1)}, f32[32,64]{1,0:T(8,128)S(1)}) custom-call(s32[4]{0:T(128)S(1)} %copy-done.2, s32[1,64]{1,0:T(1,128)S(1)} %bitcast.5, bf16[16,2048]{1,0:T(8,128)(2,1)S(1)} %copy-done.1, bf16[16,2048]{1,0:T(8,128)(2,1)S(1)} %collective-permute-done.refs_1_, ...), custom_call_target="tpu_custom_call" | custom-call | flops 1 | bytes 1 | tf_op jit(solution)/shard_map/gather_rows/pallas_call | solution.py:289
  18.1 0.1 collective-permute-start.3
  18.2 1.6 %base_part.4.refs_0_ = f32[64,2048]{1,0:T(8,128)S(1)} custom-call(bf16[64,2048]{1,0:T(8,128)(2,1)S(1)} %get-tuple-element.41.rows, bf16[2048,7168]{1,0:T(8,128)(2,1)} %weight.9, bf16[8,2048,512]{2,1,0:T(8,128)(2,1)S(1)} %get-tuple-element.42.held, f32[32,64]{1,0:T(8,128)S(1)} %get-tuple-element.40.refs_0_), custom_call_target="tpu_custom_call" | custom-call | flops 536870912 | bytes 8388608 | tf_op jit(solution)/shard_map/base_part/pallas_call | solution.py:305
  19.8 0.0 collective-permute-done.3
  19.8 1.6 %collective-permute-start.4 = (f32[16,64]{1,0:T(8,128)S(1)}, f32[16,64]{1,0:T(8,128)S(1)}, u32[]{:S(2)}, u32[]{:S(2)}) collective-permute-start(f32[16,64]{1,0:T(8,128)S(1)} %slice.8), channel_id=1, source_target_pairs={{0,2},{1,3},{2,0},{3,1},{4,6},{5,7},{6,4},{7,5},{8,10},{9,11},{10,... | collective-permute-start | bytes 12296 | tf_op jit(solution)/shard_map/ppermute | solution.py:234
  21.4 3.4 %base_part.5.refs_1_ = f32[64,2048]{1,0:T(8,128)S(1)} custom-call(bf16[64,2048]{1,0:T(8,128)(2,1)S(1)} %get-tuple-element.41.rows, bf16[2048,7168]{1,0:T(8,128)(2,1)} %weight.9, bf16[8,2048,512]{2,1,0:T(8,128)(2,1)S(1)} %get-tuple-element.42.held, f32[32,64]{1,0:T(8,128)S(1)} %add.30.refs_0_), custom_call_target="tpu_custom_call" | custom-call | flops 536870912 | bytes 8388608 | tf_op jit(solution)/shard_map/base_part/pallas_call | solution.py:305
  24.8 0.0 collective-permute-done.4
  24.8 0.0 collective-permute-done.6.refs_1_.refs_5_
  24.8 0.0 collective-permute-done.7.refs_2_.refs_6_
  24.9 3.6 %collective-permute-done.5.refs_0_.refs_4_ = bf16[16,4096]{1,0:T(8,128)(2,1)S(1)} collective-permute-done((bf16[16,4096]{1,0:T(8,128)(2,1)S(1)}, bf16[16,4096]{1,0:T(8,128)(2,1)S(1)}, u32[]{:S(2)}, u32[]{:S(2)}) %collective-permute-start.5) | collective-permute-done | bytes 131104 | tf_op jit(solution)/shard_map/ppermute | solution.py:231
  28.5 1.6 %collective-permute-start.13 = (bf16[48,3072]{1,0:T(8,128)(2,1)S(1)}, bf16[48,3072]{1,0:T(8,128)(2,1)S(1)}, u32[]{:S(2)}, u32[]{:S(2)}) collective-permute-start(bf16[48,3072]{1,0:T(8,128)(2,1)S(1)} %pack_far.1.refs_1_), channel_id=1, source_target_pairs={{0,16},{16,0},{1,17},{17,1},{2,18},{18,2},{3,19},{19,3},{4,20},{20... | collective-permute-start | bytes 884744 | tf_op jit(solution)/shard_map/ppermute | solution.py:240
  30.1 0.0 collective-permute-start.8
  30.1 3.1 %base_part.6.refs_0_ = f32[64,1536]{1,0:T(8,128)S(1)} custom-call(bf16[64,2048]{1,0:T(8,128)(2,1)S(1)} %get-tuple-element.41.rows, bf16[2048,7168]{1,0:T(8,128)(2,1)} %weight.9, bf16[8,2048,512]{2,1,0:T(8,128)(2,1)S(1)} %get-tuple-element.42.held, bf16[16,64]{1,0:T(8,128)(2,1)S(1)} %fusion.1.refs_0_, bf16[48,3072]{1,0:T(8,128)(2,1)S(1)} %pack_far.1.refs_1_), custom_call_target="tpu_custom_call" | custom-call | flops 1 | bytes 1 | tf_op jit(solution)/shard_map/base_part/pallas_call | solution.py:305
  33.1 0.5 %collective-permute-done.8 = bf16[16,64]{1,0:T(8,128)(2,1)S(1)} collective-permute-done((bf16[16,64]{1,0:T(8,128)(2,1)S(1)}, bf16[16,64]{1,0:T(8,128)(2,1)S(1)}, u32[]{:S(2)}, u32[]{:S(2)}) %collective-permute-start.8) | collective-permute-done | bytes 2080 | tf_op jit(solution)/shard_map/ppermute | solution.py:237
  33.7 2.3 %collective-permute-start.9 = (bf16[16,64]{1,0:T(8,128)(2,1)S(1)}, bf16[16,64]{1,0:T(8,128)(2,1)S(1)}, u32[]{:S(2)}, u32[]{:S(2)}) collective-permute-start(bf16[16,64]{1,0:T(8,128)(2,1)S(1)} %add.32.refs_0_), channel_id=1, source_target_pairs={{0,8},{4,12},{8,0},{12,4},{1,9},{5,13},{9,1},{13,5},{2,10},{6,14},... | collective-permute-start | bytes 6152 | tf_op jit(solution)/shard_map/ppermute | solution.py:237
  36.0 3.0 %base_part.7.refs_1_ = f32[64,1536]{1,0:T(8,128)S(1)} custom-call(bf16[64,2048]{1,0:T(8,128)(2,1)S(1)} %get-tuple-element.41.rows, bf16[2048,7168]{1,0:T(8,128)(2,1)} %weight.9, bf16[8,2048,512]{2,1,0:T(8,128)(2,1)S(1)} %get-tuple-element.42.held, bf16[16,64]{1,0:T(8,128)(2,1)S(1)} %add.32.refs_0_, bf16[48,3072]{1,0:T(8,128)(2,1)S(1)} %pack_far.1.refs_1_), custom_call_target="tpu_custom_call" | custom-call | flops 1 | bytes 1 | tf_op jit(solution)/shard_map/base_part/pallas_call | solution.py:305
  39.1 0.0 collective-permute-done.9
  39.1 0.9 %delta_part.2 = (f32[16,4096]{1,0:T(8,128)S(1)}, f32[16,4096]{1,0:T(8,128)S(1)}, f32[16,4096]{1,0:T(8,128)S(1)}, f32[16,4096]{1,0:T(8,128)S(1)}) custom-call(s32[4]{0:T(128)S(1)} %copy-done.2, s32[1,64]{1,0:T(1,128)S(1)} %bitcast.6, f32[64,2048]{1,0:T(8,128)S(1)} %base_part.4.refs_0_, f32[64,2048]{1,0:T(8,128)S(1)} %base_part.5.refs_1_, ...), custom_call_target="tpu_custom_call" | custom-call | flops 1 | bytes 1 | tf_op jit(solution)/shard_map/delta_part/pallas_call | solution.py:323
  40.0 0.1 collective-permute-start.11
  40.1 0.5 collective-permute-start.10
  40.6 0.0 collective-permute-done.13.refs_4_
  40.6 0.9 %delta_part.3 = (f32[16,3072]{1,0:T(8,128)S(1)}, f32[16,3072]{1,0:T(8,128)S(1)}, f32[16,3072]{1,0:T(8,128)S(1)}, f32[16,3072]{1,0:T(8,128)S(1)}) custom-call(s32[4]{0:T(128)S(1)} %copy-done.2, s32[1,64]{1,0:T(1,128)S(1)} %bitcast.7, f32[64,1536]{1,0:T(8,128)S(1)} %base_part.6.refs_0_, f32[64,1536]{1,0:T(8,128)S(1)} %base_part.7.refs_1_, ...), custom_call_target="tpu_custom_call" | custom-call | flops 1 | bytes 1 | tf_op jit(solution)/shard_map/delta_part/pallas_call | solution.py:323
  41.5 0.2 collective-permute-start.15
  41.7 0.0 collective-permute-done.11
  41.7 1.6 %collective-permute-start.12 = (bf16[16,4096]{1,0:T(8,128)(2,1)S(1)}, bf16[16,4096]{1,0:T(8,128)(2,1)S(1)}, u32[]{:S(2)}, u32[]{:S(2)}) collective-permute-start(bf16[16,4096]{1,0:T(8,128)(2,1)S(1)} %add_convert_fusion.1), channel_id=1, source_target_pairs={{0,2},{1,3},{2,0},{3,1},{4,6},{5,7},{6,4},{7,5},{8,10},{9,11},{10,... | collective-permute-start | bytes 393224 | tf_op jit(solution)/shard_map/ppermute | solution.py:234
  43.3 0.2 collective-permute-start.14
  43.4 0.0 collective-permute-done.15
  43.4 1.2 %collective-permute-start.16 = (bf16[16,3072]{1,0:T(8,128)(2,1)S(1)}, bf16[16,3072]{1,0:T(8,128)(2,1)S(1)}, u32[]{:S(2)}, u32[]{:S(2)}) collective-permute-start(bf16[16,3072]{1,0:T(8,128)(2,1)S(1)} %add_convert_fusion.3), channel_id=1, source_target_pairs={{0,2},{1,3},{2,0},{3,1},{4,6},{5,7},{6,4},{7,5},{8,10},{9,11},{10,... | collective-permute-start | bytes 294920 | tf_op jit(solution)/shard_map/ppermute | solution.py:234
  44.6 0.0 collective-permute-done.10
  44.6 3.5 %collective-permute-done.12 = bf16[16,4096]{1,0:T(8,128)(2,1)S(1)} collective-permute-done((bf16[16,4096]{1,0:T(8,128)(2,1)S(1)}, bf16[16,4096]{1,0:T(8,128)(2,1)S(1)}, u32[]{:S(2)}, u32[]{:S(2)}) %collective-permute-start.12) | collective-permute-done | bytes 131104 | tf_op jit(solution)/shard_map/ppermute | solution.py:234
  48.1 0.0 collective-permute-done.14
  48.1 1.6 %collective-permute-done.16 = bf16[16,3072]{1,0:T(8,128)(2,1)S(1)} collective-permute-done((bf16[16,3072]{1,0:T(8,128)(2,1)S(1)}, bf16[16,3072]{1,0:T(8,128)(2,1)S(1)}, u32[]{:S(2)}, u32[]{:S(2)}) %collective-permute-start.16) | collective-permute-done | bytes 98336 | tf_op jit(solution)/shard_map/ppermute | solution.py:234
  49.7 0.7 %maximum_select_fusion = bf16[16,7168]{1,0:T(8,128)(2,1)} fusion(bf16[16,3072]{1,0:T(8,128)(2,1)S(1)} %add_convert_fusion.2, bf16[16,4096]{1,0:T(8,128)(2,1)S(1)} %add_convert_fusion, pred[]{:T(512)S(6)} %eq.3), kind=kLoop, calls=%fused_computation.2 | loop fusion | flops 1032192 | bytes 458753 | tf_op jit(solution)/shard_map/jit(_where)/select_n | solution.py:381
  (14 shorter events, 0.2 us)
Async XLA Ops:
  0.0 17.3 %copy-start.1 = (bf16[16,2048]{1,0:T(8,128)(2,1)S(1)}, bf16[16,2048]{1,0:T(8,128)(2,1)}, u32[]{:S(2)}) copy-start(bf16[16,2048]{1,0:T(8,128)(2,1)} %refs_0_.1) | copy-start | bytes 196612
  0.0 17.3 %copy-start.3 = (s32[64,1]{0,1:T(1,128)S(1)}, s32[64,1]{0,1:T(1,128)}, u32[]{:S(2)}) copy-start(s32[64,1]{0,1:T(1,128)} %param.10) | copy-start | bytes 772
  0.0 17.3 %copy-start = (bf16[1,2048,64]{1,2,0:T(8,128)(2,1)S(1)}, bf16[1,2048,64]{1,2,0:T(8,128)(2,1)}, u32[]{:S(2)}) copy-start(bf16[1,2048,64]{1,2,0:T(8,128)(2,1)} %param.8) | copy-start | bytes 786436
  0.0 17.3 %copy-start.2 = (s32[4]{0:T(128)S(1)}, s32[4]{0:T(128)}, u32[]{:S(2)}) copy-start(s32[4]{0:T(128)} %slots.5) | copy-start | bytes 52
  0.0 16.1 %collective-permute-start = (bf16[16,2048]{1,0:T(8,128)(2,1)}, bf16[16,2048]{1,0:T(8,128)(2,1)S(1)}, u32[]{:S(2)}, u32[]{:S(2)}) collective-permute-start(bf16[16,2048]{1,0:T(8,128)(2,1)} %refs_0_.1), channel_id=1, source_target_pairs={{0,12},{4,0},{8,4},{12,8},{1,13},{5,1},{9,5},{13,9},{2,14},{6,2},{... | collective-permute-start | bytes 196616 | tf_op jit(solution)/shard_map/ppermute | solution.py:231
  5.1 12.1 %collective-permute-start.1 = (bf16[16,2048]{1,0:T(8,128)(2,1)}, bf16[16,2048]{1,0:T(8,128)(2,1)S(1)}, u32[]{:S(2)}, u32[]{:S(2)}) collective-permute-start(bf16[16,2048]{1,0:T(8,128)(2,1)} %refs_0_.1), channel_id=1, source_target_pairs={{0,8},{4,12},{8,0},{12,4},{1,9},{5,13},{9,1},{13,5},{2,10},{6,14},... | collective-permute-start | bytes 196616 | tf_op jit(solution)/shard_map/ppermute | solution.py:231
  5.1 12.1 %collective-permute-start.2 = (bf16[16,2048]{1,0:T(8,128)(2,1)}, bf16[16,2048]{1,0:T(8,128)(2,1)S(1)}, u32[]{:S(2)}, u32[]{:S(2)}) collective-permute-start(bf16[16,2048]{1,0:T(8,128)(2,1)} %refs_0_.1), channel_id=1, source_target_pairs={{0,4},{4,8},{8,12},{12,0},{1,5},{5,9},{9,13},{13,1},{2,6},{6,10},{... | collective-permute-start | bytes 196616 | tf_op jit(solution)/shard_map/ppermute | solution.py:231
  13.3 11.6 %collective-permute-start.6 = (bf16[16,4096]{1,0:T(8,128)(2,1)S(1)}, bf16[16,4096]{1,0:T(8,128)(2,1)S(1)}, u32[]{:S(2)}, u32[]{:S(2)}) collective-permute-start(bf16[16,4096]{1,0:T(8,128)(2,1)S(1)} %get-tuple-element.46), channel_id=1, source_target_pairs={{0,12},{4,0},{8,4},{12,8},{1,13},{5,1},{9,5},{13,9},{2,14},{6,2},{... | collective-permute-start | bytes 393224 | tf_op jit(solution)/shard_map/ppermute | solution.py:231
  16.1 8.7 %collective-permute-start.7 = (bf16[16,4096]{1,0:T(8,128)(2,1)S(1)}, bf16[16,4096]{1,0:T(8,128)(2,1)S(1)}, u32[]{:S(2)}, u32[]{:S(2)}) collective-permute-start(bf16[16,4096]{1,0:T(8,128)(2,1)S(1)} %get-tuple-element.47), channel_id=1, source_target_pairs={{0,4},{4,8},{8,12},{12,0},{1,5},{5,9},{9,13},{13,1},{2,6},{6,10},{... | collective-permute-start | bytes 393224 | tf_op jit(solution)/shard_map/ppermute | solution.py:231
  16.1 12.3 %collective-permute-start.5 = (bf16[16,4096]{1,0:T(8,128)(2,1)S(1)}, bf16[16,4096]{1,0:T(8,128)(2,1)S(1)}, u32[]{:S(2)}, u32[]{:S(2)}) collective-permute-start(bf16[16,4096]{1,0:T(8,128)(2,1)S(1)} %get-tuple-element.37.after), channel_id=1, source_target_pairs={{0,8},{4,12},{8,0},{12,4},{1,9},{5,13},{9,1},{13,5},{2,10},{6,14},... | collective-permute-start | bytes 393224 | tf_op jit(solution)/shard_map/ppermute | solution.py:231
  18.1 1.7 %collective-permute-start.3 = (f32[32,64]{1,0:T(8,128)S(1)}, f32[32,64]{1,0:T(8,128)S(1)}, u32[]{:S(2)}, u32[]{:S(2)}) collective-permute-start(f32[32,64]{1,0:T(8,128)S(1)} %get-tuple-element.40.refs_0_), channel_id=1, source_target_pairs={{0,1},{1,0},{2,3},{3,2},{4,5},{5,4},{6,7},{7,6},{8,9},{9,8},{10,11... | collective-permute-start | bytes 24584 | tf_op jit(solution)/shard_map/ppermute | solution.py:234
  19.8 5.0 %collective-permute-start.4 = (f32[16,64]{1,0:T(8,128)S(1)}, f32[16,64]{1,0:T(8,128)S(1)}, u32[]{:S(2)}, u32[]{:S(2)}) collective-permute-start(f32[16,64]{1,0:T(8,128)S(1)} %slice.8), channel_id=1, source_target_pairs={{0,2},{1,3},{2,0},{3,1},{4,6},{5,7},{6,4},{7,5},{8,10},{9,11},{10,... | collective-permute-start | bytes 12296 | tf_op jit(solution)/shard_map/ppermute | solution.py:234
  28.5 12.1 %collective-permute-start.13 = (bf16[48,3072]{1,0:T(8,128)(2,1)S(1)}, bf16[48,3072]{1,0:T(8,128)(2,1)S(1)}, u32[]{:S(2)}, u32[]{:S(2)}) collective-permute-start(bf16[48,3072]{1,0:T(8,128)(2,1)S(1)} %pack_far.1.refs_1_), channel_id=1, source_target_pairs={{0,16},{16,0},{1,17},{17,1},{2,18},{18,2},{3,19},{19,3},{4,20},{20... | collective-permute-start | bytes 884744 | tf_op jit(solution)/shard_map/ppermute | solution.py:240
  30.1 3.6 %collective-permute-start.8 = (bf16[16,64]{1,0:T(8,128)(2,1)S(1)}, bf16[16,64]{1,0:T(8,128)(2,1)S(1)}, u32[]{:S(2)}, u32[]{:S(2)}) collective-permute-start(bf16[16,64]{1,0:T(8,128)(2,1)S(1)} %fusion.1.refs_0_), channel_id=1, source_target_pairs={{0,4},{4,0},{8,12},{12,8},{1,5},{5,1},{9,13},{13,9},{2,6},{6,2},{1... | collective-permute-start | bytes 6152 | tf_op jit(solution)/shard_map/ppermute | solution.py:237
  33.7 5.4 %collective-permute-start.9 = (bf16[16,64]{1,0:T(8,128)(2,1)S(1)}, bf16[16,64]{1,0:T(8,128)(2,1)S(1)}, u32[]{:S(2)}, u32[]{:S(2)}) collective-permute-start(bf16[16,64]{1,0:T(8,128)(2,1)S(1)} %add.32.refs_0_), channel_id=1, source_target_pairs={{0,8},{4,12},{8,0},{12,4},{1,9},{5,13},{9,1},{13,5},{2,10},{6,14},... | collective-permute-start | bytes 6152 | tf_op jit(solution)/shard_map/ppermute | solution.py:237
  40.0 1.6 %collective-permute-start.11 = (f32[16,4096]{1,0:T(8,128)S(1)}, f32[16,4096]{1,0:T(8,128)S(1)}, u32[]{:S(2)}, u32[]{:S(2)}) collective-permute-start(f32[16,4096]{1,0:T(8,128)S(1)} %get-tuple-element.58), channel_id=1, source_target_pairs={{0,1},{1,0},{2,3},{3,2},{4,5},{5,4},{6,7},{7,6},{8,9},{9,8},{10,11... | collective-permute-start | bytes 786440 | tf_op jit(solution)/shard_map/ppermute | solution.py:234
  40.1 4.5 %collective-permute-start.10 = (f32[16,4096]{1,0:T(8,128)S(1)}, f32[16,4096]{1,0:T(8,128)S(1)}, u32[]{:S(2)}, u32[]{:S(2)}) collective-permute-start(f32[16,4096]{1,0:T(8,128)S(1)} %get-tuple-element.56), channel_id=1, source_target_pairs={{0,1},{1,0},{2,3},{3,2},{4,5},{5,4},{6,7},{7,6},{8,9},{9,8},{10,11... | collective-permute-start | bytes 786440 | tf_op jit(solution)/shard_map/ppermute | solution.py:234
  41.5 1.9 %collective-permute-start.15 = (f32[16,3072]{1,0:T(8,128)S(1)}, f32[16,3072]{1,0:T(8,128)S(1)}, u32[]{:S(2)}, u32[]{:S(2)}) collective-permute-start(f32[16,3072]{1,0:T(8,128)S(1)} %get-tuple-element.64), channel_id=1, source_target_pairs={{0,1},{1,0},{2,3},{3,2},{4,5},{5,4},{6,7},{7,6},{8,9},{9,8},{10,11... | collective-permute-start | bytes 589832 | tf_op jit(solution)/shard_map/ppermute | solution.py:234
  41.7 6.4 %collective-permute-start.12 = (bf16[16,4096]{1,0:T(8,128)(2,1)S(1)}, bf16[16,4096]{1,0:T(8,128)(2,1)S(1)}, u32[]{:S(2)}, u32[]{:S(2)}) collective-permute-start(bf16[16,4096]{1,0:T(8,128)(2,1)S(1)} %add_convert_fusion.1), channel_id=1, source_target_pairs={{0,2},{1,3},{2,0},{3,1},{4,6},{5,7},{6,4},{7,5},{8,10},{9,11},{10,... | collective-permute-start | bytes 393224 | tf_op jit(solution)/shard_map/ppermute | solution.py:234
  43.3 4.9 %collective-permute-start.14 = (f32[16,3072]{1,0:T(8,128)S(1)}, f32[16,3072]{1,0:T(8,128)S(1)}, u32[]{:S(2)}, u32[]{:S(2)}) collective-permute-start(f32[16,3072]{1,0:T(8,128)S(1)} %get-tuple-element.62), channel_id=1, source_target_pairs={{0,1},{1,0},{2,3},{3,2},{4,5},{5,4},{6,7},{7,6},{8,9},{9,8},{10,11... | collective-permute-start | bytes 589832 | tf_op jit(solution)/shard_map/ppermute | solution.py:234
  43.4 6.3 %collective-permute-start.16 = (bf16[16,3072]{1,0:T(8,128)(2,1)S(1)}, bf16[16,3072]{1,0:T(8,128)(2,1)S(1)}, u32[]{:S(2)}, u32[]{:S(2)}) collective-permute-start(bf16[16,3072]{1,0:T(8,128)(2,1)S(1)} %add_convert_fusion.3), channel_id=1, source_target_pairs={{0,2},{1,3},{2,0},{3,1},{4,6},{5,7},{6,4},{7,5},{8,10},{9,11},{10,... | collective-permute-start | bytes 294920 | tf_op jit(solution)/shard_map/ppermute | solution.py:234

commit v5 on v4

--- a/solution.py
+++ b/solution.py
@@ -47,7 +47,6 @@
 
 
 vmem = pl.BlockSpec(memory_space=pltpu.VMEM)
-smem = pl.BlockSpec(memory_space=pltpu.SMEM)
 anywhere = pl.BlockSpec(memory_space=pl.ANY)
 
 
@@ -61,17 +60,19 @@
     )
 
 
-def cut_kernel(owner_count, offsets, far_width, expand, *refs):
+def cut_kernel(owner_count, offsets, far_width, tokens, expand, *refs):
     pieces, sem = refs[:-1], refs[-1]
     g, a = lax.axis_index("groups"), lax.axis_index("adapter")
-    near_width = pieces[0].shape[1]
+    depth = tokens.shape[1]
+    near_width = pieces[-1].shape[1]
     columns = near_width + far_width
-    copies = []
+    copies = [pltpu.make_async_copy(tokens, pieces[0].at[:, pl.ds(0, depth)], sem.at[len(pieces)])]
     for n, (j, piece) in enumerate(zip(offsets, pieces)):
         to = lax.rem(a - j + owner_count, owner_count)
         start = pl.multiple_of(to * columns + g * far_width, lane)
+        target = piece.at[:, pl.ds(depth, near_width)] if n == 0 else piece
         copies.append(
-            pltpu.make_async_copy(expand.at[0, :, pl.ds(start, near_width)], piece, sem.at[n])
+            pltpu.make_async_copy(expand.at[0, :, pl.ds(start, near_width)], target, sem.at[n])
         )
     for copy in copies:
         copy.start()
@@ -103,14 +104,15 @@
         copy.wait()
 
 
-def gather_kernel(owner_count, slots, index, *refs):
+def gather_kernel(offsets, slots, index, *refs):
+    owner_count = len(offsets)
     blocks = refs[:owner_count]
-    shrink, _, rows_out, keep, send, rows, partial = refs[owner_count:]
+    shrink, _, rows_out, keep, send, slot_out, rows, partial = refs[owner_count:]
     a, t = lax.axis_index("adapter"), lax.axis_index("tensor")
-    height = blocks[0].shape[0]
-    for j in range(owner_count):
+    height, depth = blocks[0].shape
+    for j, part in zip(offsets, blocks):
         where = lax.rem(a + j, owner_count)
-        rows[pl.ds(pl.multiple_of(where * height, height), height), :] = blocks[j][...]
+        rows[pl.ds(pl.multiple_of(where * height, height), height), :] = part[:, :depth]
     quarter = rows.shape[0] // 4
     for i, flip in enumerate((0, 2, 1, 3)):
         start = pl.multiple_of(lax.bitwise_xor(t, flip) * quarter, quarter)
@@ -118,21 +120,18 @@
     product = lax.dot_general(
         shrink[...], rows[...], (((1,), (1,)), ((), ())), preferred_element_type=f32
     )
-    partial[...] = jnp.where(slot_of(index, slots) == a, product, 0.0)
+    named, table = index[...], slots[...]
+    slot = jnp.zeros_like(named)
+    for k in range(table.shape[1]):
+        slot = jnp.where(named == k, table[:, k : k + 1], slot)
+    slot_out[...] = slot
+    partial[...] = jnp.where(slot == a, product, 0.0)
     rank_block = partial.shape[0] // 4
     for i, flip in enumerate((0, 2, 1, 3)):
         start = pl.multiple_of(lax.bitwise_xor(t, flip) * rank_block, rank_block)
         target = keep if i < 2 else send
         at = i % 2 * rank_block
         target[at : at + rank_block, :] = partial[pl.ds(start, rank_block), :]
-
-
-def slot_of(index, slots):
-    named = index[...]
-    slot = jnp.zeros_like(named)
-    for k in range(slots.shape[0]):
-        slot = jnp.where(named == k, slots[k], slot)
-    return slot
 
 
 def part_start(near_width, far_width, is_far, first):
@@ -158,23 +157,25 @@
         )
 
 
-def forward_kernel(owner_count, far_width, *refs):
-    near, packed = refs[: owner_count - 1], refs[-1]
-    height, near_width = near[0].shape
+def forward_kernel(far_width, *refs):
+    *near, packed = refs
+    height, near_width = near[-1].shape
     start = pl.multiple_of(lax.axis_index("groups") * (near_width - far_width), lane)
     for n, piece in enumerate(near):
-        packed[n * height : (n + 1) * height, :] = piece[:, pl.ds(start, far_width)]
-
-
-def delta_kernel(owner_count, offsets, start_of, block, base_count, piece_count, slots, index, *refs):
+        skip = piece.shape[1] - near_width
+        packed[n * height : (n + 1) * height, :] = piece[:, pl.ds(start + skip, far_width)]
+
+
+def delta_kernel(owner_count, offsets, start_of, block, base_count, piece_count, slot, *refs):
     bases, refs = refs[:base_count], refs[base_count:]
     own, shrunk = refs[:2]
     pieces = refs[2 : 2 + piece_count]
+    width = sum(base.shape[1] for base in bases)
     *outs, flat, ordered = refs[-6:]
     a, t = lax.axis_index("adapter"), lax.axis_index("tensor")
     row_count = bases[0].shape[0]
     quarter = row_count // 4
-    slot = slot_of(index, slots)
+    slot = slot[...]
     merged = shrunk[...].astype(f32)
     spread = [
         jnp.where(slot == lax.rem(a + j, owner_count), merged, 0.0) for j in (0, *offsets)
@@ -189,7 +190,8 @@
         for column in range(0, base.shape[1], block):
             source = pl.multiple_of(start_of() + at, lane)
             expand = jnp.concatenate(
-                [own[:, pl.ds(source, block)]] + [piece[:, at : at + block] for piece in pieces],
+                [own[:, pl.ds(source, block)]]
+                + [piece[:, pl.ds(piece.shape[1] - width + at, block)] for piece in pieces],
                 axis=0,
             )
             total = base[:, column : column + block] + jnp.dot(
@@ -242,9 +244,8 @@
     weight = pltpu.with_memory_space_constraint(base_up_weight, pltpu.HBM)
     expand = pltpu.with_memory_space_constraint(adapter_expand_weight, pltpu.HBM)
     index = row_adapter_index.reshape(1, row_count)
-    others = range(1, owner_count)
     offsets = (2, 1, 3)
-    blocks = [tokens] + [from_owner(tokens, j) for j in others]
+    blocks = [from_owner(tokens, j) for j in offsets[1:]]
 
     pieces = kernel_call(
         functools.partial(cut_kernel, owner_count, offsets, far_width),
@@ -252,18 +253,20 @@
         1,
         1,
         1,
-        in_specs=[anywhere],
+        in_specs=[anywhere] * 2,
         out_specs=[vmem] * (owner_count - 1),
-        out_shape=[pltpu.VMEM((rank_block, near_width), bf16)] * (owner_count - 1),
-        scratch_shapes=[pltpu.SemaphoreType.DMA((owner_count - 1,))],
-    )(expand)
+        out_shape=[pltpu.VMEM((rank_block, depth + near_width), bf16)]
+        + [pltpu.VMEM((rank_block, near_width), bf16)] * (owner_count - 2),
+        scratch_shapes=[pltpu.SemaphoreType.DMA((owner_count,))],
+    )(tokens, expand)
+    near = [from_owner(piece, j) for piece, j in zip(pieces, offsets)]
 
     def split(count):
         return [(0, count - count // 2), (count - count // 2, count // 2)]
 
     parts = [(False, *span) for span in split(near_count)]
     parts += [(True, *span) for span in split(block_count - near_count)]
-    held_counts = [min(part[2], count) for part, count in zip(parts, (4, 2, 1, 1))]
+    held_counts = [min(part[2], count) for part, count in zip(parts, (4, 4, 3, 3))]
     starts = [
         functools.partial(part_start, near_width, far_width, is_far, first * block)
         for is_far, first, _ in parts
@@ -283,21 +286,27 @@
         scratch_shapes=[pltpu.SemaphoreType.DMA((sum(held_counts),)), pltpu.SemaphoreType.DMA],
     )(weight, expand, pieces[0])
 
-    near = [from_owner(pieces[0], offsets[0])]
-    *late, own = lax.optimization_barrier((*pieces[1:], own))
-    near += [from_owner(piece, j) for piece, j in zip(late, offsets[1:])]
-    rows, keep, send = kernel_call(
-        functools.partial(gather_kernel, owner_count),
+    rows, keep, send, slot = kernel_call(
+        functools.partial(gather_kernel, (0, *offsets)),
         "gather_rows",
         1,
         1,
         4,
-        in_specs=[smem, vmem] + [vmem] * (owner_count + 1) + [anywhere],
-        out_specs=[vmem] * 3,
+        in_specs=[vmem] * (owner_count + 3) + [anywhere],
+        out_specs=[vmem] * 4,
         out_shape=[jax.ShapeDtypeStruct((row_count, depth), bf16)]
-        + [jax.ShapeDtypeStruct((rank // 2, row_count), f32)] * 2,
+        + [jax.ShapeDtypeStruct((rank // 2, row_count), f32)] * 2
+        + [jax.ShapeDtypeStruct((1, row_count), jnp.int32)],
         scratch_shapes=[pltpu.VMEM((row_count, depth), bf16), pltpu.VMEM((rank, row_count), f32)],
-    )(adapter_slot_index, index, *blocks, adapter_shrink_weight[0].T, own)
+    )(
+        adapter_slot_index.reshape(1, owner_count),
+        index,
+        tokens,
+        near[0],
+        *blocks,
+        adapter_shrink_weight[0].T,
+        own,
+    )
 
     def base_part(n, *after):
         is_far, first, count = parts[n]
@@ -317,7 +326,7 @@
             ],
         )(rows, weight, held, *after)
 
-    def delta_part(is_far, bases, pieces, shrunk):
+    def delta_part(is_far, bases, pieces):
         start_of = functools.partial(part_start, near_width, far_width, is_far, 0)
         width = sum(base.shape[1] for base in bases)
         return kernel_call(
@@ -328,14 +337,14 @@
             1,
             1,
             8,
-            in_specs=[smem] + [vmem] * (3 + len(bases) + len(pieces)),
+            in_specs=[vmem] * (3 + len(bases) + len(pieces)),
             out_specs=[vmem] * 4,
             out_shape=[jax.ShapeDtypeStruct((row_count // 4, width), f32)] * 4,
             scratch_shapes=[
                 pltpu.VMEM((row_count, rank_block * owner_count), f32),
                 pltpu.VMEM((row_count, rank_block * owner_count), bf16),
             ],
-        )(adapter_slot_index, index, *bases, own, shrunk, *pieces)
+        )(slot, *bases, own, shrunk, *pieces)
 
     arrived = from_tensor(send, 1)
     base_0 = base_part(0, send)
@@ -346,7 +355,7 @@
     arrived, base_1, *near = lax.optimization_barrier((arrived, base_1, *near))
     shrunk = (adapter_scale * (pair[:rank_block] + arrived)).astype(bf16)
     packed = kernel_call(
-        functools.partial(forward_kernel, owner_count, far_width),
+        functools.partial(forward_kernel, far_width),
         "pack_far",
         1,
         1,
@@ -371,10 +380,10 @@
 
     halves = []
     for is_far, bases, pieces in ((False, [base_0, base_1], near), (True, base_far, [far])):
-        own_keep, cross_keep, own_send, cross_send = delta_part(is_far, bases, pieces, shrunk)
-        cross = cross_keep + from_tensor(cross_send, 1)
+        own_keep, cross_keep, own_send, cross_send = delta_part(is_far, bases, pieces)
+        cross = (cross_keep + from_tensor(cross_send, 1)).astype(bf16)
         kept = own_keep + from_tensor(own_send, 1)
-        crossed = from_tensor(cross.astype(bf16), 2)
+        crossed = from_tensor(cross, 2)
         halves.append((kept + crossed.astype(f32)).astype(bf16))
     first = jnp.concatenate(halves, axis=1)
     second = jnp.concatenate(halves[::-1], axis=1)

time: 50.6 us -> 49.1 us (0.970)
  Pallas kernels: 20.9 us -> 18.4 us
  waiting for transfers between devices: 9.24 us -> 7.32 us
  local copies, waits for them, and re-layouts: 0.02 us -> 1.86 us
  starting transfers between devices: 19.3 us -> 20.1 us
    pallas_call x4, Pallas kernels: 11.1 us -> 5.53 us  [base_part(): kernel_call(functools.partial(base_kernel, starts[n], block, sum(held_cou...]
    pallas_call x1, Pallas kernels: 6.06 us -> 9.78 us  [paired(): kernel_call(functools.partial(load_kernel, starts, held_counts, block), '...]
    ppermute x6 -> x5, waiting for transfers between devices: 3.62 us -> 0.01 us  [from_owner(): lax.ppermute(x, 'adapter', [(s, (s - j) % owner_count) for s in range(own...]
    unnamed x8 -> x14, local copies, waits for them, and re-layouts: 0.01 us -> 1.85 us
    ppermute x2, starting transfers between devices: 2.34 us -> 4.03 us  [from_mirror(): return lax.ppermute(x, 'adapter', [(s, s ^ m) for s in range(owner_count)])]
    ppermute x2, waiting for transfers between devices: 0.55 us -> 1.66 us  [from_mirror(): return lax.ppermute(x, 'adapter', [(s, s ^ m) for s in range(owner_count)])]
    ppermute x6 -> x5, starting transfers between devices: 10.1 us -> 9.28 us  [from_owner(): lax.ppermute(x, 'adapter', [(s, (s - j) % owner_count) for s in range(own...]
    ppermute x8, waiting for transfers between devices: 5.07 us -> 5.64 us  [from_tensor(): return lax.ppermute(x, 'tensor', [(s, s ^ m) for s in range(4)])]
  transfers between devices with their start and end apart: 17 -> 16, of which waited for: 4 -> 5; matrix products, arithmetic and copies ran while one was open for 0% -> 0% of each run, Pallas kernels for 41% -> 35%
where the time goes in v5:
time: 49.1 us; the launch traced here: 48.9 us
  starting transfers between devices  20.1 us (41%)
  Pallas kernels  18.4 us (37%)
  waiting for transfers between devices  7.32 us (15%)
  local copies, waits for them, and re-layouts  1.86 us (4%)
  other arithmetic  0.91 us (2%)
    pallas_call x1, Pallas kernels, paired(): kernel_call(functools.partial(load_kernel, starts, held_counts, block), '...  9.78 us
    ppermute x5, starting transfers between devices, from_owner(): lax.ppermute(x, 'adapter', [(s, (s - j) % owner_count) for s in range(own...  9.28 us
    ppermute x8, waiting for transfers between devices, from_tensor(): return lax.ppermute(x, 'tensor', [(s, s ^ m) for s in range(4)])  5.64 us
    pallas_call x4, Pallas kernels, base_part(): kernel_call(functools.partial(base_kernel, starts[n], block, sum(held_cou...  5.53 us
    ppermute x8, starting transfers between devices, from_tensor(): return lax.ppermute(x, 'tensor', [(s, s ^ m) for s in range(4)])  5.2 us
    ppermute x2, starting transfers between devices, from_mirror(): return lax.ppermute(x, 'adapter', [(s, s ^ m) for s in range(owner_count)])  4.03 us
    unnamed x14, local copies, waits for them, and re-layouts  1.85 us
    pallas_call x2, Pallas kernels, delta_part(): kernel_call(functools.partial(delta_kernel, owner_count, offsets, start_o...  1.66 us
  transfers between devices with their start and end apart: 16, of which 5 were waited for; matrix products, arithmetic and copies ran while one was open for 0% of the time, Pallas kernels for 35%

profile of v5, /device:TPU:0, one launch (start us, length us, event | category | flops | bytes accessed | tf_op | source)
XLA Modules:
  0.0 48.9 jit_solution(9379339479594466221)
XLA Ops:
  0.0 0.8 %copy-done.3 = bf16[16,2048]{1,0:T(8,128)(2,1)S(1)} copy-done((bf16[16,2048]{1,0:T(8,128)(2,1)S(1)}, bf16[16,2048]{1,0:T(8,128)(2,1)}, u32[]{:S(2)}) %copy-start.3) | copy-done | bytes 65560
  0.9 1.2 %cut_expand.1 = (bf16[16,6144]{1,0:T(8,128)(2,1)S(1)}, bf16[16,4096]{1,0:T(8,128)(2,1)S(1)}, bf16[16,4096]{1,0:T(8,128)(2,1)S(1)}) custom-call(bf16[16,2048]{1,0:T(8,128)(2,1)S(1)} %copy-done.3, bf16[1,16,28672]{2,1,0:T(8,128)(2,1)} %expand.3), custom_call_target="tpu_custom_call" | custom-call | flops 1 | bytes 1 | tf_op jit(solution)/shard_map/cut_expand/pallas_call | solution.py:250
  2.1 4.1 %collective-permute-start = (bf16[16,6144]{1,0:T(8,128)(2,1)S(1)}, bf16[16,6144]{1,0:T(8,128)(2,1)S(1)}, u32[]{:S(2)}, u32[]{:S(2)}) collective-permute-start(bf16[16,6144]{1,0:T(8,128)(2,1)S(1)} %get-tuple-element.33.after), channel_id=1, source_target_pairs={{0,8},{4,12},{8,0},{12,4},{1,9},{5,13},{9,1},{13,5},{2,10},{6,14},... | collective-permute-start | bytes 589832 | tf_op jit(solution)/shard_map/ppermute | solution.py:233
  6.2 1.3 %collective-permute-start.1 = (bf16[16,2048]{1,0:T(8,128)(2,1)}, bf16[16,2048]{1,0:T(8,128)(2,1)S(1)}, u32[]{:S(2)}, u32[]{:S(2)}) collective-permute-start(bf16[16,2048]{1,0:T(8,128)(2,1)} %refs_0_.1), channel_id=1, source_target_pairs={{0,12},{4,0},{8,4},{12,8},{1,13},{5,1},{9,5},{13,9},{2,14},{6,2},{... | collective-permute-start | bytes 196616 | tf_op jit(solution)/shard_map/ppermute | solution.py:233
  7.5 0.7 %collective-permute-start.2 = (bf16[16,2048]{1,0:T(8,128)(2,1)}, bf16[16,2048]{1,0:T(8,128)(2,1)S(1)}, u32[]{:S(2)}, u32[]{:S(2)}) collective-permute-start(bf16[16,2048]{1,0:T(8,128)(2,1)} %refs_0_.1), channel_id=1, source_target_pairs={{0,4},{4,8},{8,12},{12,0},{1,5},{5,9},{9,13},{13,1},{2,6},{6,10},{... | collective-permute-start | bytes 196616 | tf_op jit(solution)/shard_map/ppermute | solution.py:233
  8.2 3.1 %collective-permute-start.5 = (bf16[16,4096]{1,0:T(8,128)(2,1)S(1)}, bf16[16,4096]{1,0:T(8,128)(2,1)S(1)}, u32[]{:S(2)}, u32[]{:S(2)}) collective-permute-start(bf16[16,4096]{1,0:T(8,128)(2,1)S(1)} %get-tuple-element.42), channel_id=1, source_target_pairs={{0,12},{4,0},{8,4},{12,8},{1,13},{5,1},{9,5},{13,9},{2,14},{6,2},{... | collective-permute-start | bytes 393224 | tf_op jit(solution)/shard_map/ppermute | solution.py:233
  11.3 0.0 collective-permute-start.6
  11.3 9.8 %load_weights.1 = (bf16[14,2048,512]{2,1,0:T(8,128)(2,1)S(1)}, bf16[16,7168]{1,0:T(8,128)(2,1)S(1)}) custom-call(bf16[2048,7168]{1,0:T(8,128)(2,1)} %weight.9, bf16[1,16,28672]{2,1,0:T(8,128)(2,1)} %expand.3, bf16[16,6144]{1,0:T(8,128)(2,1)S(1)} %get-tuple-element.33.after), custom_call_target="tpu_custom_call" | custom-call | flops 1 | bytes 1 | tf_op jit(solution)/shard_map/load_weights/pallas_call | solution.py:274
  21.1 0.0 collective-permute-done.1.refs_2_
  21.1 0.0 collective-permute-done.2.refs_3_
  21.1 0.0 collective-permute-done.refs_1_.refs_0_.refs_4_
  21.2 0.0 copy-done.2
  21.2 0.0 copy-done.4
  21.2 0.0 copy-done.5
  21.2 0.0 copy-done.6
  21.2 0.3 gather_rows.1
  21.5 0.1 collective-permute-start.3
  21.5 1.6 %base_part.4.refs_0_ = f32[64,2048]{1,0:T(8,128)S(1)} custom-call(bf16[64,2048]{1,0:T(8,128)(2,1)S(1)} %get-tuple-element.37.rows, bf16[2048,7168]{1,0:T(8,128)(2,1)} %weight.9, bf16[14,2048,512]{2,1,0:T(8,128)(2,1)S(1)} %get-tuple-element.38.held, f32[32,64]{1,0:T(8,128)S(1)} %get-tuple-element.36.refs_0_), custom_call_target="tpu_custom_call" | custom-call | flops 536870912 | bytes 8388608 | tf_op jit(solution)/shard_map/base_part/pallas_call | solution.py:314
  23.1 0.0 collective-permute-done.3
  23.1 1.6 %collective-permute-start.4 = (f32[16,64]{1,0:T(8,128)S(1)}, f32[16,64]{1,0:T(8,128)S(1)}, u32[]{:S(2)}, u32[]{:S(2)}) collective-permute-start(f32[16,64]{1,0:T(8,128)S(1)} %slice.8), channel_id=1, source_target_pairs={{0,2},{1,3},{2,0},{3,1},{4,6},{5,7},{6,4},{7,5},{8,10},{9,11},{10,... | collective-permute-start | bytes 12296 | tf_op jit(solution)/shard_map/ppermute | solution.py:236
  24.7 1.6 %base_part.5.refs_1_ = f32[64,2048]{1,0:T(8,128)S(1)} custom-call(bf16[64,2048]{1,0:T(8,128)(2,1)S(1)} %get-tuple-element.37.rows, bf16[2048,7168]{1,0:T(8,128)(2,1)} %weight.9, bf16[14,2048,512]{2,1,0:T(8,128)(2,1)S(1)} %get-tuple-element.38.held, f32[32,64]{1,0:T(8,128)S(1)} %add.30.refs_0_), custom_call_target="tpu_custom_call" | custom-call | flops 536870912 | bytes 8388608 | tf_op jit(solution)/shard_map/base_part/pallas_call | solution.py:314
  26.3 0.0 collective-permute-done.5.refs_1_.refs_5_
  26.3 0.0 collective-permute-done.6.refs_2_.refs_6_
  26.3 0.6 %collective-permute-done.4 = f32[16,64]{1,0:T(8,128)S(1)} collective-permute-done((f32[16,64]{1,0:T(8,128)S(1)}, f32[16,64]{1,0:T(8,128)S(1)}, u32[]{:S(2)}, u32[]{:S(2)}) %collective-permute-start.4) | collective-permute-done | bytes 4128 | tf_op jit(solution)/shard_map/ppermute | solution.py:236
  26.9 1.6 %collective-permute-start.12 = (bf16[48,3072]{1,0:T(8,128)(2,1)S(1)}, bf16[48,3072]{1,0:T(8,128)(2,1)}, u32[]{:S(2)}, u32[]{:S(2)}) collective-permute-start(bf16[48,3072]{1,0:T(8,128)(2,1)S(1)} %pack_far.1.refs_1_), channel_id=1, source_target_pairs={{0,16},{16,0},{1,17},{17,1},{2,18},{18,2},{3,19},{19,3},{4,20},{20... | collective-permute-start | bytes 884744 | tf_op jit(solution)/shard_map/ppermute | solution.py:242
  28.5 1.5 %collective-permute-start.7 = (bf16[16,64]{1,0:T(8,128)(2,1)S(1)}, bf16[16,64]{1,0:T(8,128)(2,1)S(1)}, u32[]{:S(2)}, u32[]{:S(2)}) collective-permute-start(bf16[16,64]{1,0:T(8,128)(2,1)S(1)} %fusion.1.refs_0_), channel_id=1, source_target_pairs={{0,4},{4,0},{8,12},{12,8},{1,5},{5,1},{9,13},{13,9},{2,6},{6,2},{1... | collective-permute-start | bytes 6152 | tf_op jit(solution)/shard_map/ppermute | solution.py:239
  30.0 1.2 %base_part.6.refs_0_ = f32[64,1536]{1,0:T(8,128)S(1)} custom-call(bf16[64,2048]{1,0:T(8,128)(2,1)S(1)} %get-tuple-element.37.rows, bf16[2048,7168]{1,0:T(8,128)(2,1)} %weight.9, bf16[14,2048,512]{2,1,0:T(8,128)(2,1)S(1)} %get-tuple-element.38.held, bf16[16,64]{1,0:T(8,128)(2,1)S(1)} %fusion.1.refs_0_, bf16[48,3072]{1,0:T(8,128)(2,1)S(1)} %pack_far.1.refs_1_), custom_call_target="tpu_custom_call" | custom-call | flops 1 | bytes 1 | tf_op jit(solution)/shard_map/base_part/pallas_call | solution.py:314
  31.2 0.9 %collective-permute-done.7 = bf16[16,64]{1,0:T(8,128)(2,1)S(1)} collective-permute-done((bf16[16,64]{1,0:T(8,128)(2,1)S(1)}, bf16[16,64]{1,0:T(8,128)(2,1)S(1)}, u32[]{:S(2)}, u32[]{:S(2)}) %collective-permute-start.7) | collective-permute-done | bytes 2080 | tf_op jit(solution)/shard_map/ppermute | solution.py:239
  32.1 2.5 %collective-permute-start.8 = (bf16[16,64]{1,0:T(8,128)(2,1)S(1)}, bf16[16,64]{1,0:T(8,128)(2,1)S(1)}, u32[]{:S(2)}, u32[]{:S(2)}) collective-permute-start(bf16[16,64]{1,0:T(8,128)(2,1)S(1)} %add.32.refs_0_), channel_id=1, source_target_pairs={{0,8},{4,12},{8,0},{12,4},{1,9},{5,13},{9,1},{13,5},{2,10},{6,14},... | collective-permute-start | bytes 6152 | tf_op jit(solution)/shard_map/ppermute | solution.py:239
  34.6 1.2 %base_part.7.refs_1_ = f32[64,1536]{1,0:T(8,128)S(1)} custom-call(bf16[64,2048]{1,0:T(8,128)(2,1)S(1)} %get-tuple-element.37.rows, bf16[2048,7168]{1,0:T(8,128)(2,1)} %weight.9, bf16[14,2048,512]{2,1,0:T(8,128)(2,1)S(1)} %get-tuple-element.38.held, bf16[16,64]{1,0:T(8,128)(2,1)S(1)} %add.32.refs_0_, bf16[48,3072]{1,0:T(8,128)(2,1)S(1)} %pack_far.1.refs_1_), custom_call_target="tpu_custom_call" | custom-call | flops 1 | bytes 1 | tf_op jit(solution)/shard_map/base_part/pallas_call | solution.py:314
  35.8 0.8 %collective-permute-done.8 = bf16[16,64]{1,0:T(8,128)(2,1)S(1)} collective-permute-done((bf16[16,64]{1,0:T(8,128)(2,1)S(1)}, bf16[16,64]{1,0:T(8,128)(2,1)S(1)}, u32[]{:S(2)}, u32[]{:S(2)}) %collective-permute-start.8) | collective-permute-done | bytes 2080 | tf_op jit(solution)/shard_map/ppermute | solution.py:239
  36.6 0.4 delta_part.2
  37.0 0.1 collective-permute-start.10
  37.1 0.5 %collective-permute-start.9 = (f32[16,4096]{1,0:T(8,128)S(1)}, f32[16,4096]{1,0:T(8,128)S(1)}, u32[]{:S(2)}, u32[]{:S(2)}) collective-permute-start(f32[16,4096]{1,0:T(8,128)S(1)} %get-tuple-element.52), channel_id=1, source_target_pairs={{0,1},{1,0},{2,3},{3,2},{4,5},{5,4},{6,7},{7,6},{8,9},{9,8},{10,11... | collective-permute-start | bytes 786440 | tf_op jit(solution)/shard_map/ppermute | solution.py:236
  37.6 0.0 collective-permute-done.12.refs_4_
  37.6 1.0 %copy-done.1 = f32[64,1536]{1,0:T(8,128)S(1)} copy-done((f32[64,1536]{1,0:T(8,128)S(1)}, f32[64,1536]{1,0:T(8,128)}, u32[]{:S(2)}) %copy-start.1) | copy-done | bytes 393240
  38.6 1.3 %delta_part.3 = (f32[16,3072]{1,0:T(8,128)S(1)}, f32[16,3072]{1,0:T(8,128)S(1)}, f32[16,3072]{1,0:T(8,128)S(1)}, f32[16,3072]{1,0:T(8,128)S(1)}) custom-call(s32[1,64]{1,0:T(1,128)S(1)} %get-tuple-element.35.slot, f32[64,1536]{1,0:T(8,128)S(1)} %base_part.6.refs_0_, f32[64,1536]{1,0:T(8,128)S(1)} %copy-done.1, ...), custom_call_target="tpu_custom_call" | custom-call | flops 1 | bytes 1 | tf_op jit(solution)/shard_map/delta_part/pallas_call | solution.py:332
  39.9 0.1 collective-permute-start.14
  40.0 0.0 collective-permute-done.10
  40.1 1.6 %collective-permute-start.11 = (bf16[16,4096]{1,0:T(8,128)(2,1)S(1)}, bf16[16,4096]{1,0:T(8,128)(2,1)S(1)}, u32[]{:S(2)}, u32[]{:S(2)}) collective-permute-start(bf16[16,4096]{1,0:T(8,128)(2,1)S(1)} %add_convert_fusion.1), channel_id=1, source_target_pairs={{0,2},{1,3},{2,0},{3,1},{4,6},{5,7},{6,4},{7,5},{8,10},{9,11},{10,... | collective-permute-start | bytes 393224 | tf_op jit(solution)/shard_map/ppermute | solution.py:236
  41.6 0.2 collective-permute-start.13
  41.8 0.0 collective-permute-done.14
  41.8 1.2 %collective-permute-start.15 = (bf16[16,3072]{1,0:T(8,128)(2,1)S(1)}, bf16[16,3072]{1,0:T(8,128)(2,1)S(1)}, u32[]{:S(2)}, u32[]{:S(2)}) collective-permute-start(bf16[16,3072]{1,0:T(8,128)(2,1)S(1)} %add_convert_fusion.3), channel_id=1, source_target_pairs={{0,2},{1,3},{2,0},{3,1},{4,6},{5,7},{6,4},{7,5},{8,10},{9,11},{10,... | collective-permute-start | bytes 294920 | tf_op jit(solution)/shard_map/ppermute | solution.py:236
  43.0 0.0 collective-permute-done.9
  43.0 3.5 %collective-permute-done.11 = bf16[16,4096]{1,0:T(8,128)(2,1)S(1)} collective-permute-done((bf16[16,4096]{1,0:T(8,128)(2,1)S(1)}, bf16[16,4096]{1,0:T(8,128)(2,1)S(1)}, u32[]{:S(2)}, u32[]{:S(2)}) %collective-permute-start.11) | collective-permute-done | bytes 131104 | tf_op jit(solution)/shard_map/ppermute | solution.py:236
  46.5 0.0 collective-permute-done.13
  46.5 1.6 %collective-permute-done.15 = bf16[16,3072]{1,0:T(8,128)(2,1)S(1)} collective-permute-done((bf16[16,3072]{1,0:T(8,128)(2,1)S(1)}, bf16[16,3072]{1,0:T(8,128)(2,1)S(1)}, u32[]{:S(2)}, u32[]{:S(2)}) %collective-permute-start.15) | collective-permute-done | bytes 98336 | tf_op jit(solution)/shard_map/ppermute | solution.py:236
  48.1 0.7 %maximum_select_fusion = bf16[16,7168]{1,0:T(8,128)(2,1)} fusion(bf16[16,3072]{1,0:T(8,128)(2,1)S(1)} %add_convert_fusion.2, bf16[16,4096]{1,0:T(8,128)(2,1)S(1)} %add_convert_fusion, pred[]{:T(512)S(6)} %eq.3), kind=kLoop, calls=%fused_computation.2 | loop fusion | flops 1032192 | bytes 458753 | tf_op jit(solution)/shard_map/jit(_where)/select_n | solution.py:390
  (18 shorter events, 0.2 us)
Async XLA Ops:
  0.0 0.8 %copy-start.3 = (bf16[16,2048]{1,0:T(8,128)(2,1)S(1)}, bf16[16,2048]{1,0:T(8,128)(2,1)}, u32[]{:S(2)}) copy-start(bf16[16,2048]{1,0:T(8,128)(2,1)} %refs_0_.1) | copy-start | bytes 196612
  0.8 20.3 %copy-start.2 = (bf16[1,2048,64]{1,2,0:T(8,128)(2,1)S(1)}, bf16[1,2048,64]{1,2,0:T(8,128)(2,1)}, u32[]{:S(2)}) copy-start(bf16[1,2048,64]{1,2,0:T(8,128)(2,1)} %param.8) | copy-start | bytes 786436
  0.8 20.3 %copy-start.4 = (bf16[16,2048]{1,0:T(8,128)(2,1)S(1)}, bf16[16,2048]{1,0:T(8,128)(2,1)}, u32[]{:S(2)}) copy-start(bf16[16,2048]{1,0:T(8,128)(2,1)} %refs_0_.1) | copy-start | bytes 196612
  0.8 20.3 %copy-start.5 = (s32[4]{0:T(128)S(1)}, s32[4]{0:T(128)}, u32[]{:S(2)}) copy-start(s32[4]{0:T(128)} %param.11) | copy-start | bytes 52
  0.8 20.3 %copy-start.6 = (s32[64,1]{0,1:T(1,128)S(1)}, s32[64,1]{0,1:T(1,128)}, u32[]{:S(2)}) copy-start(s32[64,1]{0,1:T(1,128)} %param.10) | copy-start | bytes 772
  2.1 19.1 %collective-permute-start = (bf16[16,6144]{1,0:T(8,128)(2,1)S(1)}, bf16[16,6144]{1,0:T(8,128)(2,1)S(1)}, u32[]{:S(2)}, u32[]{:S(2)}) collective-permute-start(bf16[16,6144]{1,0:T(8,128)(2,1)S(1)} %get-tuple-element.33.after), channel_id=1, source_target_pairs={{0,8},{4,12},{8,0},{12,4},{1,9},{5,13},{9,1},{13,5},{2,10},{6,14},... | collective-permute-start | bytes 589832 | tf_op jit(solution)/shard_map/ppermute | solution.py:233
  6.2 15.0 %collective-permute-start.1 = (bf16[16,2048]{1,0:T(8,128)(2,1)}, bf16[16,2048]{1,0:T(8,128)(2,1)S(1)}, u32[]{:S(2)}, u32[]{:S(2)}) collective-permute-start(bf16[16,2048]{1,0:T(8,128)(2,1)} %refs_0_.1), channel_id=1, source_target_pairs={{0,12},{4,0},{8,4},{12,8},{1,13},{5,1},{9,5},{13,9},{2,14},{6,2},{... | collective-permute-start | bytes 196616 | tf_op jit(solution)/shard_map/ppermute | solution.py:233
  7.5 13.6 %collective-permute-start.2 = (bf16[16,2048]{1,0:T(8,128)(2,1)}, bf16[16,2048]{1,0:T(8,128)(2,1)S(1)}, u32[]{:S(2)}, u32[]{:S(2)}) collective-permute-start(bf16[16,2048]{1,0:T(8,128)(2,1)} %refs_0_.1), channel_id=1, source_target_pairs={{0,4},{4,8},{8,12},{12,0},{1,5},{5,9},{9,13},{13,1},{2,6},{6,10},{... | collective-permute-start | bytes 196616 | tf_op jit(solution)/shard_map/ppermute | solution.py:233
  8.2 18.1 %collective-permute-start.5 = (bf16[16,4096]{1,0:T(8,128)(2,1)S(1)}, bf16[16,4096]{1,0:T(8,128)(2,1)S(1)}, u32[]{:S(2)}, u32[]{:S(2)}) collective-permute-start(bf16[16,4096]{1,0:T(8,128)(2,1)S(1)} %get-tuple-element.42), channel_id=1, source_target_pairs={{0,12},{4,0},{8,4},{12,8},{1,13},{5,1},{9,5},{13,9},{2,14},{6,2},{... | collective-permute-start | bytes 393224 | tf_op jit(solution)/shard_map/ppermute | solution.py:233
  11.3 14.9 %collective-permute-start.6 = (bf16[16,4096]{1,0:T(8,128)(2,1)S(1)}, bf16[16,4096]{1,0:T(8,128)(2,1)S(1)}, u32[]{:S(2)}, u32[]{:S(2)}) collective-permute-start(bf16[16,4096]{1,0:T(8,128)(2,1)S(1)} %get-tuple-element.43), channel_id=1, source_target_pairs={{0,4},{4,8},{8,12},{12,0},{1,5},{5,9},{9,13},{13,1},{2,6},{6,10},{... | collective-permute-start | bytes 393224 | tf_op jit(solution)/shard_map/ppermute | solution.py:233
  21.5 1.7 %collective-permute-start.3 = (f32[32,64]{1,0:T(8,128)S(1)}, f32[32,64]{1,0:T(8,128)S(1)}, u32[]{:S(2)}, u32[]{:S(2)}) collective-permute-start(f32[32,64]{1,0:T(8,128)S(1)} %get-tuple-element.36.refs_0_), channel_id=1, source_target_pairs={{0,1},{1,0},{2,3},{3,2},{4,5},{5,4},{6,7},{7,6},{8,9},{9,8},{10,11... | collective-permute-start | bytes 24584 | tf_op jit(solution)/shard_map/ppermute | solution.py:236
  23.1 3.7 %collective-permute-start.4 = (f32[16,64]{1,0:T(8,128)S(1)}, f32[16,64]{1,0:T(8,128)S(1)}, u32[]{:S(2)}, u32[]{:S(2)}) collective-permute-start(f32[16,64]{1,0:T(8,128)S(1)} %slice.8), channel_id=1, source_target_pairs={{0,2},{1,3},{2,0},{3,1},{4,6},{5,7},{6,4},{7,5},{8,10},{9,11},{10,... | collective-permute-start | bytes 12296 | tf_op jit(solution)/shard_map/ppermute | solution.py:236
  26.9 10.7 %collective-permute-start.12 = (bf16[48,3072]{1,0:T(8,128)(2,1)S(1)}, bf16[48,3072]{1,0:T(8,128)(2,1)}, u32[]{:S(2)}, u32[]{:S(2)}) collective-permute-start(bf16[48,3072]{1,0:T(8,128)(2,1)S(1)} %pack_far.1.refs_1_), channel_id=1, source_target_pairs={{0,16},{16,0},{1,17},{17,1},{2,18},{18,2},{3,19},{19,3},{4,20},{20... | collective-permute-start | bytes 884744 | tf_op jit(solution)/shard_map/ppermute | solution.py:242
  28.5 3.6 %collective-permute-start.7 = (bf16[16,64]{1,0:T(8,128)(2,1)S(1)}, bf16[16,64]{1,0:T(8,128)(2,1)S(1)}, u32[]{:S(2)}, u32[]{:S(2)}) collective-permute-start(bf16[16,64]{1,0:T(8,128)(2,1)S(1)} %fusion.1.refs_0_), channel_id=1, source_target_pairs={{0,4},{4,0},{8,12},{12,8},{1,5},{5,1},{9,13},{13,9},{2,6},{6,2},{1... | collective-permute-start | bytes 6152 | tf_op jit(solution)/shard_map/ppermute | solution.py:239
  32.1 4.5 %collective-permute-start.8 = (bf16[16,64]{1,0:T(8,128)(2,1)S(1)}, bf16[16,64]{1,0:T(8,128)(2,1)S(1)}, u32[]{:S(2)}, u32[]{:S(2)}) collective-permute-start(bf16[16,64]{1,0:T(8,128)(2,1)S(1)} %add.32.refs_0_), channel_id=1, source_target_pairs={{0,8},{4,12},{8,0},{12,4},{1,9},{5,13},{9,1},{13,5},{2,10},{6,14},... | collective-permute-start | bytes 6152 | tf_op jit(solution)/shard_map/ppermute | solution.py:239
  35.8 1.2 %copy-start = (f32[64,1536]{1,0:T(8,128)}, f32[64,1536]{1,0:T(8,128)S(1)}, u32[]{:S(2)}) copy-start(f32[64,1536]{1,0:T(8,128)S(1)} %base_part.7.refs_1_) | copy-start | bytes 1179652
  37.0 3.0 %collective-permute-start.10 = (f32[16,4096]{1,0:T(8,128)S(1)}, f32[16,4096]{1,0:T(8,128)S(1)}, u32[]{:S(2)}, u32[]{:S(2)}) collective-permute-start(f32[16,4096]{1,0:T(8,128)S(1)} %get-tuple-element.54), channel_id=1, source_target_pairs={{0,1},{1,0},{2,3},{3,2},{4,5},{5,4},{6,7},{7,6},{8,9},{9,8},{10,11... | collective-permute-start | bytes 786440 | tf_op jit(solution)/shard_map/ppermute | solution.py:236
  37.1 5.9 %collective-permute-start.9 = (f32[16,4096]{1,0:T(8,128)S(1)}, f32[16,4096]{1,0:T(8,128)S(1)}, u32[]{:S(2)}, u32[]{:S(2)}) collective-permute-start(f32[16,4096]{1,0:T(8,128)S(1)} %get-tuple-element.52), channel_id=1, source_target_pairs={{0,1},{1,0},{2,3},{3,2},{4,5},{5,4},{6,7},{7,6},{8,9},{9,8},{10,11... | collective-permute-start | bytes 786440 | tf_op jit(solution)/shard_map/ppermute | solution.py:236
  37.6 1.0 %copy-start.1 = (f32[64,1536]{1,0:T(8,128)S(1)}, f32[64,1536]{1,0:T(8,128)}, u32[]{:S(2)}) copy-start(f32[64,1536]{1,0:T(8,128)} %copy-done) | copy-start | bytes 1179652
  39.9 1.9 %collective-permute-start.14 = (f32[16,3072]{1,0:T(8,128)S(1)}, f32[16,3072]{1,0:T(8,128)S(1)}, u32[]{:S(2)}, u32[]{:S(2)}) collective-permute-start(f32[16,3072]{1,0:T(8,128)S(1)} %get-tuple-element.60), channel_id=1, source_target_pairs={{0,1},{1,0},{2,3},{3,2},{4,5},{5,4},{6,7},{7,6},{8,9},{9,8},{10,11... | collective-permute-start | bytes 589832 | tf_op jit(solution)/shard_map/ppermute | solution.py:236
  40.1 6.4 %collective-permute-start.11 = (bf16[16,4096]{1,0:T(8,128)(2,1)S(1)}, bf16[16,4096]{1,0:T(8,128)(2,1)S(1)}, u32[]{:S(2)}, u32[]{:S(2)}) collective-permute-start(bf16[16,4096]{1,0:T(8,128)(2,1)S(1)} %add_convert_fusion.1), channel_id=1, source_target_pairs={{0,2},{1,3},{2,0},{3,1},{4,6},{5,7},{6,4},{7,5},{8,10},{9,11},{10,... | collective-permute-start | bytes 393224 | tf_op jit(solution)/shard_map/ppermute | solution.py:236
  41.6 4.9 %collective-permute-start.13 = (f32[16,3072]{1,0:T(8,128)S(1)}, f32[16,3072]{1,0:T(8,128)S(1)}, u32[]{:S(2)}, u32[]{:S(2)}) collective-permute-start(f32[16,3072]{1,0:T(8,128)S(1)} %get-tuple-element.58), channel_id=1, source_target_pairs={{0,1},{1,0},{2,3},{3,2},{4,5},{5,4},{6,7},{7,6},{8,9},{9,8},{10,11... | collective-permute-start | bytes 589832 | tf_op jit(solution)/shard_map/ppermute | solution.py:236
  41.8 6.3 %collective-permute-start.15 = (bf16[16,3072]{1,0:T(8,128)(2,1)S(1)}, bf16[16,3072]{1,0:T(8,128)(2,1)S(1)}, u32[]{:S(2)}, u32[]{:S(2)}) collective-permute-start(bf16[16,3072]{1,0:T(8,128)(2,1)S(1)} %add_convert_fusion.3), channel_id=1, source_target_pairs={{0,2},{1,3},{2,0},{3,1},{4,6},{5,7},{6,4},{7,5},{8,10},{9,11},{10,... | collective-permute-start | bytes 294920 | tf_op jit(solution)/shard_map/ppermute | solution.py:236

commit v6 on v5

--- a/solution.py
+++ b/solution.py
@@ -60,20 +60,25 @@
     )
 
 
-def cut_kernel(owner_count, offsets, far_width, tokens, expand, *refs):
-    pieces, sem = refs[:-1], refs[-1]
+def cut_kernel(owner_count, offsets, far_width, small_count, expand, *refs):
+    small, refs = refs[:small_count], refs[small_count:]
+    *pieces, own = refs[: owner_count]
+    loaded, sem = refs[owner_count:-1], refs[-1]
     g, a = lax.axis_index("groups"), lax.axis_index("adapter")
-    depth = tokens.shape[1]
-    near_width = pieces[-1].shape[1]
+    near_width = pieces[0].shape[1]
     columns = near_width + far_width
-    copies = [pltpu.make_async_copy(tokens, pieces[0].at[:, pl.ds(0, depth)], sem.at[len(pieces)])]
+    start = pl.multiple_of(a * columns, lane)
+    copies = [
+        pltpu.make_async_copy(expand.at[0, :, pl.ds(start, columns)], own, sem.at[len(pieces)])
+    ]
     for n, (j, piece) in enumerate(zip(offsets, pieces)):
         to = lax.rem(a - j + owner_count, owner_count)
         start = pl.multiple_of(to * columns + g * far_width, lane)
-        target = piece.at[:, pl.ds(depth, near_width)] if n == 0 else piece
         copies.append(
-            pltpu.make_async_copy(expand.at[0, :, pl.ds(start, near_width)], target, sem.at[n])
+            pltpu.make_async_copy(expand.at[0, :, pl.ds(start, near_width)], piece, sem.at[n])
         )
+    for n, (source, target) in enumerate(zip(small, loaded)):
+        copies.append(pltpu.make_async_copy(source, target, sem.at[owner_count + n]))
     for copy in copies:
         copy.start()
     for copy in copies:
@@ -81,33 +86,27 @@
 
 
 def weight_copies(start, block, weight, target, sem):
-    copies = []
+    band_count = sem.shape[1]
+    band = weight.shape[0] // band_count
+    blocks = []
     for n in range(target.shape[0]):
         span = pl.ds(pl.multiple_of(start + n * block, lane), block)
-        copies.append(pltpu.make_async_copy(weight.at[:, span], target.at[n], sem.at[n]))
-    return copies
-
-
-def load_kernel(starts, counts, block, weight, expand, after, held, own, sem, own_sem):
-    a = lax.axis_index("adapter")
-    columns = own.shape[1]
-    copies, at = [], 0
-    for start_of, count in zip(starts, counts):
-        span = pl.ds(at, count)
-        copies += weight_copies(start_of(), block, weight, held.at[span], sem.at[span])
-        at += count
-    start = pl.multiple_of(a * columns, columns)
-    copies.append(pltpu.make_async_copy(expand.at[0, :, pl.ds(start, columns)], own, own_sem))
-    for copy in copies:
-        copy.start()
-    for copy in copies:
-        copy.wait()
+        bands = []
+        for m in range(band_count):
+            rows = pl.ds(m * band, band)
+            bands.append(
+                pltpu.make_async_copy(
+                    weight.at[rows, span], target.at[n, rows], sem.at[n, m]
+                )
+            )
+        blocks.append(bands)
+    return blocks
 
 
 def gather_kernel(offsets, slots, index, *refs):
     owner_count = len(offsets)
     blocks = refs[:owner_count]
-    shrink, _, rows_out, keep, send, slot_out, rows, partial = refs[owner_count:]
+    shrink, rows_out, keep, send, slot_out, rows, partial = refs[owner_count:]
     a, t = lax.axis_index("adapter"), lax.axis_index("tensor")
     height, depth = blocks[0].shape
     for j, part in zip(offsets, blocks):
@@ -139,21 +138,17 @@
     return ((1 - g) * near_width if is_far else g * far_width) + first
 
 
-def base_kernel(start_of, block, first, held_count, rows, weight, held, *refs):
+def base_kernel(start_of, block, rows, weight, *refs):
     total, streamed, sem = refs[-3:]
-    copies = []
-    if held_count * block < total.shape[1]:
-        copies = weight_copies(start_of() + held_count * block, block, weight, streamed, sem)
-    for copy in copies:
-        copy.start()
-    for n in range(total.shape[1] // block):
-        if n < held_count:
-            part = held[first + n]
-        else:
-            copies[n - held_count].wait()
-            part = streamed[n - held_count]
+    copies = weight_copies(start_of(), block, weight, streamed, sem)
+    for bands in copies:
+        for copy in bands:
+            copy.start()
+    for n, bands in enumerate(copies):
+        for copy in bands:
+            copy.wait()
         total[:, n * block : (n + 1) * block] = jnp.dot(
-            rows[...], part, preferred_element_type=f32
+            rows[...], streamed[n], preferred_element_type=f32
         )
 
 
@@ -243,22 +238,33 @@
 
     weight = pltpu.with_memory_space_constraint(base_up_weight, pltpu.HBM)
     expand = pltpu.with_memory_space_constraint(adapter_expand_weight, pltpu.HBM)
-    index = row_adapter_index.reshape(1, row_count)
     offsets = (2, 1, 3)
-    blocks = [from_owner(tokens, j) for j in offsets[1:]]
-
-    pieces = kernel_call(
-        functools.partial(cut_kernel, owner_count, offsets, far_width),
+    blocks = [from_owner(tokens, j) for j in offsets]
+
+    small = [
+        pltpu.with_memory_space_constraint(x, pltpu.HBM)
+        for x in (
+            adapter_slot_index.reshape(1, owner_count),
+            row_adapter_index.reshape(1, row_count),
+            tokens,
+            adapter_shrink_weight[0].T,
+        )
+    ]
+    cut = kernel_call(
+        functools.partial(cut_kernel, owner_count, offsets, far_width, len(small)),
         "cut_expand",
         1,
         1,
         1,
-        in_specs=[anywhere] * 2,
-        out_specs=[vmem] * (owner_count - 1),
-        out_shape=[pltpu.VMEM((rank_block, depth + near_width), bf16)]
-        + [pltpu.VMEM((rank_block, near_width), bf16)] * (owner_count - 2),
-        scratch_shapes=[pltpu.SemaphoreType.DMA((owner_count,))],
-    )(tokens, expand)
+        in_specs=[anywhere] * (1 + len(small)),
+        out_specs=[vmem] * (owner_count + len(small)),
+        out_shape=[pltpu.VMEM((rank_block, near_width), bf16)] * (owner_count - 1)
+        + [pltpu.VMEM((rank_block, columns), bf16)]
+        + [pltpu.VMEM(x.shape, x.dtype) for x in small],
+        scratch_shapes=[pltpu.SemaphoreType.DMA((owner_count + len(small),))],
+    )(expand, *small)
+    pieces, own = cut[: owner_count - 1], cut[owner_count - 1]
+    slots, index, mine, shrink = cut[owner_count:]
     near = [from_owner(piece, j) for piece, j in zip(pieces, offsets)]
 
     def split(count):
@@ -266,65 +272,47 @@
 
     parts = [(False, *span) for span in split(near_count)]
     parts += [(True, *span) for span in split(block_count - near_count)]
-    held_counts = [min(part[2], count) for part, count in zip(parts, (4, 4, 3, 3))]
     starts = [
         functools.partial(part_start, near_width, far_width, is_far, first * block)
         for is_far, first, _ in parts
     ]
-    held, own = kernel_call(
-        functools.partial(load_kernel, starts, held_counts, block),
-        "load_weights",
-        1,
-        1,
-        1,
-        in_specs=[anywhere] * 3,
-        out_specs=[vmem] * 2,
-        out_shape=[
-            pltpu.VMEM((sum(held_counts), depth, block), bf16),
-            pltpu.VMEM((rank_block, columns), bf16),
-        ],
-        scratch_shapes=[pltpu.SemaphoreType.DMA((sum(held_counts),)), pltpu.SemaphoreType.DMA],
-    )(weight, expand, pieces[0])
-
+    bands = 4
     rows, keep, send, slot = kernel_call(
         functools.partial(gather_kernel, (0, *offsets)),
         "gather_rows",
         1,
         1,
         4,
-        in_specs=[vmem] * (owner_count + 3) + [anywhere],
+        in_specs=[vmem] * (owner_count + 3),
         out_specs=[vmem] * 4,
         out_shape=[jax.ShapeDtypeStruct((row_count, depth), bf16)]
         + [jax.ShapeDtypeStruct((rank // 2, row_count), f32)] * 2
         + [jax.ShapeDtypeStruct((1, row_count), jnp.int32)],
         scratch_shapes=[pltpu.VMEM((row_count, depth), bf16), pltpu.VMEM((rank, row_count), f32)],
     )(
-        adapter_slot_index.reshape(1, owner_count),
+        slots,
         index,
-        tokens,
-        near[0],
+        mine,
         *blocks,
-        adapter_shrink_weight[0].T,
-        own,
+        shrink,
     )
 
     def base_part(n, *after):
         is_far, first, count = parts[n]
-        stream_count = max(1, count - held_counts[n])
         return kernel_call(
-            functools.partial(base_kernel, starts[n], block, sum(held_counts[:n]), held_counts[n]),
+            functools.partial(base_kernel, starts[n], block),
             "base_part",
             1 if is_far else 2 * row_count * depth * count * block,
             1 if is_far else 2 * depth * count * block,
-            4 + (stream_count * depth * block * 2 >> 20),
-            in_specs=[vmem, anywhere, vmem] + [anywhere] * len(after),
+            4 + (count * depth * block * 2 >> 20),
+            in_specs=[vmem, anywhere] + [anywhere] * len(after),
             out_specs=vmem,
             out_shape=jax.ShapeDtypeStruct((row_count, count * block), f32),
             scratch_shapes=[
-                pltpu.VMEM((stream_count, depth, block), bf16),
-                pltpu.SemaphoreType.DMA((stream_count,)),
+                pltpu.VMEM((count, depth, block), bf16),
+                pltpu.SemaphoreType.DMA((count, bands)),
             ],
-        )(rows, weight, held, *after)
+        )(rows, weight, *after)
 
     def delta_part(is_far, bases, pieces):
         start_of = functools.partial(part_start, near_width, far_width, is_far, 0)

time: 49.1 us -> 48.7 us (level)
  starting transfers between devices: 20.1 us -> 22.9 us
  local copies, waits for them, and re-layouts: 1.86 us -> 0.01 us
  Pallas kernels: 18.4 us -> 17.3 us
    ppermute x2, starting transfers between devices: 4.03 us -> 6.92 us  [from_mirror(): return lax.ppermute(x, 'adapter', [(s, s ^ m) for s in range(owner_count)])]
    unnamed x14 -> x0, local copies, waits for them, and re-layouts: 1.85 us -> none
    ppermute x2, waiting for transfers between devices: 1.66 us -> 0.01 us  [from_mirror(): return lax.ppermute(x, 'adapter', [(s, s ^ m) for s in range(owner_count)])]
    pallas_call x2, Pallas kernels: 1.66 us -> 0.7 us  [delta_part(): kernel_call(functools.partial(delta_kernel, owner_count, offsets, start_o...]
    ppermute x5 -> x6, waiting for transfers between devices: 0.01 us -> 0.95 us  [from_owner(): lax.ppermute(x, 'adapter', [(s, (s - j) % owner_count) for s in range(own...]
    ppermute x8, starting transfers between devices: 5.2 us -> 4.32 us  [from_tensor(): return lax.ppermute(x, 'tensor', [(s, s ^ m) for s in range(4)])]
    ppermute x5 -> x6, starting transfers between devices: 9.28 us -> 10.1 us  [from_owner(): lax.ppermute(x, 'adapter', [(s, (s - j) % owner_count) for s in range(own...]
    ppermute x8, waiting for transfers between devices: 5.64 us -> 6.18 us  [from_tensor(): return lax.ppermute(x, 'tensor', [(s, s ^ m) for s in range(4)])]
  transfers between devices with their start and end apart: 16 -> 17, of which waited for: 5 -> 5; matrix products, arithmetic and copies ran while one was open for 0% -> 0% of each run, Pallas kernels for 35% -> 36%
where the time goes in v6:
time: 48.7 us; the launch traced here: 48.5 us
  starting transfers between devices  22.9 us (47%)
  Pallas kernels  17.3 us (36%)
  waiting for transfers between devices  7.14 us (15%)
  other arithmetic  0.91 us (2%)
    pallas_call x4, Pallas kernels, base_part(): kernel_call(functools.partial(base_kernel, starts[n], block), 'base_part'...  15 us
    ppermute x6, starting transfers between devices, from_owner(): lax.ppermute(x, 'adapter', [(s, (s - j) % owner_count) for s in range(own...  10.1 us
    ppermute x2, starting transfers between devices, from_mirror(): return lax.ppermute(x, 'adapter', [(s, s ^ m) for s in range(owner_count)])  6.92 us
    ppermute x8, waiting for transfers between devices, from_tensor(): return lax.ppermute(x, 'tensor', [(s, s ^ m) for s in range(4)])  6.18 us
    ppermute x8, starting transfers between devices, from_tensor(): return lax.ppermute(x, 'tensor', [(s, s ^ m) for s in range(4)])  4.32 us
    ppermute x1, starting transfers between devices, from_group(): return lax.ppermute(x, 'groups', [(0, 1), (1, 0)])  1.64 us
    pallas_call x1, Pallas kernels, paired(): kernel_call(functools.partial(cut_kernel, owner_count, offsets, far_width...  1.38 us
  transfers between devices with their start and end apart: 17, of which 5 were waited for; matrix products, arithmetic and copies ran while one was open for 0% of the time, Pallas kernels for 36%

profile of v6, /device:TPU:0, one launch (start us, length us, event | category | flops | bytes accessed | tf_op | source)
XLA Modules:
  0.0 48.5 jit_solution(15097648261550246990)
XLA Ops:
  0.0 4.0 %collective-permute-start = (bf16[16,2048]{1,0:T(8,128)(2,1)}, bf16[16,2048]{1,0:T(8,128)(2,1)S(1)}, u32[]{:S(2)}, u32[]{:S(2)}) collective-permute-start(bf16[16,2048]{1,0:T(8,128)(2,1)} %refs_2_.1), channel_id=1, source_target_pairs={{0,8},{4,12},{8,0},{12,4},{1,9},{5,13},{9,1},{13,5},{2,10},{6,14},... | collective-permute-start | bytes 196616 | tf_op jit(solution)/shard_map/ppermute | solution.py:228
  4.0 1.3 %collective-permute-start.1 = (bf16[16,2048]{1,0:T(8,128)(2,1)}, bf16[16,2048]{1,0:T(8,128)(2,1)S(1)}, u32[]{:S(2)}, u32[]{:S(2)}) collective-permute-start(bf16[16,2048]{1,0:T(8,128)(2,1)} %refs_2_.1), channel_id=1, source_target_pairs={{0,12},{4,0},{8,4},{12,8},{1,13},{5,1},{9,5},{13,9},{2,14},{6,2},{... | collective-permute-start | bytes 196616 | tf_op jit(solution)/shard_map/ppermute | solution.py:228
  5.4 0.7 %collective-permute-start.2 = (bf16[16,2048]{1,0:T(8,128)(2,1)}, bf16[16,2048]{1,0:T(8,128)(2,1)S(1)}, u32[]{:S(2)}, u32[]{:S(2)}) collective-permute-start(bf16[16,2048]{1,0:T(8,128)(2,1)} %refs_2_.1), channel_id=1, source_target_pairs={{0,4},{4,8},{8,12},{12,0},{1,5},{5,9},{9,13},{13,1},{2,6},{6,10},{... | collective-permute-start | bytes 196616 | tf_op jit(solution)/shard_map/ppermute | solution.py:228
  6.1 1.4 %cut_expand.1 = (bf16[16,4096]{1,0:T(8,128)(2,1)S(1)}, bf16[16,4096]{1,0:T(8,128)(2,1)S(1)}, bf16[16,4096]{1,0:T(8,128)(2,1)S(1)}, bf16[16,7168]{1,0:T(8,128)(2,...) custom-call(bf16[1,16,28672]{2,1,0:T(8,128)(2,1)} %expand.1, ...), custom_call_target="tpu_custom_call" | custom-call | flops 1 | bytes 1 | tf_op jit(solution)/shard_map/cut_expand/pallas_call | solution.py:253
  7.5 1.1 %collective-permute-start.5 = (bf16[16,4096]{1,0:T(8,128)(2,1)S(1)}, bf16[16,4096]{1,0:T(8,128)(2,1)S(1)}, u32[]{:S(2)}, u32[]{:S(2)}) collective-permute-start(bf16[16,4096]{1,0:T(8,128)(2,1)S(1)} %get-tuple-element.46), channel_id=1, source_target_pairs={{0,8},{4,12},{8,0},{12,4},{1,9},{5,13},{9,1},{13,5},{2,10},{6,14},... | collective-permute-start | bytes 393224 | tf_op jit(solution)/shard_map/ppermute | solution.py:228
  8.5 2.9 %collective-permute-start.6 = (bf16[16,4096]{1,0:T(8,128)(2,1)S(1)}, bf16[16,4096]{1,0:T(8,128)(2,1)S(1)}, u32[]{:S(2)}, u32[]{:S(2)}) collective-permute-start(bf16[16,4096]{1,0:T(8,128)(2,1)S(1)} %get-tuple-element.47), channel_id=1, source_target_pairs={{0,12},{4,0},{8,4},{12,8},{1,13},{5,1},{9,5},{13,9},{2,14},{6,2},{... | collective-permute-start | bytes 393224 | tf_op jit(solution)/shard_map/ppermute | solution.py:228
  11.5 0.0 collective-permute-done.refs_1_
  11.5 0.0 collective-permute-start.7
  11.5 0.0 collective-permute-done.1.refs_2_
  11.5 0.9 %collective-permute-done.2.refs_3_ = bf16[16,2048]{1,0:T(8,128)(2,1)S(1)} collective-permute-done((bf16[16,2048]{1,0:T(8,128)(2,1)}, bf16[16,2048]{1,0:T(8,128)(2,1)S(1)}, u32[]{:S(2)}, u32[]{:S(2)}) %collective-permute-start.2) | collective-permute-done | bytes 65568 | tf_op jit(solution)/shard_map/ppermute | solution.py:228
  12.4 0.3 gather_rows.1
  12.7 0.1 collective-permute-start.3
  12.7 4.1 %base_part.4.refs_0_ = f32[64,2048]{1,0:T(8,128)S(1)} custom-call(bf16[64,2048]{1,0:T(8,128)(2,1)S(1)} %get-tuple-element.42.rows, bf16[2048,7168]{1,0:T(8,128)(2,1)} %weight.7, f32[32,64]{1,0:T(8,128)S(1)} %get-tuple-element.41.refs_0_), custom_call_target="tpu_custom_call" | custom-call | flops 536870912 | bytes 8388608 | tf_op jit(solution)/shard_map/base_part/pallas_call | solution.py:302
  16.8 0.0 collective-permute-done.3
  16.9 1.6 %collective-permute-start.4 = (f32[16,64]{1,0:T(8,128)S(1)}, f32[16,64]{1,0:T(8,128)S(1)}, u32[]{:S(2)}, u32[]{:S(2)}) collective-permute-start(f32[16,64]{1,0:T(8,128)S(1)} %slice.8), channel_id=1, source_target_pairs={{0,2},{1,3},{2,0},{3,1},{4,6},{5,7},{6,4},{7,5},{8,10},{9,11},{10,... | collective-permute-start | bytes 12296 | tf_op jit(solution)/shard_map/ppermute | solution.py:231
  18.4 4.0 %base_part.5.refs_1_ = f32[64,2048]{1,0:T(8,128)S(1)} custom-call(bf16[64,2048]{1,0:T(8,128)(2,1)S(1)} %get-tuple-element.42.rows, bf16[2048,7168]{1,0:T(8,128)(2,1)} %weight.7, f32[32,64]{1,0:T(8,128)S(1)} %add.30.refs_0_), custom_call_target="tpu_custom_call" | custom-call | flops 536870912 | bytes 8388608 | tf_op jit(solution)/shard_map/base_part/pallas_call | solution.py:302
  22.5 0.0 collective-permute-done.4
  22.5 0.0 collective-permute-done.5.refs_0_.refs_4_
  22.5 0.0 collective-permute-done.6.refs_1_.refs_5_
  22.5 0.0 collective-permute-done.7.refs_2_.refs_6_
  22.5 1.6 %collective-permute-start.13 = (bf16[48,3072]{1,0:T(8,128)(2,1)S(1)}, bf16[48,3072]{1,0:T(8,128)(2,1)S(1)}, u32[]{:S(2)}, u32[]{:S(2)}) collective-permute-start(bf16[48,3072]{1,0:T(8,128)(2,1)S(1)} %pack_far.1.refs_1_), channel_id=1, source_target_pairs={{0,16},{16,0},{1,17},{17,1},{2,18},{18,2},{3,19},{19,3},{4,20},{20... | collective-permute-start | bytes 884744 | tf_op jit(solution)/shard_map/ppermute | solution.py:237
  24.2 4.8 %collective-permute-start.8 = (bf16[16,64]{1,0:T(8,128)(2,1)S(1)}, bf16[16,64]{1,0:T(8,128)(2,1)S(1)}, u32[]{:S(2)}, u32[]{:S(2)}) collective-permute-start(bf16[16,64]{1,0:T(8,128)(2,1)S(1)} %fusion.1.refs_0_), channel_id=1, source_target_pairs={{0,4},{4,0},{8,12},{12,8},{1,5},{5,1},{9,13},{13,9},{2,6},{6,2},{1... | collective-permute-start | bytes 6152 | tf_op jit(solution)/shard_map/ppermute | solution.py:234
  29.0 3.4 %base_part.6.refs_0_ = f32[64,1536]{1,0:T(8,128)S(1)} custom-call(bf16[64,2048]{1,0:T(8,128)(2,1)S(1)} %get-tuple-element.42.rows, bf16[2048,7168]{1,0:T(8,128)(2,1)} %weight.7, bf16[16,64]{1,0:T(8,128)(2,1)S(1)} %fusion.1.refs_0_, bf16[48,3072]{1,0:T(8,128)(2,1)S(1)} %pack_far.1.refs_1_), custom_call_target="tpu_custom_call" | custom-call | flops 1 | bytes 1 | tf_op jit(solution)/shard_map/base_part/pallas_call | solution.py:302
  32.5 0.0 collective-permute-done.8
  32.5 2.1 %collective-permute-start.9 = (bf16[16,64]{1,0:T(8,128)(2,1)S(1)}, bf16[16,64]{1,0:T(8,128)(2,1)S(1)}, u32[]{:S(2)}, u32[]{:S(2)}) collective-permute-start(bf16[16,64]{1,0:T(8,128)(2,1)S(1)} %add.32.refs_0_), channel_id=1, source_target_pairs={{0,8},{4,12},{8,0},{12,4},{1,9},{5,13},{9,1},{13,5},{2,10},{6,14},... | collective-permute-start | bytes 6152 | tf_op jit(solution)/shard_map/ppermute | solution.py:234
  34.6 3.4 %base_part.7.refs_1_ = f32[64,1536]{1,0:T(8,128)S(1)} custom-call(bf16[64,2048]{1,0:T(8,128)(2,1)S(1)} %get-tuple-element.42.rows, bf16[2048,7168]{1,0:T(8,128)(2,1)} %weight.7, bf16[16,64]{1,0:T(8,128)(2,1)S(1)} %add.32.refs_0_, bf16[48,3072]{1,0:T(8,128)(2,1)S(1)} %pack_far.1.refs_1_), custom_call_target="tpu_custom_call" | custom-call | flops 1 | bytes 1 | tf_op jit(solution)/shard_map/base_part/pallas_call | solution.py:302
  38.0 0.0 collective-permute-done.9
  38.0 0.4 delta_part.2
  38.4 0.1 collective-permute-start.11
  38.5 0.5 %collective-permute-start.10 = (f32[16,4096]{1,0:T(8,128)S(1)}, f32[16,4096]{1,0:T(8,128)S(1)}, u32[]{:S(2)}, u32[]{:S(2)}) collective-permute-start(f32[16,4096]{1,0:T(8,128)S(1)} %get-tuple-element.58), channel_id=1, source_target_pairs={{0,1},{1,0},{2,3},{3,2},{4,5},{5,4},{6,7},{7,6},{8,9},{9,8},{10,11... | collective-permute-start | bytes 786440 | tf_op jit(solution)/shard_map/ppermute | solution.py:231
  39.0 0.0 collective-permute-done.13.refs_4_
  39.0 0.3 delta_part.3
  39.3 0.2 collective-permute-start.15
  39.5 0.5 %collective-permute-done.11 = f32[16,4096]{1,0:T(8,128)S(1)} collective-permute-done((f32[16,4096]{1,0:T(8,128)S(1)}, f32[16,4096]{1,0:T(8,128)S(1)}, u32[]{:S(2)}, u32[]{:S(2)}) %collective-permute-start.11) | collective-permute-done | bytes 262176 | tf_op jit(solution)/shard_map/ppermute | solution.py:231
  40.0 0.6 %collective-permute-start.12 = (bf16[16,4096]{1,0:T(8,128)(2,1)S(1)}, bf16[16,4096]{1,0:T(8,128)(2,1)S(1)}, u32[]{:S(2)}, u32[]{:S(2)}) collective-permute-start(bf16[16,4096]{1,0:T(8,128)(2,1)S(1)} %add_convert_fusion.1), channel_id=1, source_target_pairs={{0,2},{1,3},{2,0},{3,1},{4,6},{5,7},{6,4},{7,5},{8,10},{9,11},{10,... | collective-permute-start | bytes 393224 | tf_op jit(solution)/shard_map/ppermute | solution.py:231
  40.6 0.0 collective-permute-start.14
  40.6 0.2 collective-permute-done.15
  40.8 1.4 %collective-permute-start.16 = (bf16[16,3072]{1,0:T(8,128)(2,1)S(1)}, bf16[16,3072]{1,0:T(8,128)(2,1)S(1)}, u32[]{:S(2)}, u32[]{:S(2)}) collective-permute-start(bf16[16,3072]{1,0:T(8,128)(2,1)S(1)} %add_convert_fusion.3), channel_id=1, source_target_pairs={{0,2},{1,3},{2,0},{3,1},{4,6},{5,7},{6,4},{7,5},{8,10},{9,11},{10,... | collective-permute-start | bytes 294920 | tf_op jit(solution)/shard_map/ppermute | solution.py:231
  42.2 0.0 collective-permute-done.10
  42.2 4.2 %collective-permute-done.12 = bf16[16,4096]{1,0:T(8,128)(2,1)S(1)} collective-permute-done((bf16[16,4096]{1,0:T(8,128)(2,1)S(1)}, bf16[16,4096]{1,0:T(8,128)(2,1)S(1)}, u32[]{:S(2)}, u32[]{:S(2)}) %collective-permute-start.12) | collective-permute-done | bytes 131104 | tf_op jit(solution)/shard_map/ppermute | solution.py:231
  46.5 0.0 collective-permute-done.14
  46.5 1.2 %collective-permute-done.16 = bf16[16,3072]{1,0:T(8,128)(2,1)S(1)} collective-permute-done((bf16[16,3072]{1,0:T(8,128)(2,1)S(1)}, bf16[16,3072]{1,0:T(8,128)(2,1)S(1)}, u32[]{:S(2)}, u32[]{:S(2)}) %collective-permute-start.16) | collective-permute-done | bytes 98336 | tf_op jit(solution)/shard_map/ppermute | solution.py:231
  47.8 0.7 %maximum_select_fusion = bf16[16,7168]{1,0:T(8,128)(2,1)} fusion(bf16[16,3072]{1,0:T(8,128)(2,1)S(1)} %add_convert_fusion.2, bf16[16,4096]{1,0:T(8,128)(2,1)S(1)} %add_convert_fusion, pred[]{:T(512)S(6)} %eq.3), kind=kLoop, calls=%fused_computation.2 | loop fusion | flops 1032192 | bytes 458753 | tf_op jit(solution)/shard_map/jit(_where)/select_n | solution.py:378
  (10 shorter events, 0.2 us)
Async XLA Ops:
  0.0 11.5 %collective-permute-start = (bf16[16,2048]{1,0:T(8,128)(2,1)}, bf16[16,2048]{1,0:T(8,128)(2,1)S(1)}, u32[]{:S(2)}, u32[]{:S(2)}) collective-permute-start(bf16[16,2048]{1,0:T(8,128)(2,1)} %refs_2_.1), channel_id=1, source_target_pairs={{0,8},{4,12},{8,0},{12,4},{1,9},{5,13},{9,1},{13,5},{2,10},{6,14},... | collective-permute-start | bytes 196616 | tf_op jit(solution)/shard_map/ppermute | solution.py:228
  4.0 7.4 %collective-permute-start.1 = (bf16[16,2048]{1,0:T(8,128)(2,1)}, bf16[16,2048]{1,0:T(8,128)(2,1)S(1)}, u32[]{:S(2)}, u32[]{:S(2)}) collective-permute-start(bf16[16,2048]{1,0:T(8,128)(2,1)} %refs_2_.1), channel_id=1, source_target_pairs={{0,12},{4,0},{8,4},{12,8},{1,13},{5,1},{9,5},{13,9},{2,14},{6,2},{... | collective-permute-start | bytes 196616 | tf_op jit(solution)/shard_map/ppermute | solution.py:228
  5.4 7.0 %collective-permute-start.2 = (bf16[16,2048]{1,0:T(8,128)(2,1)}, bf16[16,2048]{1,0:T(8,128)(2,1)S(1)}, u32[]{:S(2)}, u32[]{:S(2)}) collective-permute-start(bf16[16,2048]{1,0:T(8,128)(2,1)} %refs_2_.1), channel_id=1, source_target_pairs={{0,4},{4,8},{8,12},{12,0},{1,5},{5,9},{9,13},{13,1},{2,6},{6,10},{... | collective-permute-start | bytes 196616 | tf_op jit(solution)/shard_map/ppermute | solution.py:228
  7.5 15.0 %collective-permute-start.5 = (bf16[16,4096]{1,0:T(8,128)(2,1)S(1)}, bf16[16,4096]{1,0:T(8,128)(2,1)S(1)}, u32[]{:S(2)}, u32[]{:S(2)}) collective-permute-start(bf16[16,4096]{1,0:T(8,128)(2,1)S(1)} %get-tuple-element.46), channel_id=1, source_target_pairs={{0,8},{4,12},{8,0},{12,4},{1,9},{5,13},{9,1},{13,5},{2,10},{6,14},... | collective-permute-start | bytes 393224 | tf_op jit(solution)/shard_map/ppermute | solution.py:228
  8.5 13.9 %collective-permute-start.6 = (bf16[16,4096]{1,0:T(8,128)(2,1)S(1)}, bf16[16,4096]{1,0:T(8,128)(2,1)S(1)}, u32[]{:S(2)}, u32[]{:S(2)}) collective-permute-start(bf16[16,4096]{1,0:T(8,128)(2,1)S(1)} %get-tuple-element.47), channel_id=1, source_target_pairs={{0,12},{4,0},{8,4},{12,8},{1,13},{5,1},{9,5},{13,9},{2,14},{6,2},{... | collective-permute-start | bytes 393224 | tf_op jit(solution)/shard_map/ppermute | solution.py:228
  11.5 11.0 %collective-permute-start.7 = (bf16[16,4096]{1,0:T(8,128)(2,1)S(1)}, bf16[16,4096]{1,0:T(8,128)(2,1)S(1)}, u32[]{:S(2)}, u32[]{:S(2)}) collective-permute-start(bf16[16,4096]{1,0:T(8,128)(2,1)S(1)} %get-tuple-element.48), channel_id=1, source_target_pairs={{0,4},{4,8},{8,12},{12,0},{1,5},{5,9},{9,13},{13,1},{2,6},{6,10},{... | collective-permute-start | bytes 393224 | tf_op jit(solution)/shard_map/ppermute | solution.py:228
  12.7 4.2 %collective-permute-start.3 = (f32[32,64]{1,0:T(8,128)S(1)}, f32[32,64]{1,0:T(8,128)S(1)}, u32[]{:S(2)}, u32[]{:S(2)}) collective-permute-start(f32[32,64]{1,0:T(8,128)S(1)} %get-tuple-element.41.refs_0_), channel_id=1, source_target_pairs={{0,1},{1,0},{2,3},{3,2},{4,5},{5,4},{6,7},{7,6},{8,9},{9,8},{10,11... | collective-permute-start | bytes 24584 | tf_op jit(solution)/shard_map/ppermute | solution.py:231
  16.9 5.6 %collective-permute-start.4 = (f32[16,64]{1,0:T(8,128)S(1)}, f32[16,64]{1,0:T(8,128)S(1)}, u32[]{:S(2)}, u32[]{:S(2)}) collective-permute-start(f32[16,64]{1,0:T(8,128)S(1)} %slice.8), channel_id=1, source_target_pairs={{0,2},{1,3},{2,0},{3,1},{4,6},{5,7},{6,4},{7,5},{8,10},{9,11},{10,... | collective-permute-start | bytes 12296 | tf_op jit(solution)/shard_map/ppermute | solution.py:231
  22.5 16.4 %collective-permute-start.13 = (bf16[48,3072]{1,0:T(8,128)(2,1)S(1)}, bf16[48,3072]{1,0:T(8,128)(2,1)S(1)}, u32[]{:S(2)}, u32[]{:S(2)}) collective-permute-start(bf16[48,3072]{1,0:T(8,128)(2,1)S(1)} %pack_far.1.refs_1_), channel_id=1, source_target_pairs={{0,16},{16,0},{1,17},{17,1},{2,18},{18,2},{3,19},{19,3},{4,20},{20... | collective-permute-start | bytes 884744 | tf_op jit(solution)/shard_map/ppermute | solution.py:237
  24.2 8.3 %collective-permute-start.8 = (bf16[16,64]{1,0:T(8,128)(2,1)S(1)}, bf16[16,64]{1,0:T(8,128)(2,1)S(1)}, u32[]{:S(2)}, u32[]{:S(2)}) collective-permute-start(bf16[16,64]{1,0:T(8,128)(2,1)S(1)} %fusion.1.refs_0_), channel_id=1, source_target_pairs={{0,4},{4,0},{8,12},{12,8},{1,5},{5,1},{9,13},{13,9},{2,6},{6,2},{1... | collective-permute-start | bytes 6152 | tf_op jit(solution)/shard_map/ppermute | solution.py:234
  32.5 5.5 %collective-permute-start.9 = (bf16[16,64]{1,0:T(8,128)(2,1)S(1)}, bf16[16,64]{1,0:T(8,128)(2,1)S(1)}, u32[]{:S(2)}, u32[]{:S(2)}) collective-permute-start(bf16[16,64]{1,0:T(8,128)(2,1)S(1)} %add.32.refs_0_), channel_id=1, source_target_pairs={{0,8},{4,12},{8,0},{12,4},{1,9},{5,13},{9,1},{13,5},{2,10},{6,14},... | collective-permute-start | bytes 6152 | tf_op jit(solution)/shard_map/ppermute | solution.py:234
  38.4 1.6 %collective-permute-start.11 = (f32[16,4096]{1,0:T(8,128)S(1)}, f32[16,4096]{1,0:T(8,128)S(1)}, u32[]{:S(2)}, u32[]{:S(2)}) collective-permute-start(f32[16,4096]{1,0:T(8,128)S(1)} %get-tuple-element.60), channel_id=1, source_target_pairs={{0,1},{1,0},{2,3},{3,2},{4,5},{5,4},{6,7},{7,6},{8,9},{9,8},{10,11... | collective-permute-start | bytes 786440 | tf_op jit(solution)/shard_map/ppermute | solution.py:231
  38.5 3.7 %collective-permute-start.10 = (f32[16,4096]{1,0:T(8,128)S(1)}, f32[16,4096]{1,0:T(8,128)S(1)}, u32[]{:S(2)}, u32[]{:S(2)}) collective-permute-start(f32[16,4096]{1,0:T(8,128)S(1)} %get-tuple-element.58), channel_id=1, source_target_pairs={{0,1},{1,0},{2,3},{3,2},{4,5},{5,4},{6,7},{7,6},{8,9},{9,8},{10,11... | collective-permute-start | bytes 786440 | tf_op jit(solution)/shard_map/ppermute | solution.py:231
  39.3 1.5 %collective-permute-start.15 = (f32[16,3072]{1,0:T(8,128)S(1)}, f32[16,3072]{1,0:T(8,128)S(1)}, u32[]{:S(2)}, u32[]{:S(2)}) collective-permute-start(f32[16,3072]{1,0:T(8,128)S(1)} %get-tuple-element.66), channel_id=1, source_target_pairs={{0,1},{1,0},{2,3},{3,2},{4,5},{5,4},{6,7},{7,6},{8,9},{9,8},{10,11... | collective-permute-start | bytes 589832 | tf_op jit(solution)/shard_map/ppermute | solution.py:231
  40.0 6.4 %collective-permute-start.12 = (bf16[16,4096]{1,0:T(8,128)(2,1)S(1)}, bf16[16,4096]{1,0:T(8,128)(2,1)S(1)}, u32[]{:S(2)}, u32[]{:S(2)}) collective-permute-start(bf16[16,4096]{1,0:T(8,128)(2,1)S(1)} %add_convert_fusion.1), channel_id=1, source_target_pairs={{0,2},{1,3},{2,0},{3,1},{4,6},{5,7},{6,4},{7,5},{8,10},{9,11},{10,... | collective-permute-start | bytes 393224 | tf_op jit(solution)/shard_map/ppermute | solution.py:231
  40.6 5.8 %collective-permute-start.14 = (f32[16,3072]{1,0:T(8,128)S(1)}, f32[16,3072]{1,0:T(8,128)S(1)}, u32[]{:S(2)}, u32[]{:S(2)}) collective-permute-start(f32[16,3072]{1,0:T(8,128)S(1)} %get-tuple-element.64), channel_id=1, source_target_pairs={{0,1},{1,0},{2,3},{3,2},{4,5},{5,4},{6,7},{7,6},{8,9},{9,8},{10,11... | collective-permute-start | bytes 589832 | tf_op jit(solution)/shard_map/ppermute | solution.py:231
  40.8 6.9 %collective-permute-start.16 = (bf16[16,3072]{1,0:T(8,128)(2,1)S(1)}, bf16[16,3072]{1,0:T(8,128)(2,1)S(1)}, u32[]{:S(2)}, u32[]{:S(2)}) collective-permute-start(bf16[16,3072]{1,0:T(8,128)(2,1)S(1)} %add_convert_fusion.3), channel_id=1, source_target_pairs={{0,2},{1,3},{2,0},{3,1},{4,6},{5,7},{6,4},{7,5},{8,10},{9,11},{10,... | collective-permute-start | bytes 294920 | tf_op jit(solution)/shard_map/ppermute | solution.py:231

commit v7 on v6

--- a/solution.py
+++ b/solution.py
@@ -60,10 +60,10 @@
     )
 
 
-def cut_kernel(owner_count, offsets, far_width, small_count, expand, *refs):
+def cut_kernel(owner_count, offsets, far_width, start_of, block, small_count, expand, weight, *refs):
     small, refs = refs[:small_count], refs[small_count:]
     *pieces, own = refs[: owner_count]
-    loaded, sem = refs[owner_count:-1], refs[-1]
+    *loaded, held, sem, held_sem = refs[owner_count:]
     g, a = lax.axis_index("groups"), lax.axis_index("adapter")
     near_width = pieces[0].shape[1]
     columns = near_width + far_width
@@ -79,6 +79,8 @@
         )
     for n, (source, target) in enumerate(zip(small, loaded)):
         copies.append(pltpu.make_async_copy(source, target, sem.at[owner_count + n]))
+    for bands in weight_copies(start_of(), block, weight, held, held_sem):
+        copies += bands
     for copy in copies:
         copy.start()
     for copy in copies:
@@ -138,18 +140,22 @@
     return ((1 - g) * near_width if is_far else g * far_width) + first
 
 
-def base_kernel(start_of, block, rows, weight, *refs):
-    total, streamed, sem = refs[-3:]
-    copies = weight_copies(start_of(), block, weight, streamed, sem)
-    for bands in copies:
-        for copy in bands:
-            copy.start()
-    for n, bands in enumerate(copies):
-        for copy in bands:
-            copy.wait()
+def base_kernel(next_start_of, block, rows, weight, held, *refs):
+    copies = []
+    if next_start_of is None:
+        total = refs[-1]
+    else:
+        total, ahead, sem = refs[-3:]
+        for bands in weight_copies(next_start_of(), block, weight, ahead, sem):
+            copies += bands
+    for copy in copies:
+        copy.start()
+    for n in range(held.shape[0]):
         total[:, n * block : (n + 1) * block] = jnp.dot(
-            rows[...], streamed[n], preferred_element_type=f32
+            rows[...], held[n], preferred_element_type=f32
         )
+    for copy in copies:
+        copy.wait()
 
 
 def forward_kernel(far_width, *refs):
@@ -241,6 +247,16 @@
     offsets = (2, 1, 3)
     blocks = [from_owner(tokens, j) for j in offsets]
 
+    def split(count):
+        return [(0, count - count // 2), (count - count // 2, count // 2)]
+
+    parts = [(False, *span) for span in split(near_count)]
+    parts += [(True, *span) for span in split(block_count - near_count)]
+    starts = [
+        functools.partial(part_start, near_width, far_width, is_far, first * block)
+        for is_far, first, _ in parts
+    ]
+    bands = 4
     small = [
         pltpu.with_memory_space_constraint(x, pltpu.HBM)
         for x in (
@@ -251,32 +267,28 @@
         )
     ]
     cut = kernel_call(
-        functools.partial(cut_kernel, owner_count, offsets, far_width, len(small)),
+        functools.partial(
+            cut_kernel, owner_count, offsets, far_width, starts[0], block, len(small)
+        ),
         "cut_expand",
         1,
         1,
         1,
-        in_specs=[anywhere] * (1 + len(small)),
-        out_specs=[vmem] * (owner_count + len(small)),
+        in_specs=[anywhere] * (2 + len(small)),
+        out_specs=[vmem] * (owner_count + len(small) + 1),
         out_shape=[pltpu.VMEM((rank_block, near_width), bf16)] * (owner_count - 1)
         + [pltpu.VMEM((rank_block, columns), bf16)]
-        + [pltpu.VMEM(x.shape, x.dtype) for x in small],
-        scratch_shapes=[pltpu.SemaphoreType.DMA((owner_count + len(small),))],
-    )(expand, *small)
+        + [pltpu.VMEM(x.shape, x.dtype) for x in small]
+        + [pltpu.VMEM((parts[0][2], depth, block), bf16)],
+        scratch_shapes=[
+            pltpu.SemaphoreType.DMA((owner_count + len(small),)),
+            pltpu.SemaphoreType.DMA((parts[0][2], bands)),
+        ],
+    )(expand, weight, *small)
     pieces, own = cut[: owner_count - 1], cut[owner_count - 1]
-    slots, index, mine, shrink = cut[owner_count:]
+    slots, index, mine, shrink, held = cut[owner_count:]
     near = [from_owner(piece, j) for piece, j in zip(pieces, offsets)]
 
-    def split(count):
-        return [(0, count - count // 2), (count - count // 2, count // 2)]
-
-    parts = [(False, *span) for span in split(near_count)]
-    parts += [(True, *span) for span in split(block_count - near_count)]
-    starts = [
-        functools.partial(part_start, near_width, far_width, is_far, first * block)
-        for is_far, first, _ in parts
-    ]
-    bands = 4
     rows, keep, send, slot = kernel_call(
         functools.partial(gather_kernel, (0, *offsets)),
         "gather_rows",
@@ -297,22 +309,23 @@
         shrink,
     )
 
-    def base_part(n, *after):
-        is_far, first, count = parts[n]
+    def base_part(n, held, *after):
+        is_far, _, count = parts[n]
+        ahead, next_start_of = [], None
+        if n + 1 < len(parts):
+            ahead = [pltpu.VMEM((parts[n + 1][2], depth, block), bf16)]
+            next_start_of = starts[n + 1]
         return kernel_call(
-            functools.partial(base_kernel, starts[n], block),
+            functools.partial(base_kernel, next_start_of, block),
             "base_part",
             1 if is_far else 2 * row_count * depth * count * block,
             1 if is_far else 2 * depth * count * block,
-            4 + (count * depth * block * 2 >> 20),
-            in_specs=[vmem, anywhere] + [anywhere] * len(after),
-            out_specs=vmem,
-            out_shape=jax.ShapeDtypeStruct((row_count, count * block), f32),
-            scratch_shapes=[
-                pltpu.VMEM((count, depth, block), bf16),
-                pltpu.SemaphoreType.DMA((count, bands)),
-            ],
-        )(rows, weight, *after)
+            4,
+            in_specs=[vmem, anywhere, vmem] + [anywhere] * len(after),
+            out_specs=[vmem] * (1 + len(ahead)),
+            out_shape=[jax.ShapeDtypeStruct((row_count, count * block), f32)] + ahead,
+            scratch_shapes=[pltpu.SemaphoreType.DMA((x.shape[0], bands)) for x in ahead],
+        )(rows, weight, held, *after)
 
     def delta_part(is_far, bases, pieces):
         start_of = functools.partial(part_start, near_width, far_width, is_far, 0)
@@ -335,11 +348,11 @@
         )(slot, *bases, own, shrunk, *pieces)
 
     arrived = from_tensor(send, 1)
-    base_0 = base_part(0, send)
+    base_0, held = base_part(0, held, send)
     arrived, base_0 = lax.optimization_barrier((arrived, base_0))
     pair = keep + arrived
     arrived = from_tensor(pair[rank_block:], 2)
-    base_1 = base_part(1, pair)
+    base_1, held = base_part(1, held, pair)
     arrived, base_1, *near = lax.optimization_barrier((arrived, base_1, *near))
     shrunk = (adapter_scale * (pair[:rank_block] + arrived)).astype(bf16)
     packed = kernel_call(
@@ -358,10 +371,10 @@
     while m < owner_count:
         steps.append(m)
         m *= 2
-    base_far = []
+    base_far, held = [], [held]
     for m, n in zip(steps, (2, 3)):
         arrived = from_mirror(shrunk, m)
-        base = base_part(n, shrunk, packed)
+        base, *held = base_part(n, *held, shrunk, packed)
         arrived, base = lax.optimization_barrier((arrived, base))
         base_far.append(base)
         shrunk = shrunk + arrived

time: 48.7 us -> 48 us (0.986)
  starting transfers between devices: 22.9 us -> 20.3 us
  Pallas kernels: 17.3 us -> 19.6 us
    pallas_call x1, Pallas kernels: 1.38 us -> 4 us  [paired(): kernel_call(functools.partial(cut_kernel, owner_count, offsets, far_width...]
    ppermute x2, starting transfers between devices: 6.92 us -> 4.44 us  [from_mirror(): return lax.ppermute(x, 'adapter', [(s, s ^ m) for s in range(owner_count)])]
    ppermute x6, waiting for transfers between devices: 0.95 us -> 0.02 us  [from_owner(): lax.ppermute(x, 'adapter', [(s, (s - j) % owner_count) for s in range(own...]
    ppermute x2, waiting for transfers between devices: 0.01 us -> 0.67 us  [from_mirror(): return lax.ppermute(x, 'adapter', [(s, s ^ m) for s in range(owner_count)])]
  transfers between devices with their start and end apart: 17 -> 17, of which waited for: 5 -> 5; matrix products, arithmetic and copies ran while one was open for 0% -> 0% of each run, Pallas kernels for 36% -> 41%
where the time goes in v7:
time: 48 us; the launch traced here: 47.9 us
  starting transfers between devices  20.3 us (42%)
  Pallas kernels  19.6 us (41%)
  waiting for transfers between devices  6.86 us (14%)
  other arithmetic  0.91 us (2%)
    pallas_call x4, Pallas kernels, base_part(): kernel_call(functools.partial(base_kernel, next_start_of, block), 'base_p...  14.6 us
    ppermute x6, starting transfers between devices, from_owner(): lax.ppermute(x, 'adapter', [(s, (s - j) % owner_count) for s in range(own...  10 us
    ppermute x8, waiting for transfers between devices, from_tensor(): return lax.ppermute(x, 'tensor', [(s, s ^ m) for s in range(4)])  6.17 us
    ppermute x2, starting transfers between devices, from_mirror(): return lax.ppermute(x, 'adapter', [(s, s ^ m) for s in range(owner_count)])  4.44 us
    ppermute x8, starting transfers between devices, from_tensor(): return lax.ppermute(x, 'tensor', [(s, s ^ m) for s in range(4)])  4.33 us
    pallas_call x1, Pallas kernels, paired(): kernel_call(functools.partial(cut_kernel, owner_count, offsets, far_width...  4 us
    ppermute x1, starting transfers between devices, from_group(): return lax.ppermute(x, 'groups', [(0, 1), (1, 0)])  1.52 us
  transfers between devices with their start and end apart: 17, of which 5 were waited for; matrix products, arithmetic and copies ran while one was open for 0% of the time, Pallas kernels for 41%

profile of v7, /device:TPU:0, one launch (start us, length us, event | category | flops | bytes accessed | tf_op | source)
XLA Modules:
  0.0 47.9 jit_solution(12995454811153277458)
XLA Ops:
  0.0 4.0 %collective-permute-start = (bf16[16,2048]{1,0:T(8,128)(2,1)}, bf16[16,2048]{1,0:T(8,128)(2,1)S(1)}, u32[]{:S(2)}, u32[]{:S(2)}) collective-permute-start(bf16[16,2048]{1,0:T(8,128)(2,1)} %refs_2_.1), channel_id=1, source_target_pairs={{0,8},{4,12},{8,0},{12,4},{1,9},{5,13},{9,1},{13,5},{2,10},{6,14},... | collective-permute-start | bytes 196616 | tf_op jit(solution)/shard_map/ppermute | solution.py:234
  4.0 1.3 %collective-permute-start.1 = (bf16[16,2048]{1,0:T(8,128)(2,1)}, bf16[16,2048]{1,0:T(8,128)(2,1)S(1)}, u32[]{:S(2)}, u32[]{:S(2)}) collective-permute-start(bf16[16,2048]{1,0:T(8,128)(2,1)} %refs_2_.1), channel_id=1, source_target_pairs={{0,12},{4,0},{8,4},{12,8},{1,13},{5,1},{9,5},{13,9},{2,14},{6,2},{... | collective-permute-start | bytes 196616 | tf_op jit(solution)/shard_map/ppermute | solution.py:234
  5.4 0.7 %collective-permute-start.2 = (bf16[16,2048]{1,0:T(8,128)(2,1)}, bf16[16,2048]{1,0:T(8,128)(2,1)S(1)}, u32[]{:S(2)}, u32[]{:S(2)}) collective-permute-start(bf16[16,2048]{1,0:T(8,128)(2,1)} %refs_2_.1), channel_id=1, source_target_pairs={{0,4},{4,8},{8,12},{12,0},{1,5},{5,9},{9,13},{13,1},{2,6},{6,10},{... | collective-permute-start | bytes 196616 | tf_op jit(solution)/shard_map/ppermute | solution.py:234
  6.1 4.0 %cut_expand.1 = (bf16[16,4096]{1,0:T(8,128)(2,1)S(1)}, bf16[16,4096]{1,0:T(8,128)(2,1)S(1)}, bf16[16,4096]{1,0:T(8,128)(2,1)S(1)}, bf16[16,7168]{1,0:T(8,128)(2,...) custom-call(bf16[1,16,28672]{2,1,0:T(8,128)(2,1)} %expand.1, ...), custom_call_target="tpu_custom_call" | custom-call | flops 1 | bytes 1 | tf_op jit(solution)/shard_map/cut_expand/pallas_call | solution.py:269
  10.1 1.0 %collective-permute-start.5 = (bf16[16,4096]{1,0:T(8,128)(2,1)S(1)}, bf16[16,4096]{1,0:T(8,128)(2,1)S(1)}, u32[]{:S(2)}, u32[]{:S(2)}) collective-permute-start(bf16[16,4096]{1,0:T(8,128)(2,1)S(1)} %get-tuple-element.57), channel_id=1, source_target_pairs={{0,8},{4,12},{8,0},{12,4},{1,9},{5,13},{9,1},{13,5},{2,10},{6,14},... | collective-permute-start | bytes 393224 | tf_op jit(solution)/shard_map/ppermute | solution.py:234
  11.1 2.9 %collective-permute-start.6 = (bf16[16,4096]{1,0:T(8,128)(2,1)S(1)}, bf16[16,4096]{1,0:T(8,128)(2,1)S(1)}, u32[]{:S(2)}, u32[]{:S(2)}) collective-permute-start(bf16[16,4096]{1,0:T(8,128)(2,1)S(1)} %get-tuple-element.58), channel_id=1, source_target_pairs={{0,12},{4,0},{8,4},{12,8},{1,13},{5,1},{9,5},{13,9},{2,14},{6,2},{... | collective-permute-start | bytes 393224 | tf_op jit(solution)/shard_map/ppermute | solution.py:234
  14.1 0.0 collective-permute-done.refs_1_
  14.1 0.0 collective-permute-start.7
  14.1 0.0 collective-permute-done.1.refs_2_
  14.1 0.0 collective-permute-done.2.refs_3_
  14.1 0.3 gather_rows.1
  14.3 0.1 collective-permute-start.3
  14.4 5.0 %base_part.4 = (f32[64,2048]{1,0:T(8,128)S(1)}, bf16[4,2048,512]{2,1,0:T(8,128)(2,1)S(1)}) custom-call(bf16[64,2048]{1,0:T(8,128)(2,1)S(1)} %get-tuple-element.49.rows, bf16[2048,7168]{1,0:T(8,128)(2,1)} %weight.9, bf16[4,2048,512]{2,1,0:T(8,128)(2,1)S(1)} %get-tuple-element.50.held, f32[32,64]{1,0:T(8,128)S(1)} %get-tuple-element.48.refs_0_), custom_call_target="tpu_custom_call" | custom-call | flops 536870912 | bytes 8388608 | tf_op jit(solution)/shard_map/base_part/pallas_call | solution.py:318
  19.4 0.0 collective-permute-done.3
  19.4 1.6 %collective-permute-start.4 = (f32[16,64]{1,0:T(8,128)S(1)}, f32[16,64]{1,0:T(8,128)S(1)}, u32[]{:S(2)}, u32[]{:S(2)}) collective-permute-start(f32[16,64]{1,0:T(8,128)S(1)} %slice.8), channel_id=1, source_target_pairs={{0,2},{1,3},{2,0},{3,1},{4,6},{5,7},{6,4},{7,5},{8,10},{9,11},{10,... | collective-permute-start | bytes 12296 | tf_op jit(solution)/shard_map/ppermute | solution.py:237
  21.0 4.4 %base_part.5 = (f32[64,2048]{1,0:T(8,128)S(1)}, bf16[3,2048,512]{2,1,0:T(8,128)(2,1)S(1)}) custom-call(bf16[64,2048]{1,0:T(8,128)(2,1)S(1)} %get-tuple-element.49.rows, bf16[2048,7168]{1,0:T(8,128)(2,1)} %weight.9, bf16[4,2048,512]{2,1,0:T(8,128)(2,1)S(1)} %get-tuple-element.55.held, f32[32,64]{1,0:T(8,128)S(1)} %add.30.refs_0_), custom_call_target="tpu_custom_call" | custom-call | flops 536870912 | bytes 8388608 | tf_op jit(solution)/shard_map/base_part/pallas_call | solution.py:318
  25.4 0.0 collective-permute-done.4
  25.4 0.0 collective-permute-done.5.refs_0_.refs_4_
  25.4 0.0 collective-permute-done.6.refs_1_.refs_5_
  25.4 0.0 collective-permute-done.7.refs_2_.refs_6_
  25.5 1.5 %collective-permute-start.13 = (bf16[48,3072]{1,0:T(8,128)(2,1)S(1)}, bf16[48,3072]{1,0:T(8,128)(2,1)S(1)}, u32[]{:S(2)}, u32[]{:S(2)}) collective-permute-start(bf16[48,3072]{1,0:T(8,128)(2,1)S(1)} %pack_far.1.refs_1_), channel_id=1, source_target_pairs={{0,16},{16,0},{1,17},{17,1},{2,18},{18,2},{3,19},{19,3},{4,20},{20... | collective-permute-start | bytes 884744 | tf_op jit(solution)/shard_map/ppermute | solution.py:243
  27.0 1.8 %collective-permute-start.8 = (bf16[16,64]{1,0:T(8,128)(2,1)S(1)}, bf16[16,64]{1,0:T(8,128)(2,1)S(1)}, u32[]{:S(2)}, u32[]{:S(2)}) collective-permute-start(bf16[16,64]{1,0:T(8,128)(2,1)S(1)} %fusion.1.refs_0_), channel_id=1, source_target_pairs={{0,4},{4,0},{8,12},{12,8},{1,5},{5,1},{9,13},{13,9},{2,6},{6,2},{1... | collective-permute-start | bytes 6152 | tf_op jit(solution)/shard_map/ppermute | solution.py:240
  28.7 4.0 %base_part.6 = (f32[64,1536]{1,0:T(8,128)S(1)}, bf16[3,2048,512]{2,1,0:T(8,128)(2,1)S(1)}) custom-call(bf16[64,2048]{1,0:T(8,128)(2,1)S(1)} %get-tuple-element.49.rows, bf16[2048,7168]{1,0:T(8,128)(2,1)} %weight.9, bf16[3,2048,512]{2,1,0:T(8,128)(2,1)S(1)} %get-tuple-element.63.held, bf16[16,64]{1,0:T(8,128)(2,1)S(1)} %fusion.1.refs_0_, ...), custom_call_target="tpu_custom_call" | custom-call | flops 1 | bytes 1 | tf_op jit(solution)/shard_map/base_part/pallas_call | solution.py:318
  32.7 0.0 collective-permute-done.8
  32.8 2.7 %collective-permute-start.9 = (bf16[16,64]{1,0:T(8,128)(2,1)S(1)}, bf16[16,64]{1,0:T(8,128)(2,1)S(1)}, u32[]{:S(2)}, u32[]{:S(2)}) collective-permute-start(bf16[16,64]{1,0:T(8,128)(2,1)S(1)} %add.32.refs_0_), channel_id=1, source_target_pairs={{0,8},{4,12},{8,0},{12,4},{1,9},{5,13},{9,1},{13,5},{2,10},{6,14},... | collective-permute-start | bytes 6152 | tf_op jit(solution)/shard_map/ppermute | solution.py:240
  35.5 1.2 %base_part.7.refs_1_ = f32[64,1536]{1,0:T(8,128)S(1)} custom-call(bf16[64,2048]{1,0:T(8,128)(2,1)S(1)} %get-tuple-element.49.rows, bf16[2048,7168]{1,0:T(8,128)(2,1)} %weight.9, bf16[3,2048,512]{2,1,0:T(8,128)(2,1)S(1)} %get-tuple-element.69.held, bf16[16,64]{1,0:T(8,128)(2,1)S(1)} %add.32.refs_0_, bf16[48,3072]{1,0:T(8,128)(2,1)S(1)} %pack_far.1.refs_1_), custom_call_target="tpu_custom_call" | custom-call | flops 1 | bytes 1 | tf_op jit(solution)/shard_map/base_part/pallas_call | solution.py:318
  36.7 0.7 %collective-permute-done.9 = bf16[16,64]{1,0:T(8,128)(2,1)S(1)} collective-permute-done((bf16[16,64]{1,0:T(8,128)(2,1)S(1)}, bf16[16,64]{1,0:T(8,128)(2,1)S(1)}, u32[]{:S(2)}, u32[]{:S(2)}) %collective-permute-start.9) | collective-permute-done | bytes 2080 | tf_op jit(solution)/shard_map/ppermute | solution.py:240
  37.4 0.4 delta_part.2
  37.7 0.1 collective-permute-start.11
  37.8 0.5 %collective-permute-start.10 = (f32[16,4096]{1,0:T(8,128)S(1)}, f32[16,4096]{1,0:T(8,128)S(1)}, u32[]{:S(2)}, u32[]{:S(2)}) collective-permute-start(f32[16,4096]{1,0:T(8,128)S(1)} %get-tuple-element.72), channel_id=1, source_target_pairs={{0,1},{1,0},{2,3},{3,2},{4,5},{5,4},{6,7},{7,6},{8,9},{9,8},{10,11... | collective-permute-start | bytes 786440 | tf_op jit(solution)/shard_map/ppermute | solution.py:237
  38.3 0.0 collective-permute-done.13.refs_4_
  38.3 0.3 delta_part.3
  38.6 0.2 collective-permute-start.15
  38.8 0.5 %collective-permute-done.11 = f32[16,4096]{1,0:T(8,128)S(1)} collective-permute-done((f32[16,4096]{1,0:T(8,128)S(1)}, f32[16,4096]{1,0:T(8,128)S(1)}, u32[]{:S(2)}, u32[]{:S(2)}) %collective-permute-start.11) | collective-permute-done | bytes 262176 | tf_op jit(solution)/shard_map/ppermute | solution.py:237
  39.4 0.6 %collective-permute-start.12 = (bf16[16,4096]{1,0:T(8,128)(2,1)S(1)}, bf16[16,4096]{1,0:T(8,128)(2,1)S(1)}, u32[]{:S(2)}, u32[]{:S(2)}) collective-permute-start(bf16[16,4096]{1,0:T(8,128)(2,1)S(1)} %add_convert_fusion.1), channel_id=1, source_target_pairs={{0,2},{1,3},{2,0},{3,1},{4,6},{5,7},{6,4},{7,5},{8,10},{9,11},{10,... | collective-permute-start | bytes 393224 | tf_op jit(solution)/shard_map/ppermute | solution.py:237
  40.0 0.0 collective-permute-start.14
  40.0 0.2 collective-permute-done.15
  40.2 1.4 %collective-permute-start.16 = (bf16[16,3072]{1,0:T(8,128)(2,1)S(1)}, bf16[16,3072]{1,0:T(8,128)(2,1)S(1)}, u32[]{:S(2)}, u32[]{:S(2)}) collective-permute-start(bf16[16,3072]{1,0:T(8,128)(2,1)S(1)} %add_convert_fusion.3), channel_id=1, source_target_pairs={{0,2},{1,3},{2,0},{3,1},{4,6},{5,7},{6,4},{7,5},{8,10},{9,11},{10,... | collective-permute-start | bytes 294920 | tf_op jit(solution)/shard_map/ppermute | solution.py:237
  41.6 0.0 collective-permute-done.10
  41.6 4.2 %collective-permute-done.12 = bf16[16,4096]{1,0:T(8,128)(2,1)S(1)} collective-permute-done((bf16[16,4096]{1,0:T(8,128)(2,1)S(1)}, bf16[16,4096]{1,0:T(8,128)(2,1)S(1)}, u32[]{:S(2)}, u32[]{:S(2)}) %collective-permute-start.12) | collective-permute-done | bytes 131104 | tf_op jit(solution)/shard_map/ppermute | solution.py:237
  45.8 0.0 collective-permute-done.14
  45.8 1.2 %collective-permute-done.16 = bf16[16,3072]{1,0:T(8,128)(2,1)S(1)} collective-permute-done((bf16[16,3072]{1,0:T(8,128)(2,1)S(1)}, bf16[16,3072]{1,0:T(8,128)(2,1)S(1)}, u32[]{:S(2)}, u32[]{:S(2)}) %collective-permute-start.16) | collective-permute-done | bytes 98336 | tf_op jit(solution)/shard_map/ppermute | solution.py:237
  47.1 0.7 %maximum_select_fusion = bf16[16,7168]{1,0:T(8,128)(2,1)} fusion(bf16[16,3072]{1,0:T(8,128)(2,1)S(1)} %add_convert_fusion.2, bf16[16,4096]{1,0:T(8,128)(2,1)S(1)} %add_convert_fusion, pred[]{:T(512)S(6)} %eq.3), kind=kLoop, calls=%fused_computation.2 | loop fusion | flops 1032192 | bytes 458753 | tf_op jit(solution)/shard_map/jit(_where)/select_n | solution.py:391
  (10 shorter events, 0.2 us)
Async XLA Ops:
  0.0 14.1 %collective-permute-start = (bf16[16,2048]{1,0:T(8,128)(2,1)}, bf16[16,2048]{1,0:T(8,128)(2,1)S(1)}, u32[]{:S(2)}, u32[]{:S(2)}) collective-permute-start(bf16[16,2048]{1,0:T(8,128)(2,1)} %refs_2_.1), channel_id=1, source_target_pairs={{0,8},{4,12},{8,0},{12,4},{1,9},{5,13},{9,1},{13,5},{2,10},{6,14},... | collective-permute-start | bytes 196616 | tf_op jit(solution)/shard_map/ppermute | solution.py:234
  4.0 10.0 %collective-permute-start.1 = (bf16[16,2048]{1,0:T(8,128)(2,1)}, bf16[16,2048]{1,0:T(8,128)(2,1)S(1)}, u32[]{:S(2)}, u32[]{:S(2)}) collective-permute-start(bf16[16,2048]{1,0:T(8,128)(2,1)} %refs_2_.1), channel_id=1, source_target_pairs={{0,12},{4,0},{8,4},{12,8},{1,13},{5,1},{9,5},{13,9},{2,14},{6,2},{... | collective-permute-start | bytes 196616 | tf_op jit(solution)/shard_map/ppermute | solution.py:234
  5.4 8.7 %collective-permute-start.2 = (bf16[16,2048]{1,0:T(8,128)(2,1)}, bf16[16,2048]{1,0:T(8,128)(2,1)S(1)}, u32[]{:S(2)}, u32[]{:S(2)}) collective-permute-start(bf16[16,2048]{1,0:T(8,128)(2,1)} %refs_2_.1), channel_id=1, source_target_pairs={{0,4},{4,8},{8,12},{12,0},{1,5},{5,9},{9,13},{13,1},{2,6},{6,10},{... | collective-permute-start | bytes 196616 | tf_op jit(solution)/shard_map/ppermute | solution.py:234
  10.1 15.3 %collective-permute-start.5 = (bf16[16,4096]{1,0:T(8,128)(2,1)S(1)}, bf16[16,4096]{1,0:T(8,128)(2,1)S(1)}, u32[]{:S(2)}, u32[]{:S(2)}) collective-permute-start(bf16[16,4096]{1,0:T(8,128)(2,1)S(1)} %get-tuple-element.57), channel_id=1, source_target_pairs={{0,8},{4,12},{8,0},{12,4},{1,9},{5,13},{9,1},{13,5},{2,10},{6,14},... | collective-permute-start | bytes 393224 | tf_op jit(solution)/shard_map/ppermute | solution.py:234
  11.1 14.3 %collective-permute-start.6 = (bf16[16,4096]{1,0:T(8,128)(2,1)S(1)}, bf16[16,4096]{1,0:T(8,128)(2,1)S(1)}, u32[]{:S(2)}, u32[]{:S(2)}) collective-permute-start(bf16[16,4096]{1,0:T(8,128)(2,1)S(1)} %get-tuple-element.58), channel_id=1, source_target_pairs={{0,12},{4,0},{8,4},{12,8},{1,13},{5,1},{9,5},{13,9},{2,14},{6,2},{... | collective-permute-start | bytes 393224 | tf_op jit(solution)/shard_map/ppermute | solution.py:234
  14.1 11.4 %collective-permute-start.7 = (bf16[16,4096]{1,0:T(8,128)(2,1)S(1)}, bf16[16,4096]{1,0:T(8,128)(2,1)S(1)}, u32[]{:S(2)}, u32[]{:S(2)}) collective-permute-start(bf16[16,4096]{1,0:T(8,128)(2,1)S(1)} %get-tuple-element.59), channel_id=1, source_target_pairs={{0,4},{4,8},{8,12},{12,0},{1,5},{5,9},{9,13},{13,1},{2,6},{6,10},{... | collective-permute-start | bytes 393224 | tf_op jit(solution)/shard_map/ppermute | solution.py:234
  14.3 5.1 %collective-permute-start.3 = (f32[32,64]{1,0:T(8,128)S(1)}, f32[32,64]{1,0:T(8,128)S(1)}, u32[]{:S(2)}, u32[]{:S(2)}) collective-permute-start(f32[32,64]{1,0:T(8,128)S(1)} %get-tuple-element.48.refs_0_), channel_id=1, source_target_pairs={{0,1},{1,0},{2,3},{3,2},{4,5},{5,4},{6,7},{7,6},{8,9},{9,8},{10,11... | collective-permute-start | bytes 24584 | tf_op jit(solution)/shard_map/ppermute | solution.py:237
  19.4 5.9 %collective-permute-start.4 = (f32[16,64]{1,0:T(8,128)S(1)}, f32[16,64]{1,0:T(8,128)S(1)}, u32[]{:S(2)}, u32[]{:S(2)}) collective-permute-start(f32[16,64]{1,0:T(8,128)S(1)} %slice.8), channel_id=1, source_target_pairs={{0,2},{1,3},{2,0},{3,1},{4,6},{5,7},{6,4},{7,5},{8,10},{9,11},{10,... | collective-permute-start | bytes 12296 | tf_op jit(solution)/shard_map/ppermute | solution.py:237
  25.5 12.8 %collective-permute-start.13 = (bf16[48,3072]{1,0:T(8,128)(2,1)S(1)}, bf16[48,3072]{1,0:T(8,128)(2,1)S(1)}, u32[]{:S(2)}, u32[]{:S(2)}) collective-permute-start(bf16[48,3072]{1,0:T(8,128)(2,1)S(1)} %pack_far.1.refs_1_), channel_id=1, source_target_pairs={{0,16},{16,0},{1,17},{17,1},{2,18},{18,2},{3,19},{19,3},{4,20},{20... | collective-permute-start | bytes 884744 | tf_op jit(solution)/shard_map/ppermute | solution.py:243
  27.0 5.8 %collective-permute-start.8 = (bf16[16,64]{1,0:T(8,128)(2,1)S(1)}, bf16[16,64]{1,0:T(8,128)(2,1)S(1)}, u32[]{:S(2)}, u32[]{:S(2)}) collective-permute-start(bf16[16,64]{1,0:T(8,128)(2,1)S(1)} %fusion.1.refs_0_), channel_id=1, source_target_pairs={{0,4},{4,0},{8,12},{12,8},{1,5},{5,1},{9,13},{13,9},{2,6},{6,2},{1... | collective-permute-start | bytes 6152 | tf_op jit(solution)/shard_map/ppermute | solution.py:240
  32.8 4.6 %collective-permute-start.9 = (bf16[16,64]{1,0:T(8,128)(2,1)S(1)}, bf16[16,64]{1,0:T(8,128)(2,1)S(1)}, u32[]{:S(2)}, u32[]{:S(2)}) collective-permute-start(bf16[16,64]{1,0:T(8,128)(2,1)S(1)} %add.32.refs_0_), channel_id=1, source_target_pairs={{0,8},{4,12},{8,0},{12,4},{1,9},{5,13},{9,1},{13,5},{2,10},{6,14},... | collective-permute-start | bytes 6152 | tf_op jit(solution)/shard_map/ppermute | solution.py:240
  37.7 1.6 %collective-permute-start.11 = (f32[16,4096]{1,0:T(8,128)S(1)}, f32[16,4096]{1,0:T(8,128)S(1)}, u32[]{:S(2)}, u32[]{:S(2)}) collective-permute-start(f32[16,4096]{1,0:T(8,128)S(1)} %get-tuple-element.74), channel_id=1, source_target_pairs={{0,1},{1,0},{2,3},{3,2},{4,5},{5,4},{6,7},{7,6},{8,9},{9,8},{10,11... | collective-permute-start | bytes 786440 | tf_op jit(solution)/shard_map/ppermute | solution.py:237
  37.8 3.7 %collective-permute-start.10 = (f32[16,4096]{1,0:T(8,128)S(1)}, f32[16,4096]{1,0:T(8,128)S(1)}, u32[]{:S(2)}, u32[]{:S(2)}) collective-permute-start(f32[16,4096]{1,0:T(8,128)S(1)} %get-tuple-element.72), channel_id=1, source_target_pairs={{0,1},{1,0},{2,3},{3,2},{4,5},{5,4},{6,7},{7,6},{8,9},{9,8},{10,11... | collective-permute-start | bytes 786440 | tf_op jit(solution)/shard_map/ppermute | solution.py:237
  38.6 1.5 %collective-permute-start.15 = (f32[16,3072]{1,0:T(8,128)S(1)}, f32[16,3072]{1,0:T(8,128)S(1)}, u32[]{:S(2)}, u32[]{:S(2)}) collective-permute-start(f32[16,3072]{1,0:T(8,128)S(1)} %get-tuple-element.80), channel_id=1, source_target_pairs={{0,1},{1,0},{2,3},{3,2},{4,5},{5,4},{6,7},{7,6},{8,9},{9,8},{10,11... | collective-permute-start | bytes 589832 | tf_op jit(solution)/shard_map/ppermute | solution.py:237
  39.4 6.4 %collective-permute-start.12 = (bf16[16,4096]{1,0:T(8,128)(2,1)S(1)}, bf16[16,4096]{1,0:T(8,128)(2,1)S(1)}, u32[]{:S(2)}, u32[]{:S(2)}) collective-permute-start(bf16[16,4096]{1,0:T(8,128)(2,1)S(1)} %add_convert_fusion.1), channel_id=1, source_target_pairs={{0,2},{1,3},{2,0},{3,1},{4,6},{5,7},{6,4},{7,5},{8,10},{9,11},{10,... | collective-permute-start | bytes 393224 | tf_op jit(solution)/shard_map/ppermute | solution.py:237
  40.0 5.8 %collective-permute-start.14 = (f32[16,3072]{1,0:T(8,128)S(1)}, f32[16,3072]{1,0:T(8,128)S(1)}, u32[]{:S(2)}, u32[]{:S(2)}) collective-permute-start(f32[16,3072]{1,0:T(8,128)S(1)} %get-tuple-element.78), channel_id=1, source_target_pairs={{0,1},{1,0},{2,3},{3,2},{4,5},{5,4},{6,7},{7,6},{8,9},{9,8},{10,11... | collective-permute-start | bytes 589832 | tf_op jit(solution)/shard_map/ppermute | solution.py:237
  40.2 6.9 %collective-permute-start.16 = (bf16[16,3072]{1,0:T(8,128)(2,1)S(1)}, bf16[16,3072]{1,0:T(8,128)(2,1)S(1)}, u32[]{:S(2)}, u32[]{:S(2)}) collective-permute-start(bf16[16,3072]{1,0:T(8,128)(2,1)S(1)} %add_convert_fusion.3), channel_id=1, source_target_pairs={{0,2},{1,3},{2,0},{3,1},{4,6},{5,7},{6,4},{7,5},{8,10},{9,11},{10,... | collective-permute-start | bytes 294920 | tf_op jit(solution)/shard_map/ppermute | solution.py:237

commit v8 on v7

--- a/solution.py
+++ b/solution.py
@@ -150,10 +150,14 @@
             copies += bands
     for copy in copies:
         copy.start()
-    for n in range(held.shape[0]):
-        total[:, n * block : (n + 1) * block] = jnp.dot(
-            rows[...], held[n], preferred_element_type=f32
-        )
+
+    @pl.when(lax.axis_index("tensor") >= 0)
+    def _():
+        for n in range(held.shape[0]):
+            total[:, n * block : (n + 1) * block] = jnp.dot(
+                rows[...], held[n], preferred_element_type=f32
+            )
+
     for copy in copies:
         copy.wait()
 

time: 48 us -> 44.2 us (0.921)
  Pallas kernels: 19.6 us -> 15.7 us
    pallas_call x4, Pallas kernels: 14.6 us -> 10.7 us  [base_part(): kernel_call(functools.partial(base_kernel, next_start_of, block), 'base_p...]
  transfers between devices with their start and end apart: 17 -> 17, of which waited for: 5 -> 4; matrix products, arithmetic and copies ran while one was open for 0% -> 0% of each run, Pallas kernels for 41% -> 36%
where the time goes in v8:
time: 44.2 us; the launch traced here: 44 us
  starting transfers between devices  20.7 us (47%)
  Pallas kernels  15.7 us (36%)
  waiting for transfers between devices  6.55 us (15%)
  other arithmetic  0.91 us (2%)
    pallas_call x4, Pallas kernels, base_part(): kernel_call(functools.partial(base_kernel, next_start_of, block), 'base_p...  10.7 us
    ppermute x6, starting transfers between devices, from_owner(): lax.ppermute(x, 'adapter', [(s, (s - j) % owner_count) for s in range(own...  10 us
    ppermute x8, waiting for transfers between devices, from_tensor(): return lax.ppermute(x, 'tensor', [(s, s ^ m) for s in range(4)])  5.82 us
    ppermute x8, starting transfers between devices, from_tensor(): return lax.ppermute(x, 'tensor', [(s, s ^ m) for s in range(4)])  4.68 us
    ppermute x2, starting transfers between devices, from_mirror(): return lax.ppermute(x, 'adapter', [(s, s ^ m) for s in range(owner_count)])  4.43 us
    pallas_call x1, Pallas kernels, paired(): kernel_call(functools.partial(cut_kernel, owner_count, offsets, far_width...  4 us
    ppermute x1, starting transfers between devices, from_group(): return lax.ppermute(x, 'groups', [(0, 1), (1, 0)])  1.52 us
  transfers between devices with their start and end apart: 17, of which 4 were waited for; matrix products, arithmetic and copies ran while one was open for 0% of the time, Pallas kernels for 36%

profile of v8, /device:TPU:0, one launch (start us, length us, event | category | flops | bytes accessed | tf_op | source)
XLA Modules:
  0.0 44.0 jit_solution(4304670727916140707)
XLA Ops:
  0.0 4.0 %collective-permute-start = (bf16[16,2048]{1,0:T(8,128)(2,1)}, bf16[16,2048]{1,0:T(8,128)(2,1)S(1)}, u32[]{:S(2)}, u32[]{:S(2)}) collective-permute-start(bf16[16,2048]{1,0:T(8,128)(2,1)} %refs_2_.1), channel_id=1, source_target_pairs={{0,8},{4,12},{8,0},{12,4},{1,9},{5,13},{9,1},{13,5},{2,10},{6,14},... | collective-permute-start | bytes 196616 | tf_op jit(solution)/shard_map/ppermute | solution.py:238
  4.0 1.3 %collective-permute-start.1 = (bf16[16,2048]{1,0:T(8,128)(2,1)}, bf16[16,2048]{1,0:T(8,128)(2,1)S(1)}, u32[]{:S(2)}, u32[]{:S(2)}) collective-permute-start(bf16[16,2048]{1,0:T(8,128)(2,1)} %refs_2_.1), channel_id=1, source_target_pairs={{0,12},{4,0},{8,4},{12,8},{1,13},{5,1},{9,5},{13,9},{2,14},{6,2},{... | collective-permute-start | bytes 196616 | tf_op jit(solution)/shard_map/ppermute | solution.py:238
  5.4 0.7 %collective-permute-start.2 = (bf16[16,2048]{1,0:T(8,128)(2,1)}, bf16[16,2048]{1,0:T(8,128)(2,1)S(1)}, u32[]{:S(2)}, u32[]{:S(2)}) collective-permute-start(bf16[16,2048]{1,0:T(8,128)(2,1)} %refs_2_.1), channel_id=1, source_target_pairs={{0,4},{4,8},{8,12},{12,0},{1,5},{5,9},{9,13},{13,1},{2,6},{6,10},{... | collective-permute-start | bytes 196616 | tf_op jit(solution)/shard_map/ppermute | solution.py:238
  6.1 4.0 %cut_expand.1 = (bf16[16,4096]{1,0:T(8,128)(2,1)S(1)}, bf16[16,4096]{1,0:T(8,128)(2,1)S(1)}, bf16[16,4096]{1,0:T(8,128)(2,1)S(1)}, bf16[16,7168]{1,0:T(8,128)(2,...) custom-call(bf16[1,16,28672]{2,1,0:T(8,128)(2,1)} %expand.1, ...), custom_call_target="tpu_custom_call" | custom-call | flops 1 | bytes 1 | tf_op jit(solution)/shard_map/cut_expand/pallas_call | solution.py:273
  10.1 1.0 %collective-permute-start.5 = (bf16[16,4096]{1,0:T(8,128)(2,1)S(1)}, bf16[16,4096]{1,0:T(8,128)(2,1)S(1)}, u32[]{:S(2)}, u32[]{:S(2)}) collective-permute-start(bf16[16,4096]{1,0:T(8,128)(2,1)S(1)} %get-tuple-element.57), channel_id=1, source_target_pairs={{0,8},{4,12},{8,0},{12,4},{1,9},{5,13},{9,1},{13,5},{2,10},{6,14},... | collective-permute-start | bytes 393224 | tf_op jit(solution)/shard_map/ppermute | solution.py:238
  11.1 2.9 %collective-permute-start.6 = (bf16[16,4096]{1,0:T(8,128)(2,1)S(1)}, bf16[16,4096]{1,0:T(8,128)(2,1)S(1)}, u32[]{:S(2)}, u32[]{:S(2)}) collective-permute-start(bf16[16,4096]{1,0:T(8,128)(2,1)S(1)} %get-tuple-element.58), channel_id=1, source_target_pairs={{0,12},{4,0},{8,4},{12,8},{1,13},{5,1},{9,5},{13,9},{2,14},{6,2},{... | collective-permute-start | bytes 393224 | tf_op jit(solution)/shard_map/ppermute | solution.py:238
  14.1 0.0 collective-permute-done.refs_1_
  14.1 0.0 collective-permute-start.7
  14.1 0.0 collective-permute-done.1.refs_2_
  14.1 0.0 collective-permute-done.2.refs_3_
  14.1 0.3 gather_rows.1
  14.3 0.1 collective-permute-start.3
  14.4 3.6 %base_part.4 = (f32[64,2048]{1,0:T(8,128)S(1)}, bf16[4,2048,512]{2,1,0:T(8,128)(2,1)S(1)}) custom-call(bf16[64,2048]{1,0:T(8,128)(2,1)S(1)} %get-tuple-element.49.rows, bf16[2048,7168]{1,0:T(8,128)(2,1)} %weight.9, bf16[4,2048,512]{2,1,0:T(8,128)(2,1)S(1)} %get-tuple-element.50.held, f32[32,64]{1,0:T(8,128)S(1)} %get-tuple-element.48.refs_0_), custom_call_target="tpu_custom_call" | custom-call | flops 536870912 | bytes 8388608 | tf_op jit(solution)/shard_map/base_part/pallas_call | solution.py:322
  18.0 0.0 collective-permute-done.3
  18.1 1.6 %collective-permute-start.4 = (f32[16,64]{1,0:T(8,128)S(1)}, f32[16,64]{1,0:T(8,128)S(1)}, u32[]{:S(2)}, u32[]{:S(2)}) collective-permute-start(f32[16,64]{1,0:T(8,128)S(1)} %slice.8), channel_id=1, source_target_pairs={{0,2},{1,3},{2,0},{3,1},{4,6},{5,7},{6,4},{7,5},{8,10},{9,11},{10,... | collective-permute-start | bytes 12296 | tf_op jit(solution)/shard_map/ppermute | solution.py:241
  19.6 3.0 %base_part.5 = (f32[64,2048]{1,0:T(8,128)S(1)}, bf16[3,2048,512]{2,1,0:T(8,128)(2,1)S(1)}) custom-call(bf16[64,2048]{1,0:T(8,128)(2,1)S(1)} %get-tuple-element.49.rows, bf16[2048,7168]{1,0:T(8,128)(2,1)} %weight.9, bf16[4,2048,512]{2,1,0:T(8,128)(2,1)S(1)} %get-tuple-element.55.held, f32[32,64]{1,0:T(8,128)S(1)} %add.30.refs_0_), custom_call_target="tpu_custom_call" | custom-call | flops 536870912 | bytes 8388608 | tf_op jit(solution)/shard_map/base_part/pallas_call | solution.py:322
  22.6 0.0 collective-permute-done.4
  22.6 0.0 collective-permute-done.5.refs_0_.refs_4_
  22.6 0.0 collective-permute-done.6.refs_1_.refs_5_
  22.6 0.0 collective-permute-done.7.refs_2_.refs_6_
  22.7 1.5 %collective-permute-start.13 = (bf16[48,3072]{1,0:T(8,128)(2,1)S(1)}, bf16[48,3072]{1,0:T(8,128)(2,1)S(1)}, u32[]{:S(2)}, u32[]{:S(2)}) collective-permute-start(bf16[48,3072]{1,0:T(8,128)(2,1)S(1)} %pack_far.1.refs_1_), channel_id=1, source_target_pairs={{0,16},{16,0},{1,17},{17,1},{2,18},{18,2},{3,19},{19,3},{4,20},{20... | collective-permute-start | bytes 884744 | tf_op jit(solution)/shard_map/ppermute | solution.py:247
  24.2 1.8 %collective-permute-start.8 = (bf16[16,64]{1,0:T(8,128)(2,1)S(1)}, bf16[16,64]{1,0:T(8,128)(2,1)S(1)}, u32[]{:S(2)}, u32[]{:S(2)}) collective-permute-start(bf16[16,64]{1,0:T(8,128)(2,1)S(1)} %fusion.1.refs_0_), channel_id=1, source_target_pairs={{0,4},{4,0},{8,12},{12,8},{1,5},{5,1},{9,13},{13,9},{2,6},{6,2},{1... | collective-permute-start | bytes 6152 | tf_op jit(solution)/shard_map/ppermute | solution.py:244
  26.0 2.9 %base_part.6 = (f32[64,1536]{1,0:T(8,128)S(1)}, bf16[3,2048,512]{2,1,0:T(8,128)(2,1)S(1)}) custom-call(bf16[64,2048]{1,0:T(8,128)(2,1)S(1)} %get-tuple-element.49.rows, bf16[2048,7168]{1,0:T(8,128)(2,1)} %weight.9, bf16[3,2048,512]{2,1,0:T(8,128)(2,1)S(1)} %get-tuple-element.63.held, bf16[16,64]{1,0:T(8,128)(2,1)S(1)} %fusion.1.refs_0_, ...), custom_call_target="tpu_custom_call" | custom-call | flops 1 | bytes 1 | tf_op jit(solution)/shard_map/base_part/pallas_call | solution.py:322
  28.9 0.0 collective-permute-done.8
  28.9 2.6 %collective-permute-start.9 = (bf16[16,64]{1,0:T(8,128)(2,1)S(1)}, bf16[16,64]{1,0:T(8,128)(2,1)S(1)}, u32[]{:S(2)}, u32[]{:S(2)}) collective-permute-start(bf16[16,64]{1,0:T(8,128)(2,1)S(1)} %add.32.refs_0_), channel_id=1, source_target_pairs={{0,8},{4,12},{8,0},{12,4},{1,9},{5,13},{9,1},{13,5},{2,10},{6,14},... | collective-permute-start | bytes 6152 | tf_op jit(solution)/shard_map/ppermute | solution.py:244
  31.6 1.2 %base_part.7.refs_1_ = f32[64,1536]{1,0:T(8,128)S(1)} custom-call(bf16[64,2048]{1,0:T(8,128)(2,1)S(1)} %get-tuple-element.49.rows, bf16[2048,7168]{1,0:T(8,128)(2,1)} %weight.9, bf16[3,2048,512]{2,1,0:T(8,128)(2,1)S(1)} %get-tuple-element.69.held, bf16[16,64]{1,0:T(8,128)(2,1)S(1)} %add.32.refs_0_, bf16[48,3072]{1,0:T(8,128)(2,1)S(1)} %pack_far.1.refs_1_), custom_call_target="tpu_custom_call" | custom-call | flops 1 | bytes 1 | tf_op jit(solution)/shard_map/base_part/pallas_call | solution.py:322
  32.8 0.7 %collective-permute-done.9 = bf16[16,64]{1,0:T(8,128)(2,1)S(1)} collective-permute-done((bf16[16,64]{1,0:T(8,128)(2,1)S(1)}, bf16[16,64]{1,0:T(8,128)(2,1)S(1)}, u32[]{:S(2)}, u32[]{:S(2)}) %collective-permute-start.9) | collective-permute-done | bytes 2080 | tf_op jit(solution)/shard_map/ppermute | solution.py:244
  33.5 0.4 delta_part.2
  33.9 0.1 collective-permute-start.11
  34.0 0.5 %collective-permute-start.10 = (f32[16,4096]{1,0:T(8,128)S(1)}, f32[16,4096]{1,0:T(8,128)S(1)}, u32[]{:S(2)}, u32[]{:S(2)}) collective-permute-start(f32[16,4096]{1,0:T(8,128)S(1)} %get-tuple-element.72), channel_id=1, source_target_pairs={{0,1},{1,0},{2,3},{3,2},{4,5},{5,4},{6,7},{7,6},{8,9},{9,8},{10,11... | collective-permute-start | bytes 786440 | tf_op jit(solution)/shard_map/ppermute | solution.py:241
  34.5 0.0 collective-permute-done.13.refs_4_
  34.5 0.3 delta_part.3
  34.8 0.2 collective-permute-start.15
  35.0 0.5 %collective-permute-done.11 = f32[16,4096]{1,0:T(8,128)S(1)} collective-permute-done((f32[16,4096]{1,0:T(8,128)S(1)}, f32[16,4096]{1,0:T(8,128)S(1)}, u32[]{:S(2)}, u32[]{:S(2)}) %collective-permute-start.11) | collective-permute-done | bytes 262176 | tf_op jit(solution)/shard_map/ppermute | solution.py:241
  35.6 1.6 %collective-permute-start.12 = (bf16[16,4096]{1,0:T(8,128)(2,1)S(1)}, bf16[16,4096]{1,0:T(8,128)(2,1)S(1)}, u32[]{:S(2)}, u32[]{:S(2)}) collective-permute-start(bf16[16,4096]{1,0:T(8,128)(2,1)S(1)} %add_convert_fusion.1), channel_id=1, source_target_pairs={{0,2},{1,3},{2,0},{3,1},{4,6},{5,7},{6,4},{7,5},{8,10},{9,11},{10,... | collective-permute-start | bytes 393224 | tf_op jit(solution)/shard_map/ppermute | solution.py:241
  37.1 0.0 collective-permute-start.14
  37.1 0.0 collective-permute-done.15
  37.1 0.8 %collective-permute-start.16 = (bf16[16,3072]{1,0:T(8,128)(2,1)S(1)}, bf16[16,3072]{1,0:T(8,128)(2,1)S(1)}, u32[]{:S(2)}, u32[]{:S(2)}) collective-permute-start(bf16[16,3072]{1,0:T(8,128)(2,1)S(1)} %add_convert_fusion.3), channel_id=1, source_target_pairs={{0,2},{1,3},{2,0},{3,1},{4,6},{5,7},{6,4},{7,5},{8,10},{9,11},{10,... | collective-permute-start | bytes 294920 | tf_op jit(solution)/shard_map/ppermute | solution.py:241
  37.9 0.0 collective-permute-done.10
  37.9 4.0 %collective-permute-done.12 = bf16[16,4096]{1,0:T(8,128)(2,1)S(1)} collective-permute-done((bf16[16,4096]{1,0:T(8,128)(2,1)S(1)}, bf16[16,4096]{1,0:T(8,128)(2,1)S(1)}, u32[]{:S(2)}, u32[]{:S(2)}) %collective-permute-start.12) | collective-permute-done | bytes 131104 | tf_op jit(solution)/shard_map/ppermute | solution.py:241
  42.0 0.0 collective-permute-done.14
  42.0 1.2 %collective-permute-done.16 = bf16[16,3072]{1,0:T(8,128)(2,1)S(1)} collective-permute-done((bf16[16,3072]{1,0:T(8,128)(2,1)S(1)}, bf16[16,3072]{1,0:T(8,128)(2,1)S(1)}, u32[]{:S(2)}, u32[]{:S(2)}) %collective-permute-start.16) | collective-permute-done | bytes 98336 | tf_op jit(solution)/shard_map/ppermute | solution.py:241
  43.3 0.7 %maximum_select_fusion = bf16[16,7168]{1,0:T(8,128)(2,1)} fusion(bf16[16,3072]{1,0:T(8,128)(2,1)S(1)} %add_convert_fusion.2, bf16[16,4096]{1,0:T(8,128)(2,1)S(1)} %add_convert_fusion, pred[]{:T(512)S(6)} %eq.3), kind=kLoop, calls=%fused_computation.2 | loop fusion | flops 1032192 | bytes 458753 | tf_op jit(solution)/shard_map/jit(_where)/select_n | solution.py:395
  (10 shorter events, 0.2 us)
Async XLA Ops:
  0.0 14.1 %collective-permute-start = (bf16[16,2048]{1,0:T(8,128)(2,1)}, bf16[16,2048]{1,0:T(8,128)(2,1)S(1)}, u32[]{:S(2)}, u32[]{:S(2)}) collective-permute-start(bf16[16,2048]{1,0:T(8,128)(2,1)} %refs_2_.1), channel_id=1, source_target_pairs={{0,8},{4,12},{8,0},{12,4},{1,9},{5,13},{9,1},{13,5},{2,10},{6,14},... | collective-permute-start | bytes 196616 | tf_op jit(solution)/shard_map/ppermute | solution.py:238
  4.0 10.0 %collective-permute-start.1 = (bf16[16,2048]{1,0:T(8,128)(2,1)}, bf16[16,2048]{1,0:T(8,128)(2,1)S(1)}, u32[]{:S(2)}, u32[]{:S(2)}) collective-permute-start(bf16[16,2048]{1,0:T(8,128)(2,1)} %refs_2_.1), channel_id=1, source_target_pairs={{0,12},{4,0},{8,4},{12,8},{1,13},{5,1},{9,5},{13,9},{2,14},{6,2},{... | collective-permute-start | bytes 196616 | tf_op jit(solution)/shard_map/ppermute | solution.py:238
  5.4 8.7 %collective-permute-start.2 = (bf16[16,2048]{1,0:T(8,128)(2,1)}, bf16[16,2048]{1,0:T(8,128)(2,1)S(1)}, u32[]{:S(2)}, u32[]{:S(2)}) collective-permute-start(bf16[16,2048]{1,0:T(8,128)(2,1)} %refs_2_.1), channel_id=1, source_target_pairs={{0,4},{4,8},{8,12},{12,0},{1,5},{5,9},{9,13},{13,1},{2,6},{6,10},{... | collective-permute-start | bytes 196616 | tf_op jit(solution)/shard_map/ppermute | solution.py:238
  10.1 12.5 %collective-permute-start.5 = (bf16[16,4096]{1,0:T(8,128)(2,1)S(1)}, bf16[16,4096]{1,0:T(8,128)(2,1)S(1)}, u32[]{:S(2)}, u32[]{:S(2)}) collective-permute-start(bf16[16,4096]{1,0:T(8,128)(2,1)S(1)} %get-tuple-element.57), channel_id=1, source_target_pairs={{0,8},{4,12},{8,0},{12,4},{1,9},{5,13},{9,1},{13,5},{2,10},{6,14},... | collective-permute-start | bytes 393224 | tf_op jit(solution)/shard_map/ppermute | solution.py:238
  11.1 11.5 %collective-permute-start.6 = (bf16[16,4096]{1,0:T(8,128)(2,1)S(1)}, bf16[16,4096]{1,0:T(8,128)(2,1)S(1)}, u32[]{:S(2)}, u32[]{:S(2)}) collective-permute-start(bf16[16,4096]{1,0:T(8,128)(2,1)S(1)} %get-tuple-element.58), channel_id=1, source_target_pairs={{0,12},{4,0},{8,4},{12,8},{1,13},{5,1},{9,5},{13,9},{2,14},{6,2},{... | collective-permute-start | bytes 393224 | tf_op jit(solution)/shard_map/ppermute | solution.py:238
  14.1 8.6 %collective-permute-start.7 = (bf16[16,4096]{1,0:T(8,128)(2,1)S(1)}, bf16[16,4096]{1,0:T(8,128)(2,1)S(1)}, u32[]{:S(2)}, u32[]{:S(2)}) collective-permute-start(bf16[16,4096]{1,0:T(8,128)(2,1)S(1)} %get-tuple-element.59), channel_id=1, source_target_pairs={{0,4},{4,8},{8,12},{12,0},{1,5},{5,9},{9,13},{13,1},{2,6},{6,10},{... | collective-permute-start | bytes 393224 | tf_op jit(solution)/shard_map/ppermute | solution.py:238
  14.3 3.7 %collective-permute-start.3 = (f32[32,64]{1,0:T(8,128)S(1)}, f32[32,64]{1,0:T(8,128)S(1)}, u32[]{:S(2)}, u32[]{:S(2)}) collective-permute-start(f32[32,64]{1,0:T(8,128)S(1)} %get-tuple-element.48.refs_0_), channel_id=1, source_target_pairs={{0,1},{1,0},{2,3},{3,2},{4,5},{5,4},{6,7},{7,6},{8,9},{9,8},{10,11... | collective-permute-start | bytes 24584 | tf_op jit(solution)/shard_map/ppermute | solution.py:241
  18.1 4.5 %collective-permute-start.4 = (f32[16,64]{1,0:T(8,128)S(1)}, f32[16,64]{1,0:T(8,128)S(1)}, u32[]{:S(2)}, u32[]{:S(2)}) collective-permute-start(f32[16,64]{1,0:T(8,128)S(1)} %slice.8), channel_id=1, source_target_pairs={{0,2},{1,3},{2,0},{3,1},{4,6},{5,7},{6,4},{7,5},{8,10},{9,11},{10,... | collective-permute-start | bytes 12296 | tf_op jit(solution)/shard_map/ppermute | solution.py:241
  22.7 11.8 %collective-permute-start.13 = (bf16[48,3072]{1,0:T(8,128)(2,1)S(1)}, bf16[48,3072]{1,0:T(8,128)(2,1)S(1)}, u32[]{:S(2)}, u32[]{:S(2)}) collective-permute-start(bf16[48,3072]{1,0:T(8,128)(2,1)S(1)} %pack_far.1.refs_1_), channel_id=1, source_target_pairs={{0,16},{16,0},{1,17},{17,1},{2,18},{18,2},{3,19},{19,3},{4,20},{20... | collective-permute-start | bytes 884744 | tf_op jit(solution)/shard_map/ppermute | solution.py:247
  24.2 4.7 %collective-permute-start.8 = (bf16[16,64]{1,0:T(8,128)(2,1)S(1)}, bf16[16,64]{1,0:T(8,128)(2,1)S(1)}, u32[]{:S(2)}, u32[]{:S(2)}) collective-permute-start(bf16[16,64]{1,0:T(8,128)(2,1)S(1)} %fusion.1.refs_0_), channel_id=1, source_target_pairs={{0,4},{4,0},{8,12},{12,8},{1,5},{5,1},{9,13},{13,9},{2,6},{6,2},{1... | collective-permute-start | bytes 6152 | tf_op jit(solution)/shard_map/ppermute | solution.py:244
  28.9 4.6 %collective-permute-start.9 = (bf16[16,64]{1,0:T(8,128)(2,1)S(1)}, bf16[16,64]{1,0:T(8,128)(2,1)S(1)}, u32[]{:S(2)}, u32[]{:S(2)}) collective-permute-start(bf16[16,64]{1,0:T(8,128)(2,1)S(1)} %add.32.refs_0_), channel_id=1, source_target_pairs={{0,8},{4,12},{8,0},{12,4},{1,9},{5,13},{9,1},{13,5},{2,10},{6,14},... | collective-permute-start | bytes 6152 | tf_op jit(solution)/shard_map/ppermute | solution.py:244
  33.9 1.6 %collective-permute-start.11 = (f32[16,4096]{1,0:T(8,128)S(1)}, f32[16,4096]{1,0:T(8,128)S(1)}, u32[]{:S(2)}, u32[]{:S(2)}) collective-permute-start(f32[16,4096]{1,0:T(8,128)S(1)} %get-tuple-element.74), channel_id=1, source_target_pairs={{0,1},{1,0},{2,3},{3,2},{4,5},{5,4},{6,7},{7,6},{8,9},{9,8},{10,11... | collective-permute-start | bytes 786440 | tf_op jit(solution)/shard_map/ppermute | solution.py:241
  34.0 3.9 %collective-permute-start.10 = (f32[16,4096]{1,0:T(8,128)S(1)}, f32[16,4096]{1,0:T(8,128)S(1)}, u32[]{:S(2)}, u32[]{:S(2)}) collective-permute-start(f32[16,4096]{1,0:T(8,128)S(1)} %get-tuple-element.72), channel_id=1, source_target_pairs={{0,1},{1,0},{2,3},{3,2},{4,5},{5,4},{6,7},{7,6},{8,9},{9,8},{10,11... | collective-permute-start | bytes 786440 | tf_op jit(solution)/shard_map/ppermute | solution.py:241
  34.8 2.3 %collective-permute-start.15 = (f32[16,3072]{1,0:T(8,128)S(1)}, f32[16,3072]{1,0:T(8,128)S(1)}, u32[]{:S(2)}, u32[]{:S(2)}) collective-permute-start(f32[16,3072]{1,0:T(8,128)S(1)} %get-tuple-element.80), channel_id=1, source_target_pairs={{0,1},{1,0},{2,3},{3,2},{4,5},{5,4},{6,7},{7,6},{8,9},{9,8},{10,11... | collective-permute-start | bytes 589832 | tf_op jit(solution)/shard_map/ppermute | solution.py:241
  35.6 6.4 %collective-permute-start.12 = (bf16[16,4096]{1,0:T(8,128)(2,1)S(1)}, bf16[16,4096]{1,0:T(8,128)(2,1)S(1)}, u32[]{:S(2)}, u32[]{:S(2)}) collective-permute-start(bf16[16,4096]{1,0:T(8,128)(2,1)S(1)} %add_convert_fusion.1), channel_id=1, source_target_pairs={{0,2},{1,3},{2,0},{3,1},{4,6},{5,7},{6,4},{7,5},{8,10},{9,11},{10,... | collective-permute-start | bytes 393224 | tf_op jit(solution)/shard_map/ppermute | solution.py:241
  37.1 4.9 %collective-permute-start.14 = (f32[16,3072]{1,0:T(8,128)S(1)}, f32[16,3072]{1,0:T(8,128)S(1)}, u32[]{:S(2)}, u32[]{:S(2)}) collective-permute-start(f32[16,3072]{1,0:T(8,128)S(1)} %get-tuple-element.78), channel_id=1, source_target_pairs={{0,1},{1,0},{2,3},{3,2},{4,5},{5,4},{6,7},{7,6},{8,9},{9,8},{10,11... | collective-permute-start | bytes 589832 | tf_op jit(solution)/shard_map/ppermute | solution.py:241
  37.1 6.1 %collective-permute-start.16 = (bf16[16,3072]{1,0:T(8,128)(2,1)S(1)}, bf16[16,3072]{1,0:T(8,128)(2,1)S(1)}, u32[]{:S(2)}, u32[]{:S(2)}) collective-permute-start(bf16[16,3072]{1,0:T(8,128)(2,1)S(1)} %add_convert_fusion.3), channel_id=1, source_target_pairs={{0,2},{1,3},{2,0},{3,1},{4,6},{5,7},{6,4},{7,5},{8,10},{9,11},{10,... | collective-permute-start | bytes 294920 | tf_op jit(solution)/shard_map/ppermute | solution.py:241

commit v9 on v8

--- a/solution.py
+++ b/solution.py
@@ -60,7 +60,9 @@
     )
 
 
-def cut_kernel(owner_count, offsets, far_width, start_of, block, small_count, expand, weight, *refs):
+def cut_kernel(
+    owner_count, offsets, far_width, start_of, block, numbers, small_count, expand, weight, *refs
+):
     small, refs = refs[:small_count], refs[small_count:]
     *pieces, own = refs[: owner_count]
     *loaded, held, sem, held_sem = refs[owner_count:]
@@ -79,30 +81,30 @@
         )
     for n, (source, target) in enumerate(zip(small, loaded)):
         copies.append(pltpu.make_async_copy(source, target, sem.at[owner_count + n]))
-    for bands in weight_copies(start_of(), block, weight, held, held_sem):
-        copies += bands
+    copies += weight_copies(start_of, block, numbers, weight, held, held_sem)
     for copy in copies:
         copy.start()
     for copy in copies:
         copy.wait()
 
 
-def weight_copies(start, block, weight, target, sem):
+def block_start(near_width, far_width, block, number):
+    g, at = lax.axis_index("groups"), number * block
+    return g * far_width + at if at < near_width else (1 - g) * near_width + at - near_width
+
+
+def weight_copies(start_of, block, numbers, weight, target, sem):
     band_count = sem.shape[1]
     band = weight.shape[0] // band_count
-    blocks = []
-    for n in range(target.shape[0]):
-        span = pl.ds(pl.multiple_of(start + n * block, lane), block)
-        bands = []
+    copies = []
+    for n, number in enumerate(numbers):
+        span = pl.ds(pl.multiple_of(start_of(number), lane), block)
         for m in range(band_count):
             rows = pl.ds(m * band, band)
-            bands.append(
-                pltpu.make_async_copy(
-                    weight.at[rows, span], target.at[n, rows], sem.at[n, m]
-                )
+            copies.append(
+                pltpu.make_async_copy(weight.at[rows, span], target.at[n, rows], sem.at[n, m])
             )
-        blocks.append(bands)
-    return blocks
+    return copies
 
 
 def gather_kernel(offsets, slots, index, *refs):
@@ -135,27 +137,21 @@
         target[at : at + rank_block, :] = partial[pl.ds(start, rank_block), :]
 
 
-def part_start(near_width, far_width, is_far, first):
-    g = lax.axis_index("groups")
-    return ((1 - g) * near_width if is_far else g * far_width) + first
-
-
-def base_kernel(next_start_of, block, rows, weight, held, *refs):
+def base_kernel(start_of, block, places, numbers, rows, weight, *refs):
     copies = []
-    if next_start_of is None:
+    if numbers:
+        total, ahead, sem = refs[-3:]
+        copies = weight_copies(start_of, block, numbers, weight, ahead, sem)
+    else:
         total = refs[-1]
-    else:
-        total, ahead, sem = refs[-3:]
-        for bands in weight_copies(next_start_of(), block, weight, ahead, sem):
-            copies += bands
     for copy in copies:
         copy.start()
 
     @pl.when(lax.axis_index("tensor") >= 0)
     def _():
-        for n in range(held.shape[0]):
+        for n, (which, index) in enumerate(places):
             total[:, n * block : (n + 1) * block] = jnp.dot(
-                rows[...], held[n], preferred_element_type=f32
+                rows[...], refs[which][index], preferred_element_type=f32
             )
 
     for copy in copies:
@@ -171,7 +167,7 @@
         packed[n * height : (n + 1) * height, :] = piece[:, pl.ds(start + skip, far_width)]
 
 
-def delta_kernel(owner_count, offsets, start_of, block, base_count, piece_count, slot, *refs):
+def delta_kernel(owner_count, offsets, start_of, first, block, base_count, piece_count, slot, *refs):
     bases, refs = refs[:base_count], refs[base_count:]
     own, shrunk = refs[:2]
     pieces = refs[2 : 2 + piece_count]
@@ -193,7 +189,7 @@
     at = 0
     for base in bases:
         for column in range(0, base.shape[1], block):
-            source = pl.multiple_of(start_of() + at, lane)
+            source = pl.multiple_of(start_of(first + at // block), lane)
             expand = jnp.concatenate(
                 [own[:, pl.ds(source, block)]]
                 + [piece[:, pl.ds(piece.shape[1] - width + at, block)] for piece in pieces],
@@ -249,18 +245,14 @@
     weight = pltpu.with_memory_space_constraint(base_up_weight, pltpu.HBM)
     expand = pltpu.with_memory_space_constraint(adapter_expand_weight, pltpu.HBM)
     offsets = (2, 1, 3)
-    blocks = [from_owner(tokens, j) for j in offsets]
-
-    def split(count):
-        return [(0, count - count // 2), (count - count // 2, count // 2)]
-
-    parts = [(False, *span) for span in split(near_count)]
-    parts += [(True, *span) for span in split(block_count - near_count)]
-    starts = [
-        functools.partial(part_start, near_width, far_width, is_far, first * block)
-        for is_far, first, _ in parts
-    ]
+
+    near_half, far_half = near_count - near_count // 2, (block_count - near_count + 1) // 2
+    cuts = (0, near_half, near_count, near_count + far_half, block_count)
+    parts = list(zip(cuts[:-1], cuts[1:]))
+    loads = (0, min(6, block_count), min(10, block_count), block_count, block_count, block_count)
+    start_of = functools.partial(block_start, near_width, far_width, block)
     bands = 4
+
     small = [
         pltpu.with_memory_space_constraint(x, pltpu.HBM)
         for x in (
@@ -272,7 +264,7 @@
     ]
     cut = kernel_call(
         functools.partial(
-            cut_kernel, owner_count, offsets, far_width, starts[0], block, len(small)
+            cut_kernel, owner_count, offsets, far_width, start_of, block, range(loads[1]), len(small)
         ),
         "cut_expand",
         1,
@@ -283,14 +275,16 @@
         out_shape=[pltpu.VMEM((rank_block, near_width), bf16)] * (owner_count - 1)
         + [pltpu.VMEM((rank_block, columns), bf16)]
         + [pltpu.VMEM(x.shape, x.dtype) for x in small]
-        + [pltpu.VMEM((parts[0][2], depth, block), bf16)],
+        + [pltpu.VMEM((loads[1], depth, block), bf16)],
         scratch_shapes=[
             pltpu.SemaphoreType.DMA((owner_count + len(small),)),
-            pltpu.SemaphoreType.DMA((parts[0][2], bands)),
+            pltpu.SemaphoreType.DMA((loads[1], bands)),
         ],
     )(expand, weight, *small)
     pieces, own = cut[: owner_count - 1], cut[owner_count - 1]
     slots, index, mine, shrink, held = cut[owner_count:]
+    blocks = [from_owner(mine, j) for j in offsets]
+    loaded = [held]
     near = [from_owner(piece, j) for piece, j in zip(pieces, offsets)]
 
     rows, keep, send, slot = kernel_call(
@@ -313,30 +307,37 @@
         shrink,
     )
 
-    def base_part(n, held, *after):
-        is_far, _, count = parts[n]
-        ahead, next_start_of = [], None
-        if n + 1 < len(parts):
-            ahead = [pltpu.VMEM((parts[n + 1][2], depth, block), bf16)]
-            next_start_of = starts[n + 1]
-        return kernel_call(
-            functools.partial(base_kernel, next_start_of, block),
+    def base_part(n, *after):
+        first, last = parts[n]
+        numbers = range(loads[n + 1], loads[n + 2])
+        places, used = [], []
+        for number in range(first, last):
+            source = max(k for k in range(len(loads) - 1) if loads[k] <= number)
+            if source not in used:
+                used.append(source)
+            places.append((used.index(source), number - loads[source]))
+        near = first < near_count
+        out = kernel_call(
+            functools.partial(base_kernel, start_of, block, places, numbers),
             "base_part",
-            1 if is_far else 2 * row_count * depth * count * block,
-            1 if is_far else 2 * depth * count * block,
+            2 * row_count * depth * (last - first) * block if near else 1,
+            2 * depth * (last - first) * block if near else 1,
             4,
-            in_specs=[vmem, anywhere, vmem] + [anywhere] * len(after),
-            out_specs=[vmem] * (1 + len(ahead)),
-            out_shape=[jax.ShapeDtypeStruct((row_count, count * block), f32)] + ahead,
-            scratch_shapes=[pltpu.SemaphoreType.DMA((x.shape[0], bands)) for x in ahead],
-        )(rows, weight, held, *after)
+            in_specs=[vmem, anywhere] + [vmem] * len(used) + [anywhere] * len(after),
+            out_specs=[vmem] * (2 if numbers else 1),
+            out_shape=[jax.ShapeDtypeStruct((row_count, (last - first) * block), f32)]
+            + ([pltpu.VMEM((len(numbers), depth, block), bf16)] if numbers else []),
+            scratch_shapes=[pltpu.SemaphoreType.DMA((len(numbers), bands))] if numbers else [],
+        )(rows, weight, *[loaded[k] for k in used], *after)
+        loaded.append(out[1] if numbers else None)
+        return out[0]
 
     def delta_part(is_far, bases, pieces):
-        start_of = functools.partial(part_start, near_width, far_width, is_far, 0)
+        first = near_count if is_far else 0
         width = sum(base.shape[1] for base in bases)
         return kernel_call(
             functools.partial(
-                delta_kernel, owner_count, offsets, start_of, block, len(bases), len(pieces)
+                delta_kernel, owner_count, offsets, start_of, first, block, len(bases), len(pieces)
             ),
             "delta_part",
             1,
@@ -352,11 +353,11 @@
         )(slot, *bases, own, shrunk, *pieces)
 
     arrived = from_tensor(send, 1)
-    base_0, held = base_part(0, held, send)
+    base_0 = base_part(0, send)
     arrived, base_0 = lax.optimization_barrier((arrived, base_0))
     pair = keep + arrived
     arrived = from_tensor(pair[rank_block:], 2)
-    base_1, held = base_part(1, held, pair)
+    base_1 = base_part(1, pair)
     arrived, base_1, *near = lax.optimization_barrier((arrived, base_1, *near))
     shrunk = (adapter_scale * (pair[:rank_block] + arrived)).astype(bf16)
     packed = kernel_call(
@@ -375,10 +376,10 @@
     while m < owner_count:
         steps.append(m)
         m *= 2
-    base_far, held = [], [held]
+    base_far = []
     for m, n in zip(steps, (2, 3)):
         arrived = from_mirror(shrunk, m)
-        base, *held = base_part(n, *held, shrunk, packed)
+        base = base_part(n, shrunk, packed)
         arrived, base = lax.optimization_barrier((arrived, base))
         base_far.append(base)
         shrunk = shrunk + arrived
@@ -398,7 +399,8 @@
 def on_device(tokens, base_up_weight, adapter_shrink_weight, adapter_expand_weight, *index):
     pairs = lax.axis_size("groups") == 2 and lax.axis_size("tensor") == 4
     few = lax.axis_size("adapter") == 4
-    even = base_up_weight.shape[1] % (2 * lane) == 0 and tokens.shape[0] % 16 == 0
+    columns = base_up_weight.shape[1]
+    even = columns % 512 == 0 and columns >= 4096 and tokens.shape[0] % 16 == 0
     arrange = paired if pairs and few and even else general
     return arrange(
         tokens, base_up_weight, adapter_shrink_weight, adapter_expand_weight, *index

time: 44.2 us -> 51 us (1.15)
  starting transfers between devices: 20.7 us -> 25.1 us
  waiting for transfers between devices: 6.55 us -> 8.81 us
    ppermute x2, starting transfers between devices: 4.43 us -> 8.83 us  [from_mirror(): return lax.ppermute(x, 'adapter', [(s, s ^ m) for s in range(owner_count)])]
    ppermute x6, waiting for transfers between devices: 0.02 us -> 1.91 us  [from_owner(): lax.ppermute(x, 'adapter', [(s, (s - j) % owner_count) for s in range(own...]
    pallas_call x1, Pallas kernels: 4 us -> 5.26 us  [paired(): kernel_call(functools.partial(cut_kernel, owner_count, offsets, far_width...]
    pallas_call x4, Pallas kernels: 10.7 us -> 9.64 us  [base_part(): kernel_call(functools.partial(base_kernel, start_of, block, places, numbe...]
  transfers between devices with their start and end apart: 17 -> 17, of which waited for: 4 -> 7; matrix products, arithmetic and copies ran while one was open for 0% -> 0% of each run, Pallas kernels for 36% -> 21%
where the time goes in v9:
time: 51 us; the launch traced here: 50.9 us
  starting transfers between devices  25.1 us (49%)
  Pallas kernels  15.9 us (31%)
  waiting for transfers between devices  8.81 us (17%)
  other arithmetic  0.91 us (2%)
    ppermute x6, starting transfers between devices, from_owner(): lax.ppermute(x, 'adapter', [(s, (s - j) % owner_count) for s in range(own...  10.4 us
    pallas_call x4, Pallas kernels, base_part(): kernel_call(functools.partial(base_kernel, start_of, block, places, numbe...  9.64 us
    ppermute x2, starting transfers between devices, from_mirror(): return lax.ppermute(x, 'adapter', [(s, s ^ m) for s in range(owner_count)])  8.83 us
    ppermute x8, waiting for transfers between devices, from_tensor(): return lax.ppermute(x, 'tensor', [(s, s ^ m) for s in range(4)])  6.17 us
    pallas_call x1, Pallas kernels, paired(): kernel_call(functools.partial(cut_kernel, owner_count, offsets, far_width...  5.26 us
    ppermute x8, starting transfers between devices, from_tensor(): return lax.ppermute(x, 'tensor', [(s, s ^ m) for s in range(4)])  4.33 us
    ppermute x6, waiting for transfers between devices, from_owner(): lax.ppermute(x, 'adapter', [(s, (s - j) % owner_count) for s in range(own...  1.91 us
    ppermute x1, starting transfers between devices, from_group(): return lax.ppermute(x, 'groups', [(0, 1), (1, 0)])  1.53 us
  transfers between devices with their start and end apart: 17, of which 7 were waited for; matrix products, arithmetic and copies ran while one was open for 0% of the time, Pallas kernels for 21%

profile of v9, /device:TPU:0, one launch (start us, length us, event | category | flops | bytes accessed | tf_op | source)
XLA Modules:
  0.0 50.9 jit_solution(5037100203682573837)
XLA Ops:
  0.0 5.3 %cut_expand.1 = (bf16[16,4096]{1,0:T(8,128)(2,1)S(1)}, bf16[16,4096]{1,0:T(8,128)(2,1)S(1)}, bf16[16,4096]{1,0:T(8,128)(2,1)S(1)}, bf16[16,7168]{1,0:T(8,128)(2,...) custom-call(bf16[1,16,28672]{2,1,0:T(8,128)(2,1)} %expand.1, ...), custom_call_target="tpu_custom_call" | custom-call | flops 1 | bytes 1 | tf_op jit(solution)/shard_map/cut_expand/pallas_call | solution.py:265
  5.3 4.1 %collective-permute-start = (bf16[16,2048]{1,0:T(8,128)(2,1)S(1)}, bf16[16,2048]{1,0:T(8,128)(2,1)S(1)}, u32[]{:S(2)}, u32[]{:S(2)}) collective-permute-start(bf16[16,2048]{1,0:T(8,128)(2,1)S(1)} %get-tuple-element.43.refs_0_), channel_id=1, source_target_pairs={{0,8},{4,12},{8,0},{12,4},{1,9},{5,13},{9,1},{13,5},{2,10},{6,14},... | collective-permute-start | bytes 196616 | tf_op jit(solution)/shard_map/ppermute | solution.py:234
  9.4 1.3 %collective-permute-start.1 = (bf16[16,2048]{1,0:T(8,128)(2,1)S(1)}, bf16[16,2048]{1,0:T(8,128)(2,1)S(1)}, u32[]{:S(2)}, u32[]{:S(2)}) collective-permute-start(bf16[16,2048]{1,0:T(8,128)(2,1)S(1)} %get-tuple-element.43.refs_0_), channel_id=1, source_target_pairs={{0,12},{4,0},{8,4},{12,8},{1,13},{5,1},{9,5},{13,9},{2,14},{6,2},{... | collective-permute-start | bytes 196616 | tf_op jit(solution)/shard_map/ppermute | solution.py:234
  10.7 0.7 %collective-permute-start.2 = (bf16[16,2048]{1,0:T(8,128)(2,1)S(1)}, bf16[16,2048]{1,0:T(8,128)(2,1)S(1)}, u32[]{:S(2)}, u32[]{:S(2)}) collective-permute-start(bf16[16,2048]{1,0:T(8,128)(2,1)S(1)} %get-tuple-element.43.refs_0_), channel_id=1, source_target_pairs={{0,4},{4,8},{8,12},{12,0},{1,5},{5,9},{9,13},{13,1},{2,6},{6,10},{... | collective-permute-start | bytes 196616 | tf_op jit(solution)/shard_map/ppermute | solution.py:234
  11.4 1.0 %collective-permute-start.5 = (bf16[16,4096]{1,0:T(8,128)(2,1)S(1)}, bf16[16,4096]{1,0:T(8,128)(2,1)S(1)}, u32[]{:S(2)}, u32[]{:S(2)}) collective-permute-start(bf16[16,4096]{1,0:T(8,128)(2,1)S(1)} %get-tuple-element.55), channel_id=1, source_target_pairs={{0,8},{4,12},{8,0},{12,4},{1,9},{5,13},{9,1},{13,5},{2,10},{6,14},... | collective-permute-start | bytes 393224 | tf_op jit(solution)/shard_map/ppermute | solution.py:234
  12.4 2.9 %collective-permute-start.6 = (bf16[16,4096]{1,0:T(8,128)(2,1)S(1)}, bf16[16,4096]{1,0:T(8,128)(2,1)S(1)}, u32[]{:S(2)}, u32[]{:S(2)}) collective-permute-start(bf16[16,4096]{1,0:T(8,128)(2,1)S(1)} %get-tuple-element.56), channel_id=1, source_target_pairs={{0,12},{4,0},{8,4},{12,8},{1,13},{5,1},{9,5},{13,9},{2,14},{6,2},{... | collective-permute-start | bytes 393224 | tf_op jit(solution)/shard_map/ppermute | solution.py:234
  15.3 0.0 collective-permute-done.refs_1_
  15.3 0.3 collective-permute-start.7
  15.6 0.0 collective-permute-done.1.refs_2_
  15.6 1.9 %collective-permute-done.2.refs_3_ = bf16[16,2048]{1,0:T(8,128)(2,1)S(1)} collective-permute-done((bf16[16,2048]{1,0:T(8,128)(2,1)S(1)}, bf16[16,2048]{1,0:T(8,128)(2,1)S(1)}, u32[]{:S(2)}, u32[]{:S(2)}) %collective-permute-start.2) | collective-permute-done | bytes 65568 | tf_op jit(solution)/shard_map/ppermute | solution.py:234
  17.5 0.3 gather_rows.1
  17.8 0.1 collective-permute-start.3
  17.9 3.6 %base_part.4 = (f32[64,2048]{1,0:T(8,128)S(1)}, bf16[4,2048,512]{2,1,0:T(8,128)(2,1)S(1)}) custom-call(bf16[64,2048]{1,0:T(8,128)(2,1)S(1)} %get-tuple-element.47.rows, bf16[2048,7168]{1,0:T(8,128)(2,1)} %weight.9, bf16[6,2048,512]{2,1,0:T(8,128)(2,1)S(1)} %get-tuple-element.48.refs_0_, f32[32,64]{1,0:T(8,128)S(1)} %get-tuple-element.46.refs_1_), custom_call_target="tpu_custom_call" | custom-call | flops 536870912 | bytes 8388608 | tf_op jit(solution)/shard_map/base_part/pallas_call | solution.py:320
  21.5 0.0 collective-permute-done.3
  21.6 1.6 %collective-permute-start.4 = (f32[16,64]{1,0:T(8,128)S(1)}, f32[16,64]{1,0:T(8,128)S(1)}, u32[]{:S(2)}, u32[]{:S(2)}) collective-permute-start(f32[16,64]{1,0:T(8,128)S(1)} %slice.8), channel_id=1, source_target_pairs={{0,2},{1,3},{2,0},{3,1},{4,6},{5,7},{6,4},{7,5},{8,10},{9,11},{10,... | collective-permute-start | bytes 12296 | tf_op jit(solution)/shard_map/ppermute | solution.py:237
  23.1 3.6 %base_part.5 = (f32[64,2048]{1,0:T(8,128)S(1)}, bf16[4,2048,512]{2,1,0:T(8,128)(2,1)S(1)}) custom-call(bf16[64,2048]{1,0:T(8,128)(2,1)S(1)} %get-tuple-element.47.rows, bf16[2048,7168]{1,0:T(8,128)(2,1)} %weight.9, bf16[6,2048,512]{2,1,0:T(8,128)(2,1)S(1)} %get-tuple-element.48.refs_0_, bf16[4,2048,512]{2,1,0:T(8,128)(2,1)S(1)} %get-tuple-element.53.refs_1_.refs_0_, ...), custom_call_target="tpu_custom_call" | custom-call | flops 536870912 | bytes 8388608 | tf_op jit(solution)/shard_map/base_part/pallas_call | solution.py:320
  26.7 0.0 collective-permute-done.4
  26.7 0.0 collective-permute-done.5.refs_0_.refs_4_
  26.7 0.0 collective-permute-done.6.refs_1_.refs_5_
  26.7 0.0 collective-permute-done.7.refs_2_.refs_6_
  26.8 1.5 %collective-permute-start.13 = (bf16[48,3072]{1,0:T(8,128)(2,1)S(1)}, bf16[48,3072]{1,0:T(8,128)(2,1)S(1)}, u32[]{:S(2)}, u32[]{:S(2)}) collective-permute-start(bf16[48,3072]{1,0:T(8,128)(2,1)S(1)} %pack_far.1.refs_3_.refs_2_), channel_id=1, source_target_pairs={{0,16},{16,0},{1,17},{17,1},{2,18},{18,2},{3,19},{19,3},{4,20},{20... | collective-permute-start | bytes 884744 | tf_op jit(solution)/shard_map/ppermute | solution.py:243
  28.3 4.8 %collective-permute-start.8 = (bf16[16,64]{1,0:T(8,128)(2,1)S(1)}, bf16[16,64]{1,0:T(8,128)(2,1)S(1)}, u32[]{:S(2)}, u32[]{:S(2)}) collective-permute-start(bf16[16,64]{1,0:T(8,128)(2,1)S(1)} %fusion.1.refs_2_), channel_id=1, source_target_pairs={{0,4},{4,0},{8,12},{12,8},{1,5},{5,1},{9,13},{13,9},{2,6},{6,2},{1... | collective-permute-start | bytes 6152 | tf_op jit(solution)/shard_map/ppermute | solution.py:240
  33.1 1.2 %base_part.6.refs_0_ = f32[64,1536]{1,0:T(8,128)S(1)} custom-call(bf16[64,2048]{1,0:T(8,128)(2,1)S(1)} %get-tuple-element.47.rows, bf16[2048,7168]{1,0:T(8,128)(2,1)} %weight.9, bf16[4,2048,512]{2,1,0:T(8,128)(2,1)S(1)} %get-tuple-element.53.refs_1_.refs_0_, bf16[4,2048,512]{2,1,0:T(8,128)(2,1)S(1)} %get-tuple-element.61.refs_1_.refs_0_, ...), custom_call_target="tpu_custom_call" | custom-call | flops 1 | bytes 1 | tf_op jit(solution)/shard_map/base_part/pallas_call | solution.py:320
  34.3 0.4 collective-permute-done.8
  34.7 4.1 %collective-permute-start.9 = (bf16[16,64]{1,0:T(8,128)(2,1)S(1)}, bf16[16,64]{1,0:T(8,128)(2,1)S(1)}, u32[]{:S(2)}, u32[]{:S(2)}) collective-permute-start(bf16[16,64]{1,0:T(8,128)(2,1)S(1)} %add.32.refs_1_), channel_id=1, source_target_pairs={{0,8},{4,12},{8,0},{12,4},{1,9},{5,13},{9,1},{13,5},{2,10},{6,14},... | collective-permute-start | bytes 6152 | tf_op jit(solution)/shard_map/ppermute | solution.py:240
  38.8 1.2 %base_part.7.refs_1_ = f32[64,1536]{1,0:T(8,128)S(1)} custom-call(bf16[64,2048]{1,0:T(8,128)(2,1)S(1)} %get-tuple-element.47.rows, bf16[2048,7168]{1,0:T(8,128)(2,1)} %weight.9, bf16[4,2048,512]{2,1,0:T(8,128)(2,1)S(1)} %get-tuple-element.61.refs_1_.refs_0_, bf16[16,64]{1,0:T(8,128)(2,1)S(1)} %add.32.refs_1_, bf16[48,3072]{1,0:T(8,128)(2,1)S(1)} %pack_far.1.refs_3_.refs_2_), custom_call_target="tpu_custom_call" | custom-call | flops 1 | bytes 1 | tf_op jit(solution)/shard_map/base_part/pallas_call | solution.py:320
  40.0 0.4 collective-permute-done.9
  40.3 0.4 delta_part.2
  40.7 0.1 collective-permute-start.11
  40.8 0.5 collective-permute-start.10
  41.3 0.0 collective-permute-done.13.refs_4_
  41.3 0.3 delta_part.3
  41.6 0.2 collective-permute-start.15
  41.8 0.5 %collective-permute-done.11 = f32[16,4096]{1,0:T(8,128)S(1)} collective-permute-done((f32[16,4096]{1,0:T(8,128)S(1)}, f32[16,4096]{1,0:T(8,128)S(1)}, u32[]{:S(2)}, u32[]{:S(2)}) %collective-permute-start.11) | collective-permute-done | bytes 262176 | tf_op jit(solution)/shard_map/ppermute | solution.py:237
  42.4 0.6 %collective-permute-start.12 = (bf16[16,4096]{1,0:T(8,128)(2,1)S(1)}, bf16[16,4096]{1,0:T(8,128)(2,1)S(1)}, u32[]{:S(2)}, u32[]{:S(2)}) collective-permute-start(bf16[16,4096]{1,0:T(8,128)(2,1)S(1)} %add_convert_fusion.1), channel_id=1, source_target_pairs={{0,2},{1,3},{2,0},{3,1},{4,6},{5,7},{6,4},{7,5},{8,10},{9,11},{10,... | collective-permute-start | bytes 393224 | tf_op jit(solution)/shard_map/ppermute | solution.py:237
  43.0 0.0 collective-permute-start.14
  43.0 0.2 collective-permute-done.15
  43.2 1.4 %collective-permute-start.16 = (bf16[16,3072]{1,0:T(8,128)(2,1)S(1)}, bf16[16,3072]{1,0:T(8,128)(2,1)S(1)}, u32[]{:S(2)}, u32[]{:S(2)}) collective-permute-start(bf16[16,3072]{1,0:T(8,128)(2,1)S(1)} %add_convert_fusion.3), channel_id=1, source_target_pairs={{0,2},{1,3},{2,0},{3,1},{4,6},{5,7},{6,4},{7,5},{8,10},{9,11},{10,... | collective-permute-start | bytes 294920 | tf_op jit(solution)/shard_map/ppermute | solution.py:237
  44.6 0.0 collective-permute-done.10
  44.6 4.2 %collective-permute-done.12 = bf16[16,4096]{1,0:T(8,128)(2,1)S(1)} collective-permute-done((bf16[16,4096]{1,0:T(8,128)(2,1)S(1)}, bf16[16,4096]{1,0:T(8,128)(2,1)S(1)}, u32[]{:S(2)}, u32[]{:S(2)}) %collective-permute-start.12) | collective-permute-done | bytes 131104 | tf_op jit(solution)/shard_map/ppermute | solution.py:237
  48.8 0.0 collective-permute-done.14
  48.8 1.2 %collective-permute-done.16 = bf16[16,3072]{1,0:T(8,128)(2,1)S(1)} collective-permute-done((bf16[16,3072]{1,0:T(8,128)(2,1)S(1)}, bf16[16,3072]{1,0:T(8,128)(2,1)S(1)}, u32[]{:S(2)}, u32[]{:S(2)}) %collective-permute-start.16) | collective-permute-done | bytes 98336 | tf_op jit(solution)/shard_map/ppermute | solution.py:237
  50.1 0.7 %maximum_select_fusion = bf16[16,7168]{1,0:T(8,128)(2,1)} fusion(bf16[16,3072]{1,0:T(8,128)(2,1)S(1)} %add_convert_fusion.2, bf16[16,4096]{1,0:T(8,128)(2,1)S(1)} %add_convert_fusion, pred[]{:T(512)S(6)} %eq.3), kind=kLoop, calls=%fused_computation.2 | loop fusion | flops 1032192 | bytes 458753 | tf_op jit(solution)/shard_map/jit(_where)/select_n | solution.py:396
  (10 shorter events, 0.2 us)
Async XLA Ops:
  5.3 10.1 %collective-permute-start = (bf16[16,2048]{1,0:T(8,128)(2,1)S(1)}, bf16[16,2048]{1,0:T(8,128)(2,1)S(1)}, u32[]{:S(2)}, u32[]{:S(2)}) collective-permute-start(bf16[16,2048]{1,0:T(8,128)(2,1)S(1)} %get-tuple-element.43.refs_0_), channel_id=1, source_target_pairs={{0,8},{4,12},{8,0},{12,4},{1,9},{5,13},{9,1},{13,5},{2,10},{6,14},... | collective-permute-start | bytes 196616 | tf_op jit(solution)/shard_map/ppermute | solution.py:234
  9.4 6.3 %collective-permute-start.1 = (bf16[16,2048]{1,0:T(8,128)(2,1)S(1)}, bf16[16,2048]{1,0:T(8,128)(2,1)S(1)}, u32[]{:S(2)}, u32[]{:S(2)}) collective-permute-start(bf16[16,2048]{1,0:T(8,128)(2,1)S(1)} %get-tuple-element.43.refs_0_), channel_id=1, source_target_pairs={{0,12},{4,0},{8,4},{12,8},{1,13},{5,1},{9,5},{13,9},{2,14},{6,2},{... | collective-permute-start | bytes 196616 | tf_op jit(solution)/shard_map/ppermute | solution.py:234
  10.7 6.8 %collective-permute-start.2 = (bf16[16,2048]{1,0:T(8,128)(2,1)S(1)}, bf16[16,2048]{1,0:T(8,128)(2,1)S(1)}, u32[]{:S(2)}, u32[]{:S(2)}) collective-permute-start(bf16[16,2048]{1,0:T(8,128)(2,1)S(1)} %get-tuple-element.43.refs_0_), channel_id=1, source_target_pairs={{0,4},{4,8},{8,12},{12,0},{1,5},{5,9},{9,13},{13,1},{2,6},{6,10},{... | collective-permute-start | bytes 196616 | tf_op jit(solution)/shard_map/ppermute | solution.py:234
  11.4 15.3 %collective-permute-start.5 = (bf16[16,4096]{1,0:T(8,128)(2,1)S(1)}, bf16[16,4096]{1,0:T(8,128)(2,1)S(1)}, u32[]{:S(2)}, u32[]{:S(2)}) collective-permute-start(bf16[16,4096]{1,0:T(8,128)(2,1)S(1)} %get-tuple-element.55), channel_id=1, source_target_pairs={{0,8},{4,12},{8,0},{12,4},{1,9},{5,13},{9,1},{13,5},{2,10},{6,14},... | collective-permute-start | bytes 393224 | tf_op jit(solution)/shard_map/ppermute | solution.py:234
  12.4 14.3 %collective-permute-start.6 = (bf16[16,4096]{1,0:T(8,128)(2,1)S(1)}, bf16[16,4096]{1,0:T(8,128)(2,1)S(1)}, u32[]{:S(2)}, u32[]{:S(2)}) collective-permute-start(bf16[16,4096]{1,0:T(8,128)(2,1)S(1)} %get-tuple-element.56), channel_id=1, source_target_pairs={{0,12},{4,0},{8,4},{12,8},{1,13},{5,1},{9,5},{13,9},{2,14},{6,2},{... | collective-permute-start | bytes 393224 | tf_op jit(solution)/shard_map/ppermute | solution.py:234
  15.3 11.4 %collective-permute-start.7 = (bf16[16,4096]{1,0:T(8,128)(2,1)S(1)}, bf16[16,4096]{1,0:T(8,128)(2,1)S(1)}, u32[]{:S(2)}, u32[]{:S(2)}) collective-permute-start(bf16[16,4096]{1,0:T(8,128)(2,1)S(1)} %get-tuple-element.57), channel_id=1, source_target_pairs={{0,4},{4,8},{8,12},{12,0},{1,5},{5,9},{9,13},{13,1},{2,6},{6,10},{... | collective-permute-start | bytes 393224 | tf_op jit(solution)/shard_map/ppermute | solution.py:234
  17.8 3.7 %collective-permute-start.3 = (f32[32,64]{1,0:T(8,128)S(1)}, f32[32,64]{1,0:T(8,128)S(1)}, u32[]{:S(2)}, u32[]{:S(2)}) collective-permute-start(f32[32,64]{1,0:T(8,128)S(1)} %get-tuple-element.46.refs_1_), channel_id=1, source_target_pairs={{0,1},{1,0},{2,3},{3,2},{4,5},{5,4},{6,7},{7,6},{8,9},{9,8},{10,11... | collective-permute-start | bytes 24584 | tf_op jit(solution)/shard_map/ppermute | solution.py:237
  21.6 5.1 %collective-permute-start.4 = (f32[16,64]{1,0:T(8,128)S(1)}, f32[16,64]{1,0:T(8,128)S(1)}, u32[]{:S(2)}, u32[]{:S(2)}) collective-permute-start(f32[16,64]{1,0:T(8,128)S(1)} %slice.8), channel_id=1, source_target_pairs={{0,2},{1,3},{2,0},{3,1},{4,6},{5,7},{6,4},{7,5},{8,10},{9,11},{10,... | collective-permute-start | bytes 12296 | tf_op jit(solution)/shard_map/ppermute | solution.py:237
  26.8 14.5 %collective-permute-start.13 = (bf16[48,3072]{1,0:T(8,128)(2,1)S(1)}, bf16[48,3072]{1,0:T(8,128)(2,1)S(1)}, u32[]{:S(2)}, u32[]{:S(2)}) collective-permute-start(bf16[48,3072]{1,0:T(8,128)(2,1)S(1)} %pack_far.1.refs_3_.refs_2_), channel_id=1, source_target_pairs={{0,16},{16,0},{1,17},{17,1},{2,18},{18,2},{3,19},{19,3},{4,20},{20... | collective-permute-start | bytes 884744 | tf_op jit(solution)/shard_map/ppermute | solution.py:243
  28.3 6.3 %collective-permute-start.8 = (bf16[16,64]{1,0:T(8,128)(2,1)S(1)}, bf16[16,64]{1,0:T(8,128)(2,1)S(1)}, u32[]{:S(2)}, u32[]{:S(2)}) collective-permute-start(bf16[16,64]{1,0:T(8,128)(2,1)S(1)} %fusion.1.refs_2_), channel_id=1, source_target_pairs={{0,4},{4,0},{8,12},{12,8},{1,5},{5,1},{9,13},{13,9},{2,6},{6,2},{1... | collective-permute-start | bytes 6152 | tf_op jit(solution)/shard_map/ppermute | solution.py:240
  34.7 5.7 %collective-permute-start.9 = (bf16[16,64]{1,0:T(8,128)(2,1)S(1)}, bf16[16,64]{1,0:T(8,128)(2,1)S(1)}, u32[]{:S(2)}, u32[]{:S(2)}) collective-permute-start(bf16[16,64]{1,0:T(8,128)(2,1)S(1)} %add.32.refs_1_), channel_id=1, source_target_pairs={{0,8},{4,12},{8,0},{12,4},{1,9},{5,13},{9,1},{13,5},{2,10},{6,14},... | collective-permute-start | bytes 6152 | tf_op jit(solution)/shard_map/ppermute | solution.py:240
  40.7 1.6 %collective-permute-start.11 = (f32[16,4096]{1,0:T(8,128)S(1)}, f32[16,4096]{1,0:T(8,128)S(1)}, u32[]{:S(2)}, u32[]{:S(2)}) collective-permute-start(f32[16,4096]{1,0:T(8,128)S(1)} %get-tuple-element.70), channel_id=1, source_target_pairs={{0,1},{1,0},{2,3},{3,2},{4,5},{5,4},{6,7},{7,6},{8,9},{9,8},{10,11... | collective-permute-start | bytes 786440 | tf_op jit(solution)/shard_map/ppermute | solution.py:237
  40.8 3.7 %collective-permute-start.10 = (f32[16,4096]{1,0:T(8,128)S(1)}, f32[16,4096]{1,0:T(8,128)S(1)}, u32[]{:S(2)}, u32[]{:S(2)}) collective-permute-start(f32[16,4096]{1,0:T(8,128)S(1)} %get-tuple-element.68), channel_id=1, source_target_pairs={{0,1},{1,0},{2,3},{3,2},{4,5},{5,4},{6,7},{7,6},{8,9},{9,8},{10,11... | collective-permute-start | bytes 786440 | tf_op jit(solution)/shard_map/ppermute | solution.py:237
  41.6 1.5 %collective-permute-start.15 = (f32[16,3072]{1,0:T(8,128)S(1)}, f32[16,3072]{1,0:T(8,128)S(1)}, u32[]{:S(2)}, u32[]{:S(2)}) collective-permute-start(f32[16,3072]{1,0:T(8,128)S(1)} %get-tuple-element.76), channel_id=1, source_target_pairs={{0,1},{1,0},{2,3},{3,2},{4,5},{5,4},{6,7},{7,6},{8,9},{9,8},{10,11... | collective-permute-start | bytes 589832 | tf_op jit(solution)/shard_map/ppermute | solution.py:237
  42.4 6.4 %collective-permute-start.12 = (bf16[16,4096]{1,0:T(8,128)(2,1)S(1)}, bf16[16,4096]{1,0:T(8,128)(2,1)S(1)}, u32[]{:S(2)}, u32[]{:S(2)}) collective-permute-start(bf16[16,4096]{1,0:T(8,128)(2,1)S(1)} %add_convert_fusion.1), channel_id=1, source_target_pairs={{0,2},{1,3},{2,0},{3,1},{4,6},{5,7},{6,4},{7,5},{8,10},{9,11},{10,... | collective-permute-start | bytes 393224 | tf_op jit(solution)/shard_map/ppermute | solution.py:237
  43.0 5.8 %collective-permute-start.14 = (f32[16,3072]{1,0:T(8,128)S(1)}, f32[16,3072]{1,0:T(8,128)S(1)}, u32[]{:S(2)}, u32[]{:S(2)}) collective-permute-start(f32[16,3072]{1,0:T(8,128)S(1)} %get-tuple-element.74), channel_id=1, source_target_pairs={{0,1},{1,0},{2,3},{3,2},{4,5},{5,4},{6,7},{7,6},{8,9},{9,8},{10,11... | collective-permute-start | bytes 589832 | tf_op jit(solution)/shard_map/ppermute | solution.py:237
  43.2 6.9 %collective-permute-start.16 = (bf16[16,3072]{1,0:T(8,128)(2,1)S(1)}, bf16[16,3072]{1,0:T(8,128)(2,1)S(1)}, u32[]{:S(2)}, u32[]{:S(2)}) collective-permute-start(bf16[16,3072]{1,0:T(8,128)(2,1)S(1)} %add_convert_fusion.3), channel_id=1, source_target_pairs={{0,2},{1,3},{2,0},{3,1},{4,6},{5,7},{6,4},{7,5},{8,10},{9,11},{10,... | collective-permute-start | bytes 294920 | tf_op jit(solution)/shard_map/ppermute | solution.py:237

commit v10 on v9

v10 whole, which is shorter than its diff:
```python
import functools

import jax
import jax.numpy as jnp
from jax import lax
from jax.experimental import pallas as pl
from jax.experimental.pallas import tpu as pltpu
from jax.sharding import PartitionSpec as P

adapter_scale = 0.5
lane = 128
f32 = jnp.float32
bf16 = jnp.bfloat16


def general(
    tokens,
    base_up_weight,
    adapter_shrink_weight,
    adapter_expand_weight,
    row_adapter_index,
    adapter_slot_index,
):
    owner_count = lax.axis_size("adapter")
    owner_index = lax.axis_index("adapter")
    tensor_index = lax.axis_index("tensor")
    rank_block = adapter_expand_weight.shape[1]
    columns = base_up_weight.shape[1]
    slot = jnp.take(adapter_slot_index, row_adapter_index[:, 0], axis=0)
    rows = lax.all_gather(tokens, "adapter", axis=0, tiled=True)
    expand = adapter_expand_weight[0].reshape(rank_block, owner_count, columns)
    expand = lax.all_to_all(expand, "adapter", split_axis=1, concat_axis=1, tiled=True)
    shrunk = jnp.dot(rows, adapter_shrink_weight[0], preferred_element_type=f32)
    shrunk = jnp.where((slot == owner_index)[:, None], shrunk, 0.0)
    shrunk = lax.psum(shrunk, ("adapter", "tensor"))
    shrunk = (adapter_scale * shrunk).astype(bf16)
    shrunk = lax.dynamic_slice_in_dim(shrunk, tensor_index * rank_block, rank_block, 1)
    chosen = slot[:, None] == jnp.arange(owner_count, dtype=jnp.int32)[None, :]
    spread = jnp.where(chosen[:, None, :], shrunk[:, :, None], jnp.zeros((), bf16))
    total = jnp.dot(rows, base_up_weight, preferred_element_type=f32)
    total = total + jnp.dot(
        spread.reshape(-1, rank_block * owner_count),
        expand.reshape(rank_block * owner_count, columns),
        preferred_element_type=f32,
    )
    return lax.psum_scatter(total, "tensor", scatter_dimension=0, tiled=True).astype(bf16)


vmem = pl.BlockSpec(memory_space=pltpu.VMEM)
anywhere = pl.BlockSpec(memory_space=pl.ANY)


def kernel_call(kernel, name, flops, moved, mib, **specs):
    return pl.pallas_call(
        kernel,
        cost_estimate=pl.CostEstimate(flops=flops, bytes_accessed=moved, transcendentals=0),
        compiler_params=pltpu.CompilerParams(vmem_limit_bytes=mib << 20),
        name=name,
        **specs,
    )


def cut_kernel(block, numbers, small_count, expand, weight, *refs):
    small, refs = refs[:small_count], refs[small_count:]
    whole, half, own, *loaded, held, sem, held_sem = refs
    g, a = lax.axis_index("groups"), lax.axis_index("adapter")
    columns, half_width = whole.shape[1], half.shape[1]
    firsts = (
        lax.rem(a + 3 - 2 * g, 4) * columns,
        lax.rem(a + 2, 4) * columns + g * half_width,
        a * columns,
    )
    copies = []
    for n, (first, target) in enumerate(zip(firsts, (whole, half, own))):
        span = pl.ds(pl.multiple_of(first, lane), target.shape[1])
        copies.append(pltpu.make_async_copy(expand.at[0, :, span], target, sem.at[n]))
    for n, (source, target) in enumerate(zip(small, loaded)):
        copies.append(pltpu.make_async_copy(source, target, sem.at[len(firsts) + n]))
    copies += weight_copies(block, numbers, weight, held, held_sem)
    for copy in copies:
        copy.start()
    for copy in copies:
        copy.wait()


def weight_copies(block, numbers, weight, target, sem):
    band_count = sem.shape[1]
    band = weight.shape[0] // band_count
    copies = []
    for n, number in enumerate(numbers):
        span = pl.ds(number * block, block)
        for m in range(band_count):
            rows = pl.ds(m * band, band)
            copies.append(
                pltpu.make_async_copy(weight.at[rows, span], target.at[n, rows], sem.at[n, m])
            )
    return copies


def gather_kernel(offsets, slots, index, *refs):
    owner_count = len(offsets)
    blocks = refs[:owner_count]
    shrink, rows_out, keep, send, slot_out, rows, partial = refs[owner_count:]
    a, t = lax.axis_index("adapter"), lax.axis_index("tensor")
    height, depth = blocks[0].shape
    for j, part in zip(offsets, blocks):
        where = lax.rem(a + j, owner_count)
        rows[pl.ds(pl.multiple_of(where * height, height), height), :] = part[:, :depth]
    quarter = rows.shape[0] // 4
    for i, flip in enumerate((0, 2, 1, 3)):
        start = pl.multiple_of(lax.bitwise_xor(t, flip) * quarter, quarter)
        rows_out[i * quarter : (i + 1) * quarter, :] = rows[pl.ds(start, quarter), :]
    product = lax.dot_general(
        shrink[...], rows[...], (((1,), (1,)), ((), ())), preferred_element_type=f32
    )
    named, table = index[...], slots[...]
    slot = jnp.zeros_like(named)
    for k in range(table.shape[1]):
        slot = jnp.where(named == k, table[:, k : k + 1], slot)
    slot_out[...] = slot
    partial[...] = jnp.where(slot == a, product, 0.0)
    rank_block = partial.shape[0] // 4
    for i, flip in enumerate((0, 2, 1, 3)):
        start = pl.multiple_of(lax.bitwise_xor(t, flip) * rank_block, rank_block)
        target = keep if i < 2 else send
        at = i % 2 * rank_block
        target[at : at + rank_block, :] = partial[pl.ds(start, rank_block), :]


def base_kernel(block, places, numbers, streamed, rows, weight, *refs):
    total, ahead, sem = refs[-3:]
    copies = weight_copies(block, numbers, weight, ahead, sem)
    for copy in copies:
        copy.start()

    @pl.when(lax.axis_index("tensor") >= 0)
    def _():
        for n, (which, index) in enumerate(places):
            total[:, n * block : (n + 1) * block] = jnp.dot(
                rows[...], refs[which][index], preferred_element_type=f32
            )

    bands = sem.shape[1]
    for n in range(len(numbers)):
        for copy in copies[n * bands : (n + 1) * bands]:
            copy.wait()
        if streamed:
            at = (len(places) + n) * block
            total[:, at : at + block] = jnp.dot(
                rows[...], ahead[n], preferred_element_type=f32
            )


def pack_kernel(whole, half, packed):
    columns = whole.shape[1]
    packed[:, :columns] = whole[...]
    packed[:, columns:] = half[...]


def delta_kernel(block, splits, slot, *refs):
    bases, refs = refs[: -len(splits) * 2 - 10], refs[-len(splits) * 2 - 10 :]
    own, shrunk, whole, half, packed, own_keep, own_send = refs[:7]
    cross_keep, cross_send = refs[7 : 7 + len(splits)], refs[7 + len(splits) : 7 + 2 * len(splits)]
    flat, ordered, two = refs[-3:]
    g, a, t = (lax.axis_index(name) for name in ("groups", "adapter", "tensor"))
    row_count = bases[0].shape[0]
    quarter = row_count // 4
    columns, half_width = whole.shape[1], half.shape[1]

    @pl.when(g == 0)
    def _():
        two[:, :half_width] = half[...]
        two[:, half_width:] = packed[:, columns:]

    @pl.when(g != 0)
    def _():
        two[:, :half_width] = packed[:, columns:]
        two[:, half_width:] = half[...]

    merged = shrunk[...].astype(f32)
    spread = [
        jnp.where(slot[...] == lax.rem(a + j, 4), merged, 0.0)
        for j in (0, 1 + 2 * g, 3 - 2 * g, 2)
    ]
    flat[...] = jnp.concatenate(spread, axis=0).T
    for i, turn in enumerate((0, 2, 1, 3)):
        start = pl.multiple_of(lax.bitwise_xor(t, turn) * quarter, quarter)
        ordered[i * quarter : (i + 1) * quarter, :] = flat[pl.ds(start, quarter), :].astype(bf16)
    left = ordered[...]
    at, split = 0, 0
    for base in bases:
        for column in range(0, base.shape[1], block):
            span = slice(at, at + block)
            expand = jnp.concatenate(
                [own[:, span], whole[:, span], packed[:, span], two[:, span]], axis=0
            )
            total = base[:, column : column + block] + jnp.dot(
                left, expand, preferred_element_type=f32
            )
            if at >= splits[split][1]:
                split += 1
            here = slice(at - splits[split][0], at - splits[split][0] + block)
            own_keep[:, span] = total[:quarter]
            cross_keep[split][:, here] = total[quarter : 2 * quarter]
            own_send[:, span] = total[2 * quarter : 3 * quarter]
            cross_send[split][:, here] = total[3 * quarter :]
            at += block


def column_block(width):
    for size in (512, 256, 128):
        if width % size == 0:
            return size


def paired(
    tokens,
    base_up_weight,
    adapter_shrink_weight,
    adapter_expand_weight,
    row_adapter_index,
    adapter_slot_index,
):
    owner_count = lax.axis_size("adapter")
    g = lax.axis_index("groups")
    height, depth = tokens.shape
    row_count = height * owner_count
    columns = base_up_weight.shape[1]
    rank_block = adapter_expand_weight.shape[1]
    rank = adapter_shrink_weight.shape[2]
    half_width = columns // 2
    block = column_block(columns)
    block_count = columns // block

    def from_owner(x, j):
        return lax.ppermute(x, "adapter", [(s, (s - j) % owner_count) for s in range(owner_count)])

    def from_either(x):
        pairs = []
        for group, j in ((0, 1), (1, 3)):
            for s in range(owner_count):
                pairs.append(
                    (group * owner_count + s, group * owner_count + (s - j) % owner_count)
                )
        return lax.ppermute(x, ("groups", "adapter"), pairs)

    def from_tensor(x, m):
        return lax.ppermute(x, "tensor", [(s, s ^ m) for s in range(4)])

    def from_mirror(x, m):
        return lax.ppermute(x, "adapter", [(s, s ^ m) for s in range(owner_count)])

    def from_group(x):
        return lax.ppermute(x, "groups", [(0, 1), (1, 0)])

    weight = pltpu.with_memory_space_constraint(base_up_weight, pltpu.HBM)
    expand = pltpu.with_memory_space_constraint(adapter_expand_weight, pltpu.HBM)
    offsets = (2, 1, 3)
    blocks = [from_owner(tokens, j) for j in offsets]

    cuts = [block_count * k // 14 for k in (0, 4, 8, 11, 14)]
    parts = list(zip(cuts[:-1], cuts[1:]))
    loads = [block_count * k // 14 for k in (0, 4, 8, 11, 12, 14)]
    bands = 4
    small = [
        pltpu.with_memory_space_constraint(x, pltpu.HBM)
        for x in (
            adapter_slot_index.reshape(1, owner_count),
            row_adapter_index.reshape(1, row_count),
            tokens,
            adapter_shrink_weight[0].T,
        )
    ]
    whole, half, own, slots, index, mine, shrink, held = kernel_call(
        functools.partial(cut_kernel, block, range(loads[1]), len(small)),
        "cut_expand",
        1,
        1,
        1,
        in_specs=[anywhere] * (2 + len(small)),
        out_specs=[vmem] * (4 + len(small)),
        out_shape=[pltpu.VMEM((rank_block, w), bf16) for w in (columns, half_width, columns)]
        + [pltpu.VMEM(x.shape, x.dtype) for x in small]
        + [pltpu.VMEM((loads[1], depth, block), bf16)],
        scratch_shapes=[
            pltpu.SemaphoreType.DMA((3 + len(small),)),
            pltpu.SemaphoreType.DMA((loads[1], bands)),
        ],
    )(expand, weight, *small)
    loaded = [held]
    whole, half = from_either(whole), from_owner(half, 2)

    rows, keep, send, slot = kernel_call(
        functools.partial(gather_kernel, (0, *offsets)),
        "gather_rows",
        1,
        1,
        4,
        in_specs=[vmem] * (owner_count + 3),
        out_specs=[vmem] * 4,
        out_shape=[jax.ShapeDtypeStruct((row_count, depth), bf16)]
        + [jax.ShapeDtypeStruct((rank // 2, row_count), f32)] * 2
        + [jax.ShapeDtypeStruct((1, row_count), jnp.int32)],
        scratch_shapes=[pltpu.VMEM((row_count, depth), bf16), pltpu.VMEM((rank, row_count), f32)],
    )(
        slots,
        index,
        mine,
        *blocks,
        shrink,
    )

    def base_part(n, *after):
        first, last = parts[n]
        streamed = n + 1 == len(parts)
        numbers = range(loads[n + 1], loads[n + 2])
        places, used = [], []
        for number in range(first, numbers[0] if streamed else last):
            source = max(k for k in range(len(loads) - 1) if loads[k] <= number)
            if source not in used:
                used.append(source)
            places.append((used.index(source), number - loads[source]))
        near = n < 2
        ahead = pltpu.VMEM((len(numbers), depth, block), bf16)
        out = kernel_call(
            functools.partial(base_kernel, block, places, numbers, streamed),
            "base_part",
            3 * 2 * row_count * depth * (last - first) * block if near else 1,
            3 * 2 * depth * (last - first) * block if near else 1,
            12,
            in_specs=[vmem, anywhere] + [vmem] * len(used) + [anywhere] * len(after),
            out_specs=[vmem] * (1 if streamed else 2),
            out_shape=[jax.ShapeDtypeStruct((row_count, (last - first) * block), f32)]
            + ([] if streamed else [ahead]),
            scratch_shapes=([ahead] if streamed else [])
            + [pltpu.SemaphoreType.DMA((len(numbers), bands))],
        )(rows, weight, *[loaded[k] for k in used], *after)
        loaded.append(out[-1])
        return out[0]

    arrived = from_tensor(send, 1)
    base_0 = base_part(0, send)
    arrived, base_0 = lax.optimization_barrier((arrived, base_0))
    pair = keep + arrived
    arrived = from_tensor(pair[rank_block:], 2)
    base_1 = base_part(1, pair)
    arrived, base_1, whole, half = lax.optimization_barrier((arrived, base_1, whole, half))
    shrunk = (adapter_scale * (pair[:rank_block] + arrived)).astype(bf16)
    packed = kernel_call(
        pack_kernel,
        "pack_pieces",
        1,
        1,
        2,
        in_specs=[vmem] * 2,
        out_specs=vmem,
        out_shape=jax.ShapeDtypeStruct((rank_block, columns + half_width), bf16),
    )(whole, half)
    swapped = from_group(packed)
    bases = [base_0, base_1]
    for m, n in ((1, 2), (2, 3)):
        arrived = from_mirror(shrunk, m)
        base = base_part(n, shrunk, packed)
        arrived, base = lax.optimization_barrier((arrived, base))
        bases.append(base)
        shrunk = shrunk + arrived

    middle = block_count // 2 * block
    splits = [(0, middle), (middle, columns)]
    widths = [last - first for first, last in splits]
    quarter = row_count // 4
    out = kernel_call(
        functools.partial(delta_kernel, block, splits),
        "add_delta",
        1,
        1,
        8,
        in_specs=[vmem] * (len(bases) + 6),
        out_specs=[vmem] * (2 + 2 * len(splits)),
        out_shape=[
            jax.ShapeDtypeStruct((quarter, w), f32) for w in (columns, columns, *widths, *widths)
        ],
        scratch_shapes=[
            pltpu.VMEM((row_count, rank_block * owner_count), f32),
            pltpu.VMEM((row_count, rank_block * owner_count), bf16),
            pltpu.VMEM((rank_block, columns), bf16),
        ],
    )(slot, *bases, own, shrunk, whole, half, swapped)
    own_keep, own_send = out[:2]
    crossed = []
    for keep, send in zip(out[2:4], out[4:6]):
        crossed.append(from_tensor((keep + from_tensor(send, 1)).astype(bf16), 2))
    kept = own_keep + from_tensor(own_send, 1)
    return jnp.concatenate(
        [
            (kept[:, first:last] + part.astype(f32)).astype(bf16)
            for (first, last), part in zip(splits, crossed)
        ],
        axis=1,
    )


def on_device(tokens, base_up_weight, adapter_shrink_weight, adapter_expand_weight, *index):
    pairs = lax.axis_size("groups") == 2 and lax.axis_size("tensor") == 4
    few = lax.axis_size("adapter") == 4
    columns = base_up_weight.shape[1]
    even = columns % 512 == 0 and columns >= 4096 and tokens.shape[0] % 16 == 0
    arrange = paired if pairs and few and even else general
    return arrange(
        tokens, base_up_weight, adapter_shrink_weight, adapter_expand_weight, *index
    )


def solution(mesh):
    placed = (
        P(("groups", "adapter"), "tensor"),
        P("tensor", "adapter"),
        P("adapter", "tensor", None),
        P("adapter", "tensor", None),
        P("groups", None),
        P(),
    )
    return jax.shard_map(
        on_device,
        mesh=mesh,
        in_specs=placed,
        out_specs=P(("groups", "tensor"), "adapter"),
        check_vma=False,
    )
```

time: 51 us -> 43.8 us (0.86)
  starting transfers between devices: 25.1 us -> 16 us
  waiting for transfers between devices: 8.81 us -> 11.1 us
    ppermute x2, starting transfers between devices: 8.83 us -> 0.01 us  [from_mirror(): return lax.ppermute(x, 'adapter', [(s, s ^ m) for s in range(owner_count)])]
    ppermute x6 -> x4, starting transfers between devices: 10.4 us -> 6.06 us  [from_owner(): lax.ppermute(x, 'adapter', [(s, (s - j) % owner_count) for s in range(own...]
    ppermute x0 -> x1, starting transfers between devices: none -> 3.13 us  [from_either(): return lax.ppermute(x, ('groups', 'adapter'), pairs)]
    ppermute x2, waiting for transfers between devices: 0.72 us -> 3.79 us  [from_mirror(): return lax.ppermute(x, 'adapter', [(s, s ^ m) for s in range(owner_count)])]
    ppermute x6 -> x4, waiting for transfers between devices: 1.91 us -> 0.78 us  [from_owner(): lax.ppermute(x, 'adapter', [(s, (s - j) % owner_count) for s in range(own...]
    ppermute x1, starting transfers between devices: 1.53 us -> 2.35 us  [from_group(): return lax.ppermute(x, 'groups', [(0, 1), (1, 0)])]
    select_n x1 -> x0, other arithmetic: 0.75 us -> none  [paired(): return jnp.where(g == 0, first, second)]
    concatenate x0 -> x1, other arithmetic: none -> 0.7 us  [paired(): jnp.concatenate([(kept[:, first:last] + part.astype(f32)).astype(bf16) fo...]
  transfers between devices with their start and end apart: 17 -> 15, of which waited for: 7 -> 7; matrix products, arithmetic and copies ran while one was open for 0% -> 0% of each run, Pallas kernels for 21% -> 35%
where the time goes in v10:
time: 43.8 us; the launch traced here: 43.7 us
  starting transfers between devices  16 us (37%)
  Pallas kernels  15.6 us (36%)
  waiting for transfers between devices  11.1 us (25%)
  other arithmetic  0.88 us (2%)
    pallas_call x4, Pallas kernels, base_part(): kernel_call(functools.partial(base_kernel, block, places, numbers, stream...  10.8 us
    ppermute x7, waiting for transfers between devices, from_tensor(): return lax.ppermute(x, 'tensor', [(s, s ^ m) for s in range(4)])  6.38 us
    ppermute x4, starting transfers between devices, from_owner(): lax.ppermute(x, 'adapter', [(s, (s - j) % owner_count) for s in range(own...  6.06 us
    ppermute x7, starting transfers between devices, from_tensor(): return lax.ppermute(x, 'tensor', [(s, s ^ m) for s in range(4)])  4.42 us
    pallas_call x1, Pallas kernels, paired(): kernel_call(functools.partial(cut_kernel, block, range(loads[1]), len(sma...  3.99 us
    ppermute x2, waiting for transfers between devices, from_mirror(): return lax.ppermute(x, 'adapter', [(s, s ^ m) for s in range(owner_count)])  3.79 us
    ppermute x1, starting transfers between devices, from_either(): return lax.ppermute(x, ('groups', 'adapter'), pairs)  3.13 us
    ppermute x1, starting transfers between devices, from_group(): return lax.ppermute(x, 'groups', [(0, 1), (1, 0)])  2.35 us
  transfers between devices with their start and end apart: 15, of which 7 were waited for; matrix products, arithmetic and copies ran while one was open for 0% of the time, Pallas kernels for 35%

profile of v10, /device:TPU:0, one launch (start us, length us, event | category | flops | bytes accessed | tf_op | source)
XLA Modules:
  0.0 43.7 jit_solution(11641568793248740417)
XLA Ops:
  0.0 4.0 %collective-permute-start = (bf16[16,2048]{1,0:T(8,128)(2,1)}, bf16[16,2048]{1,0:T(8,128)(2,1)S(1)}, u32[]{:S(2)}, u32[]{:S(2)}) collective-permute-start(bf16[16,2048]{1,0:T(8,128)(2,1)} %refs_2_.1), channel_id=1, source_target_pairs={{0,8},{4,12},{8,0},{12,4},{1,9},{5,13},{9,1},{13,5},{2,10},{6,14},... | collective-permute-start | bytes 196616 | tf_op jit(solution)/shard_map/ppermute | solution.py:236
  4.0 1.3 %collective-permute-start.1 = (bf16[16,2048]{1,0:T(8,128)(2,1)}, bf16[16,2048]{1,0:T(8,128)(2,1)S(1)}, u32[]{:S(2)}, u32[]{:S(2)}) collective-permute-start(bf16[16,2048]{1,0:T(8,128)(2,1)} %refs_2_.1), channel_id=1, source_target_pairs={{0,12},{4,0},{8,4},{12,8},{1,13},{5,1},{9,5},{13,9},{2,14},{6,2},{... | collective-permute-start | bytes 196616 | tf_op jit(solution)/shard_map/ppermute | solution.py:236
  5.4 0.7 %collective-permute-start.2 = (bf16[16,2048]{1,0:T(8,128)(2,1)}, bf16[16,2048]{1,0:T(8,128)(2,1)S(1)}, u32[]{:S(2)}, u32[]{:S(2)}) collective-permute-start(bf16[16,2048]{1,0:T(8,128)(2,1)} %refs_2_.1), channel_id=1, source_target_pairs={{0,4},{4,8},{8,12},{12,0},{1,5},{5,9},{9,13},{13,1},{2,6},{6,10},{... | collective-permute-start | bytes 196616 | tf_op jit(solution)/shard_map/ppermute | solution.py:236
  6.1 4.0 %cut_expand.1 = (bf16[16,7168]{1,0:T(8,128)(2,1)S(1)}, bf16[16,3584]{1,0:T(8,128)(2,1)S(1)}, bf16[16,7168]{1,0:T(8,128)(2,1)S(1)}, s32[1,4]{1,0:T(1,128)S(1)}, s...) custom-call(bf16[1,16,28672]{2,1,0:T(8,128)(2,1)} %expand.1, ...), custom_call_target="tpu_custom_call" | custom-call | flops 1 | bytes 1 | tf_op jit(solution)/shard_map/cut_expand/pallas_call | solution.py:274
  10.1 3.1 %collective-permute-start.5 = (bf16[16,7168]{1,0:T(8,128)(2,1)S(1)}, bf16[16,7168]{1,0:T(8,128)(2,1)S(1)}, u32[]{:S(2)}, u32[]{:S(2)}) collective-permute-start(bf16[16,7168]{1,0:T(8,128)(2,1)S(1)} %get-tuple-element.53), channel_id=1, source_target_pairs={{0,12},{4,0},{8,4},{12,8},{16,20},{20,24},{24,28},{28,16},{1,13},{... | collective-permute-start | bytes 688136 | tf_op jit(solution)/shard_map/ppermute | solution.py:245
  13.2 0.0 collective-permute-start.6
  13.2 0.0 collective-permute-done.refs_1_
  13.2 0.0 collective-permute-done.1.refs_2_
  13.2 0.0 collective-permute-done.2.refs_3_
  13.2 0.3 gather_rows.1
  13.5 0.1 collective-permute-start.3
  13.6 3.6 %base_part.4 = (f32[64,2048]{1,0:T(8,128)S(1)}, bf16[4,2048,512]{2,1,0:T(8,128)(2,1)S(1)}) custom-call(bf16[64,2048]{1,0:T(8,128)(2,1)S(1)} %get-tuple-element.45.rows, bf16[2048,7168]{1,0:T(8,128)(2,1)} %weight.9, bf16[4,2048,512]{2,1,0:T(8,128)(2,1)S(1)} %get-tuple-element.46.refs_0_, f32[32,64]{1,0:T(8,128)S(1)} %get-tuple-element.44.refs_1_), custom_call_target="tpu_custom_call" | custom-call | flops 1610612736 | bytes 25165824 | tf_op jit(solution)/shard_map/base_part/pallas_call | solution.py:325
  17.1 0.0 collective-permute-done.3
  17.2 1.6 %collective-permute-start.4 = (f32[16,64]{1,0:T(8,128)S(1)}, f32[16,64]{1,0:T(8,128)S(1)}, u32[]{:S(2)}, u32[]{:S(2)}) collective-permute-start(f32[16,64]{1,0:T(8,128)S(1)} %slice.16), channel_id=1, source_target_pairs={{0,2},{1,3},{2,0},{3,1},{4,6},{5,7},{6,4},{7,5},{8,10},{9,11},{10,... | collective-permute-start | bytes 12296 | tf_op jit(solution)/shard_map/ppermute | solution.py:248
  18.7 3.0 %base_part.5 = (f32[64,2048]{1,0:T(8,128)S(1)}, bf16[3,2048,512]{2,1,0:T(8,128)(2,1)S(1)}) custom-call(bf16[64,2048]{1,0:T(8,128)(2,1)S(1)} %get-tuple-element.45.rows, bf16[2048,7168]{1,0:T(8,128)(2,1)} %weight.9, bf16[4,2048,512]{2,1,0:T(8,128)(2,1)S(1)} %get-tuple-element.51.refs_0_, f32[32,64]{1,0:T(8,128)S(1)} %add.27.refs_1_), custom_call_target="tpu_custom_call" | custom-call | flops 1610612736 | bytes 25165824 | tf_op jit(solution)/shard_map/base_part/pallas_call | solution.py:325
  21.7 0.0 collective-permute-done.4
  21.7 0.8 %collective-permute-done.6.half.refs_7_ = bf16[16,3584]{1,0:T(8,128)(2,1)S(1)} collective-permute-done((bf16[16,3584]{1,0:T(8,128)(2,1)S(1)}, bf16[16,3584]{1,0:T(8,128)(2,1)S(1)}, u32[]{:S(2)}, u32[]{:S(2)}) %collective-permute-start.6) | collective-permute-done | bytes 114720 | tf_op jit(solution)/shard_map/ppermute | solution.py:236
  22.5 0.0 collective-permute-done.5.whole.refs_6_
  22.5 2.3 %collective-permute-start.9 = (bf16[16,10752]{1,0:T(8,128)(2,1)S(1)}, bf16[16,10752]{1,0:T(8,128)(2,1)S(1)}, u32[]{:S(2)}, u32[]{:S(2)}) collective-permute-start(bf16[16,10752]{1,0:T(8,128)(2,1)S(1)} %pack_pieces.1.refs_2_), channel_id=1, source_target_pairs={{0,16},{16,0},{1,17},{17,1},{2,18},{18,2},{3,19},{19,3},{4,20},{20... | collective-permute-start | bytes 1032200 | tf_op jit(solution)/shard_map/ppermute | solution.py:254
  24.9 0.0 collective-permute-start.7
  24.9 1.6 %base_part.6 = (f32[64,1536]{1,0:T(8,128)S(1)}, bf16[1,2048,512]{2,1,0:T(8,128)(2,1)S(1)}) custom-call(bf16[64,2048]{1,0:T(8,128)(2,1)S(1)} %get-tuple-element.45.rows, bf16[2048,7168]{1,0:T(8,128)(2,1)} %weight.9, bf16[3,2048,512]{2,1,0:T(8,128)(2,1)S(1)} %get-tuple-element.57.refs_0_, bf16[16,64]{1,0:T(8,128)(2,1)S(1)} %fusion.3.refs_1_, ...), custom_call_target="tpu_custom_call" | custom-call | flops 1 | bytes 1 | tf_op jit(solution)/shard_map/base_part/pallas_call | solution.py:325
  26.4 2.0 %collective-permute-done.7 = bf16[16,64]{1,0:T(8,128)(2,1)S(1)} collective-permute-done((bf16[16,64]{1,0:T(8,128)(2,1)S(1)}, bf16[16,64]{1,0:T(8,128)(2,1)S(1)}, u32[]{:S(2)}, u32[]{:S(2)}) %collective-permute-start.7) | collective-permute-done | bytes 2080 | tf_op jit(solution)/shard_map/ppermute | solution.py:251
  28.5 0.0 collective-permute-start.8
  28.5 2.7 %base_part.7.refs_3_ = f32[64,1536]{1,0:T(8,128)S(1)} custom-call(bf16[64,2048]{1,0:T(8,128)(2,1)S(1)} %get-tuple-element.45.rows, bf16[2048,7168]{1,0:T(8,128)(2,1)} %weight.9, bf16[1,2048,512]{2,1,0:T(8,128)(2,1)S(1)} %get-tuple-element.63.refs_0_, bf16[16,64]{1,0:T(8,128)(2,1)S(1)} %add.29.refs_1_, bf16[16,10752]{1,0:T(8,128)(2,1)S(1)} %pack_pieces.1.refs_2_), custom_call_target="tpu_custom_call" | custom-call | flops 1 | bytes 1 | tf_op jit(solution)/shard_map/base_part/pallas_call | solution.py:325
  31.2 1.8 %collective-permute-done.8 = bf16[16,64]{1,0:T(8,128)(2,1)S(1)} collective-permute-done((bf16[16,64]{1,0:T(8,128)(2,1)S(1)}, bf16[16,64]{1,0:T(8,128)(2,1)S(1)}, u32[]{:S(2)}, u32[]{:S(2)}) %collective-permute-start.8) | collective-permute-done | bytes 2080 | tf_op jit(solution)/shard_map/ppermute | solution.py:251
  33.0 0.1 collective-permute-done.9.refs_8_
  33.1 0.5 %add_delta.1 = (f32[16,7168]{1,0:T(8,128)S(1)}, f32[16,7168]{1,0:T(8,128)S(1)}, f32[16,3584]{1,0:T(8,128)S(1)}, f32[16,3584]{1,0:T(8,128)S(1)}, f32[16,3584]{1,0:T(8,128)S(1)}, /*index=5*/f32[16,3584]{1,0:T(8,128)S(1)}) custom-call(s32[1,64]{1,0:T(1,128)S(1)} %get-tuple-element.43.slot, f32[64,2048]{1,0:T(8,128)S(1)} %get-tuple-element.48.refs_0_, ...), custom_call_target="tpu_custom_call" | custom-call | flops 1 | bytes 1 | tf_op jit(solution)/shard_map/add_delta/pallas_call | solution.py:372
  33.6 0.1 collective-permute-start.13
  33.7 0.5 %collective-permute-start.11 = (f32[16,3584]{1,0:T(8,128)S(1)}, f32[16,3584]{1,0:T(8,128)S(1)}, u32[]{:S(2)}, u32[]{:S(2)}) collective-permute-start(f32[16,3584]{1,0:T(8,128)S(1)} %get-tuple-element.70), channel_id=1, source_target_pairs={{0,1},{1,0},{2,3},{3,2},{4,5},{5,4},{6,7},{7,6},{8,9},{9,8},{10,11... | collective-permute-start | bytes 688136 | tf_op jit(solution)/shard_map/ppermute | solution.py:248
  34.2 0.1 collective-permute-start.10
  34.3 0.9 %collective-permute-done.13 = f32[16,3584]{1,0:T(8,128)S(1)} collective-permute-done((f32[16,3584]{1,0:T(8,128)S(1)}, f32[16,3584]{1,0:T(8,128)S(1)}, u32[]{:S(2)}, u32[]{:S(2)}) %collective-permute-start.13) | collective-permute-done | bytes 229408 | tf_op jit(solution)/shard_map/ppermute | solution.py:248
  35.2 1.6 %collective-permute-start.14 = (bf16[16,3584]{1,0:T(8,128)(2,1)S(1)}, bf16[16,3584]{1,0:T(8,128)(2,1)S(1)}, u32[]{:S(2)}, u32[]{:S(2)}) collective-permute-start(bf16[16,3584]{1,0:T(8,128)(2,1)S(1)} %add_convert_fusion), channel_id=1, source_target_pairs={{0,2},{1,3},{2,0},{3,1},{4,6},{5,7},{6,4},{7,5},{8,10},{9,11},{10,... | collective-permute-start | bytes 344072 | tf_op jit(solution)/shard_map/ppermute | solution.py:248
  36.8 0.0 collective-permute-done.11
  36.8 0.6 %collective-permute-start.12 = (bf16[16,3584]{1,0:T(8,128)(2,1)S(1)}, bf16[16,3584]{1,0:T(8,128)(2,1)S(1)}, u32[]{:S(2)}, u32[]{:S(2)}) collective-permute-start(bf16[16,3584]{1,0:T(8,128)(2,1)S(1)} %add_convert_fusion.1), channel_id=1, source_target_pairs={{0,2},{1,3},{2,0},{3,1},{4,6},{5,7},{6,4},{7,5},{8,10},{9,11},{10,... | collective-permute-start | bytes 344072 | tf_op jit(solution)/shard_map/ppermute | solution.py:248
  37.4 0.0 collective-permute-done.10
  37.4 3.8 %collective-permute-done.14 = bf16[16,3584]{1,0:T(8,128)(2,1)S(1)} collective-permute-done((bf16[16,3584]{1,0:T(8,128)(2,1)S(1)}, bf16[16,3584]{1,0:T(8,128)(2,1)S(1)}, u32[]{:S(2)}, u32[]{:S(2)}) %collective-permute-start.14) | collective-permute-done | bytes 114720 | tf_op jit(solution)/shard_map/ppermute | solution.py:248
  41.3 1.7 %collective-permute-done.12 = bf16[16,3584]{1,0:T(8,128)(2,1)S(1)} collective-permute-done((bf16[16,3584]{1,0:T(8,128)(2,1)S(1)}, bf16[16,3584]{1,0:T(8,128)(2,1)S(1)}, u32[]{:S(2)}, u32[]{:S(2)}) %collective-permute-start.12) | collective-permute-done | bytes 114720 | tf_op jit(solution)/shard_map/ppermute | solution.py:248
  42.9 0.1 fusion.1
  43.0 0.7 %pad_maximum_fusion = bf16[16,7168]{1,0:T(8,128)(2,1)} fusion(bf16[16,3584]{1,0:T(8,128)(2,1)S(1)} %get-tuple-element.74, bf16[16,3584]{1,0:T(8,128)(2,1)S(1)} %get-tuple-element.73), kind=kLoop, calls=%fused_computation.4 | loop fusion | flops 458752 | bytes 458752 | tf_op jit(solution)/shard_map/concatenate | solution.py:394
  (9 shorter events, 0.1 us)
Async XLA Ops:
  0.0 13.2 %collective-permute-start = (bf16[16,2048]{1,0:T(8,128)(2,1)}, bf16[16,2048]{1,0:T(8,128)(2,1)S(1)}, u32[]{:S(2)}, u32[]{:S(2)}) collective-permute-start(bf16[16,2048]{1,0:T(8,128)(2,1)} %refs_2_.1), channel_id=1, source_target_pairs={{0,8},{4,12},{8,0},{12,4},{1,9},{5,13},{9,1},{13,5},{2,10},{6,14},... | collective-permute-start | bytes 196616 | tf_op jit(solution)/shard_map/ppermute | solution.py:236
  4.0 9.2 %collective-permute-start.1 = (bf16[16,2048]{1,0:T(8,128)(2,1)}, bf16[16,2048]{1,0:T(8,128)(2,1)S(1)}, u32[]{:S(2)}, u32[]{:S(2)}) collective-permute-start(bf16[16,2048]{1,0:T(8,128)(2,1)} %refs_2_.1), channel_id=1, source_target_pairs={{0,12},{4,0},{8,4},{12,8},{1,13},{5,1},{9,5},{13,9},{2,14},{6,2},{... | collective-permute-start | bytes 196616 | tf_op jit(solution)/shard_map/ppermute | solution.py:236
  5.4 7.8 %collective-permute-start.2 = (bf16[16,2048]{1,0:T(8,128)(2,1)}, bf16[16,2048]{1,0:T(8,128)(2,1)S(1)}, u32[]{:S(2)}, u32[]{:S(2)}) collective-permute-start(bf16[16,2048]{1,0:T(8,128)(2,1)} %refs_2_.1), channel_id=1, source_target_pairs={{0,4},{4,8},{8,12},{12,0},{1,5},{5,9},{9,13},{13,1},{2,6},{6,10},{... | collective-permute-start | bytes 196616 | tf_op jit(solution)/shard_map/ppermute | solution.py:236
  10.1 12.4 %collective-permute-start.5 = (bf16[16,7168]{1,0:T(8,128)(2,1)S(1)}, bf16[16,7168]{1,0:T(8,128)(2,1)S(1)}, u32[]{:S(2)}, u32[]{:S(2)}) collective-permute-start(bf16[16,7168]{1,0:T(8,128)(2,1)S(1)} %get-tuple-element.53), channel_id=1, source_target_pairs={{0,12},{4,0},{8,4},{12,8},{16,20},{20,24},{24,28},{28,16},{1,13},{... | collective-permute-start | bytes 688136 | tf_op jit(solution)/shard_map/ppermute | solution.py:245
  13.2 9.3 %collective-permute-start.6 = (bf16[16,3584]{1,0:T(8,128)(2,1)S(1)}, bf16[16,3584]{1,0:T(8,128)(2,1)S(1)}, u32[]{:S(2)}, u32[]{:S(2)}) collective-permute-start(bf16[16,3584]{1,0:T(8,128)(2,1)S(1)} %get-tuple-element.54), channel_id=1, source_target_pairs={{0,8},{4,12},{8,0},{12,4},{1,9},{5,13},{9,1},{13,5},{2,10},{6,14},... | collective-permute-start | bytes 344072 | tf_op jit(solution)/shard_map/ppermute | solution.py:236
  13.5 3.7 %collective-permute-start.3 = (f32[32,64]{1,0:T(8,128)S(1)}, f32[32,64]{1,0:T(8,128)S(1)}, u32[]{:S(2)}, u32[]{:S(2)}) collective-permute-start(f32[32,64]{1,0:T(8,128)S(1)} %get-tuple-element.44.refs_1_), channel_id=1, source_target_pairs={{0,1},{1,0},{2,3},{3,2},{4,5},{5,4},{6,7},{7,6},{8,9},{9,8},{10,11... | collective-permute-start | bytes 24584 | tf_op jit(solution)/shard_map/ppermute | solution.py:248
  17.2 4.5 %collective-permute-start.4 = (f32[16,64]{1,0:T(8,128)S(1)}, f32[16,64]{1,0:T(8,128)S(1)}, u32[]{:S(2)}, u32[]{:S(2)}) collective-permute-start(f32[16,64]{1,0:T(8,128)S(1)} %slice.16), channel_id=1, source_target_pairs={{0,2},{1,3},{2,0},{3,1},{4,6},{5,7},{6,4},{7,5},{8,10},{9,11},{10,... | collective-permute-start | bytes 12296 | tf_op jit(solution)/shard_map/ppermute | solution.py:248
  22.5 10.6 %collective-permute-start.9 = (bf16[16,10752]{1,0:T(8,128)(2,1)S(1)}, bf16[16,10752]{1,0:T(8,128)(2,1)S(1)}, u32[]{:S(2)}, u32[]{:S(2)}) collective-permute-start(bf16[16,10752]{1,0:T(8,128)(2,1)S(1)} %pack_pieces.1.refs_2_), channel_id=1, source_target_pairs={{0,16},{16,0},{1,17},{17,1},{2,18},{18,2},{3,19},{19,3},{4,20},{20... | collective-permute-start | bytes 1032200 | tf_op jit(solution)/shard_map/ppermute | solution.py:254
  24.9 3.6 %collective-permute-start.7 = (bf16[16,64]{1,0:T(8,128)(2,1)S(1)}, bf16[16,64]{1,0:T(8,128)(2,1)S(1)}, u32[]{:S(2)}, u32[]{:S(2)}) collective-permute-start(bf16[16,64]{1,0:T(8,128)(2,1)S(1)} %fusion.3.refs_1_), channel_id=1, source_target_pairs={{0,4},{4,0},{8,12},{12,8},{1,5},{5,1},{9,13},{13,9},{2,6},{6,2},{1... | collective-permute-start | bytes 6152 | tf_op jit(solution)/shard_map/ppermute | solution.py:251
  28.5 4.5 %collective-permute-start.8 = (bf16[16,64]{1,0:T(8,128)(2,1)S(1)}, bf16[16,64]{1,0:T(8,128)(2,1)S(1)}, u32[]{:S(2)}, u32[]{:S(2)}) collective-permute-start(bf16[16,64]{1,0:T(8,128)(2,1)S(1)} %add.29.refs_1_), channel_id=1, source_target_pairs={{0,8},{4,12},{8,0},{12,4},{1,9},{5,13},{9,1},{13,5},{2,10},{6,14},... | collective-permute-start | bytes 6152 | tf_op jit(solution)/shard_map/ppermute | solution.py:251
  33.6 1.6 %collective-permute-start.13 = (f32[16,3584]{1,0:T(8,128)S(1)}, f32[16,3584]{1,0:T(8,128)S(1)}, u32[]{:S(2)}, u32[]{:S(2)}) collective-permute-start(f32[16,3584]{1,0:T(8,128)S(1)} %get-tuple-element.72), channel_id=1, source_target_pairs={{0,1},{1,0},{2,3},{3,2},{4,5},{5,4},{6,7},{7,6},{8,9},{9,8},{10,11... | collective-permute-start | bytes 688136 | tf_op jit(solution)/shard_map/ppermute | solution.py:248
  33.7 3.1 %collective-permute-start.11 = (f32[16,3584]{1,0:T(8,128)S(1)}, f32[16,3584]{1,0:T(8,128)S(1)}, u32[]{:S(2)}, u32[]{:S(2)}) collective-permute-start(f32[16,3584]{1,0:T(8,128)S(1)} %get-tuple-element.70), channel_id=1, source_target_pairs={{0,1},{1,0},{2,3},{3,2},{4,5},{5,4},{6,7},{7,6},{8,9},{9,8},{10,11... | collective-permute-start | bytes 688136 | tf_op jit(solution)/shard_map/ppermute | solution.py:248
  34.2 3.2 %collective-permute-start.10 = (f32[16,7168]{1,0:T(8,128)S(1)}, f32[16,7168]{1,0:T(8,128)S(1)}, u32[]{:S(2)}, u32[]{:S(2)}) collective-permute-start(f32[16,7168]{1,0:T(8,128)S(1)} %get-tuple-element.68), channel_id=1, source_target_pairs={{0,1},{1,0},{2,3},{3,2},{4,5},{5,4},{6,7},{7,6},{8,9},{9,8},{10,11... | collective-permute-start | bytes 1376264 | tf_op jit(solution)/shard_map/ppermute | solution.py:248
  35.2 6.1 %collective-permute-start.14 = (bf16[16,3584]{1,0:T(8,128)(2,1)S(1)}, bf16[16,3584]{1,0:T(8,128)(2,1)S(1)}, u32[]{:S(2)}, u32[]{:S(2)}) collective-permute-start(bf16[16,3584]{1,0:T(8,128)(2,1)S(1)} %add_convert_fusion), channel_id=1, source_target_pairs={{0,2},{1,3},{2,0},{3,1},{4,6},{5,7},{6,4},{7,5},{8,10},{9,11},{10,... | collective-permute-start | bytes 344072 | tf_op jit(solution)/shard_map/ppermute | solution.py:248
  36.8 6.1 %collective-permute-start.12 = (bf16[16,3584]{1,0:T(8,128)(2,1)S(1)}, bf16[16,3584]{1,0:T(8,128)(2,1)S(1)}, u32[]{:S(2)}, u32[]{:S(2)}) collective-permute-start(bf16[16,3584]{1,0:T(8,128)(2,1)S(1)} %add_convert_fusion.1), channel_id=1, source_target_pairs={{0,2},{1,3},{2,0},{3,1},{4,6},{5,7},{6,4},{7,5},{8,10},{9,11},{10,... | collective-permute-start | bytes 344072 | tf_op jit(solution)/shard_map/ppermute | solution.py:248

commit v11 on v9

--- a/solution.py
+++ b/solution.py
@@ -137,7 +137,7 @@
         target[at : at + rank_block, :] = partial[pl.ds(start, rank_block), :]
 
 
-def base_kernel(start_of, block, places, numbers, rows, weight, *refs):
+def base_kernel(start_of, block, numbers, rows, weight, held, *refs):
     copies = []
     if numbers:
         total, ahead, sem = refs[-3:]
@@ -149,9 +149,9 @@
 
     @pl.when(lax.axis_index("tensor") >= 0)
     def _():
-        for n, (which, index) in enumerate(places):
+        for n in range(held.shape[0]):
             total[:, n * block : (n + 1) * block] = jnp.dot(
-                rows[...], refs[which][index], preferred_element_type=f32
+                rows[...], held[n], preferred_element_type=f32
             )
 
     for copy in copies:
@@ -249,7 +249,7 @@
     near_half, far_half = near_count - near_count // 2, (block_count - near_count + 1) // 2
     cuts = (0, near_half, near_count, near_count + far_half, block_count)
     parts = list(zip(cuts[:-1], cuts[1:]))
-    loads = (0, min(6, block_count), min(10, block_count), block_count, block_count, block_count)
+    loads = [*cuts, block_count]
     start_of = functools.partial(block_start, near_width, far_width, block)
     bands = 4
 
@@ -283,9 +283,8 @@
     )(expand, weight, *small)
     pieces, own = cut[: owner_count - 1], cut[owner_count - 1]
     slots, index, mine, shrink, held = cut[owner_count:]
-    blocks = [from_owner(mine, j) for j in offsets]
+    blocks = [from_owner(tokens, j) for j in offsets]
     loaded = [held]
-    near = [from_owner(piece, j) for piece, j in zip(pieces, offsets)]
 
     rows, keep, send, slot = kernel_call(
         functools.partial(gather_kernel, (0, *offsets)),
@@ -310,26 +309,19 @@
     def base_part(n, *after):
         first, last = parts[n]
         numbers = range(loads[n + 1], loads[n + 2])
-        places, used = [], []
-        for number in range(first, last):
-            source = max(k for k in range(len(loads) - 1) if loads[k] <= number)
-            if source not in used:
-                used.append(source)
-            places.append((used.index(source), number - loads[source]))
-        near = first < near_count
         out = kernel_call(
-            functools.partial(base_kernel, start_of, block, places, numbers),
+            functools.partial(base_kernel, start_of, block, numbers),
             "base_part",
-            2 * row_count * depth * (last - first) * block if near else 1,
-            2 * depth * (last - first) * block if near else 1,
+            10**10,
+            1,
             4,
-            in_specs=[vmem, anywhere] + [vmem] * len(used) + [anywhere] * len(after),
+            in_specs=[vmem, anywhere, vmem] + [anywhere] * len(after),
             out_specs=[vmem] * (2 if numbers else 1),
             out_shape=[jax.ShapeDtypeStruct((row_count, (last - first) * block), f32)]
             + ([pltpu.VMEM((len(numbers), depth, block), bf16)] if numbers else []),
             scratch_shapes=[pltpu.SemaphoreType.DMA((len(numbers), bands))] if numbers else [],
-        )(rows, weight, *[loaded[k] for k in used], *after)
-        loaded.append(out[1] if numbers else None)
+        )(rows, weight, loaded[n], *after)
+        loaded.append(out[-1])
         return out[0]
 
     def delta_part(is_far, bases, pieces):
@@ -352,14 +344,19 @@
             ],
         )(slot, *bases, own, shrunk, *pieces)
 
+    *pieces, own, send = lax.optimization_barrier((*pieces, own, send))
     arrived = from_tensor(send, 1)
-    base_0 = base_part(0, send)
-    arrived, base_0 = lax.optimization_barrier((arrived, base_0))
+    near = [from_owner(piece, j) for piece, j in zip(pieces, offsets)]
     pair = keep + arrived
     arrived = from_tensor(pair[rank_block:], 2)
-    base_1 = base_part(1, pair)
+    base_0 = base_part(0, pair)
+    arrived, base_0 = lax.optimization_barrier((arrived, base_0))
+    shrunk = (adapter_scale * (pair[:rank_block] + arrived)).astype(bf16)
+    arrived = from_mirror(shrunk, 1)
+    base_1 = base_part(1, shrunk)
     arrived, base_1, *near = lax.optimization_barrier((arrived, base_1, *near))
-    shrunk = (adapter_scale * (pair[:rank_block] + arrived)).astype(bf16)
+    shrunk = shrunk + arrived
+    arrived = from_mirror(shrunk, 2)
     packed = kernel_call(
         functools.partial(forward_kernel, far_width),
         "pack_far",
@@ -371,26 +368,23 @@
         out_shape=jax.ShapeDtypeStruct(((owner_count - 1) * rank_block, far_width), bf16),
     )(*near)
     far = from_group(packed)
-    steps = []
-    m = 1
-    while m < owner_count:
-        steps.append(m)
-        m *= 2
-    base_far = []
-    for m, n in zip(steps, (2, 3)):
-        arrived = from_mirror(shrunk, m)
-        base = base_part(n, shrunk, packed)
-        arrived, base = lax.optimization_barrier((arrived, base))
-        base_far.append(base)
-        shrunk = shrunk + arrived
-
-    halves = []
-    for is_far, bases, pieces in ((False, [base_0, base_1], near), (True, base_far, [far])):
-        own_keep, cross_keep, own_send, cross_send = delta_part(is_far, bases, pieces)
-        cross = (cross_keep + from_tensor(cross_send, 1)).astype(bf16)
-        kept = own_keep + from_tensor(own_send, 1)
-        crossed = from_tensor(cross, 2)
-        halves.append((kept + crossed.astype(f32)).astype(bf16))
+    arrived, packed = lax.optimization_barrier((arrived, packed))
+    shrunk = shrunk + arrived
+
+    own_keep, cross_keep, own_send, cross_send = delta_part(False, [base_0, base_1], near)
+    arrived = from_tensor(cross_send, 1)
+    kept = own_keep + from_tensor(own_send, 1)
+    base_2 = base_part(2, cross_send)
+    arrived, base_2 = lax.optimization_barrier((arrived, base_2))
+    cross = (cross_keep + arrived).astype(bf16)
+    crossed = from_tensor(cross, 2)
+    base_3 = base_part(3, cross)
+    own_keep, cross_keep, own_send, cross_send = delta_part(True, [base_2, base_3], [far])
+    own_send, cross_send, crossed = lax.optimization_barrier((own_send, cross_send, crossed))
+    halves = [(kept + crossed.astype(f32)).astype(bf16)]
+    cross = (cross_keep + from_tensor(cross_send, 1)).astype(bf16)
+    kept = own_keep + from_tensor(own_send, 1)
+    halves.append((kept + from_tensor(cross, 2).astype(f32)).astype(bf16))
     first = jnp.concatenate(halves, axis=1)
     second = jnp.concatenate(halves[::-1], axis=1)
     return jnp.where(g == 0, first, second)

time: 51 us -> 46.3 us (0.908)
  starting transfers between devices: 25.1 us -> 20.3 us
    ppermute x2, starting transfers between devices: 8.83 us -> 3.77 us  [from_mirror(): return lax.ppermute(x, 'adapter', [(s, s ^ m) for s in range(owner_count)])]
    pallas_call x1, Pallas kernels: 5.26 us -> 4 us  [paired(): kernel_call(functools.partial(cut_kernel, owner_count, offsets, far_width...]
    pallas_call x4, Pallas kernels: 9.64 us -> 10.7 us  [base_part(): kernel_call(functools.partial(base_kernel, start_of, block, numbers), 'ba...]
    ppermute x8, starting transfers between devices: 4.33 us -> 5.35 us  [from_tensor(): return lax.ppermute(x, 'tensor', [(s, s ^ m) for s in range(4)])]
    ppermute x6, starting transfers between devices: 10.4 us -> 9.69 us  [from_owner(): lax.ppermute(x, 'adapter', [(s, (s - j) % owner_count) for s in range(own...]
    ppermute x1, waiting for transfers between devices: 0.01 us -> 0.55 us  [from_group(): return lax.ppermute(x, 'groups', [(0, 1), (1, 0)])]
  transfers between devices with their start and end apart: 17 -> 17, of which waited for: 7 -> 6; matrix products, arithmetic and copies ran while one was open for 0% -> 0% of each run, Pallas kernels for 21% -> 33%
where the time goes in v11:
time: 46.3 us; the launch traced here: 46.1 us
  starting transfers between devices  20.3 us (44%)
  Pallas kernels  15.7 us (34%)
  waiting for transfers between devices  9.02 us (19%)
  other arithmetic  0.9 us (2%)
    pallas_call x4, Pallas kernels, base_part(): kernel_call(functools.partial(base_kernel, start_of, block, numbers), 'ba...  10.7 us
    ppermute x6, starting transfers between devices, from_owner(): lax.ppermute(x, 'adapter', [(s, (s - j) % owner_count) for s in range(own...  9.69 us
    ppermute x8, waiting for transfers between devices, from_tensor(): return lax.ppermute(x, 'tensor', [(s, s ^ m) for s in range(4)])  6.49 us
    ppermute x8, starting transfers between devices, from_tensor(): return lax.ppermute(x, 'tensor', [(s, s ^ m) for s in range(4)])  5.35 us
    pallas_call x1, Pallas kernels, paired(): kernel_call(functools.partial(cut_kernel, owner_count, offsets, far_width...  4 us
    ppermute x2, starting transfers between devices, from_mirror(): return lax.ppermute(x, 'adapter', [(s, s ^ m) for s in range(owner_count)])  3.77 us
    ppermute x6, waiting for transfers between devices, from_owner(): lax.ppermute(x, 'adapter', [(s, (s - j) % owner_count) for s in range(own...  1.58 us
    ppermute x1, starting transfers between devices, from_group(): return lax.ppermute(x, 'groups', [(0, 1), (1, 0)])  1.54 us
  transfers between devices with their start and end apart: 17, of which 6 were waited for; matrix products, arithmetic and copies ran while one was open for 0% of the time, Pallas kernels for 33%

profile of v11, /device:TPU:0, one launch (start us, length us, event | category | flops | bytes accessed | tf_op | source)
XLA Modules:
  0.0 46.1 jit_solution(12170254245005332838)
XLA Ops:
  0.0 4.0 %collective-permute-start = (bf16[16,2048]{1,0:T(8,128)(2,1)}, bf16[16,2048]{1,0:T(8,128)(2,1)S(1)}, u32[]{:S(2)}, u32[]{:S(2)}) collective-permute-start(bf16[16,2048]{1,0:T(8,128)(2,1)} %refs_2_.1), channel_id=1, source_target_pairs={{0,8},{4,12},{8,0},{12,4},{1,9},{5,13},{9,1},{13,5},{2,10},{6,14},... | collective-permute-start | bytes 196616 | tf_op jit(solution)/shard_map/ppermute | solution.py:234
  4.0 1.3 %collective-permute-start.1 = (bf16[16,2048]{1,0:T(8,128)(2,1)}, bf16[16,2048]{1,0:T(8,128)(2,1)S(1)}, u32[]{:S(2)}, u32[]{:S(2)}) collective-permute-start(bf16[16,2048]{1,0:T(8,128)(2,1)} %refs_2_.1), channel_id=1, source_target_pairs={{0,12},{4,0},{8,4},{12,8},{1,13},{5,1},{9,5},{13,9},{2,14},{6,2},{... | collective-permute-start | bytes 196616 | tf_op jit(solution)/shard_map/ppermute | solution.py:234
  5.4 0.7 %collective-permute-start.2 = (bf16[16,2048]{1,0:T(8,128)(2,1)}, bf16[16,2048]{1,0:T(8,128)(2,1)S(1)}, u32[]{:S(2)}, u32[]{:S(2)}) collective-permute-start(bf16[16,2048]{1,0:T(8,128)(2,1)} %refs_2_.1), channel_id=1, source_target_pairs={{0,4},{4,8},{8,12},{12,0},{1,5},{5,9},{9,13},{13,1},{2,6},{6,10},{... | collective-permute-start | bytes 196616 | tf_op jit(solution)/shard_map/ppermute | solution.py:234
  6.1 4.0 %cut_expand.1 = (bf16[16,4096]{1,0:T(8,128)(2,1)S(1)}, bf16[16,4096]{1,0:T(8,128)(2,1)S(1)}, bf16[16,4096]{1,0:T(8,128)(2,1)S(1)}, bf16[16,7168]{1,0:T(8,128)(2,...) custom-call(bf16[1,16,28672]{2,1,0:T(8,128)(2,1)} %expand.1, ...), custom_call_target="tpu_custom_call" | custom-call | flops 1 | bytes 1 | tf_op jit(solution)/shard_map/cut_expand/pallas_call | solution.py:265
  10.1 0.0 collective-permute-done.refs_1_
  10.1 0.0 collective-permute-done.1.refs_2_
  10.1 1.6 %collective-permute-done.2.refs_3_ = bf16[16,2048]{1,0:T(8,128)(2,1)S(1)} collective-permute-done((bf16[16,2048]{1,0:T(8,128)(2,1)}, bf16[16,2048]{1,0:T(8,128)(2,1)S(1)}, u32[]{:S(2)}, u32[]{:S(2)}) %collective-permute-start.2) | collective-permute-done | bytes 65568 | tf_op jit(solution)/shard_map/ppermute | solution.py:234
  11.7 0.3 gather_rows.1
  11.9 0.1 collective-permute-start.3
  12.0 1.6 %collective-permute-start.6 = (bf16[16,4096]{1,0:T(8,128)(2,1)S(1)}, bf16[16,4096]{1,0:T(8,128)(2,1)S(1)}, u32[]{:S(2)}, u32[]{:S(2)}) collective-permute-start(bf16[16,4096]{1,0:T(8,128)(2,1)S(1)} %get-tuple-element.69), channel_id=1, source_target_pairs={{0,8},{4,12},{8,0},{12,4},{1,9},{5,13},{9,1},{13,5},{2,10},{6,14},... | collective-permute-start | bytes 393224 | tf_op jit(solution)/shard_map/ppermute | solution.py:234
  13.6 0.8 %collective-permute-start.7 = (bf16[16,4096]{1,0:T(8,128)(2,1)S(1)}, bf16[16,4096]{1,0:T(8,128)(2,1)S(1)}, u32[]{:S(2)}, u32[]{:S(2)}) collective-permute-start(bf16[16,4096]{1,0:T(8,128)(2,1)S(1)} %get-tuple-element.70), channel_id=1, source_target_pairs={{0,12},{4,0},{8,4},{12,8},{1,13},{5,1},{9,5},{13,9},{2,14},{6,2},{... | collective-permute-start | bytes 393224 | tf_op jit(solution)/shard_map/ppermute | solution.py:234
  14.4 1.2 %collective-permute-start.8 = (bf16[16,4096]{1,0:T(8,128)(2,1)S(1)}, bf16[16,4096]{1,0:T(8,128)(2,1)S(1)}, u32[]{:S(2)}, u32[]{:S(2)}) collective-permute-start(bf16[16,4096]{1,0:T(8,128)(2,1)S(1)} %get-tuple-element.71), channel_id=1, source_target_pairs={{0,4},{4,8},{8,12},{12,0},{1,5},{5,9},{9,13},{13,1},{2,6},{6,10},{... | collective-permute-start | bytes 393224 | tf_op jit(solution)/shard_map/ppermute | solution.py:234
  15.6 0.0 collective-permute-done.3
  15.6 1.6 %collective-permute-start.4 = (f32[16,64]{1,0:T(8,128)S(1)}, f32[16,64]{1,0:T(8,128)S(1)}, u32[]{:S(2)}, u32[]{:S(2)}) collective-permute-start(f32[16,64]{1,0:T(8,128)S(1)} %slice.8), channel_id=1, source_target_pairs={{0,2},{1,3},{2,0},{3,1},{4,6},{5,7},{6,4},{7,5},{8,10},{9,11},{10,... | collective-permute-start | bytes 12296 | tf_op jit(solution)/shard_map/ppermute | solution.py:237
  17.2 3.6 %base_part.4 = (f32[64,2048]{1,0:T(8,128)S(1)}, bf16[4,2048,512]{2,1,0:T(8,128)(2,1)S(1)}) custom-call(bf16[64,2048]{1,0:T(8,128)(2,1)S(1)} %get-tuple-element.62.rows, bf16[2048,7168]{1,0:T(8,128)(2,1)} %weight.9, bf16[4,2048,512]{2,1,0:T(8,128)(2,1)S(1)} %get-tuple-element.63.held, f32[32,64]{1,0:T(8,128)S(1)} %add.30.refs_0_), custom_call_target="tpu_custom_call" | custom-call | flops 10000000000 | bytes 1 | tf_op jit(solution)/shard_map/base_part/pallas_call | solution.py:312
  20.8 0.0 collective-permute-done.4
  20.8 0.7 %collective-permute-start.5 = (bf16[16,64]{1,0:T(8,128)(2,1)S(1)}, bf16[16,64]{1,0:T(8,128)(2,1)S(1)}, u32[]{:S(2)}, u32[]{:S(2)}) collective-permute-start(bf16[16,64]{1,0:T(8,128)(2,1)S(1)} %fusion.1.refs_0_), channel_id=1, source_target_pairs={{0,4},{4,0},{8,12},{12,8},{1,5},{5,1},{9,13},{13,9},{2,6},{6,2},{1... | collective-permute-start | bytes 6152 | tf_op jit(solution)/shard_map/ppermute | solution.py:240
  21.5 3.0 %base_part.5 = (f32[64,2048]{1,0:T(8,128)S(1)}, bf16[3,2048,512]{2,1,0:T(8,128)(2,1)S(1)}) custom-call(bf16[64,2048]{1,0:T(8,128)(2,1)S(1)} %get-tuple-element.62.rows, bf16[2048,7168]{1,0:T(8,128)(2,1)} %weight.9, bf16[4,2048,512]{2,1,0:T(8,128)(2,1)S(1)} %get-tuple-element.67.held, bf16[16,64]{1,0:T(8,128)(2,1)S(1)} %fusion.1.refs_0_), custom_call_target="tpu_custom_call" | custom-call | flops 10000000000 | bytes 1 | tf_op jit(solution)/shard_map/base_part/pallas_call | solution.py:312
  24.5 0.4 collective-permute-done.5
  24.8 0.0 collective-permute-done.6.refs_0_.refs_4_
  24.8 0.0 collective-permute-done.7.refs_1_.refs_5_
  24.8 0.0 collective-permute-done.8.refs_2_.refs_6_
  24.9 3.1 %collective-permute-start.9 = (bf16[16,64]{1,0:T(8,128)(2,1)S(1)}, bf16[16,64]{1,0:T(8,128)(2,1)S(1)}, u32[]{:S(2)}, u32[]{:S(2)}) collective-permute-start(bf16[16,64]{1,0:T(8,128)(2,1)S(1)} %add.32), channel_id=1, source_target_pairs={{0,8},{4,12},{8,0},{12,4},{1,9},{5,13},{9,1},{13,5},{2,10},{6,14},... | collective-permute-start | bytes 6152 | tf_op jit(solution)/shard_map/ppermute | solution.py:240
  28.0 1.5 %collective-permute-start.12 = (bf16[48,3072]{1,0:T(8,128)(2,1)S(1)}, bf16[48,3072]{1,0:T(8,128)(2,1)S(1)}, u32[]{:S(2)}, u32[]{:S(2)}) collective-permute-start(bf16[48,3072]{1,0:T(8,128)(2,1)S(1)} %pack_far.1), channel_id=1, source_target_pairs={{0,16},{16,0},{1,17},{17,1},{2,18},{18,2},{3,19},{19,3},{4,20},{20... | collective-permute-start | bytes 884744 | tf_op jit(solution)/shard_map/ppermute | solution.py:243
  29.5 0.0 collective-permute-done.9
  29.6 0.4 delta_part.2
  29.9 0.1 collective-permute-start.11
  30.0 2.9 %base_part.6 = (f32[64,1536]{1,0:T(8,128)S(1)}, bf16[3,2048,512]{2,1,0:T(8,128)(2,1)S(1)}) custom-call(bf16[64,2048]{1,0:T(8,128)(2,1)S(1)} %get-tuple-element.62.rows, bf16[2048,7168]{1,0:T(8,128)(2,1)} %weight.9, bf16[3,2048,512]{2,1,0:T(8,128)(2,1)S(1)} %get-tuple-element.82.held, f32[16,4096]{1,0:T(8,128)S(1)} %get-tuple-element.81.refs_0_), custom_call_target="tpu_custom_call" | custom-call | flops 10000000000 | bytes 1 | tf_op jit(solution)/shard_map/base_part/pallas_call | solution.py:312
  33.0 0.0 collective-permute-done.11
  33.0 1.6 %collective-permute-start.13 = (bf16[16,4096]{1,0:T(8,128)(2,1)S(1)}, bf16[16,4096]{1,0:T(8,128)(2,1)S(1)}, u32[]{:S(2)}, u32[]{:S(2)}) collective-permute-start(bf16[16,4096]{1,0:T(8,128)(2,1)S(1)} %add_convert_fusion.1.refs_0_), channel_id=1, source_target_pairs={{0,2},{1,3},{2,0},{3,1},{4,6},{5,7},{6,4},{7,5},{8,10},{9,11},{10,... | collective-permute-start | bytes 393224 | tf_op jit(solution)/shard_map/ppermute | solution.py:237
  34.6 1.2 %base_part.7.refs_1_ = f32[64,1536]{1,0:T(8,128)S(1)} custom-call(bf16[64,2048]{1,0:T(8,128)(2,1)S(1)} %get-tuple-element.62.rows, bf16[2048,7168]{1,0:T(8,128)(2,1)} %weight.9, bf16[3,2048,512]{2,1,0:T(8,128)(2,1)S(1)} %get-tuple-element.85.held, bf16[16,4096]{1,0:T(8,128)(2,1)S(1)} %add_convert_fusion.1.refs_0_), custom_call_target="tpu_custom_call" | custom-call | flops 10000000000 | bytes 1 | tf_op jit(solution)/shard_map/base_part/pallas_call | solution.py:312
  35.8 0.5 %collective-permute-done.12.refs_4_ = bf16[48,3072]{1,0:T(8,128)(2,1)S(1)} collective-permute-done((bf16[48,3072]{1,0:T(8,128)(2,1)S(1)}, bf16[48,3072]{1,0:T(8,128)(2,1)S(1)}, u32[]{:S(2)}, u32[]{:S(2)}) %collective-permute-start.12) | collective-permute-done | bytes 294944 | tf_op jit(solution)/shard_map/ppermute | solution.py:243
  36.3 0.3 delta_part.3
  36.7 2.3 %collective-permute-done.13 = bf16[16,4096]{1,0:T(8,128)(2,1)S(1)} collective-permute-done((bf16[16,4096]{1,0:T(8,128)(2,1)S(1)}, bf16[16,4096]{1,0:T(8,128)(2,1)S(1)}, u32[]{:S(2)}, u32[]{:S(2)}) %collective-permute-start.13) | collective-permute-done | bytes 131104 | tf_op jit(solution)/shard_map/ppermute | solution.py:237
  39.0 0.0 collective-permute-start.15
  39.0 0.5 %collective-permute-start.10 = (f32[16,4096]{1,0:T(8,128)S(1)}, f32[16,4096]{1,0:T(8,128)S(1)}, u32[]{:S(2)}, u32[]{:S(2)}) collective-permute-start(f32[16,4096]{1,0:T(8,128)S(1)} %get-tuple-element.80), channel_id=1, source_target_pairs={{0,1},{1,0},{2,3},{3,2},{4,5},{5,4},{6,7},{7,6},{8,9},{9,8},{10,11... | collective-permute-start | bytes 786440 | tf_op jit(solution)/shard_map/ppermute | solution.py:237
  39.5 0.0 collective-permute-start.14
  39.5 0.9 %collective-permute-done.15 = f32[16,3072]{1,0:T(8,128)S(1)} collective-permute-done((f32[16,3072]{1,0:T(8,128)S(1)}, f32[16,3072]{1,0:T(8,128)S(1)}, u32[]{:S(2)}, u32[]{:S(2)}) %collective-permute-start.15) | collective-permute-done | bytes 196640 | tf_op jit(solution)/shard_map/ppermute | solution.py:237
  40.4 1.6 %collective-permute-start.16 = (bf16[16,3072]{1,0:T(8,128)(2,1)S(1)}, bf16[16,3072]{1,0:T(8,128)(2,1)S(1)}, u32[]{:S(2)}, u32[]{:S(2)}) collective-permute-start(bf16[16,3072]{1,0:T(8,128)(2,1)S(1)} %add_convert_fusion.3), channel_id=1, source_target_pairs={{0,2},{1,3},{2,0},{3,1},{4,6},{5,7},{6,4},{7,5},{8,10},{9,11},{10,... | collective-permute-start | bytes 294920 | tf_op jit(solution)/shard_map/ppermute | solution.py:237
  42.0 0.0 collective-permute-done.10
  42.0 0.0 collective-permute-done.14
  42.1 3.3 %collective-permute-done.16 = bf16[16,3072]{1,0:T(8,128)(2,1)S(1)} collective-permute-done((bf16[16,3072]{1,0:T(8,128)(2,1)S(1)}, bf16[16,3072]{1,0:T(8,128)(2,1)S(1)}, u32[]{:S(2)}, u32[]{:S(2)}) %collective-permute-start.16) | collective-permute-done | bytes 98336 | tf_op jit(solution)/shard_map/ppermute | solution.py:237
  45.4 0.8 %maximum_select_fusion = bf16[16,7168]{1,0:T(8,128)(2,1)} fusion(bf16[16,3072]{1,0:T(8,128)(2,1)S(1)} %add_convert_fusion.2, bf16[16,4096]{1,0:T(8,128)(2,1)S(1)} %add_convert_fusion, pred[]{:T(512)S(6)} %eq.3), kind=kLoop, calls=%fused_computation.2 | loop fusion | flops 1032192 | bytes 458753 | tf_op jit(solution)/shard_map/jit(_where)/select_n | solution.py:390
  (10 shorter events, 0.2 us)
Async XLA Ops:
  0.0 10.1 %collective-permute-start = (bf16[16,2048]{1,0:T(8,128)(2,1)}, bf16[16,2048]{1,0:T(8,128)(2,1)S(1)}, u32[]{:S(2)}, u32[]{:S(2)}) collective-permute-start(bf16[16,2048]{1,0:T(8,128)(2,1)} %refs_2_.1), channel_id=1, source_target_pairs={{0,8},{4,12},{8,0},{12,4},{1,9},{5,13},{9,1},{13,5},{2,10},{6,14},... | collective-permute-start | bytes 196616 | tf_op jit(solution)/shard_map/ppermute | solution.py:234
  4.0 6.0 %collective-permute-start.1 = (bf16[16,2048]{1,0:T(8,128)(2,1)}, bf16[16,2048]{1,0:T(8,128)(2,1)S(1)}, u32[]{:S(2)}, u32[]{:S(2)}) collective-permute-start(bf16[16,2048]{1,0:T(8,128)(2,1)} %refs_2_.1), channel_id=1, source_target_pairs={{0,12},{4,0},{8,4},{12,8},{1,13},{5,1},{9,5},{13,9},{2,14},{6,2},{... | collective-permute-start | bytes 196616 | tf_op jit(solution)/shard_map/ppermute | solution.py:234
  5.4 6.3 %collective-permute-start.2 = (bf16[16,2048]{1,0:T(8,128)(2,1)}, bf16[16,2048]{1,0:T(8,128)(2,1)S(1)}, u32[]{:S(2)}, u32[]{:S(2)}) collective-permute-start(bf16[16,2048]{1,0:T(8,128)(2,1)} %refs_2_.1), channel_id=1, source_target_pairs={{0,4},{4,8},{8,12},{12,0},{1,5},{5,9},{9,13},{13,1},{2,6},{6,10},{... | collective-permute-start | bytes 196616 | tf_op jit(solution)/shard_map/ppermute | solution.py:234
  11.9 3.7 %collective-permute-start.3 = (f32[32,64]{1,0:T(8,128)S(1)}, f32[32,64]{1,0:T(8,128)S(1)}, u32[]{:S(2)}, u32[]{:S(2)}) collective-permute-start(f32[32,64]{1,0:T(8,128)S(1)} %get-tuple-element.61), channel_id=1, source_target_pairs={{0,1},{1,0},{2,3},{3,2},{4,5},{5,4},{6,7},{7,6},{8,9},{9,8},{10,11... | collective-permute-start | bytes 24584 | tf_op jit(solution)/shard_map/ppermute | solution.py:237
  12.0 12.8 %collective-permute-start.6 = (bf16[16,4096]{1,0:T(8,128)(2,1)S(1)}, bf16[16,4096]{1,0:T(8,128)(2,1)S(1)}, u32[]{:S(2)}, u32[]{:S(2)}) collective-permute-start(bf16[16,4096]{1,0:T(8,128)(2,1)S(1)} %get-tuple-element.69), channel_id=1, source_target_pairs={{0,8},{4,12},{8,0},{12,4},{1,9},{5,13},{9,1},{13,5},{2,10},{6,14},... | collective-permute-start | bytes 393224 | tf_op jit(solution)/shard_map/ppermute | solution.py:234
  13.6 11.2 %collective-permute-start.7 = (bf16[16,4096]{1,0:T(8,128)(2,1)S(1)}, bf16[16,4096]{1,0:T(8,128)(2,1)S(1)}, u32[]{:S(2)}, u32[]{:S(2)}) collective-permute-start(bf16[16,4096]{1,0:T(8,128)(2,1)S(1)} %get-tuple-element.70), channel_id=1, source_target_pairs={{0,12},{4,0},{8,4},{12,8},{1,13},{5,1},{9,5},{13,9},{2,14},{6,2},{... | collective-permute-start | bytes 393224 | tf_op jit(solution)/shard_map/ppermute | solution.py:234
  14.4 10.4 %collective-permute-start.8 = (bf16[16,4096]{1,0:T(8,128)(2,1)S(1)}, bf16[16,4096]{1,0:T(8,128)(2,1)S(1)}, u32[]{:S(2)}, u32[]{:S(2)}) collective-permute-start(bf16[16,4096]{1,0:T(8,128)(2,1)S(1)} %get-tuple-element.71), channel_id=1, source_target_pairs={{0,4},{4,8},{8,12},{12,0},{1,5},{5,9},{9,13},{13,1},{2,6},{6,10},{... | collective-permute-start | bytes 393224 | tf_op jit(solution)/shard_map/ppermute | solution.py:234
  15.6 5.1 %collective-permute-start.4 = (f32[16,64]{1,0:T(8,128)S(1)}, f32[16,64]{1,0:T(8,128)S(1)}, u32[]{:S(2)}, u32[]{:S(2)}) collective-permute-start(f32[16,64]{1,0:T(8,128)S(1)} %slice.8), channel_id=1, source_target_pairs={{0,2},{1,3},{2,0},{3,1},{4,6},{5,7},{6,4},{7,5},{8,10},{9,11},{10,... | collective-permute-start | bytes 12296 | tf_op jit(solution)/shard_map/ppermute | solution.py:237
  20.8 4.0 %collective-permute-start.5 = (bf16[16,64]{1,0:T(8,128)(2,1)S(1)}, bf16[16,64]{1,0:T(8,128)(2,1)S(1)}, u32[]{:S(2)}, u32[]{:S(2)}) collective-permute-start(bf16[16,64]{1,0:T(8,128)(2,1)S(1)} %fusion.1.refs_0_), channel_id=1, source_target_pairs={{0,4},{4,0},{8,12},{12,8},{1,5},{5,1},{9,13},{13,9},{2,6},{6,2},{1... | collective-permute-start | bytes 6152 | tf_op jit(solution)/shard_map/ppermute | solution.py:240
  24.9 4.7 %collective-permute-start.9 = (bf16[16,64]{1,0:T(8,128)(2,1)S(1)}, bf16[16,64]{1,0:T(8,128)(2,1)S(1)}, u32[]{:S(2)}, u32[]{:S(2)}) collective-permute-start(bf16[16,64]{1,0:T(8,128)(2,1)S(1)} %add.32), channel_id=1, source_target_pairs={{0,8},{4,12},{8,0},{12,4},{1,9},{5,13},{9,1},{13,5},{2,10},{6,14},... | collective-permute-start | bytes 6152 | tf_op jit(solution)/shard_map/ppermute | solution.py:240
  28.0 8.4 %collective-permute-start.12 = (bf16[48,3072]{1,0:T(8,128)(2,1)S(1)}, bf16[48,3072]{1,0:T(8,128)(2,1)S(1)}, u32[]{:S(2)}, u32[]{:S(2)}) collective-permute-start(bf16[48,3072]{1,0:T(8,128)(2,1)S(1)} %pack_far.1), channel_id=1, source_target_pairs={{0,16},{16,0},{1,17},{17,1},{2,18},{18,2},{3,19},{19,3},{4,20},{20... | collective-permute-start | bytes 884744 | tf_op jit(solution)/shard_map/ppermute | solution.py:243
  29.9 3.0 %collective-permute-start.11 = (f32[16,4096]{1,0:T(8,128)S(1)}, f32[16,4096]{1,0:T(8,128)S(1)}, u32[]{:S(2)}, u32[]{:S(2)}) collective-permute-start(f32[16,4096]{1,0:T(8,128)S(1)} %get-tuple-element.81.refs_0_), channel_id=1, source_target_pairs={{0,1},{1,0},{2,3},{3,2},{4,5},{5,4},{6,7},{7,6},{8,9},{9,8},{10,11... | collective-permute-start | bytes 786440 | tf_op jit(solution)/shard_map/ppermute | solution.py:237
  33.0 6.0 %collective-permute-start.13 = (bf16[16,4096]{1,0:T(8,128)(2,1)S(1)}, bf16[16,4096]{1,0:T(8,128)(2,1)S(1)}, u32[]{:S(2)}, u32[]{:S(2)}) collective-permute-start(bf16[16,4096]{1,0:T(8,128)(2,1)S(1)} %add_convert_fusion.1.refs_0_), channel_id=1, source_target_pairs={{0,2},{1,3},{2,0},{3,1},{4,6},{5,7},{6,4},{7,5},{8,10},{9,11},{10,... | collective-permute-start | bytes 393224 | tf_op jit(solution)/shard_map/ppermute | solution.py:237
  39.0 1.4 %collective-permute-start.15 = (f32[16,3072]{1,0:T(8,128)S(1)}, f32[16,3072]{1,0:T(8,128)S(1)}, u32[]{:S(2)}, u32[]{:S(2)}) collective-permute-start(f32[16,3072]{1,0:T(8,128)S(1)} %get-tuple-element.94), channel_id=1, source_target_pairs={{0,1},{1,0},{2,3},{3,2},{4,5},{5,4},{6,7},{7,6},{8,9},{9,8},{10,11... | collective-permute-start | bytes 589832 | tf_op jit(solution)/shard_map/ppermute | solution.py:237
  39.0 3.0 %collective-permute-start.10 = (f32[16,4096]{1,0:T(8,128)S(1)}, f32[16,4096]{1,0:T(8,128)S(1)}, u32[]{:S(2)}, u32[]{:S(2)}) collective-permute-start(f32[16,4096]{1,0:T(8,128)S(1)} %get-tuple-element.80), channel_id=1, source_target_pairs={{0,1},{1,0},{2,3},{3,2},{4,5},{5,4},{6,7},{7,6},{8,9},{9,8},{10,11... | collective-permute-start | bytes 786440 | tf_op jit(solution)/shard_map/ppermute | solution.py:237
  39.5 2.6 %collective-permute-start.14 = (f32[16,3072]{1,0:T(8,128)S(1)}, f32[16,3072]{1,0:T(8,128)S(1)}, u32[]{:S(2)}, u32[]{:S(2)}) collective-permute-start(f32[16,3072]{1,0:T(8,128)S(1)} %get-tuple-element.92), channel_id=1, source_target_pairs={{0,1},{1,0},{2,3},{3,2},{4,5},{5,4},{6,7},{7,6},{8,9},{9,8},{10,11... | collective-permute-start | bytes 589832 | tf_op jit(solution)/shard_map/ppermute | solution.py:237
  40.4 4.9 %collective-permute-start.16 = (bf16[16,3072]{1,0:T(8,128)(2,1)S(1)}, bf16[16,3072]{1,0:T(8,128)(2,1)S(1)}, u32[]{:S(2)}, u32[]{:S(2)}) collective-permute-start(bf16[16,3072]{1,0:T(8,128)(2,1)S(1)} %add_convert_fusion.3), channel_id=1, source_target_pairs={{0,2},{1,3},{2,0},{3,1},{4,6},{5,7},{6,4},{7,5},{8,10},{9,11},{10,... | collective-permute-start | bytes 294920 | tf_op jit(solution)/shard_map/ppermute | solution.py:237

commit v12 on v10

--- a/solution.py
+++ b/solution.py
@@ -127,9 +127,13 @@
         target[at : at + rank_block, :] = partial[pl.ds(start, rank_block), :]
 
 
-def base_kernel(block, places, numbers, streamed, rows, weight, *refs):
-    total, ahead, sem = refs[-3:]
-    copies = weight_copies(block, numbers, weight, ahead, sem)
+def base_kernel(block, places, numbers, rows, weight, *refs):
+    copies = []
+    if numbers:
+        total, ahead, sem = refs[-3:]
+        copies = weight_copies(block, numbers, weight, ahead, sem)
+    else:
+        total = refs[-1]
     for copy in copies:
         copy.start()
 
@@ -140,41 +144,28 @@
                 rows[...], refs[which][index], preferred_element_type=f32
             )
 
-    bands = sem.shape[1]
-    for n in range(len(numbers)):
-        for copy in copies[n * bands : (n + 1) * bands]:
-            copy.wait()
-        if streamed:
-            at = (len(places) + n) * block
-            total[:, at : at + block] = jnp.dot(
-                rows[...], ahead[n], preferred_element_type=f32
-            )
-
-
-def pack_kernel(whole, half, packed):
-    columns = whole.shape[1]
-    packed[:, :columns] = whole[...]
-    packed[:, columns:] = half[...]
+    for copy in copies:
+        copy.wait()
 
 
 def delta_kernel(block, splits, slot, *refs):
-    bases, refs = refs[: -len(splits) * 2 - 10], refs[-len(splits) * 2 - 10 :]
-    own, shrunk, whole, half, packed, own_keep, own_send = refs[:7]
-    cross_keep, cross_send = refs[7 : 7 + len(splits)], refs[7 + len(splits) : 7 + 2 * len(splits)]
+    bases, refs = refs[: -len(splits) * 2 - 11], refs[-len(splits) * 2 - 11 :]
+    own, shrunk, whole, half, far_whole, far_half, own_keep, own_send = refs[:8]
+    cross_keep, cross_send = refs[8 : 8 + len(splits)], refs[8 + len(splits) : 8 + 2 * len(splits)]
     flat, ordered, two = refs[-3:]
     g, a, t = (lax.axis_index(name) for name in ("groups", "adapter", "tensor"))
     row_count = bases[0].shape[0]
     quarter = row_count // 4
-    columns, half_width = whole.shape[1], half.shape[1]
+    half_width = half.shape[1]
 
     @pl.when(g == 0)
     def _():
         two[:, :half_width] = half[...]
-        two[:, half_width:] = packed[:, columns:]
+        two[:, half_width:] = far_half[...]
 
     @pl.when(g != 0)
     def _():
-        two[:, :half_width] = packed[:, columns:]
+        two[:, :half_width] = far_half[...]
         two[:, half_width:] = half[...]
 
     merged = shrunk[...].astype(f32)
@@ -192,7 +183,7 @@
         for column in range(0, base.shape[1], block):
             span = slice(at, at + block)
             expand = jnp.concatenate(
-                [own[:, span], whole[:, span], packed[:, span], two[:, span]], axis=0
+                [own[:, span], whole[:, span], far_whole[:, span], two[:, span]], axis=0
             )
             total = base[:, column : column + block] + jnp.dot(
                 left, expand, preferred_element_type=f32
@@ -260,7 +251,7 @@
 
     cuts = [block_count * k // 14 for k in (0, 4, 8, 11, 14)]
     parts = list(zip(cuts[:-1], cuts[1:]))
-    loads = [block_count * k // 14 for k in (0, 4, 8, 11, 12, 14)]
+    loads = [block_count * k // 14 for k in (0, 5, 8, 11, 14, 14)]
     bands = 4
     small = [
         pltpu.with_memory_space_constraint(x, pltpu.HBM)
@@ -288,7 +279,7 @@
         ],
     )(expand, weight, *small)
     loaded = [held]
-    whole, half = from_either(whole), from_owner(half, 2)
+    whole = from_either(whole)
 
     rows, keep, send, slot = kernel_call(
         functools.partial(gather_kernel, (0, *offsets)),
@@ -312,58 +303,47 @@
 
     def base_part(n, *after):
         first, last = parts[n]
-        streamed = n + 1 == len(parts)
         numbers = range(loads[n + 1], loads[n + 2])
         places, used = [], []
-        for number in range(first, numbers[0] if streamed else last):
+        for number in range(first, last):
             source = max(k for k in range(len(loads) - 1) if loads[k] <= number)
             if source not in used:
                 used.append(source)
             places.append((used.index(source), number - loads[source]))
-        near = n < 2
-        ahead = pltpu.VMEM((len(numbers), depth, block), bf16)
         out = kernel_call(
-            functools.partial(base_kernel, block, places, numbers, streamed),
+            functools.partial(base_kernel, block, places, numbers),
             "base_part",
-            3 * 2 * row_count * depth * (last - first) * block if near else 1,
-            3 * 2 * depth * (last - first) * block if near else 1,
-            12,
+            (2 * 10**9, 10**10, 1, 1)[n],
+            1,
+            4,
             in_specs=[vmem, anywhere] + [vmem] * len(used) + [anywhere] * len(after),
-            out_specs=[vmem] * (1 if streamed else 2),
+            out_specs=[vmem] * (2 if numbers else 1),
             out_shape=[jax.ShapeDtypeStruct((row_count, (last - first) * block), f32)]
-            + ([] if streamed else [ahead]),
-            scratch_shapes=([ahead] if streamed else [])
-            + [pltpu.SemaphoreType.DMA((len(numbers), bands))],
+            + ([pltpu.VMEM((len(numbers), depth, block), bf16)] if numbers else []),
+            scratch_shapes=[pltpu.SemaphoreType.DMA((len(numbers), bands))] if numbers else [],
         )(rows, weight, *[loaded[k] for k in used], *after)
         loaded.append(out[-1])
         return out[0]
 
+    half, send = lax.optimization_barrier((half, send))
     arrived = from_tensor(send, 1)
-    base_0 = base_part(0, send)
-    arrived, base_0 = lax.optimization_barrier((arrived, base_0))
+    half = from_owner(half, 2)
     pair = keep + arrived
     arrived = from_tensor(pair[rank_block:], 2)
-    base_1 = base_part(1, pair)
-    arrived, base_1, whole, half = lax.optimization_barrier((arrived, base_1, whole, half))
+    bases = [base_part(0, pair)]
+    arrived, whole, bases[0] = lax.optimization_barrier((arrived, whole, bases[0]))
     shrunk = (adapter_scale * (pair[:rank_block] + arrived)).astype(bf16)
-    packed = kernel_call(
-        pack_kernel,
-        "pack_pieces",
-        1,
-        1,
-        2,
-        in_specs=[vmem] * 2,
-        out_specs=vmem,
-        out_shape=jax.ShapeDtypeStruct((rank_block, columns + half_width), bf16),
-    )(whole, half)
-    swapped = from_group(packed)
-    bases = [base_0, base_1]
-    for m, n in ((1, 2), (2, 3)):
-        arrived = from_mirror(shrunk, m)
-        base = base_part(n, shrunk, packed)
-        arrived, base = lax.optimization_barrier((arrived, base))
-        bases.append(base)
-        shrunk = shrunk + arrived
+    arrived = from_mirror(shrunk, 1)
+    far_whole = from_group(whole)
+    bases.append(base_part(1, shrunk))
+    arrived, half, bases[1] = lax.optimization_barrier((arrived, half, bases[1]))
+    shrunk = shrunk + arrived
+    arrived = from_mirror(shrunk, 2)
+    far_half = from_group(half)
+    bases.append(base_part(2, shrunk))
+    arrived, bases[2] = lax.optimization_barrier((arrived, bases[2]))
+    shrunk = shrunk + arrived
+    bases.append(base_part(3, shrunk))
 
     middle = block_count // 2 * block
     splits = [(0, middle), (middle, columns)]
@@ -375,7 +355,7 @@
         1,
         1,
         8,
-        in_specs=[vmem] * (len(bases) + 6),
+        in_specs=[vmem] * (len(bases) + 7),
         out_specs=[vmem] * (2 + 2 * len(splits)),
         out_shape=[
             jax.ShapeDtypeStruct((quarter, w), f32) for w in (columns, columns, *widths, *widths)
@@ -385,7 +365,7 @@
             pltpu.VMEM((row_count, rank_block * owner_count), bf16),
             pltpu.VMEM((rank_block, columns), bf16),
         ],
-    )(slot, *bases, own, shrunk, whole, half, swapped)
+    )(slot, *bases, own, shrunk, whole, half, far_whole, far_half)
     own_keep, own_send = out[:2]
     crossed = []
     for keep, send in zip(out[2:4], out[4:6]):

time: 43.8 us -> 44 us (level)
  starting transfers between devices: 16 us -> 19 us
  waiting for transfers between devices: 11.1 us -> 8.53 us
    ppermute x2, starting transfers between devices: 0.01 us -> 3.24 us  [from_mirror(): return lax.ppermute(x, 'adapter', [(s, s ^ m) for s in range(owner_count)])]
    ppermute x1, starting transfers between devices: 3.13 us -> 0.06 us  [from_either(): return lax.ppermute(x, ('groups', 'adapter'), pairs)]
    ppermute x4, starting transfers between devices: 6.06 us -> 9.13 us  [from_owner(): lax.ppermute(x, 'adapter', [(s, (s - j) % owner_count) for s in range(own...]
    ppermute x2, waiting for transfers between devices: 3.79 us -> 1.07 us  [from_mirror(): return lax.ppermute(x, 'adapter', [(s, s ^ m) for s in range(owner_count)])]
    ppermute x1, waiting for transfers between devices: 0.01 us -> 1.07 us  [from_either(): return lax.ppermute(x, ('groups', 'adapter'), pairs)]
    pallas_call x5 -> x4, Pallas kernels: 10.9 us -> 10 us  [base_part(): kernel_call(functools.partial(base_kernel, block, places, numbers), 'base...]
    ppermute x4, waiting for transfers between devices: 0.78 us -> 0.01 us  [from_owner(): lax.ppermute(x, 'adapter', [(s, (s - j) % owner_count) for s in range(own...]
    pallas_call x1, Pallas kernels: 3.99 us -> 4.56 us  [paired(): kernel_call(functools.partial(cut_kernel, block, range(loads[1]), len(sma...]
  transfers between devices with their start and end apart: 15 -> 16, of which waited for: 7 -> 5; matrix products, arithmetic and copies ran while one was open for 0% -> 0% of each run, Pallas kernels for 35% -> 34%
where the time goes in v12:
time: 44 us; the launch traced here: 43.9 us
  starting transfers between devices  19 us (43%)
  Pallas kernels  15.3 us (35%)
  waiting for transfers between devices  8.53 us (19%)
  other arithmetic  0.86 us (2%)
    pallas_call x4, Pallas kernels, base_part(): kernel_call(functools.partial(base_kernel, block, places, numbers), 'base...  10 us
    ppermute x4, starting transfers between devices, from_owner(): lax.ppermute(x, 'adapter', [(s, (s - j) % owner_count) for s in range(own...  9.13 us
    ppermute x7, waiting for transfers between devices, from_tensor(): return lax.ppermute(x, 'tensor', [(s, s ^ m) for s in range(4)])  6.38 us
    pallas_call x1, Pallas kernels, paired(): kernel_call(functools.partial(cut_kernel, block, range(loads[1]), len(sma...  4.56 us
    ppermute x7, starting transfers between devices, from_tensor(): return lax.ppermute(x, 'tensor', [(s, s ^ m) for s in range(4)])  4.44 us
    ppermute x2, starting transfers between devices, from_mirror(): return lax.ppermute(x, 'adapter', [(s, s ^ m) for s in range(owner_count)])  3.24 us
    ppermute x2, starting transfers between devices, from_group(): return lax.ppermute(x, 'groups', [(0, 1), (1, 0)])  2.09 us
    ppermute x2, waiting for transfers between devices, from_mirror(): return lax.ppermute(x, 'adapter', [(s, s ^ m) for s in range(owner_count)])  1.07 us
  transfers between devices with their start and end apart: 16, of which 5 were waited for; matrix products, arithmetic and copies ran while one was open for 0% of the time, Pallas kernels for 34%

profile of v12, /device:TPU:0, one launch (start us, length us, event | category | flops | bytes accessed | tf_op | source)
XLA Modules:
  0.0 43.9 jit_solution(7049625352677528033)
XLA Ops:
  0.0 4.0 %collective-permute-start = (bf16[16,2048]{1,0:T(8,128)(2,1)}, bf16[16,2048]{1,0:T(8,128)(2,1)S(1)}, u32[]{:S(2)}, u32[]{:S(2)}) collective-permute-start(bf16[16,2048]{1,0:T(8,128)(2,1)} %refs_2_.1), channel_id=1, source_target_pairs={{0,8},{4,12},{8,0},{12,4},{1,9},{5,13},{9,1},{13,5},{2,10},{6,14},... | collective-permute-start | bytes 196616 | tf_op jit(solution)/shard_map/ppermute | solution.py:227
  4.0 1.6 %collective-permute-start.2 = (bf16[16,2048]{1,0:T(8,128)(2,1)}, bf16[16,2048]{1,0:T(8,128)(2,1)S(1)}, u32[]{:S(2)}, u32[]{:S(2)}) collective-permute-start(bf16[16,2048]{1,0:T(8,128)(2,1)} %refs_2_.1), channel_id=1, source_target_pairs={{0,4},{4,8},{8,12},{12,0},{1,5},{5,9},{9,13},{13,1},{2,6},{6,10},{... | collective-permute-start | bytes 196616 | tf_op jit(solution)/shard_map/ppermute | solution.py:227
  5.6 2.2 %collective-permute-start.1 = (bf16[16,2048]{1,0:T(8,128)(2,1)}, bf16[16,2048]{1,0:T(8,128)(2,1)S(1)}, u32[]{:S(2)}, u32[]{:S(2)}) collective-permute-start(bf16[16,2048]{1,0:T(8,128)(2,1)} %refs_2_.1), channel_id=1, source_target_pairs={{0,12},{4,0},{8,4},{12,8},{1,13},{5,1},{9,5},{13,9},{2,14},{6,2},{... | collective-permute-start | bytes 196616 | tf_op jit(solution)/shard_map/ppermute | solution.py:227
  7.9 4.6 %cut_expand.1 = (bf16[16,7168]{1,0:T(8,128)(2,1)S(1)}, bf16[16,3584]{1,0:T(8,128)(2,1)S(1)}, bf16[16,7168]{1,0:T(8,128)(2,1)S(1)}, s32[1,4]{1,0:T(1,128)S(1)}, s...) custom-call(bf16[1,16,28672]{2,1,0:T(8,128)(2,1)} %expand.1, ...), custom_call_target="tpu_custom_call" | custom-call | flops 1 | bytes 1 | tf_op jit(solution)/shard_map/cut_expand/pallas_call | solution.py:265
  12.4 0.1 collective-permute-start.5
  12.5 0.0 collective-permute-done.refs_1_
  12.5 0.0 collective-permute-done.2.refs_3_
  12.5 0.0 collective-permute-done.1.refs_2_
  12.5 0.3 gather_rows.1
  12.8 0.1 collective-permute-start.3
  12.9 1.3 %collective-permute-start.7 = (bf16[16,3584]{1,0:T(8,128)(2,1)S(1)}, bf16[16,3584]{1,0:T(8,128)(2,1)S(1)}, u32[]{:S(2)}, u32[]{:S(2)}) collective-permute-start(bf16[16,3584]{1,0:T(8,128)(2,1)S(1)} %get-tuple-element.54), channel_id=1, source_target_pairs={{0,8},{4,12},{8,0},{12,4},{1,9},{5,13},{9,1},{13,5},{2,10},{6,14},... | collective-permute-start | bytes 344072 | tf_op jit(solution)/shard_map/ppermute | solution.py:227
  14.1 0.0 collective-permute-done.3
  14.2 1.6 %collective-permute-start.4 = (f32[16,64]{1,0:T(8,128)S(1)}, f32[16,64]{1,0:T(8,128)S(1)}, u32[]{:S(2)}, u32[]{:S(2)}) collective-permute-start(f32[16,64]{1,0:T(8,128)S(1)} %slice.16), channel_id=1, source_target_pairs={{0,2},{1,3},{2,0},{3,1},{4,6},{5,7},{6,4},{7,5},{8,10},{9,11},{10,... | collective-permute-start | bytes 12296 | tf_op jit(solution)/shard_map/ppermute | solution.py:239
  15.7 2.9 %base_part.4 = (f32[64,2048]{1,0:T(8,128)S(1)}, bf16[3,2048,512]{2,1,0:T(8,128)(2,1)S(1)}) custom-call(bf16[64,2048]{1,0:T(8,128)(2,1)S(1)} %get-tuple-element.49.rows, bf16[2048,7168]{1,0:T(8,128)(2,1)} %weight.9, bf16[5,2048,512]{2,1,0:T(8,128)(2,1)S(1)} %get-tuple-element.50.refs_0_, f32[32,64]{1,0:T(8,128)S(1)} %add.27.refs_1_), custom_call_target="tpu_custom_call" | custom-call | flops 2000000000 | bytes 1 | tf_op jit(solution)/shard_map/base_part/pallas_call | solution.py:313
  18.6 0.0 collective-permute-done.4
  18.7 1.1 %collective-permute-done.5.refs_6_ = bf16[16,7168]{1,0:T(8,128)(2,1)S(1)} collective-permute-done((bf16[16,7168]{1,0:T(8,128)(2,1)S(1)}, bf16[16,7168]{1,0:T(8,128)(2,1)S(1)}, u32[]{:S(2)}, u32[]{:S(2)}) %collective-permute-start.5) | collective-permute-done | bytes 229408 | tf_op jit(solution)/shard_map/ppermute | solution.py:236
  19.7 2.7 %collective-permute-start.6 = (bf16[16,64]{1,0:T(8,128)(2,1)S(1)}, bf16[16,64]{1,0:T(8,128)(2,1)S(1)}, u32[]{:S(2)}, u32[]{:S(2)}) collective-permute-start(bf16[16,64]{1,0:T(8,128)(2,1)S(1)} %fusion.3.refs_2_), channel_id=1, source_target_pairs={{0,4},{4,0},{8,12},{12,8},{1,5},{5,1},{9,13},{13,9},{2,6},{6,2},{1... | collective-permute-start | bytes 6152 | tf_op jit(solution)/shard_map/ppermute | solution.py:242
  22.5 1.2 %collective-permute-start.9 = (bf16[16,7168]{1,0:T(8,128)(2,1)S(1)}, bf16[16,7168]{1,0:T(8,128)(2,1)S(1)}, u32[]{:S(2)}, u32[]{:S(2)}) collective-permute-start(bf16[16,7168]{1,0:T(8,128)(2,1)S(1)} %collective-permute-done.5.refs_6_), channel_id=1, source_target_pairs={{0,16},{16,0},{1,17},{17,1},{2,18},{18,2},{3,19},{19,3},{4,20},{20... | collective-permute-start | bytes 688136 | tf_op jit(solution)/shard_map/ppermute | solution.py:245
  23.7 3.0 %base_part.5 = (f32[64,2048]{1,0:T(8,128)S(1)}, bf16[3,2048,512]{2,1,0:T(8,128)(2,1)S(1)}) custom-call(bf16[64,2048]{1,0:T(8,128)(2,1)S(1)} %get-tuple-element.49.rows, bf16[2048,7168]{1,0:T(8,128)(2,1)} %weight.9, bf16[5,2048,512]{2,1,0:T(8,128)(2,1)S(1)} %get-tuple-element.50.refs_0_, bf16[3,2048,512]{2,1,0:T(8,128)(2,1)S(1)} %get-tuple-element.55.refs_1_, ...), custom_call_target="tpu_custom_call" | custom-call | flops 10000000000 | bytes 1 | tf_op jit(solution)/shard_map/base_part/pallas_call | solution.py:313
  26.7 0.0 collective-permute-done.7.refs_7_
  26.7 0.0 collective-permute-done.6
  26.7 0.8 %collective-permute-start.10 = (bf16[16,3584]{1,0:T(8,128)(2,1)S(1)}, bf16[16,3584]{1,0:T(8,128)(2,1)S(1)}, u32[]{:S(2)}, u32[]{:S(2)}) collective-permute-start(bf16[16,3584]{1,0:T(8,128)(2,1)S(1)} %collective-permute-done.7.refs_7_), channel_id=1, source_target_pairs={{0,16},{16,0},{1,17},{17,1},{2,18},{18,2},{3,19},{19,3},{4,20},{20... | collective-permute-start | bytes 344072 | tf_op jit(solution)/shard_map/ppermute | solution.py:245
  27.6 0.5 %collective-permute-start.8 = (bf16[16,64]{1,0:T(8,128)(2,1)S(1)}, bf16[16,64]{1,0:T(8,128)(2,1)S(1)}, u32[]{:S(2)}, u32[]{:S(2)}) collective-permute-start(bf16[16,64]{1,0:T(8,128)(2,1)S(1)} %add.29.refs_1_), channel_id=1, source_target_pairs={{0,8},{4,12},{8,0},{12,4},{1,9},{5,13},{9,1},{13,5},{2,10},{6,14},... | collective-permute-start | bytes 6152 | tf_op jit(solution)/shard_map/ppermute | solution.py:242
  28.1 2.9 %base_part.6 = (f32[64,1536]{1,0:T(8,128)S(1)}, bf16[3,2048,512]{2,1,0:T(8,128)(2,1)S(1)}) custom-call(bf16[64,2048]{1,0:T(8,128)(2,1)S(1)} %get-tuple-element.49.rows, bf16[2048,7168]{1,0:T(8,128)(2,1)} %weight.9, bf16[3,2048,512]{2,1,0:T(8,128)(2,1)S(1)} %get-tuple-element.59.refs_0_, bf16[16,64]{1,0:T(8,128)(2,1)S(1)} %add.29.refs_1_), custom_call_target="tpu_custom_call" | custom-call | flops 1 | bytes 1 | tf_op jit(solution)/shard_map/base_part/pallas_call | solution.py:313
  31.0 1.1 %collective-permute-done.8 = bf16[16,64]{1,0:T(8,128)(2,1)S(1)} collective-permute-done((bf16[16,64]{1,0:T(8,128)(2,1)S(1)}, bf16[16,64]{1,0:T(8,128)(2,1)S(1)}, u32[]{:S(2)}, u32[]{:S(2)}) %collective-permute-start.8) | collective-permute-done | bytes 2080 | tf_op jit(solution)/shard_map/ppermute | solution.py:242
  32.1 1.2 %base_part.7.refs_3_ = f32[64,1536]{1,0:T(8,128)S(1)} custom-call(bf16[64,2048]{1,0:T(8,128)(2,1)S(1)} %get-tuple-element.49.rows, bf16[2048,7168]{1,0:T(8,128)(2,1)} %weight.9, bf16[3,2048,512]{2,1,0:T(8,128)(2,1)S(1)} %get-tuple-element.62.refs_0_, bf16[16,64]{1,0:T(8,128)(2,1)S(1)} %add.30.refs_1_.refs_5_), custom_call_target="tpu_custom_call" | custom-call | flops 1 | bytes 1 | tf_op jit(solution)/shard_map/base_part/pallas_call | solution.py:313
  33.3 0.0 collective-permute-done.10.refs_9_
  33.3 0.0 collective-permute-done.9.refs_8_
  33.3 0.5 %add_delta.1 = (f32[16,7168]{1,0:T(8,128)S(1)}, f32[16,7168]{1,0:T(8,128)S(1)}, f32[16,3584]{1,0:T(8,128)S(1)}, f32[16,3584]{1,0:T(8,128)S(1)}, f32[16,3584]{1,0:T(8,128)S(1)}, /*index=5*/f32[16,3584]{1,0:T(8,128)S(1)}) custom-call(s32[1,64]{1,0:T(1,128)S(1)} %get-tuple-element.43.slot, f32[64,2048]{1,0:T(8,128)S(1)} %get-tuple-element.52.refs_0_, ...), custom_call_target="tpu_custom_call" | custom-call | flops 1 | bytes 1 | tf_op jit(solution)/shard_map/add_delta/pallas_call | solution.py:352
  33.8 0.1 collective-permute-start.12
  33.9 0.5 %collective-permute-start.14 = (f32[16,3584]{1,0:T(8,128)S(1)}, f32[16,3584]{1,0:T(8,128)S(1)}, u32[]{:S(2)}, u32[]{:S(2)}) collective-permute-start(f32[16,3584]{1,0:T(8,128)S(1)} %get-tuple-element.72), channel_id=1, source_target_pairs={{0,1},{1,0},{2,3},{3,2},{4,5},{5,4},{6,7},{7,6},{8,9},{9,8},{10,11... | collective-permute-start | bytes 688136 | tf_op jit(solution)/shard_map/ppermute | solution.py:239
  34.4 0.1 collective-permute-start.11
  34.5 0.9 %collective-permute-done.12 = f32[16,3584]{1,0:T(8,128)S(1)} collective-permute-done((f32[16,3584]{1,0:T(8,128)S(1)}, f32[16,3584]{1,0:T(8,128)S(1)}, u32[]{:S(2)}, u32[]{:S(2)}) %collective-permute-start.12) | collective-permute-done | bytes 229408 | tf_op jit(solution)/shard_map/ppermute | solution.py:239
  35.4 1.6 %collective-permute-start.13 = (bf16[16,3584]{1,0:T(8,128)(2,1)S(1)}, bf16[16,3584]{1,0:T(8,128)(2,1)S(1)}, u32[]{:S(2)}, u32[]{:S(2)}) collective-permute-start(bf16[16,3584]{1,0:T(8,128)(2,1)S(1)} %add_convert_fusion.1), channel_id=1, source_target_pairs={{0,2},{1,3},{2,0},{3,1},{4,6},{5,7},{6,4},{7,5},{8,10},{9,11},{10,... | collective-permute-start | bytes 344072 | tf_op jit(solution)/shard_map/ppermute | solution.py:239
  36.9 0.0 collective-permute-done.14
  37.0 0.6 %collective-permute-start.15 = (bf16[16,3584]{1,0:T(8,128)(2,1)S(1)}, bf16[16,3584]{1,0:T(8,128)(2,1)S(1)}, u32[]{:S(2)}, u32[]{:S(2)}) collective-permute-start(bf16[16,3584]{1,0:T(8,128)(2,1)S(1)} %add_convert_fusion), channel_id=1, source_target_pairs={{0,2},{1,3},{2,0},{3,1},{4,6},{5,7},{6,4},{7,5},{8,10},{9,11},{10,... | collective-permute-start | bytes 344072 | tf_op jit(solution)/shard_map/ppermute | solution.py:239
  37.6 0.0 collective-permute-done.11
  37.6 3.8 %collective-permute-done.13 = bf16[16,3584]{1,0:T(8,128)(2,1)S(1)} collective-permute-done((bf16[16,3584]{1,0:T(8,128)(2,1)S(1)}, bf16[16,3584]{1,0:T(8,128)(2,1)S(1)}, u32[]{:S(2)}, u32[]{:S(2)}) %collective-permute-start.13) | collective-permute-done | bytes 114720 | tf_op jit(solution)/shard_map/ppermute | solution.py:239
  41.4 1.7 %collective-permute-done.15 = bf16[16,3584]{1,0:T(8,128)(2,1)S(1)} collective-permute-done((bf16[16,3584]{1,0:T(8,128)(2,1)S(1)}, bf16[16,3584]{1,0:T(8,128)(2,1)S(1)}, u32[]{:S(2)}, u32[]{:S(2)}) %collective-permute-start.15) | collective-permute-done | bytes 114720 | tf_op jit(solution)/shard_map/ppermute | solution.py:239
  43.1 0.7 %pad_maximum_fusion = bf16[16,7168]{1,0:T(8,128)(2,1)} fusion(bf16[16,3584]{1,0:T(8,128)(2,1)S(1)} %get-tuple-element.74, bf16[16,3584]{1,0:T(8,128)(2,1)S(1)} %get-tuple-element.73), kind=kLoop, calls=%fused_computation.4 | loop fusion | flops 458752 | bytes 458752 | tf_op jit(solution)/shard_map/concatenate | solution.py:374
  (9 shorter events, 0.2 us)
Async XLA Ops:
  0.0 12.5 %collective-permute-start = (bf16[16,2048]{1,0:T(8,128)(2,1)}, bf16[16,2048]{1,0:T(8,128)(2,1)S(1)}, u32[]{:S(2)}, u32[]{:S(2)}) collective-permute-start(bf16[16,2048]{1,0:T(8,128)(2,1)} %refs_2_.1), channel_id=1, source_target_pairs={{0,8},{4,12},{8,0},{12,4},{1,9},{5,13},{9,1},{13,5},{2,10},{6,14},... | collective-permute-start | bytes 196616 | tf_op jit(solution)/shard_map/ppermute | solution.py:227
  4.0 8.5 %collective-permute-start.2 = (bf16[16,2048]{1,0:T(8,128)(2,1)}, bf16[16,2048]{1,0:T(8,128)(2,1)S(1)}, u32[]{:S(2)}, u32[]{:S(2)}) collective-permute-start(bf16[16,2048]{1,0:T(8,128)(2,1)} %refs_2_.1), channel_id=1, source_target_pairs={{0,4},{4,8},{8,12},{12,0},{1,5},{5,9},{9,13},{13,1},{2,6},{6,10},{... | collective-permute-start | bytes 196616 | tf_op jit(solution)/shard_map/ppermute | solution.py:227
  5.6 6.9 %collective-permute-start.1 = (bf16[16,2048]{1,0:T(8,128)(2,1)}, bf16[16,2048]{1,0:T(8,128)(2,1)S(1)}, u32[]{:S(2)}, u32[]{:S(2)}) collective-permute-start(bf16[16,2048]{1,0:T(8,128)(2,1)} %refs_2_.1), channel_id=1, source_target_pairs={{0,12},{4,0},{8,4},{12,8},{1,13},{5,1},{9,5},{13,9},{2,14},{6,2},{... | collective-permute-start | bytes 196616 | tf_op jit(solution)/shard_map/ppermute | solution.py:227
  12.4 7.3 %collective-permute-start.5 = (bf16[16,7168]{1,0:T(8,128)(2,1)S(1)}, bf16[16,7168]{1,0:T(8,128)(2,1)S(1)}, u32[]{:S(2)}, u32[]{:S(2)}) collective-permute-start(bf16[16,7168]{1,0:T(8,128)(2,1)S(1)} %get-tuple-element.48), channel_id=1, source_target_pairs={{0,12},{4,0},{8,4},{12,8},{16,20},{20,24},{24,28},{28,16},{1,13},{... | collective-permute-start | bytes 688136 | tf_op jit(solution)/shard_map/ppermute | solution.py:236
  12.8 1.3 %collective-permute-start.3 = (f32[32,64]{1,0:T(8,128)S(1)}, f32[32,64]{1,0:T(8,128)S(1)}, u32[]{:S(2)}, u32[]{:S(2)}) collective-permute-start(f32[32,64]{1,0:T(8,128)S(1)} %get-tuple-element.47), channel_id=1, source_target_pairs={{0,1},{1,0},{2,3},{3,2},{4,5},{5,4},{6,7},{7,6},{8,9},{9,8},{10,11... | collective-permute-start | bytes 24584 | tf_op jit(solution)/shard_map/ppermute | solution.py:239
  12.9 13.8 %collective-permute-start.7 = (bf16[16,3584]{1,0:T(8,128)(2,1)S(1)}, bf16[16,3584]{1,0:T(8,128)(2,1)S(1)}, u32[]{:S(2)}, u32[]{:S(2)}) collective-permute-start(bf16[16,3584]{1,0:T(8,128)(2,1)S(1)} %get-tuple-element.54), channel_id=1, source_target_pairs={{0,8},{4,12},{8,0},{12,4},{1,9},{5,13},{9,1},{13,5},{2,10},{6,14},... | collective-permute-start | bytes 344072 | tf_op jit(solution)/shard_map/ppermute | solution.py:227
  14.2 4.5 %collective-permute-start.4 = (f32[16,64]{1,0:T(8,128)S(1)}, f32[16,64]{1,0:T(8,128)S(1)}, u32[]{:S(2)}, u32[]{:S(2)}) collective-permute-start(f32[16,64]{1,0:T(8,128)S(1)} %slice.16), channel_id=1, source_target_pairs={{0,2},{1,3},{2,0},{3,1},{4,6},{5,7},{6,4},{7,5},{8,10},{9,11},{10,... | collective-permute-start | bytes 12296 | tf_op jit(solution)/shard_map/ppermute | solution.py:239
  19.7 7.0 %collective-permute-start.6 = (bf16[16,64]{1,0:T(8,128)(2,1)S(1)}, bf16[16,64]{1,0:T(8,128)(2,1)S(1)}, u32[]{:S(2)}, u32[]{:S(2)}) collective-permute-start(bf16[16,64]{1,0:T(8,128)(2,1)S(1)} %fusion.3.refs_2_), channel_id=1, source_target_pairs={{0,4},{4,0},{8,12},{12,8},{1,5},{5,1},{9,13},{13,9},{2,6},{6,2},{1... | collective-permute-start | bytes 6152 | tf_op jit(solution)/shard_map/ppermute | solution.py:242
  22.5 10.8 %collective-permute-start.9 = (bf16[16,7168]{1,0:T(8,128)(2,1)S(1)}, bf16[16,7168]{1,0:T(8,128)(2,1)S(1)}, u32[]{:S(2)}, u32[]{:S(2)}) collective-permute-start(bf16[16,7168]{1,0:T(8,128)(2,1)S(1)} %collective-permute-done.5.refs_6_), channel_id=1, source_target_pairs={{0,16},{16,0},{1,17},{17,1},{2,18},{18,2},{3,19},{19,3},{4,20},{20... | collective-permute-start | bytes 688136 | tf_op jit(solution)/shard_map/ppermute | solution.py:245
  26.7 6.6 %collective-permute-start.10 = (bf16[16,3584]{1,0:T(8,128)(2,1)S(1)}, bf16[16,3584]{1,0:T(8,128)(2,1)S(1)}, u32[]{:S(2)}, u32[]{:S(2)}) collective-permute-start(bf16[16,3584]{1,0:T(8,128)(2,1)S(1)} %collective-permute-done.7.refs_7_), channel_id=1, source_target_pairs={{0,16},{16,0},{1,17},{17,1},{2,18},{18,2},{3,19},{19,3},{4,20},{20... | collective-permute-start | bytes 344072 | tf_op jit(solution)/shard_map/ppermute | solution.py:245
  27.6 4.5 %collective-permute-start.8 = (bf16[16,64]{1,0:T(8,128)(2,1)S(1)}, bf16[16,64]{1,0:T(8,128)(2,1)S(1)}, u32[]{:S(2)}, u32[]{:S(2)}) collective-permute-start(bf16[16,64]{1,0:T(8,128)(2,1)S(1)} %add.29.refs_1_), channel_id=1, source_target_pairs={{0,8},{4,12},{8,0},{12,4},{1,9},{5,13},{9,1},{13,5},{2,10},{6,14},... | collective-permute-start | bytes 6152 | tf_op jit(solution)/shard_map/ppermute | solution.py:242
  33.8 1.6 %collective-permute-start.12 = (f32[16,3584]{1,0:T(8,128)S(1)}, f32[16,3584]{1,0:T(8,128)S(1)}, u32[]{:S(2)}, u32[]{:S(2)}) collective-permute-start(f32[16,3584]{1,0:T(8,128)S(1)} %get-tuple-element.70), channel_id=1, source_target_pairs={{0,1},{1,0},{2,3},{3,2},{4,5},{5,4},{6,7},{7,6},{8,9},{9,8},{10,11... | collective-permute-start | bytes 688136 | tf_op jit(solution)/shard_map/ppermute | solution.py:239
  33.9 3.1 %collective-permute-start.14 = (f32[16,3584]{1,0:T(8,128)S(1)}, f32[16,3584]{1,0:T(8,128)S(1)}, u32[]{:S(2)}, u32[]{:S(2)}) collective-permute-start(f32[16,3584]{1,0:T(8,128)S(1)} %get-tuple-element.72), channel_id=1, source_target_pairs={{0,1},{1,0},{2,3},{3,2},{4,5},{5,4},{6,7},{7,6},{8,9},{9,8},{10,11... | collective-permute-start | bytes 688136 | tf_op jit(solution)/shard_map/ppermute | solution.py:239
  34.4 3.2 %collective-permute-start.11 = (f32[16,7168]{1,0:T(8,128)S(1)}, f32[16,7168]{1,0:T(8,128)S(1)}, u32[]{:S(2)}, u32[]{:S(2)}) collective-permute-start(f32[16,7168]{1,0:T(8,128)S(1)} %get-tuple-element.68), channel_id=1, source_target_pairs={{0,1},{1,0},{2,3},{3,2},{4,5},{5,4},{6,7},{7,6},{8,9},{9,8},{10,11... | collective-permute-start | bytes 1376264 | tf_op jit(solution)/shard_map/ppermute | solution.py:239
  35.4 6.1 %collective-permute-start.13 = (bf16[16,3584]{1,0:T(8,128)(2,1)S(1)}, bf16[16,3584]{1,0:T(8,128)(2,1)S(1)}, u32[]{:S(2)}, u32[]{:S(2)}) collective-permute-start(bf16[16,3584]{1,0:T(8,128)(2,1)S(1)} %add_convert_fusion.1), channel_id=1, source_target_pairs={{0,2},{1,3},{2,0},{3,1},{4,6},{5,7},{6,4},{7,5},{8,10},{9,11},{10,... | collective-permute-start | bytes 344072 | tf_op jit(solution)/shard_map/ppermute | solution.py:239
  37.0 6.1 %collective-permute-start.15 = (bf16[16,3584]{1,0:T(8,128)(2,1)S(1)}, bf16[16,3584]{1,0:T(8,128)(2,1)S(1)}, u32[]{:S(2)}, u32[]{:S(2)}) collective-permute-start(bf16[16,3584]{1,0:T(8,128)(2,1)S(1)} %add_convert_fusion), channel_id=1, source_target_pairs={{0,2},{1,3},{2,0},{3,1},{4,6},{5,7},{6,4},{7,5},{8,10},{9,11},{10,... | collective-permute-start | bytes 344072 | tf_op jit(solution)/shard_map/ppermute | solution.py:239

commit v13 on v10

--- a/solution.py
+++ b/solution.py
@@ -66,8 +66,8 @@
     g, a = lax.axis_index("groups"), lax.axis_index("adapter")
     columns, half_width = whole.shape[1], half.shape[1]
     firsts = (
-        lax.rem(a + 3 - 2 * g, 4) * columns,
-        lax.rem(a + 2, 4) * columns + g * half_width,
+        lax.bitwise_xor(a, 2 + g) * columns,
+        lax.bitwise_xor(a, 1) * columns + g * half_width,
         a * columns,
     )
     copies = []
@@ -104,7 +104,7 @@
     a, t = lax.axis_index("adapter"), lax.axis_index("tensor")
     height, depth = blocks[0].shape
     for j, part in zip(offsets, blocks):
-        where = lax.rem(a + j, owner_count)
+        where = lax.bitwise_xor(a, j)
         rows[pl.ds(pl.multiple_of(where * height, height), height), :] = part[:, :depth]
     quarter = rows.shape[0] // 4
     for i, flip in enumerate((0, 2, 1, 3)):
@@ -151,36 +151,30 @@
             )
 
 
-def pack_kernel(whole, half, packed):
-    columns = whole.shape[1]
-    packed[:, :columns] = whole[...]
-    packed[:, columns:] = half[...]
-
-
 def delta_kernel(block, splits, slot, *refs):
-    bases, refs = refs[: -len(splits) * 2 - 10], refs[-len(splits) * 2 - 10 :]
-    own, shrunk, whole, half, packed, own_keep, own_send = refs[:7]
-    cross_keep, cross_send = refs[7 : 7 + len(splits)], refs[7 + len(splits) : 7 + 2 * len(splits)]
+    bases, refs = refs[: -len(splits) * 2 - 11], refs[-len(splits) * 2 - 11 :]
+    own, shrunk, whole, half, far_whole, far_half, own_keep, own_send = refs[:8]
+    cross_keep, cross_send = refs[8 : 8 + len(splits)], refs[8 + len(splits) : 8 + 2 * len(splits)]
     flat, ordered, two = refs[-3:]
     g, a, t = (lax.axis_index(name) for name in ("groups", "adapter", "tensor"))
     row_count = bases[0].shape[0]
     quarter = row_count // 4
-    columns, half_width = whole.shape[1], half.shape[1]
+    half_width = half.shape[1]
 
     @pl.when(g == 0)
     def _():
         two[:, :half_width] = half[...]
-        two[:, half_width:] = packed[:, columns:]
+        two[:, half_width:] = far_half[...]
 
     @pl.when(g != 0)
     def _():
-        two[:, :half_width] = packed[:, columns:]
+        two[:, :half_width] = far_half[...]
         two[:, half_width:] = half[...]
 
     merged = shrunk[...].astype(f32)
     spread = [
-        jnp.where(slot[...] == lax.rem(a + j, 4), merged, 0.0)
-        for j in (0, 1 + 2 * g, 3 - 2 * g, 2)
+        jnp.where(slot[...] == lax.bitwise_xor(a, j), merged, 0.0)
+        for j in (0, 2 + g, 3 - g, 1)
     ]
     flat[...] = jnp.concatenate(spread, axis=0).T
     for i, turn in enumerate((0, 2, 1, 3)):
@@ -192,7 +186,7 @@
         for column in range(0, base.shape[1], block):
             span = slice(at, at + block)
             expand = jnp.concatenate(
-                [own[:, span], whole[:, span], packed[:, span], two[:, span]], axis=0
+                [own[:, span], whole[:, span], far_whole[:, span], two[:, span]], axis=0
             )
             total = base[:, column : column + block] + jnp.dot(
                 left, expand, preferred_element_type=f32
@@ -232,31 +226,23 @@
     block = column_block(columns)
     block_count = columns // block
 
-    def from_owner(x, j):
-        return lax.ppermute(x, "adapter", [(s, (s - j) % owner_count) for s in range(owner_count)])
-
-    def from_either(x):
+    def from_owner(x, first, second):
         pairs = []
-        for group, j in ((0, 1), (1, 3)):
+        for group, m in ((0, first), (1, second)):
             for s in range(owner_count):
-                pairs.append(
-                    (group * owner_count + s, group * owner_count + (s - j) % owner_count)
-                )
+                pairs.append((group * owner_count + s, group * owner_count + (s ^ m)))
         return lax.ppermute(x, ("groups", "adapter"), pairs)
 
     def from_tensor(x, m):
         return lax.ppermute(x, "tensor", [(s, s ^ m) for s in range(4)])
 
-    def from_mirror(x, m):
-        return lax.ppermute(x, "adapter", [(s, s ^ m) for s in range(owner_count)])
-
     def from_group(x):
         return lax.ppermute(x, "groups", [(0, 1), (1, 0)])
 
     weight = pltpu.with_memory_space_constraint(base_up_weight, pltpu.HBM)
     expand = pltpu.with_memory_space_constraint(adapter_expand_weight, pltpu.HBM)
-    offsets = (2, 1, 3)
-    blocks = [from_owner(tokens, j) for j in offsets]
+    offsets = (2, 3, 1)
+    blocks = [from_owner(tokens, j, j) for j in offsets]
 
     cuts = [block_count * k // 14 for k in (0, 4, 8, 11, 14)]
     parts = list(zip(cuts[:-1], cuts[1:]))
@@ -288,7 +274,7 @@
         ],
     )(expand, weight, *small)
     loaded = [held]
-    whole, half = from_either(whole), from_owner(half, 2)
+    whole, half = from_owner(whole, 2, 3), from_owner(half, 1, 1)
 
     rows, keep, send, slot = kernel_call(
         functools.partial(gather_kernel, (0, *offsets)),
@@ -346,21 +332,11 @@
     base_1 = base_part(1, pair)
     arrived, base_1, whole, half = lax.optimization_barrier((arrived, base_1, whole, half))
     shrunk = (adapter_scale * (pair[:rank_block] + arrived)).astype(bf16)
-    packed = kernel_call(
-        pack_kernel,
-        "pack_pieces",
-        1,
-        1,
-        2,
-        in_specs=[vmem] * 2,
-        out_specs=vmem,
-        out_shape=jax.ShapeDtypeStruct((rank_block, columns + half_width), bf16),
-    )(whole, half)
-    swapped = from_group(packed)
+    far_whole, far_half = from_group(whole), from_group(half)
     bases = [base_0, base_1]
     for m, n in ((1, 2), (2, 3)):
-        arrived = from_mirror(shrunk, m)
-        base = base_part(n, shrunk, packed)
+        arrived = from_owner(shrunk, m, m)
+        base = base_part(n, shrunk, whole, half)
         arrived, base = lax.optimization_barrier((arrived, base))
         bases.append(base)
         shrunk = shrunk + arrived
@@ -375,7 +351,7 @@
         1,
         1,
         8,
-        in_specs=[vmem] * (len(bases) + 6),
+        in_specs=[vmem] * (len(bases) + 7),
         out_specs=[vmem] * (2 + 2 * len(splits)),
         out_shape=[
             jax.ShapeDtypeStruct((quarter, w), f32) for w in (columns, columns, *widths, *widths)
@@ -385,7 +361,7 @@
             pltpu.VMEM((row_count, rank_block * owner_count), bf16),
             pltpu.VMEM((rank_block, columns), bf16),
         ],
-    )(slot, *bases, own, shrunk, whole, half, swapped)
+    )(slot, *bases, own, shrunk, whole, half, far_whole, far_half)
     own_keep, own_send = out[:2]
     crossed = []
     for keep, send in zip(out[2:4], out[4:6]):

time: 43.8 us -> 43.1 us (0.984)
  waiting for transfers between devices: 11.1 us -> 8.61 us
  starting transfers between devices: 16 us -> 17.8 us
    ppermute x7, waiting for transfers between devices: 4.58 us -> 2.23 us  [from_owner(): return lax.ppermute(x, ('groups', 'adapter'), pairs)]
    ppermute x7, starting transfers between devices: 9.2 us -> 11.3 us  [from_owner(): return lax.ppermute(x, ('groups', 'adapter'), pairs)]
    ppermute x1 -> x2, starting transfers between devices: 2.35 us -> 2.03 us  [from_group(): return lax.ppermute(x, 'groups', [(0, 1), (1, 0)])]
  transfers between devices with their start and end apart: 15 -> 16, of which waited for: 7 -> 6; matrix products, arithmetic and copies ran while one was open for 0% -> 0% of each run, Pallas kernels for 35% -> 35%
where the time goes in v13:
time: 43.1 us; the launch traced here: 43 us
  starting transfers between devices  17.8 us (41%)
  Pallas kernels  15.5 us (36%)
  waiting for transfers between devices  8.61 us (20%)
  other arithmetic  0.88 us (2%)
    ppermute x7, starting transfers between devices, from_owner(): return lax.ppermute(x, ('groups', 'adapter'), pairs)  11.3 us
    pallas_call x4, Pallas kernels, base_part(): kernel_call(functools.partial(base_kernel, block, places, numbers, stream...  10.8 us
    ppermute x7, waiting for transfers between devices, from_tensor(): return lax.ppermute(x, 'tensor', [(s, s ^ m) for s in range(4)])  6.37 us
    ppermute x7, starting transfers between devices, from_tensor(): return lax.ppermute(x, 'tensor', [(s, s ^ m) for s in range(4)])  4.44 us
    pallas_call x1, Pallas kernels, paired(): kernel_call(functools.partial(cut_kernel, block, range(loads[1]), len(sma...  3.92 us
    ppermute x7, waiting for transfers between devices, from_owner(): return lax.ppermute(x, ('groups', 'adapter'), pairs)  2.23 us
    ppermute x2, starting transfers between devices, from_group(): return lax.ppermute(x, 'groups', [(0, 1), (1, 0)])  2.03 us
  transfers between devices with their start and end apart: 16, of which 6 were waited for; matrix products, arithmetic and copies ran while one was open for 0% of the time, Pallas kernels for 35%

profile of v13, /device:TPU:0, one launch (start us, length us, event | category | flops | bytes accessed | tf_op | source)
XLA Modules:
  0.0 43.0 jit_solution(16151982997138202141)
XLA Ops:
  0.0 4.0 %collective-permute-start = (bf16[16,2048]{1,0:T(8,128)(2,1)}, bf16[16,2048]{1,0:T(8,128)(2,1)S(1)}, u32[]{:S(2)}, u32[]{:S(2)}) collective-permute-start(bf16[16,2048]{1,0:T(8,128)(2,1)} %refs_2_.1), channel_id=1, source_target_pairs={{0,8},{4,12},{8,0},{12,4},{16,24},{20,28},{24,16},{28,20},{1,9},{5... | collective-permute-start | bytes 196616 | tf_op jit(solution)/shard_map/ppermute | solution.py:234
  4.0 1.3 %collective-permute-start.1 = (bf16[16,2048]{1,0:T(8,128)(2,1)}, bf16[16,2048]{1,0:T(8,128)(2,1)S(1)}, u32[]{:S(2)}, u32[]{:S(2)}) collective-permute-start(bf16[16,2048]{1,0:T(8,128)(2,1)} %refs_2_.1), channel_id=1, source_target_pairs={{0,12},{4,8},{8,4},{12,0},{16,28},{20,24},{24,20},{28,16},{1,13},{... | collective-permute-start | bytes 196616 | tf_op jit(solution)/shard_map/ppermute | solution.py:234
  5.4 0.2 collective-permute-start.2
  5.6 3.9 %cut_expand.1 = (bf16[16,7168]{1,0:T(8,128)(2,1)S(1)}, bf16[16,3584]{1,0:T(8,128)(2,1)S(1)}, bf16[16,7168]{1,0:T(8,128)(2,1)S(1)}, s32[1,4]{1,0:T(1,128)S(1)}, s...) custom-call(bf16[1,16,28672]{2,1,0:T(8,128)(2,1)} %expand.1, ...), custom_call_target="tpu_custom_call" | custom-call | flops 1 | bytes 1 | tf_op jit(solution)/shard_map/cut_expand/pallas_call | solution.py:260
  9.5 2.9 %collective-permute-start.5 = (bf16[16,7168]{1,0:T(8,128)(2,1)S(1)}, bf16[16,7168]{1,0:T(8,128)(2,1)S(1)}, u32[]{:S(2)}, u32[]{:S(2)}) collective-permute-start(bf16[16,7168]{1,0:T(8,128)(2,1)S(1)} %get-tuple-element.53), channel_id=1, source_target_pairs={{0,8},{4,12},{8,0},{12,4},{16,28},{20,24},{24,20},{28,16},{1,9},{5... | collective-permute-start | bytes 688136 | tf_op jit(solution)/shard_map/ppermute | solution.py:234
  12.5 0.7 %collective-permute-start.6 = (bf16[16,3584]{1,0:T(8,128)(2,1)S(1)}, bf16[16,3584]{1,0:T(8,128)(2,1)S(1)}, u32[]{:S(2)}, u32[]{:S(2)}) collective-permute-start(bf16[16,3584]{1,0:T(8,128)(2,1)S(1)} %get-tuple-element.54), channel_id=1, source_target_pairs={{0,4},{4,0},{8,12},{12,8},{16,20},{20,16},{24,28},{28,24},{1,5},{5... | collective-permute-start | bytes 344072 | tf_op jit(solution)/shard_map/ppermute | solution.py:234
  13.1 0.0 collective-permute-done.refs_1_
  13.1 0.0 collective-permute-done.1.refs_2_
  13.1 0.0 collective-permute-done.2.refs_3_
  13.1 0.3 gather_rows.1
  13.4 0.1 collective-permute-start.3
  13.5 3.6 %base_part.4 = (f32[64,2048]{1,0:T(8,128)S(1)}, bf16[4,2048,512]{2,1,0:T(8,128)(2,1)S(1)}) custom-call(bf16[64,2048]{1,0:T(8,128)(2,1)S(1)} %get-tuple-element.45.rows, bf16[2048,7168]{1,0:T(8,128)(2,1)} %weight.9, bf16[4,2048,512]{2,1,0:T(8,128)(2,1)S(1)} %get-tuple-element.46.refs_0_, f32[32,64]{1,0:T(8,128)S(1)} %get-tuple-element.44.refs_1_), custom_call_target="tpu_custom_call" | custom-call | flops 1610612736 | bytes 25165824 | tf_op jit(solution)/shard_map/base_part/pallas_call | solution.py:311
  17.0 0.0 collective-permute-done.3
  17.1 1.6 %collective-permute-start.4 = (f32[16,64]{1,0:T(8,128)S(1)}, f32[16,64]{1,0:T(8,128)S(1)}, u32[]{:S(2)}, u32[]{:S(2)}) collective-permute-start(f32[16,64]{1,0:T(8,128)S(1)} %slice.16), channel_id=1, source_target_pairs={{0,2},{1,3},{2,0},{3,1},{4,6},{5,7},{6,4},{7,5},{8,10},{9,11},{10,... | collective-permute-start | bytes 12296 | tf_op jit(solution)/shard_map/ppermute | solution.py:237
  18.6 3.0 %base_part.5 = (f32[64,2048]{1,0:T(8,128)S(1)}, bf16[3,2048,512]{2,1,0:T(8,128)(2,1)S(1)}) custom-call(bf16[64,2048]{1,0:T(8,128)(2,1)S(1)} %get-tuple-element.45.rows, bf16[2048,7168]{1,0:T(8,128)(2,1)} %weight.9, bf16[4,2048,512]{2,1,0:T(8,128)(2,1)S(1)} %get-tuple-element.51.refs_0_, f32[32,64]{1,0:T(8,128)S(1)} %add.27.refs_1_), custom_call_target="tpu_custom_call" | custom-call | flops 1610612736 | bytes 25165824 | tf_op jit(solution)/shard_map/base_part/pallas_call | solution.py:311
  21.6 0.0 collective-permute-done.4
  21.6 0.0 collective-permute-done.6.refs_3_.refs_7_
  21.6 0.6 %collective-permute-done.5.refs_2_.refs_6_ = bf16[16,7168]{1,0:T(8,128)(2,1)S(1)} collective-permute-done((bf16[16,7168]{1,0:T(8,128)(2,1)S(1)}, bf16[16,7168]{1,0:T(8,128)(2,1)S(1)}, u32[]{:S(2)}, u32[]{:S(2)}) %collective-permute-start.5) | collective-permute-done | bytes 229408 | tf_op jit(solution)/shard_map/ppermute | solution.py:234
  22.2 0.9 %collective-permute-start.9 = (bf16[16,7168]{1,0:T(8,128)(2,1)S(1)}, bf16[16,7168]{1,0:T(8,128)(2,1)S(1)}, u32[]{:S(2)}, u32[]{:S(2)}) collective-permute-start(bf16[16,7168]{1,0:T(8,128)(2,1)S(1)} %collective-permute-done.5.refs_2_.refs_6_), channel_id=1, source_target_pairs={{0,16},{16,0},{1,17},{17,1},{2,18},{18,2},{3,19},{19,3},{4,20},{20... | collective-permute-start | bytes 688136 | tf_op jit(solution)/shard_map/ppermute | solution.py:240
  23.1 1.1 %collective-permute-start.10 = (bf16[16,3584]{1,0:T(8,128)(2,1)S(1)}, bf16[16,3584]{1,0:T(8,128)(2,1)S(1)}, u32[]{:S(2)}, u32[]{:S(2)}) collective-permute-start(bf16[16,3584]{1,0:T(8,128)(2,1)S(1)} %collective-permute-done.6.refs_3_.refs_7_), channel_id=1, source_target_pairs={{0,16},{16,0},{1,17},{17,1},{2,18},{18,2},{3,19},{19,3},{4,20},{20... | collective-permute-start | bytes 344072 | tf_op jit(solution)/shard_map/ppermute | solution.py:240
  24.2 0.9 %collective-permute-start.7 = (bf16[16,64]{1,0:T(8,128)(2,1)S(1)}, bf16[16,64]{1,0:T(8,128)(2,1)S(1)}, u32[]{:S(2)}, u32[]{:S(2)}) collective-permute-start(bf16[16,64]{1,0:T(8,128)(2,1)S(1)} %fusion.3.refs_1_), channel_id=1, source_target_pairs={{0,4},{4,0},{8,12},{12,8},{16,20},{20,16},{24,28},{28,24},{1,5},{5... | collective-permute-start | bytes 6152 | tf_op jit(solution)/shard_map/ppermute | solution.py:234
  25.1 1.6 %base_part.6 = (f32[64,1536]{1,0:T(8,128)S(1)}, bf16[1,2048,512]{2,1,0:T(8,128)(2,1)S(1)}) custom-call(bf16[64,2048]{1,0:T(8,128)(2,1)S(1)} %get-tuple-element.45.rows, bf16[2048,7168]{1,0:T(8,128)(2,1)} %weight.9, bf16[3,2048,512]{2,1,0:T(8,128)(2,1)S(1)} %get-tuple-element.57.refs_0_, bf16[16,64]{1,0:T(8,128)(2,1)S(1)} %fusion.3.refs_1_, ...), custom_call_target="tpu_custom_call" | custom-call | flops 1 | bytes 1 | tf_op jit(solution)/shard_map/base_part/pallas_call | solution.py:311
  26.7 1.2 %collective-permute-done.7 = bf16[16,64]{1,0:T(8,128)(2,1)S(1)} collective-permute-done((bf16[16,64]{1,0:T(8,128)(2,1)S(1)}, bf16[16,64]{1,0:T(8,128)(2,1)S(1)}, u32[]{:S(2)}, u32[]{:S(2)}) %collective-permute-start.7) | collective-permute-done | bytes 2080 | tf_op jit(solution)/shard_map/ppermute | solution.py:234
  27.9 1.3 %collective-permute-start.8 = (bf16[16,64]{1,0:T(8,128)(2,1)S(1)}, bf16[16,64]{1,0:T(8,128)(2,1)S(1)}, u32[]{:S(2)}, u32[]{:S(2)}) collective-permute-start(bf16[16,64]{1,0:T(8,128)(2,1)S(1)} %add.29.refs_1_), channel_id=1, source_target_pairs={{0,8},{4,12},{8,0},{12,4},{16,24},{20,28},{24,16},{28,20},{1,9},{5... | collective-permute-start | bytes 6152 | tf_op jit(solution)/shard_map/ppermute | solution.py:234
  29.1 2.7 %base_part.7.refs_3_ = f32[64,1536]{1,0:T(8,128)S(1)} custom-call(bf16[64,2048]{1,0:T(8,128)(2,1)S(1)} %get-tuple-element.45.rows, bf16[2048,7168]{1,0:T(8,128)(2,1)} %weight.9, bf16[1,2048,512]{2,1,0:T(8,128)(2,1)S(1)} %get-tuple-element.63.refs_0_, bf16[16,64]{1,0:T(8,128)(2,1)S(1)} %add.29.refs_1_, ...), custom_call_target="tpu_custom_call" | custom-call | flops 1 | bytes 1 | tf_op jit(solution)/shard_map/base_part/pallas_call | solution.py:311
  31.9 0.5 %collective-permute-done.8 = bf16[16,64]{1,0:T(8,128)(2,1)S(1)} collective-permute-done((bf16[16,64]{1,0:T(8,128)(2,1)S(1)}, bf16[16,64]{1,0:T(8,128)(2,1)S(1)}, u32[]{:S(2)}, u32[]{:S(2)}) %collective-permute-start.8) | collective-permute-done | bytes 2080 | tf_op jit(solution)/shard_map/ppermute | solution.py:234
  32.4 0.0 collective-permute-done.10.refs_9_
  32.4 0.0 collective-permute-done.9.refs_8_
  32.4 0.5 %add_delta.1 = (f32[16,7168]{1,0:T(8,128)S(1)}, f32[16,7168]{1,0:T(8,128)S(1)}, f32[16,3584]{1,0:T(8,128)S(1)}, f32[16,3584]{1,0:T(8,128)S(1)}, f32[16,3584]{1,0:T(8,128)S(1)}, /*index=5*/f32[16,3584]{1,0:T(8,128)S(1)}) custom-call(s32[1,64]{1,0:T(1,128)S(1)} %get-tuple-element.43.slot, f32[64,2048]{1,0:T(8,128)S(1)} %get-tuple-element.48.refs_0_, ...), custom_call_target="tpu_custom_call" | custom-call | flops 1 | bytes 1 | tf_op jit(solution)/shard_map/add_delta/pallas_call | solution.py:348
  32.9 0.1 collective-permute-start.14
  33.0 0.5 %collective-permute-start.12 = (f32[16,3584]{1,0:T(8,128)S(1)}, f32[16,3584]{1,0:T(8,128)S(1)}, u32[]{:S(2)}, u32[]{:S(2)}) collective-permute-start(f32[16,3584]{1,0:T(8,128)S(1)} %get-tuple-element.70), channel_id=1, source_target_pairs={{0,1},{1,0},{2,3},{3,2},{4,5},{5,4},{6,7},{7,6},{8,9},{9,8},{10,11... | collective-permute-start | bytes 688136 | tf_op jit(solution)/shard_map/ppermute | solution.py:237
  33.5 0.1 collective-permute-start.11
  33.6 0.9 %collective-permute-done.14 = f32[16,3584]{1,0:T(8,128)S(1)} collective-permute-done((f32[16,3584]{1,0:T(8,128)S(1)}, f32[16,3584]{1,0:T(8,128)S(1)}, u32[]{:S(2)}, u32[]{:S(2)}) %collective-permute-start.14) | collective-permute-done | bytes 229408 | tf_op jit(solution)/shard_map/ppermute | solution.py:237
  34.5 1.5 %collective-permute-start.15 = (bf16[16,3584]{1,0:T(8,128)(2,1)S(1)}, bf16[16,3584]{1,0:T(8,128)(2,1)S(1)}, u32[]{:S(2)}, u32[]{:S(2)}) collective-permute-start(bf16[16,3584]{1,0:T(8,128)(2,1)S(1)} %add_convert_fusion), channel_id=1, source_target_pairs={{0,2},{1,3},{2,0},{3,1},{4,6},{5,7},{6,4},{7,5},{8,10},{9,11},{10,... | collective-permute-start | bytes 344072 | tf_op jit(solution)/shard_map/ppermute | solution.py:237
  36.0 0.0 collective-permute-done.12
  36.1 0.6 %collective-permute-start.13 = (bf16[16,3584]{1,0:T(8,128)(2,1)S(1)}, bf16[16,3584]{1,0:T(8,128)(2,1)S(1)}, u32[]{:S(2)}, u32[]{:S(2)}) collective-permute-start(bf16[16,3584]{1,0:T(8,128)(2,1)S(1)} %add_convert_fusion.1), channel_id=1, source_target_pairs={{0,2},{1,3},{2,0},{3,1},{4,6},{5,7},{6,4},{7,5},{8,10},{9,11},{10,... | collective-permute-start | bytes 344072 | tf_op jit(solution)/shard_map/ppermute | solution.py:237
  36.7 0.0 collective-permute-done.11
  36.7 3.8 %collective-permute-done.15 = bf16[16,3584]{1,0:T(8,128)(2,1)S(1)} collective-permute-done((bf16[16,3584]{1,0:T(8,128)(2,1)S(1)}, bf16[16,3584]{1,0:T(8,128)(2,1)S(1)}, u32[]{:S(2)}, u32[]{:S(2)}) %collective-permute-start.15) | collective-permute-done | bytes 114720 | tf_op jit(solution)/shard_map/ppermute | solution.py:237
  40.5 1.7 %collective-permute-done.13 = bf16[16,3584]{1,0:T(8,128)(2,1)S(1)} collective-permute-done((bf16[16,3584]{1,0:T(8,128)(2,1)S(1)}, bf16[16,3584]{1,0:T(8,128)(2,1)S(1)}, u32[]{:S(2)}, u32[]{:S(2)}) %collective-permute-start.13) | collective-permute-done | bytes 114720 | tf_op jit(solution)/shard_map/ppermute | solution.py:237
  42.2 0.7 %pad_maximum_fusion = bf16[16,7168]{1,0:T(8,128)(2,1)} fusion(bf16[16,3584]{1,0:T(8,128)(2,1)S(1)} %get-tuple-element.74, bf16[16,3584]{1,0:T(8,128)(2,1)S(1)} %get-tuple-element.73), kind=kLoop, calls=%fused_computation.4 | loop fusion | flops 458752 | bytes 458752 | tf_op jit(solution)/shard_map/concatenate | solution.py:370
  (9 shorter events, 0.2 us)
Async XLA Ops:
  0.0 13.1 %collective-permute-start = (bf16[16,2048]{1,0:T(8,128)(2,1)}, bf16[16,2048]{1,0:T(8,128)(2,1)S(1)}, u32[]{:S(2)}, u32[]{:S(2)}) collective-permute-start(bf16[16,2048]{1,0:T(8,128)(2,1)} %refs_2_.1), channel_id=1, source_target_pairs={{0,8},{4,12},{8,0},{12,4},{16,24},{20,28},{24,16},{28,20},{1,9},{5... | collective-permute-start | bytes 196616 | tf_op jit(solution)/shard_map/ppermute | solution.py:234
  4.0 9.1 %collective-permute-start.1 = (bf16[16,2048]{1,0:T(8,128)(2,1)}, bf16[16,2048]{1,0:T(8,128)(2,1)S(1)}, u32[]{:S(2)}, u32[]{:S(2)}) collective-permute-start(bf16[16,2048]{1,0:T(8,128)(2,1)} %refs_2_.1), channel_id=1, source_target_pairs={{0,12},{4,8},{8,4},{12,0},{16,28},{20,24},{24,20},{28,16},{1,13},{... | collective-permute-start | bytes 196616 | tf_op jit(solution)/shard_map/ppermute | solution.py:234
  5.4 7.7 %collective-permute-start.2 = (bf16[16,2048]{1,0:T(8,128)(2,1)}, bf16[16,2048]{1,0:T(8,128)(2,1)S(1)}, u32[]{:S(2)}, u32[]{:S(2)}) collective-permute-start(bf16[16,2048]{1,0:T(8,128)(2,1)} %refs_2_.1), channel_id=1, source_target_pairs={{0,4},{4,0},{8,12},{12,8},{16,20},{20,16},{24,28},{28,24},{1,5},{5... | collective-permute-start | bytes 196616 | tf_op jit(solution)/shard_map/ppermute | solution.py:234
  9.5 12.7 %collective-permute-start.5 = (bf16[16,7168]{1,0:T(8,128)(2,1)S(1)}, bf16[16,7168]{1,0:T(8,128)(2,1)S(1)}, u32[]{:S(2)}, u32[]{:S(2)}) collective-permute-start(bf16[16,7168]{1,0:T(8,128)(2,1)S(1)} %get-tuple-element.53), channel_id=1, source_target_pairs={{0,8},{4,12},{8,0},{12,4},{16,28},{20,24},{24,20},{28,16},{1,9},{5... | collective-permute-start | bytes 688136 | tf_op jit(solution)/shard_map/ppermute | solution.py:234
  12.5 9.2 %collective-permute-start.6 = (bf16[16,3584]{1,0:T(8,128)(2,1)S(1)}, bf16[16,3584]{1,0:T(8,128)(2,1)S(1)}, u32[]{:S(2)}, u32[]{:S(2)}) collective-permute-start(bf16[16,3584]{1,0:T(8,128)(2,1)S(1)} %get-tuple-element.54), channel_id=1, source_target_pairs={{0,4},{4,0},{8,12},{12,8},{16,20},{20,16},{24,28},{28,24},{1,5},{5... | collective-permute-start | bytes 344072 | tf_op jit(solution)/shard_map/ppermute | solution.py:234
  13.4 3.7 %collective-permute-start.3 = (f32[32,64]{1,0:T(8,128)S(1)}, f32[32,64]{1,0:T(8,128)S(1)}, u32[]{:S(2)}, u32[]{:S(2)}) collective-permute-start(f32[32,64]{1,0:T(8,128)S(1)} %get-tuple-element.44.refs_1_), channel_id=1, source_target_pairs={{0,1},{1,0},{2,3},{3,2},{4,5},{5,4},{6,7},{7,6},{8,9},{9,8},{10,11... | collective-permute-start | bytes 24584 | tf_op jit(solution)/shard_map/ppermute | solution.py:237
  17.1 4.5 %collective-permute-start.4 = (f32[16,64]{1,0:T(8,128)S(1)}, f32[16,64]{1,0:T(8,128)S(1)}, u32[]{:S(2)}, u32[]{:S(2)}) collective-permute-start(f32[16,64]{1,0:T(8,128)S(1)} %slice.16), channel_id=1, source_target_pairs={{0,2},{1,3},{2,0},{3,1},{4,6},{5,7},{6,4},{7,5},{8,10},{9,11},{10,... | collective-permute-start | bytes 12296 | tf_op jit(solution)/shard_map/ppermute | solution.py:237
  22.2 10.2 %collective-permute-start.9 = (bf16[16,7168]{1,0:T(8,128)(2,1)S(1)}, bf16[16,7168]{1,0:T(8,128)(2,1)S(1)}, u32[]{:S(2)}, u32[]{:S(2)}) collective-permute-start(bf16[16,7168]{1,0:T(8,128)(2,1)S(1)} %collective-permute-done.5.refs_2_.refs_6_), channel_id=1, source_target_pairs={{0,16},{16,0},{1,17},{17,1},{2,18},{18,2},{3,19},{19,3},{4,20},{20... | collective-permute-start | bytes 688136 | tf_op jit(solution)/shard_map/ppermute | solution.py:240
  23.1 9.3 %collective-permute-start.10 = (bf16[16,3584]{1,0:T(8,128)(2,1)S(1)}, bf16[16,3584]{1,0:T(8,128)(2,1)S(1)}, u32[]{:S(2)}, u32[]{:S(2)}) collective-permute-start(bf16[16,3584]{1,0:T(8,128)(2,1)S(1)} %collective-permute-done.6.refs_3_.refs_7_), channel_id=1, source_target_pairs={{0,16},{16,0},{1,17},{17,1},{2,18},{18,2},{3,19},{19,3},{4,20},{20... | collective-permute-start | bytes 344072 | tf_op jit(solution)/shard_map/ppermute | solution.py:240
  24.2 3.6 %collective-permute-start.7 = (bf16[16,64]{1,0:T(8,128)(2,1)S(1)}, bf16[16,64]{1,0:T(8,128)(2,1)S(1)}, u32[]{:S(2)}, u32[]{:S(2)}) collective-permute-start(bf16[16,64]{1,0:T(8,128)(2,1)S(1)} %fusion.3.refs_1_), channel_id=1, source_target_pairs={{0,4},{4,0},{8,12},{12,8},{16,20},{20,16},{24,28},{28,24},{1,5},{5... | collective-permute-start | bytes 6152 | tf_op jit(solution)/shard_map/ppermute | solution.py:234
  27.9 4.5 %collective-permute-start.8 = (bf16[16,64]{1,0:T(8,128)(2,1)S(1)}, bf16[16,64]{1,0:T(8,128)(2,1)S(1)}, u32[]{:S(2)}, u32[]{:S(2)}) collective-permute-start(bf16[16,64]{1,0:T(8,128)(2,1)S(1)} %add.29.refs_1_), channel_id=1, source_target_pairs={{0,8},{4,12},{8,0},{12,4},{16,24},{20,28},{24,16},{28,20},{1,9},{5... | collective-permute-start | bytes 6152 | tf_op jit(solution)/shard_map/ppermute | solution.py:234
  32.9 1.6 %collective-permute-start.14 = (f32[16,3584]{1,0:T(8,128)S(1)}, f32[16,3584]{1,0:T(8,128)S(1)}, u32[]{:S(2)}, u32[]{:S(2)}) collective-permute-start(f32[16,3584]{1,0:T(8,128)S(1)} %get-tuple-element.72), channel_id=1, source_target_pairs={{0,1},{1,0},{2,3},{3,2},{4,5},{5,4},{6,7},{7,6},{8,9},{9,8},{10,11... | collective-permute-start | bytes 688136 | tf_op jit(solution)/shard_map/ppermute | solution.py:237
  33.0 3.1 %collective-permute-start.12 = (f32[16,3584]{1,0:T(8,128)S(1)}, f32[16,3584]{1,0:T(8,128)S(1)}, u32[]{:S(2)}, u32[]{:S(2)}) collective-permute-start(f32[16,3584]{1,0:T(8,128)S(1)} %get-tuple-element.70), channel_id=1, source_target_pairs={{0,1},{1,0},{2,3},{3,2},{4,5},{5,4},{6,7},{7,6},{8,9},{9,8},{10,11... | collective-permute-start | bytes 688136 | tf_op jit(solution)/shard_map/ppermute | solution.py:237
  33.5 3.2 %collective-permute-start.11 = (f32[16,7168]{1,0:T(8,128)S(1)}, f32[16,7168]{1,0:T(8,128)S(1)}, u32[]{:S(2)}, u32[]{:S(2)}) collective-permute-start(f32[16,7168]{1,0:T(8,128)S(1)} %get-tuple-element.68), channel_id=1, source_target_pairs={{0,1},{1,0},{2,3},{3,2},{4,5},{5,4},{6,7},{7,6},{8,9},{9,8},{10,11... | collective-permute-start | bytes 1376264 | tf_op jit(solution)/shard_map/ppermute | solution.py:237
  34.5 6.1 %collective-permute-start.15 = (bf16[16,3584]{1,0:T(8,128)(2,1)S(1)}, bf16[16,3584]{1,0:T(8,128)(2,1)S(1)}, u32[]{:S(2)}, u32[]{:S(2)}) collective-permute-start(bf16[16,3584]{1,0:T(8,128)(2,1)S(1)} %add_convert_fusion), channel_id=1, source_target_pairs={{0,2},{1,3},{2,0},{3,1},{4,6},{5,7},{6,4},{7,5},{8,10},{9,11},{10,... | collective-permute-start | bytes 344072 | tf_op jit(solution)/shard_map/ppermute | solution.py:237
  36.1 6.1 %collective-permute-start.13 = (bf16[16,3584]{1,0:T(8,128)(2,1)S(1)}, bf16[16,3584]{1,0:T(8,128)(2,1)S(1)}, u32[]{:S(2)}, u32[]{:S(2)}) collective-permute-start(bf16[16,3584]{1,0:T(8,128)(2,1)S(1)} %add_convert_fusion.1), channel_id=1, source_target_pairs={{0,2},{1,3},{2,0},{3,1},{4,6},{5,7},{6,4},{7,5},{8,10},{9,11},{10,... | collective-permute-start | bytes 344072 | tf_op jit(solution)/shard_map/ppermute | solution.py:237

commit v14 on v13

--- a/solution.py
+++ b/solution.py
@@ -62,17 +62,17 @@
 
 def cut_kernel(block, numbers, small_count, expand, weight, *refs):
     small, refs = refs[:small_count], refs[small_count:]
-    whole, half, own, *loaded, held, sem, held_sem = refs
+    across, beside, own, *loaded, held, sem, held_sem = refs
     g, a = lax.axis_index("groups"), lax.axis_index("adapter")
-    columns, half_width = whole.shape[1], half.shape[1]
+    columns = own.shape[1]
     firsts = (
         lax.bitwise_xor(a, 2 + g) * columns,
-        lax.bitwise_xor(a, 1) * columns + g * half_width,
+        lax.bitwise_xor(a, 1) * columns,
         a * columns,
     )
     copies = []
-    for n, (first, target) in enumerate(zip(firsts, (whole, half, own))):
-        span = pl.ds(pl.multiple_of(first, lane), target.shape[1])
+    for n, (first, target) in enumerate(zip(firsts, (across, beside, own))):
+        span = pl.ds(pl.multiple_of(first, lane), columns)
         copies.append(pltpu.make_async_copy(expand.at[0, :, span], target, sem.at[n]))
     for n, (source, target) in enumerate(zip(small, loaded)):
         copies.append(pltpu.make_async_copy(source, target, sem.at[len(firsts) + n]))
@@ -152,29 +152,17 @@
 
 
 def delta_kernel(block, splits, slot, *refs):
-    bases, refs = refs[: -len(splits) * 2 - 11], refs[-len(splits) * 2 - 11 :]
-    own, shrunk, whole, half, far_whole, far_half, own_keep, own_send = refs[:8]
-    cross_keep, cross_send = refs[8 : 8 + len(splits)], refs[8 + len(splits) : 8 + 2 * len(splits)]
-    flat, ordered, two = refs[-3:]
+    bases, refs = refs[: -len(splits) * 2 - 9], refs[-len(splits) * 2 - 9 :]
+    own, shrunk, across, beside, swapped, own_keep, own_send = refs[:7]
+    cross_keep, cross_send = refs[7 : 7 + len(splits)], refs[7 + len(splits) : 7 + 2 * len(splits)]
+    flat, ordered = refs[-2:]
     g, a, t = (lax.axis_index(name) for name in ("groups", "adapter", "tensor"))
     row_count = bases[0].shape[0]
     quarter = row_count // 4
-    half_width = half.shape[1]
-
-    @pl.when(g == 0)
-    def _():
-        two[:, :half_width] = half[...]
-        two[:, half_width:] = far_half[...]
-
-    @pl.when(g != 0)
-    def _():
-        two[:, :half_width] = far_half[...]
-        two[:, half_width:] = half[...]
-
     merged = shrunk[...].astype(f32)
     spread = [
         jnp.where(slot[...] == lax.bitwise_xor(a, j), merged, 0.0)
-        for j in (0, 2 + g, 3 - g, 1)
+        for j in (0, 2 + g, 1, 3 - g)
     ]
     flat[...] = jnp.concatenate(spread, axis=0).T
     for i, turn in enumerate((0, 2, 1, 3)):
@@ -186,7 +174,7 @@
         for column in range(0, base.shape[1], block):
             span = slice(at, at + block)
             expand = jnp.concatenate(
-                [own[:, span], whole[:, span], far_whole[:, span], two[:, span]], axis=0
+                [own[:, span], across[:, span], beside[:, span], swapped[:, span]], axis=0
             )
             total = base[:, column : column + block] + jnp.dot(
                 left, expand, preferred_element_type=f32
@@ -222,7 +210,6 @@
     columns = base_up_weight.shape[1]
     rank_block = adapter_expand_weight.shape[1]
     rank = adapter_shrink_weight.shape[2]
-    half_width = columns // 2
     block = column_block(columns)
     block_count = columns // block
 
@@ -257,7 +244,7 @@
             adapter_shrink_weight[0].T,
         )
     ]
-    whole, half, own, slots, index, mine, shrink, held = kernel_call(
+    across, beside, own, slots, index, mine, shrink, held = kernel_call(
         functools.partial(cut_kernel, block, range(loads[1]), len(small)),
         "cut_expand",
         1,
@@ -265,7 +252,7 @@
         1,
         in_specs=[anywhere] * (2 + len(small)),
         out_specs=[vmem] * (4 + len(small)),
-        out_shape=[pltpu.VMEM((rank_block, w), bf16) for w in (columns, half_width, columns)]
+        out_shape=[pltpu.VMEM((rank_block, w), bf16) for w in (columns,) * 3]
         + [pltpu.VMEM(x.shape, x.dtype) for x in small]
         + [pltpu.VMEM((loads[1], depth, block), bf16)],
         scratch_shapes=[
@@ -274,7 +261,7 @@
         ],
     )(expand, weight, *small)
     loaded = [held]
-    whole, half = from_owner(whole, 2, 3), from_owner(half, 1, 1)
+    across = from_owner(across, 2, 3)
 
     rows, keep, send, slot = kernel_call(
         functools.partial(gather_kernel, (0, *offsets)),
@@ -330,13 +317,15 @@
     pair = keep + arrived
     arrived = from_tensor(pair[rank_block:], 2)
     base_1 = base_part(1, pair)
-    arrived, base_1, whole, half = lax.optimization_barrier((arrived, base_1, whole, half))
+    arrived, base_1, across = lax.optimization_barrier((arrived, base_1, across))
     shrunk = (adapter_scale * (pair[:rank_block] + arrived)).astype(bf16)
-    far_whole, far_half = from_group(whole), from_group(half)
+    swapped = from_group(across)
+    beside, shrunk = lax.optimization_barrier((beside, shrunk))
+    beside = from_owner(beside, 1, 1)
     bases = [base_0, base_1]
     for m, n in ((1, 2), (2, 3)):
         arrived = from_owner(shrunk, m, m)
-        base = base_part(n, shrunk, whole, half)
+        base = base_part(n, shrunk, across)
         arrived, base = lax.optimization_barrier((arrived, base))
         bases.append(base)
         shrunk = shrunk + arrived
@@ -351,7 +340,7 @@
         1,
         1,
         8,
-        in_specs=[vmem] * (len(bases) + 7),
+        in_specs=[vmem] * (len(bases) + 6),
         out_specs=[vmem] * (2 + 2 * len(splits)),
         out_shape=[
             jax.ShapeDtypeStruct((quarter, w), f32) for w in (columns, columns, *widths, *widths)
@@ -359,9 +348,8 @@
         scratch_shapes=[
             pltpu.VMEM((row_count, rank_block * owner_count), f32),
             pltpu.VMEM((row_count, rank_block * owner_count), bf16),
-            pltpu.VMEM((rank_block, columns), bf16),
         ],
-    )(slot, *bases, own, shrunk, whole, half, far_whole, far_half)
+    )(slot, *bases, own, shrunk, across, beside, swapped)
     own_keep, own_send = out[:2]
     crossed = []
     for keep, send in zip(out[2:4], out[4:6]):

time: 43.1 us -> 44.1 us (1.023)
  waiting for transfers between devices: 8.61 us -> 10.5 us
  starting transfers between devices: 17.8 us -> 17 us
    ppermute x7, waiting for transfers between devices: 2.23 us -> 4.08 us  [from_owner(): return lax.ppermute(x, ('groups', 'adapter'), pairs)]
    ppermute x7, starting transfers between devices: 11.3 us -> 10.4 us  [from_owner(): return lax.ppermute(x, ('groups', 'adapter'), pairs)]
    ppermute x2 -> x1, starting transfers between devices: 2.03 us -> 2.13 us  [from_group(): return lax.ppermute(x, 'groups', [(0, 1), (1, 0)])]
  transfers between devices with their start and end apart: 16 -> 15, of which waited for: 6 -> 6; matrix products, arithmetic and copies ran while one was open for 0% -> 0% of each run, Pallas kernels for 35% -> 34%
where the time goes in v14:
time: 44.1 us; the launch traced here: 44 us
  starting transfers between devices  17 us (39%)
  Pallas kernels  15.5 us (35%)
  waiting for transfers between devices  10.5 us (24%)
  other arithmetic  0.88 us (2%)
    pallas_call x4, Pallas kernels, base_part(): kernel_call(functools.partial(base_kernel, block, places, numbers, stream...  10.8 us
    ppermute x7, starting transfers between devices, from_owner(): return lax.ppermute(x, ('groups', 'adapter'), pairs)  10.4 us
    ppermute x7, waiting for transfers between devices, from_tensor(): return lax.ppermute(x, 'tensor', [(s, s ^ m) for s in range(4)])  6.38 us
    ppermute x7, starting transfers between devices, from_tensor(): return lax.ppermute(x, 'tensor', [(s, s ^ m) for s in range(4)])  4.43 us
    ppermute x7, waiting for transfers between devices, from_owner(): return lax.ppermute(x, ('groups', 'adapter'), pairs)  4.08 us
    pallas_call x1, Pallas kernels, paired(): kernel_call(functools.partial(cut_kernel, block, range(loads[1]), len(sma...  3.94 us
    ppermute x1, starting transfers between devices, from_group(): return lax.ppermute(x, 'groups', [(0, 1), (1, 0)])  2.13 us
  transfers between devices with their start and end apart: 15, of which 6 were waited for; matrix products, arithmetic and copies ran while one was open for 0% of the time, Pallas kernels for 34%

profile of v14, /device:TPU:0, one launch (start us, length us, event | category | flops | bytes accessed | tf_op | source)
XLA Modules:
  0.0 44.0 jit_solution(16223524890123690379)
XLA Ops:
  0.0 4.0 %collective-permute-start = (bf16[16,2048]{1,0:T(8,128)(2,1)}, bf16[16,2048]{1,0:T(8,128)(2,1)S(1)}, u32[]{:S(2)}, u32[]{:S(2)}) collective-permute-start(bf16[16,2048]{1,0:T(8,128)(2,1)} %refs_2_.1), channel_id=1, source_target_pairs={{0,8},{4,12},{8,0},{12,4},{16,24},{20,28},{24,16},{28,20},{1,9},{5... | collective-permute-start | bytes 196616 | tf_op jit(solution)/shard_map/ppermute | solution.py:221
  4.0 1.3 %collective-permute-start.1 = (bf16[16,2048]{1,0:T(8,128)(2,1)}, bf16[16,2048]{1,0:T(8,128)(2,1)S(1)}, u32[]{:S(2)}, u32[]{:S(2)}) collective-permute-start(bf16[16,2048]{1,0:T(8,128)(2,1)} %refs_2_.1), channel_id=1, source_target_pairs={{0,12},{4,8},{8,4},{12,0},{16,28},{20,24},{24,20},{28,16},{1,13},{... | collective-permute-start | bytes 196616 | tf_op jit(solution)/shard_map/ppermute | solution.py:221
  5.4 0.2 collective-permute-start.2
  5.6 3.9 %cut_expand.1 = (bf16[16,7168]{1,0:T(8,128)(2,1)S(1)}, bf16[16,7168]{1,0:T(8,128)(2,1)S(1)}, bf16[16,7168]{1,0:T(8,128)(2,1)S(1)}, s32[1,4]{1,0:T(1,128)S(1)}, s...) custom-call(bf16[1,16,28672]{2,1,0:T(8,128)(2,1)} %expand.1, ...), custom_call_target="tpu_custom_call" | custom-call | flops 1 | bytes 1 | tf_op jit(solution)/shard_map/cut_expand/pallas_call | solution.py:247
  9.6 2.9 %collective-permute-start.5 = (bf16[16,7168]{1,0:T(8,128)(2,1)S(1)}, bf16[16,7168]{1,0:T(8,128)(2,1)S(1)}, u32[]{:S(2)}, u32[]{:S(2)}) collective-permute-start(bf16[16,7168]{1,0:T(8,128)(2,1)S(1)} %get-tuple-element.54), channel_id=1, source_target_pairs={{0,8},{4,12},{8,0},{12,4},{16,28},{20,24},{24,20},{28,16},{1,9},{5... | collective-permute-start | bytes 688136 | tf_op jit(solution)/shard_map/ppermute | solution.py:221
  12.5 0.0 collective-permute-done.refs_1_
  12.5 0.0 collective-permute-done.1.refs_2_
  12.5 0.0 collective-permute-done.2.refs_3_
  12.5 0.3 gather_rows.1
  12.8 0.1 collective-permute-start.3
  12.8 3.6 %base_part.4 = (f32[64,2048]{1,0:T(8,128)S(1)}, bf16[4,2048,512]{2,1,0:T(8,128)(2,1)S(1)}) custom-call(bf16[64,2048]{1,0:T(8,128)(2,1)S(1)} %get-tuple-element.46.rows, bf16[2048,7168]{1,0:T(8,128)(2,1)} %weight.9, bf16[4,2048,512]{2,1,0:T(8,128)(2,1)S(1)} %get-tuple-element.47.refs_0_, f32[32,64]{1,0:T(8,128)S(1)} %get-tuple-element.45.refs_1_), custom_call_target="tpu_custom_call" | custom-call | flops 1610612736 | bytes 25165824 | tf_op jit(solution)/shard_map/base_part/pallas_call | solution.py:298
  16.4 0.0 collective-permute-done.3
  16.5 1.6 %collective-permute-start.4 = (f32[16,64]{1,0:T(8,128)S(1)}, f32[16,64]{1,0:T(8,128)S(1)}, u32[]{:S(2)}, u32[]{:S(2)}) collective-permute-start(f32[16,64]{1,0:T(8,128)S(1)} %slice.16), channel_id=1, source_target_pairs={{0,2},{1,3},{2,0},{3,1},{4,6},{5,7},{6,4},{7,5},{8,10},{9,11},{10,... | collective-permute-start | bytes 12296 | tf_op jit(solution)/shard_map/ppermute | solution.py:224
  18.0 3.0 %base_part.5 = (f32[64,2048]{1,0:T(8,128)S(1)}, bf16[3,2048,512]{2,1,0:T(8,128)(2,1)S(1)}) custom-call(bf16[64,2048]{1,0:T(8,128)(2,1)S(1)} %get-tuple-element.46.rows, bf16[2048,7168]{1,0:T(8,128)(2,1)} %weight.9, bf16[4,2048,512]{2,1,0:T(8,128)(2,1)S(1)} %get-tuple-element.52.refs_0_, f32[32,64]{1,0:T(8,128)S(1)} %add.27.refs_1_), custom_call_target="tpu_custom_call" | custom-call | flops 1610612736 | bytes 25165824 | tf_op jit(solution)/shard_map/base_part/pallas_call | solution.py:298
  21.0 0.0 collective-permute-done.4
  21.0 1.2 %collective-permute-done.5.refs_2_.refs_6_ = bf16[16,7168]{1,0:T(8,128)(2,1)S(1)} collective-permute-done((bf16[16,7168]{1,0:T(8,128)(2,1)S(1)}, bf16[16,7168]{1,0:T(8,128)(2,1)S(1)}, u32[]{:S(2)}, u32[]{:S(2)}) %collective-permute-start.5) | collective-permute-done | bytes 229408 | tf_op jit(solution)/shard_map/ppermute | solution.py:221
  22.2 0.0 collective-permute-start.8
  22.2 2.1 %collective-permute-start.9 = (bf16[16,7168]{1,0:T(8,128)(2,1)S(1)}, bf16[16,7168]{1,0:T(8,128)(2,1)S(1)}, u32[]{:S(2)}, u32[]{:S(2)}) collective-permute-start(bf16[16,7168]{1,0:T(8,128)(2,1)S(1)} %collective-permute-done.5.refs_2_.refs_6_), channel_id=1, source_target_pairs={{0,16},{16,0},{1,17},{17,1},{2,18},{18,2},{3,19},{19,3},{4,20},{20... | collective-permute-start | bytes 688136 | tf_op jit(solution)/shard_map/ppermute | solution.py:227
  24.4 0.4 collective-permute-start.6
  24.8 1.6 %base_part.6 = (f32[64,1536]{1,0:T(8,128)S(1)}, bf16[1,2048,512]{2,1,0:T(8,128)(2,1)S(1)}) custom-call(bf16[64,2048]{1,0:T(8,128)(2,1)S(1)} %get-tuple-element.46.rows, bf16[2048,7168]{1,0:T(8,128)(2,1)} %weight.9, bf16[3,2048,512]{2,1,0:T(8,128)(2,1)S(1)} %get-tuple-element.59.refs_0_, bf16[16,64]{1,0:T(8,128)(2,1)S(1)} %fusion.3.refs_1_, ...), custom_call_target="tpu_custom_call" | custom-call | flops 1 | bytes 1 | tf_op jit(solution)/shard_map/base_part/pallas_call | solution.py:298
  26.3 2.6 %collective-permute-done.6 = bf16[16,64]{1,0:T(8,128)(2,1)S(1)} collective-permute-done((bf16[16,64]{1,0:T(8,128)(2,1)S(1)}, bf16[16,64]{1,0:T(8,128)(2,1)S(1)}, u32[]{:S(2)}, u32[]{:S(2)}) %collective-permute-start.6) | collective-permute-done | bytes 2080 | tf_op jit(solution)/shard_map/ppermute | solution.py:221
  28.9 1.5 %collective-permute-start.7 = (bf16[16,64]{1,0:T(8,128)(2,1)S(1)}, bf16[16,64]{1,0:T(8,128)(2,1)S(1)}, u32[]{:S(2)}, u32[]{:S(2)}) collective-permute-start(bf16[16,64]{1,0:T(8,128)(2,1)S(1)} %add.29.refs_1_), channel_id=1, source_target_pairs={{0,8},{4,12},{8,0},{12,4},{16,24},{20,28},{24,16},{28,20},{1,9},{5... | collective-permute-start | bytes 6152 | tf_op jit(solution)/shard_map/ppermute | solution.py:221
  30.4 2.7 %base_part.7.refs_3_ = f32[64,1536]{1,0:T(8,128)S(1)} custom-call(bf16[64,2048]{1,0:T(8,128)(2,1)S(1)} %get-tuple-element.46.rows, bf16[2048,7168]{1,0:T(8,128)(2,1)} %weight.9, bf16[1,2048,512]{2,1,0:T(8,128)(2,1)S(1)} %get-tuple-element.64.refs_0_, bf16[16,64]{1,0:T(8,128)(2,1)S(1)} %add.29.refs_1_, bf16[16,7168]{1,0:T(8,128)(2,1)S(1)} %collective-permute-done.5.refs_2_.refs_6_), custom_call_target="tpu_custom_call" | custom-call | flops 1 | bytes 1 | tf_op jit(solution)/shard_map/base_part/pallas_call | solution.py:298
  33.2 0.3 collective-permute-done.7
  33.4 0.0 collective-permute-done.8.refs_7_
  33.4 0.0 collective-permute-done.9.refs_8_
  33.4 0.5 %add_delta.1 = (f32[16,7168]{1,0:T(8,128)S(1)}, f32[16,7168]{1,0:T(8,128)S(1)}, f32[16,3584]{1,0:T(8,128)S(1)}, f32[16,3584]{1,0:T(8,128)S(1)}, f32[16,3584]{1,0:T(8,128)S(1)}, /*index=5*/f32[16,3584]{1,0:T(8,128)S(1)}) custom-call(s32[1,64]{1,0:T(1,128)S(1)} %get-tuple-element.44.slot, f32[64,2048]{1,0:T(8,128)S(1)} %get-tuple-element.49.refs_0_, ...), custom_call_target="tpu_custom_call" | custom-call | flops 1 | bytes 1 | tf_op jit(solution)/shard_map/add_delta/pallas_call | solution.py:337
  33.9 0.1 collective-permute-start.13
  34.0 0.5 %collective-permute-start.11 = (f32[16,3584]{1,0:T(8,128)S(1)}, f32[16,3584]{1,0:T(8,128)S(1)}, u32[]{:S(2)}, u32[]{:S(2)}) collective-permute-start(f32[16,3584]{1,0:T(8,128)S(1)} %get-tuple-element.72), channel_id=1, source_target_pairs={{0,1},{1,0},{2,3},{3,2},{4,5},{5,4},{6,7},{7,6},{8,9},{9,8},{10,11... | collective-permute-start | bytes 688136 | tf_op jit(solution)/shard_map/ppermute | solution.py:224
  34.5 0.1 collective-permute-start.10
  34.6 0.9 %collective-permute-done.13 = f32[16,3584]{1,0:T(8,128)S(1)} collective-permute-done((f32[16,3584]{1,0:T(8,128)S(1)}, f32[16,3584]{1,0:T(8,128)S(1)}, u32[]{:S(2)}, u32[]{:S(2)}) %collective-permute-start.13) | collective-permute-done | bytes 229408 | tf_op jit(solution)/shard_map/ppermute | solution.py:224
  35.5 1.5 %collective-permute-start.14 = (bf16[16,3584]{1,0:T(8,128)(2,1)S(1)}, bf16[16,3584]{1,0:T(8,128)(2,1)S(1)}, u32[]{:S(2)}, u32[]{:S(2)}) collective-permute-start(bf16[16,3584]{1,0:T(8,128)(2,1)S(1)} %add_convert_fusion), channel_id=1, source_target_pairs={{0,2},{1,3},{2,0},{3,1},{4,6},{5,7},{6,4},{7,5},{8,10},{9,11},{10,... | collective-permute-start | bytes 344072 | tf_op jit(solution)/shard_map/ppermute | solution.py:224
  37.0 0.0 collective-permute-done.11
  37.0 0.7 %collective-permute-start.12 = (bf16[16,3584]{1,0:T(8,128)(2,1)S(1)}, bf16[16,3584]{1,0:T(8,128)(2,1)S(1)}, u32[]{:S(2)}, u32[]{:S(2)}) collective-permute-start(bf16[16,3584]{1,0:T(8,128)(2,1)S(1)} %add_convert_fusion.1), channel_id=1, source_target_pairs={{0,2},{1,3},{2,0},{3,1},{4,6},{5,7},{6,4},{7,5},{8,10},{9,11},{10,... | collective-permute-start | bytes 344072 | tf_op jit(solution)/shard_map/ppermute | solution.py:224
  37.7 0.0 collective-permute-done.10
  37.8 3.8 %collective-permute-done.14 = bf16[16,3584]{1,0:T(8,128)(2,1)S(1)} collective-permute-done((bf16[16,3584]{1,0:T(8,128)(2,1)S(1)}, bf16[16,3584]{1,0:T(8,128)(2,1)S(1)}, u32[]{:S(2)}, u32[]{:S(2)}) %collective-permute-start.14) | collective-permute-done | bytes 114720 | tf_op jit(solution)/shard_map/ppermute | solution.py:224
  41.6 1.7 %collective-permute-done.12 = bf16[16,3584]{1,0:T(8,128)(2,1)S(1)} collective-permute-done((bf16[16,3584]{1,0:T(8,128)(2,1)S(1)}, bf16[16,3584]{1,0:T(8,128)(2,1)S(1)}, u32[]{:S(2)}, u32[]{:S(2)}) %collective-permute-start.12) | collective-permute-done | bytes 114720 | tf_op jit(solution)/shard_map/ppermute | solution.py:224
  43.2 0.1 fusion.1
  43.3 0.7 %pad_maximum_fusion = bf16[16,7168]{1,0:T(8,128)(2,1)} fusion(bf16[16,3584]{1,0:T(8,128)(2,1)S(1)} %get-tuple-element.76, bf16[16,3584]{1,0:T(8,128)(2,1)S(1)} %get-tuple-element.75), kind=kLoop, calls=%fused_computation.4 | loop fusion | flops 458752 | bytes 458752 | tf_op jit(solution)/shard_map/concatenate | solution.py:358
  (8 shorter events, 0.1 us)
Async XLA Ops:
  0.0 12.5 %collective-permute-start = (bf16[16,2048]{1,0:T(8,128)(2,1)}, bf16[16,2048]{1,0:T(8,128)(2,1)S(1)}, u32[]{:S(2)}, u32[]{:S(2)}) collective-permute-start(bf16[16,2048]{1,0:T(8,128)(2,1)} %refs_2_.1), channel_id=1, source_target_pairs={{0,8},{4,12},{8,0},{12,4},{16,24},{20,28},{24,16},{28,20},{1,9},{5... | collective-permute-start | bytes 196616 | tf_op jit(solution)/shard_map/ppermute | solution.py:221
  4.0 8.5 %collective-permute-start.1 = (bf16[16,2048]{1,0:T(8,128)(2,1)}, bf16[16,2048]{1,0:T(8,128)(2,1)S(1)}, u32[]{:S(2)}, u32[]{:S(2)}) collective-permute-start(bf16[16,2048]{1,0:T(8,128)(2,1)} %refs_2_.1), channel_id=1, source_target_pairs={{0,12},{4,8},{8,4},{12,0},{16,28},{20,24},{24,20},{28,16},{1,13},{... | collective-permute-start | bytes 196616 | tf_op jit(solution)/shard_map/ppermute | solution.py:221
  5.4 7.1 %collective-permute-start.2 = (bf16[16,2048]{1,0:T(8,128)(2,1)}, bf16[16,2048]{1,0:T(8,128)(2,1)S(1)}, u32[]{:S(2)}, u32[]{:S(2)}) collective-permute-start(bf16[16,2048]{1,0:T(8,128)(2,1)} %refs_2_.1), channel_id=1, source_target_pairs={{0,4},{4,0},{8,12},{12,8},{16,20},{20,16},{24,28},{28,24},{1,5},{5... | collective-permute-start | bytes 196616 | tf_op jit(solution)/shard_map/ppermute | solution.py:221
  9.6 12.7 %collective-permute-start.5 = (bf16[16,7168]{1,0:T(8,128)(2,1)S(1)}, bf16[16,7168]{1,0:T(8,128)(2,1)S(1)}, u32[]{:S(2)}, u32[]{:S(2)}) collective-permute-start(bf16[16,7168]{1,0:T(8,128)(2,1)S(1)} %get-tuple-element.54), channel_id=1, source_target_pairs={{0,8},{4,12},{8,0},{12,4},{16,28},{20,24},{24,20},{28,16},{1,9},{5... | collective-permute-start | bytes 688136 | tf_op jit(solution)/shard_map/ppermute | solution.py:221
  12.8 3.7 %collective-permute-start.3 = (f32[32,64]{1,0:T(8,128)S(1)}, f32[32,64]{1,0:T(8,128)S(1)}, u32[]{:S(2)}, u32[]{:S(2)}) collective-permute-start(f32[32,64]{1,0:T(8,128)S(1)} %get-tuple-element.45.refs_1_), channel_id=1, source_target_pairs={{0,1},{1,0},{2,3},{3,2},{4,5},{5,4},{6,7},{7,6},{8,9},{9,8},{10,11... | collective-permute-start | bytes 24584 | tf_op jit(solution)/shard_map/ppermute | solution.py:224
  16.5 4.5 %collective-permute-start.4 = (f32[16,64]{1,0:T(8,128)S(1)}, f32[16,64]{1,0:T(8,128)S(1)}, u32[]{:S(2)}, u32[]{:S(2)}) collective-permute-start(f32[16,64]{1,0:T(8,128)S(1)} %slice.16), channel_id=1, source_target_pairs={{0,2},{1,3},{2,0},{3,1},{4,6},{5,7},{6,4},{7,5},{8,10},{9,11},{10,... | collective-permute-start | bytes 12296 | tf_op jit(solution)/shard_map/ppermute | solution.py:224
  22.2 11.2 %collective-permute-start.8 = (bf16[16,7168]{1,0:T(8,128)(2,1)S(1)}, bf16[16,7168]{1,0:T(8,128)(2,1)S(1)}, u32[]{:S(2)}, u32[]{:S(2)}) collective-permute-start(bf16[16,7168]{1,0:T(8,128)(2,1)S(1)} %get-tuple-element.68), channel_id=1, source_target_pairs={{0,4},{4,0},{8,12},{12,8},{16,20},{20,16},{24,28},{28,24},{1,5},{5... | collective-permute-start | bytes 688136 | tf_op jit(solution)/shard_map/ppermute | solution.py:221
  22.2 11.2 %collective-permute-start.9 = (bf16[16,7168]{1,0:T(8,128)(2,1)S(1)}, bf16[16,7168]{1,0:T(8,128)(2,1)S(1)}, u32[]{:S(2)}, u32[]{:S(2)}) collective-permute-start(bf16[16,7168]{1,0:T(8,128)(2,1)S(1)} %collective-permute-done.5.refs_2_.refs_6_), channel_id=1, source_target_pairs={{0,16},{16,0},{1,17},{17,1},{2,18},{18,2},{3,19},{19,3},{4,20},{20... | collective-permute-start | bytes 688136 | tf_op jit(solution)/shard_map/ppermute | solution.py:227
  24.4 4.5 %collective-permute-start.6 = (bf16[16,64]{1,0:T(8,128)(2,1)S(1)}, bf16[16,64]{1,0:T(8,128)(2,1)S(1)}, u32[]{:S(2)}, u32[]{:S(2)}) collective-permute-start(bf16[16,64]{1,0:T(8,128)(2,1)S(1)} %fusion.3.refs_1_), channel_id=1, source_target_pairs={{0,4},{4,0},{8,12},{12,8},{16,20},{20,16},{24,28},{28,24},{1,5},{5... | collective-permute-start | bytes 6152 | tf_op jit(solution)/shard_map/ppermute | solution.py:221
  28.9 4.5 %collective-permute-start.7 = (bf16[16,64]{1,0:T(8,128)(2,1)S(1)}, bf16[16,64]{1,0:T(8,128)(2,1)S(1)}, u32[]{:S(2)}, u32[]{:S(2)}) collective-permute-start(bf16[16,64]{1,0:T(8,128)(2,1)S(1)} %add.29.refs_1_), channel_id=1, source_target_pairs={{0,8},{4,12},{8,0},{12,4},{16,24},{20,28},{24,16},{28,20},{1,9},{5... | collective-permute-start | bytes 6152 | tf_op jit(solution)/shard_map/ppermute | solution.py:221
  33.9 1.6 %collective-permute-start.13 = (f32[16,3584]{1,0:T(8,128)S(1)}, f32[16,3584]{1,0:T(8,128)S(1)}, u32[]{:S(2)}, u32[]{:S(2)}) collective-permute-start(f32[16,3584]{1,0:T(8,128)S(1)} %get-tuple-element.74), channel_id=1, source_target_pairs={{0,1},{1,0},{2,3},{3,2},{4,5},{5,4},{6,7},{7,6},{8,9},{9,8},{10,11... | collective-permute-start | bytes 688136 | tf_op jit(solution)/shard_map/ppermute | solution.py:224
  34.0 3.0 %collective-permute-start.11 = (f32[16,3584]{1,0:T(8,128)S(1)}, f32[16,3584]{1,0:T(8,128)S(1)}, u32[]{:S(2)}, u32[]{:S(2)}) collective-permute-start(f32[16,3584]{1,0:T(8,128)S(1)} %get-tuple-element.72), channel_id=1, source_target_pairs={{0,1},{1,0},{2,3},{3,2},{4,5},{5,4},{6,7},{7,6},{8,9},{9,8},{10,11... | collective-permute-start | bytes 688136 | tf_op jit(solution)/shard_map/ppermute | solution.py:224
  34.5 3.2 %collective-permute-start.10 = (f32[16,7168]{1,0:T(8,128)S(1)}, f32[16,7168]{1,0:T(8,128)S(1)}, u32[]{:S(2)}, u32[]{:S(2)}) collective-permute-start(f32[16,7168]{1,0:T(8,128)S(1)} %get-tuple-element.70), channel_id=1, source_target_pairs={{0,1},{1,0},{2,3},{3,2},{4,5},{5,4},{6,7},{7,6},{8,9},{9,8},{10,11... | collective-permute-start | bytes 1376264 | tf_op jit(solution)/shard_map/ppermute | solution.py:224
  35.5 6.1 %collective-permute-start.14 = (bf16[16,3584]{1,0:T(8,128)(2,1)S(1)}, bf16[16,3584]{1,0:T(8,128)(2,1)S(1)}, u32[]{:S(2)}, u32[]{:S(2)}) collective-permute-start(bf16[16,3584]{1,0:T(8,128)(2,1)S(1)} %add_convert_fusion), channel_id=1, source_target_pairs={{0,2},{1,3},{2,0},{3,1},{4,6},{5,7},{6,4},{7,5},{8,10},{9,11},{10,... | collective-permute-start | bytes 344072 | tf_op jit(solution)/shard_map/ppermute | solution.py:224
  37.0 6.2 %collective-permute-start.12 = (bf16[16,3584]{1,0:T(8,128)(2,1)S(1)}, bf16[16,3584]{1,0:T(8,128)(2,1)S(1)}, u32[]{:S(2)}, u32[]{:S(2)}) collective-permute-start(bf16[16,3584]{1,0:T(8,128)(2,1)S(1)} %add_convert_fusion.1), channel_id=1, source_target_pairs={{0,2},{1,3},{2,0},{3,1},{4,6},{5,7},{6,4},{7,5},{8,10},{9,11},{10,... | collective-permute-start | bytes 344072 | tf_op jit(solution)/shard_map/ppermute | solution.py:224

commit v15 on v14

--- a/solution.py
+++ b/solution.py
@@ -233,7 +233,7 @@
 
     cuts = [block_count * k // 14 for k in (0, 4, 8, 11, 14)]
     parts = list(zip(cuts[:-1], cuts[1:]))
-    loads = [block_count * k // 14 for k in (0, 4, 8, 11, 12, 14)]
+    loads = [block_count * k // 14 for k in (0, 4, 8, 11, 13, 14)]
     bands = 4
     small = [
         pltpu.with_memory_space_constraint(x, pltpu.HBM)
@@ -261,7 +261,7 @@
         ],
     )(expand, weight, *small)
     loaded = [held]
-    across = from_owner(across, 2, 3)
+    across, beside = from_owner(across, 2, 3), from_owner(beside, 1, 1)
 
     rows, keep, send, slot = kernel_call(
         functools.partial(gather_kernel, (0, *offsets)),
@@ -320,8 +320,6 @@
     arrived, base_1, across = lax.optimization_barrier((arrived, base_1, across))
     shrunk = (adapter_scale * (pair[:rank_block] + arrived)).astype(bf16)
     swapped = from_group(across)
-    beside, shrunk = lax.optimization_barrier((beside, shrunk))
-    beside = from_owner(beside, 1, 1)
     bases = [base_0, base_1]
     for m, n in ((1, 2), (2, 3)):
         arrived = from_owner(shrunk, m, m)

time: 44.1 us -> 42.3 us (0.959)
  waiting for transfers between devices: 10.5 us -> 7.63 us
  starting transfers between devices: 17 us -> 18 us
    ppermute x7, waiting for transfers between devices: 4.08 us -> 1.25 us  [from_owner(): return lax.ppermute(x, ('groups', 'adapter'), pairs)]
    ppermute x7, starting transfers between devices: 10.4 us -> 12.8 us  [from_owner(): return lax.ppermute(x, ('groups', 'adapter'), pairs)]
    ppermute x1, starting transfers between devices: 2.13 us -> 0.78 us  [from_group(): return lax.ppermute(x, 'groups', [(0, 1), (1, 0)])]
  transfers between devices with their start and end apart: 15 -> 15, of which waited for: 6 -> 5; matrix products, arithmetic and copies ran while one was open for 0% -> 0% of each run, Pallas kernels for 34% -> 36%
where the time goes in v15:
time: 42.3 us; the launch traced here: 42.1 us
  starting transfers between devices  18 us (43%)
  Pallas kernels  15.5 us (37%)
  waiting for transfers between devices  7.63 us (18%)
  other arithmetic  0.87 us (2%)
    ppermute x7, starting transfers between devices, from_owner(): return lax.ppermute(x, ('groups', 'adapter'), pairs)  12.8 us
    pallas_call x4, Pallas kernels, base_part(): kernel_call(functools.partial(base_kernel, block, places, numbers, stream...  10.8 us
    ppermute x7, waiting for transfers between devices, from_tensor(): return lax.ppermute(x, 'tensor', [(s, s ^ m) for s in range(4)])  6.38 us
    ppermute x7, starting transfers between devices, from_tensor(): return lax.ppermute(x, 'tensor', [(s, s ^ m) for s in range(4)])  4.44 us
    pallas_call x1, Pallas kernels, paired(): kernel_call(functools.partial(cut_kernel, block, range(loads[1]), len(sma...  3.94 us
    ppermute x7, waiting for transfers between devices, from_owner(): return lax.ppermute(x, ('groups', 'adapter'), pairs)  1.25 us
  transfers between devices with their start and end apart: 15, of which 5 were waited for; matrix products, arithmetic and copies ran while one was open for 0% of the time, Pallas kernels for 36%

profile of v15, /device:TPU:0, one launch (start us, length us, event | category | flops | bytes accessed | tf_op | source)
XLA Modules:
  0.0 42.1 jit_solution(7464328288190239110)
XLA Ops:
  0.0 4.0 %collective-permute-start = (bf16[16,2048]{1,0:T(8,128)(2,1)}, bf16[16,2048]{1,0:T(8,128)(2,1)S(1)}, u32[]{:S(2)}, u32[]{:S(2)}) collective-permute-start(bf16[16,2048]{1,0:T(8,128)(2,1)} %refs_2_.1), channel_id=1, source_target_pairs={{0,8},{4,12},{8,0},{12,4},{16,24},{20,28},{24,16},{28,20},{1,9},{5... | collective-permute-start | bytes 196616 | tf_op jit(solution)/shard_map/ppermute | solution.py:221
  4.0 1.3 %collective-permute-start.1 = (bf16[16,2048]{1,0:T(8,128)(2,1)}, bf16[16,2048]{1,0:T(8,128)(2,1)S(1)}, u32[]{:S(2)}, u32[]{:S(2)}) collective-permute-start(bf16[16,2048]{1,0:T(8,128)(2,1)} %refs_2_.1), channel_id=1, source_target_pairs={{0,12},{4,8},{8,4},{12,0},{16,28},{20,24},{24,20},{28,16},{1,13},{... | collective-permute-start | bytes 196616 | tf_op jit(solution)/shard_map/ppermute | solution.py:221
  5.4 0.2 collective-permute-start.2
  5.6 3.9 %cut_expand.1 = (bf16[16,7168]{1,0:T(8,128)(2,1)S(1)}, bf16[16,7168]{1,0:T(8,128)(2,1)S(1)}, bf16[16,7168]{1,0:T(8,128)(2,1)S(1)}, s32[1,4]{1,0:T(1,128)S(1)}, s...) custom-call(bf16[1,16,28672]{2,1,0:T(8,128)(2,1)} %expand.1, ...), custom_call_target="tpu_custom_call" | custom-call | flops 1 | bytes 1 | tf_op jit(solution)/shard_map/cut_expand/pallas_call | solution.py:247
  9.6 2.9 %collective-permute-start.5 = (bf16[16,7168]{1,0:T(8,128)(2,1)S(1)}, bf16[16,7168]{1,0:T(8,128)(2,1)S(1)}, u32[]{:S(2)}, u32[]{:S(2)}) collective-permute-start(bf16[16,7168]{1,0:T(8,128)(2,1)S(1)} %get-tuple-element.52), channel_id=1, source_target_pairs={{0,8},{4,12},{8,0},{12,4},{16,28},{20,24},{24,20},{28,16},{1,9},{5... | collective-permute-start | bytes 688136 | tf_op jit(solution)/shard_map/ppermute | solution.py:221
  12.5 0.6 %collective-permute-start.8 = (bf16[16,7168]{1,0:T(8,128)(2,1)S(1)}, bf16[16,7168]{1,0:T(8,128)(2,1)S(1)}, u32[]{:S(2)}, u32[]{:S(2)}) collective-permute-start(bf16[16,7168]{1,0:T(8,128)(2,1)S(1)} %get-tuple-element.64), channel_id=1, source_target_pairs={{0,4},{4,0},{8,12},{12,8},{16,20},{20,16},{24,28},{28,24},{1,5},{5... | collective-permute-start | bytes 688136 | tf_op jit(solution)/shard_map/ppermute | solution.py:221
  13.1 0.0 collective-permute-done.refs_1_
  13.1 0.0 collective-permute-done.1.refs_2_
  13.1 0.0 collective-permute-done.2.refs_3_
  13.1 0.3 gather_rows.1
  13.4 0.1 collective-permute-start.3
  13.5 3.6 %base_part.4 = (f32[64,2048]{1,0:T(8,128)S(1)}, bf16[4,2048,512]{2,1,0:T(8,128)(2,1)S(1)}) custom-call(bf16[64,2048]{1,0:T(8,128)(2,1)S(1)} %get-tuple-element.44.rows, bf16[2048,7168]{1,0:T(8,128)(2,1)} %weight.9, bf16[4,2048,512]{2,1,0:T(8,128)(2,1)S(1)} %get-tuple-element.45.refs_0_, f32[32,64]{1,0:T(8,128)S(1)} %get-tuple-element.43.refs_1_), custom_call_target="tpu_custom_call" | custom-call | flops 1610612736 | bytes 25165824 | tf_op jit(solution)/shard_map/base_part/pallas_call | solution.py:298
  17.1 0.0 collective-permute-done.3
  17.1 1.6 %collective-permute-start.4 = (f32[16,64]{1,0:T(8,128)S(1)}, f32[16,64]{1,0:T(8,128)S(1)}, u32[]{:S(2)}, u32[]{:S(2)}) collective-permute-start(f32[16,64]{1,0:T(8,128)S(1)} %slice.16), channel_id=1, source_target_pairs={{0,2},{1,3},{2,0},{3,1},{4,6},{5,7},{6,4},{7,5},{8,10},{9,11},{10,... | collective-permute-start | bytes 12296 | tf_op jit(solution)/shard_map/ppermute | solution.py:224
  18.7 3.0 %base_part.5 = (f32[64,2048]{1,0:T(8,128)S(1)}, bf16[3,2048,512]{2,1,0:T(8,128)(2,1)S(1)}) custom-call(bf16[64,2048]{1,0:T(8,128)(2,1)S(1)} %get-tuple-element.44.rows, bf16[2048,7168]{1,0:T(8,128)(2,1)} %weight.9, bf16[4,2048,512]{2,1,0:T(8,128)(2,1)S(1)} %get-tuple-element.50.refs_0_, f32[32,64]{1,0:T(8,128)S(1)} %add.27.refs_1_), custom_call_target="tpu_custom_call" | custom-call | flops 1610612736 | bytes 25165824 | tf_op jit(solution)/shard_map/base_part/pallas_call | solution.py:298
  21.6 0.0 collective-permute-done.4
  21.6 0.7 %collective-permute-done.5.refs_2_.refs_6_ = bf16[16,7168]{1,0:T(8,128)(2,1)S(1)} collective-permute-done((bf16[16,7168]{1,0:T(8,128)(2,1)S(1)}, bf16[16,7168]{1,0:T(8,128)(2,1)S(1)}, u32[]{:S(2)}, u32[]{:S(2)}) %collective-permute-start.5) | collective-permute-done | bytes 229408 | tf_op jit(solution)/shard_map/ppermute | solution.py:221
  22.3 0.8 %collective-permute-start.9 = (bf16[16,7168]{1,0:T(8,128)(2,1)S(1)}, bf16[16,7168]{1,0:T(8,128)(2,1)S(1)}, u32[]{:S(2)}, u32[]{:S(2)}) collective-permute-start(bf16[16,7168]{1,0:T(8,128)(2,1)S(1)} %collective-permute-done.5.refs_2_.refs_6_), channel_id=1, source_target_pairs={{0,16},{16,0},{1,17},{17,1},{2,18},{18,2},{3,19},{19,3},{4,20},{20... | collective-permute-start | bytes 688136 | tf_op jit(solution)/shard_map/ppermute | solution.py:227
  23.1 1.6 %collective-permute-start.6 = (bf16[16,64]{1,0:T(8,128)(2,1)S(1)}, bf16[16,64]{1,0:T(8,128)(2,1)S(1)}, u32[]{:S(2)}, u32[]{:S(2)}) collective-permute-start(bf16[16,64]{1,0:T(8,128)(2,1)S(1)} %fusion.3.refs_1_), channel_id=1, source_target_pairs={{0,4},{4,0},{8,12},{12,8},{16,20},{20,16},{24,28},{28,24},{1,5},{5... | collective-permute-start | bytes 6152 | tf_op jit(solution)/shard_map/ppermute | solution.py:221
  24.7 2.2 %base_part.6 = (f32[64,1536]{1,0:T(8,128)S(1)}, bf16[2,2048,512]{2,1,0:T(8,128)(2,1)S(1)}) custom-call(bf16[64,2048]{1,0:T(8,128)(2,1)S(1)} %get-tuple-element.44.rows, bf16[2048,7168]{1,0:T(8,128)(2,1)} %weight.9, bf16[3,2048,512]{2,1,0:T(8,128)(2,1)S(1)} %get-tuple-element.55.refs_0_, bf16[16,64]{1,0:T(8,128)(2,1)S(1)} %fusion.3.refs_1_, ...), custom_call_target="tpu_custom_call" | custom-call | flops 1 | bytes 1 | tf_op jit(solution)/shard_map/base_part/pallas_call | solution.py:298
  27.0 0.0 collective-permute-done.6
  27.0 2.0 %collective-permute-start.7 = (bf16[16,64]{1,0:T(8,128)(2,1)S(1)}, bf16[16,64]{1,0:T(8,128)(2,1)S(1)}, u32[]{:S(2)}, u32[]{:S(2)}) collective-permute-start(bf16[16,64]{1,0:T(8,128)(2,1)S(1)} %add.29.refs_1_), channel_id=1, source_target_pairs={{0,8},{4,12},{8,0},{12,4},{16,24},{20,28},{24,16},{28,20},{1,9},{5... | collective-permute-start | bytes 6152 | tf_op jit(solution)/shard_map/ppermute | solution.py:221
  29.0 2.0 %base_part.7.refs_3_ = f32[64,1536]{1,0:T(8,128)S(1)} custom-call(bf16[64,2048]{1,0:T(8,128)(2,1)S(1)} %get-tuple-element.44.rows, bf16[2048,7168]{1,0:T(8,128)(2,1)} %weight.9, bf16[2,2048,512]{2,1,0:T(8,128)(2,1)S(1)} %get-tuple-element.60.refs_0_, bf16[16,64]{1,0:T(8,128)(2,1)S(1)} %add.29.refs_1_, bf16[16,7168]{1,0:T(8,128)(2,1)S(1)} %collective-permute-done.5.refs_2_.refs_6_), custom_call_target="tpu_custom_call" | custom-call | flops 1 | bytes 1 | tf_op jit(solution)/shard_map/base_part/pallas_call | solution.py:298
  31.1 0.5 %collective-permute-done.7 = bf16[16,64]{1,0:T(8,128)(2,1)S(1)} collective-permute-done((bf16[16,64]{1,0:T(8,128)(2,1)S(1)}, bf16[16,64]{1,0:T(8,128)(2,1)S(1)}, u32[]{:S(2)}, u32[]{:S(2)}) %collective-permute-start.7) | collective-permute-done | bytes 2080 | tf_op jit(solution)/shard_map/ppermute | solution.py:221
  31.6 0.0 collective-permute-done.8.refs_7_
  31.6 0.0 collective-permute-done.9.refs_8_
  31.6 0.5 %add_delta.1 = (f32[16,7168]{1,0:T(8,128)S(1)}, f32[16,7168]{1,0:T(8,128)S(1)}, f32[16,3584]{1,0:T(8,128)S(1)}, f32[16,3584]{1,0:T(8,128)S(1)}, f32[16,3584]{1,0:T(8,128)S(1)}, /*index=5*/f32[16,3584]{1,0:T(8,128)S(1)}) custom-call(s32[1,64]{1,0:T(1,128)S(1)} %get-tuple-element.42.slot, f32[64,2048]{1,0:T(8,128)S(1)} %get-tuple-element.47.refs_0_, ...), custom_call_target="tpu_custom_call" | custom-call | flops 1 | bytes 1 | tf_op jit(solution)/shard_map/add_delta/pallas_call | solution.py:335
  32.1 0.1 collective-permute-start.13
  32.2 0.5 %collective-permute-start.11 = (f32[16,3584]{1,0:T(8,128)S(1)}, f32[16,3584]{1,0:T(8,128)S(1)}, u32[]{:S(2)}, u32[]{:S(2)}) collective-permute-start(f32[16,3584]{1,0:T(8,128)S(1)} %get-tuple-element.68), channel_id=1, source_target_pairs={{0,1},{1,0},{2,3},{3,2},{4,5},{5,4},{6,7},{7,6},{8,9},{9,8},{10,11... | collective-permute-start | bytes 688136 | tf_op jit(solution)/shard_map/ppermute | solution.py:224
  32.7 0.1 collective-permute-start.10
  32.8 0.9 %collective-permute-done.13 = f32[16,3584]{1,0:T(8,128)S(1)} collective-permute-done((f32[16,3584]{1,0:T(8,128)S(1)}, f32[16,3584]{1,0:T(8,128)S(1)}, u32[]{:S(2)}, u32[]{:S(2)}) %collective-permute-start.13) | collective-permute-done | bytes 229408 | tf_op jit(solution)/shard_map/ppermute | solution.py:224
  33.7 1.2 %collective-permute-start.14 = (bf16[16,3584]{1,0:T(8,128)(2,1)S(1)}, bf16[16,3584]{1,0:T(8,128)(2,1)S(1)}, u32[]{:S(2)}, u32[]{:S(2)}) collective-permute-start(bf16[16,3584]{1,0:T(8,128)(2,1)S(1)} %add_convert_fusion), channel_id=1, source_target_pairs={{0,2},{1,3},{2,0},{3,1},{4,6},{5,7},{6,4},{7,5},{8,10},{9,11},{10,... | collective-permute-start | bytes 344072 | tf_op jit(solution)/shard_map/ppermute | solution.py:224
  34.9 0.0 collective-permute-done.11
  34.9 1.0 %collective-permute-start.12 = (bf16[16,3584]{1,0:T(8,128)(2,1)S(1)}, bf16[16,3584]{1,0:T(8,128)(2,1)S(1)}, u32[]{:S(2)}, u32[]{:S(2)}) collective-permute-start(bf16[16,3584]{1,0:T(8,128)(2,1)S(1)} %add_convert_fusion.1), channel_id=1, source_target_pairs={{0,2},{1,3},{2,0},{3,1},{4,6},{5,7},{6,4},{7,5},{8,10},{9,11},{10,... | collective-permute-start | bytes 344072 | tf_op jit(solution)/shard_map/ppermute | solution.py:224
  35.9 0.0 collective-permute-done.10
  35.9 3.8 %collective-permute-done.14 = bf16[16,3584]{1,0:T(8,128)(2,1)S(1)} collective-permute-done((bf16[16,3584]{1,0:T(8,128)(2,1)S(1)}, bf16[16,3584]{1,0:T(8,128)(2,1)S(1)}, u32[]{:S(2)}, u32[]{:S(2)}) %collective-permute-start.14) | collective-permute-done | bytes 114720 | tf_op jit(solution)/shard_map/ppermute | solution.py:224
  39.7 1.7 %collective-permute-done.12 = bf16[16,3584]{1,0:T(8,128)(2,1)S(1)} collective-permute-done((bf16[16,3584]{1,0:T(8,128)(2,1)S(1)}, bf16[16,3584]{1,0:T(8,128)(2,1)S(1)}, u32[]{:S(2)}, u32[]{:S(2)}) %collective-permute-start.12) | collective-permute-done | bytes 114720 | tf_op jit(solution)/shard_map/ppermute | solution.py:224
  41.4 0.7 %pad_maximum_fusion = bf16[16,7168]{1,0:T(8,128)(2,1)} fusion(bf16[16,3584]{1,0:T(8,128)(2,1)S(1)} %get-tuple-element.72, bf16[16,3584]{1,0:T(8,128)(2,1)S(1)} %get-tuple-element.71), kind=kLoop, calls=%fused_computation.4 | loop fusion | flops 458752 | bytes 458752 | tf_op jit(solution)/shard_map/concatenate | solution.py:356
  (9 shorter events, 0.2 us)
Async XLA Ops:
  0.0 13.1 %collective-permute-start = (bf16[16,2048]{1,0:T(8,128)(2,1)}, bf16[16,2048]{1,0:T(8,128)(2,1)S(1)}, u32[]{:S(2)}, u32[]{:S(2)}) collective-permute-start(bf16[16,2048]{1,0:T(8,128)(2,1)} %refs_2_.1), channel_id=1, source_target_pairs={{0,8},{4,12},{8,0},{12,4},{16,24},{20,28},{24,16},{28,20},{1,9},{5... | collective-permute-start | bytes 196616 | tf_op jit(solution)/shard_map/ppermute | solution.py:221
  4.0 9.1 %collective-permute-start.1 = (bf16[16,2048]{1,0:T(8,128)(2,1)}, bf16[16,2048]{1,0:T(8,128)(2,1)S(1)}, u32[]{:S(2)}, u32[]{:S(2)}) collective-permute-start(bf16[16,2048]{1,0:T(8,128)(2,1)} %refs_2_.1), channel_id=1, source_target_pairs={{0,12},{4,8},{8,4},{12,0},{16,28},{20,24},{24,20},{28,16},{1,13},{... | collective-permute-start | bytes 196616 | tf_op jit(solution)/shard_map/ppermute | solution.py:221
  5.4 7.7 %collective-permute-start.2 = (bf16[16,2048]{1,0:T(8,128)(2,1)}, bf16[16,2048]{1,0:T(8,128)(2,1)S(1)}, u32[]{:S(2)}, u32[]{:S(2)}) collective-permute-start(bf16[16,2048]{1,0:T(8,128)(2,1)} %refs_2_.1), channel_id=1, source_target_pairs={{0,4},{4,0},{8,12},{12,8},{16,20},{20,16},{24,28},{28,24},{1,5},{5... | collective-permute-start | bytes 196616 | tf_op jit(solution)/shard_map/ppermute | solution.py:221
  9.6 12.8 %collective-permute-start.5 = (bf16[16,7168]{1,0:T(8,128)(2,1)S(1)}, bf16[16,7168]{1,0:T(8,128)(2,1)S(1)}, u32[]{:S(2)}, u32[]{:S(2)}) collective-permute-start(bf16[16,7168]{1,0:T(8,128)(2,1)S(1)} %get-tuple-element.52), channel_id=1, source_target_pairs={{0,8},{4,12},{8,0},{12,4},{16,28},{20,24},{24,20},{28,16},{1,9},{5... | collective-permute-start | bytes 688136 | tf_op jit(solution)/shard_map/ppermute | solution.py:221
  12.5 19.1 %collective-permute-start.8 = (bf16[16,7168]{1,0:T(8,128)(2,1)S(1)}, bf16[16,7168]{1,0:T(8,128)(2,1)S(1)}, u32[]{:S(2)}, u32[]{:S(2)}) collective-permute-start(bf16[16,7168]{1,0:T(8,128)(2,1)S(1)} %get-tuple-element.64), channel_id=1, source_target_pairs={{0,4},{4,0},{8,12},{12,8},{16,20},{20,16},{24,28},{28,24},{1,5},{5... | collective-permute-start | bytes 688136 | tf_op jit(solution)/shard_map/ppermute | solution.py:221
  13.4 3.7 %collective-permute-start.3 = (f32[32,64]{1,0:T(8,128)S(1)}, f32[32,64]{1,0:T(8,128)S(1)}, u32[]{:S(2)}, u32[]{:S(2)}) collective-permute-start(f32[32,64]{1,0:T(8,128)S(1)} %get-tuple-element.43.refs_1_), channel_id=1, source_target_pairs={{0,1},{1,0},{2,3},{3,2},{4,5},{5,4},{6,7},{7,6},{8,9},{9,8},{10,11... | collective-permute-start | bytes 24584 | tf_op jit(solution)/shard_map/ppermute | solution.py:224
  17.1 4.5 %collective-permute-start.4 = (f32[16,64]{1,0:T(8,128)S(1)}, f32[16,64]{1,0:T(8,128)S(1)}, u32[]{:S(2)}, u32[]{:S(2)}) collective-permute-start(f32[16,64]{1,0:T(8,128)S(1)} %slice.16), channel_id=1, source_target_pairs={{0,2},{1,3},{2,0},{3,1},{4,6},{5,7},{6,4},{7,5},{8,10},{9,11},{10,... | collective-permute-start | bytes 12296 | tf_op jit(solution)/shard_map/ppermute | solution.py:224
  22.3 9.3 %collective-permute-start.9 = (bf16[16,7168]{1,0:T(8,128)(2,1)S(1)}, bf16[16,7168]{1,0:T(8,128)(2,1)S(1)}, u32[]{:S(2)}, u32[]{:S(2)}) collective-permute-start(bf16[16,7168]{1,0:T(8,128)(2,1)S(1)} %collective-permute-done.5.refs_2_.refs_6_), channel_id=1, source_target_pairs={{0,16},{16,0},{1,17},{17,1},{2,18},{18,2},{3,19},{19,3},{4,20},{20... | collective-permute-start | bytes 688136 | tf_op jit(solution)/shard_map/ppermute | solution.py:227
  23.1 3.9 %collective-permute-start.6 = (bf16[16,64]{1,0:T(8,128)(2,1)S(1)}, bf16[16,64]{1,0:T(8,128)(2,1)S(1)}, u32[]{:S(2)}, u32[]{:S(2)}) collective-permute-start(bf16[16,64]{1,0:T(8,128)(2,1)S(1)} %fusion.3.refs_1_), channel_id=1, source_target_pairs={{0,4},{4,0},{8,12},{12,8},{16,20},{20,16},{24,28},{28,24},{1,5},{5... | collective-permute-start | bytes 6152 | tf_op jit(solution)/shard_map/ppermute | solution.py:221
  27.0 4.6 %collective-permute-start.7 = (bf16[16,64]{1,0:T(8,128)(2,1)S(1)}, bf16[16,64]{1,0:T(8,128)(2,1)S(1)}, u32[]{:S(2)}, u32[]{:S(2)}) collective-permute-start(bf16[16,64]{1,0:T(8,128)(2,1)S(1)} %add.29.refs_1_), channel_id=1, source_target_pairs={{0,8},{4,12},{8,0},{12,4},{16,24},{20,28},{24,16},{28,20},{1,9},{5... | collective-permute-start | bytes 6152 | tf_op jit(solution)/shard_map/ppermute | solution.py:221
  32.1 1.6 %collective-permute-start.13 = (f32[16,3584]{1,0:T(8,128)S(1)}, f32[16,3584]{1,0:T(8,128)S(1)}, u32[]{:S(2)}, u32[]{:S(2)}) collective-permute-start(f32[16,3584]{1,0:T(8,128)S(1)} %get-tuple-element.70), channel_id=1, source_target_pairs={{0,1},{1,0},{2,3},{3,2},{4,5},{5,4},{6,7},{7,6},{8,9},{9,8},{10,11... | collective-permute-start | bytes 688136 | tf_op jit(solution)/shard_map/ppermute | solution.py:224
  32.2 2.7 %collective-permute-start.11 = (f32[16,3584]{1,0:T(8,128)S(1)}, f32[16,3584]{1,0:T(8,128)S(1)}, u32[]{:S(2)}, u32[]{:S(2)}) collective-permute-start(f32[16,3584]{1,0:T(8,128)S(1)} %get-tuple-element.68), channel_id=1, source_target_pairs={{0,1},{1,0},{2,3},{3,2},{4,5},{5,4},{6,7},{7,6},{8,9},{9,8},{10,11... | collective-permute-start | bytes 688136 | tf_op jit(solution)/shard_map/ppermute | solution.py:224
  32.7 3.2 %collective-permute-start.10 = (f32[16,7168]{1,0:T(8,128)S(1)}, f32[16,7168]{1,0:T(8,128)S(1)}, u32[]{:S(2)}, u32[]{:S(2)}) collective-permute-start(f32[16,7168]{1,0:T(8,128)S(1)} %get-tuple-element.66), channel_id=1, source_target_pairs={{0,1},{1,0},{2,3},{3,2},{4,5},{5,4},{6,7},{7,6},{8,9},{9,8},{10,11... | collective-permute-start | bytes 1376264 | tf_op jit(solution)/shard_map/ppermute | solution.py:224
  33.7 6.1 %collective-permute-start.14 = (bf16[16,3584]{1,0:T(8,128)(2,1)S(1)}, bf16[16,3584]{1,0:T(8,128)(2,1)S(1)}, u32[]{:S(2)}, u32[]{:S(2)}) collective-permute-start(bf16[16,3584]{1,0:T(8,128)(2,1)S(1)} %add_convert_fusion), channel_id=1, source_target_pairs={{0,2},{1,3},{2,0},{3,1},{4,6},{5,7},{6,4},{7,5},{8,10},{9,11},{10,... | collective-permute-start | bytes 344072 | tf_op jit(solution)/shard_map/ppermute | solution.py:224
  34.9 6.5 %collective-permute-start.12 = (bf16[16,3584]{1,0:T(8,128)(2,1)S(1)}, bf16[16,3584]{1,0:T(8,128)(2,1)S(1)}, u32[]{:S(2)}, u32[]{:S(2)}) collective-permute-start(bf16[16,3584]{1,0:T(8,128)(2,1)S(1)} %add_convert_fusion.1), channel_id=1, source_target_pairs={{0,2},{1,3},{2,0},{3,1},{4,6},{5,7},{6,4},{7,5},{8,10},{9,11},{10,... | collective-permute-start | bytes 344072 | tf_op jit(solution)/shard_map/ppermute | solution.py:224

commit v16 on v15

--- a/solution.py
+++ b/solution.py
@@ -127,9 +127,13 @@
         target[at : at + rank_block, :] = partial[pl.ds(start, rank_block), :]
 
 
-def base_kernel(block, places, numbers, streamed, rows, weight, *refs):
-    total, ahead, sem = refs[-3:]
-    copies = weight_copies(block, numbers, weight, ahead, sem)
+def base_kernel(block, places, numbers, rows, weight, *refs):
+    copies = []
+    if numbers:
+        total, ahead, sem = refs[-3:]
+        copies = weight_copies(block, numbers, weight, ahead, sem)
+    else:
+        total = refs[-1]
     for copy in copies:
         copy.start()
 
@@ -140,18 +144,11 @@
                 rows[...], refs[which][index], preferred_element_type=f32
             )
 
-    bands = sem.shape[1]
-    for n in range(len(numbers)):
-        for copy in copies[n * bands : (n + 1) * bands]:
-            copy.wait()
-        if streamed:
-            at = (len(places) + n) * block
-            total[:, at : at + block] = jnp.dot(
-                rows[...], ahead[n], preferred_element_type=f32
-            )
-
-
-def delta_kernel(block, splits, slot, *refs):
+    for copy in copies:
+        copy.wait()
+
+
+def delta_kernel(block, first, splits, slot, *refs):
     bases, refs = refs[: -len(splits) * 2 - 9], refs[-len(splits) * 2 - 9 :]
     own, shrunk, across, beside, swapped, own_keep, own_send = refs[:7]
     cross_keep, cross_send = refs[7 : 7 + len(splits)], refs[7 + len(splits) : 7 + 2 * len(splits)]
@@ -172,9 +169,9 @@
     at, split = 0, 0
     for base in bases:
         for column in range(0, base.shape[1], block):
-            span = slice(at, at + block)
+            span, there = slice(at, at + block), slice(first + at, first + at + block)
             expand = jnp.concatenate(
-                [own[:, span], across[:, span], beside[:, span], swapped[:, span]], axis=0
+                [piece[:, there] for piece in (own, across, beside, swapped)], axis=0
             )
             total = base[:, column : column + block] + jnp.dot(
                 left, expand, preferred_element_type=f32
@@ -231,10 +228,11 @@
     offsets = (2, 3, 1)
     blocks = [from_owner(tokens, j, j) for j in offsets]
 
-    cuts = [block_count * k // 14 for k in (0, 4, 8, 11, 14)]
+    cuts = [block_count * k // 14 for k in (0, 4, 8, 11, 12, 14)]
     parts = list(zip(cuts[:-1], cuts[1:]))
-    loads = [block_count * k // 14 for k in (0, 4, 8, 11, 13, 14)]
+    loads = [block_count * k // 14 for k in (0, 4, 8, 11, 13, 14, 14)]
     bands = 4
+    costs = (15 * 10**8, 15 * 10**8, 1, 1, 1)
     small = [
         pltpu.with_memory_space_constraint(x, pltpu.HBM)
         for x in (
@@ -285,28 +283,24 @@
 
     def base_part(n, *after):
         first, last = parts[n]
-        streamed = n + 1 == len(parts)
         numbers = range(loads[n + 1], loads[n + 2])
         places, used = [], []
-        for number in range(first, numbers[0] if streamed else last):
+        for number in range(first, last):
             source = max(k for k in range(len(loads) - 1) if loads[k] <= number)
             if source not in used:
                 used.append(source)
             places.append((used.index(source), number - loads[source]))
-        near = n < 2
-        ahead = pltpu.VMEM((len(numbers), depth, block), bf16)
         out = kernel_call(
-            functools.partial(base_kernel, block, places, numbers, streamed),
+            functools.partial(base_kernel, block, places, numbers),
             "base_part",
-            3 * 2 * row_count * depth * (last - first) * block if near else 1,
-            3 * 2 * depth * (last - first) * block if near else 1,
-            12,
+            costs[n],
+            1,
+            4,
             in_specs=[vmem, anywhere] + [vmem] * len(used) + [anywhere] * len(after),
-            out_specs=[vmem] * (1 if streamed else 2),
+            out_specs=[vmem] * (2 if numbers else 1),
             out_shape=[jax.ShapeDtypeStruct((row_count, (last - first) * block), f32)]
-            + ([] if streamed else [ahead]),
-            scratch_shapes=([ahead] if streamed else [])
-            + [pltpu.SemaphoreType.DMA((len(numbers), bands))],
+            + ([pltpu.VMEM((len(numbers), depth, block), bf16)] if numbers else []),
+            scratch_shapes=[pltpu.SemaphoreType.DMA((len(numbers), bands))] if numbers else [],
         )(rows, weight, *[loaded[k] for k in used], *after)
         loaded.append(out[-1])
         return out[0]
@@ -328,38 +322,53 @@
         bases.append(base)
         shrunk = shrunk + arrived
 
-    middle = block_count // 2 * block
-    splits = [(0, middle), (middle, columns)]
-    widths = [last - first for first, last in splits]
     quarter = row_count // 4
-    out = kernel_call(
-        functools.partial(delta_kernel, block, splits),
-        "add_delta",
-        1,
-        1,
-        8,
-        in_specs=[vmem] * (len(bases) + 6),
-        out_specs=[vmem] * (2 + 2 * len(splits)),
-        out_shape=[
-            jax.ShapeDtypeStruct((quarter, w), f32) for w in (columns, columns, *widths, *widths)
-        ],
-        scratch_shapes=[
-            pltpu.VMEM((row_count, rank_block * owner_count), f32),
-            pltpu.VMEM((row_count, rank_block * owner_count), bf16),
-        ],
-    )(slot, *bases, own, shrunk, across, beside, swapped)
-    own_keep, own_send = out[:2]
-    crossed = []
-    for keep, send in zip(out[2:4], out[4:6]):
-        crossed.append(from_tensor((keep + from_tensor(send, 1)).astype(bf16), 2))
-    kept = own_keep + from_tensor(own_send, 1)
-    return jnp.concatenate(
-        [
-            (kept[:, first:last] + part.astype(f32)).astype(bf16)
-            for (first, last), part in zip(splits, crossed)
-        ],
-        axis=1,
-    )
+
+    def delta_part(first, bases, splits):
+        width = splits[-1][1]
+        widths = [last - begin for begin, last in splits]
+        out = kernel_call(
+            functools.partial(delta_kernel, block, first * block, splits),
+            "add_delta",
+            1,
+            1,
+            8,
+            in_specs=[vmem] * (len(bases) + 6),
+            out_specs=[vmem] * (2 + 2 * len(splits)),
+            out_shape=[
+                jax.ShapeDtypeStruct((quarter, w), f32) for w in (width, width, *widths, *widths)
+            ],
+            scratch_shapes=[
+                pltpu.VMEM((row_count, rank_block * owner_count), f32),
+                pltpu.VMEM((row_count, rank_block * owner_count), bf16),
+            ],
+        )(slot, *bases, own, shrunk, across, beside, swapped)
+        return out[0], out[1], out[2 : 2 + len(splits)], out[2 + len(splits) :]
+
+    def finish(own_keep, own_send, cross_keep, arrived, splits, before=()):
+        crossed = [
+            from_tensor((keep + other).astype(bf16), 2) for keep, other in zip(cross_keep, arrived)
+        ]
+        *before, crossed[0] = lax.optimization_barrier((*before, crossed[0]))
+        kept = own_keep + from_tensor(own_send, 1)
+        return before + [
+            (kept[:, begin:last] + part.astype(f32)).astype(bf16)
+            for (begin, last), part in zip(splits, crossed)
+        ]
+
+    most = parts[-1][0]
+    middle = most // 2 * block
+    splits = [(0, middle), (middle, most * block)]
+    own_keep, own_send, cross_keep, cross_send = delta_part(0, bases, splits)
+    arrived = [from_tensor(x, 1) for x in cross_send]
+    last_base = base_part(4, cross_send[0])
+    *arrived, last_base = lax.optimization_barrier((*arrived, last_base))
+    pieces = finish(own_keep, own_send, cross_keep, arrived, splits)
+    splits = [(0, (block_count - most) * block)]
+    own_keep, own_send, cross_keep, cross_send = delta_part(most, [last_base], splits)
+    arrived = [from_tensor(x, 1) for x in cross_send]
+    pieces = finish(own_keep, own_send, cross_keep, arrived, splits, pieces)
+    return jnp.concatenate(pieces, axis=1)
 
 
 def on_device(tokens, base_up_weight, adapter_shrink_weight, adapter_expand_weight, *index):

time: 42.3 us -> 43.2 us (1.021)
  starting transfers between devices: 18 us -> 19.5 us
  waiting for transfers between devices: 7.63 us -> 6.33 us
  Pallas kernels: 15.5 us -> 16.1 us
    ppermute x7 -> x10, waiting for transfers between devices: 6.38 us -> 4.6 us  [from_tensor(): return lax.ppermute(x, 'tensor', [(s, s ^ m) for s in range(4)])]
    ppermute x7 -> x10, starting transfers between devices: 4.44 us -> 5.99 us  [from_tensor(): return lax.ppermute(x, 'tensor', [(s, s ^ m) for s in range(4)])]
    pallas_call x5 -> x7, Pallas kernels: 11.3 us -> 11.9 us  [the longest x5 11.2 us: base_part(): kernel_call(functools.partial(base_kernel, block, places, numbers), 'base...]
    ppermute x7, waiting for transfers between devices: 1.25 us -> 1.73 us  [from_owner(): return lax.ppermute(x, ('groups', 'adapter'), pairs)]
  transfers between devices with their start and end apart: 15 -> 18, of which waited for: 5 -> 6; matrix products, arithmetic and copies ran while one was open for 0% -> 0% of each run, Pallas kernels for 36% -> 36%
where the time goes in v16:
time: 43.2 us; the launch traced here: 43 us
  starting transfers between devices  19.5 us (45%)
  Pallas kernels  16.1 us (37%)
  waiting for transfers between devices  6.33 us (15%)
  other arithmetic  0.91 us (2%)
    ppermute x7, starting transfers between devices, from_owner(): return lax.ppermute(x, ('groups', 'adapter'), pairs)  12.8 us
    pallas_call x5, Pallas kernels, base_part(): kernel_call(functools.partial(base_kernel, block, places, numbers), 'base...  11.2 us
    ppermute x10, starting transfers between devices, from_tensor(): return lax.ppermute(x, 'tensor', [(s, s ^ m) for s in range(4)])  5.99 us
    ppermute x10, waiting for transfers between devices, from_tensor(): return lax.ppermute(x, 'tensor', [(s, s ^ m) for s in range(4)])  4.6 us
    pallas_call x1, Pallas kernels, paired(): kernel_call(functools.partial(cut_kernel, block, range(loads[1]), len(sma...  3.94 us
    ppermute x7, waiting for transfers between devices, from_owner(): return lax.ppermute(x, ('groups', 'adapter'), pairs)  1.73 us
  transfers between devices with their start and end apart: 18, of which 6 were waited for; matrix products, arithmetic and copies ran while one was open for 0% of the time, Pallas kernels for 36%

profile of v16, /device:TPU:0, one launch (start us, length us, event | category | flops | bytes accessed | tf_op | source)
XLA Modules:
  0.0 43.0 jit_solution(16228346756693842412)
XLA Ops:
  0.0 4.0 %collective-permute-start = (bf16[16,2048]{1,0:T(8,128)(2,1)}, bf16[16,2048]{1,0:T(8,128)(2,1)S(1)}, u32[]{:S(2)}, u32[]{:S(2)}) collective-permute-start(bf16[16,2048]{1,0:T(8,128)(2,1)} %refs_2_.1), channel_id=1, source_target_pairs={{0,8},{4,12},{8,0},{12,4},{16,24},{20,28},{24,16},{28,20},{1,9},{5... | collective-permute-start | bytes 196616 | tf_op jit(solution)/shard_map/ppermute | solution.py:218
  4.0 1.3 %collective-permute-start.1 = (bf16[16,2048]{1,0:T(8,128)(2,1)}, bf16[16,2048]{1,0:T(8,128)(2,1)S(1)}, u32[]{:S(2)}, u32[]{:S(2)}) collective-permute-start(bf16[16,2048]{1,0:T(8,128)(2,1)} %refs_2_.1), channel_id=1, source_target_pairs={{0,12},{4,8},{8,4},{12,0},{16,28},{20,24},{24,20},{28,16},{1,13},{... | collective-permute-start | bytes 196616 | tf_op jit(solution)/shard_map/ppermute | solution.py:218
  5.4 0.2 collective-permute-start.2
  5.6 3.9 %cut_expand.1 = (bf16[16,7168]{1,0:T(8,128)(2,1)S(1)}, bf16[16,7168]{1,0:T(8,128)(2,1)S(1)}, bf16[16,7168]{1,0:T(8,128)(2,1)S(1)}, s32[1,4]{1,0:T(1,128)S(1)}, s...) custom-call(bf16[1,16,28672]{2,1,0:T(8,128)(2,1)} %expand.1, ...), custom_call_target="tpu_custom_call" | custom-call | flops 1 | bytes 1 | tf_op jit(solution)/shard_map/cut_expand/pallas_call | solution.py:245
  9.6 2.9 %collective-permute-start.5 = (bf16[16,7168]{1,0:T(8,128)(2,1)S(1)}, bf16[16,7168]{1,0:T(8,128)(2,1)S(1)}, u32[]{:S(2)}, u32[]{:S(2)}) collective-permute-start(bf16[16,7168]{1,0:T(8,128)(2,1)S(1)} %get-tuple-element.64), channel_id=1, source_target_pairs={{0,8},{4,12},{8,0},{12,4},{16,28},{20,24},{24,20},{28,16},{1,9},{5... | collective-permute-start | bytes 688136 | tf_op jit(solution)/shard_map/ppermute | solution.py:218
  12.5 0.6 %collective-permute-start.8 = (bf16[16,7168]{1,0:T(8,128)(2,1)S(1)}, bf16[16,7168]{1,0:T(8,128)(2,1)S(1)}, u32[]{:S(2)}, u32[]{:S(2)}) collective-permute-start(bf16[16,7168]{1,0:T(8,128)(2,1)S(1)} %get-tuple-element.77), channel_id=1, source_target_pairs={{0,4},{4,0},{8,12},{12,8},{16,20},{20,16},{24,28},{28,24},{1,5},{5... | collective-permute-start | bytes 688136 | tf_op jit(solution)/shard_map/ppermute | solution.py:218
  13.1 0.0 collective-permute-done.refs_1_
  13.1 0.0 collective-permute-done.1.refs_2_
  13.1 0.0 collective-permute-done.2.refs_3_
  13.1 0.3 gather_rows.1
  13.4 0.1 collective-permute-start.3
  13.5 3.6 %base_part.5 = (f32[64,2048]{1,0:T(8,128)S(1)}, bf16[4,2048,512]{2,1,0:T(8,128)(2,1)S(1)}) custom-call(bf16[64,2048]{1,0:T(8,128)(2,1)S(1)} %get-tuple-element.56.rows, bf16[2048,7168]{1,0:T(8,128)(2,1)} %weight.11, bf16[4,2048,512]{2,1,0:T(8,128)(2,1)S(1)} %get-tuple-element.57.refs_0_, f32[32,64]{1,0:T(8,128)S(1)} %get-tuple-element.55.refs_1_), custom_call_target="tpu_custom_call" | custom-call | flops 1500000000 | bytes 1 | tf_op jit(solution)/shard_map/base_part/pallas_call | solution.py:293
  17.1 0.0 collective-permute-done.3
  17.1 1.6 %collective-permute-start.4 = (f32[16,64]{1,0:T(8,128)S(1)}, f32[16,64]{1,0:T(8,128)S(1)}, u32[]{:S(2)}, u32[]{:S(2)}) collective-permute-start(f32[16,64]{1,0:T(8,128)S(1)} %slice.16), channel_id=1, source_target_pairs={{0,2},{1,3},{2,0},{3,1},{4,6},{5,7},{6,4},{7,5},{8,10},{9,11},{10,... | collective-permute-start | bytes 12296 | tf_op jit(solution)/shard_map/ppermute | solution.py:221
  18.7 3.0 %base_part.6 = (f32[64,2048]{1,0:T(8,128)S(1)}, bf16[3,2048,512]{2,1,0:T(8,128)(2,1)S(1)}) custom-call(bf16[64,2048]{1,0:T(8,128)(2,1)S(1)} %get-tuple-element.56.rows, bf16[2048,7168]{1,0:T(8,128)(2,1)} %weight.11, bf16[4,2048,512]{2,1,0:T(8,128)(2,1)S(1)} %get-tuple-element.62.refs_0_, f32[32,64]{1,0:T(8,128)S(1)} %add.36.refs_1_), custom_call_target="tpu_custom_call" | custom-call | flops 1500000000 | bytes 1 | tf_op jit(solution)/shard_map/base_part/pallas_call | solution.py:293
  21.6 0.0 collective-permute-done.4
  21.6 0.7 %collective-permute-done.5.refs_2_.refs_6_.refs_3_ = bf16[16,7168]{1,0:T(8,128)(2,1)S(1)} collective-permute-done((bf16[16,7168]{1,0:T(8,128)(2,1)S(1)}, bf16[16,7168]{1,0:T(8,128)(2,1)S(1)}, u32[]{:S(2)}, u32[]{:S(2)}) %collective-permute-start.5) | collective-permute-done | bytes 229408 | tf_op jit(solution)/shard_map/ppermute | solution.py:218
  22.3 0.8 %collective-permute-start.9 = (bf16[16,7168]{1,0:T(8,128)(2,1)S(1)}, bf16[16,7168]{1,0:T(8,128)(2,1)S(1)}, u32[]{:S(2)}, u32[]{:S(2)}) collective-permute-start(bf16[16,7168]{1,0:T(8,128)(2,1)S(1)} %collective-permute-done.5.refs_2_.refs_6_.refs_3_), channel_id=1, source_target_pairs={{0,16},{16,0},{1,17},{17,1},{2,18},{18,2},{3,19},{19,3},{4,20},{20... | collective-permute-start | bytes 688136 | tf_op jit(solution)/shard_map/ppermute | solution.py:224
  23.1 1.6 %collective-permute-start.6 = (bf16[16,64]{1,0:T(8,128)(2,1)S(1)}, bf16[16,64]{1,0:T(8,128)(2,1)S(1)}, u32[]{:S(2)}, u32[]{:S(2)}) collective-permute-start(bf16[16,64]{1,0:T(8,128)(2,1)S(1)} %fusion.3.refs_1_), channel_id=1, source_target_pairs={{0,4},{4,0},{8,12},{12,8},{16,20},{20,16},{24,28},{28,24},{1,5},{5... | collective-permute-start | bytes 6152 | tf_op jit(solution)/shard_map/ppermute | solution.py:218
  24.7 2.2 %base_part.7 = (f32[64,1536]{1,0:T(8,128)S(1)}, bf16[2,2048,512]{2,1,0:T(8,128)(2,1)S(1)}) custom-call(bf16[64,2048]{1,0:T(8,128)(2,1)S(1)} %get-tuple-element.56.rows, bf16[2048,7168]{1,0:T(8,128)(2,1)} %weight.11, bf16[3,2048,512]{2,1,0:T(8,128)(2,1)S(1)} %get-tuple-element.67.refs_0_, bf16[16,64]{1,0:T(8,128)(2,1)S(1)} %fusion.3.refs_1_, ...), custom_call_target="tpu_custom_call" | custom-call | flops 1 | bytes 1 | tf_op jit(solution)/shard_map/base_part/pallas_call | solution.py:293
  27.0 0.0 collective-permute-done.6
  27.0 2.0 %collective-permute-start.7 = (bf16[16,64]{1,0:T(8,128)(2,1)S(1)}, bf16[16,64]{1,0:T(8,128)(2,1)S(1)}, u32[]{:S(2)}, u32[]{:S(2)}) collective-permute-start(bf16[16,64]{1,0:T(8,128)(2,1)S(1)} %add.38.refs_1_), channel_id=1, source_target_pairs={{0,8},{4,12},{8,0},{12,4},{16,24},{20,28},{24,16},{28,20},{1,9},{5... | collective-permute-start | bytes 6152 | tf_op jit(solution)/shard_map/ppermute | solution.py:218
  29.0 1.6 %base_part.8 = (f32[64,512]{1,0:T(8,128)S(1)}, bf16[1,2048,512]{2,1,0:T(8,128)(2,1)S(1)}) custom-call(bf16[64,2048]{1,0:T(8,128)(2,1)S(1)} %get-tuple-element.56.rows, bf16[2048,7168]{1,0:T(8,128)(2,1)} %weight.11, bf16[2,2048,512]{2,1,0:T(8,128)(2,1)S(1)} %get-tuple-element.72.refs_0_, bf16[16,64]{1,0:T(8,128)(2,1)S(1)} %add.38.refs_1_, ...), custom_call_target="tpu_custom_call" | custom-call | flops 1 | bytes 1 | tf_op jit(solution)/shard_map/base_part/pallas_call | solution.py:293
  30.6 1.0 %collective-permute-done.7 = bf16[16,64]{1,0:T(8,128)(2,1)S(1)} collective-permute-done((bf16[16,64]{1,0:T(8,128)(2,1)S(1)}, bf16[16,64]{1,0:T(8,128)(2,1)S(1)}, u32[]{:S(2)}, u32[]{:S(2)}) %collective-permute-start.7) | collective-permute-done | bytes 2080 | tf_op jit(solution)/shard_map/ppermute | solution.py:218
  31.6 0.0 collective-permute-done.8.refs_7_.refs_4_
  31.6 0.0 collective-permute-done.9.refs_8_.refs_5_
  31.6 0.4 %add_delta.2 = (f32[16,6144]{1,0:T(8,128)S(1)}, f32[16,6144]{1,0:T(8,128)S(1)}, f32[16,3072]{1,0:T(8,128)S(1)}, f32[16,3072]{1,0:T(8,128)S(1)}, f32[16,3072]{1,0:T(8,128)S(1)}, /*index=5*/f32[16,3072]{1,0:T(8,128)S(1)}) custom-call(s32[1,64]{1,0:T(1,128)S(1)} %get-tuple-element.54.slot, f32[64,2048]{1,0:T(8,128)S(1)} %get-tuple-element.59.refs_0_, ...), custom_call_target="tpu_custom_call" | custom-call | flops 1 | bytes 1 | tf_op jit(solution)/shard_map/add_delta/pallas_call | solution.py:330
  32.1 0.1 collective-permute-start.11
  32.1 0.5 %collective-permute-start.12 = (f32[16,3072]{1,0:T(8,128)S(1)}, f32[16,3072]{1,0:T(8,128)S(1)}, u32[]{:S(2)}, u32[]{:S(2)}) collective-permute-start(f32[16,3072]{1,0:T(8,128)S(1)} %get-tuple-element.82), channel_id=1, source_target_pairs={{0,1},{1,0},{2,3},{3,2},{4,5},{5,4},{6,7},{7,6},{8,9},{9,8},{10,11... | collective-permute-start | bytes 589832 | tf_op jit(solution)/shard_map/ppermute | solution.py:221
  32.6 0.8 %base_part.9.refs_0_ = f32[64,1024]{1,0:T(8,128)S(1)} custom-call(bf16[64,2048]{1,0:T(8,128)(2,1)S(1)} %get-tuple-element.56.rows, bf16[2048,7168]{1,0:T(8,128)(2,1)} %weight.11, bf16[2,2048,512]{2,1,0:T(8,128)(2,1)S(1)} %get-tuple-element.72.refs_0_, bf16[1,2048,512]{2,1,0:T(8,128)(2,1)S(1)} %get-tuple-element.83.refs_1_, ...), custom_call_target="tpu_custom_call" | custom-call | flops 1 | bytes 1 | tf_op jit(solution)/shard_map/base_part/pallas_call | solution.py:293
  33.5 0.1 collective-permute-start.10
  33.6 0.0 collective-permute-done.11
  33.6 0.2 collective-permute-done.12
  33.9 0.3 add_delta.3
  34.1 0.3 collective-permute-start.15
  34.4 1.2 %collective-permute-start.13 = (bf16[16,3072]{1,0:T(8,128)(2,1)S(1)}, bf16[16,3072]{1,0:T(8,128)(2,1)S(1)}, u32[]{:S(2)}, u32[]{:S(2)}) collective-permute-start(bf16[16,3072]{1,0:T(8,128)(2,1)S(1)} %add_convert_fusion.1), channel_id=1, source_target_pairs={{0,2},{1,3},{2,0},{3,1},{4,6},{5,7},{6,4},{7,5},{8,10},{9,11},{10,... | collective-permute-start | bytes 294920 | tf_op jit(solution)/shard_map/ppermute | solution.py:221
  35.7 1.0 %collective-permute-start.14 = (bf16[16,3072]{1,0:T(8,128)(2,1)S(1)}, bf16[16,3072]{1,0:T(8,128)(2,1)S(1)}, u32[]{:S(2)}, u32[]{:S(2)}) collective-permute-start(bf16[16,3072]{1,0:T(8,128)(2,1)S(1)} %add_convert_fusion), channel_id=1, source_target_pairs={{0,2},{1,3},{2,0},{3,1},{4,6},{5,7},{6,4},{7,5},{8,10},{9,11},{10,... | collective-permute-start | bytes 294920 | tf_op jit(solution)/shard_map/ppermute | solution.py:221
  36.6 0.0 collective-permute-start.17
  36.6 0.0 collective-permute-done.15
  36.6 1.2 %collective-permute-start.16 = (bf16[16,1024]{1,0:T(8,128)(2,1)S(1)}, bf16[16,1024]{1,0:T(8,128)(2,1)S(1)}, u32[]{:S(2)}, u32[]{:S(2)}) collective-permute-start(bf16[16,1024]{1,0:T(8,128)(2,1)S(1)} %add_convert_fusion.3), channel_id=1, source_target_pairs={{0,2},{1,3},{2,0},{3,1},{4,6},{5,7},{6,4},{7,5},{8,10},{9,11},{10,... | collective-permute-start | bytes 98312 | tf_op jit(solution)/shard_map/ppermute | solution.py:221
  37.8 2.3 %collective-permute-done.13 = bf16[16,3072]{1,0:T(8,128)(2,1)S(1)} collective-permute-done((bf16[16,3072]{1,0:T(8,128)(2,1)S(1)}, bf16[16,3072]{1,0:T(8,128)(2,1)S(1)}, u32[]{:S(2)}, u32[]{:S(2)}) %collective-permute-start.13) | collective-permute-done | bytes 98336 | tf_op jit(solution)/shard_map/ppermute | solution.py:221
  40.1 0.0 collective-permute-done.10
  40.1 0.1 add.40
  40.2 1.8 %collective-permute-done.14 = bf16[16,3072]{1,0:T(8,128)(2,1)S(1)} collective-permute-done((bf16[16,3072]{1,0:T(8,128)(2,1)S(1)}, bf16[16,3072]{1,0:T(8,128)(2,1)S(1)}, u32[]{:S(2)}, u32[]{:S(2)}) %collective-permute-start.14) | collective-permute-done | bytes 98336 | tf_op jit(solution)/shard_map/ppermute | solution.py:221
  42.0 0.3 collective-permute-done.16
  42.3 0.0 collective-permute-done.17
  42.3 0.7 %pad_maximum_fusion = bf16[16,7168]{1,0:T(8,128)(2,1)} fusion(bf16[16,1024]{1,0:T(8,128)(2,1)S(1)} %add_convert_fusion.2, bf16[16,3072]{1,0:T(8,128)(2,1)S(1)} %get-tuple-element.91, bf16[16,3072]{1,0:T(8,128)(2,1)S(1)} %get-tuple-element.90), kind=kLoop, calls=%fused_computation | loop fusion | flops 688128 | bytes 458752 | tf_op jit(solution)/shard_map/concatenate | solution.py:371
  (10 shorter events, 0.2 us)
Async XLA Ops:
  0.0 13.1 %collective-permute-start = (bf16[16,2048]{1,0:T(8,128)(2,1)}, bf16[16,2048]{1,0:T(8,128)(2,1)S(1)}, u32[]{:S(2)}, u32[]{:S(2)}) collective-permute-start(bf16[16,2048]{1,0:T(8,128)(2,1)} %refs_2_.1), channel_id=1, source_target_pairs={{0,8},{4,12},{8,0},{12,4},{16,24},{20,28},{24,16},{28,20},{1,9},{5... | collective-permute-start | bytes 196616 | tf_op jit(solution)/shard_map/ppermute | solution.py:218
  4.0 9.1 %collective-permute-start.1 = (bf16[16,2048]{1,0:T(8,128)(2,1)}, bf16[16,2048]{1,0:T(8,128)(2,1)S(1)}, u32[]{:S(2)}, u32[]{:S(2)}) collective-permute-start(bf16[16,2048]{1,0:T(8,128)(2,1)} %refs_2_.1), channel_id=1, source_target_pairs={{0,12},{4,8},{8,4},{12,0},{16,28},{20,24},{24,20},{28,16},{1,13},{... | collective-permute-start | bytes 196616 | tf_op jit(solution)/shard_map/ppermute | solution.py:218
  5.4 7.7 %collective-permute-start.2 = (bf16[16,2048]{1,0:T(8,128)(2,1)}, bf16[16,2048]{1,0:T(8,128)(2,1)S(1)}, u32[]{:S(2)}, u32[]{:S(2)}) collective-permute-start(bf16[16,2048]{1,0:T(8,128)(2,1)} %refs_2_.1), channel_id=1, source_target_pairs={{0,4},{4,0},{8,12},{12,8},{16,20},{20,16},{24,28},{28,24},{1,5},{5... | collective-permute-start | bytes 196616 | tf_op jit(solution)/shard_map/ppermute | solution.py:218
  9.6 12.8 %collective-permute-start.5 = (bf16[16,7168]{1,0:T(8,128)(2,1)S(1)}, bf16[16,7168]{1,0:T(8,128)(2,1)S(1)}, u32[]{:S(2)}, u32[]{:S(2)}) collective-permute-start(bf16[16,7168]{1,0:T(8,128)(2,1)S(1)} %get-tuple-element.64), channel_id=1, source_target_pairs={{0,8},{4,12},{8,0},{12,4},{16,28},{20,24},{24,20},{28,16},{1,9},{5... | collective-permute-start | bytes 688136 | tf_op jit(solution)/shard_map/ppermute | solution.py:218
  12.5 19.1 %collective-permute-start.8 = (bf16[16,7168]{1,0:T(8,128)(2,1)S(1)}, bf16[16,7168]{1,0:T(8,128)(2,1)S(1)}, u32[]{:S(2)}, u32[]{:S(2)}) collective-permute-start(bf16[16,7168]{1,0:T(8,128)(2,1)S(1)} %get-tuple-element.77), channel_id=1, source_target_pairs={{0,4},{4,0},{8,12},{12,8},{16,20},{20,16},{24,28},{28,24},{1,5},{5... | collective-permute-start | bytes 688136 | tf_op jit(solution)/shard_map/ppermute | solution.py:218
  13.4 3.7 %collective-permute-start.3 = (f32[32,64]{1,0:T(8,128)S(1)}, f32[32,64]{1,0:T(8,128)S(1)}, u32[]{:S(2)}, u32[]{:S(2)}) collective-permute-start(f32[32,64]{1,0:T(8,128)S(1)} %get-tuple-element.55.refs_1_), channel_id=1, source_target_pairs={{0,1},{1,0},{2,3},{3,2},{4,5},{5,4},{6,7},{7,6},{8,9},{9,8},{10,11... | collective-permute-start | bytes 24584 | tf_op jit(solution)/shard_map/ppermute | solution.py:221
  17.1 4.5 %collective-permute-start.4 = (f32[16,64]{1,0:T(8,128)S(1)}, f32[16,64]{1,0:T(8,128)S(1)}, u32[]{:S(2)}, u32[]{:S(2)}) collective-permute-start(f32[16,64]{1,0:T(8,128)S(1)} %slice.16), channel_id=1, source_target_pairs={{0,2},{1,3},{2,0},{3,1},{4,6},{5,7},{6,4},{7,5},{8,10},{9,11},{10,... | collective-permute-start | bytes 12296 | tf_op jit(solution)/shard_map/ppermute | solution.py:221
  22.3 9.3 %collective-permute-start.9 = (bf16[16,7168]{1,0:T(8,128)(2,1)S(1)}, bf16[16,7168]{1,0:T(8,128)(2,1)S(1)}, u32[]{:S(2)}, u32[]{:S(2)}) collective-permute-start(bf16[16,7168]{1,0:T(8,128)(2,1)S(1)} %collective-permute-done.5.refs_2_.refs_6_.refs_3_), channel_id=1, source_target_pairs={{0,16},{16,0},{1,17},{17,1},{2,18},{18,2},{3,19},{19,3},{4,20},{20... | collective-permute-start | bytes 688136 | tf_op jit(solution)/shard_map/ppermute | solution.py:224
  23.1 3.9 %collective-permute-start.6 = (bf16[16,64]{1,0:T(8,128)(2,1)S(1)}, bf16[16,64]{1,0:T(8,128)(2,1)S(1)}, u32[]{:S(2)}, u32[]{:S(2)}) collective-permute-start(bf16[16,64]{1,0:T(8,128)(2,1)S(1)} %fusion.3.refs_1_), channel_id=1, source_target_pairs={{0,4},{4,0},{8,12},{12,8},{16,20},{20,16},{24,28},{28,24},{1,5},{5... | collective-permute-start | bytes 6152 | tf_op jit(solution)/shard_map/ppermute | solution.py:218
  27.0 4.6 %collective-permute-start.7 = (bf16[16,64]{1,0:T(8,128)(2,1)S(1)}, bf16[16,64]{1,0:T(8,128)(2,1)S(1)}, u32[]{:S(2)}, u32[]{:S(2)}) collective-permute-start(bf16[16,64]{1,0:T(8,128)(2,1)S(1)} %add.38.refs_1_), channel_id=1, source_target_pairs={{0,8},{4,12},{8,0},{12,4},{16,24},{20,28},{24,16},{28,20},{1,9},{5... | collective-permute-start | bytes 6152 | tf_op jit(solution)/shard_map/ppermute | solution.py:218
  32.1 1.6 %collective-permute-start.11 = (f32[16,3072]{1,0:T(8,128)S(1)}, f32[16,3072]{1,0:T(8,128)S(1)}, u32[]{:S(2)}, u32[]{:S(2)}) collective-permute-start(f32[16,3072]{1,0:T(8,128)S(1)} %get-tuple-element.81.refs_2_), channel_id=1, source_target_pairs={{0,1},{1,0},{2,3},{3,2},{4,5},{5,4},{6,7},{7,6},{8,9},{9,8},{10,11... | collective-permute-start | bytes 589832 | tf_op jit(solution)/shard_map/ppermute | solution.py:221
  32.1 1.7 %collective-permute-start.12 = (f32[16,3072]{1,0:T(8,128)S(1)}, f32[16,3072]{1,0:T(8,128)S(1)}, u32[]{:S(2)}, u32[]{:S(2)}) collective-permute-start(f32[16,3072]{1,0:T(8,128)S(1)} %get-tuple-element.82), channel_id=1, source_target_pairs={{0,1},{1,0},{2,3},{3,2},{4,5},{5,4},{6,7},{7,6},{8,9},{9,8},{10,11... | collective-permute-start | bytes 589832 | tf_op jit(solution)/shard_map/ppermute | solution.py:221
  33.5 6.7 %collective-permute-start.10 = (f32[16,6144]{1,0:T(8,128)S(1)}, f32[16,6144]{1,0:T(8,128)S(1)}, u32[]{:S(2)}, u32[]{:S(2)}) collective-permute-start(f32[16,6144]{1,0:T(8,128)S(1)} %get-tuple-element.79), channel_id=1, source_target_pairs={{0,1},{1,0},{2,3},{3,2},{4,5},{5,4},{6,7},{7,6},{8,9},{9,8},{10,11... | collective-permute-start | bytes 1179656 | tf_op jit(solution)/shard_map/ppermute | solution.py:221
  34.1 2.5 %collective-permute-start.15 = (f32[16,1024]{1,0:T(8,128)S(1)}, f32[16,1024]{1,0:T(8,128)S(1)}, u32[]{:S(2)}, u32[]{:S(2)}) collective-permute-start(f32[16,1024]{1,0:T(8,128)S(1)} %get-tuple-element.89), channel_id=1, source_target_pairs={{0,1},{1,0},{2,3},{3,2},{4,5},{5,4},{6,7},{7,6},{8,9},{9,8},{10,11... | collective-permute-start | bytes 196616 | tf_op jit(solution)/shard_map/ppermute | solution.py:221
  34.4 5.7 %collective-permute-start.13 = (bf16[16,3072]{1,0:T(8,128)(2,1)S(1)}, bf16[16,3072]{1,0:T(8,128)(2,1)S(1)}, u32[]{:S(2)}, u32[]{:S(2)}) collective-permute-start(bf16[16,3072]{1,0:T(8,128)(2,1)S(1)} %add_convert_fusion.1), channel_id=1, source_target_pairs={{0,2},{1,3},{2,0},{3,1},{4,6},{5,7},{6,4},{7,5},{8,10},{9,11},{10,... | collective-permute-start | bytes 294920 | tf_op jit(solution)/shard_map/ppermute | solution.py:221
  35.7 6.3 %collective-permute-start.14 = (bf16[16,3072]{1,0:T(8,128)(2,1)S(1)}, bf16[16,3072]{1,0:T(8,128)(2,1)S(1)}, u32[]{:S(2)}, u32[]{:S(2)}) collective-permute-start(bf16[16,3072]{1,0:T(8,128)(2,1)S(1)} %add_convert_fusion), channel_id=1, source_target_pairs={{0,2},{1,3},{2,0},{3,1},{4,6},{5,7},{6,4},{7,5},{8,10},{9,11},{10,... | collective-permute-start | bytes 294920 | tf_op jit(solution)/shard_map/ppermute | solution.py:221
  36.6 5.7 %collective-permute-start.17 = (f32[16,1024]{1,0:T(8,128)S(1)}, f32[16,1024]{1,0:T(8,128)S(1)}, u32[]{:S(2)}, u32[]{:S(2)}) collective-permute-start(f32[16,1024]{1,0:T(8,128)S(1)} %get-tuple-element.93), channel_id=1, source_target_pairs={{0,1},{1,0},{2,3},{3,2},{4,5},{5,4},{6,7},{7,6},{8,9},{9,8},{10,11... | collective-permute-start | bytes 196616 | tf_op jit(solution)/shard_map/ppermute | solution.py:221
  36.6 5.6 %collective-permute-start.16 = (bf16[16,1024]{1,0:T(8,128)(2,1)S(1)}, bf16[16,1024]{1,0:T(8,128)(2,1)S(1)}, u32[]{:S(2)}, u32[]{:S(2)}) collective-permute-start(bf16[16,1024]{1,0:T(8,128)(2,1)S(1)} %add_convert_fusion.3), channel_id=1, source_target_pairs={{0,2},{1,3},{2,0},{3,1},{4,6},{5,7},{6,4},{7,5},{8,10},{9,11},{10,... | collective-permute-start | bytes 98312 | tf_op jit(solution)/shard_map/ppermute | solution.py:221

commit v17 on v15

--- a/solution.py
+++ b/solution.py
@@ -100,7 +100,7 @@
 def gather_kernel(offsets, slots, index, *refs):
     owner_count = len(offsets)
     blocks = refs[:owner_count]
-    shrink, rows_out, keep, send, slot_out, rows, partial = refs[owner_count:]
+    shrink, rows_out, *parts_out, slot_out, rows, partial = refs[owner_count:]
     a, t = lax.axis_index("adapter"), lax.axis_index("tensor")
     height, depth = blocks[0].shape
     for j, part in zip(offsets, blocks):
@@ -120,11 +120,9 @@
     slot_out[...] = slot
     partial[...] = jnp.where(slot == a, product, 0.0)
     rank_block = partial.shape[0] // 4
-    for i, flip in enumerate((0, 2, 1, 3)):
+    for flip, part in enumerate(parts_out):
         start = pl.multiple_of(lax.bitwise_xor(t, flip) * rank_block, rank_block)
-        target = keep if i < 2 else send
-        at = i % 2 * rank_block
-        target[at : at + rank_block, :] = partial[pl.ds(start, rank_block), :]
+        part[...] = partial[pl.ds(start, rank_block), :]
 
 
 def base_kernel(block, places, numbers, streamed, rows, weight, *refs):
@@ -263,16 +261,16 @@
     loaded = [held]
     across, beside = from_owner(across, 2, 3), from_owner(beside, 1, 1)
 
-    rows, keep, send, slot = kernel_call(
+    rows, *mine_parts, slot = kernel_call(
         functools.partial(gather_kernel, (0, *offsets)),
         "gather_rows",
         1,
         1,
         4,
         in_specs=[vmem] * (owner_count + 3),
-        out_specs=[vmem] * 4,
+        out_specs=[vmem] * 6,
         out_shape=[jax.ShapeDtypeStruct((row_count, depth), bf16)]
-        + [jax.ShapeDtypeStruct((rank // 2, row_count), f32)] * 2
+        + [jax.ShapeDtypeStruct((rank_block, row_count), f32)] * 4
         + [jax.ShapeDtypeStruct((1, row_count), jnp.int32)],
         scratch_shapes=[pltpu.VMEM((row_count, depth), bf16), pltpu.VMEM((rank, row_count), f32)],
     )(
@@ -311,22 +309,18 @@
         loaded.append(out[-1])
         return out[0]
 
-    arrived = from_tensor(send, 1)
-    base_0 = base_part(0, send)
-    arrived, base_0 = lax.optimization_barrier((arrived, base_0))
-    pair = keep + arrived
-    arrived = from_tensor(pair[rank_block:], 2)
-    base_1 = base_part(1, pair)
-    arrived, base_1, across = lax.optimization_barrier((arrived, base_1, across))
-    shrunk = (adapter_scale * (pair[:rank_block] + arrived)).astype(bf16)
+    arrived = [from_tensor(mine_parts[m], m) for m in (1, 2, 3)]
+    bases = [base_part(0, *mine_parts[1:])]
+    bases.append(base_part(1, bases[0]))
+    *arrived, across, bases[1] = lax.optimization_barrier((*arrived, across, bases[1]))
     swapped = from_group(across)
-    bases = [base_0, base_1]
-    for m, n in ((1, 2), (2, 3)):
-        arrived = from_owner(shrunk, m, m)
-        base = base_part(n, shrunk, across)
-        arrived, base = lax.optimization_barrier((arrived, base))
-        bases.append(base)
-        shrunk = shrunk + arrived
+    shrunk = adapter_scale * (mine_parts[0] + arrived[0] + arrived[1] + arrived[2])
+    shrunk = shrunk.astype(bf16)
+    arrived = [from_owner(shrunk, m, m) for m in (1, 2, 3)]
+    bases.append(base_part(2, shrunk, across))
+    bases.append(base_part(3, bases[2]))
+    *arrived, bases[3] = lax.optimization_barrier((*arrived, bases[3]))
+    shrunk = shrunk + arrived[0] + arrived[1] + arrived[2]
 
     middle = block_count // 2 * block
     splits = [(0, middle), (middle, columns)]

time: 42.3 us -> 42.9 us (1.014)
  starting transfers between devices: 18 us -> 19.4 us
  waiting for transfers between devices: 7.63 us -> 6.79 us
    ppermute x7 -> x8, waiting for transfers between devices: 1.25 us -> 0.43 us  [from_owner(): return lax.ppermute(x, ('groups', 'adapter'), pairs)]
    ppermute x7 -> x8, starting transfers between devices: 12.8 us -> 13.6 us  [from_owner(): return lax.ppermute(x, ('groups', 'adapter'), pairs)]
    ppermute x7 -> x8, starting transfers between devices: 4.44 us -> 4.74 us  [from_tensor(): return lax.ppermute(x, 'tensor', [(s, s ^ m) for s in range(4)])]
    ppermute x7 -> x8, waiting for transfers between devices: 6.38 us -> 6.36 us  [from_tensor(): return lax.ppermute(x, 'tensor', [(s, s ^ m) for s in range(4)])]
  transfers between devices with their start and end apart: 15 -> 17, of which waited for: 5 -> 4; matrix products, arithmetic and copies ran while one was open for 0% -> 0% of each run, Pallas kernels for 36% -> 35%
where the time goes in v17:
time: 42.9 us; the launch traced here: 42.7 us
  starting transfers between devices  19.4 us (45%)
  Pallas kernels  15.5 us (36%)
  waiting for transfers between devices  6.79 us (16%)
  other arithmetic  0.89 us (2%)
    ppermute x8, starting transfers between devices, from_owner(): return lax.ppermute(x, ('groups', 'adapter'), pairs)  13.6 us
    pallas_call x4, Pallas kernels, base_part(): kernel_call(functools.partial(base_kernel, block, places, numbers, stream...  10.8 us
    ppermute x8, waiting for transfers between devices, from_tensor(): return lax.ppermute(x, 'tensor', [(s, s ^ m) for s in range(4)])  6.36 us
    ppermute x8, starting transfers between devices, from_tensor(): return lax.ppermute(x, 'tensor', [(s, s ^ m) for s in range(4)])  4.74 us
    pallas_call x1, Pallas kernels, paired(): kernel_call(functools.partial(cut_kernel, block, range(loads[1]), len(sma...  3.94 us
    ppermute x1, starting transfers between devices, from_group(): return lax.ppermute(x, 'groups', [(0, 1), (1, 0)])  1.07 us
  transfers between devices with their start and end apart: 17, of which 4 were waited for; matrix products, arithmetic and copies ran while one was open for 0% of the time, Pallas kernels for 35%

profile of v17, /device:TPU:0, one launch (start us, length us, event | category | flops | bytes accessed | tf_op | source)
XLA Modules:
  0.0 42.7 jit_solution(17996640980883295214)
XLA Ops:
  0.0 4.0 %collective-permute-start = (bf16[16,2048]{1,0:T(8,128)(2,1)}, bf16[16,2048]{1,0:T(8,128)(2,1)S(1)}, u32[]{:S(2)}, u32[]{:S(2)}) collective-permute-start(bf16[16,2048]{1,0:T(8,128)(2,1)} %refs_2_.1), channel_id=1, source_target_pairs={{0,8},{4,12},{8,0},{12,4},{16,24},{20,28},{24,16},{28,20},{1,9},{5... | collective-permute-start | bytes 196616 | tf_op jit(solution)/shard_map/ppermute | solution.py:219
  4.0 1.3 %collective-permute-start.1 = (bf16[16,2048]{1,0:T(8,128)(2,1)}, bf16[16,2048]{1,0:T(8,128)(2,1)S(1)}, u32[]{:S(2)}, u32[]{:S(2)}) collective-permute-start(bf16[16,2048]{1,0:T(8,128)(2,1)} %refs_2_.1), channel_id=1, source_target_pairs={{0,12},{4,8},{8,4},{12,0},{16,28},{20,24},{24,20},{28,16},{1,13},{... | collective-permute-start | bytes 196616 | tf_op jit(solution)/shard_map/ppermute | solution.py:219
  5.4 0.2 collective-permute-start.2
  5.6 3.9 %cut_expand.1 = (bf16[16,7168]{1,0:T(8,128)(2,1)S(1)}, bf16[16,7168]{1,0:T(8,128)(2,1)S(1)}, bf16[16,7168]{1,0:T(8,128)(2,1)S(1)}, s32[1,4]{1,0:T(1,128)S(1)}, s...) custom-call(bf16[1,16,28672]{2,1,0:T(8,128)(2,1)} %expand.1, ...), custom_call_target="tpu_custom_call" | custom-call | flops 1 | bytes 1 | tf_op jit(solution)/shard_map/cut_expand/pallas_call | solution.py:245
  9.6 2.9 %collective-permute-start.6 = (bf16[16,7168]{1,0:T(8,128)(2,1)S(1)}, bf16[16,7168]{1,0:T(8,128)(2,1)S(1)}, u32[]{:S(2)}, u32[]{:S(2)}) collective-permute-start(bf16[16,7168]{1,0:T(8,128)(2,1)S(1)} %get-tuple-element.51), channel_id=1, source_target_pairs={{0,8},{4,12},{8,0},{12,4},{16,28},{20,24},{24,20},{28,16},{1,9},{5... | collective-permute-start | bytes 688136 | tf_op jit(solution)/shard_map/ppermute | solution.py:219
  12.5 0.6 %collective-permute-start.10 = (bf16[16,7168]{1,0:T(8,128)(2,1)S(1)}, bf16[16,7168]{1,0:T(8,128)(2,1)S(1)}, u32[]{:S(2)}, u32[]{:S(2)}) collective-permute-start(bf16[16,7168]{1,0:T(8,128)(2,1)S(1)} %get-tuple-element.68), channel_id=1, source_target_pairs={{0,4},{4,0},{8,12},{12,8},{16,20},{20,16},{24,28},{28,24},{1,5},{5... | collective-permute-start | bytes 688136 | tf_op jit(solution)/shard_map/ppermute | solution.py:219
  13.1 0.0 collective-permute-done.refs_1_
  13.1 0.0 collective-permute-done.1.refs_2_
  13.1 0.0 collective-permute-done.2.refs_3_
  13.1 0.3 gather_rows.1
  13.4 0.1 collective-permute-start.3
  13.5 1.6 %collective-permute-start.4 = (f32[16,64]{1,0:T(8,128)S(1)}, f32[16,64]{1,0:T(8,128)S(1)}, u32[]{:S(2)}, u32[]{:S(2)}) collective-permute-start(f32[16,64]{1,0:T(8,128)S(1)} %get-tuple-element.48.refs_2_), channel_id=1, source_target_pairs={{0,2},{1,3},{2,0},{3,1},{4,6},{5,7},{6,4},{7,5},{8,10},{9,11},{10,... | collective-permute-start | bytes 12296 | tf_op jit(solution)/shard_map/ppermute | solution.py:222
  15.0 0.3 collective-permute-start.5
  15.3 3.6 %base_part.4 = (f32[64,2048]{1,0:T(8,128)S(1)}, bf16[4,2048,512]{2,1,0:T(8,128)(2,1)S(1)}) custom-call(bf16[64,2048]{1,0:T(8,128)(2,1)S(1)} %get-tuple-element.45.rows, bf16[2048,7168]{1,0:T(8,128)(2,1)} %weight.9, bf16[4,2048,512]{2,1,0:T(8,128)(2,1)S(1)} %get-tuple-element.46.refs_0_, f32[16,64]{1,0:T(8,128)S(1)} %get-tuple-element.47.refs_1_, ...), custom_call_target="tpu_custom_call" | custom-call | flops 1610612736 | bytes 25165824 | tf_op jit(solution)/shard_map/base_part/pallas_call | solution.py:296
  18.9 3.0 %base_part.5 = (f32[64,2048]{1,0:T(8,128)S(1)}, bf16[3,2048,512]{2,1,0:T(8,128)(2,1)S(1)}) custom-call(bf16[64,2048]{1,0:T(8,128)(2,1)S(1)} %get-tuple-element.45.rows, bf16[2048,7168]{1,0:T(8,128)(2,1)} %weight.9, bf16[4,2048,512]{2,1,0:T(8,128)(2,1)S(1)} %get-tuple-element.52.refs_0_, f32[64,2048]{1,0:T(8,128)S(1)} %get-tuple-element.50.refs_1_.refs_0_), custom_call_target="tpu_custom_call" | custom-call | flops 1610612736 | bytes 25165824 | tf_op jit(solution)/shard_map/base_part/pallas_call | solution.py:296
  21.9 0.0 collective-permute-done.3
  21.9 0.0 collective-permute-done.4
  21.9 0.0 collective-permute-done.5
  21.9 0.4 collective-permute-done.6.refs_2_.refs_6_
  22.3 1.1 %collective-permute-start.11 = (bf16[16,7168]{1,0:T(8,128)(2,1)S(1)}, bf16[16,7168]{1,0:T(8,128)(2,1)S(1)}, u32[]{:S(2)}, u32[]{:S(2)}) collective-permute-start(bf16[16,7168]{1,0:T(8,128)(2,1)S(1)} %collective-permute-done.6.refs_2_.refs_6_), channel_id=1, source_target_pairs={{0,16},{16,0},{1,17},{17,1},{2,18},{18,2},{3,19},{19,3},{4,20},{20... | collective-permute-start | bytes 688136 | tf_op jit(solution)/shard_map/ppermute | solution.py:225
  23.4 1.6 %collective-permute-start.7 = (bf16[16,64]{1,0:T(8,128)(2,1)S(1)}, bf16[16,64]{1,0:T(8,128)(2,1)S(1)}, u32[]{:S(2)}, u32[]{:S(2)}) collective-permute-start(bf16[16,64]{1,0:T(8,128)(2,1)S(1)} %multiply_convert_fusion.refs_1_), channel_id=1, source_target_pairs={{0,4},{4,0},{8,12},{12,8},{16,20},{20,16},{24,28},{28,24},{1,5},{5... | collective-permute-start | bytes 6152 | tf_op jit(solution)/shard_map/ppermute | solution.py:219
  25.0 0.5 %collective-permute-start.8 = (bf16[16,64]{1,0:T(8,128)(2,1)S(1)}, bf16[16,64]{1,0:T(8,128)(2,1)S(1)}, u32[]{:S(2)}, u32[]{:S(2)}) collective-permute-start(bf16[16,64]{1,0:T(8,128)(2,1)S(1)} %multiply_convert_fusion.refs_1_), channel_id=1, source_target_pairs={{0,8},{4,12},{8,0},{12,4},{16,24},{20,28},{24,16},{28,20},{1,9},{5... | collective-permute-start | bytes 6152 | tf_op jit(solution)/shard_map/ppermute | solution.py:219
  25.5 2.3 %collective-permute-start.9 = (bf16[16,64]{1,0:T(8,128)(2,1)S(1)}, bf16[16,64]{1,0:T(8,128)(2,1)S(1)}, u32[]{:S(2)}, u32[]{:S(2)}) collective-permute-start(bf16[16,64]{1,0:T(8,128)(2,1)S(1)} %multiply_convert_fusion.refs_1_), channel_id=1, source_target_pairs={{0,12},{4,8},{8,4},{12,0},{16,28},{20,24},{24,20},{28,16},{1,13},{... | collective-permute-start | bytes 6152 | tf_op jit(solution)/shard_map/ppermute | solution.py:219
  27.8 2.2 %base_part.6 = (f32[64,1536]{1,0:T(8,128)S(1)}, bf16[2,2048,512]{2,1,0:T(8,128)(2,1)S(1)}) custom-call(bf16[64,2048]{1,0:T(8,128)(2,1)S(1)} %get-tuple-element.45.rows, bf16[2048,7168]{1,0:T(8,128)(2,1)} %weight.9, bf16[3,2048,512]{2,1,0:T(8,128)(2,1)S(1)} %get-tuple-element.55.refs_0_, bf16[16,64]{1,0:T(8,128)(2,1)S(1)} %multiply_convert_fusion.refs_1_, ...), custom_call_target="tpu_custom_call" | custom-call | flops 1 | bytes 1 | tf_op jit(solution)/shard_map/base_part/pallas_call | solution.py:296
  30.1 2.1 %base_part.7.refs_3_ = f32[64,1536]{1,0:T(8,128)S(1)} custom-call(bf16[64,2048]{1,0:T(8,128)(2,1)S(1)} %get-tuple-element.45.rows, bf16[2048,7168]{1,0:T(8,128)(2,1)} %weight.9, bf16[2,2048,512]{2,1,0:T(8,128)(2,1)S(1)} %get-tuple-element.62.refs_0_, f32[64,1536]{1,0:T(8,128)S(1)} %get-tuple-element.61.refs_1_.refs_2_), custom_call_target="tpu_custom_call" | custom-call | flops 1 | bytes 1 | tf_op jit(solution)/shard_map/base_part/pallas_call | solution.py:296
  32.1 0.0 collective-permute-done.7
  32.1 0.0 collective-permute-done.8
  32.1 0.0 collective-permute-done.9
  32.2 0.0 collective-permute-done.10.refs_7_
  32.2 0.0 collective-permute-done.11.refs_8_
  32.2 0.5 %add_delta.1 = (f32[16,7168]{1,0:T(8,128)S(1)}, f32[16,7168]{1,0:T(8,128)S(1)}, f32[16,3584]{1,0:T(8,128)S(1)}, f32[16,3584]{1,0:T(8,128)S(1)}, f32[16,3584]{1,0:T(8,128)S(1)}, /*index=5*/f32[16,3584]{1,0:T(8,128)S(1)}) custom-call(s32[1,64]{1,0:T(1,128)S(1)} %get-tuple-element.44.slot, f32[64,2048]{1,0:T(8,128)S(1)} %get-tuple-element.50.refs_1_.refs_0_, ...), custom_call_target="tpu_custom_call" | custom-call | flops 1 | bytes 1 | tf_op jit(solution)/shard_map/add_delta/pallas_call | solution.py:329
  32.7 0.1 collective-permute-start.15
  32.8 0.5 %collective-permute-start.13 = (f32[16,3584]{1,0:T(8,128)S(1)}, f32[16,3584]{1,0:T(8,128)S(1)}, u32[]{:S(2)}, u32[]{:S(2)}) collective-permute-start(f32[16,3584]{1,0:T(8,128)S(1)} %get-tuple-element.72), channel_id=1, source_target_pairs={{0,1},{1,0},{2,3},{3,2},{4,5},{5,4},{6,7},{7,6},{8,9},{9,8},{10,11... | collective-permute-start | bytes 688136 | tf_op jit(solution)/shard_map/ppermute | solution.py:222
  33.3 0.1 collective-permute-start.12
  33.3 0.9 %collective-permute-done.15 = f32[16,3584]{1,0:T(8,128)S(1)} collective-permute-done((f32[16,3584]{1,0:T(8,128)S(1)}, f32[16,3584]{1,0:T(8,128)S(1)}, u32[]{:S(2)}, u32[]{:S(2)}) %collective-permute-start.15) | collective-permute-done | bytes 229408 | tf_op jit(solution)/shard_map/ppermute | solution.py:222
  34.3 1.5 %collective-permute-start.16 = (bf16[16,3584]{1,0:T(8,128)(2,1)S(1)}, bf16[16,3584]{1,0:T(8,128)(2,1)S(1)}, u32[]{:S(2)}, u32[]{:S(2)}) collective-permute-start(bf16[16,3584]{1,0:T(8,128)(2,1)S(1)} %add_convert_fusion), channel_id=1, source_target_pairs={{0,2},{1,3},{2,0},{3,1},{4,6},{5,7},{6,4},{7,5},{8,10},{9,11},{10,... | collective-permute-start | bytes 344072 | tf_op jit(solution)/shard_map/ppermute | solution.py:222
  35.8 0.0 collective-permute-done.13
  35.8 0.6 %collective-permute-start.14 = (bf16[16,3584]{1,0:T(8,128)(2,1)S(1)}, bf16[16,3584]{1,0:T(8,128)(2,1)S(1)}, u32[]{:S(2)}, u32[]{:S(2)}) collective-permute-start(bf16[16,3584]{1,0:T(8,128)(2,1)S(1)} %add_convert_fusion.1), channel_id=1, source_target_pairs={{0,2},{1,3},{2,0},{3,1},{4,6},{5,7},{6,4},{7,5},{8,10},{9,11},{10,... | collective-permute-start | bytes 344072 | tf_op jit(solution)/shard_map/ppermute | solution.py:222
  36.5 0.0 collective-permute-done.12
  36.5 0.1 add.39
  36.5 3.8 %collective-permute-done.16 = bf16[16,3584]{1,0:T(8,128)(2,1)S(1)} collective-permute-done((bf16[16,3584]{1,0:T(8,128)(2,1)S(1)}, bf16[16,3584]{1,0:T(8,128)(2,1)S(1)}, u32[]{:S(2)}, u32[]{:S(2)}) %collective-permute-start.16) | collective-permute-done | bytes 114720 | tf_op jit(solution)/shard_map/ppermute | solution.py:222
  40.3 1.7 %collective-permute-done.14 = bf16[16,3584]{1,0:T(8,128)(2,1)S(1)} collective-permute-done((bf16[16,3584]{1,0:T(8,128)(2,1)S(1)}, bf16[16,3584]{1,0:T(8,128)(2,1)S(1)}, u32[]{:S(2)}, u32[]{:S(2)}) %collective-permute-start.14) | collective-permute-done | bytes 114720 | tf_op jit(solution)/shard_map/ppermute | solution.py:222
  42.0 0.7 %pad_maximum_fusion = bf16[16,7168]{1,0:T(8,128)(2,1)} fusion(bf16[16,3584]{1,0:T(8,128)(2,1)S(1)} %get-tuple-element.76, bf16[16,3584]{1,0:T(8,128)(2,1)S(1)} %get-tuple-element.75), kind=kLoop, calls=%fused_computation.4 | loop fusion | flops 458752 | bytes 458752 | tf_op jit(solution)/shard_map/concatenate | solution.py:350
  (5 shorter events, 0.1 us)
Async XLA Ops:
  0.0 13.1 %collective-permute-start = (bf16[16,2048]{1,0:T(8,128)(2,1)}, bf16[16,2048]{1,0:T(8,128)(2,1)S(1)}, u32[]{:S(2)}, u32[]{:S(2)}) collective-permute-start(bf16[16,2048]{1,0:T(8,128)(2,1)} %refs_2_.1), channel_id=1, source_target_pairs={{0,8},{4,12},{8,0},{12,4},{16,24},{20,28},{24,16},{28,20},{1,9},{5... | collective-permute-start | bytes 196616 | tf_op jit(solution)/shard_map/ppermute | solution.py:219
  4.0 9.1 %collective-permute-start.1 = (bf16[16,2048]{1,0:T(8,128)(2,1)}, bf16[16,2048]{1,0:T(8,128)(2,1)S(1)}, u32[]{:S(2)}, u32[]{:S(2)}) collective-permute-start(bf16[16,2048]{1,0:T(8,128)(2,1)} %refs_2_.1), channel_id=1, source_target_pairs={{0,12},{4,8},{8,4},{12,0},{16,28},{20,24},{24,20},{28,16},{1,13},{... | collective-permute-start | bytes 196616 | tf_op jit(solution)/shard_map/ppermute | solution.py:219
  5.4 7.7 %collective-permute-start.2 = (bf16[16,2048]{1,0:T(8,128)(2,1)}, bf16[16,2048]{1,0:T(8,128)(2,1)S(1)}, u32[]{:S(2)}, u32[]{:S(2)}) collective-permute-start(bf16[16,2048]{1,0:T(8,128)(2,1)} %refs_2_.1), channel_id=1, source_target_pairs={{0,4},{4,0},{8,12},{12,8},{16,20},{20,16},{24,28},{28,24},{1,5},{5... | collective-permute-start | bytes 196616 | tf_op jit(solution)/shard_map/ppermute | solution.py:219
  9.6 12.8 %collective-permute-start.6 = (bf16[16,7168]{1,0:T(8,128)(2,1)S(1)}, bf16[16,7168]{1,0:T(8,128)(2,1)S(1)}, u32[]{:S(2)}, u32[]{:S(2)}) collective-permute-start(bf16[16,7168]{1,0:T(8,128)(2,1)S(1)} %get-tuple-element.51), channel_id=1, source_target_pairs={{0,8},{4,12},{8,0},{12,4},{16,28},{20,24},{24,20},{28,16},{1,9},{5... | collective-permute-start | bytes 688136 | tf_op jit(solution)/shard_map/ppermute | solution.py:219
  12.5 19.7 %collective-permute-start.10 = (bf16[16,7168]{1,0:T(8,128)(2,1)S(1)}, bf16[16,7168]{1,0:T(8,128)(2,1)S(1)}, u32[]{:S(2)}, u32[]{:S(2)}) collective-permute-start(bf16[16,7168]{1,0:T(8,128)(2,1)S(1)} %get-tuple-element.68), channel_id=1, source_target_pairs={{0,4},{4,0},{8,12},{12,8},{16,20},{20,16},{24,28},{28,24},{1,5},{5... | collective-permute-start | bytes 688136 | tf_op jit(solution)/shard_map/ppermute | solution.py:219
  13.4 8.5 %collective-permute-start.3 = (f32[16,64]{1,0:T(8,128)S(1)}, f32[16,64]{1,0:T(8,128)S(1)}, u32[]{:S(2)}, u32[]{:S(2)}) collective-permute-start(f32[16,64]{1,0:T(8,128)S(1)} %get-tuple-element.47.refs_1_), channel_id=1, source_target_pairs={{0,1},{1,0},{2,3},{3,2},{4,5},{5,4},{6,7},{7,6},{8,9},{9,8},{10,11... | collective-permute-start | bytes 12296 | tf_op jit(solution)/shard_map/ppermute | solution.py:222
  13.5 8.4 %collective-permute-start.4 = (f32[16,64]{1,0:T(8,128)S(1)}, f32[16,64]{1,0:T(8,128)S(1)}, u32[]{:S(2)}, u32[]{:S(2)}) collective-permute-start(f32[16,64]{1,0:T(8,128)S(1)} %get-tuple-element.48.refs_2_), channel_id=1, source_target_pairs={{0,2},{1,3},{2,0},{3,1},{4,6},{5,7},{6,4},{7,5},{8,10},{9,11},{10,... | collective-permute-start | bytes 12296 | tf_op jit(solution)/shard_map/ppermute | solution.py:222
  15.0 6.9 %collective-permute-start.5 = (f32[16,64]{1,0:T(8,128)S(1)}, f32[16,64]{1,0:T(8,128)S(1)}, u32[]{:S(2)}, u32[]{:S(2)}) collective-permute-start(f32[16,64]{1,0:T(8,128)S(1)} %get-tuple-element.49.refs_3_), channel_id=1, source_target_pairs={{0,3},{1,2},{2,1},{3,0},{4,7},{5,6},{6,5},{7,4},{8,11},{9,10},{10,... | collective-permute-start | bytes 12296 | tf_op jit(solution)/shard_map/ppermute | solution.py:222
  22.3 9.8 %collective-permute-start.11 = (bf16[16,7168]{1,0:T(8,128)(2,1)S(1)}, bf16[16,7168]{1,0:T(8,128)(2,1)S(1)}, u32[]{:S(2)}, u32[]{:S(2)}) collective-permute-start(bf16[16,7168]{1,0:T(8,128)(2,1)S(1)} %collective-permute-done.6.refs_2_.refs_6_), channel_id=1, source_target_pairs={{0,16},{16,0},{1,17},{17,1},{2,18},{18,2},{3,19},{19,3},{4,20},{20... | collective-permute-start | bytes 688136 | tf_op jit(solution)/shard_map/ppermute | solution.py:225
  23.4 8.7 %collective-permute-start.7 = (bf16[16,64]{1,0:T(8,128)(2,1)S(1)}, bf16[16,64]{1,0:T(8,128)(2,1)S(1)}, u32[]{:S(2)}, u32[]{:S(2)}) collective-permute-start(bf16[16,64]{1,0:T(8,128)(2,1)S(1)} %multiply_convert_fusion.refs_1_), channel_id=1, source_target_pairs={{0,4},{4,0},{8,12},{12,8},{16,20},{20,16},{24,28},{28,24},{1,5},{5... | collective-permute-start | bytes 6152 | tf_op jit(solution)/shard_map/ppermute | solution.py:219
  25.0 7.1 %collective-permute-start.8 = (bf16[16,64]{1,0:T(8,128)(2,1)S(1)}, bf16[16,64]{1,0:T(8,128)(2,1)S(1)}, u32[]{:S(2)}, u32[]{:S(2)}) collective-permute-start(bf16[16,64]{1,0:T(8,128)(2,1)S(1)} %multiply_convert_fusion.refs_1_), channel_id=1, source_target_pairs={{0,8},{4,12},{8,0},{12,4},{16,24},{20,28},{24,16},{28,20},{1,9},{5... | collective-permute-start | bytes 6152 | tf_op jit(solution)/shard_map/ppermute | solution.py:219
  25.5 6.6 %collective-permute-start.9 = (bf16[16,64]{1,0:T(8,128)(2,1)S(1)}, bf16[16,64]{1,0:T(8,128)(2,1)S(1)}, u32[]{:S(2)}, u32[]{:S(2)}) collective-permute-start(bf16[16,64]{1,0:T(8,128)(2,1)S(1)} %multiply_convert_fusion.refs_1_), channel_id=1, source_target_pairs={{0,12},{4,8},{8,4},{12,0},{16,28},{20,24},{24,20},{28,16},{1,13},{... | collective-permute-start | bytes 6152 | tf_op jit(solution)/shard_map/ppermute | solution.py:219
  32.7 1.6 %collective-permute-start.15 = (f32[16,3584]{1,0:T(8,128)S(1)}, f32[16,3584]{1,0:T(8,128)S(1)}, u32[]{:S(2)}, u32[]{:S(2)}) collective-permute-start(f32[16,3584]{1,0:T(8,128)S(1)} %get-tuple-element.74), channel_id=1, source_target_pairs={{0,1},{1,0},{2,3},{3,2},{4,5},{5,4},{6,7},{7,6},{8,9},{9,8},{10,11... | collective-permute-start | bytes 688136 | tf_op jit(solution)/shard_map/ppermute | solution.py:222
  32.8 3.1 %collective-permute-start.13 = (f32[16,3584]{1,0:T(8,128)S(1)}, f32[16,3584]{1,0:T(8,128)S(1)}, u32[]{:S(2)}, u32[]{:S(2)}) collective-permute-start(f32[16,3584]{1,0:T(8,128)S(1)} %get-tuple-element.72), channel_id=1, source_target_pairs={{0,1},{1,0},{2,3},{3,2},{4,5},{5,4},{6,7},{7,6},{8,9},{9,8},{10,11... | collective-permute-start | bytes 688136 | tf_op jit(solution)/shard_map/ppermute | solution.py:222
  33.3 3.2 %collective-permute-start.12 = (f32[16,7168]{1,0:T(8,128)S(1)}, f32[16,7168]{1,0:T(8,128)S(1)}, u32[]{:S(2)}, u32[]{:S(2)}) collective-permute-start(f32[16,7168]{1,0:T(8,128)S(1)} %get-tuple-element.70), channel_id=1, source_target_pairs={{0,1},{1,0},{2,3},{3,2},{4,5},{5,4},{6,7},{7,6},{8,9},{9,8},{10,11... | collective-permute-start | bytes 1376264 | tf_op jit(solution)/shard_map/ppermute | solution.py:222
  34.3 6.1 %collective-permute-start.16 = (bf16[16,3584]{1,0:T(8,128)(2,1)S(1)}, bf16[16,3584]{1,0:T(8,128)(2,1)S(1)}, u32[]{:S(2)}, u32[]{:S(2)}) collective-permute-start(bf16[16,3584]{1,0:T(8,128)(2,1)S(1)} %add_convert_fusion), channel_id=1, source_target_pairs={{0,2},{1,3},{2,0},{3,1},{4,6},{5,7},{6,4},{7,5},{8,10},{9,11},{10,... | collective-permute-start | bytes 344072 | tf_op jit(solution)/shard_map/ppermute | solution.py:222
  35.8 6.1 %collective-permute-start.14 = (bf16[16,3584]{1,0:T(8,128)(2,1)S(1)}, bf16[16,3584]{1,0:T(8,128)(2,1)S(1)}, u32[]{:S(2)}, u32[]{:S(2)}) collective-permute-start(bf16[16,3584]{1,0:T(8,128)(2,1)S(1)} %add_convert_fusion.1), channel_id=1, source_target_pairs={{0,2},{1,3},{2,0},{3,1},{4,6},{5,7},{6,4},{7,5},{8,10},{9,11},{10,... | collective-permute-start | bytes 344072 | tf_op jit(solution)/shard_map/ppermute | solution.py:222

commit v18 on v15

--- a/solution.py
+++ b/solution.py
@@ -127,28 +127,38 @@
         target[at : at + rank_block, :] = partial[pl.ds(start, rank_block), :]
 
 
-def base_kernel(block, places, numbers, streamed, rows, weight, *refs):
-    total, ahead, sem = refs[-3:]
-    copies = weight_copies(block, numbers, weight, ahead, sem)
-    for copy in copies:
+def base_kernel(block, stream, ahead, rows, weight, held, *refs):
+    refs = list(refs)
+    copies, streamed, later = [], None, []
+    if ahead:
+        sem = refs.pop()
+    if stream:
+        streamed, stream_sem = refs[-2:]
+        refs = refs[:-2]
+        copies = weight_copies(block, stream, weight, streamed, stream_sem)
+    if ahead:
+        later = weight_copies(block, ahead, weight, refs.pop(), sem)
+    total = refs[-1]
+    for copy in copies + later:
         copy.start()
 
     @pl.when(lax.axis_index("tensor") >= 0)
     def _():
-        for n, (which, index) in enumerate(places):
+        for n in range(held.shape[0]):
             total[:, n * block : (n + 1) * block] = jnp.dot(
-                rows[...], refs[which][index], preferred_element_type=f32
+                rows[...], held[n], preferred_element_type=f32
             )
 
-    bands = sem.shape[1]
-    for n in range(len(numbers)):
+    for n in range(len(stream)):
+        bands = len(copies) // len(stream)
         for copy in copies[n * bands : (n + 1) * bands]:
             copy.wait()
-        if streamed:
-            at = (len(places) + n) * block
-            total[:, at : at + block] = jnp.dot(
-                rows[...], ahead[n], preferred_element_type=f32
-            )
+        at = (held.shape[0] + n) * block
+        total[:, at : at + block] = jnp.dot(
+            rows[...], streamed[n], preferred_element_type=f32
+        )
+    for copy in later:
+        copy.wait()
 
 
 def delta_kernel(block, splits, slot, *refs):
@@ -231,9 +241,9 @@
     offsets = (2, 3, 1)
     blocks = [from_owner(tokens, j, j) for j in offsets]
 
-    cuts = [block_count * k // 14 for k in (0, 4, 8, 11, 14)]
-    parts = list(zip(cuts[:-1], cuts[1:]))
-    loads = [block_count * k // 14 for k in (0, 4, 8, 11, 13, 14)]
+    loads = [block_count * k // 14 for k in (0, 4, 8, 11, 14)]
+    streams = [range(loads[1], loads[2]), range(0), range(0)]
+    aheads = [range(loads[2], loads[3]), range(loads[3], loads[4]), range(0)]
     bands = 4
     small = [
         pltpu.with_memory_space_constraint(x, pltpu.HBM)
@@ -260,8 +270,7 @@
             pltpu.SemaphoreType.DMA((loads[1], bands)),
         ],
     )(expand, weight, *small)
-    loaded = [held]
-    across, beside = from_owner(across, 2, 3), from_owner(beside, 1, 1)
+    across = from_owner(across, 2, 3)
 
     rows, keep, send, slot = kernel_call(
         functools.partial(gather_kernel, (0, *offsets)),
@@ -283,50 +292,50 @@
         shrink,
     )
 
-    def base_part(n, *after):
-        first, last = parts[n]
-        streamed = n + 1 == len(parts)
-        numbers = range(loads[n + 1], loads[n + 2])
-        places, used = [], []
-        for number in range(first, numbers[0] if streamed else last):
-            source = max(k for k in range(len(loads) - 1) if loads[k] <= number)
-            if source not in used:
-                used.append(source)
-            places.append((used.index(source), number - loads[source]))
-        near = n < 2
-        ahead = pltpu.VMEM((len(numbers), depth, block), bf16)
-        out = kernel_call(
-            functools.partial(base_kernel, block, places, numbers, streamed),
+    def base_part(n, held, *after):
+        stream, ahead = streams[n], aheads[n]
+        width = (held.shape[0] + len(stream)) * block
+        extra, scratch = [], []
+        if ahead:
+            extra = [pltpu.VMEM((len(ahead), depth, block), bf16)]
+        if stream:
+            scratch += [
+                pltpu.VMEM((len(stream), depth, block), bf16),
+                pltpu.SemaphoreType.DMA((len(stream), bands)),
+            ]
+        if ahead:
+            scratch += [pltpu.SemaphoreType.DMA((len(ahead), bands))]
+        return kernel_call(
+            functools.partial(base_kernel, block, stream, ahead),
             "base_part",
-            3 * 2 * row_count * depth * (last - first) * block if near else 1,
-            3 * 2 * depth * (last - first) * block if near else 1,
+            (2 * 10**9, 1, 1)[n],
+            1,
             12,
-            in_specs=[vmem, anywhere] + [vmem] * len(used) + [anywhere] * len(after),
-            out_specs=[vmem] * (1 if streamed else 2),
-            out_shape=[jax.ShapeDtypeStruct((row_count, (last - first) * block), f32)]
-            + ([] if streamed else [ahead]),
-            scratch_shapes=([ahead] if streamed else [])
-            + [pltpu.SemaphoreType.DMA((len(numbers), bands))],
-        )(rows, weight, *[loaded[k] for k in used], *after)
-        loaded.append(out[-1])
-        return out[0]
-
+            in_specs=[vmem, anywhere, vmem] + [anywhere] * len(after),
+            out_specs=[vmem] * (1 + len(extra)),
+            out_shape=[jax.ShapeDtypeStruct((row_count, width), f32)] + extra,
+            scratch_shapes=scratch,
+        )(rows, weight, held, *after)
+
+    beside, send = lax.optimization_barrier((beside, send))
     arrived = from_tensor(send, 1)
-    base_0 = base_part(0, send)
-    arrived, base_0 = lax.optimization_barrier((arrived, base_0))
+    beside = from_owner(beside, 1, 1)
     pair = keep + arrived
     arrived = from_tensor(pair[rank_block:], 2)
-    base_1 = base_part(1, pair)
-    arrived, base_1, across = lax.optimization_barrier((arrived, base_1, across))
+    base, held = base_part(0, held, pair)
+    arrived, across, base = lax.optimization_barrier((arrived, across, base))
+    bases = [base]
     shrunk = (adapter_scale * (pair[:rank_block] + arrived)).astype(bf16)
+    arrived = from_owner(shrunk, 1, 1)
     swapped = from_group(across)
-    bases = [base_0, base_1]
-    for m, n in ((1, 2), (2, 3)):
-        arrived = from_owner(shrunk, m, m)
-        base = base_part(n, shrunk, across)
-        arrived, base = lax.optimization_barrier((arrived, base))
-        bases.append(base)
-        shrunk = shrunk + arrived
+    base, held = base_part(1, held, shrunk, across)
+    bases.append(base)
+    arrived, base = lax.optimization_barrier((arrived, base))
+    shrunk = shrunk + arrived
+    arrived = from_owner(shrunk, 2, 2)
+    bases += base_part(2, held, shrunk)
+    arrived, base = lax.optimization_barrier((arrived, bases[-1]))
+    shrunk = shrunk + arrived
 
     middle = block_count // 2 * block
     splits = [(0, middle), (middle, columns)]

time: 42.3 us -> 43.2 us (1.021)
  waiting for transfers between devices: 7.63 us -> 9.48 us
  Pallas kernels: 15.5 us -> 14.7 us
    ppermute x7, waiting for transfers between devices: 1.25 us -> 3.1 us  [from_owner(): return lax.ppermute(x, ('groups', 'adapter'), pairs)]
    ppermute x7, starting transfers between devices: 12.8 us -> 11.9 us  [from_owner(): return lax.ppermute(x, ('groups', 'adapter'), pairs)]
    ppermute x1, starting transfers between devices: 0.78 us -> 1.66 us  [from_group(): return lax.ppermute(x, 'groups', [(0, 1), (1, 0)])]
    pallas_call x4 -> x3, Pallas kernels: 10.8 us -> 9.98 us  [base_part(): kernel_call(functools.partial(base_kernel, block, stream, ahead), 'base_p...]
  transfers between devices with their start and end apart: 15 -> 15, of which waited for: 5 -> 6; matrix products, arithmetic and copies ran while one was open for 0% -> 0% of each run, Pallas kernels for 36% -> 33%
where the time goes in v18:
time: 43.2 us; the launch traced here: 43.1 us
  starting transfers between devices  17.9 us (41%)
  Pallas kernels  14.7 us (34%)
  waiting for transfers between devices  9.48 us (22%)
  other arithmetic  0.86 us (2%)
    ppermute x7, starting transfers between devices, from_owner(): return lax.ppermute(x, ('groups', 'adapter'), pairs)  11.9 us
    pallas_call x3, Pallas kernels, base_part(): kernel_call(functools.partial(base_kernel, block, stream, ahead), 'base_p...  9.98 us
    ppermute x7, waiting for transfers between devices, from_tensor(): return lax.ppermute(x, 'tensor', [(s, s ^ m) for s in range(4)])  6.38 us
    ppermute x7, starting transfers between devices, from_tensor(): return lax.ppermute(x, 'tensor', [(s, s ^ m) for s in range(4)])  4.43 us
    pallas_call x1, Pallas kernels, paired(): kernel_call(functools.partial(cut_kernel, block, range(loads[1]), len(sma...  3.95 us
    ppermute x7, waiting for transfers between devices, from_owner(): return lax.ppermute(x, ('groups', 'adapter'), pairs)  3.1 us
    ppermute x1, starting transfers between devices, from_group(): return lax.ppermute(x, 'groups', [(0, 1), (1, 0)])  1.66 us
  transfers between devices with their start and end apart: 15, of which 6 were waited for; matrix products, arithmetic and copies ran while one was open for 0% of the time, Pallas kernels for 33%

profile of v18, /device:TPU:0, one launch (start us, length us, event | category | flops | bytes accessed | tf_op | source)
XLA Modules:
  0.0 43.1 jit_solution(17669867094211751775)
XLA Ops:
  0.0 4.0 %collective-permute-start = (bf16[16,2048]{1,0:T(8,128)(2,1)}, bf16[16,2048]{1,0:T(8,128)(2,1)S(1)}, u32[]{:S(2)}, u32[]{:S(2)}) collective-permute-start(bf16[16,2048]{1,0:T(8,128)(2,1)} %refs_2_.1), channel_id=1, source_target_pairs={{0,8},{4,12},{8,0},{12,4},{16,24},{20,28},{24,16},{28,20},{1,9},{5... | collective-permute-start | bytes 196616 | tf_op jit(solution)/shard_map/ppermute | solution.py:231
  4.0 1.6 %collective-permute-start.2 = (bf16[16,2048]{1,0:T(8,128)(2,1)}, bf16[16,2048]{1,0:T(8,128)(2,1)S(1)}, u32[]{:S(2)}, u32[]{:S(2)}) collective-permute-start(bf16[16,2048]{1,0:T(8,128)(2,1)} %refs_2_.1), channel_id=1, source_target_pairs={{0,4},{4,0},{8,12},{12,8},{16,20},{20,16},{24,28},{28,24},{1,5},{5... | collective-permute-start | bytes 196616 | tf_op jit(solution)/shard_map/ppermute | solution.py:231
  5.6 0.0 collective-permute-start.1
  5.6 3.9 %cut_expand.1 = (bf16[16,7168]{1,0:T(8,128)(2,1)S(1)}, bf16[16,7168]{1,0:T(8,128)(2,1)S(1)}, bf16[16,7168]{1,0:T(8,128)(2,1)S(1)}, s32[1,4]{1,0:T(1,128)S(1)}, s...) custom-call(bf16[1,16,28672]{2,1,0:T(8,128)(2,1)} %expand.1, ...), custom_call_target="tpu_custom_call" | custom-call | flops 1 | bytes 1 | tf_op jit(solution)/shard_map/cut_expand/pallas_call | solution.py:257
  9.6 2.0 %collective-permute-start.5 = (bf16[16,7168]{1,0:T(8,128)(2,1)S(1)}, bf16[16,7168]{1,0:T(8,128)(2,1)S(1)}, u32[]{:S(2)}, u32[]{:S(2)}) collective-permute-start(bf16[16,7168]{1,0:T(8,128)(2,1)S(1)} %get-tuple-element.43), channel_id=1, source_target_pairs={{0,8},{4,12},{8,0},{12,4},{16,28},{20,24},{24,20},{28,16},{1,9},{5... | collective-permute-start | bytes 688136 | tf_op jit(solution)/shard_map/ppermute | solution.py:231
  11.6 0.0 collective-permute-done.refs_1_
  11.6 0.0 collective-permute-done.2.refs_3_
  11.6 0.3 collective-permute-done.1.refs_2_
  11.9 0.3 gather_rows.1
  12.1 0.1 collective-permute-start.3
  12.2 2.2 %collective-permute-start.8 = (bf16[16,7168]{1,0:T(8,128)(2,1)S(1)}, bf16[16,7168]{1,0:T(8,128)(2,1)S(1)}, u32[]{:S(2)}, u32[]{:S(2)}) collective-permute-start(bf16[16,7168]{1,0:T(8,128)(2,1)S(1)} %get-tuple-element.56), channel_id=1, source_target_pairs={{0,4},{4,0},{8,12},{12,8},{16,20},{20,16},{24,28},{28,24},{1,5},{5... | collective-permute-start | bytes 688136 | tf_op jit(solution)/shard_map/ppermute | solution.py:231
  14.4 0.0 collective-permute-done.3
  14.4 1.6 %collective-permute-start.4 = (f32[16,64]{1,0:T(8,128)S(1)}, f32[16,64]{1,0:T(8,128)S(1)}, u32[]{:S(2)}, u32[]{:S(2)}) collective-permute-start(f32[16,64]{1,0:T(8,128)S(1)} %slice.16), channel_id=1, source_target_pairs={{0,2},{1,3},{2,0},{3,1},{4,6},{5,7},{6,4},{7,5},{8,10},{9,11},{10,... | collective-permute-start | bytes 12296 | tf_op jit(solution)/shard_map/ppermute | solution.py:234
  16.0 5.9 %base_part.3 = (f32[64,4096]{1,0:T(8,128)S(1)}, bf16[3,2048,512]{2,1,0:T(8,128)(2,1)S(1)}) custom-call(bf16[64,2048]{1,0:T(8,128)(2,1)S(1)} %get-tuple-element.44.rows, bf16[2048,7168]{1,0:T(8,128)(2,1)} %weight.7, bf16[4,2048,512]{2,1,0:T(8,128)(2,1)S(1)} %get-tuple-element.45.held, f32[32,64]{1,0:T(8,128)S(1)} %add.27.refs_0_), custom_call_target="tpu_custom_call" | custom-call | flops 2000000000 | bytes 1 | tf_op jit(solution)/shard_map/base_part/pallas_call | solution.py:308
  21.9 0.0 collective-permute-done.4
  21.9 0.4 %collective-permute-done.5.refs_1_.refs_5_ = bf16[16,7168]{1,0:T(8,128)(2,1)S(1)} collective-permute-done((bf16[16,7168]{1,0:T(8,128)(2,1)S(1)}, bf16[16,7168]{1,0:T(8,128)(2,1)S(1)}, u32[]{:S(2)}, u32[]{:S(2)}) %collective-permute-start.5) | collective-permute-done | bytes 229408 | tf_op jit(solution)/shard_map/ppermute | solution.py:231
  22.3 1.7 %collective-permute-start.9 = (bf16[16,7168]{1,0:T(8,128)(2,1)S(1)}, bf16[16,7168]{1,0:T(8,128)(2,1)S(1)}, u32[]{:S(2)}, u32[]{:S(2)}) collective-permute-start(bf16[16,7168]{1,0:T(8,128)(2,1)S(1)} %collective-permute-done.5.refs_1_.refs_5_), channel_id=1, source_target_pairs={{0,16},{16,0},{1,17},{17,1},{2,18},{18,2},{3,19},{19,3},{4,20},{20... | collective-permute-start | bytes 688136 | tf_op jit(solution)/shard_map/ppermute | solution.py:237
  24.0 1.0 %collective-permute-start.6 = (bf16[16,64]{1,0:T(8,128)(2,1)S(1)}, bf16[16,64]{1,0:T(8,128)(2,1)S(1)}, u32[]{:S(2)}, u32[]{:S(2)}) collective-permute-start(bf16[16,64]{1,0:T(8,128)(2,1)S(1)} %fusion.3.refs_0_), channel_id=1, source_target_pairs={{0,4},{4,0},{8,12},{12,8},{16,20},{20,16},{24,28},{28,24},{1,5},{5... | collective-permute-start | bytes 6152 | tf_op jit(solution)/shard_map/ppermute | solution.py:231
  25.0 2.9 %base_part.4 = (f32[64,1536]{1,0:T(8,128)S(1)}, bf16[3,2048,512]{2,1,0:T(8,128)(2,1)S(1)}) custom-call(bf16[64,2048]{1,0:T(8,128)(2,1)S(1)} %get-tuple-element.44.rows, bf16[2048,7168]{1,0:T(8,128)(2,1)} %weight.7, bf16[3,2048,512]{2,1,0:T(8,128)(2,1)S(1)} %get-tuple-element.48.held, bf16[16,64]{1,0:T(8,128)(2,1)S(1)} %fusion.3.refs_0_, ...), custom_call_target="tpu_custom_call" | custom-call | flops 1 | bytes 1 | tf_op jit(solution)/shard_map/base_part/pallas_call | solution.py:308
  27.9 0.0 collective-permute-done.6
  28.0 1.0 %collective-permute-start.7 = (bf16[16,64]{1,0:T(8,128)(2,1)S(1)}, bf16[16,64]{1,0:T(8,128)(2,1)S(1)}, u32[]{:S(2)}, u32[]{:S(2)}) collective-permute-start(bf16[16,64]{1,0:T(8,128)(2,1)S(1)} %add.29.refs_0_), channel_id=1, source_target_pairs={{0,8},{4,12},{8,0},{12,4},{16,24},{20,28},{24,16},{28,20},{1,9},{5... | collective-permute-start | bytes 6152 | tf_op jit(solution)/shard_map/ppermute | solution.py:231
  29.0 1.2 %base_part.5.refs_2_ = f32[64,1536]{1,0:T(8,128)S(1)} custom-call(bf16[64,2048]{1,0:T(8,128)(2,1)S(1)} %get-tuple-element.44.rows, bf16[2048,7168]{1,0:T(8,128)(2,1)} %weight.7, bf16[3,2048,512]{2,1,0:T(8,128)(2,1)S(1)} %get-tuple-element.52.held, bf16[16,64]{1,0:T(8,128)(2,1)S(1)} %add.29.refs_0_), custom_call_target="tpu_custom_call" | custom-call | flops 1 | bytes 1 | tf_op jit(solution)/shard_map/base_part/pallas_call | solution.py:308
  30.2 2.4 %collective-permute-done.7 = bf16[16,64]{1,0:T(8,128)(2,1)S(1)} collective-permute-done((bf16[16,64]{1,0:T(8,128)(2,1)S(1)}, bf16[16,64]{1,0:T(8,128)(2,1)S(1)}, u32[]{:S(2)}, u32[]{:S(2)}) %collective-permute-start.7) | collective-permute-done | bytes 2080 | tf_op jit(solution)/shard_map/ppermute | solution.py:231
  32.5 0.0 collective-permute-done.8.refs_6_
  32.5 0.0 collective-permute-done.9.refs_7_
  32.5 0.5 %add_delta.1 = (f32[16,7168]{1,0:T(8,128)S(1)}, f32[16,7168]{1,0:T(8,128)S(1)}, f32[16,3584]{1,0:T(8,128)S(1)}, f32[16,3584]{1,0:T(8,128)S(1)}, f32[16,3584]{1,0:T(8,128)S(1)}, /*index=5*/f32[16,3584]{1,0:T(8,128)S(1)}) custom-call(s32[1,64]{1,0:T(1,128)S(1)} %get-tuple-element.38.slot, f32[64,4096]{1,0:T(8,128)S(1)} %get-tuple-element.47.refs_0_, ...), custom_call_target="tpu_custom_call" | custom-call | flops 1 | bytes 1 | tf_op jit(solution)/shard_map/add_delta/pallas_call | solution.py:344
  33.0 0.1 collective-permute-start.11
  33.1 0.5 %collective-permute-start.13 = (f32[16,3584]{1,0:T(8,128)S(1)}, f32[16,3584]{1,0:T(8,128)S(1)}, u32[]{:S(2)}, u32[]{:S(2)}) collective-permute-start(f32[16,3584]{1,0:T(8,128)S(1)} %get-tuple-element.62), channel_id=1, source_target_pairs={{0,1},{1,0},{2,3},{3,2},{4,5},{5,4},{6,7},{7,6},{8,9},{9,8},{10,11... | collective-permute-start | bytes 688136 | tf_op jit(solution)/shard_map/ppermute | solution.py:234
  33.6 0.1 collective-permute-start.10
  33.7 0.9 %collective-permute-done.11 = f32[16,3584]{1,0:T(8,128)S(1)} collective-permute-done((f32[16,3584]{1,0:T(8,128)S(1)}, f32[16,3584]{1,0:T(8,128)S(1)}, u32[]{:S(2)}, u32[]{:S(2)}) %collective-permute-start.11) | collective-permute-done | bytes 229408 | tf_op jit(solution)/shard_map/ppermute | solution.py:234
  34.6 0.6 %collective-permute-start.12 = (bf16[16,3584]{1,0:T(8,128)(2,1)S(1)}, bf16[16,3584]{1,0:T(8,128)(2,1)S(1)}, u32[]{:S(2)}, u32[]{:S(2)}) collective-permute-start(bf16[16,3584]{1,0:T(8,128)(2,1)S(1)} %add_convert_fusion.1), channel_id=1, source_target_pairs={{0,2},{1,3},{2,0},{3,1},{4,6},{5,7},{6,4},{7,5},{8,10},{9,11},{10,... | collective-permute-start | bytes 344072 | tf_op jit(solution)/shard_map/ppermute | solution.py:234
  35.2 0.0 collective-permute-done.13
  35.2 1.6 %collective-permute-start.14 = (bf16[16,3584]{1,0:T(8,128)(2,1)S(1)}, bf16[16,3584]{1,0:T(8,128)(2,1)S(1)}, u32[]{:S(2)}, u32[]{:S(2)}) collective-permute-start(bf16[16,3584]{1,0:T(8,128)(2,1)S(1)} %add_convert_fusion), channel_id=1, source_target_pairs={{0,2},{1,3},{2,0},{3,1},{4,6},{5,7},{6,4},{7,5},{8,10},{9,11},{10,... | collective-permute-start | bytes 344072 | tf_op jit(solution)/shard_map/ppermute | solution.py:234
  36.8 0.0 collective-permute-done.10
  36.9 3.8 %collective-permute-done.12 = bf16[16,3584]{1,0:T(8,128)(2,1)S(1)} collective-permute-done((bf16[16,3584]{1,0:T(8,128)(2,1)S(1)}, bf16[16,3584]{1,0:T(8,128)(2,1)S(1)}, u32[]{:S(2)}, u32[]{:S(2)}) %collective-permute-start.12) | collective-permute-done | bytes 114720 | tf_op jit(solution)/shard_map/ppermute | solution.py:234
  40.7 1.7 %collective-permute-done.14 = bf16[16,3584]{1,0:T(8,128)(2,1)S(1)} collective-permute-done((bf16[16,3584]{1,0:T(8,128)(2,1)S(1)}, bf16[16,3584]{1,0:T(8,128)(2,1)S(1)}, u32[]{:S(2)}, u32[]{:S(2)}) %collective-permute-start.14) | collective-permute-done | bytes 114720 | tf_op jit(solution)/shard_map/ppermute | solution.py:234
  42.4 0.7 %pad_maximum_fusion = bf16[16,7168]{1,0:T(8,128)(2,1)} fusion(bf16[16,3584]{1,0:T(8,128)(2,1)S(1)} %get-tuple-element.64, bf16[16,3584]{1,0:T(8,128)(2,1)S(1)} %get-tuple-element.63), kind=kLoop, calls=%fused_computation.4 | loop fusion | flops 458752 | bytes 458752 | tf_op jit(solution)/shard_map/concatenate | solution.py:365
  (9 shorter events, 0.2 us)
Async XLA Ops:
  0.0 11.6 %collective-permute-start = (bf16[16,2048]{1,0:T(8,128)(2,1)}, bf16[16,2048]{1,0:T(8,128)(2,1)S(1)}, u32[]{:S(2)}, u32[]{:S(2)}) collective-permute-start(bf16[16,2048]{1,0:T(8,128)(2,1)} %refs_2_.1), channel_id=1, source_target_pairs={{0,8},{4,12},{8,0},{12,4},{16,24},{20,28},{24,16},{28,20},{1,9},{5... | collective-permute-start | bytes 196616 | tf_op jit(solution)/shard_map/ppermute | solution.py:231
  4.0 7.6 %collective-permute-start.2 = (bf16[16,2048]{1,0:T(8,128)(2,1)}, bf16[16,2048]{1,0:T(8,128)(2,1)S(1)}, u32[]{:S(2)}, u32[]{:S(2)}) collective-permute-start(bf16[16,2048]{1,0:T(8,128)(2,1)} %refs_2_.1), channel_id=1, source_target_pairs={{0,4},{4,0},{8,12},{12,8},{16,20},{20,16},{24,28},{28,24},{1,5},{5... | collective-permute-start | bytes 196616 | tf_op jit(solution)/shard_map/ppermute | solution.py:231
  5.6 6.3 %collective-permute-start.1 = (bf16[16,2048]{1,0:T(8,128)(2,1)}, bf16[16,2048]{1,0:T(8,128)(2,1)S(1)}, u32[]{:S(2)}, u32[]{:S(2)}) collective-permute-start(bf16[16,2048]{1,0:T(8,128)(2,1)} %refs_2_.1), channel_id=1, source_target_pairs={{0,12},{4,8},{8,4},{12,0},{16,28},{20,24},{24,20},{28,16},{1,13},{... | collective-permute-start | bytes 196616 | tf_op jit(solution)/shard_map/ppermute | solution.py:231
  9.6 12.8 %collective-permute-start.5 = (bf16[16,7168]{1,0:T(8,128)(2,1)S(1)}, bf16[16,7168]{1,0:T(8,128)(2,1)S(1)}, u32[]{:S(2)}, u32[]{:S(2)}) collective-permute-start(bf16[16,7168]{1,0:T(8,128)(2,1)S(1)} %get-tuple-element.43), channel_id=1, source_target_pairs={{0,8},{4,12},{8,0},{12,4},{16,28},{20,24},{24,20},{28,16},{1,9},{5... | collective-permute-start | bytes 688136 | tf_op jit(solution)/shard_map/ppermute | solution.py:231
  12.1 2.3 %collective-permute-start.3 = (f32[32,64]{1,0:T(8,128)S(1)}, f32[32,64]{1,0:T(8,128)S(1)}, u32[]{:S(2)}, u32[]{:S(2)}) collective-permute-start(f32[32,64]{1,0:T(8,128)S(1)} %get-tuple-element.42), channel_id=1, source_target_pairs={{0,1},{1,0},{2,3},{3,2},{4,5},{5,4},{6,7},{7,6},{8,9},{9,8},{10,11... | collective-permute-start | bytes 24584 | tf_op jit(solution)/shard_map/ppermute | solution.py:234
  12.2 20.3 %collective-permute-start.8 = (bf16[16,7168]{1,0:T(8,128)(2,1)S(1)}, bf16[16,7168]{1,0:T(8,128)(2,1)S(1)}, u32[]{:S(2)}, u32[]{:S(2)}) collective-permute-start(bf16[16,7168]{1,0:T(8,128)(2,1)S(1)} %get-tuple-element.56), channel_id=1, source_target_pairs={{0,4},{4,0},{8,12},{12,8},{16,20},{20,16},{24,28},{28,24},{1,5},{5... | collective-permute-start | bytes 688136 | tf_op jit(solution)/shard_map/ppermute | solution.py:231
  14.4 7.4 %collective-permute-start.4 = (f32[16,64]{1,0:T(8,128)S(1)}, f32[16,64]{1,0:T(8,128)S(1)}, u32[]{:S(2)}, u32[]{:S(2)}) collective-permute-start(f32[16,64]{1,0:T(8,128)S(1)} %slice.16), channel_id=1, source_target_pairs={{0,2},{1,3},{2,0},{3,1},{4,6},{5,7},{6,4},{7,5},{8,10},{9,11},{10,... | collective-permute-start | bytes 12296 | tf_op jit(solution)/shard_map/ppermute | solution.py:234
  22.3 10.2 %collective-permute-start.9 = (bf16[16,7168]{1,0:T(8,128)(2,1)S(1)}, bf16[16,7168]{1,0:T(8,128)(2,1)S(1)}, u32[]{:S(2)}, u32[]{:S(2)}) collective-permute-start(bf16[16,7168]{1,0:T(8,128)(2,1)S(1)} %collective-permute-done.5.refs_1_.refs_5_), channel_id=1, source_target_pairs={{0,16},{16,0},{1,17},{17,1},{2,18},{18,2},{3,19},{19,3},{4,20},{20... | collective-permute-start | bytes 688136 | tf_op jit(solution)/shard_map/ppermute | solution.py:237
  24.0 3.9 %collective-permute-start.6 = (bf16[16,64]{1,0:T(8,128)(2,1)S(1)}, bf16[16,64]{1,0:T(8,128)(2,1)S(1)}, u32[]{:S(2)}, u32[]{:S(2)}) collective-permute-start(bf16[16,64]{1,0:T(8,128)(2,1)S(1)} %fusion.3.refs_0_), channel_id=1, source_target_pairs={{0,4},{4,0},{8,12},{12,8},{16,20},{20,16},{24,28},{28,24},{1,5},{5... | collective-permute-start | bytes 6152 | tf_op jit(solution)/shard_map/ppermute | solution.py:231
  28.0 4.6 %collective-permute-start.7 = (bf16[16,64]{1,0:T(8,128)(2,1)S(1)}, bf16[16,64]{1,0:T(8,128)(2,1)S(1)}, u32[]{:S(2)}, u32[]{:S(2)}) collective-permute-start(bf16[16,64]{1,0:T(8,128)(2,1)S(1)} %add.29.refs_0_), channel_id=1, source_target_pairs={{0,8},{4,12},{8,0},{12,4},{16,24},{20,28},{24,16},{28,20},{1,9},{5... | collective-permute-start | bytes 6152 | tf_op jit(solution)/shard_map/ppermute | solution.py:231
  33.0 1.6 %collective-permute-start.11 = (f32[16,3584]{1,0:T(8,128)S(1)}, f32[16,3584]{1,0:T(8,128)S(1)}, u32[]{:S(2)}, u32[]{:S(2)}) collective-permute-start(f32[16,3584]{1,0:T(8,128)S(1)} %get-tuple-element.60), channel_id=1, source_target_pairs={{0,1},{1,0},{2,3},{3,2},{4,5},{5,4},{6,7},{7,6},{8,9},{9,8},{10,11... | collective-permute-start | bytes 688136 | tf_op jit(solution)/shard_map/ppermute | solution.py:234
  33.1 2.1 %collective-permute-start.13 = (f32[16,3584]{1,0:T(8,128)S(1)}, f32[16,3584]{1,0:T(8,128)S(1)}, u32[]{:S(2)}, u32[]{:S(2)}) collective-permute-start(f32[16,3584]{1,0:T(8,128)S(1)} %get-tuple-element.62), channel_id=1, source_target_pairs={{0,1},{1,0},{2,3},{3,2},{4,5},{5,4},{6,7},{7,6},{8,9},{9,8},{10,11... | collective-permute-start | bytes 688136 | tf_op jit(solution)/shard_map/ppermute | solution.py:234
  33.6 3.2 %collective-permute-start.10 = (f32[16,7168]{1,0:T(8,128)S(1)}, f32[16,7168]{1,0:T(8,128)S(1)}, u32[]{:S(2)}, u32[]{:S(2)}) collective-permute-start(f32[16,7168]{1,0:T(8,128)S(1)} %get-tuple-element.58), channel_id=1, source_target_pairs={{0,1},{1,0},{2,3},{3,2},{4,5},{5,4},{6,7},{7,6},{8,9},{9,8},{10,11... | collective-permute-start | bytes 1376264 | tf_op jit(solution)/shard_map/ppermute | solution.py:234
  34.6 6.1 %collective-permute-start.12 = (bf16[16,3584]{1,0:T(8,128)(2,1)S(1)}, bf16[16,3584]{1,0:T(8,128)(2,1)S(1)}, u32[]{:S(2)}, u32[]{:S(2)}) collective-permute-start(bf16[16,3584]{1,0:T(8,128)(2,1)S(1)} %add_convert_fusion.1), channel_id=1, source_target_pairs={{0,2},{1,3},{2,0},{3,1},{4,6},{5,7},{6,4},{7,5},{8,10},{9,11},{10,... | collective-permute-start | bytes 344072 | tf_op jit(solution)/shard_map/ppermute | solution.py:234
  35.2 7.1 %collective-permute-start.14 = (bf16[16,3584]{1,0:T(8,128)(2,1)S(1)}, bf16[16,3584]{1,0:T(8,128)(2,1)S(1)}, u32[]{:S(2)}, u32[]{:S(2)}) collective-permute-start(bf16[16,3584]{1,0:T(8,128)(2,1)S(1)} %add_convert_fusion), channel_id=1, source_target_pairs={{0,2},{1,3},{2,0},{3,1},{4,6},{5,7},{6,4},{7,5},{8,10},{9,11},{10,... | collective-permute-start | bytes 344072 | tf_op jit(solution)/shard_map/ppermute | solution.py:234

commit v19 on v15

--- a/solution.py
+++ b/solution.py
@@ -293,13 +293,12 @@
             if source not in used:
                 used.append(source)
             places.append((used.index(source), number - loads[source]))
-        near = n < 2
         ahead = pltpu.VMEM((len(numbers), depth, block), bf16)
         out = kernel_call(
             functools.partial(base_kernel, block, places, numbers, streamed),
             "base_part",
-            3 * 2 * row_count * depth * (last - first) * block if near else 1,
-            3 * 2 * depth * (last - first) * block if near else 1,
+            (15 * 10**8, 15 * 10**8, 10**10, 1)[n],
+            1,
             12,
             in_specs=[vmem, anywhere] + [vmem] * len(used) + [anywhere] * len(after),
             out_specs=[vmem] * (1 if streamed else 2),
@@ -317,18 +316,19 @@
     pair = keep + arrived
     arrived = from_tensor(pair[rank_block:], 2)
     base_1 = base_part(1, pair)
-    arrived, base_1, across = lax.optimization_barrier((arrived, base_1, across))
+    arrived, base_1 = lax.optimization_barrier((arrived, base_1))
     shrunk = (adapter_scale * (pair[:rank_block] + arrived)).astype(bf16)
+    across, _ = lax.optimization_barrier((across, shrunk))
     swapped = from_group(across)
     bases = [base_0, base_1]
-    for m, n in ((1, 2), (2, 3)):
+    for m, n in ((2, 2), (1, 3)):
         arrived = from_owner(shrunk, m, m)
         base = base_part(n, shrunk, across)
         arrived, base = lax.optimization_barrier((arrived, base))
         bases.append(base)
         shrunk = shrunk + arrived
 
-    middle = block_count // 2 * block
+    middle = block_count * 5 // 14 * block
     splits = [(0, middle), (middle, columns)]
     widths = [last - first for first, last in splits]
     quarter = row_count // 4
@@ -349,9 +349,11 @@
         ],
     )(slot, *bases, own, shrunk, across, beside, swapped)
     own_keep, own_send = out[:2]
-    crossed = []
-    for keep, send in zip(out[2:4], out[4:6]):
-        crossed.append(from_tensor((keep + from_tensor(send, 1)).astype(bf16), 2))
+    arrived = [from_tensor(x, 1) for x in out[4:6]]
+    arrived[1], own_send = lax.optimization_barrier((arrived[1], own_send))
+    crossed = [
+        from_tensor((keep + other).astype(bf16), 2) for keep, other in zip(out[2:4], arrived)
+    ]
     kept = own_keep + from_tensor(own_send, 1)
     return jnp.concatenate(
         [

time: 42.3 us -> 41 us (0.969)
  starting transfers between devices: 18 us -> 17.2 us
  waiting for transfers between devices: 7.63 us -> 7.09 us
    ppermute x7, starting transfers between devices: 12.8 us -> 11.7 us  [from_owner(): return lax.ppermute(x, ('groups', 'adapter'), pairs)]
    ppermute x7, waiting for transfers between devices: 1.25 us -> 0.47 us  [from_owner(): return lax.ppermute(x, ('groups', 'adapter'), pairs)]
  transfers between devices with their start and end apart: 15 -> 15, of which waited for: 5 -> 6; matrix products, arithmetic and copies ran while one was open for 0% -> 0% of each run, Pallas kernels for 36% -> 37%
where the time goes in v19:
time: 41 us; the launch traced here: 40.8 us
  starting transfers between devices  17.2 us (42%)
  Pallas kernels  15.5 us (38%)
  waiting for transfers between devices  7.09 us (17%)
  other arithmetic  0.89 us (2%)
    ppermute x7, starting transfers between devices, from_owner(): return lax.ppermute(x, ('groups', 'adapter'), pairs)  11.7 us
    pallas_call x4, Pallas kernels, base_part(): kernel_call(functools.partial(base_kernel, block, places, numbers, stream...  10.8 us
    ppermute x7, waiting for transfers between devices, from_tensor(): return lax.ppermute(x, 'tensor', [(s, s ^ m) for s in range(4)])  6.33 us
    ppermute x7, starting transfers between devices, from_tensor(): return lax.ppermute(x, 'tensor', [(s, s ^ m) for s in range(4)])  4.36 us
    pallas_call x1, Pallas kernels, paired(): kernel_call(functools.partial(cut_kernel, block, range(loads[1]), len(sma...  3.94 us
    ppermute x1, starting transfers between devices, from_group(): return lax.ppermute(x, 'groups', [(0, 1), (1, 0)])  1.19 us
  transfers between devices with their start and end apart: 15, of which 6 were waited for; matrix products, arithmetic and copies ran while one was open for 0% of the time, Pallas kernels for 37%

profile of v19, /device:TPU:0, one launch (start us, length us, event | category | flops | bytes accessed | tf_op | source)
XLA Modules:
  0.0 40.8 jit_solution(8729494974495790273)
XLA Ops:
  0.0 4.0 %collective-permute-start = (bf16[16,2048]{1,0:T(8,128)(2,1)}, bf16[16,2048]{1,0:T(8,128)(2,1)S(1)}, u32[]{:S(2)}, u32[]{:S(2)}) collective-permute-start(bf16[16,2048]{1,0:T(8,128)(2,1)} %refs_2_.1), channel_id=1, source_target_pairs={{0,8},{4,12},{8,0},{12,4},{16,24},{20,28},{24,16},{28,20},{1,9},{5... | collective-permute-start | bytes 196616 | tf_op jit(solution)/shard_map/ppermute | solution.py:221
  4.0 1.3 %collective-permute-start.1 = (bf16[16,2048]{1,0:T(8,128)(2,1)}, bf16[16,2048]{1,0:T(8,128)(2,1)S(1)}, u32[]{:S(2)}, u32[]{:S(2)}) collective-permute-start(bf16[16,2048]{1,0:T(8,128)(2,1)} %refs_2_.1), channel_id=1, source_target_pairs={{0,12},{4,8},{8,4},{12,0},{16,28},{20,24},{24,20},{28,16},{1,13},{... | collective-permute-start | bytes 196616 | tf_op jit(solution)/shard_map/ppermute | solution.py:221
  5.4 0.2 collective-permute-start.2
  5.6 3.9 %cut_expand.1 = (bf16[16,7168]{1,0:T(8,128)(2,1)S(1)}, bf16[16,7168]{1,0:T(8,128)(2,1)S(1)}, bf16[16,7168]{1,0:T(8,128)(2,1)S(1)}, s32[1,4]{1,0:T(1,128)S(1)}, s...) custom-call(bf16[1,16,28672]{2,1,0:T(8,128)(2,1)} %expand.1, ...), custom_call_target="tpu_custom_call" | custom-call | flops 1 | bytes 1 | tf_op jit(solution)/shard_map/cut_expand/pallas_call | solution.py:247
  9.6 2.9 %collective-permute-start.6 = (bf16[16,7168]{1,0:T(8,128)(2,1)S(1)}, bf16[16,7168]{1,0:T(8,128)(2,1)S(1)}, u32[]{:S(2)}, u32[]{:S(2)}) collective-permute-start(bf16[16,7168]{1,0:T(8,128)(2,1)S(1)} %get-tuple-element.57), channel_id=1, source_target_pairs={{0,8},{4,12},{8,0},{12,4},{16,28},{20,24},{24,20},{28,16},{1,9},{5... | collective-permute-start | bytes 688136 | tf_op jit(solution)/shard_map/ppermute | solution.py:221
  12.5 0.6 %collective-permute-start.8 = (bf16[16,7168]{1,0:T(8,128)(2,1)S(1)}, bf16[16,7168]{1,0:T(8,128)(2,1)S(1)}, u32[]{:S(2)}, u32[]{:S(2)}) collective-permute-start(bf16[16,7168]{1,0:T(8,128)(2,1)S(1)} %get-tuple-element.66), channel_id=1, source_target_pairs={{0,4},{4,0},{8,12},{12,8},{16,20},{20,16},{24,28},{28,24},{1,5},{5... | collective-permute-start | bytes 688136 | tf_op jit(solution)/shard_map/ppermute | solution.py:221
  13.1 0.0 collective-permute-done.refs_1_
  13.1 0.0 collective-permute-done.1.refs_2_
  13.1 0.0 collective-permute-done.2.refs_3_
  13.1 0.3 gather_rows.1
  13.4 0.1 collective-permute-start.3
  13.5 3.6 %base_part.4 = (f32[64,2048]{1,0:T(8,128)S(1)}, bf16[4,2048,512]{2,1,0:T(8,128)(2,1)S(1)}) custom-call(bf16[64,2048]{1,0:T(8,128)(2,1)S(1)} %get-tuple-element.46.rows, bf16[2048,7168]{1,0:T(8,128)(2,1)} %weight.9, bf16[4,2048,512]{2,1,0:T(8,128)(2,1)S(1)} %get-tuple-element.47.refs_0_, f32[32,64]{1,0:T(8,128)S(1)} %get-tuple-element.45.refs_1_), custom_call_target="tpu_custom_call" | custom-call | flops 1500000000 | bytes 1 | tf_op jit(solution)/shard_map/base_part/pallas_call | solution.py:297
  17.1 0.0 collective-permute-done.3
  17.1 1.6 %collective-permute-start.4 = (f32[16,64]{1,0:T(8,128)S(1)}, f32[16,64]{1,0:T(8,128)S(1)}, u32[]{:S(2)}, u32[]{:S(2)}) collective-permute-start(f32[16,64]{1,0:T(8,128)S(1)} %slice.16), channel_id=1, source_target_pairs={{0,2},{1,3},{2,0},{3,1},{4,6},{5,7},{6,4},{7,5},{8,10},{9,11},{10,... | collective-permute-start | bytes 12296 | tf_op jit(solution)/shard_map/ppermute | solution.py:224
  18.7 3.0 %base_part.5 = (f32[64,2048]{1,0:T(8,128)S(1)}, bf16[3,2048,512]{2,1,0:T(8,128)(2,1)S(1)}) custom-call(bf16[64,2048]{1,0:T(8,128)(2,1)S(1)} %get-tuple-element.46.rows, bf16[2048,7168]{1,0:T(8,128)(2,1)} %weight.9, bf16[4,2048,512]{2,1,0:T(8,128)(2,1)S(1)} %get-tuple-element.52.refs_0_, f32[32,64]{1,0:T(8,128)S(1)} %add.27.refs_1_), custom_call_target="tpu_custom_call" | custom-call | flops 1500000000 | bytes 1 | tf_op jit(solution)/shard_map/base_part/pallas_call | solution.py:297
  21.6 0.0 collective-permute-done.4
  21.7 1.3 %collective-permute-start.5 = (bf16[16,64]{1,0:T(8,128)(2,1)S(1)}, bf16[16,64]{1,0:T(8,128)(2,1)S(1)}, u32[]{:S(2)}, u32[]{:S(2)}) collective-permute-start(bf16[16,64]{1,0:T(8,128)(2,1)S(1)} %fusion.3.refs_1_), channel_id=1, source_target_pairs={{0,8},{4,12},{8,0},{12,4},{16,24},{20,28},{24,16},{28,20},{1,9},{5... | collective-permute-start | bytes 6152 | tf_op jit(solution)/shard_map/ppermute | solution.py:221
  23.0 0.0 collective-permute-done.6.refs_2_.refs_6_
  23.0 1.2 %collective-permute-start.9 = (bf16[16,7168]{1,0:T(8,128)(2,1)S(1)}, bf16[16,7168]{1,0:T(8,128)(2,1)S(1)}, u32[]{:S(2)}, u32[]{:S(2)}) collective-permute-start(bf16[16,7168]{1,0:T(8,128)(2,1)S(1)} %collective-permute-done.6.refs_2_.refs_6_), channel_id=1, source_target_pairs={{0,16},{16,0},{1,17},{17,1},{2,18},{18,2},{3,19},{19,3},{4,20},{20... | collective-permute-start | bytes 688136 | tf_op jit(solution)/shard_map/ppermute | solution.py:227
  24.2 2.2 %base_part.6 = (f32[64,1536]{1,0:T(8,128)S(1)}, bf16[2,2048,512]{2,1,0:T(8,128)(2,1)S(1)}) custom-call(bf16[64,2048]{1,0:T(8,128)(2,1)S(1)} %get-tuple-element.46.rows, bf16[2048,7168]{1,0:T(8,128)(2,1)} %weight.9, bf16[3,2048,512]{2,1,0:T(8,128)(2,1)S(1)} %get-tuple-element.56.refs_0_, bf16[16,64]{1,0:T(8,128)(2,1)S(1)} %fusion.3.refs_1_, ...), custom_call_target="tpu_custom_call" | custom-call | flops 10000000000 | bytes 1 | tf_op jit(solution)/shard_map/base_part/pallas_call | solution.py:297
  26.4 0.0 collective-permute-done.5
  26.4 1.2 %collective-permute-start.7 = (bf16[16,64]{1,0:T(8,128)(2,1)S(1)}, bf16[16,64]{1,0:T(8,128)(2,1)S(1)}, u32[]{:S(2)}, u32[]{:S(2)}) collective-permute-start(bf16[16,64]{1,0:T(8,128)(2,1)S(1)} %add.29.refs_1_), channel_id=1, source_target_pairs={{0,4},{4,0},{8,12},{12,8},{16,20},{20,16},{24,28},{28,24},{1,5},{5... | collective-permute-start | bytes 6152 | tf_op jit(solution)/shard_map/ppermute | solution.py:221
  27.6 2.0 %base_part.7.refs_3_ = f32[64,1536]{1,0:T(8,128)S(1)} custom-call(bf16[64,2048]{1,0:T(8,128)(2,1)S(1)} %get-tuple-element.46.rows, bf16[2048,7168]{1,0:T(8,128)(2,1)} %weight.9, bf16[2,2048,512]{2,1,0:T(8,128)(2,1)S(1)} %get-tuple-element.62.refs_0_, bf16[16,64]{1,0:T(8,128)(2,1)S(1)} %add.29.refs_1_, bf16[16,7168]{1,0:T(8,128)(2,1)S(1)} %collective-permute-done.6.refs_2_.refs_6_), custom_call_target="tpu_custom_call" | custom-call | flops 1 | bytes 1 | tf_op jit(solution)/shard_map/base_part/pallas_call | solution.py:297
  29.7 0.5 %collective-permute-done.7 = bf16[16,64]{1,0:T(8,128)(2,1)S(1)} collective-permute-done((bf16[16,64]{1,0:T(8,128)(2,1)S(1)}, bf16[16,64]{1,0:T(8,128)(2,1)S(1)}, u32[]{:S(2)}, u32[]{:S(2)}) %collective-permute-start.7) | collective-permute-done | bytes 2080 | tf_op jit(solution)/shard_map/ppermute | solution.py:221
  30.1 0.0 collective-permute-done.8.refs_7_
  30.1 0.3 collective-permute-done.9.refs_8_
  30.4 0.5 %add_delta.1 = (f32[16,7168]{1,0:T(8,128)S(1)}, f32[16,7168]{1,0:T(8,128)S(1)}, f32[16,2560]{1,0:T(8,128)S(1)}, f32[16,4608]{1,0:T(8,128)S(1)}, f32[16,2560]{1,0:T(8,128)S(1)}, /*index=5*/f32[16,4608]{1,0:T(8,128)S(1)}) custom-call(s32[1,64]{1,0:T(1,128)S(1)} %get-tuple-element.44.slot, f32[64,2048]{1,0:T(8,128)S(1)} %get-tuple-element.49.refs_0_, ...), custom_call_target="tpu_custom_call" | custom-call | flops 1 | bytes 1 | tf_op jit(solution)/shard_map/add_delta/pallas_call | solution.py:335
  30.9 0.1 collective-permute-start.12
  31.0 0.5 %collective-permute-start.10 = (f32[16,4608]{1,0:T(8,128)S(1)}, f32[16,4608]{1,0:T(8,128)S(1)}, u32[]{:S(2)}, u32[]{:S(2)}) collective-permute-start(f32[16,4608]{1,0:T(8,128)S(1)} %get-tuple-element.68), channel_id=1, source_target_pairs={{0,1},{1,0},{2,3},{3,2},{4,5},{5,4},{6,7},{7,6},{8,9},{9,8},{10,11... | collective-permute-start | bytes 884744 | tf_op jit(solution)/shard_map/ppermute | solution.py:224
  31.5 0.9 %collective-permute-done.12 = f32[16,2560]{1,0:T(8,128)S(1)} collective-permute-done((f32[16,2560]{1,0:T(8,128)S(1)}, f32[16,2560]{1,0:T(8,128)S(1)}, u32[]{:S(2)}, u32[]{:S(2)}) %collective-permute-start.12) | collective-permute-done | bytes 163872 | tf_op jit(solution)/shard_map/ppermute | solution.py:224
  32.4 0.6 %collective-permute-start.13 = (bf16[16,2560]{1,0:T(8,128)(2,1)S(1)}, bf16[16,2560]{1,0:T(8,128)(2,1)S(1)}, u32[]{:S(2)}, u32[]{:S(2)}) collective-permute-start(bf16[16,2560]{1,0:T(8,128)(2,1)S(1)} %add_convert_fusion.1), channel_id=1, source_target_pairs={{0,2},{1,3},{2,0},{3,1},{4,6},{5,7},{6,4},{7,5},{8,10},{9,11},{10,... | collective-permute-start | bytes 245768 | tf_op jit(solution)/shard_map/ppermute | solution.py:224
  33.0 0.0 collective-permute-done.10
  33.0 0.1 collective-permute-start.11
  33.1 1.5 %collective-permute-start.14 = (bf16[16,4608]{1,0:T(8,128)(2,1)S(1)}, bf16[16,4608]{1,0:T(8,128)(2,1)S(1)}, u32[]{:S(2)}, u32[]{:S(2)}) collective-permute-start(bf16[16,4608]{1,0:T(8,128)(2,1)S(1)} %add_convert_fusion), channel_id=1, source_target_pairs={{0,2},{1,3},{2,0},{3,1},{4,6},{5,7},{6,4},{7,5},{8,10},{9,11},{10,... | collective-permute-start | bytes 442376 | tf_op jit(solution)/shard_map/ppermute | solution.py:224
  34.6 0.2 collective-permute-done.11
  34.9 2.8 %collective-permute-done.13 = bf16[16,2560]{1,0:T(8,128)(2,1)S(1)} collective-permute-done((bf16[16,2560]{1,0:T(8,128)(2,1)S(1)}, bf16[16,2560]{1,0:T(8,128)(2,1)S(1)}, u32[]{:S(2)}, u32[]{:S(2)}) %collective-permute-start.13) | collective-permute-done | bytes 81952 | tf_op jit(solution)/shard_map/ppermute | solution.py:224
  37.7 2.4 %collective-permute-done.14 = bf16[16,4608]{1,0:T(8,128)(2,1)S(1)} collective-permute-done((bf16[16,4608]{1,0:T(8,128)(2,1)S(1)}, bf16[16,4608]{1,0:T(8,128)(2,1)S(1)}, u32[]{:S(2)}, u32[]{:S(2)}) %collective-permute-start.14) | collective-permute-done | bytes 147488 | tf_op jit(solution)/shard_map/ppermute | solution.py:224
  40.1 0.7 %pad_maximum_fusion = bf16[16,7168]{1,0:T(8,128)(2,1)} fusion(bf16[16,4608]{1,0:T(8,128)(2,1)S(1)} %fusion, bf16[16,2560]{1,0:T(8,128)(2,1)S(1)} %fusion.1), kind=kLoop, calls=%fused_computation.3 | loop fusion | flops 458752 | bytes 458752 | tf_op jit(solution)/shard_map/concatenate | solution.py:358
  (10 shorter events, 0.2 us)
Async XLA Ops:
  0.0 13.1 %collective-permute-start = (bf16[16,2048]{1,0:T(8,128)(2,1)}, bf16[16,2048]{1,0:T(8,128)(2,1)S(1)}, u32[]{:S(2)}, u32[]{:S(2)}) collective-permute-start(bf16[16,2048]{1,0:T(8,128)(2,1)} %refs_2_.1), channel_id=1, source_target_pairs={{0,8},{4,12},{8,0},{12,4},{16,24},{20,28},{24,16},{28,20},{1,9},{5... | collective-permute-start | bytes 196616 | tf_op jit(solution)/shard_map/ppermute | solution.py:221
  4.0 9.1 %collective-permute-start.1 = (bf16[16,2048]{1,0:T(8,128)(2,1)}, bf16[16,2048]{1,0:T(8,128)(2,1)S(1)}, u32[]{:S(2)}, u32[]{:S(2)}) collective-permute-start(bf16[16,2048]{1,0:T(8,128)(2,1)} %refs_2_.1), channel_id=1, source_target_pairs={{0,12},{4,8},{8,4},{12,0},{16,28},{20,24},{24,20},{28,16},{1,13},{... | collective-permute-start | bytes 196616 | tf_op jit(solution)/shard_map/ppermute | solution.py:221
  5.4 7.7 %collective-permute-start.2 = (bf16[16,2048]{1,0:T(8,128)(2,1)}, bf16[16,2048]{1,0:T(8,128)(2,1)S(1)}, u32[]{:S(2)}, u32[]{:S(2)}) collective-permute-start(bf16[16,2048]{1,0:T(8,128)(2,1)} %refs_2_.1), channel_id=1, source_target_pairs={{0,4},{4,0},{8,12},{12,8},{16,20},{20,16},{24,28},{28,24},{1,5},{5... | collective-permute-start | bytes 196616 | tf_op jit(solution)/shard_map/ppermute | solution.py:221
  9.6 13.4 %collective-permute-start.6 = (bf16[16,7168]{1,0:T(8,128)(2,1)S(1)}, bf16[16,7168]{1,0:T(8,128)(2,1)S(1)}, u32[]{:S(2)}, u32[]{:S(2)}) collective-permute-start(bf16[16,7168]{1,0:T(8,128)(2,1)S(1)} %get-tuple-element.57), channel_id=1, source_target_pairs={{0,8},{4,12},{8,0},{12,4},{16,28},{20,24},{24,20},{28,16},{1,9},{5... | collective-permute-start | bytes 688136 | tf_op jit(solution)/shard_map/ppermute | solution.py:221
  12.5 17.6 %collective-permute-start.8 = (bf16[16,7168]{1,0:T(8,128)(2,1)S(1)}, bf16[16,7168]{1,0:T(8,128)(2,1)S(1)}, u32[]{:S(2)}, u32[]{:S(2)}) collective-permute-start(bf16[16,7168]{1,0:T(8,128)(2,1)S(1)} %get-tuple-element.66), channel_id=1, source_target_pairs={{0,4},{4,0},{8,12},{12,8},{16,20},{20,16},{24,28},{28,24},{1,5},{5... | collective-permute-start | bytes 688136 | tf_op jit(solution)/shard_map/ppermute | solution.py:221
  13.4 3.7 %collective-permute-start.3 = (f32[32,64]{1,0:T(8,128)S(1)}, f32[32,64]{1,0:T(8,128)S(1)}, u32[]{:S(2)}, u32[]{:S(2)}) collective-permute-start(f32[32,64]{1,0:T(8,128)S(1)} %get-tuple-element.45.refs_1_), channel_id=1, source_target_pairs={{0,1},{1,0},{2,3},{3,2},{4,5},{5,4},{6,7},{7,6},{8,9},{9,8},{10,11... | collective-permute-start | bytes 24584 | tf_op jit(solution)/shard_map/ppermute | solution.py:224
  17.1 4.5 %collective-permute-start.4 = (f32[16,64]{1,0:T(8,128)S(1)}, f32[16,64]{1,0:T(8,128)S(1)}, u32[]{:S(2)}, u32[]{:S(2)}) collective-permute-start(f32[16,64]{1,0:T(8,128)S(1)} %slice.16), channel_id=1, source_target_pairs={{0,2},{1,3},{2,0},{3,1},{4,6},{5,7},{6,4},{7,5},{8,10},{9,11},{10,... | collective-permute-start | bytes 12296 | tf_op jit(solution)/shard_map/ppermute | solution.py:224
  21.7 4.8 %collective-permute-start.5 = (bf16[16,64]{1,0:T(8,128)(2,1)S(1)}, bf16[16,64]{1,0:T(8,128)(2,1)S(1)}, u32[]{:S(2)}, u32[]{:S(2)}) collective-permute-start(bf16[16,64]{1,0:T(8,128)(2,1)S(1)} %fusion.3.refs_1_), channel_id=1, source_target_pairs={{0,8},{4,12},{8,0},{12,4},{16,24},{20,28},{24,16},{28,20},{1,9},{5... | collective-permute-start | bytes 6152 | tf_op jit(solution)/shard_map/ppermute | solution.py:221
  23.0 7.4 %collective-permute-start.9 = (bf16[16,7168]{1,0:T(8,128)(2,1)S(1)}, bf16[16,7168]{1,0:T(8,128)(2,1)S(1)}, u32[]{:S(2)}, u32[]{:S(2)}) collective-permute-start(bf16[16,7168]{1,0:T(8,128)(2,1)S(1)} %collective-permute-done.6.refs_2_.refs_6_), channel_id=1, source_target_pairs={{0,16},{16,0},{1,17},{17,1},{2,18},{18,2},{3,19},{19,3},{4,20},{20... | collective-permute-start | bytes 688136 | tf_op jit(solution)/shard_map/ppermute | solution.py:227
  26.4 3.7 %collective-permute-start.7 = (bf16[16,64]{1,0:T(8,128)(2,1)S(1)}, bf16[16,64]{1,0:T(8,128)(2,1)S(1)}, u32[]{:S(2)}, u32[]{:S(2)}) collective-permute-start(bf16[16,64]{1,0:T(8,128)(2,1)S(1)} %add.29.refs_1_), channel_id=1, source_target_pairs={{0,4},{4,0},{8,12},{12,8},{16,20},{20,16},{24,28},{28,24},{1,5},{5... | collective-permute-start | bytes 6152 | tf_op jit(solution)/shard_map/ppermute | solution.py:221
  30.9 1.5 %collective-permute-start.12 = (f32[16,2560]{1,0:T(8,128)S(1)}, f32[16,2560]{1,0:T(8,128)S(1)}, u32[]{:S(2)}, u32[]{:S(2)}) collective-permute-start(f32[16,2560]{1,0:T(8,128)S(1)} %get-tuple-element.72), channel_id=1, source_target_pairs={{0,1},{1,0},{2,3},{3,2},{4,5},{5,4},{6,7},{7,6},{8,9},{9,8},{10,11... | collective-permute-start | bytes 491528 | tf_op jit(solution)/shard_map/ppermute | solution.py:224
  31.0 2.0 %collective-permute-start.10 = (f32[16,4608]{1,0:T(8,128)S(1)}, f32[16,4608]{1,0:T(8,128)S(1)}, u32[]{:S(2)}, u32[]{:S(2)}) collective-permute-start(f32[16,4608]{1,0:T(8,128)S(1)} %get-tuple-element.68), channel_id=1, source_target_pairs={{0,1},{1,0},{2,3},{3,2},{4,5},{5,4},{6,7},{7,6},{8,9},{9,8},{10,11... | collective-permute-start | bytes 884744 | tf_op jit(solution)/shard_map/ppermute | solution.py:224
  32.4 5.3 %collective-permute-start.13 = (bf16[16,2560]{1,0:T(8,128)(2,1)S(1)}, bf16[16,2560]{1,0:T(8,128)(2,1)S(1)}, u32[]{:S(2)}, u32[]{:S(2)}) collective-permute-start(bf16[16,2560]{1,0:T(8,128)(2,1)S(1)} %add_convert_fusion.1), channel_id=1, source_target_pairs={{0,2},{1,3},{2,0},{3,1},{4,6},{5,7},{6,4},{7,5},{8,10},{9,11},{10,... | collective-permute-start | bytes 245768 | tf_op jit(solution)/shard_map/ppermute | solution.py:224
  33.0 1.8 %collective-permute-start.11 = (f32[16,7168]{1,0:T(8,128)S(1)}, f32[16,7168]{1,0:T(8,128)S(1)}, u32[]{:S(2)}, u32[]{:S(2)}) collective-permute-start(f32[16,7168]{1,0:T(8,128)S(1)} %get-tuple-element.70), channel_id=1, source_target_pairs={{0,1},{1,0},{2,3},{3,2},{4,5},{5,4},{6,7},{7,6},{8,9},{9,8},{10,11... | collective-permute-start | bytes 1376264 | tf_op jit(solution)/shard_map/ppermute | solution.py:224
  33.1 7.0 %collective-permute-start.14 = (bf16[16,4608]{1,0:T(8,128)(2,1)S(1)}, bf16[16,4608]{1,0:T(8,128)(2,1)S(1)}, u32[]{:S(2)}, u32[]{:S(2)}) collective-permute-start(bf16[16,4608]{1,0:T(8,128)(2,1)S(1)} %add_convert_fusion), channel_id=1, source_target_pairs={{0,2},{1,3},{2,0},{3,1},{4,6},{5,7},{6,4},{7,5},{8,10},{9,11},{10,... | collective-permute-start | bytes 442376 | tf_op jit(solution)/shard_map/ppermute | solution.py:224

commit v20 on v19

--- a/solution.py
+++ b/solution.py
@@ -328,8 +328,8 @@
         bases.append(base)
         shrunk = shrunk + arrived
 
-    middle = block_count * 5 // 14 * block
-    splits = [(0, middle), (middle, columns)]
+    edges = [block_count * k // 14 * block for k in (0, 4, 9, 14)]
+    splits = list(zip(edges[:-1], edges[1:]))
     widths = [last - first for first, last in splits]
     quarter = row_count // 4
     out = kernel_call(
@@ -349,10 +349,11 @@
         ],
     )(slot, *bases, own, shrunk, across, beside, swapped)
     own_keep, own_send = out[:2]
-    arrived = [from_tensor(x, 1) for x in out[4:6]]
-    arrived[1], own_send = lax.optimization_barrier((arrived[1], own_send))
+    cross_keep, cross_send = out[2 : 2 + len(splits)], out[2 + len(splits) :]
+    arrived = [from_tensor(x, 1) for x in cross_send]
+    arrived[-1], own_send = lax.optimization_barrier((arrived[-1], own_send))
     crossed = [
-        from_tensor((keep + other).astype(bf16), 2) for keep, other in zip(out[2:4], arrived)
+        from_tensor((keep + other).astype(bf16), 2) for keep, other in zip(cross_keep, arrived)
     ]
     kept = own_keep + from_tensor(own_send, 1)
     return jnp.concatenate(

time: 41 us -> 41.1 us (level)
  starting transfers between devices: 17.2 us -> 17.9 us
  waiting for transfers between devices: 7.09 us -> 6.47 us
    ppermute x7 -> x9, starting transfers between devices: 4.36 us -> 5.05 us  [from_tensor(): return lax.ppermute(x, 'tensor', [(s, s ^ m) for s in range(4)])]
    ppermute x7 -> x9, waiting for transfers between devices: 6.33 us -> 5.71 us  [from_tensor(): return lax.ppermute(x, 'tensor', [(s, s ^ m) for s in range(4)])]
  transfers between devices with their start and end apart: 15 -> 17, of which waited for: 6 -> 6; matrix products, arithmetic and copies ran while one was open for 0% -> 0% of each run, Pallas kernels for 37% -> 37%
where the time goes in v20:
time: 41.1 us; the launch traced here: 40.9 us
  starting transfers between devices  17.9 us (44%)
  Pallas kernels  15.5 us (38%)
  waiting for transfers between devices  6.47 us (16%)
  other arithmetic  0.87 us (2%)
    ppermute x7, starting transfers between devices, from_owner(): return lax.ppermute(x, ('groups', 'adapter'), pairs)  11.7 us
    pallas_call x4, Pallas kernels, base_part(): kernel_call(functools.partial(base_kernel, block, places, numbers, stream...  10.8 us
    ppermute x9, waiting for transfers between devices, from_tensor(): return lax.ppermute(x, 'tensor', [(s, s ^ m) for s in range(4)])  5.71 us
    ppermute x9, starting transfers between devices, from_tensor(): return lax.ppermute(x, 'tensor', [(s, s ^ m) for s in range(4)])  5.05 us
    pallas_call x1, Pallas kernels, paired(): kernel_call(functools.partial(cut_kernel, block, range(loads[1]), len(sma...  3.94 us
    ppermute x1, starting transfers between devices, from_group(): return lax.ppermute(x, 'groups', [(0, 1), (1, 0)])  1.19 us
  transfers between devices with their start and end apart: 17, of which 6 were waited for; matrix products, arithmetic and copies ran while one was open for 0% of the time, Pallas kernels for 37%

profile of v20, /device:TPU:0, one launch (start us, length us, event | category | flops | bytes accessed | tf_op | source)
XLA Modules:
  0.0 40.9 jit_solution(2829932181539899149)
XLA Ops:
  0.0 4.0 %collective-permute-start = (bf16[16,2048]{1,0:T(8,128)(2,1)}, bf16[16,2048]{1,0:T(8,128)(2,1)S(1)}, u32[]{:S(2)}, u32[]{:S(2)}) collective-permute-start(bf16[16,2048]{1,0:T(8,128)(2,1)} %refs_2_.1), channel_id=1, source_target_pairs={{0,8},{4,12},{8,0},{12,4},{16,24},{20,28},{24,16},{28,20},{1,9},{5... | collective-permute-start | bytes 196616 | tf_op jit(solution)/shard_map/ppermute | solution.py:221
  4.0 1.3 %collective-permute-start.1 = (bf16[16,2048]{1,0:T(8,128)(2,1)}, bf16[16,2048]{1,0:T(8,128)(2,1)S(1)}, u32[]{:S(2)}, u32[]{:S(2)}) collective-permute-start(bf16[16,2048]{1,0:T(8,128)(2,1)} %refs_2_.1), channel_id=1, source_target_pairs={{0,12},{4,8},{8,4},{12,0},{16,28},{20,24},{24,20},{28,16},{1,13},{... | collective-permute-start | bytes 196616 | tf_op jit(solution)/shard_map/ppermute | solution.py:221
  5.4 0.2 collective-permute-start.2
  5.6 3.9 %cut_expand.1 = (bf16[16,7168]{1,0:T(8,128)(2,1)S(1)}, bf16[16,7168]{1,0:T(8,128)(2,1)S(1)}, bf16[16,7168]{1,0:T(8,128)(2,1)S(1)}, s32[1,4]{1,0:T(1,128)S(1)}, s...) custom-call(bf16[1,16,28672]{2,1,0:T(8,128)(2,1)} %expand.1, ...), custom_call_target="tpu_custom_call" | custom-call | flops 1 | bytes 1 | tf_op jit(solution)/shard_map/cut_expand/pallas_call | solution.py:247
  9.6 2.9 %collective-permute-start.6 = (bf16[16,7168]{1,0:T(8,128)(2,1)S(1)}, bf16[16,7168]{1,0:T(8,128)(2,1)S(1)}, u32[]{:S(2)}, u32[]{:S(2)}) collective-permute-start(bf16[16,7168]{1,0:T(8,128)(2,1)S(1)} %get-tuple-element.59), channel_id=1, source_target_pairs={{0,8},{4,12},{8,0},{12,4},{16,28},{20,24},{24,20},{28,16},{1,9},{5... | collective-permute-start | bytes 688136 | tf_op jit(solution)/shard_map/ppermute | solution.py:221
  12.5 0.6 %collective-permute-start.8 = (bf16[16,7168]{1,0:T(8,128)(2,1)S(1)}, bf16[16,7168]{1,0:T(8,128)(2,1)S(1)}, u32[]{:S(2)}, u32[]{:S(2)}) collective-permute-start(bf16[16,7168]{1,0:T(8,128)(2,1)S(1)} %get-tuple-element.68), channel_id=1, source_target_pairs={{0,4},{4,0},{8,12},{12,8},{16,20},{20,16},{24,28},{28,24},{1,5},{5... | collective-permute-start | bytes 688136 | tf_op jit(solution)/shard_map/ppermute | solution.py:221
  13.1 0.0 collective-permute-done.refs_1_
  13.1 0.0 collective-permute-done.1.refs_2_
  13.1 0.0 collective-permute-done.2.refs_3_
  13.1 0.3 gather_rows.1
  13.4 0.1 collective-permute-start.3
  13.5 3.6 %base_part.4 = (f32[64,2048]{1,0:T(8,128)S(1)}, bf16[4,2048,512]{2,1,0:T(8,128)(2,1)S(1)}) custom-call(bf16[64,2048]{1,0:T(8,128)(2,1)S(1)} %get-tuple-element.48.rows, bf16[2048,7168]{1,0:T(8,128)(2,1)} %weight.9, bf16[4,2048,512]{2,1,0:T(8,128)(2,1)S(1)} %get-tuple-element.49.refs_0_, f32[32,64]{1,0:T(8,128)S(1)} %get-tuple-element.47.refs_1_), custom_call_target="tpu_custom_call" | custom-call | flops 1500000000 | bytes 1 | tf_op jit(solution)/shard_map/base_part/pallas_call | solution.py:297
  17.1 0.0 collective-permute-done.3
  17.1 1.6 %collective-permute-start.4 = (f32[16,64]{1,0:T(8,128)S(1)}, f32[16,64]{1,0:T(8,128)S(1)}, u32[]{:S(2)}, u32[]{:S(2)}) collective-permute-start(f32[16,64]{1,0:T(8,128)S(1)} %slice.20), channel_id=1, source_target_pairs={{0,2},{1,3},{2,0},{3,1},{4,6},{5,7},{6,4},{7,5},{8,10},{9,11},{10,... | collective-permute-start | bytes 12296 | tf_op jit(solution)/shard_map/ppermute | solution.py:224
  18.7 3.0 %base_part.5 = (f32[64,2048]{1,0:T(8,128)S(1)}, bf16[3,2048,512]{2,1,0:T(8,128)(2,1)S(1)}) custom-call(bf16[64,2048]{1,0:T(8,128)(2,1)S(1)} %get-tuple-element.48.rows, bf16[2048,7168]{1,0:T(8,128)(2,1)} %weight.9, bf16[4,2048,512]{2,1,0:T(8,128)(2,1)S(1)} %get-tuple-element.54.refs_0_, f32[32,64]{1,0:T(8,128)S(1)} %add.33.refs_1_), custom_call_target="tpu_custom_call" | custom-call | flops 1500000000 | bytes 1 | tf_op jit(solution)/shard_map/base_part/pallas_call | solution.py:297
  21.6 0.0 collective-permute-done.4
  21.7 1.3 %collective-permute-start.5 = (bf16[16,64]{1,0:T(8,128)(2,1)S(1)}, bf16[16,64]{1,0:T(8,128)(2,1)S(1)}, u32[]{:S(2)}, u32[]{:S(2)}) collective-permute-start(bf16[16,64]{1,0:T(8,128)(2,1)S(1)} %fusion.4.refs_1_), channel_id=1, source_target_pairs={{0,8},{4,12},{8,0},{12,4},{16,24},{20,28},{24,16},{28,20},{1,9},{5... | collective-permute-start | bytes 6152 | tf_op jit(solution)/shard_map/ppermute | solution.py:221
  23.0 0.0 collective-permute-done.6.refs_2_.refs_6_
  23.0 1.2 %collective-permute-start.9 = (bf16[16,7168]{1,0:T(8,128)(2,1)S(1)}, bf16[16,7168]{1,0:T(8,128)(2,1)S(1)}, u32[]{:S(2)}, u32[]{:S(2)}) collective-permute-start(bf16[16,7168]{1,0:T(8,128)(2,1)S(1)} %collective-permute-done.6.refs_2_.refs_6_), channel_id=1, source_target_pairs={{0,16},{16,0},{1,17},{17,1},{2,18},{18,2},{3,19},{19,3},{4,20},{20... | collective-permute-start | bytes 688136 | tf_op jit(solution)/shard_map/ppermute | solution.py:227
  24.2 2.2 %base_part.6 = (f32[64,1536]{1,0:T(8,128)S(1)}, bf16[2,2048,512]{2,1,0:T(8,128)(2,1)S(1)}) custom-call(bf16[64,2048]{1,0:T(8,128)(2,1)S(1)} %get-tuple-element.48.rows, bf16[2048,7168]{1,0:T(8,128)(2,1)} %weight.9, bf16[3,2048,512]{2,1,0:T(8,128)(2,1)S(1)} %get-tuple-element.58.refs_0_, bf16[16,64]{1,0:T(8,128)(2,1)S(1)} %fusion.4.refs_1_, ...), custom_call_target="tpu_custom_call" | custom-call | flops 10000000000 | bytes 1 | tf_op jit(solution)/shard_map/base_part/pallas_call | solution.py:297
  26.4 0.0 collective-permute-done.5
  26.4 1.2 %collective-permute-start.7 = (bf16[16,64]{1,0:T(8,128)(2,1)S(1)}, bf16[16,64]{1,0:T(8,128)(2,1)S(1)}, u32[]{:S(2)}, u32[]{:S(2)}) collective-permute-start(bf16[16,64]{1,0:T(8,128)(2,1)S(1)} %add.35.refs_1_), channel_id=1, source_target_pairs={{0,4},{4,0},{8,12},{12,8},{16,20},{20,16},{24,28},{28,24},{1,5},{5... | collective-permute-start | bytes 6152 | tf_op jit(solution)/shard_map/ppermute | solution.py:221
  27.6 2.0 %base_part.7.refs_3_ = f32[64,1536]{1,0:T(8,128)S(1)} custom-call(bf16[64,2048]{1,0:T(8,128)(2,1)S(1)} %get-tuple-element.48.rows, bf16[2048,7168]{1,0:T(8,128)(2,1)} %weight.9, bf16[2,2048,512]{2,1,0:T(8,128)(2,1)S(1)} %get-tuple-element.64.refs_0_, bf16[16,64]{1,0:T(8,128)(2,1)S(1)} %add.35.refs_1_, bf16[16,7168]{1,0:T(8,128)(2,1)S(1)} %collective-permute-done.6.refs_2_.refs_6_), custom_call_target="tpu_custom_call" | custom-call | flops 1 | bytes 1 | tf_op jit(solution)/shard_map/base_part/pallas_call | solution.py:297
  29.7 0.5 %collective-permute-done.7 = bf16[16,64]{1,0:T(8,128)(2,1)S(1)} collective-permute-done((bf16[16,64]{1,0:T(8,128)(2,1)S(1)}, bf16[16,64]{1,0:T(8,128)(2,1)S(1)}, u32[]{:S(2)}, u32[]{:S(2)}) %collective-permute-start.7) | collective-permute-done | bytes 2080 | tf_op jit(solution)/shard_map/ppermute | solution.py:221
  30.1 0.0 collective-permute-done.8.refs_7_
  30.1 0.3 collective-permute-done.9.refs_8_
  30.4 0.5 %add_delta.1 = (f32[16,7168]{1,0:T(8,128)S(1)}, f32[16,7168]{1,0:T(8,128)S(1)}, f32[16,2048]{1,0:T(8,128)S(1)}, f32[16,2560]{1,0:T(8,128)S(1)}, f32[16,2560]{1,0...) custom-call(s32[1,64]{1,0:T(1,128)S(1)} %get-tuple-element.46.slot, ...), custom_call_target="tpu_custom_call" | custom-call | flops 1 | bytes 1 | tf_op jit(solution)/shard_map/add_delta/pallas_call | solution.py:335
  30.9 0.1 collective-permute-start.12
  31.0 0.5 %collective-permute-start.10 = (f32[16,2560]{1,0:T(8,128)S(1)}, f32[16,2560]{1,0:T(8,128)S(1)}, u32[]{:S(2)}, u32[]{:S(2)}) collective-permute-start(f32[16,2560]{1,0:T(8,128)S(1)} %get-tuple-element.70), channel_id=1, source_target_pairs={{0,1},{1,0},{2,3},{3,2},{4,5},{5,4},{6,7},{7,6},{8,9},{9,8},{10,11... | collective-permute-start | bytes 491528 | tf_op jit(solution)/shard_map/ppermute | solution.py:224
  31.5 0.1 collective-permute-start.14
  31.6 0.8 %collective-permute-done.12 = f32[16,2048]{1,0:T(8,128)S(1)} collective-permute-done((f32[16,2048]{1,0:T(8,128)S(1)}, f32[16,2048]{1,0:T(8,128)S(1)}, u32[]{:S(2)}, u32[]{:S(2)}) %collective-permute-start.12) | collective-permute-done | bytes 131104 | tf_op jit(solution)/shard_map/ppermute | solution.py:224
  32.3 0.6 %collective-permute-start.13 = (bf16[16,2048]{1,0:T(8,128)(2,1)S(1)}, bf16[16,2048]{1,0:T(8,128)(2,1)S(1)}, u32[]{:S(2)}, u32[]{:S(2)}) collective-permute-start(bf16[16,2048]{1,0:T(8,128)(2,1)S(1)} %add_convert_fusion.2), channel_id=1, source_target_pairs={{0,2},{1,3},{2,0},{3,1},{4,6},{5,7},{6,4},{7,5},{8,10},{9,11},{10,... | collective-permute-start | bytes 196616 | tf_op jit(solution)/shard_map/ppermute | solution.py:224
  33.0 0.0 collective-permute-done.10
  33.0 0.0 collective-permute-start.11
  33.0 1.5 %collective-permute-start.16 = (bf16[16,2560]{1,0:T(8,128)(2,1)S(1)}, bf16[16,2560]{1,0:T(8,128)(2,1)S(1)}, u32[]{:S(2)}, u32[]{:S(2)}) collective-permute-start(bf16[16,2560]{1,0:T(8,128)(2,1)S(1)} %add_convert_fusion), channel_id=1, source_target_pairs={{0,2},{1,3},{2,0},{3,1},{4,6},{5,7},{6,4},{7,5},{8,10},{9,11},{10,... | collective-permute-start | bytes 245768 | tf_op jit(solution)/shard_map/ppermute | solution.py:224
  34.5 0.0 collective-permute-done.14
  34.5 0.6 %collective-permute-start.15 = (bf16[16,2560]{1,0:T(8,128)(2,1)S(1)}, bf16[16,2560]{1,0:T(8,128)(2,1)S(1)}, u32[]{:S(2)}, u32[]{:S(2)}) collective-permute-start(bf16[16,2560]{1,0:T(8,128)(2,1)S(1)} %add_convert_fusion.1), channel_id=1, source_target_pairs={{0,2},{1,3},{2,0},{3,1},{4,6},{5,7},{6,4},{7,5},{8,10},{9,11},{10,... | collective-permute-start | bytes 245768 | tf_op jit(solution)/shard_map/ppermute | solution.py:224
  35.2 0.0 collective-permute-done.11
  35.2 2.0 %collective-permute-done.13 = bf16[16,2048]{1,0:T(8,128)(2,1)S(1)} collective-permute-done((bf16[16,2048]{1,0:T(8,128)(2,1)S(1)}, bf16[16,2048]{1,0:T(8,128)(2,1)S(1)}, u32[]{:S(2)}, u32[]{:S(2)}) %collective-permute-start.13) | collective-permute-done | bytes 65568 | tf_op jit(solution)/shard_map/ppermute | solution.py:224
  37.2 1.7 %collective-permute-done.16 = bf16[16,2560]{1,0:T(8,128)(2,1)S(1)} collective-permute-done((bf16[16,2560]{1,0:T(8,128)(2,1)S(1)}, bf16[16,2560]{1,0:T(8,128)(2,1)S(1)}, u32[]{:S(2)}, u32[]{:S(2)}) %collective-permute-start.16) | collective-permute-done | bytes 81952 | tf_op jit(solution)/shard_map/ppermute | solution.py:224
  38.9 1.2 %collective-permute-done.15 = bf16[16,2560]{1,0:T(8,128)(2,1)S(1)} collective-permute-done((bf16[16,2560]{1,0:T(8,128)(2,1)S(1)}, bf16[16,2560]{1,0:T(8,128)(2,1)S(1)}, u32[]{:S(2)}, u32[]{:S(2)}) %collective-permute-start.15) | collective-permute-done | bytes 81952 | tf_op jit(solution)/shard_map/ppermute | solution.py:224
  40.2 0.7 %pad_maximum_fusion = bf16[16,7168]{1,0:T(8,128)(2,1)} fusion(bf16[16,2560]{1,0:T(8,128)(2,1)S(1)} %get-tuple-element.80, bf16[16,2560]{1,0:T(8,128)(2,1)S(1)} %get-tuple-element.79, bf16[16,2048]{1,0:T(8,128)(2,1)S(1)} %fusion.2), kind=kLoop, calls=%fused_computation | loop fusion | flops 688128 | bytes 458752 | tf_op jit(solution)/shard_map/concatenate | solution.py:359
  (11 shorter events, 0.2 us)
Async XLA Ops:
  0.0 13.1 %collective-permute-start = (bf16[16,2048]{1,0:T(8,128)(2,1)}, bf16[16,2048]{1,0:T(8,128)(2,1)S(1)}, u32[]{:S(2)}, u32[]{:S(2)}) collective-permute-start(bf16[16,2048]{1,0:T(8,128)(2,1)} %refs_2_.1), channel_id=1, source_target_pairs={{0,8},{4,12},{8,0},{12,4},{16,24},{20,28},{24,16},{28,20},{1,9},{5... | collective-permute-start | bytes 196616 | tf_op jit(solution)/shard_map/ppermute | solution.py:221
  4.0 9.1 %collective-permute-start.1 = (bf16[16,2048]{1,0:T(8,128)(2,1)}, bf16[16,2048]{1,0:T(8,128)(2,1)S(1)}, u32[]{:S(2)}, u32[]{:S(2)}) collective-permute-start(bf16[16,2048]{1,0:T(8,128)(2,1)} %refs_2_.1), channel_id=1, source_target_pairs={{0,12},{4,8},{8,4},{12,0},{16,28},{20,24},{24,20},{28,16},{1,13},{... | collective-permute-start | bytes 196616 | tf_op jit(solution)/shard_map/ppermute | solution.py:221
  5.4 7.7 %collective-permute-start.2 = (bf16[16,2048]{1,0:T(8,128)(2,1)}, bf16[16,2048]{1,0:T(8,128)(2,1)S(1)}, u32[]{:S(2)}, u32[]{:S(2)}) collective-permute-start(bf16[16,2048]{1,0:T(8,128)(2,1)} %refs_2_.1), channel_id=1, source_target_pairs={{0,4},{4,0},{8,12},{12,8},{16,20},{20,16},{24,28},{28,24},{1,5},{5... | collective-permute-start | bytes 196616 | tf_op jit(solution)/shard_map/ppermute | solution.py:221
  9.6 13.4 %collective-permute-start.6 = (bf16[16,7168]{1,0:T(8,128)(2,1)S(1)}, bf16[16,7168]{1,0:T(8,128)(2,1)S(1)}, u32[]{:S(2)}, u32[]{:S(2)}) collective-permute-start(bf16[16,7168]{1,0:T(8,128)(2,1)S(1)} %get-tuple-element.59), channel_id=1, source_target_pairs={{0,8},{4,12},{8,0},{12,4},{16,28},{20,24},{24,20},{28,16},{1,9},{5... | collective-permute-start | bytes 688136 | tf_op jit(solution)/shard_map/ppermute | solution.py:221
  12.5 17.6 %collective-permute-start.8 = (bf16[16,7168]{1,0:T(8,128)(2,1)S(1)}, bf16[16,7168]{1,0:T(8,128)(2,1)S(1)}, u32[]{:S(2)}, u32[]{:S(2)}) collective-permute-start(bf16[16,7168]{1,0:T(8,128)(2,1)S(1)} %get-tuple-element.68), channel_id=1, source_target_pairs={{0,4},{4,0},{8,12},{12,8},{16,20},{20,16},{24,28},{28,24},{1,5},{5... | collective-permute-start | bytes 688136 | tf_op jit(solution)/shard_map/ppermute | solution.py:221
  13.4 3.7 %collective-permute-start.3 = (f32[32,64]{1,0:T(8,128)S(1)}, f32[32,64]{1,0:T(8,128)S(1)}, u32[]{:S(2)}, u32[]{:S(2)}) collective-permute-start(f32[32,64]{1,0:T(8,128)S(1)} %get-tuple-element.47.refs_1_), channel_id=1, source_target_pairs={{0,1},{1,0},{2,3},{3,2},{4,5},{5,4},{6,7},{7,6},{8,9},{9,8},{10,11... | collective-permute-start | bytes 24584 | tf_op jit(solution)/shard_map/ppermute | solution.py:224
  17.1 4.5 %collective-permute-start.4 = (f32[16,64]{1,0:T(8,128)S(1)}, f32[16,64]{1,0:T(8,128)S(1)}, u32[]{:S(2)}, u32[]{:S(2)}) collective-permute-start(f32[16,64]{1,0:T(8,128)S(1)} %slice.20), channel_id=1, source_target_pairs={{0,2},{1,3},{2,0},{3,1},{4,6},{5,7},{6,4},{7,5},{8,10},{9,11},{10,... | collective-permute-start | bytes 12296 | tf_op jit(solution)/shard_map/ppermute | solution.py:224
  21.7 4.8 %collective-permute-start.5 = (bf16[16,64]{1,0:T(8,128)(2,1)S(1)}, bf16[16,64]{1,0:T(8,128)(2,1)S(1)}, u32[]{:S(2)}, u32[]{:S(2)}) collective-permute-start(bf16[16,64]{1,0:T(8,128)(2,1)S(1)} %fusion.4.refs_1_), channel_id=1, source_target_pairs={{0,8},{4,12},{8,0},{12,4},{16,24},{20,28},{24,16},{28,20},{1,9},{5... | collective-permute-start | bytes 6152 | tf_op jit(solution)/shard_map/ppermute | solution.py:221
  23.0 7.4 %collective-permute-start.9 = (bf16[16,7168]{1,0:T(8,128)(2,1)S(1)}, bf16[16,7168]{1,0:T(8,128)(2,1)S(1)}, u32[]{:S(2)}, u32[]{:S(2)}) collective-permute-start(bf16[16,7168]{1,0:T(8,128)(2,1)S(1)} %collective-permute-done.6.refs_2_.refs_6_), channel_id=1, source_target_pairs={{0,16},{16,0},{1,17},{17,1},{2,18},{18,2},{3,19},{19,3},{4,20},{20... | collective-permute-start | bytes 688136 | tf_op jit(solution)/shard_map/ppermute | solution.py:227
  26.4 3.7 %collective-permute-start.7 = (bf16[16,64]{1,0:T(8,128)(2,1)S(1)}, bf16[16,64]{1,0:T(8,128)(2,1)S(1)}, u32[]{:S(2)}, u32[]{:S(2)}) collective-permute-start(bf16[16,64]{1,0:T(8,128)(2,1)S(1)} %add.35.refs_1_), channel_id=1, source_target_pairs={{0,4},{4,0},{8,12},{12,8},{16,20},{20,16},{24,28},{28,24},{1,5},{5... | collective-permute-start | bytes 6152 | tf_op jit(solution)/shard_map/ppermute | solution.py:221
  30.9 1.4 %collective-permute-start.12 = (f32[16,2048]{1,0:T(8,128)S(1)}, f32[16,2048]{1,0:T(8,128)S(1)}, u32[]{:S(2)}, u32[]{:S(2)}) collective-permute-start(f32[16,2048]{1,0:T(8,128)S(1)} %get-tuple-element.74), channel_id=1, source_target_pairs={{0,1},{1,0},{2,3},{3,2},{4,5},{5,4},{6,7},{7,6},{8,9},{9,8},{10,11... | collective-permute-start | bytes 393224 | tf_op jit(solution)/shard_map/ppermute | solution.py:224
  31.0 2.0 %collective-permute-start.10 = (f32[16,2560]{1,0:T(8,128)S(1)}, f32[16,2560]{1,0:T(8,128)S(1)}, u32[]{:S(2)}, u32[]{:S(2)}) collective-permute-start(f32[16,2560]{1,0:T(8,128)S(1)} %get-tuple-element.70), channel_id=1, source_target_pairs={{0,1},{1,0},{2,3},{3,2},{4,5},{5,4},{6,7},{7,6},{8,9},{9,8},{10,11... | collective-permute-start | bytes 491528 | tf_op jit(solution)/shard_map/ppermute | solution.py:224
  31.5 3.0 %collective-permute-start.14 = (f32[16,2560]{1,0:T(8,128)S(1)}, f32[16,2560]{1,0:T(8,128)S(1)}, u32[]{:S(2)}, u32[]{:S(2)}) collective-permute-start(f32[16,2560]{1,0:T(8,128)S(1)} %get-tuple-element.76), channel_id=1, source_target_pairs={{0,1},{1,0},{2,3},{3,2},{4,5},{5,4},{6,7},{7,6},{8,9},{9,8},{10,11... | collective-permute-start | bytes 491528 | tf_op jit(solution)/shard_map/ppermute | solution.py:224
  32.3 4.9 %collective-permute-start.13 = (bf16[16,2048]{1,0:T(8,128)(2,1)S(1)}, bf16[16,2048]{1,0:T(8,128)(2,1)S(1)}, u32[]{:S(2)}, u32[]{:S(2)}) collective-permute-start(bf16[16,2048]{1,0:T(8,128)(2,1)S(1)} %add_convert_fusion.2), channel_id=1, source_target_pairs={{0,2},{1,3},{2,0},{3,1},{4,6},{5,7},{6,4},{7,5},{8,10},{9,11},{10,... | collective-permute-start | bytes 196616 | tf_op jit(solution)/shard_map/ppermute | solution.py:224
  33.0 2.2 %collective-permute-start.11 = (f32[16,7168]{1,0:T(8,128)S(1)}, f32[16,7168]{1,0:T(8,128)S(1)}, u32[]{:S(2)}, u32[]{:S(2)}) collective-permute-start(f32[16,7168]{1,0:T(8,128)S(1)} %get-tuple-element.72), channel_id=1, source_target_pairs={{0,1},{1,0},{2,3},{3,2},{4,5},{5,4},{6,7},{7,6},{8,9},{9,8},{10,11... | collective-permute-start | bytes 1376264 | tf_op jit(solution)/shard_map/ppermute | solution.py:224
  33.0 6.0 %collective-permute-start.16 = (bf16[16,2560]{1,0:T(8,128)(2,1)S(1)}, bf16[16,2560]{1,0:T(8,128)(2,1)S(1)}, u32[]{:S(2)}, u32[]{:S(2)}) collective-permute-start(bf16[16,2560]{1,0:T(8,128)(2,1)S(1)} %add_convert_fusion), channel_id=1, source_target_pairs={{0,2},{1,3},{2,0},{3,1},{4,6},{5,7},{6,4},{7,5},{8,10},{9,11},{10,... | collective-permute-start | bytes 245768 | tf_op jit(solution)/shard_map/ppermute | solution.py:224
  34.5 5.6 %collective-permute-start.15 = (bf16[16,2560]{1,0:T(8,128)(2,1)S(1)}, bf16[16,2560]{1,0:T(8,128)(2,1)S(1)}, u32[]{:S(2)}, u32[]{:S(2)}) collective-permute-start(bf16[16,2560]{1,0:T(8,128)(2,1)S(1)} %add_convert_fusion.1), channel_id=1, source_target_pairs={{0,2},{1,3},{2,0},{3,1},{4,6},{5,7},{6,4},{7,5},{8,10},{9,11},{10,... | collective-permute-start | bytes 245768 | tf_op jit(solution)/shard_map/ppermute | solution.py:224

commit v21 on v19

--- a/solution.py
+++ b/solution.py
@@ -233,7 +233,7 @@
 
     cuts = [block_count * k // 14 for k in (0, 4, 8, 11, 14)]
     parts = list(zip(cuts[:-1], cuts[1:]))
-    loads = [block_count * k // 14 for k in (0, 4, 8, 11, 13, 14)]
+    loads = [block_count * k // 14 for k in (0, 5, 8, 11, 13, 14)]
     bands = 4
     small = [
         pltpu.with_memory_space_constraint(x, pltpu.HBM)

time: 41 us -> 41.5 us (1.012)
  waiting for transfers between devices: 7.09 us -> 8 us
    ppermute x7, waiting for transfers between devices: 0.47 us -> 1.47 us  [from_owner(): return lax.ppermute(x, ('groups', 'adapter'), pairs)]
    pallas_call x1, Pallas kernels: 3.94 us -> 4.6 us  [paired(): kernel_call(functools.partial(cut_kernel, block, range(loads[1]), len(sma...]
    pallas_call x4, Pallas kernels: 10.8 us -> 10.2 us  [base_part(): kernel_call(functools.partial(base_kernel, block, places, numbers, stream...]
    ppermute x7, starting transfers between devices: 11.7 us -> 11.1 us  [from_owner(): return lax.ppermute(x, ('groups', 'adapter'), pairs)]
  transfers between devices with their start and end apart: 15 -> 15, of which waited for: 6 -> 7; matrix products, arithmetic and copies ran while one was open for 0% -> 0% of each run, Pallas kernels for 37% -> 36%
where the time goes in v21:
time: 41.5 us; the launch traced here: 41.4 us
  starting transfers between devices  16.8 us (40%)
  Pallas kernels  15.5 us (37%)
  waiting for transfers between devices  8 us (19%)
  other arithmetic  0.89 us (2%)
    ppermute x7, starting transfers between devices, from_owner(): return lax.ppermute(x, ('groups', 'adapter'), pairs)  11.1 us
    pallas_call x4, Pallas kernels, base_part(): kernel_call(functools.partial(base_kernel, block, places, numbers, stream...  10.2 us
    ppermute x7, waiting for transfers between devices, from_tensor(): return lax.ppermute(x, 'tensor', [(s, s ^ m) for s in range(4)])  6.52 us
    pallas_call x1, Pallas kernels, paired(): kernel_call(functools.partial(cut_kernel, block, range(loads[1]), len(sma...  4.6 us
    ppermute x7, starting transfers between devices, from_tensor(): return lax.ppermute(x, 'tensor', [(s, s ^ m) for s in range(4)])  4.35 us
    ppermute x7, waiting for transfers between devices, from_owner(): return lax.ppermute(x, ('groups', 'adapter'), pairs)  1.47 us
    ppermute x1, starting transfers between devices, from_group(): return lax.ppermute(x, 'groups', [(0, 1), (1, 0)])  1.36 us
  transfers between devices with their start and end apart: 15, of which 7 were waited for; matrix products, arithmetic and copies ran while one was open for 0% of the time, Pallas kernels for 36%

profile of v21, /device:TPU:0, one launch (start us, length us, event | category | flops | bytes accessed | tf_op | source)
XLA Modules:
  0.0 41.4 jit_solution(2705188327792362642)
XLA Ops:
  0.0 4.0 %collective-permute-start = (bf16[16,2048]{1,0:T(8,128)(2,1)}, bf16[16,2048]{1,0:T(8,128)(2,1)S(1)}, u32[]{:S(2)}, u32[]{:S(2)}) collective-permute-start(bf16[16,2048]{1,0:T(8,128)(2,1)} %refs_2_.1), channel_id=1, source_target_pairs={{0,8},{4,12},{8,0},{12,4},{16,24},{20,28},{24,16},{28,20},{1,9},{5... | collective-permute-start | bytes 196616 | tf_op jit(solution)/shard_map/ppermute | solution.py:221
  4.0 1.6 %collective-permute-start.2 = (bf16[16,2048]{1,0:T(8,128)(2,1)}, bf16[16,2048]{1,0:T(8,128)(2,1)S(1)}, u32[]{:S(2)}, u32[]{:S(2)}) collective-permute-start(bf16[16,2048]{1,0:T(8,128)(2,1)} %refs_2_.1), channel_id=1, source_target_pairs={{0,4},{4,0},{8,12},{12,8},{16,20},{20,16},{24,28},{28,24},{1,5},{5... | collective-permute-start | bytes 196616 | tf_op jit(solution)/shard_map/ppermute | solution.py:221
  5.6 0.0 collective-permute-start.1
  5.6 4.6 %cut_expand.1 = (bf16[16,7168]{1,0:T(8,128)(2,1)S(1)}, bf16[16,7168]{1,0:T(8,128)(2,1)S(1)}, bf16[16,7168]{1,0:T(8,128)(2,1)S(1)}, s32[1,4]{1,0:T(1,128)S(1)}, s...) custom-call(bf16[1,16,28672]{2,1,0:T(8,128)(2,1)} %expand.1, ...), custom_call_target="tpu_custom_call" | custom-call | flops 1 | bytes 1 | tf_op jit(solution)/shard_map/cut_expand/pallas_call | solution.py:247
  10.2 2.0 %collective-permute-start.6 = (bf16[16,7168]{1,0:T(8,128)(2,1)S(1)}, bf16[16,7168]{1,0:T(8,128)(2,1)S(1)}, u32[]{:S(2)}, u32[]{:S(2)}) collective-permute-start(bf16[16,7168]{1,0:T(8,128)(2,1)S(1)} %get-tuple-element.57), channel_id=1, source_target_pairs={{0,8},{4,12},{8,0},{12,4},{16,28},{20,24},{24,20},{28,16},{1,9},{5... | collective-permute-start | bytes 688136 | tf_op jit(solution)/shard_map/ppermute | solution.py:221
  12.2 2.5 %collective-permute-start.8 = (bf16[16,7168]{1,0:T(8,128)(2,1)S(1)}, bf16[16,7168]{1,0:T(8,128)(2,1)S(1)}, u32[]{:S(2)}, u32[]{:S(2)}) collective-permute-start(bf16[16,7168]{1,0:T(8,128)(2,1)S(1)} %get-tuple-element.66), channel_id=1, source_target_pairs={{0,4},{4,0},{8,12},{12,8},{16,20},{20,16},{24,28},{28,24},{1,5},{5... | collective-permute-start | bytes 688136 | tf_op jit(solution)/shard_map/ppermute | solution.py:221
  14.7 0.0 collective-permute-done.refs_1_
  14.7 0.0 collective-permute-done.2.refs_3_
  14.7 0.0 collective-permute-done.1.refs_2_
  14.7 0.3 gather_rows.1
  14.9 0.1 collective-permute-start.3
  15.0 2.9 %base_part.4 = (f32[64,2048]{1,0:T(8,128)S(1)}, bf16[3,2048,512]{2,1,0:T(8,128)(2,1)S(1)}) custom-call(bf16[64,2048]{1,0:T(8,128)(2,1)S(1)} %get-tuple-element.46.rows, bf16[2048,7168]{1,0:T(8,128)(2,1)} %weight.9, bf16[5,2048,512]{2,1,0:T(8,128)(2,1)S(1)} %get-tuple-element.47.refs_0_, f32[32,64]{1,0:T(8,128)S(1)} %get-tuple-element.45.refs_1_), custom_call_target="tpu_custom_call" | custom-call | flops 1500000000 | bytes 1 | tf_op jit(solution)/shard_map/base_part/pallas_call | solution.py:297
  18.0 0.0 collective-permute-done.3
  18.0 1.6 %collective-permute-start.4 = (f32[16,64]{1,0:T(8,128)S(1)}, f32[16,64]{1,0:T(8,128)S(1)}, u32[]{:S(2)}, u32[]{:S(2)}) collective-permute-start(f32[16,64]{1,0:T(8,128)S(1)} %slice.16), channel_id=1, source_target_pairs={{0,2},{1,3},{2,0},{3,1},{4,6},{5,7},{6,4},{7,5},{8,10},{9,11},{10,... | collective-permute-start | bytes 12296 | tf_op jit(solution)/shard_map/ppermute | solution.py:224
  19.5 3.0 %base_part.5 = (f32[64,2048]{1,0:T(8,128)S(1)}, bf16[3,2048,512]{2,1,0:T(8,128)(2,1)S(1)}) custom-call(bf16[64,2048]{1,0:T(8,128)(2,1)S(1)} %get-tuple-element.46.rows, bf16[2048,7168]{1,0:T(8,128)(2,1)} %weight.9, bf16[5,2048,512]{2,1,0:T(8,128)(2,1)S(1)} %get-tuple-element.47.refs_0_, bf16[3,2048,512]{2,1,0:T(8,128)(2,1)S(1)} %get-tuple-element.52.refs_1_, ...), custom_call_target="tpu_custom_call" | custom-call | flops 1500000000 | bytes 1 | tf_op jit(solution)/shard_map/base_part/pallas_call | solution.py:297
  22.5 0.0 collective-permute-done.4
  22.6 0.1 collective-permute-start.5
  22.7 0.3 collective-permute-done.6.refs_2_.refs_6_
  23.0 1.4 %collective-permute-start.9 = (bf16[16,7168]{1,0:T(8,128)(2,1)S(1)}, bf16[16,7168]{1,0:T(8,128)(2,1)S(1)}, u32[]{:S(2)}, u32[]{:S(2)}) collective-permute-start(bf16[16,7168]{1,0:T(8,128)(2,1)S(1)} %collective-permute-done.6.refs_2_.refs_6_), channel_id=1, source_target_pairs={{0,16},{16,0},{1,17},{17,1},{2,18},{18,2},{3,19},{19,3},{4,20},{20... | collective-permute-start | bytes 688136 | tf_op jit(solution)/shard_map/ppermute | solution.py:227
  24.4 2.2 %base_part.6 = (f32[64,1536]{1,0:T(8,128)S(1)}, bf16[2,2048,512]{2,1,0:T(8,128)(2,1)S(1)}) custom-call(bf16[64,2048]{1,0:T(8,128)(2,1)S(1)} %get-tuple-element.46.rows, bf16[2048,7168]{1,0:T(8,128)(2,1)} %weight.9, bf16[3,2048,512]{2,1,0:T(8,128)(2,1)S(1)} %get-tuple-element.56.refs_0_, bf16[16,64]{1,0:T(8,128)(2,1)S(1)} %fusion.3.refs_1_, ...), custom_call_target="tpu_custom_call" | custom-call | flops 10000000000 | bytes 1 | tf_op jit(solution)/shard_map/base_part/pallas_call | solution.py:297
  26.6 0.5 %collective-permute-done.5 = bf16[16,64]{1,0:T(8,128)(2,1)S(1)} collective-permute-done((bf16[16,64]{1,0:T(8,128)(2,1)S(1)}, bf16[16,64]{1,0:T(8,128)(2,1)S(1)}, u32[]{:S(2)}, u32[]{:S(2)}) %collective-permute-start.5) | collective-permute-done | bytes 2080 | tf_op jit(solution)/shard_map/ppermute | solution.py:221
  27.1 0.9 %collective-permute-start.7 = (bf16[16,64]{1,0:T(8,128)(2,1)S(1)}, bf16[16,64]{1,0:T(8,128)(2,1)S(1)}, u32[]{:S(2)}, u32[]{:S(2)}) collective-permute-start(bf16[16,64]{1,0:T(8,128)(2,1)S(1)} %add.29.refs_1_), channel_id=1, source_target_pairs={{0,4},{4,0},{8,12},{12,8},{16,20},{20,16},{24,28},{28,24},{1,5},{5... | collective-permute-start | bytes 6152 | tf_op jit(solution)/shard_map/ppermute | solution.py:221
  28.0 2.0 %base_part.7.refs_3_ = f32[64,1536]{1,0:T(8,128)S(1)} custom-call(bf16[64,2048]{1,0:T(8,128)(2,1)S(1)} %get-tuple-element.46.rows, bf16[2048,7168]{1,0:T(8,128)(2,1)} %weight.9, bf16[2,2048,512]{2,1,0:T(8,128)(2,1)S(1)} %get-tuple-element.62.refs_0_, bf16[16,64]{1,0:T(8,128)(2,1)S(1)} %add.29.refs_1_, bf16[16,7168]{1,0:T(8,128)(2,1)S(1)} %collective-permute-done.6.refs_2_.refs_6_), custom_call_target="tpu_custom_call" | custom-call | flops 1 | bytes 1 | tf_op jit(solution)/shard_map/base_part/pallas_call | solution.py:297
  30.1 0.7 %collective-permute-done.7 = bf16[16,64]{1,0:T(8,128)(2,1)S(1)} collective-permute-done((bf16[16,64]{1,0:T(8,128)(2,1)S(1)}, bf16[16,64]{1,0:T(8,128)(2,1)S(1)}, u32[]{:S(2)}, u32[]{:S(2)}) %collective-permute-start.7) | collective-permute-done | bytes 2080 | tf_op jit(solution)/shard_map/ppermute | solution.py:221
  30.7 0.0 collective-permute-done.8.refs_7_
  30.7 0.0 collective-permute-done.9.refs_8_
  30.8 0.5 %add_delta.1 = (f32[16,7168]{1,0:T(8,128)S(1)}, f32[16,7168]{1,0:T(8,128)S(1)}, f32[16,2560]{1,0:T(8,128)S(1)}, f32[16,4608]{1,0:T(8,128)S(1)}, f32[16,2560]{1,0:T(8,128)S(1)}, /*index=5*/f32[16,4608]{1,0:T(8,128)S(1)}) custom-call(s32[1,64]{1,0:T(1,128)S(1)} %get-tuple-element.44.slot, f32[64,2048]{1,0:T(8,128)S(1)} %get-tuple-element.49.refs_0_, ...), custom_call_target="tpu_custom_call" | custom-call | flops 1 | bytes 1 | tf_op jit(solution)/shard_map/add_delta/pallas_call | solution.py:335
  31.2 0.1 collective-permute-start.10
  31.3 0.5 %collective-permute-start.12 = (f32[16,2560]{1,0:T(8,128)S(1)}, f32[16,2560]{1,0:T(8,128)S(1)}, u32[]{:S(2)}, u32[]{:S(2)}) collective-permute-start(f32[16,2560]{1,0:T(8,128)S(1)} %get-tuple-element.72), channel_id=1, source_target_pairs={{0,1},{1,0},{2,3},{3,2},{4,5},{5,4},{6,7},{7,6},{8,9},{9,8},{10,11... | collective-permute-start | bytes 491528 | tf_op jit(solution)/shard_map/ppermute | solution.py:224
  31.8 1.1 %collective-permute-done.10 = f32[16,4608]{1,0:T(8,128)S(1)} collective-permute-done((f32[16,4608]{1,0:T(8,128)S(1)}, f32[16,4608]{1,0:T(8,128)S(1)}, u32[]{:S(2)}, u32[]{:S(2)}) %collective-permute-start.10) | collective-permute-done | bytes 294944 | tf_op jit(solution)/shard_map/ppermute | solution.py:224
  32.9 0.7 %collective-permute-start.14 = (bf16[16,4608]{1,0:T(8,128)(2,1)S(1)}, bf16[16,4608]{1,0:T(8,128)(2,1)S(1)}, u32[]{:S(2)}, u32[]{:S(2)}) collective-permute-start(bf16[16,4608]{1,0:T(8,128)(2,1)S(1)} %add_convert_fusion), channel_id=1, source_target_pairs={{0,2},{1,3},{2,0},{3,1},{4,6},{5,7},{6,4},{7,5},{8,10},{9,11},{10,... | collective-permute-start | bytes 442376 | tf_op jit(solution)/shard_map/ppermute | solution.py:224
  33.6 0.0 collective-permute-start.11
  33.6 0.0 collective-permute-done.12
  33.6 1.5 %collective-permute-start.13 = (bf16[16,2560]{1,0:T(8,128)(2,1)S(1)}, bf16[16,2560]{1,0:T(8,128)(2,1)S(1)}, u32[]{:S(2)}, u32[]{:S(2)}) collective-permute-start(bf16[16,2560]{1,0:T(8,128)(2,1)S(1)} %add_convert_fusion.1), channel_id=1, source_target_pairs={{0,2},{1,3},{2,0},{3,1},{4,6},{5,7},{6,4},{7,5},{8,10},{9,11},{10,... | collective-permute-start | bytes 245768 | tf_op jit(solution)/shard_map/ppermute | solution.py:224
  35.1 0.3 collective-permute-done.11
  35.5 4.2 %collective-permute-done.14 = bf16[16,4608]{1,0:T(8,128)(2,1)S(1)} collective-permute-done((bf16[16,4608]{1,0:T(8,128)(2,1)S(1)}, bf16[16,4608]{1,0:T(8,128)(2,1)S(1)}, u32[]{:S(2)}, u32[]{:S(2)}) %collective-permute-start.14) | collective-permute-done | bytes 147488 | tf_op jit(solution)/shard_map/ppermute | solution.py:224
  39.7 0.9 %collective-permute-done.13 = bf16[16,2560]{1,0:T(8,128)(2,1)S(1)} collective-permute-done((bf16[16,2560]{1,0:T(8,128)(2,1)S(1)}, bf16[16,2560]{1,0:T(8,128)(2,1)S(1)}, u32[]{:S(2)}, u32[]{:S(2)}) %collective-permute-start.13) | collective-permute-done | bytes 81952 | tf_op jit(solution)/shard_map/ppermute | solution.py:224
  40.7 0.7 %pad_maximum_fusion = bf16[16,7168]{1,0:T(8,128)(2,1)} fusion(bf16[16,4608]{1,0:T(8,128)(2,1)S(1)} %fusion, bf16[16,2560]{1,0:T(8,128)(2,1)S(1)} %fusion.1), kind=kLoop, calls=%fused_computation.3 | loop fusion | flops 458752 | bytes 458752 | tf_op jit(solution)/shard_map/concatenate | solution.py:358
  (10 shorter events, 0.2 us)
Async XLA Ops:
  0.0 14.7 %collective-permute-start = (bf16[16,2048]{1,0:T(8,128)(2,1)}, bf16[16,2048]{1,0:T(8,128)(2,1)S(1)}, u32[]{:S(2)}, u32[]{:S(2)}) collective-permute-start(bf16[16,2048]{1,0:T(8,128)(2,1)} %refs_2_.1), channel_id=1, source_target_pairs={{0,8},{4,12},{8,0},{12,4},{16,24},{20,28},{24,16},{28,20},{1,9},{5... | collective-permute-start | bytes 196616 | tf_op jit(solution)/shard_map/ppermute | solution.py:221
  4.0 10.6 %collective-permute-start.2 = (bf16[16,2048]{1,0:T(8,128)(2,1)}, bf16[16,2048]{1,0:T(8,128)(2,1)S(1)}, u32[]{:S(2)}, u32[]{:S(2)}) collective-permute-start(bf16[16,2048]{1,0:T(8,128)(2,1)} %refs_2_.1), channel_id=1, source_target_pairs={{0,4},{4,0},{8,12},{12,8},{16,20},{20,16},{24,28},{28,24},{1,5},{5... | collective-permute-start | bytes 196616 | tf_op jit(solution)/shard_map/ppermute | solution.py:221
  5.6 9.1 %collective-permute-start.1 = (bf16[16,2048]{1,0:T(8,128)(2,1)}, bf16[16,2048]{1,0:T(8,128)(2,1)S(1)}, u32[]{:S(2)}, u32[]{:S(2)}) collective-permute-start(bf16[16,2048]{1,0:T(8,128)(2,1)} %refs_2_.1), channel_id=1, source_target_pairs={{0,12},{4,8},{8,4},{12,0},{16,28},{20,24},{24,20},{28,16},{1,13},{... | collective-permute-start | bytes 196616 | tf_op jit(solution)/shard_map/ppermute | solution.py:221
  10.2 12.8 %collective-permute-start.6 = (bf16[16,7168]{1,0:T(8,128)(2,1)S(1)}, bf16[16,7168]{1,0:T(8,128)(2,1)S(1)}, u32[]{:S(2)}, u32[]{:S(2)}) collective-permute-start(bf16[16,7168]{1,0:T(8,128)(2,1)S(1)} %get-tuple-element.57), channel_id=1, source_target_pairs={{0,8},{4,12},{8,0},{12,4},{16,28},{20,24},{24,20},{28,16},{1,9},{5... | collective-permute-start | bytes 688136 | tf_op jit(solution)/shard_map/ppermute | solution.py:221
  12.2 18.6 %collective-permute-start.8 = (bf16[16,7168]{1,0:T(8,128)(2,1)S(1)}, bf16[16,7168]{1,0:T(8,128)(2,1)S(1)}, u32[]{:S(2)}, u32[]{:S(2)}) collective-permute-start(bf16[16,7168]{1,0:T(8,128)(2,1)S(1)} %get-tuple-element.66), channel_id=1, source_target_pairs={{0,4},{4,0},{8,12},{12,8},{16,20},{20,16},{24,28},{28,24},{1,5},{5... | collective-permute-start | bytes 688136 | tf_op jit(solution)/shard_map/ppermute | solution.py:221
  14.9 3.0 %collective-permute-start.3 = (f32[32,64]{1,0:T(8,128)S(1)}, f32[32,64]{1,0:T(8,128)S(1)}, u32[]{:S(2)}, u32[]{:S(2)}) collective-permute-start(f32[32,64]{1,0:T(8,128)S(1)} %get-tuple-element.45.refs_1_), channel_id=1, source_target_pairs={{0,1},{1,0},{2,3},{3,2},{4,5},{5,4},{6,7},{7,6},{8,9},{9,8},{10,11... | collective-permute-start | bytes 24584 | tf_op jit(solution)/shard_map/ppermute | solution.py:224
  18.0 4.5 %collective-permute-start.4 = (f32[16,64]{1,0:T(8,128)S(1)}, f32[16,64]{1,0:T(8,128)S(1)}, u32[]{:S(2)}, u32[]{:S(2)}) collective-permute-start(f32[16,64]{1,0:T(8,128)S(1)} %slice.16), channel_id=1, source_target_pairs={{0,2},{1,3},{2,0},{3,1},{4,6},{5,7},{6,4},{7,5},{8,10},{9,11},{10,... | collective-permute-start | bytes 12296 | tf_op jit(solution)/shard_map/ppermute | solution.py:224
  22.6 4.6 %collective-permute-start.5 = (bf16[16,64]{1,0:T(8,128)(2,1)S(1)}, bf16[16,64]{1,0:T(8,128)(2,1)S(1)}, u32[]{:S(2)}, u32[]{:S(2)}) collective-permute-start(bf16[16,64]{1,0:T(8,128)(2,1)S(1)} %fusion.3.refs_1_), channel_id=1, source_target_pairs={{0,8},{4,12},{8,0},{12,4},{16,24},{20,28},{24,16},{28,20},{1,9},{5... | collective-permute-start | bytes 6152 | tf_op jit(solution)/shard_map/ppermute | solution.py:221
  23.0 7.8 %collective-permute-start.9 = (bf16[16,7168]{1,0:T(8,128)(2,1)S(1)}, bf16[16,7168]{1,0:T(8,128)(2,1)S(1)}, u32[]{:S(2)}, u32[]{:S(2)}) collective-permute-start(bf16[16,7168]{1,0:T(8,128)(2,1)S(1)} %collective-permute-done.6.refs_2_.refs_6_), channel_id=1, source_target_pairs={{0,16},{16,0},{1,17},{17,1},{2,18},{18,2},{3,19},{19,3},{4,20},{20... | collective-permute-start | bytes 688136 | tf_op jit(solution)/shard_map/ppermute | solution.py:227
  27.1 3.6 %collective-permute-start.7 = (bf16[16,64]{1,0:T(8,128)(2,1)S(1)}, bf16[16,64]{1,0:T(8,128)(2,1)S(1)}, u32[]{:S(2)}, u32[]{:S(2)}) collective-permute-start(bf16[16,64]{1,0:T(8,128)(2,1)S(1)} %add.29.refs_1_), channel_id=1, source_target_pairs={{0,4},{4,0},{8,12},{12,8},{16,20},{20,16},{24,28},{28,24},{1,5},{5... | collective-permute-start | bytes 6152 | tf_op jit(solution)/shard_map/ppermute | solution.py:221
  31.2 1.6 %collective-permute-start.10 = (f32[16,4608]{1,0:T(8,128)S(1)}, f32[16,4608]{1,0:T(8,128)S(1)}, u32[]{:S(2)}, u32[]{:S(2)}) collective-permute-start(f32[16,4608]{1,0:T(8,128)S(1)} %get-tuple-element.68), channel_id=1, source_target_pairs={{0,1},{1,0},{2,3},{3,2},{4,5},{5,4},{6,7},{7,6},{8,9},{9,8},{10,11... | collective-permute-start | bytes 884744 | tf_op jit(solution)/shard_map/ppermute | solution.py:224
  31.3 2.3 %collective-permute-start.12 = (f32[16,2560]{1,0:T(8,128)S(1)}, f32[16,2560]{1,0:T(8,128)S(1)}, u32[]{:S(2)}, u32[]{:S(2)}) collective-permute-start(f32[16,2560]{1,0:T(8,128)S(1)} %get-tuple-element.72), channel_id=1, source_target_pairs={{0,1},{1,0},{2,3},{3,2},{4,5},{5,4},{6,7},{7,6},{8,9},{9,8},{10,11... | collective-permute-start | bytes 491528 | tf_op jit(solution)/shard_map/ppermute | solution.py:224
  32.9 6.8 %collective-permute-start.14 = (bf16[16,4608]{1,0:T(8,128)(2,1)S(1)}, bf16[16,4608]{1,0:T(8,128)(2,1)S(1)}, u32[]{:S(2)}, u32[]{:S(2)}) collective-permute-start(bf16[16,4608]{1,0:T(8,128)(2,1)S(1)} %add_convert_fusion), channel_id=1, source_target_pairs={{0,2},{1,3},{2,0},{3,1},{4,6},{5,7},{6,4},{7,5},{8,10},{9,11},{10,... | collective-permute-start | bytes 442376 | tf_op jit(solution)/shard_map/ppermute | solution.py:224
  33.6 1.8 %collective-permute-start.11 = (f32[16,7168]{1,0:T(8,128)S(1)}, f32[16,7168]{1,0:T(8,128)S(1)}, u32[]{:S(2)}, u32[]{:S(2)}) collective-permute-start(f32[16,7168]{1,0:T(8,128)S(1)} %get-tuple-element.70), channel_id=1, source_target_pairs={{0,1},{1,0},{2,3},{3,2},{4,5},{5,4},{6,7},{7,6},{8,9},{9,8},{10,11... | collective-permute-start | bytes 1376264 | tf_op jit(solution)/shard_map/ppermute | solution.py:224
  33.6 7.0 %collective-permute-start.13 = (bf16[16,2560]{1,0:T(8,128)(2,1)S(1)}, bf16[16,2560]{1,0:T(8,128)(2,1)S(1)}, u32[]{:S(2)}, u32[]{:S(2)}) collective-permute-start(bf16[16,2560]{1,0:T(8,128)(2,1)S(1)} %add_convert_fusion.1), channel_id=1, source_target_pairs={{0,2},{1,3},{2,0},{3,1},{4,6},{5,7},{6,4},{7,5},{8,10},{9,11},{10,... | collective-permute-start | bytes 245768 | tf_op jit(solution)/shard_map/ppermute | solution.py:224

commit v22 on v21

--- a/solution.py
+++ b/solution.py
@@ -233,7 +233,7 @@
 
     cuts = [block_count * k // 14 for k in (0, 4, 8, 11, 14)]
     parts = list(zip(cuts[:-1], cuts[1:]))
-    loads = [block_count * k // 14 for k in (0, 5, 8, 11, 13, 14)]
+    loads = [block_count * k // 14 for k in (0, 4, 8, 11, 12, 14)]
     bands = 4
     small = [
         pltpu.with_memory_space_constraint(x, pltpu.HBM)
@@ -297,7 +297,7 @@
         out = kernel_call(
             functools.partial(base_kernel, block, places, numbers, streamed),
             "base_part",
-            (15 * 10**8, 15 * 10**8, 10**10, 1)[n],
+            (15 * 10**8, 15 * 10**8, 1, 1)[n],
             1,
             12,
             in_specs=[vmem, anywhere] + [vmem] * len(used) + [anywhere] * len(after),

time: 41.5 us -> 42.6 us (1.027)
  starting transfers between devices: 16.8 us -> 18.2 us
    ppermute x7, starting transfers between devices: 11.1 us -> 13 us  [from_owner(): return lax.ppermute(x, ('groups', 'adapter'), pairs)]
    pallas_call x1, Pallas kernels: 4.6 us -> 3.94 us  [paired(): kernel_call(functools.partial(cut_kernel, block, range(loads[1]), len(sma...]
    pallas_call x4, Pallas kernels: 10.2 us -> 10.8 us  [base_part(): kernel_call(functools.partial(base_kernel, block, places, numbers, stream...]
    ppermute x1, starting transfers between devices: 1.36 us -> 0.79 us  [from_group(): return lax.ppermute(x, 'groups', [(0, 1), (1, 0)])]
  transfers between devices with their start and end apart: 15 -> 15, of which waited for: 7 -> 6; matrix products, arithmetic and copies ran while one was open for 0% -> 0% of each run, Pallas kernels for 36% -> 35%
where the time goes in v22:
time: 42.6 us; the launch traced here: 42.5 us
  starting transfers between devices  18.2 us (43%)
  Pallas kernels  15.5 us (36%)
  waiting for transfers between devices  7.72 us (18%)
  other arithmetic  0.89 us (2%)
    ppermute x7, starting transfers between devices, from_owner(): return lax.ppermute(x, ('groups', 'adapter'), pairs)  13 us
    pallas_call x4, Pallas kernels, base_part(): kernel_call(functools.partial(base_kernel, block, places, numbers, stream...  10.8 us
    ppermute x7, waiting for transfers between devices, from_tensor(): return lax.ppermute(x, 'tensor', [(s, s ^ m) for s in range(4)])  6.33 us
    ppermute x7, starting transfers between devices, from_tensor(): return lax.ppermute(x, 'tensor', [(s, s ^ m) for s in range(4)])  4.36 us
    pallas_call x1, Pallas kernels, paired(): kernel_call(functools.partial(cut_kernel, block, range(loads[1]), len(sma...  3.94 us
    ppermute x7, waiting for transfers between devices, from_owner(): return lax.ppermute(x, ('groups', 'adapter'), pairs)  1.39 us
  transfers between devices with their start and end apart: 15, of which 6 were waited for; matrix products, arithmetic and copies ran while one was open for 0% of the time, Pallas kernels for 35%

profile of v22, /device:TPU:0, one launch (start us, length us, event | category | flops | bytes accessed | tf_op | source)
XLA Modules:
  0.0 42.5 jit_solution(6682503594760736319)
XLA Ops:
  0.0 4.0 %collective-permute-start = (bf16[16,2048]{1,0:T(8,128)(2,1)}, bf16[16,2048]{1,0:T(8,128)(2,1)S(1)}, u32[]{:S(2)}, u32[]{:S(2)}) collective-permute-start(bf16[16,2048]{1,0:T(8,128)(2,1)} %refs_2_.1), channel_id=1, source_target_pairs={{0,8},{4,12},{8,0},{12,4},{16,24},{20,28},{24,16},{28,20},{1,9},{5... | collective-permute-start | bytes 196616 | tf_op jit(solution)/shard_map/ppermute | solution.py:221
  4.0 1.3 %collective-permute-start.1 = (bf16[16,2048]{1,0:T(8,128)(2,1)}, bf16[16,2048]{1,0:T(8,128)(2,1)S(1)}, u32[]{:S(2)}, u32[]{:S(2)}) collective-permute-start(bf16[16,2048]{1,0:T(8,128)(2,1)} %refs_2_.1), channel_id=1, source_target_pairs={{0,12},{4,8},{8,4},{12,0},{16,28},{20,24},{24,20},{28,16},{1,13},{... | collective-permute-start | bytes 196616 | tf_op jit(solution)/shard_map/ppermute | solution.py:221
  5.4 0.2 collective-permute-start.2
  5.6 3.9 %cut_expand.1 = (bf16[16,7168]{1,0:T(8,128)(2,1)S(1)}, bf16[16,7168]{1,0:T(8,128)(2,1)S(1)}, bf16[16,7168]{1,0:T(8,128)(2,1)S(1)}, s32[1,4]{1,0:T(1,128)S(1)}, s...) custom-call(bf16[1,16,28672]{2,1,0:T(8,128)(2,1)} %expand.1, ...), custom_call_target="tpu_custom_call" | custom-call | flops 1 | bytes 1 | tf_op jit(solution)/shard_map/cut_expand/pallas_call | solution.py:247
  9.6 2.9 %collective-permute-start.6 = (bf16[16,7168]{1,0:T(8,128)(2,1)S(1)}, bf16[16,7168]{1,0:T(8,128)(2,1)S(1)}, u32[]{:S(2)}, u32[]{:S(2)}) collective-permute-start(bf16[16,7168]{1,0:T(8,128)(2,1)S(1)} %get-tuple-element.57), channel_id=1, source_target_pairs={{0,8},{4,12},{8,0},{12,4},{16,28},{20,24},{24,20},{28,16},{1,9},{5... | collective-permute-start | bytes 688136 | tf_op jit(solution)/shard_map/ppermute | solution.py:221
  12.5 0.6 %collective-permute-start.8 = (bf16[16,7168]{1,0:T(8,128)(2,1)S(1)}, bf16[16,7168]{1,0:T(8,128)(2,1)S(1)}, u32[]{:S(2)}, u32[]{:S(2)}) collective-permute-start(bf16[16,7168]{1,0:T(8,128)(2,1)S(1)} %get-tuple-element.66), channel_id=1, source_target_pairs={{0,4},{4,0},{8,12},{12,8},{16,20},{20,16},{24,28},{28,24},{1,5},{5... | collective-permute-start | bytes 688136 | tf_op jit(solution)/shard_map/ppermute | solution.py:221
  13.1 0.0 collective-permute-done.refs_1_
  13.1 0.0 collective-permute-done.1.refs_2_
  13.1 0.0 collective-permute-done.2.refs_3_
  13.1 0.3 gather_rows.1
  13.4 0.1 collective-permute-start.3
  13.5 3.6 %base_part.4 = (f32[64,2048]{1,0:T(8,128)S(1)}, bf16[4,2048,512]{2,1,0:T(8,128)(2,1)S(1)}) custom-call(bf16[64,2048]{1,0:T(8,128)(2,1)S(1)} %get-tuple-element.46.rows, bf16[2048,7168]{1,0:T(8,128)(2,1)} %weight.9, bf16[4,2048,512]{2,1,0:T(8,128)(2,1)S(1)} %get-tuple-element.47.refs_0_, f32[32,64]{1,0:T(8,128)S(1)} %get-tuple-element.45.refs_1_), custom_call_target="tpu_custom_call" | custom-call | flops 1500000000 | bytes 1 | tf_op jit(solution)/shard_map/base_part/pallas_call | solution.py:297
  17.1 0.0 collective-permute-done.3
  17.1 1.6 %collective-permute-start.4 = (f32[16,64]{1,0:T(8,128)S(1)}, f32[16,64]{1,0:T(8,128)S(1)}, u32[]{:S(2)}, u32[]{:S(2)}) collective-permute-start(f32[16,64]{1,0:T(8,128)S(1)} %slice.16), channel_id=1, source_target_pairs={{0,2},{1,3},{2,0},{3,1},{4,6},{5,7},{6,4},{7,5},{8,10},{9,11},{10,... | collective-permute-start | bytes 12296 | tf_op jit(solution)/shard_map/ppermute | solution.py:224
  18.7 3.0 %base_part.5 = (f32[64,2048]{1,0:T(8,128)S(1)}, bf16[3,2048,512]{2,1,0:T(8,128)(2,1)S(1)}) custom-call(bf16[64,2048]{1,0:T(8,128)(2,1)S(1)} %get-tuple-element.46.rows, bf16[2048,7168]{1,0:T(8,128)(2,1)} %weight.9, bf16[4,2048,512]{2,1,0:T(8,128)(2,1)S(1)} %get-tuple-element.52.refs_0_, f32[32,64]{1,0:T(8,128)S(1)} %add.27.refs_1_), custom_call_target="tpu_custom_call" | custom-call | flops 1500000000 | bytes 1 | tf_op jit(solution)/shard_map/base_part/pallas_call | solution.py:297
  21.6 0.0 collective-permute-done.4
  21.7 0.7 %collective-permute-done.6.refs_2_.refs_6_ = bf16[16,7168]{1,0:T(8,128)(2,1)S(1)} collective-permute-done((bf16[16,7168]{1,0:T(8,128)(2,1)S(1)}, bf16[16,7168]{1,0:T(8,128)(2,1)S(1)}, u32[]{:S(2)}, u32[]{:S(2)}) %collective-permute-start.6) | collective-permute-done | bytes 229408 | tf_op jit(solution)/shard_map/ppermute | solution.py:221
  22.3 0.8 %collective-permute-start.9 = (bf16[16,7168]{1,0:T(8,128)(2,1)S(1)}, bf16[16,7168]{1,0:T(8,128)(2,1)S(1)}, u32[]{:S(2)}, u32[]{:S(2)}) collective-permute-start(bf16[16,7168]{1,0:T(8,128)(2,1)S(1)} %collective-permute-done.6.refs_2_.refs_6_), channel_id=1, source_target_pairs={{0,16},{16,0},{1,17},{17,1},{2,18},{18,2},{3,19},{19,3},{4,20},{20... | collective-permute-start | bytes 688136 | tf_op jit(solution)/shard_map/ppermute | solution.py:227
  23.1 2.2 %collective-permute-start.5 = (bf16[16,64]{1,0:T(8,128)(2,1)S(1)}, bf16[16,64]{1,0:T(8,128)(2,1)S(1)}, u32[]{:S(2)}, u32[]{:S(2)}) collective-permute-start(bf16[16,64]{1,0:T(8,128)(2,1)S(1)} %fusion.3.refs_1_), channel_id=1, source_target_pairs={{0,8},{4,12},{8,0},{12,4},{16,24},{20,28},{24,16},{28,20},{1,9},{5... | collective-permute-start | bytes 6152 | tf_op jit(solution)/shard_map/ppermute | solution.py:221
  25.4 1.6 %base_part.6 = (f32[64,1536]{1,0:T(8,128)S(1)}, bf16[1,2048,512]{2,1,0:T(8,128)(2,1)S(1)}) custom-call(bf16[64,2048]{1,0:T(8,128)(2,1)S(1)} %get-tuple-element.46.rows, bf16[2048,7168]{1,0:T(8,128)(2,1)} %weight.9, bf16[3,2048,512]{2,1,0:T(8,128)(2,1)S(1)} %get-tuple-element.56.refs_0_, bf16[16,64]{1,0:T(8,128)(2,1)S(1)} %fusion.3.refs_1_, ...), custom_call_target="tpu_custom_call" | custom-call | flops 1 | bytes 1 | tf_op jit(solution)/shard_map/base_part/pallas_call | solution.py:297
  26.9 0.7 %collective-permute-done.5 = bf16[16,64]{1,0:T(8,128)(2,1)S(1)} collective-permute-done((bf16[16,64]{1,0:T(8,128)(2,1)S(1)}, bf16[16,64]{1,0:T(8,128)(2,1)S(1)}, u32[]{:S(2)}, u32[]{:S(2)}) %collective-permute-start.5) | collective-permute-done | bytes 2080 | tf_op jit(solution)/shard_map/ppermute | solution.py:221
  27.7 1.6 %collective-permute-start.7 = (bf16[16,64]{1,0:T(8,128)(2,1)S(1)}, bf16[16,64]{1,0:T(8,128)(2,1)S(1)}, u32[]{:S(2)}, u32[]{:S(2)}) collective-permute-start(bf16[16,64]{1,0:T(8,128)(2,1)S(1)} %add.29.refs_1_), channel_id=1, source_target_pairs={{0,4},{4,0},{8,12},{12,8},{16,20},{20,16},{24,28},{28,24},{1,5},{5... | collective-permute-start | bytes 6152 | tf_op jit(solution)/shard_map/ppermute | solution.py:221
  29.3 2.7 %base_part.7.refs_3_ = f32[64,1536]{1,0:T(8,128)S(1)} custom-call(bf16[64,2048]{1,0:T(8,128)(2,1)S(1)} %get-tuple-element.46.rows, bf16[2048,7168]{1,0:T(8,128)(2,1)} %weight.9, bf16[1,2048,512]{2,1,0:T(8,128)(2,1)S(1)} %get-tuple-element.62.refs_0_, bf16[16,64]{1,0:T(8,128)(2,1)S(1)} %add.29.refs_1_, bf16[16,7168]{1,0:T(8,128)(2,1)S(1)} %collective-permute-done.6.refs_2_.refs_6_), custom_call_target="tpu_custom_call" | custom-call | flops 1 | bytes 1 | tf_op jit(solution)/shard_map/base_part/pallas_call | solution.py:297
  32.0 0.0 collective-permute-done.7
  32.0 0.0 collective-permute-done.8.refs_7_
  32.0 0.0 collective-permute-done.9.refs_8_
  32.0 0.5 %add_delta.1 = (f32[16,7168]{1,0:T(8,128)S(1)}, f32[16,7168]{1,0:T(8,128)S(1)}, f32[16,2560]{1,0:T(8,128)S(1)}, f32[16,4608]{1,0:T(8,128)S(1)}, f32[16,2560]{1,0:T(8,128)S(1)}, /*index=5*/f32[16,4608]{1,0:T(8,128)S(1)}) custom-call(s32[1,64]{1,0:T(1,128)S(1)} %get-tuple-element.44.slot, f32[64,2048]{1,0:T(8,128)S(1)} %get-tuple-element.49.refs_0_, ...), custom_call_target="tpu_custom_call" | custom-call | flops 1 | bytes 1 | tf_op jit(solution)/shard_map/add_delta/pallas_call | solution.py:335
  32.5 0.1 collective-permute-start.12
  32.6 0.5 %collective-permute-start.10 = (f32[16,4608]{1,0:T(8,128)S(1)}, f32[16,4608]{1,0:T(8,128)S(1)}, u32[]{:S(2)}, u32[]{:S(2)}) collective-permute-start(f32[16,4608]{1,0:T(8,128)S(1)} %get-tuple-element.68), channel_id=1, source_target_pairs={{0,1},{1,0},{2,3},{3,2},{4,5},{5,4},{6,7},{7,6},{8,9},{9,8},{10,11... | collective-permute-start | bytes 884744 | tf_op jit(solution)/shard_map/ppermute | solution.py:224
  33.1 0.9 %collective-permute-done.12 = f32[16,2560]{1,0:T(8,128)S(1)} collective-permute-done((f32[16,2560]{1,0:T(8,128)S(1)}, f32[16,2560]{1,0:T(8,128)S(1)}, u32[]{:S(2)}, u32[]{:S(2)}) %collective-permute-start.12) | collective-permute-done | bytes 163872 | tf_op jit(solution)/shard_map/ppermute | solution.py:224
  34.0 1.2 %collective-permute-start.13 = (bf16[16,2560]{1,0:T(8,128)(2,1)S(1)}, bf16[16,2560]{1,0:T(8,128)(2,1)S(1)}, u32[]{:S(2)}, u32[]{:S(2)}) collective-permute-start(bf16[16,2560]{1,0:T(8,128)(2,1)S(1)} %add_convert_fusion.1), channel_id=1, source_target_pairs={{0,2},{1,3},{2,0},{3,1},{4,6},{5,7},{6,4},{7,5},{8,10},{9,11},{10,... | collective-permute-start | bytes 245768 | tf_op jit(solution)/shard_map/ppermute | solution.py:224
  35.2 0.0 collective-permute-done.10
  35.2 0.0 collective-permute-start.11
  35.2 1.0 %collective-permute-start.14 = (bf16[16,4608]{1,0:T(8,128)(2,1)S(1)}, bf16[16,4608]{1,0:T(8,128)(2,1)S(1)}, u32[]{:S(2)}, u32[]{:S(2)}) collective-permute-start(bf16[16,4608]{1,0:T(8,128)(2,1)S(1)} %add_convert_fusion), channel_id=1, source_target_pairs={{0,2},{1,3},{2,0},{3,1},{4,6},{5,7},{6,4},{7,5},{8,10},{9,11},{10,... | collective-permute-start | bytes 442376 | tf_op jit(solution)/shard_map/ppermute | solution.py:224
  36.2 0.8 %collective-permute-done.11 = f32[16,7168]{1,0:T(8,128)S(1)} collective-permute-done((f32[16,7168]{1,0:T(8,128)S(1)}, f32[16,7168]{1,0:T(8,128)S(1)}, u32[]{:S(2)}, u32[]{:S(2)}) %collective-permute-start.11) | collective-permute-done | bytes 458784 | tf_op jit(solution)/shard_map/ppermute | solution.py:224
  37.1 1.7 %collective-permute-done.13 = bf16[16,2560]{1,0:T(8,128)(2,1)S(1)} collective-permute-done((bf16[16,2560]{1,0:T(8,128)(2,1)S(1)}, bf16[16,2560]{1,0:T(8,128)(2,1)S(1)}, u32[]{:S(2)}, u32[]{:S(2)}) %collective-permute-start.13) | collective-permute-done | bytes 81952 | tf_op jit(solution)/shard_map/ppermute | solution.py:224
  38.8 3.0 %collective-permute-done.14 = bf16[16,4608]{1,0:T(8,128)(2,1)S(1)} collective-permute-done((bf16[16,4608]{1,0:T(8,128)(2,1)S(1)}, bf16[16,4608]{1,0:T(8,128)(2,1)S(1)}, u32[]{:S(2)}, u32[]{:S(2)}) %collective-permute-start.14) | collective-permute-done | bytes 147488 | tf_op jit(solution)/shard_map/ppermute | solution.py:224
  41.8 0.7 %pad_maximum_fusion = bf16[16,7168]{1,0:T(8,128)(2,1)} fusion(bf16[16,4608]{1,0:T(8,128)(2,1)S(1)} %fusion, bf16[16,2560]{1,0:T(8,128)(2,1)S(1)} %fusion.1), kind=kLoop, calls=%fused_computation.3 | loop fusion | flops 458752 | bytes 458752 | tf_op jit(solution)/shard_map/concatenate | solution.py:358
  (10 shorter events, 0.2 us)
Async XLA Ops:
  0.0 13.1 %collective-permute-start = (bf16[16,2048]{1,0:T(8,128)(2,1)}, bf16[16,2048]{1,0:T(8,128)(2,1)S(1)}, u32[]{:S(2)}, u32[]{:S(2)}) collective-permute-start(bf16[16,2048]{1,0:T(8,128)(2,1)} %refs_2_.1), channel_id=1, source_target_pairs={{0,8},{4,12},{8,0},{12,4},{16,24},{20,28},{24,16},{28,20},{1,9},{5... | collective-permute-start | bytes 196616 | tf_op jit(solution)/shard_map/ppermute | solution.py:221
  4.0 9.1 %collective-permute-start.1 = (bf16[16,2048]{1,0:T(8,128)(2,1)}, bf16[16,2048]{1,0:T(8,128)(2,1)S(1)}, u32[]{:S(2)}, u32[]{:S(2)}) collective-permute-start(bf16[16,2048]{1,0:T(8,128)(2,1)} %refs_2_.1), channel_id=1, source_target_pairs={{0,12},{4,8},{8,4},{12,0},{16,28},{20,24},{24,20},{28,16},{1,13},{... | collective-permute-start | bytes 196616 | tf_op jit(solution)/shard_map/ppermute | solution.py:221
  5.4 7.7 %collective-permute-start.2 = (bf16[16,2048]{1,0:T(8,128)(2,1)}, bf16[16,2048]{1,0:T(8,128)(2,1)S(1)}, u32[]{:S(2)}, u32[]{:S(2)}) collective-permute-start(bf16[16,2048]{1,0:T(8,128)(2,1)} %refs_2_.1), channel_id=1, source_target_pairs={{0,4},{4,0},{8,12},{12,8},{16,20},{20,16},{24,28},{28,24},{1,5},{5... | collective-permute-start | bytes 196616 | tf_op jit(solution)/shard_map/ppermute | solution.py:221
  9.6 12.8 %collective-permute-start.6 = (bf16[16,7168]{1,0:T(8,128)(2,1)S(1)}, bf16[16,7168]{1,0:T(8,128)(2,1)S(1)}, u32[]{:S(2)}, u32[]{:S(2)}) collective-permute-start(bf16[16,7168]{1,0:T(8,128)(2,1)S(1)} %get-tuple-element.57), channel_id=1, source_target_pairs={{0,8},{4,12},{8,0},{12,4},{16,28},{20,24},{24,20},{28,16},{1,9},{5... | collective-permute-start | bytes 688136 | tf_op jit(solution)/shard_map/ppermute | solution.py:221
  12.5 19.5 %collective-permute-start.8 = (bf16[16,7168]{1,0:T(8,128)(2,1)S(1)}, bf16[16,7168]{1,0:T(8,128)(2,1)S(1)}, u32[]{:S(2)}, u32[]{:S(2)}) collective-permute-start(bf16[16,7168]{1,0:T(8,128)(2,1)S(1)} %get-tuple-element.66), channel_id=1, source_target_pairs={{0,4},{4,0},{8,12},{12,8},{16,20},{20,16},{24,28},{28,24},{1,5},{5... | collective-permute-start | bytes 688136 | tf_op jit(solution)/shard_map/ppermute | solution.py:221
  13.4 3.7 %collective-permute-start.3 = (f32[32,64]{1,0:T(8,128)S(1)}, f32[32,64]{1,0:T(8,128)S(1)}, u32[]{:S(2)}, u32[]{:S(2)}) collective-permute-start(f32[32,64]{1,0:T(8,128)S(1)} %get-tuple-element.45.refs_1_), channel_id=1, source_target_pairs={{0,1},{1,0},{2,3},{3,2},{4,5},{5,4},{6,7},{7,6},{8,9},{9,8},{10,11... | collective-permute-start | bytes 24584 | tf_op jit(solution)/shard_map/ppermute | solution.py:224
  17.1 4.5 %collective-permute-start.4 = (f32[16,64]{1,0:T(8,128)S(1)}, f32[16,64]{1,0:T(8,128)S(1)}, u32[]{:S(2)}, u32[]{:S(2)}) collective-permute-start(f32[16,64]{1,0:T(8,128)S(1)} %slice.16), channel_id=1, source_target_pairs={{0,2},{1,3},{2,0},{3,1},{4,6},{5,7},{6,4},{7,5},{8,10},{9,11},{10,... | collective-permute-start | bytes 12296 | tf_op jit(solution)/shard_map/ppermute | solution.py:224
  22.3 9.7 %collective-permute-start.9 = (bf16[16,7168]{1,0:T(8,128)(2,1)S(1)}, bf16[16,7168]{1,0:T(8,128)(2,1)S(1)}, u32[]{:S(2)}, u32[]{:S(2)}) collective-permute-start(bf16[16,7168]{1,0:T(8,128)(2,1)S(1)} %collective-permute-done.6.refs_2_.refs_6_), channel_id=1, source_target_pairs={{0,16},{16,0},{1,17},{17,1},{2,18},{18,2},{3,19},{19,3},{4,20},{20... | collective-permute-start | bytes 688136 | tf_op jit(solution)/shard_map/ppermute | solution.py:227
  23.1 4.5 %collective-permute-start.5 = (bf16[16,64]{1,0:T(8,128)(2,1)S(1)}, bf16[16,64]{1,0:T(8,128)(2,1)S(1)}, u32[]{:S(2)}, u32[]{:S(2)}) collective-permute-start(bf16[16,64]{1,0:T(8,128)(2,1)S(1)} %fusion.3.refs_1_), channel_id=1, source_target_pairs={{0,8},{4,12},{8,0},{12,4},{16,24},{20,28},{24,16},{28,20},{1,9},{5... | collective-permute-start | bytes 6152 | tf_op jit(solution)/shard_map/ppermute | solution.py:221
  27.7 4.4 %collective-permute-start.7 = (bf16[16,64]{1,0:T(8,128)(2,1)S(1)}, bf16[16,64]{1,0:T(8,128)(2,1)S(1)}, u32[]{:S(2)}, u32[]{:S(2)}) collective-permute-start(bf16[16,64]{1,0:T(8,128)(2,1)S(1)} %add.29.refs_1_), channel_id=1, source_target_pairs={{0,4},{4,0},{8,12},{12,8},{16,20},{20,16},{24,28},{28,24},{1,5},{5... | collective-permute-start | bytes 6152 | tf_op jit(solution)/shard_map/ppermute | solution.py:221
  32.5 1.5 %collective-permute-start.12 = (f32[16,2560]{1,0:T(8,128)S(1)}, f32[16,2560]{1,0:T(8,128)S(1)}, u32[]{:S(2)}, u32[]{:S(2)}) collective-permute-start(f32[16,2560]{1,0:T(8,128)S(1)} %get-tuple-element.72), channel_id=1, source_target_pairs={{0,1},{1,0},{2,3},{3,2},{4,5},{5,4},{6,7},{7,6},{8,9},{9,8},{10,11... | collective-permute-start | bytes 491528 | tf_op jit(solution)/shard_map/ppermute | solution.py:224
  32.6 2.6 %collective-permute-start.10 = (f32[16,4608]{1,0:T(8,128)S(1)}, f32[16,4608]{1,0:T(8,128)S(1)}, u32[]{:S(2)}, u32[]{:S(2)}) collective-permute-start(f32[16,4608]{1,0:T(8,128)S(1)} %get-tuple-element.68), channel_id=1, source_target_pairs={{0,1},{1,0},{2,3},{3,2},{4,5},{5,4},{6,7},{7,6},{8,9},{9,8},{10,11... | collective-permute-start | bytes 884744 | tf_op jit(solution)/shard_map/ppermute | solution.py:224
  34.0 4.7 %collective-permute-start.13 = (bf16[16,2560]{1,0:T(8,128)(2,1)S(1)}, bf16[16,2560]{1,0:T(8,128)(2,1)S(1)}, u32[]{:S(2)}, u32[]{:S(2)}) collective-permute-start(bf16[16,2560]{1,0:T(8,128)(2,1)S(1)} %add_convert_fusion.1), channel_id=1, source_target_pairs={{0,2},{1,3},{2,0},{3,1},{4,6},{5,7},{6,4},{7,5},{8,10},{9,11},{10,... | collective-permute-start | bytes 245768 | tf_op jit(solution)/shard_map/ppermute | solution.py:224
  35.2 1.8 %collective-permute-start.11 = (f32[16,7168]{1,0:T(8,128)S(1)}, f32[16,7168]{1,0:T(8,128)S(1)}, u32[]{:S(2)}, u32[]{:S(2)}) collective-permute-start(f32[16,7168]{1,0:T(8,128)S(1)} %get-tuple-element.70), channel_id=1, source_target_pairs={{0,1},{1,0},{2,3},{3,2},{4,5},{5,4},{6,7},{7,6},{8,9},{9,8},{10,11... | collective-permute-start | bytes 1376264 | tf_op jit(solution)/shard_map/ppermute | solution.py:224
  35.2 6.5 %collective-permute-start.14 = (bf16[16,4608]{1,0:T(8,128)(2,1)S(1)}, bf16[16,4608]{1,0:T(8,128)(2,1)S(1)}, u32[]{:S(2)}, u32[]{:S(2)}) collective-permute-start(bf16[16,4608]{1,0:T(8,128)(2,1)S(1)} %add_convert_fusion), channel_id=1, source_target_pairs={{0,2},{1,3},{2,0},{3,1},{4,6},{5,7},{6,4},{7,5},{8,10},{9,11},{10,... | collective-permute-start | bytes 442376 | tf_op jit(solution)/shard_map/ppermute | solution.py:224

commit v23 on v19

--- a/solution.py
+++ b/solution.py
@@ -261,7 +261,9 @@
         ],
     )(expand, weight, *small)
     loaded = [held]
-    across, beside = from_owner(across, 2, 3), from_owner(beside, 1, 1)
+    across, blocks[0] = lax.optimization_barrier((across, blocks[0]))
+    beside = from_owner(beside, 1, 1)
+    across = from_owner(across, 2, 3)
 
     rows, keep, send, slot = kernel_call(
         functools.partial(gather_kernel, (0, *offsets)),
@@ -297,7 +299,7 @@
         out = kernel_call(
             functools.partial(base_kernel, block, places, numbers, streamed),
             "base_part",
-            (15 * 10**8, 15 * 10**8, 10**10, 1)[n],
+            (10**9, 1, 10**10, 1)[n],
             1,
             12,
             in_specs=[vmem, anywhere] + [vmem] * len(used) + [anywhere] * len(after),

time: 41 us -> 42.9 us (1.046)
  waiting for transfers between devices: 7.09 us -> 10.1 us
  starting transfers between devices: 17.2 us -> 16 us
    ppermute x7, waiting for transfers between devices: 0.47 us -> 2.8 us  [from_owner(): return lax.ppermute(x, ('groups', 'adapter'), pairs)]
    ppermute x1, starting transfers between devices: 1.19 us -> 0.26 us  [from_group(): return lax.ppermute(x, 'groups', [(0, 1), (1, 0)])]
    ppermute x1, waiting for transfers between devices: 0.29 us -> 0.82 us  [from_group(): return lax.ppermute(x, 'groups', [(0, 1), (1, 0)])]
  transfers between devices with their start and end apart: 15 -> 15, of which waited for: 6 -> 8; matrix products, arithmetic and copies ran while one was open for 0% -> 0% of each run, Pallas kernels for 37% -> 35%
where the time goes in v23:
time: 42.9 us; the launch traced here: 42.7 us
  starting transfers between devices  16 us (37%)
  Pallas kernels  15.5 us (36%)
  waiting for transfers between devices  10.1 us (24%)
  other arithmetic  0.89 us (2%)
    ppermute x7, starting transfers between devices, from_owner(): return lax.ppermute(x, ('groups', 'adapter'), pairs)  11.4 us
    pallas_call x4, Pallas kernels, base_part(): kernel_call(functools.partial(base_kernel, block, places, numbers, stream...  10.8 us
    ppermute x7, waiting for transfers between devices, from_tensor(): return lax.ppermute(x, 'tensor', [(s, s ^ m) for s in range(4)])  6.48 us
    ppermute x7, starting transfers between devices, from_tensor(): return lax.ppermute(x, 'tensor', [(s, s ^ m) for s in range(4)])  4.41 us
    pallas_call x1, Pallas kernels, paired(): kernel_call(functools.partial(cut_kernel, block, range(loads[1]), len(sma...  3.94 us
    ppermute x7, waiting for transfers between devices, from_owner(): return lax.ppermute(x, ('groups', 'adapter'), pairs)  2.8 us
  transfers between devices with their start and end apart: 15, of which 8 were waited for; matrix products, arithmetic and copies ran while one was open for 0% of the time, Pallas kernels for 35%

profile of v23, /device:TPU:0, one launch (start us, length us, event | category | flops | bytes accessed | tf_op | source)
XLA Modules:
  0.0 42.7 jit_solution(5266293779688499174)
XLA Ops:
  0.0 4.0 %collective-permute-start = (bf16[16,2048]{1,0:T(8,128)(2,1)}, bf16[16,2048]{1,0:T(8,128)(2,1)S(1)}, u32[]{:S(2)}, u32[]{:S(2)}) collective-permute-start(bf16[16,2048]{1,0:T(8,128)(2,1)} %refs_2_.1), channel_id=1, source_target_pairs={{0,8},{4,12},{8,0},{12,4},{16,24},{20,28},{24,16},{28,20},{1,9},{5... | collective-permute-start | bytes 196616 | tf_op jit(solution)/shard_map/ppermute | solution.py:221
  4.0 1.3 %collective-permute-start.1 = (bf16[16,2048]{1,0:T(8,128)(2,1)}, bf16[16,2048]{1,0:T(8,128)(2,1)S(1)}, u32[]{:S(2)}, u32[]{:S(2)}) collective-permute-start(bf16[16,2048]{1,0:T(8,128)(2,1)} %refs_2_.1), channel_id=1, source_target_pairs={{0,12},{4,8},{8,4},{12,0},{16,28},{20,24},{24,20},{28,16},{1,13},{... | collective-permute-start | bytes 196616 | tf_op jit(solution)/shard_map/ppermute | solution.py:221
  5.4 0.2 collective-permute-start.2
  5.6 3.9 %cut_expand.1 = (bf16[16,7168]{1,0:T(8,128)(2,1)S(1)}, bf16[16,7168]{1,0:T(8,128)(2,1)S(1)}, bf16[16,7168]{1,0:T(8,128)(2,1)S(1)}, s32[1,4]{1,0:T(1,128)S(1)}, s...) custom-call(bf16[1,16,28672]{2,1,0:T(8,128)(2,1)} %expand.1, ...), custom_call_target="tpu_custom_call" | custom-call | flops 1 | bytes 1 | tf_op jit(solution)/shard_map/cut_expand/pallas_call | solution.py:247
  9.6 0.0 collective-permute-done.refs_1_
  9.6 0.9 %collective-permute-done.1.refs_2_ = bf16[16,2048]{1,0:T(8,128)(2,1)S(1)} collective-permute-done((bf16[16,2048]{1,0:T(8,128)(2,1)}, bf16[16,2048]{1,0:T(8,128)(2,1)S(1)}, u32[]{:S(2)}, u32[]{:S(2)}) %collective-permute-start.1) | collective-permute-done | bytes 65568 | tf_op jit(solution)/shard_map/ppermute | solution.py:221
  10.5 0.1 collective-permute-done.2.refs_3_
  10.6 0.2 gather_rows.1
  10.8 0.1 collective-permute-start.3
  10.9 2.7 %collective-permute-start.6 = (bf16[16,7168]{1,0:T(8,128)(2,1)S(1)}, bf16[16,7168]{1,0:T(8,128)(2,1)S(1)}, u32[]{:S(2)}, u32[]{:S(2)}) collective-permute-start(bf16[16,7168]{1,0:T(8,128)(2,1)S(1)} %get-tuple-element.61), channel_id=1, source_target_pairs={{0,8},{4,12},{8,0},{12,4},{16,28},{20,24},{24,20},{28,16},{1,9},{5... | collective-permute-start | bytes 688136 | tf_op jit(solution)/shard_map/ppermute | solution.py:221
  13.6 3.6 %base_part.4 = (f32[64,2048]{1,0:T(8,128)S(1)}, bf16[4,2048,512]{2,1,0:T(8,128)(2,1)S(1)}) custom-call(bf16[64,2048]{1,0:T(8,128)(2,1)S(1)} %get-tuple-element.50.rows, bf16[2048,7168]{1,0:T(8,128)(2,1)} %weight.9, bf16[4,2048,512]{2,1,0:T(8,128)(2,1)S(1)} %get-tuple-element.51.refs_0_, f32[32,64]{1,0:T(8,128)S(1)} %get-tuple-element.49.refs_1_), custom_call_target="tpu_custom_call" | custom-call | flops 1000000000 | bytes 1 | tf_op jit(solution)/shard_map/base_part/pallas_call | solution.py:299
  17.2 0.0 collective-permute-done.3
  17.3 1.6 %collective-permute-start.4 = (f32[16,64]{1,0:T(8,128)S(1)}, f32[16,64]{1,0:T(8,128)S(1)}, u32[]{:S(2)}, u32[]{:S(2)}) collective-permute-start(f32[16,64]{1,0:T(8,128)S(1)} %slice.16), channel_id=1, source_target_pairs={{0,2},{1,3},{2,0},{3,1},{4,6},{5,7},{6,4},{7,5},{8,10},{9,11},{10,... | collective-permute-start | bytes 12296 | tf_op jit(solution)/shard_map/ppermute | solution.py:224
  18.8 0.9 %collective-permute-start.8 = (bf16[16,7168]{1,0:T(8,128)(2,1)S(1)}, bf16[16,7168]{1,0:T(8,128)(2,1)S(1)}, u32[]{:S(2)}, u32[]{:S(2)}) collective-permute-start(bf16[16,7168]{1,0:T(8,128)(2,1)S(1)} %get-tuple-element.70), channel_id=1, source_target_pairs={{0,4},{4,0},{8,12},{12,8},{16,20},{20,16},{24,28},{28,24},{1,5},{5... | collective-permute-start | bytes 688136 | tf_op jit(solution)/shard_map/ppermute | solution.py:221
  19.7 3.0 %base_part.5 = (f32[64,2048]{1,0:T(8,128)S(1)}, bf16[3,2048,512]{2,1,0:T(8,128)(2,1)S(1)}) custom-call(bf16[64,2048]{1,0:T(8,128)(2,1)S(1)} %get-tuple-element.50.rows, bf16[2048,7168]{1,0:T(8,128)(2,1)} %weight.9, bf16[4,2048,512]{2,1,0:T(8,128)(2,1)S(1)} %get-tuple-element.56.refs_0_, f32[32,64]{1,0:T(8,128)S(1)} %add.27.refs_1_), custom_call_target="tpu_custom_call" | custom-call | flops 1 | bytes 1 | tf_op jit(solution)/shard_map/base_part/pallas_call | solution.py:299
  22.7 0.0 collective-permute-done.4
  22.7 0.4 collective-permute-start.5
  23.1 1.8 %collective-permute-done.6.refs_2_.refs_6_ = bf16[16,7168]{1,0:T(8,128)(2,1)S(1)} collective-permute-done((bf16[16,7168]{1,0:T(8,128)(2,1)S(1)}, bf16[16,7168]{1,0:T(8,128)(2,1)S(1)}, u32[]{:S(2)}, u32[]{:S(2)}) %collective-permute-start.6) | collective-permute-done | bytes 229408 | tf_op jit(solution)/shard_map/ppermute | solution.py:221
  24.9 0.3 collective-permute-start.9
  25.1 2.2 %base_part.6 = (f32[64,1536]{1,0:T(8,128)S(1)}, bf16[2,2048,512]{2,1,0:T(8,128)(2,1)S(1)}) custom-call(bf16[64,2048]{1,0:T(8,128)(2,1)S(1)} %get-tuple-element.50.rows, bf16[2048,7168]{1,0:T(8,128)(2,1)} %weight.9, bf16[3,2048,512]{2,1,0:T(8,128)(2,1)S(1)} %get-tuple-element.60.refs_0_, bf16[16,64]{1,0:T(8,128)(2,1)S(1)} %fusion.3.refs_1_, ...), custom_call_target="tpu_custom_call" | custom-call | flops 10000000000 | bytes 1 | tf_op jit(solution)/shard_map/base_part/pallas_call | solution.py:299
  27.4 0.0 collective-permute-done.5
  27.4 1.8 %collective-permute-start.7 = (bf16[16,64]{1,0:T(8,128)(2,1)S(1)}, bf16[16,64]{1,0:T(8,128)(2,1)S(1)}, u32[]{:S(2)}, u32[]{:S(2)}) collective-permute-start(bf16[16,64]{1,0:T(8,128)(2,1)S(1)} %add.29.refs_1_), channel_id=1, source_target_pairs={{0,4},{4,0},{8,12},{12,8},{16,20},{20,16},{24,28},{28,24},{1,5},{5... | collective-permute-start | bytes 6152 | tf_op jit(solution)/shard_map/ppermute | solution.py:221
  29.2 2.0 %base_part.7.refs_3_ = f32[64,1536]{1,0:T(8,128)S(1)} custom-call(bf16[64,2048]{1,0:T(8,128)(2,1)S(1)} %get-tuple-element.50.rows, bf16[2048,7168]{1,0:T(8,128)(2,1)} %weight.9, bf16[2,2048,512]{2,1,0:T(8,128)(2,1)S(1)} %get-tuple-element.66.refs_0_, bf16[16,64]{1,0:T(8,128)(2,1)S(1)} %add.29.refs_1_, bf16[16,7168]{1,0:T(8,128)(2,1)S(1)} %collective-permute-done.6.refs_2_.refs_6_), custom_call_target="tpu_custom_call" | custom-call | flops 1 | bytes 1 | tf_op jit(solution)/shard_map/base_part/pallas_call | solution.py:299
  31.2 0.0 collective-permute-done.7
  31.2 0.0 collective-permute-done.8.refs_7_
  31.3 0.8 %collective-permute-done.9.refs_8_ = bf16[16,7168]{1,0:T(8,128)(2,1)S(1)} collective-permute-done((bf16[16,7168]{1,0:T(8,128)(2,1)S(1)}, bf16[16,7168]{1,0:T(8,128)(2,1)S(1)}, u32[]{:S(2)}, u32[]{:S(2)}) %collective-permute-start.9) | collective-permute-done | bytes 229408 | tf_op jit(solution)/shard_map/ppermute | solution.py:227
  32.1 0.5 %add_delta.1 = (f32[16,7168]{1,0:T(8,128)S(1)}, f32[16,7168]{1,0:T(8,128)S(1)}, f32[16,2560]{1,0:T(8,128)S(1)}, f32[16,4608]{1,0:T(8,128)S(1)}, f32[16,2560]{1,0:T(8,128)S(1)}, /*index=5*/f32[16,4608]{1,0:T(8,128)S(1)}) custom-call(s32[1,64]{1,0:T(1,128)S(1)} %get-tuple-element.48.slot, f32[64,2048]{1,0:T(8,128)S(1)} %get-tuple-element.53.refs_0_, ...), custom_call_target="tpu_custom_call" | custom-call | flops 1 | bytes 1 | tf_op jit(solution)/shard_map/add_delta/pallas_call | solution.py:337
  32.6 0.1 collective-permute-start.12
  32.6 0.5 %collective-permute-start.10 = (f32[16,4608]{1,0:T(8,128)S(1)}, f32[16,4608]{1,0:T(8,128)S(1)}, u32[]{:S(2)}, u32[]{:S(2)}) collective-permute-start(f32[16,4608]{1,0:T(8,128)S(1)} %get-tuple-element.72), channel_id=1, source_target_pairs={{0,1},{1,0},{2,3},{3,2},{4,5},{5,4},{6,7},{7,6},{8,9},{9,8},{10,11... | collective-permute-start | bytes 884744 | tf_op jit(solution)/shard_map/ppermute | solution.py:224
  33.1 0.9 %collective-permute-done.12 = f32[16,2560]{1,0:T(8,128)S(1)} collective-permute-done((f32[16,2560]{1,0:T(8,128)S(1)}, f32[16,2560]{1,0:T(8,128)S(1)}, u32[]{:S(2)}, u32[]{:S(2)}) %collective-permute-start.12) | collective-permute-done | bytes 163872 | tf_op jit(solution)/shard_map/ppermute | solution.py:224
  34.1 1.5 %collective-permute-start.13 = (bf16[16,2560]{1,0:T(8,128)(2,1)S(1)}, bf16[16,2560]{1,0:T(8,128)(2,1)S(1)}, u32[]{:S(2)}, u32[]{:S(2)}) collective-permute-start(bf16[16,2560]{1,0:T(8,128)(2,1)S(1)} %add_convert_fusion.1), channel_id=1, source_target_pairs={{0,2},{1,3},{2,0},{3,1},{4,6},{5,7},{6,4},{7,5},{8,10},{9,11},{10,... | collective-permute-start | bytes 245768 | tf_op jit(solution)/shard_map/ppermute | solution.py:224
  35.6 0.0 collective-permute-done.10
  35.6 0.0 collective-permute-start.11
  35.6 0.7 %collective-permute-start.14 = (bf16[16,4608]{1,0:T(8,128)(2,1)S(1)}, bf16[16,4608]{1,0:T(8,128)(2,1)S(1)}, u32[]{:S(2)}, u32[]{:S(2)}) collective-permute-start(bf16[16,4608]{1,0:T(8,128)(2,1)S(1)} %add_convert_fusion), channel_id=1, source_target_pairs={{0,2},{1,3},{2,0},{3,1},{4,6},{5,7},{6,4},{7,5},{8,10},{9,11},{10,... | collective-permute-start | bytes 442376 | tf_op jit(solution)/shard_map/ppermute | solution.py:224
  36.3 1.1 %collective-permute-done.11 = f32[16,7168]{1,0:T(8,128)S(1)} collective-permute-done((f32[16,7168]{1,0:T(8,128)S(1)}, f32[16,7168]{1,0:T(8,128)S(1)}, u32[]{:S(2)}, u32[]{:S(2)}) %collective-permute-start.11) | collective-permute-done | bytes 458784 | tf_op jit(solution)/shard_map/ppermute | solution.py:224
  37.5 1.1 %collective-permute-done.13 = bf16[16,2560]{1,0:T(8,128)(2,1)S(1)} collective-permute-done((bf16[16,2560]{1,0:T(8,128)(2,1)S(1)}, bf16[16,2560]{1,0:T(8,128)(2,1)S(1)}, u32[]{:S(2)}, u32[]{:S(2)}) %collective-permute-start.13) | collective-permute-done | bytes 81952 | tf_op jit(solution)/shard_map/ppermute | solution.py:224
  38.6 3.3 %collective-permute-done.14 = bf16[16,4608]{1,0:T(8,128)(2,1)S(1)} collective-permute-done((bf16[16,4608]{1,0:T(8,128)(2,1)S(1)}, bf16[16,4608]{1,0:T(8,128)(2,1)S(1)}, u32[]{:S(2)}, u32[]{:S(2)}) %collective-permute-start.14) | collective-permute-done | bytes 147488 | tf_op jit(solution)/shard_map/ppermute | solution.py:224
  42.0 0.7 %pad_maximum_fusion = bf16[16,7168]{1,0:T(8,128)(2,1)} fusion(bf16[16,4608]{1,0:T(8,128)(2,1)S(1)} %fusion, bf16[16,2560]{1,0:T(8,128)(2,1)S(1)} %fusion.1), kind=kLoop, calls=%fused_computation.3 | loop fusion | flops 458752 | bytes 458752 | tf_op jit(solution)/shard_map/concatenate | solution.py:360
  (10 shorter events, 0.2 us)
Async XLA Ops:
  0.0 9.6 %collective-permute-start = (bf16[16,2048]{1,0:T(8,128)(2,1)}, bf16[16,2048]{1,0:T(8,128)(2,1)S(1)}, u32[]{:S(2)}, u32[]{:S(2)}) collective-permute-start(bf16[16,2048]{1,0:T(8,128)(2,1)} %refs_2_.1), channel_id=1, source_target_pairs={{0,8},{4,12},{8,0},{12,4},{16,24},{20,28},{24,16},{28,20},{1,9},{5... | collective-permute-start | bytes 196616 | tf_op jit(solution)/shard_map/ppermute | solution.py:221
  4.0 6.4 %collective-permute-start.1 = (bf16[16,2048]{1,0:T(8,128)(2,1)}, bf16[16,2048]{1,0:T(8,128)(2,1)S(1)}, u32[]{:S(2)}, u32[]{:S(2)}) collective-permute-start(bf16[16,2048]{1,0:T(8,128)(2,1)} %refs_2_.1), channel_id=1, source_target_pairs={{0,12},{4,8},{8,4},{12,0},{16,28},{20,24},{24,20},{28,16},{1,13},{... | collective-permute-start | bytes 196616 | tf_op jit(solution)/shard_map/ppermute | solution.py:221
  5.4 5.2 %collective-permute-start.2 = (bf16[16,2048]{1,0:T(8,128)(2,1)}, bf16[16,2048]{1,0:T(8,128)(2,1)S(1)}, u32[]{:S(2)}, u32[]{:S(2)}) collective-permute-start(bf16[16,2048]{1,0:T(8,128)(2,1)} %refs_2_.1), channel_id=1, source_target_pairs={{0,4},{4,0},{8,12},{12,8},{16,20},{20,16},{24,28},{28,24},{1,5},{5... | collective-permute-start | bytes 196616 | tf_op jit(solution)/shard_map/ppermute | solution.py:221
  10.8 6.4 %collective-permute-start.3 = (f32[32,64]{1,0:T(8,128)S(1)}, f32[32,64]{1,0:T(8,128)S(1)}, u32[]{:S(2)}, u32[]{:S(2)}) collective-permute-start(f32[32,64]{1,0:T(8,128)S(1)} %get-tuple-element.49.refs_1_), channel_id=1, source_target_pairs={{0,1},{1,0},{2,3},{3,2},{4,5},{5,4},{6,7},{7,6},{8,9},{9,8},{10,11... | collective-permute-start | bytes 24584 | tf_op jit(solution)/shard_map/ppermute | solution.py:224
  10.9 14.0 %collective-permute-start.6 = (bf16[16,7168]{1,0:T(8,128)(2,1)S(1)}, bf16[16,7168]{1,0:T(8,128)(2,1)S(1)}, u32[]{:S(2)}, u32[]{:S(2)}) collective-permute-start(bf16[16,7168]{1,0:T(8,128)(2,1)S(1)} %get-tuple-element.61), channel_id=1, source_target_pairs={{0,8},{4,12},{8,0},{12,4},{16,28},{20,24},{24,20},{28,16},{1,9},{5... | collective-permute-start | bytes 688136 | tf_op jit(solution)/shard_map/ppermute | solution.py:221
  17.3 5.4 %collective-permute-start.4 = (f32[16,64]{1,0:T(8,128)S(1)}, f32[16,64]{1,0:T(8,128)S(1)}, u32[]{:S(2)}, u32[]{:S(2)}) collective-permute-start(f32[16,64]{1,0:T(8,128)S(1)} %slice.16), channel_id=1, source_target_pairs={{0,2},{1,3},{2,0},{3,1},{4,6},{5,7},{6,4},{7,5},{8,10},{9,11},{10,... | collective-permute-start | bytes 12296 | tf_op jit(solution)/shard_map/ppermute | solution.py:224
  18.8 12.4 %collective-permute-start.8 = (bf16[16,7168]{1,0:T(8,128)(2,1)S(1)}, bf16[16,7168]{1,0:T(8,128)(2,1)S(1)}, u32[]{:S(2)}, u32[]{:S(2)}) collective-permute-start(bf16[16,7168]{1,0:T(8,128)(2,1)S(1)} %get-tuple-element.70), channel_id=1, source_target_pairs={{0,4},{4,0},{8,12},{12,8},{16,20},{20,16},{24,28},{28,24},{1,5},{5... | collective-permute-start | bytes 688136 | tf_op jit(solution)/shard_map/ppermute | solution.py:221
  22.7 4.7 %collective-permute-start.5 = (bf16[16,64]{1,0:T(8,128)(2,1)S(1)}, bf16[16,64]{1,0:T(8,128)(2,1)S(1)}, u32[]{:S(2)}, u32[]{:S(2)}) collective-permute-start(bf16[16,64]{1,0:T(8,128)(2,1)S(1)} %fusion.3.refs_1_), channel_id=1, source_target_pairs={{0,8},{4,12},{8,0},{12,4},{16,24},{20,28},{24,16},{28,20},{1,9},{5... | collective-permute-start | bytes 6152 | tf_op jit(solution)/shard_map/ppermute | solution.py:221
  24.9 7.2 %collective-permute-start.9 = (bf16[16,7168]{1,0:T(8,128)(2,1)S(1)}, bf16[16,7168]{1,0:T(8,128)(2,1)S(1)}, u32[]{:S(2)}, u32[]{:S(2)}) collective-permute-start(bf16[16,7168]{1,0:T(8,128)(2,1)S(1)} %collective-permute-done.6.refs_2_.refs_6_), channel_id=1, source_target_pairs={{0,16},{16,0},{1,17},{17,1},{2,18},{18,2},{3,19},{19,3},{4,20},{20... | collective-permute-start | bytes 688136 | tf_op jit(solution)/shard_map/ppermute | solution.py:227
  27.4 3.8 %collective-permute-start.7 = (bf16[16,64]{1,0:T(8,128)(2,1)S(1)}, bf16[16,64]{1,0:T(8,128)(2,1)S(1)}, u32[]{:S(2)}, u32[]{:S(2)}) collective-permute-start(bf16[16,64]{1,0:T(8,128)(2,1)S(1)} %add.29.refs_1_), channel_id=1, source_target_pairs={{0,4},{4,0},{8,12},{12,8},{16,20},{20,16},{24,28},{28,24},{1,5},{5... | collective-permute-start | bytes 6152 | tf_op jit(solution)/shard_map/ppermute | solution.py:221
  32.6 1.5 %collective-permute-start.12 = (f32[16,2560]{1,0:T(8,128)S(1)}, f32[16,2560]{1,0:T(8,128)S(1)}, u32[]{:S(2)}, u32[]{:S(2)}) collective-permute-start(f32[16,2560]{1,0:T(8,128)S(1)} %get-tuple-element.76), channel_id=1, source_target_pairs={{0,1},{1,0},{2,3},{3,2},{4,5},{5,4},{6,7},{7,6},{8,9},{9,8},{10,11... | collective-permute-start | bytes 491528 | tf_op jit(solution)/shard_map/ppermute | solution.py:224
  32.6 3.0 %collective-permute-start.10 = (f32[16,4608]{1,0:T(8,128)S(1)}, f32[16,4608]{1,0:T(8,128)S(1)}, u32[]{:S(2)}, u32[]{:S(2)}) collective-permute-start(f32[16,4608]{1,0:T(8,128)S(1)} %get-tuple-element.72), channel_id=1, source_target_pairs={{0,1},{1,0},{2,3},{3,2},{4,5},{5,4},{6,7},{7,6},{8,9},{9,8},{10,11... | collective-permute-start | bytes 884744 | tf_op jit(solution)/shard_map/ppermute | solution.py:224
  34.1 4.6 %collective-permute-start.13 = (bf16[16,2560]{1,0:T(8,128)(2,1)S(1)}, bf16[16,2560]{1,0:T(8,128)(2,1)S(1)}, u32[]{:S(2)}, u32[]{:S(2)}) collective-permute-start(bf16[16,2560]{1,0:T(8,128)(2,1)S(1)} %add_convert_fusion.1), channel_id=1, source_target_pairs={{0,2},{1,3},{2,0},{3,1},{4,6},{5,7},{6,4},{7,5},{8,10},{9,11},{10,... | collective-permute-start | bytes 245768 | tf_op jit(solution)/shard_map/ppermute | solution.py:224
  35.6 1.8 %collective-permute-start.11 = (f32[16,7168]{1,0:T(8,128)S(1)}, f32[16,7168]{1,0:T(8,128)S(1)}, u32[]{:S(2)}, u32[]{:S(2)}) collective-permute-start(f32[16,7168]{1,0:T(8,128)S(1)} %get-tuple-element.74), channel_id=1, source_target_pairs={{0,1},{1,0},{2,3},{3,2},{4,5},{5,4},{6,7},{7,6},{8,9},{9,8},{10,11... | collective-permute-start | bytes 1376264 | tf_op jit(solution)/shard_map/ppermute | solution.py:224
  35.6 6.3 %collective-permute-start.14 = (bf16[16,4608]{1,0:T(8,128)(2,1)S(1)}, bf16[16,4608]{1,0:T(8,128)(2,1)S(1)}, u32[]{:S(2)}, u32[]{:S(2)}) collective-permute-start(bf16[16,4608]{1,0:T(8,128)(2,1)S(1)} %add_convert_fusion), channel_id=1, source_target_pairs={{0,2},{1,3},{2,0},{3,1},{4,6},{5,7},{6,4},{7,5},{8,10},{9,11},{10,... | collective-permute-start | bytes 442376 | tf_op jit(solution)/shard_map/ppermute | solution.py:224

commit v24 on v19

--- a/solution.py
+++ b/solution.py
@@ -151,11 +151,10 @@
             )
 
 
-def delta_kernel(block, splits, slot, *refs):
-    bases, refs = refs[: -len(splits) * 2 - 9], refs[-len(splits) * 2 - 9 :]
-    own, shrunk, across, beside, swapped, own_keep, own_send = refs[:7]
-    cross_keep, cross_send = refs[7 : 7 + len(splits)], refs[7 + len(splits) : 7 + 2 * len(splits)]
-    flat, ordered = refs[-2:]
+def delta_kernel(block, begin, end, slot, *refs):
+    bases, refs = refs[:-11], refs[-11:]
+    own, shrunk, across, beside, swapped = refs[:5]
+    outs, (flat, ordered) = refs[5:9], refs[9:]
     g, a, t = (lax.axis_index(name) for name in ("groups", "adapter", "tensor"))
     row_count = bases[0].shape[0]
     quarter = row_count // 4
@@ -169,24 +168,21 @@
         start = pl.multiple_of(lax.bitwise_xor(t, turn) * quarter, quarter)
         ordered[i * quarter : (i + 1) * quarter, :] = flat[pl.ds(start, quarter), :].astype(bf16)
     left = ordered[...]
-    at, split = 0, 0
+    at = 0
     for base in bases:
         for column in range(0, base.shape[1], block):
-            span = slice(at, at + block)
+            span, here = slice(at, at + block), slice(at - begin, at - begin + block)
+            at += block
+            if not begin < at <= end:
+                continue
             expand = jnp.concatenate(
                 [own[:, span], across[:, span], beside[:, span], swapped[:, span]], axis=0
             )
             total = base[:, column : column + block] + jnp.dot(
                 left, expand, preferred_element_type=f32
             )
-            if at >= splits[split][1]:
-                split += 1
-            here = slice(at - splits[split][0], at - splits[split][0] + block)
-            own_keep[:, span] = total[:quarter]
-            cross_keep[split][:, here] = total[quarter : 2 * quarter]
-            own_send[:, span] = total[2 * quarter : 3 * quarter]
-            cross_send[split][:, here] = total[3 * quarter :]
-            at += block
+            for n, out in enumerate(outs):
+                out[:, here] = total[n * quarter : (n + 1) * quarter]
 
 
 def column_block(width):
@@ -330,38 +326,35 @@
 
     middle = block_count * 5 // 14 * block
     splits = [(0, middle), (middle, columns)]
-    widths = [last - first for first, last in splits]
     quarter = row_count // 4
-    out = kernel_call(
-        functools.partial(delta_kernel, block, splits),
-        "add_delta",
-        1,
-        1,
-        8,
-        in_specs=[vmem] * (len(bases) + 6),
-        out_specs=[vmem] * (2 + 2 * len(splits)),
-        out_shape=[
-            jax.ShapeDtypeStruct((quarter, w), f32) for w in (columns, columns, *widths, *widths)
-        ],
-        scratch_shapes=[
-            pltpu.VMEM((row_count, rank_block * owner_count), f32),
-            pltpu.VMEM((row_count, rank_block * owner_count), bf16),
-        ],
-    )(slot, *bases, own, shrunk, across, beside, swapped)
-    own_keep, own_send = out[:2]
-    arrived = [from_tensor(x, 1) for x in out[4:6]]
-    arrived[1], own_send = lax.optimization_barrier((arrived[1], own_send))
-    crossed = [
-        from_tensor((keep + other).astype(bf16), 2) for keep, other in zip(out[2:4], arrived)
-    ]
-    kept = own_keep + from_tensor(own_send, 1)
-    return jnp.concatenate(
-        [
-            (kept[:, first:last] + part.astype(f32)).astype(bf16)
-            for (first, last), part in zip(splits, crossed)
-        ],
-        axis=1,
-    )
+
+    def delta_part(begin, end):
+        return kernel_call(
+            functools.partial(delta_kernel, block, begin, end),
+            "add_delta",
+            1,
+            1,
+            8,
+            in_specs=[vmem] * (len(bases) + 6),
+            out_specs=[vmem] * 4,
+            out_shape=[jax.ShapeDtypeStruct((quarter, end - begin), f32)] * 4,
+            scratch_shapes=[
+                pltpu.VMEM((row_count, rank_block * owner_count), f32),
+                pltpu.VMEM((row_count, rank_block * owner_count), bf16),
+            ],
+        )(slot, *bases, own, shrunk, across, beside, swapped)
+
+    first, second = delta_part(*splits[0]), delta_part(*splits[1])
+    arrived = [from_tensor(first[3], 1), from_tensor(second[3], 1)]
+    arrived[0], *rest = lax.optimization_barrier((arrived[0], *second[:3]))
+    second = [*rest, second[3]]
+    arrived[1], sent_a, sent_b = lax.optimization_barrier((arrived[1], first[2], second[2]))
+    halves = []
+    for part, other, sent in ((first, arrived[0], sent_a), (second, arrived[1], sent_b)):
+        crossed = from_tensor((part[1] + other).astype(bf16), 2)
+        kept = part[0] + from_tensor(sent, 1)
+        halves.append((kept + crossed.astype(f32)).astype(bf16))
+    return jnp.concatenate(halves, axis=1)
 
 
 def on_device(tokens, base_up_weight, adapter_shrink_weight, adapter_expand_weight, *index):

time: 41 us -> 40.8 us (level)
  waiting for transfers between devices: 7.09 us -> 6.32 us
    ppermute x7 -> x8, waiting for transfers between devices: 6.33 us -> 5.56 us  [from_tensor(): return lax.ppermute(x, 'tensor', [(s, s ^ m) for s in range(4)])]
    ppermute x7 -> x8, starting transfers between devices: 4.36 us -> 4.78 us  [from_tensor(): return lax.ppermute(x, 'tensor', [(s, s ^ m) for s in range(4)])]
  transfers between devices with their start and end apart: 15 -> 16, of which waited for: 6 -> 6; matrix products, arithmetic and copies ran while one was open for 0% -> 0% of each run, Pallas kernels for 37% -> 38%
where the time goes in v24:
time: 40.8 us; the launch traced here: 40.7 us
  starting transfers between devices  17.6 us (43%)
  Pallas kernels  15.7 us (38%)
  waiting for transfers between devices  6.32 us (15%)
  other arithmetic  0.84 us (2%)
    ppermute x7, starting transfers between devices, from_owner(): return lax.ppermute(x, ('groups', 'adapter'), pairs)  11.7 us
    pallas_call x4, Pallas kernels, base_part(): kernel_call(functools.partial(base_kernel, block, places, numbers, stream...  10.8 us
    ppermute x8, waiting for transfers between devices, from_tensor(): return lax.ppermute(x, 'tensor', [(s, s ^ m) for s in range(4)])  5.56 us
    ppermute x8, starting transfers between devices, from_tensor(): return lax.ppermute(x, 'tensor', [(s, s ^ m) for s in range(4)])  4.78 us
    pallas_call x1, Pallas kernels, paired(): kernel_call(functools.partial(cut_kernel, block, range(loads[1]), len(sma...  3.94 us
    ppermute x1, starting transfers between devices, from_group(): return lax.ppermute(x, 'groups', [(0, 1), (1, 0)])  1.19 us
  transfers between devices with their start and end apart: 16, of which 6 were waited for; matrix products, arithmetic and copies ran while one was open for 0% of the time, Pallas kernels for 38%

profile of v24, /device:TPU:0, one launch (start us, length us, event | category | flops | bytes accessed | tf_op | source)
XLA Modules:
  0.0 40.7 jit_solution(14972178056053293004)
XLA Ops:
  0.0 4.0 %collective-permute-start = (bf16[16,2048]{1,0:T(8,128)(2,1)}, bf16[16,2048]{1,0:T(8,128)(2,1)S(1)}, u32[]{:S(2)}, u32[]{:S(2)}) collective-permute-start(bf16[16,2048]{1,0:T(8,128)(2,1)} %refs_2_.1), channel_id=1, source_target_pairs={{0,8},{4,12},{8,0},{12,4},{16,24},{20,28},{24,16},{28,20},{1,9},{5... | collective-permute-start | bytes 196616 | tf_op jit(solution)/shard_map/ppermute | solution.py:217
  4.0 1.3 %collective-permute-start.1 = (bf16[16,2048]{1,0:T(8,128)(2,1)}, bf16[16,2048]{1,0:T(8,128)(2,1)S(1)}, u32[]{:S(2)}, u32[]{:S(2)}) collective-permute-start(bf16[16,2048]{1,0:T(8,128)(2,1)} %refs_2_.1), channel_id=1, source_target_pairs={{0,12},{4,8},{8,4},{12,0},{16,28},{20,24},{24,20},{28,16},{1,13},{... | collective-permute-start | bytes 196616 | tf_op jit(solution)/shard_map/ppermute | solution.py:217
  5.4 0.2 collective-permute-start.2
  5.6 3.9 %cut_expand.1 = (bf16[16,7168]{1,0:T(8,128)(2,1)S(1)}, bf16[16,7168]{1,0:T(8,128)(2,1)S(1)}, bf16[16,7168]{1,0:T(8,128)(2,1)S(1)}, s32[1,4]{1,0:T(1,128)S(1)}, s...) custom-call(bf16[1,16,28672]{2,1,0:T(8,128)(2,1)} %expand.1, ...), custom_call_target="tpu_custom_call" | custom-call | flops 1 | bytes 1 | tf_op jit(solution)/shard_map/cut_expand/pallas_call | solution.py:243
  9.6 2.9 %collective-permute-start.6 = (bf16[16,7168]{1,0:T(8,128)(2,1)S(1)}, bf16[16,7168]{1,0:T(8,128)(2,1)S(1)}, u32[]{:S(2)}, u32[]{:S(2)}) collective-permute-start(bf16[16,7168]{1,0:T(8,128)(2,1)S(1)} %get-tuple-element.64), channel_id=1, source_target_pairs={{0,8},{4,12},{8,0},{12,4},{16,28},{20,24},{24,20},{28,16},{1,9},{5... | collective-permute-start | bytes 688136 | tf_op jit(solution)/shard_map/ppermute | solution.py:217
  12.5 0.6 %collective-permute-start.8 = (bf16[16,7168]{1,0:T(8,128)(2,1)S(1)}, bf16[16,7168]{1,0:T(8,128)(2,1)S(1)}, u32[]{:S(2)}, u32[]{:S(2)}) collective-permute-start(bf16[16,7168]{1,0:T(8,128)(2,1)S(1)} %get-tuple-element.73), channel_id=1, source_target_pairs={{0,4},{4,0},{8,12},{12,8},{16,20},{20,16},{24,28},{28,24},{1,5},{5... | collective-permute-start | bytes 688136 | tf_op jit(solution)/shard_map/ppermute | solution.py:217
  13.1 0.0 collective-permute-done.refs_1_
  13.1 0.0 collective-permute-done.1.refs_2_
  13.1 0.0 collective-permute-done.2.refs_3_
  13.1 0.3 gather_rows.1
  13.4 0.1 collective-permute-start.3
  13.5 3.6 %base_part.4 = (f32[64,2048]{1,0:T(8,128)S(1)}, bf16[4,2048,512]{2,1,0:T(8,128)(2,1)S(1)}) custom-call(bf16[64,2048]{1,0:T(8,128)(2,1)S(1)} %get-tuple-element.53.rows, bf16[2048,7168]{1,0:T(8,128)(2,1)} %weight.9, bf16[4,2048,512]{2,1,0:T(8,128)(2,1)S(1)} %get-tuple-element.54.refs_0_, f32[32,64]{1,0:T(8,128)S(1)} %get-tuple-element.52.refs_1_), custom_call_target="tpu_custom_call" | custom-call | flops 1500000000 | bytes 1 | tf_op jit(solution)/shard_map/base_part/pallas_call | solution.py:293
  17.1 0.0 collective-permute-done.3
  17.1 1.6 %collective-permute-start.4 = (f32[16,64]{1,0:T(8,128)S(1)}, f32[16,64]{1,0:T(8,128)S(1)}, u32[]{:S(2)}, u32[]{:S(2)}) collective-permute-start(f32[16,64]{1,0:T(8,128)S(1)} %slice.8), channel_id=1, source_target_pairs={{0,2},{1,3},{2,0},{3,1},{4,6},{5,7},{6,4},{7,5},{8,10},{9,11},{10,... | collective-permute-start | bytes 12296 | tf_op jit(solution)/shard_map/ppermute | solution.py:220
  18.7 3.0 %base_part.5 = (f32[64,2048]{1,0:T(8,128)S(1)}, bf16[3,2048,512]{2,1,0:T(8,128)(2,1)S(1)}) custom-call(bf16[64,2048]{1,0:T(8,128)(2,1)S(1)} %get-tuple-element.53.rows, bf16[2048,7168]{1,0:T(8,128)(2,1)} %weight.9, bf16[4,2048,512]{2,1,0:T(8,128)(2,1)S(1)} %get-tuple-element.59.refs_0_, f32[32,64]{1,0:T(8,128)S(1)} %add.30.refs_1_), custom_call_target="tpu_custom_call" | custom-call | flops 1500000000 | bytes 1 | tf_op jit(solution)/shard_map/base_part/pallas_call | solution.py:293
  21.6 0.0 collective-permute-done.4
  21.7 1.3 %collective-permute-start.5 = (bf16[16,64]{1,0:T(8,128)(2,1)S(1)}, bf16[16,64]{1,0:T(8,128)(2,1)S(1)}, u32[]{:S(2)}, u32[]{:S(2)}) collective-permute-start(bf16[16,64]{1,0:T(8,128)(2,1)S(1)} %fusion.1.refs_1_), channel_id=1, source_target_pairs={{0,8},{4,12},{8,0},{12,4},{16,24},{20,28},{24,16},{28,20},{1,9},{5... | collective-permute-start | bytes 6152 | tf_op jit(solution)/shard_map/ppermute | solution.py:217
  23.0 0.0 collective-permute-done.6.refs_2_.refs_6_
  23.0 1.2 %collective-permute-start.9 = (bf16[16,7168]{1,0:T(8,128)(2,1)S(1)}, bf16[16,7168]{1,0:T(8,128)(2,1)S(1)}, u32[]{:S(2)}, u32[]{:S(2)}) collective-permute-start(bf16[16,7168]{1,0:T(8,128)(2,1)S(1)} %collective-permute-done.6.refs_2_.refs_6_), channel_id=1, source_target_pairs={{0,16},{16,0},{1,17},{17,1},{2,18},{18,2},{3,19},{19,3},{4,20},{20... | collective-permute-start | bytes 688136 | tf_op jit(solution)/shard_map/ppermute | solution.py:223
  24.2 2.2 %base_part.6 = (f32[64,1536]{1,0:T(8,128)S(1)}, bf16[2,2048,512]{2,1,0:T(8,128)(2,1)S(1)}) custom-call(bf16[64,2048]{1,0:T(8,128)(2,1)S(1)} %get-tuple-element.53.rows, bf16[2048,7168]{1,0:T(8,128)(2,1)} %weight.9, bf16[3,2048,512]{2,1,0:T(8,128)(2,1)S(1)} %get-tuple-element.63.refs_0_, bf16[16,64]{1,0:T(8,128)(2,1)S(1)} %fusion.1.refs_1_, ...), custom_call_target="tpu_custom_call" | custom-call | flops 10000000000 | bytes 1 | tf_op jit(solution)/shard_map/base_part/pallas_call | solution.py:293
  26.4 0.0 collective-permute-done.5
  26.4 1.2 %collective-permute-start.7 = (bf16[16,64]{1,0:T(8,128)(2,1)S(1)}, bf16[16,64]{1,0:T(8,128)(2,1)S(1)}, u32[]{:S(2)}, u32[]{:S(2)}) collective-permute-start(bf16[16,64]{1,0:T(8,128)(2,1)S(1)} %add.32.refs_1_), channel_id=1, source_target_pairs={{0,4},{4,0},{8,12},{12,8},{16,20},{20,16},{24,28},{28,24},{1,5},{5... | collective-permute-start | bytes 6152 | tf_op jit(solution)/shard_map/ppermute | solution.py:217
  27.6 2.0 %base_part.7.refs_3_ = f32[64,1536]{1,0:T(8,128)S(1)} custom-call(bf16[64,2048]{1,0:T(8,128)(2,1)S(1)} %get-tuple-element.53.rows, bf16[2048,7168]{1,0:T(8,128)(2,1)} %weight.9, bf16[2,2048,512]{2,1,0:T(8,128)(2,1)S(1)} %get-tuple-element.69.refs_0_, bf16[16,64]{1,0:T(8,128)(2,1)S(1)} %add.32.refs_1_, bf16[16,7168]{1,0:T(8,128)(2,1)S(1)} %collective-permute-done.6.refs_2_.refs_6_), custom_call_target="tpu_custom_call" | custom-call | flops 1 | bytes 1 | tf_op jit(solution)/shard_map/base_part/pallas_call | solution.py:293
  29.7 0.5 %collective-permute-done.7 = bf16[16,64]{1,0:T(8,128)(2,1)S(1)} collective-permute-done((bf16[16,64]{1,0:T(8,128)(2,1)S(1)}, bf16[16,64]{1,0:T(8,128)(2,1)S(1)}, u32[]{:S(2)}, u32[]{:S(2)}) %collective-permute-start.7) | collective-permute-done | bytes 2080 | tf_op jit(solution)/shard_map/ppermute | solution.py:217
  30.1 0.0 collective-permute-done.8.refs_7_
  30.1 0.3 collective-permute-done.9.refs_8_
  30.4 0.3 add_delta.2
  30.7 0.1 collective-permute-start.11
  30.8 0.4 add_delta.3
  31.2 0.6 %collective-permute-start.10 = (f32[16,4608]{1,0:T(8,128)S(1)}, f32[16,4608]{1,0:T(8,128)S(1)}, u32[]{:S(2)}, u32[]{:S(2)}) collective-permute-start(f32[16,4608]{1,0:T(8,128)S(1)} %get-tuple-element.75), channel_id=1, source_target_pairs={{0,1},{1,0},{2,3},{3,2},{4,5},{5,4},{6,7},{7,6},{8,9},{9,8},{10,11... | collective-permute-start | bytes 884744 | tf_op jit(solution)/shard_map/ppermute | solution.py:220
  31.8 0.4 %collective-permute-done.11 = f32[16,2560]{1,0:T(8,128)S(1)} collective-permute-done((f32[16,2560]{1,0:T(8,128)S(1)}, f32[16,2560]{1,0:T(8,128)S(1)}, u32[]{:S(2)}, u32[]{:S(2)}) %collective-permute-start.11) | collective-permute-done | bytes 163872 | tf_op jit(solution)/shard_map/ppermute | solution.py:220
  32.2 0.6 %collective-permute-start.13 = (bf16[16,2560]{1,0:T(8,128)(2,1)S(1)}, bf16[16,2560]{1,0:T(8,128)(2,1)S(1)}, u32[]{:S(2)}, u32[]{:S(2)}) collective-permute-start(bf16[16,2560]{1,0:T(8,128)(2,1)S(1)} %add_convert_fusion.3), channel_id=1, source_target_pairs={{0,2},{1,3},{2,0},{3,1},{4,6},{5,7},{6,4},{7,5},{8,10},{9,11},{10,... | collective-permute-start | bytes 245768 | tf_op jit(solution)/shard_map/ppermute | solution.py:220
  32.8 0.2 collective-permute-done.10
  33.0 0.4 collective-permute-start.12
  33.4 0.1 collective-permute-start.14
  33.5 1.4 %collective-permute-start.15 = (bf16[16,4608]{1,0:T(8,128)(2,1)S(1)}, bf16[16,4608]{1,0:T(8,128)(2,1)S(1)}, u32[]{:S(2)}, u32[]{:S(2)}) collective-permute-start(bf16[16,4608]{1,0:T(8,128)(2,1)S(1)} %add_convert_fusion.1), channel_id=1, source_target_pairs={{0,2},{1,3},{2,0},{3,1},{4,6},{5,7},{6,4},{7,5},{8,10},{9,11},{10,... | collective-permute-start | bytes 442376 | tf_op jit(solution)/shard_map/ppermute | solution.py:220
  34.9 2.1 %collective-permute-done.13 = bf16[16,2560]{1,0:T(8,128)(2,1)S(1)} collective-permute-done((bf16[16,2560]{1,0:T(8,128)(2,1)S(1)}, bf16[16,2560]{1,0:T(8,128)(2,1)S(1)}, u32[]{:S(2)}, u32[]{:S(2)}) %collective-permute-start.13) | collective-permute-done | bytes 81952 | tf_op jit(solution)/shard_map/ppermute | solution.py:220
  37.0 0.0 collective-permute-done.12
  37.1 2.9 %collective-permute-done.15 = bf16[16,4608]{1,0:T(8,128)(2,1)S(1)} collective-permute-done((bf16[16,4608]{1,0:T(8,128)(2,1)S(1)}, bf16[16,4608]{1,0:T(8,128)(2,1)S(1)}, u32[]{:S(2)}, u32[]{:S(2)}) %collective-permute-start.15) | collective-permute-done | bytes 147488 | tf_op jit(solution)/shard_map/ppermute | solution.py:220
  39.9 0.0 collective-permute-done.14
  40.0 0.7 %pad_maximum_fusion = bf16[16,7168]{1,0:T(8,128)(2,1)} fusion(bf16[16,4608]{1,0:T(8,128)(2,1)S(1)} %add_convert_fusion, bf16[16,2560]{1,0:T(8,128)(2,1)S(1)} %add_convert_fusion.2), kind=kLoop, calls=%fused_computation.2 | loop fusion | flops 458752 | bytes 458752 | tf_op jit(solution)/shard_map/concatenate | solution.py:357
  (9 shorter events, 0.1 us)
Async XLA Ops:
  0.0 13.1 %collective-permute-start = (bf16[16,2048]{1,0:T(8,128)(2,1)}, bf16[16,2048]{1,0:T(8,128)(2,1)S(1)}, u32[]{:S(2)}, u32[]{:S(2)}) collective-permute-start(bf16[16,2048]{1,0:T(8,128)(2,1)} %refs_2_.1), channel_id=1, source_target_pairs={{0,8},{4,12},{8,0},{12,4},{16,24},{20,28},{24,16},{28,20},{1,9},{5... | collective-permute-start | bytes 196616 | tf_op jit(solution)/shard_map/ppermute | solution.py:217
  4.0 9.1 %collective-permute-start.1 = (bf16[16,2048]{1,0:T(8,128)(2,1)}, bf16[16,2048]{1,0:T(8,128)(2,1)S(1)}, u32[]{:S(2)}, u32[]{:S(2)}) collective-permute-start(bf16[16,2048]{1,0:T(8,128)(2,1)} %refs_2_.1), channel_id=1, source_target_pairs={{0,12},{4,8},{8,4},{12,0},{16,28},{20,24},{24,20},{28,16},{1,13},{... | collective-permute-start | bytes 196616 | tf_op jit(solution)/shard_map/ppermute | solution.py:217
  5.4 7.7 %collective-permute-start.2 = (bf16[16,2048]{1,0:T(8,128)(2,1)}, bf16[16,2048]{1,0:T(8,128)(2,1)S(1)}, u32[]{:S(2)}, u32[]{:S(2)}) collective-permute-start(bf16[16,2048]{1,0:T(8,128)(2,1)} %refs_2_.1), channel_id=1, source_target_pairs={{0,4},{4,0},{8,12},{12,8},{16,20},{20,16},{24,28},{28,24},{1,5},{5... | collective-permute-start | bytes 196616 | tf_op jit(solution)/shard_map/ppermute | solution.py:217
  9.6 13.4 %collective-permute-start.6 = (bf16[16,7168]{1,0:T(8,128)(2,1)S(1)}, bf16[16,7168]{1,0:T(8,128)(2,1)S(1)}, u32[]{:S(2)}, u32[]{:S(2)}) collective-permute-start(bf16[16,7168]{1,0:T(8,128)(2,1)S(1)} %get-tuple-element.64), channel_id=1, source_target_pairs={{0,8},{4,12},{8,0},{12,4},{16,28},{20,24},{24,20},{28,16},{1,9},{5... | collective-permute-start | bytes 688136 | tf_op jit(solution)/shard_map/ppermute | solution.py:217
  12.5 17.6 %collective-permute-start.8 = (bf16[16,7168]{1,0:T(8,128)(2,1)S(1)}, bf16[16,7168]{1,0:T(8,128)(2,1)S(1)}, u32[]{:S(2)}, u32[]{:S(2)}) collective-permute-start(bf16[16,7168]{1,0:T(8,128)(2,1)S(1)} %get-tuple-element.73), channel_id=1, source_target_pairs={{0,4},{4,0},{8,12},{12,8},{16,20},{20,16},{24,28},{28,24},{1,5},{5... | collective-permute-start | bytes 688136 | tf_op jit(solution)/shard_map/ppermute | solution.py:217
  13.4 3.7 %collective-permute-start.3 = (f32[32,64]{1,0:T(8,128)S(1)}, f32[32,64]{1,0:T(8,128)S(1)}, u32[]{:S(2)}, u32[]{:S(2)}) collective-permute-start(f32[32,64]{1,0:T(8,128)S(1)} %get-tuple-element.52.refs_1_), channel_id=1, source_target_pairs={{0,1},{1,0},{2,3},{3,2},{4,5},{5,4},{6,7},{7,6},{8,9},{9,8},{10,11... | collective-permute-start | bytes 24584 | tf_op jit(solution)/shard_map/ppermute | solution.py:220
  17.1 4.5 %collective-permute-start.4 = (f32[16,64]{1,0:T(8,128)S(1)}, f32[16,64]{1,0:T(8,128)S(1)}, u32[]{:S(2)}, u32[]{:S(2)}) collective-permute-start(f32[16,64]{1,0:T(8,128)S(1)} %slice.8), channel_id=1, source_target_pairs={{0,2},{1,3},{2,0},{3,1},{4,6},{5,7},{6,4},{7,5},{8,10},{9,11},{10,... | collective-permute-start | bytes 12296 | tf_op jit(solution)/shard_map/ppermute | solution.py:220
  21.7 4.8 %collective-permute-start.5 = (bf16[16,64]{1,0:T(8,128)(2,1)S(1)}, bf16[16,64]{1,0:T(8,128)(2,1)S(1)}, u32[]{:S(2)}, u32[]{:S(2)}) collective-permute-start(bf16[16,64]{1,0:T(8,128)(2,1)S(1)} %fusion.1.refs_1_), channel_id=1, source_target_pairs={{0,8},{4,12},{8,0},{12,4},{16,24},{20,28},{24,16},{28,20},{1,9},{5... | collective-permute-start | bytes 6152 | tf_op jit(solution)/shard_map/ppermute | solution.py:217
  23.0 7.4 %collective-permute-start.9 = (bf16[16,7168]{1,0:T(8,128)(2,1)S(1)}, bf16[16,7168]{1,0:T(8,128)(2,1)S(1)}, u32[]{:S(2)}, u32[]{:S(2)}) collective-permute-start(bf16[16,7168]{1,0:T(8,128)(2,1)S(1)} %collective-permute-done.6.refs_2_.refs_6_), channel_id=1, source_target_pairs={{0,16},{16,0},{1,17},{17,1},{2,18},{18,2},{3,19},{19,3},{4,20},{20... | collective-permute-start | bytes 688136 | tf_op jit(solution)/shard_map/ppermute | solution.py:223
  26.4 3.7 %collective-permute-start.7 = (bf16[16,64]{1,0:T(8,128)(2,1)S(1)}, bf16[16,64]{1,0:T(8,128)(2,1)S(1)}, u32[]{:S(2)}, u32[]{:S(2)}) collective-permute-start(bf16[16,64]{1,0:T(8,128)(2,1)S(1)} %add.32.refs_1_), channel_id=1, source_target_pairs={{0,4},{4,0},{8,12},{12,8},{16,20},{20,16},{24,28},{28,24},{1,5},{5... | collective-permute-start | bytes 6152 | tf_op jit(solution)/shard_map/ppermute | solution.py:217
  30.7 1.5 %collective-permute-start.11 = (f32[16,2560]{1,0:T(8,128)S(1)}, f32[16,2560]{1,0:T(8,128)S(1)}, u32[]{:S(2)}, u32[]{:S(2)}) collective-permute-start(f32[16,2560]{1,0:T(8,128)S(1)} %get-tuple-element.77), channel_id=1, source_target_pairs={{0,1},{1,0},{2,3},{3,2},{4,5},{5,4},{6,7},{7,6},{8,9},{9,8},{10,11... | collective-permute-start | bytes 491528 | tf_op jit(solution)/shard_map/ppermute | solution.py:220
  31.2 1.8 %collective-permute-start.10 = (f32[16,4608]{1,0:T(8,128)S(1)}, f32[16,4608]{1,0:T(8,128)S(1)}, u32[]{:S(2)}, u32[]{:S(2)}) collective-permute-start(f32[16,4608]{1,0:T(8,128)S(1)} %get-tuple-element.75), channel_id=1, source_target_pairs={{0,1},{1,0},{2,3},{3,2},{4,5},{5,4},{6,7},{7,6},{8,9},{9,8},{10,11... | collective-permute-start | bytes 884744 | tf_op jit(solution)/shard_map/ppermute | solution.py:220
  32.2 4.8 %collective-permute-start.13 = (bf16[16,2560]{1,0:T(8,128)(2,1)S(1)}, bf16[16,2560]{1,0:T(8,128)(2,1)S(1)}, u32[]{:S(2)}, u32[]{:S(2)}) collective-permute-start(bf16[16,2560]{1,0:T(8,128)(2,1)S(1)} %add_convert_fusion.3), channel_id=1, source_target_pairs={{0,2},{1,3},{2,0},{3,1},{4,6},{5,7},{6,4},{7,5},{8,10},{9,11},{10,... | collective-permute-start | bytes 245768 | tf_op jit(solution)/shard_map/ppermute | solution.py:220
  33.0 4.0 %collective-permute-start.12 = (f32[16,2560]{1,0:T(8,128)S(1)}, f32[16,2560]{1,0:T(8,128)S(1)}, u32[]{:S(2)}, u32[]{:S(2)}) collective-permute-start(f32[16,2560]{1,0:T(8,128)S(1)} %get-tuple-element.82), channel_id=1, source_target_pairs={{0,1},{1,0},{2,3},{3,2},{4,5},{5,4},{6,7},{7,6},{8,9},{9,8},{10,11... | collective-permute-start | bytes 491528 | tf_op jit(solution)/shard_map/ppermute | solution.py:220
  33.4 6.6 %collective-permute-start.14 = (f32[16,4608]{1,0:T(8,128)S(1)}, f32[16,4608]{1,0:T(8,128)S(1)}, u32[]{:S(2)}, u32[]{:S(2)}) collective-permute-start(f32[16,4608]{1,0:T(8,128)S(1)} %get-tuple-element.86), channel_id=1, source_target_pairs={{0,1},{1,0},{2,3},{3,2},{4,5},{5,4},{6,7},{7,6},{8,9},{9,8},{10,11... | collective-permute-start | bytes 884744 | tf_op jit(solution)/shard_map/ppermute | solution.py:220
  33.5 6.4 %collective-permute-start.15 = (bf16[16,4608]{1,0:T(8,128)(2,1)S(1)}, bf16[16,4608]{1,0:T(8,128)(2,1)S(1)}, u32[]{:S(2)}, u32[]{:S(2)}) collective-permute-start(bf16[16,4608]{1,0:T(8,128)(2,1)S(1)} %add_convert_fusion.1), channel_id=1, source_target_pairs={{0,2},{1,3},{2,0},{3,1},{4,6},{5,7},{6,4},{7,5},{8,10},{9,11},{10,... | collective-permute-start | bytes 442376 | tf_op jit(solution)/shard_map/ppermute | solution.py:220

commit v25 on v24

--- a/solution.py
+++ b/solution.py
@@ -348,12 +348,13 @@
     arrived = [from_tensor(first[3], 1), from_tensor(second[3], 1)]
     arrived[0], *rest = lax.optimization_barrier((arrived[0], *second[:3]))
     second = [*rest, second[3]]
-    arrived[1], sent_a, sent_b = lax.optimization_barrier((arrived[1], first[2], second[2]))
+    summed = [(part[1] + other).astype(bf16) for part, other in zip((first, second), arrived)]
+    crossed = [from_tensor(x, 2) for x in summed]
+    _, *sent = lax.optimization_barrier((summed[1], first[2], second[2]))
     halves = []
-    for part, other, sent in ((first, arrived[0], sent_a), (second, arrived[1], sent_b)):
-        crossed = from_tensor((part[1] + other).astype(bf16), 2)
-        kept = part[0] + from_tensor(sent, 1)
-        halves.append((kept + crossed.astype(f32)).astype(bf16))
+    for part, across_x, own_rows in zip((first, second), crossed, sent):
+        kept = part[0] + from_tensor(own_rows, 1)
+        halves.append((kept + across_x.astype(f32)).astype(bf16))
     return jnp.concatenate(halves, axis=1)
 
 

time: 40.8 us -> 41.9 us (1.027)
  waiting for transfers between devices: 6.32 us -> 7.39 us
    ppermute x8, waiting for transfers between devices: 5.56 us -> 6.63 us  [from_tensor(): return lax.ppermute(x, 'tensor', [(s, s ^ m) for s in range(4)])]
  transfers between devices with their start and end apart: 16 -> 16, of which waited for: 6 -> 5; matrix products, arithmetic and copies ran while one was open for 0% -> 0% of each run, Pallas kernels for 38% -> 37%
where the time goes in v25:
time: 41.9 us; the launch traced here: 41.8 us
  starting transfers between devices  17.6 us (42%)
  Pallas kernels  15.7 us (37%)
  waiting for transfers between devices  7.39 us (18%)
  other arithmetic  0.84 us (2%)
    ppermute x7, starting transfers between devices, from_owner(): return lax.ppermute(x, ('groups', 'adapter'), pairs)  11.7 us
    pallas_call x4, Pallas kernels, base_part(): kernel_call(functools.partial(base_kernel, block, places, numbers, stream...  10.8 us
    ppermute x8, waiting for transfers between devices, from_tensor(): return lax.ppermute(x, 'tensor', [(s, s ^ m) for s in range(4)])  6.63 us
    ppermute x8, starting transfers between devices, from_tensor(): return lax.ppermute(x, 'tensor', [(s, s ^ m) for s in range(4)])  4.79 us
    pallas_call x1, Pallas kernels, paired(): kernel_call(functools.partial(cut_kernel, block, range(loads[1]), len(sma...  3.94 us
    ppermute x1, starting transfers between devices, from_group(): return lax.ppermute(x, 'groups', [(0, 1), (1, 0)])  1.19 us
  transfers between devices with their start and end apart: 16, of which 5 were waited for; matrix products, arithmetic and copies ran while one was open for 0% of the time, Pallas kernels for 37%

profile of v25, /device:TPU:0, one launch (start us, length us, event | category | flops | bytes accessed | tf_op | source)
XLA Modules:
  0.0 41.8 jit_solution(5271608238874944988)
XLA Ops:
  0.0 4.0 %collective-permute-start = (bf16[16,2048]{1,0:T(8,128)(2,1)}, bf16[16,2048]{1,0:T(8,128)(2,1)S(1)}, u32[]{:S(2)}, u32[]{:S(2)}) collective-permute-start(bf16[16,2048]{1,0:T(8,128)(2,1)} %refs_2_.1), channel_id=1, source_target_pairs={{0,8},{4,12},{8,0},{12,4},{16,24},{20,28},{24,16},{28,20},{1,9},{5... | collective-permute-start | bytes 196616 | tf_op jit(solution)/shard_map/ppermute | solution.py:217
  4.0 1.3 %collective-permute-start.1 = (bf16[16,2048]{1,0:T(8,128)(2,1)}, bf16[16,2048]{1,0:T(8,128)(2,1)S(1)}, u32[]{:S(2)}, u32[]{:S(2)}) collective-permute-start(bf16[16,2048]{1,0:T(8,128)(2,1)} %refs_2_.1), channel_id=1, source_target_pairs={{0,12},{4,8},{8,4},{12,0},{16,28},{20,24},{24,20},{28,16},{1,13},{... | collective-permute-start | bytes 196616 | tf_op jit(solution)/shard_map/ppermute | solution.py:217
  5.4 0.2 collective-permute-start.2
  5.6 3.9 %cut_expand.1 = (bf16[16,7168]{1,0:T(8,128)(2,1)S(1)}, bf16[16,7168]{1,0:T(8,128)(2,1)S(1)}, bf16[16,7168]{1,0:T(8,128)(2,1)S(1)}, s32[1,4]{1,0:T(1,128)S(1)}, s...) custom-call(bf16[1,16,28672]{2,1,0:T(8,128)(2,1)} %expand.1, ...), custom_call_target="tpu_custom_call" | custom-call | flops 1 | bytes 1 | tf_op jit(solution)/shard_map/cut_expand/pallas_call | solution.py:243
  9.6 2.9 %collective-permute-start.6 = (bf16[16,7168]{1,0:T(8,128)(2,1)S(1)}, bf16[16,7168]{1,0:T(8,128)(2,1)S(1)}, u32[]{:S(2)}, u32[]{:S(2)}) collective-permute-start(bf16[16,7168]{1,0:T(8,128)(2,1)S(1)} %get-tuple-element.63), channel_id=1, source_target_pairs={{0,8},{4,12},{8,0},{12,4},{16,28},{20,24},{24,20},{28,16},{1,9},{5... | collective-permute-start | bytes 688136 | tf_op jit(solution)/shard_map/ppermute | solution.py:217
  12.5 0.6 %collective-permute-start.8 = (bf16[16,7168]{1,0:T(8,128)(2,1)S(1)}, bf16[16,7168]{1,0:T(8,128)(2,1)S(1)}, u32[]{:S(2)}, u32[]{:S(2)}) collective-permute-start(bf16[16,7168]{1,0:T(8,128)(2,1)S(1)} %get-tuple-element.72), channel_id=1, source_target_pairs={{0,4},{4,0},{8,12},{12,8},{16,20},{20,16},{24,28},{28,24},{1,5},{5... | collective-permute-start | bytes 688136 | tf_op jit(solution)/shard_map/ppermute | solution.py:217
  13.1 0.0 collective-permute-done.refs_1_
  13.1 0.0 collective-permute-done.1.refs_2_
  13.1 0.0 collective-permute-done.2.refs_3_
  13.1 0.3 gather_rows.1
  13.4 0.1 collective-permute-start.3
  13.5 3.6 %base_part.4 = (f32[64,2048]{1,0:T(8,128)S(1)}, bf16[4,2048,512]{2,1,0:T(8,128)(2,1)S(1)}) custom-call(bf16[64,2048]{1,0:T(8,128)(2,1)S(1)} %get-tuple-element.52.rows, bf16[2048,7168]{1,0:T(8,128)(2,1)} %weight.9, bf16[4,2048,512]{2,1,0:T(8,128)(2,1)S(1)} %get-tuple-element.53.refs_0_, f32[32,64]{1,0:T(8,128)S(1)} %get-tuple-element.51.refs_1_), custom_call_target="tpu_custom_call" | custom-call | flops 1500000000 | bytes 1 | tf_op jit(solution)/shard_map/base_part/pallas_call | solution.py:293
  17.1 0.0 collective-permute-done.3
  17.1 1.6 %collective-permute-start.4 = (f32[16,64]{1,0:T(8,128)S(1)}, f32[16,64]{1,0:T(8,128)S(1)}, u32[]{:S(2)}, u32[]{:S(2)}) collective-permute-start(f32[16,64]{1,0:T(8,128)S(1)} %slice.8), channel_id=1, source_target_pairs={{0,2},{1,3},{2,0},{3,1},{4,6},{5,7},{6,4},{7,5},{8,10},{9,11},{10,... | collective-permute-start | bytes 12296 | tf_op jit(solution)/shard_map/ppermute | solution.py:220
  18.7 3.0 %base_part.5 = (f32[64,2048]{1,0:T(8,128)S(1)}, bf16[3,2048,512]{2,1,0:T(8,128)(2,1)S(1)}) custom-call(bf16[64,2048]{1,0:T(8,128)(2,1)S(1)} %get-tuple-element.52.rows, bf16[2048,7168]{1,0:T(8,128)(2,1)} %weight.9, bf16[4,2048,512]{2,1,0:T(8,128)(2,1)S(1)} %get-tuple-element.58.refs_0_, f32[32,64]{1,0:T(8,128)S(1)} %add.30.refs_1_), custom_call_target="tpu_custom_call" | custom-call | flops 1500000000 | bytes 1 | tf_op jit(solution)/shard_map/base_part/pallas_call | solution.py:293
  21.6 0.0 collective-permute-done.4
  21.7 1.3 %collective-permute-start.5 = (bf16[16,64]{1,0:T(8,128)(2,1)S(1)}, bf16[16,64]{1,0:T(8,128)(2,1)S(1)}, u32[]{:S(2)}, u32[]{:S(2)}) collective-permute-start(bf16[16,64]{1,0:T(8,128)(2,1)S(1)} %fusion.1.refs_1_), channel_id=1, source_target_pairs={{0,8},{4,12},{8,0},{12,4},{16,24},{20,28},{24,16},{28,20},{1,9},{5... | collective-permute-start | bytes 6152 | tf_op jit(solution)/shard_map/ppermute | solution.py:217
  23.0 0.0 collective-permute-done.6.refs_2_.refs_6_
  23.0 1.2 %collective-permute-start.9 = (bf16[16,7168]{1,0:T(8,128)(2,1)S(1)}, bf16[16,7168]{1,0:T(8,128)(2,1)S(1)}, u32[]{:S(2)}, u32[]{:S(2)}) collective-permute-start(bf16[16,7168]{1,0:T(8,128)(2,1)S(1)} %collective-permute-done.6.refs_2_.refs_6_), channel_id=1, source_target_pairs={{0,16},{16,0},{1,17},{17,1},{2,18},{18,2},{3,19},{19,3},{4,20},{20... | collective-permute-start | bytes 688136 | tf_op jit(solution)/shard_map/ppermute | solution.py:223
  24.2 2.2 %base_part.6 = (f32[64,1536]{1,0:T(8,128)S(1)}, bf16[2,2048,512]{2,1,0:T(8,128)(2,1)S(1)}) custom-call(bf16[64,2048]{1,0:T(8,128)(2,1)S(1)} %get-tuple-element.52.rows, bf16[2048,7168]{1,0:T(8,128)(2,1)} %weight.9, bf16[3,2048,512]{2,1,0:T(8,128)(2,1)S(1)} %get-tuple-element.62.refs_0_, bf16[16,64]{1,0:T(8,128)(2,1)S(1)} %fusion.1.refs_1_, ...), custom_call_target="tpu_custom_call" | custom-call | flops 10000000000 | bytes 1 | tf_op jit(solution)/shard_map/base_part/pallas_call | solution.py:293
  26.4 0.0 collective-permute-done.5
  26.4 1.2 %collective-permute-start.7 = (bf16[16,64]{1,0:T(8,128)(2,1)S(1)}, bf16[16,64]{1,0:T(8,128)(2,1)S(1)}, u32[]{:S(2)}, u32[]{:S(2)}) collective-permute-start(bf16[16,64]{1,0:T(8,128)(2,1)S(1)} %add.32.refs_1_), channel_id=1, source_target_pairs={{0,4},{4,0},{8,12},{12,8},{16,20},{20,16},{24,28},{28,24},{1,5},{5... | collective-permute-start | bytes 6152 | tf_op jit(solution)/shard_map/ppermute | solution.py:217
  27.6 2.0 %base_part.7.refs_3_ = f32[64,1536]{1,0:T(8,128)S(1)} custom-call(bf16[64,2048]{1,0:T(8,128)(2,1)S(1)} %get-tuple-element.52.rows, bf16[2048,7168]{1,0:T(8,128)(2,1)} %weight.9, bf16[2,2048,512]{2,1,0:T(8,128)(2,1)S(1)} %get-tuple-element.68.refs_0_, bf16[16,64]{1,0:T(8,128)(2,1)S(1)} %add.32.refs_1_, bf16[16,7168]{1,0:T(8,128)(2,1)S(1)} %collective-permute-done.6.refs_2_.refs_6_), custom_call_target="tpu_custom_call" | custom-call | flops 1 | bytes 1 | tf_op jit(solution)/shard_map/base_part/pallas_call | solution.py:293
  29.7 0.5 %collective-permute-done.7 = bf16[16,64]{1,0:T(8,128)(2,1)S(1)} collective-permute-done((bf16[16,64]{1,0:T(8,128)(2,1)S(1)}, bf16[16,64]{1,0:T(8,128)(2,1)S(1)}, u32[]{:S(2)}, u32[]{:S(2)}) %collective-permute-start.7) | collective-permute-done | bytes 2080 | tf_op jit(solution)/shard_map/ppermute | solution.py:217
  30.1 0.0 collective-permute-done.8.refs_7_
  30.1 0.3 collective-permute-done.9.refs_8_
  30.4 0.4 add_delta.3
  30.8 0.1 collective-permute-start.11
  30.9 0.3 add_delta.2
  31.2 0.6 %collective-permute-start.10 = (f32[16,2560]{1,0:T(8,128)S(1)}, f32[16,2560]{1,0:T(8,128)S(1)}, u32[]{:S(2)}, u32[]{:S(2)}) collective-permute-start(f32[16,2560]{1,0:T(8,128)S(1)} %get-tuple-element.74), channel_id=1, source_target_pairs={{0,1},{1,0},{2,3},{3,2},{4,5},{5,4},{6,7},{7,6},{8,9},{9,8},{10,11... | collective-permute-start | bytes 491528 | tf_op jit(solution)/shard_map/ppermute | solution.py:220
  31.8 1.0 %collective-permute-done.10 = f32[16,2560]{1,0:T(8,128)S(1)} collective-permute-done((f32[16,2560]{1,0:T(8,128)S(1)}, f32[16,2560]{1,0:T(8,128)S(1)}, u32[]{:S(2)}, u32[]{:S(2)}) %collective-permute-start.10) | collective-permute-done | bytes 163872 | tf_op jit(solution)/shard_map/ppermute | solution.py:220
  32.8 0.0 collective-permute-done.11
  32.9 0.4 %collective-permute-start.12 = (f32[16,2560]{1,0:T(8,128)S(1)}, f32[16,2560]{1,0:T(8,128)S(1)}, u32[]{:S(2)}, u32[]{:S(2)}) collective-permute-start(f32[16,2560]{1,0:T(8,128)S(1)} %get-tuple-element.82), channel_id=1, source_target_pairs={{0,1},{1,0},{2,3},{3,2},{4,5},{5,4},{6,7},{7,6},{8,9},{9,8},{10,11... | collective-permute-start | bytes 491528 | tf_op jit(solution)/shard_map/ppermute | solution.py:220
  33.3 0.6 %collective-permute-start.13 = (bf16[16,2560]{1,0:T(8,128)(2,1)S(1)}, bf16[16,2560]{1,0:T(8,128)(2,1)S(1)}, u32[]{:S(2)}, u32[]{:S(2)}) collective-permute-start(bf16[16,2560]{1,0:T(8,128)(2,1)S(1)} %add_convert_fusion.3), channel_id=1, source_target_pairs={{0,2},{1,3},{2,0},{3,1},{4,6},{5,7},{6,4},{7,5},{8,10},{9,11},{10,... | collective-permute-start | bytes 245768 | tf_op jit(solution)/shard_map/ppermute | solution.py:220
  33.9 1.5 %collective-permute-start.15 = (bf16[16,4608]{1,0:T(8,128)(2,1)S(1)}, bf16[16,4608]{1,0:T(8,128)(2,1)S(1)}, u32[]{:S(2)}, u32[]{:S(2)}) collective-permute-start(bf16[16,4608]{1,0:T(8,128)(2,1)S(1)} %add_convert_fusion.1), channel_id=1, source_target_pairs={{0,2},{1,3},{2,0},{3,1},{4,6},{5,7},{6,4},{7,5},{8,10},{9,11},{10,... | collective-permute-start | bytes 442376 | tf_op jit(solution)/shard_map/ppermute | solution.py:220
  35.4 0.0 collective-permute-start.14
  35.4 3.3 %collective-permute-done.13 = bf16[16,2560]{1,0:T(8,128)(2,1)S(1)} collective-permute-done((bf16[16,2560]{1,0:T(8,128)(2,1)S(1)}, bf16[16,2560]{1,0:T(8,128)(2,1)S(1)}, u32[]{:S(2)}, u32[]{:S(2)}) %collective-permute-start.13) | collective-permute-done | bytes 81952 | tf_op jit(solution)/shard_map/ppermute | solution.py:220
  38.7 0.0 collective-permute-done.12
  38.7 2.3 %collective-permute-done.15 = bf16[16,4608]{1,0:T(8,128)(2,1)S(1)} collective-permute-done((bf16[16,4608]{1,0:T(8,128)(2,1)S(1)}, bf16[16,4608]{1,0:T(8,128)(2,1)S(1)}, u32[]{:S(2)}, u32[]{:S(2)}) %collective-permute-start.15) | collective-permute-done | bytes 147488 | tf_op jit(solution)/shard_map/ppermute | solution.py:220
  41.0 0.0 collective-permute-done.14
  41.1 0.7 %pad_maximum_fusion = bf16[16,7168]{1,0:T(8,128)(2,1)} fusion(bf16[16,4608]{1,0:T(8,128)(2,1)S(1)} %add_convert_fusion, bf16[16,2560]{1,0:T(8,128)(2,1)S(1)} %add_convert_fusion.2), kind=kLoop, calls=%fused_computation.2 | loop fusion | flops 458752 | bytes 458752 | tf_op jit(solution)/shard_map/concatenate | solution.py:358
  (9 shorter events, 0.1 us)
Async XLA Ops:
  0.0 13.1 %collective-permute-start = (bf16[16,2048]{1,0:T(8,128)(2,1)}, bf16[16,2048]{1,0:T(8,128)(2,1)S(1)}, u32[]{:S(2)}, u32[]{:S(2)}) collective-permute-start(bf16[16,2048]{1,0:T(8,128)(2,1)} %refs_2_.1), channel_id=1, source_target_pairs={{0,8},{4,12},{8,0},{12,4},{16,24},{20,28},{24,16},{28,20},{1,9},{5... | collective-permute-start | bytes 196616 | tf_op jit(solution)/shard_map/ppermute | solution.py:217
  4.0 9.1 %collective-permute-start.1 = (bf16[16,2048]{1,0:T(8,128)(2,1)}, bf16[16,2048]{1,0:T(8,128)(2,1)S(1)}, u32[]{:S(2)}, u32[]{:S(2)}) collective-permute-start(bf16[16,2048]{1,0:T(8,128)(2,1)} %refs_2_.1), channel_id=1, source_target_pairs={{0,12},{4,8},{8,4},{12,0},{16,28},{20,24},{24,20},{28,16},{1,13},{... | collective-permute-start | bytes 196616 | tf_op jit(solution)/shard_map/ppermute | solution.py:217
  5.4 7.7 %collective-permute-start.2 = (bf16[16,2048]{1,0:T(8,128)(2,1)}, bf16[16,2048]{1,0:T(8,128)(2,1)S(1)}, u32[]{:S(2)}, u32[]{:S(2)}) collective-permute-start(bf16[16,2048]{1,0:T(8,128)(2,1)} %refs_2_.1), channel_id=1, source_target_pairs={{0,4},{4,0},{8,12},{12,8},{16,20},{20,16},{24,28},{28,24},{1,5},{5... | collective-permute-start | bytes 196616 | tf_op jit(solution)/shard_map/ppermute | solution.py:217
  9.6 13.4 %collective-permute-start.6 = (bf16[16,7168]{1,0:T(8,128)(2,1)S(1)}, bf16[16,7168]{1,0:T(8,128)(2,1)S(1)}, u32[]{:S(2)}, u32[]{:S(2)}) collective-permute-start(bf16[16,7168]{1,0:T(8,128)(2,1)S(1)} %get-tuple-element.63), channel_id=1, source_target_pairs={{0,8},{4,12},{8,0},{12,4},{16,28},{20,24},{24,20},{28,16},{1,9},{5... | collective-permute-start | bytes 688136 | tf_op jit(solution)/shard_map/ppermute | solution.py:217
  12.5 17.6 %collective-permute-start.8 = (bf16[16,7168]{1,0:T(8,128)(2,1)S(1)}, bf16[16,7168]{1,0:T(8,128)(2,1)S(1)}, u32[]{:S(2)}, u32[]{:S(2)}) collective-permute-start(bf16[16,7168]{1,0:T(8,128)(2,1)S(1)} %get-tuple-element.72), channel_id=1, source_target_pairs={{0,4},{4,0},{8,12},{12,8},{16,20},{20,16},{24,28},{28,24},{1,5},{5... | collective-permute-start | bytes 688136 | tf_op jit(solution)/shard_map/ppermute | solution.py:217
  13.4 3.7 %collective-permute-start.3 = (f32[32,64]{1,0:T(8,128)S(1)}, f32[32,64]{1,0:T(8,128)S(1)}, u32[]{:S(2)}, u32[]{:S(2)}) collective-permute-start(f32[32,64]{1,0:T(8,128)S(1)} %get-tuple-element.51.refs_1_), channel_id=1, source_target_pairs={{0,1},{1,0},{2,3},{3,2},{4,5},{5,4},{6,7},{7,6},{8,9},{9,8},{10,11... | collective-permute-start | bytes 24584 | tf_op jit(solution)/shard_map/ppermute | solution.py:220
  17.1 4.5 %collective-permute-start.4 = (f32[16,64]{1,0:T(8,128)S(1)}, f32[16,64]{1,0:T(8,128)S(1)}, u32[]{:S(2)}, u32[]{:S(2)}) collective-permute-start(f32[16,64]{1,0:T(8,128)S(1)} %slice.8), channel_id=1, source_target_pairs={{0,2},{1,3},{2,0},{3,1},{4,6},{5,7},{6,4},{7,5},{8,10},{9,11},{10,... | collective-permute-start | bytes 12296 | tf_op jit(solution)/shard_map/ppermute | solution.py:220
  21.7 4.8 %collective-permute-start.5 = (bf16[16,64]{1,0:T(8,128)(2,1)S(1)}, bf16[16,64]{1,0:T(8,128)(2,1)S(1)}, u32[]{:S(2)}, u32[]{:S(2)}) collective-permute-start(bf16[16,64]{1,0:T(8,128)(2,1)S(1)} %fusion.1.refs_1_), channel_id=1, source_target_pairs={{0,8},{4,12},{8,0},{12,4},{16,24},{20,28},{24,16},{28,20},{1,9},{5... | collective-permute-start | bytes 6152 | tf_op jit(solution)/shard_map/ppermute | solution.py:217
  23.0 7.4 %collective-permute-start.9 = (bf16[16,7168]{1,0:T(8,128)(2,1)S(1)}, bf16[16,7168]{1,0:T(8,128)(2,1)S(1)}, u32[]{:S(2)}, u32[]{:S(2)}) collective-permute-start(bf16[16,7168]{1,0:T(8,128)(2,1)S(1)} %collective-permute-done.6.refs_2_.refs_6_), channel_id=1, source_target_pairs={{0,16},{16,0},{1,17},{17,1},{2,18},{18,2},{3,19},{19,3},{4,20},{20... | collective-permute-start | bytes 688136 | tf_op jit(solution)/shard_map/ppermute | solution.py:223
  26.4 3.7 %collective-permute-start.7 = (bf16[16,64]{1,0:T(8,128)(2,1)S(1)}, bf16[16,64]{1,0:T(8,128)(2,1)S(1)}, u32[]{:S(2)}, u32[]{:S(2)}) collective-permute-start(bf16[16,64]{1,0:T(8,128)(2,1)S(1)} %add.32.refs_1_), channel_id=1, source_target_pairs={{0,4},{4,0},{8,12},{12,8},{16,20},{20,16},{24,28},{28,24},{1,5},{5... | collective-permute-start | bytes 6152 | tf_op jit(solution)/shard_map/ppermute | solution.py:217
  30.8 2.0 %collective-permute-start.11 = (f32[16,4608]{1,0:T(8,128)S(1)}, f32[16,4608]{1,0:T(8,128)S(1)}, u32[]{:S(2)}, u32[]{:S(2)}) collective-permute-start(f32[16,4608]{1,0:T(8,128)S(1)} %get-tuple-element.79), channel_id=1, source_target_pairs={{0,1},{1,0},{2,3},{3,2},{4,5},{5,4},{6,7},{7,6},{8,9},{9,8},{10,11... | collective-permute-start | bytes 884744 | tf_op jit(solution)/shard_map/ppermute | solution.py:220
  31.2 1.6 %collective-permute-start.10 = (f32[16,2560]{1,0:T(8,128)S(1)}, f32[16,2560]{1,0:T(8,128)S(1)}, u32[]{:S(2)}, u32[]{:S(2)}) collective-permute-start(f32[16,2560]{1,0:T(8,128)S(1)} %get-tuple-element.74), channel_id=1, source_target_pairs={{0,1},{1,0},{2,3},{3,2},{4,5},{5,4},{6,7},{7,6},{8,9},{9,8},{10,11... | collective-permute-start | bytes 491528 | tf_op jit(solution)/shard_map/ppermute | solution.py:220
  32.9 5.8 %collective-permute-start.12 = (f32[16,2560]{1,0:T(8,128)S(1)}, f32[16,2560]{1,0:T(8,128)S(1)}, u32[]{:S(2)}, u32[]{:S(2)}) collective-permute-start(f32[16,2560]{1,0:T(8,128)S(1)} %get-tuple-element.82), channel_id=1, source_target_pairs={{0,1},{1,0},{2,3},{3,2},{4,5},{5,4},{6,7},{7,6},{8,9},{9,8},{10,11... | collective-permute-start | bytes 491528 | tf_op jit(solution)/shard_map/ppermute | solution.py:220
  33.3 5.4 %collective-permute-start.13 = (bf16[16,2560]{1,0:T(8,128)(2,1)S(1)}, bf16[16,2560]{1,0:T(8,128)(2,1)S(1)}, u32[]{:S(2)}, u32[]{:S(2)}) collective-permute-start(bf16[16,2560]{1,0:T(8,128)(2,1)S(1)} %add_convert_fusion.3), channel_id=1, source_target_pairs={{0,2},{1,3},{2,0},{3,1},{4,6},{5,7},{6,4},{7,5},{8,10},{9,11},{10,... | collective-permute-start | bytes 245768 | tf_op jit(solution)/shard_map/ppermute | solution.py:220
  33.9 7.1 %collective-permute-start.15 = (bf16[16,4608]{1,0:T(8,128)(2,1)S(1)}, bf16[16,4608]{1,0:T(8,128)(2,1)S(1)}, u32[]{:S(2)}, u32[]{:S(2)}) collective-permute-start(bf16[16,4608]{1,0:T(8,128)(2,1)S(1)} %add_convert_fusion.1), channel_id=1, source_target_pairs={{0,2},{1,3},{2,0},{3,1},{4,6},{5,7},{6,4},{7,5},{8,10},{9,11},{10,... | collective-permute-start | bytes 442376 | tf_op jit(solution)/shard_map/ppermute | solution.py:220
  35.4 5.6 %collective-permute-start.14 = (f32[16,4608]{1,0:T(8,128)S(1)}, f32[16,4608]{1,0:T(8,128)S(1)}, u32[]{:S(2)}, u32[]{:S(2)}) collective-permute-start(f32[16,4608]{1,0:T(8,128)S(1)} %get-tuple-element.86), channel_id=1, source_target_pairs={{0,1},{1,0},{2,3},{3,2},{4,5},{5,4},{6,7},{7,6},{8,9},{9,8},{10,11... | collective-permute-start | bytes 884744 | tf_op jit(solution)/shard_map/ppermute | solution.py:220
